TPU v7x, 32 devices: a whole 2x2x4 slice. The times are simulated.
32 devices in a mesh: groups: 2 (over y), epoch: 4 (over z), space: 2 (over x), sub: 2 (over core).
Axes of the slice: x: 2, y: 2, z: 4, core: 2. Of those that a mesh axis runs over, the one named last changes fastest.
Arguments:
- slc: bfloat16 [2, 64, 128, 1024], P(None, ('groups', 'epoch'), 'space', 'sub'), parts along dimension 1, may hold values from -8 to 8
- offsets: int32 [64, 4], P(('groups', 'epoch')), parts along dimension 0, may hold values from 1 to 8, as said below
- weights: float32 [64, 4], P(('groups', 'epoch')), parts along dimension 0, may hold values from 0.3 to 3
- estimate: float32 [64, 32, 1024], P(('groups', 'epoch'), 'space', 'sub'), parts along dimension 0, may hold values from -2 to 2
- direction: float32 [64, 32, 1024], P(('groups', 'epoch'), 'space', 'sub'), parts along dimension 0, may hold values from -2 to 2
- prev_mean: float32 [1], replicated, may hold values from 0.05 to 0.5
Outputs:
- new_estimate: float32 [64, 32, 1024], P(('groups', 'epoch'), 'space', 'sub'), parts along dimension 0
- new_direction: float32 [64, 32, 1024], P(('groups', 'epoch'), 'space', 'sub'), parts along dimension 0
There are 2 independent parts, one for each index of `groups`. A program takes and returns all parts, laid end to end along the dimension named above; an argument that names none is the same for every part. Nothing has to cross between parts.
Inputs may be any that keep to these rules, and one draw needn't show every extreme that they name: `offsets`: each row holds 4 different distances; partners wrap past the last epoch to the first.
All inputs are finite; a program needn't handle non-finite values.
Results may differ from a plain program's by a relative error of at most 0.0003.
Values may be sent and summed in bfloat16 or wider, within the bound.
No kernel may reach another device: no remote copies, remote signals or barrier semaphores. Data moves between devices by JAX's collectives and lax.ppermute only.
A program may use at most 64 MiB of HBM per device.

v0:
```python
import jax
import jax.numpy as jnp
from jax import lax
from jax.sharding import PartitionSpec as P

SLOTS = 4
OFFS = 8
LOOK = 4
RADIUS = 3


EPSILON = 1e-06


def passed_along(x, axis, by):
    size = lax.axis_size(axis)
    return lax.ppermute(x, axis, [(i, (i + by) % size) for i in range(size)])


def extended_2(block, sides, width):
    for axis, dim in sides:
        count = lax.axis_size(axis)
        forward = [(i, i + 1) for i in range(count - 1)]
        backward = [(target, source) for source, target in forward]
        low = lax.ppermute(
            lax.slice_in_dim(block, block.shape[dim] - width, None, axis=dim), axis, forward
        )
        high = lax.ppermute(lax.slice_in_dim(block, 0, width, axis=dim), axis, backward)
        block = jnp.concatenate([low, block, high], axis=dim)
    return block


def looked_sum(field):
    shape = field.shape
    return jnp.sum(field.reshape(shape[:-2] + (shape[-2] // LOOK, LOOK, shape[-1])), axis=-2)


def window_sum(padded, axis):
    length = padded.shape[axis] - 2 * RADIUS
    total = lax.slice_in_dim(padded, 0, length, axis=axis)
    for shift_at in range(1, 2 * RADIUS + 1):
        total = total + lax.slice_in_dim(padded, shift_at, shift_at + length, axis=axis)
    return total


def on_device(slc, offsets, weights, estimate, direction, prev_mean):
    epochs_here = slc.shape[1]
    look_rows = slc.shape[2] // LOOK
    col_count = slc.shape[3]
    ahead = passed_along(slc, "epoch", -1)
    extended = jnp.concatenate([slc, ahead], axis=1)
    numbers = jnp.arange(epochs_here, dtype=jnp.int32)
    partner = numbers[:, None] + offsets
    own_real = slc[0].astype(jnp.float32)
    own_imag = slc[1].astype(jnp.float32)
    ext_real = extended[0].astype(jnp.float32)
    ext_imag = extended[1].astype(jnp.float32)
    powers = looked_sum(ext_real * ext_real + ext_imag * ext_imag)
    pieces = []
    for slot_index in range(SLOTS):
        mate_real = jnp.take(ext_real, partner[:, slot_index], axis=0)
        mate_imag = jnp.take(ext_imag, partner[:, slot_index], axis=0)
        pieces.append(looked_sum(own_real * mate_real + own_imag * mate_imag))
        pieces.append(looked_sum(own_imag * mate_real - own_real * mate_imag))
    pair_count = epochs_here * 2 * SLOTS
    stacked = jnp.concatenate(
        [jnp.stack(pieces, axis=1).reshape(pair_count, look_rows, col_count), powers], axis=0
    )
    padded = extended_2(stacked, (("space", 1), ("sub", 2)), RADIUS)
    boxed = window_sum(window_sum(padded, 1), 2)
    pair_boxed = boxed[:pair_count].reshape(epochs_here, 2 * SLOTS, look_rows, col_count)
    power_box = boxed[pair_count:]
    coh_real = pair_boxed[:, 0::2]
    coh_imag = pair_boxed[:, 1::2]
    denominator = power_box[:epochs_here, None] * jnp.take(power_box, partner, axis=0) + EPSILON
    coherence = (coh_real * coh_real + coh_imag * coh_imag) / denominator
    observed = coh_imag / jnp.sqrt(denominator)
    est_ahead = passed_along(estimate, "epoch", -1)
    est_extended = jnp.concatenate([estimate, est_ahead], axis=0)
    fitted = estimate[:, None] - jnp.take(est_extended, partner, axis=0)
    factor = weights[:, :, None, None] * coherence
    weighted = factor * (observed - fitted)
    flattened = weighted.reshape(epochs_here * SLOTS, look_rows * col_count)
    selector = (
        jnp.arange(epochs_here + OFFS, dtype=jnp.int32)[:, None] == partner.reshape(1, -1)
    ).astype(jnp.float32)
    gathered = jnp.dot(
        selector, flattened, precision=lax.Precision.HIGHEST, preferred_element_type=jnp.float32
    ).reshape(epochs_here + OFFS, look_rows, col_count)
    own_part = jnp.sum(weighted, axis=1) - gathered[:epochs_here]
    returned = passed_along(-gathered[epochs_here:], "epoch", 1)
    gradient = jnp.concatenate([own_part + returned, own_part[OFFS:]], axis=0)
    cell_count = float(
        epochs_here
        * lax.axis_size("epoch")
        * look_rows
        * lax.axis_size("space")
        * col_count
        * lax.axis_size("sub")
    )
    local_norm = jnp.sum(gradient * gradient)
    local_crossed = jnp.sum(gradient * direction)
    mean_before = prev_mean[0]
    fields_ahead = passed_along(
        jnp.stack([gradient, direction]).astype(jnp.bfloat16), "epoch", -1
    ).astype(jnp.float32)
    grad_extended = jnp.concatenate([gradient, fields_ahead[0]], axis=0)
    old_extended = jnp.concatenate([direction, fields_ahead[1]], axis=0)
    grad_spread = gradient[:, None] - jnp.take(grad_extended, partner, axis=0)
    old_spread = direction[:, None] - jnp.take(old_extended, partner, axis=0)
    totals = lax.psum(
        (
            local_norm,
            local_crossed,
            jnp.sum(factor * grad_spread * grad_spread),
            jnp.sum(factor * grad_spread * old_spread),
            jnp.sum(factor * old_spread * old_spread),
        ),
        ("epoch", "space", "sub"),
    )
    grad_norm, crossed, grad_term, mixed_term, old_term = totals
    momentum = grad_norm / cell_count / mean_before
    new_direction = gradient + momentum * direction
    curvature = grad_term + 2.0 * momentum * mixed_term + momentum * momentum * old_term
    along_sum = grad_norm + momentum * crossed
    step_size = along_sum / curvature
    return (estimate + step_size * new_direction, new_direction)


def solution(mesh):
    return jax.shard_map(
        on_device,
        mesh=mesh,
        in_specs=(
            P(None, ("groups", "epoch"), "space", "sub"),
            P(("groups", "epoch"), None),
            P(("groups", "epoch"), None),
            P(("groups", "epoch"), "space", "sub"),
            P(("groups", "epoch"), "space", "sub"),
            P(),
        ),
        out_specs=(P(("groups", "epoch"), "space", "sub"), P(("groups", "epoch"), "space", "sub")),
        check_vma=False,
    )
```

profile of v0, /device:TPU:0, one launch (start us, length us, event | category | flops | bytes accessed | tf_op | source)
XLA Modules:
  0.0 223.1 jit_solution(3602358008610256752)
XLA Ops:
  0.6 5.1 %collective-permute-start = (bf16[2,8,64,512]{3,2,1,0:T(8,128)(2,1)}, bf16[2,8,64,512]{3,2,1,0:T(8,128)(2,1)S(1)}, u32[]{:S(2)}, u32[]{:S(2)}) collective-permute-start(bf16[2,8,64,512]{3,2,1,0:T(8,128)(2,1)} %param.10), channel_id=1, source_target_pairs={{0,12},{4,0},{8,4},{12,8},{1,13},{5,1},{9,5},{13,9},{2,14},{6,2},{... | collective-permute-start | bytes 3145736 | tf_op jit(solution)/shard_map/ppermute | solution.py:17
  7.8 20.7 %collective-permute-done = bf16[2,8,64,512]{3,2,1,0:T(8,128)(2,1)S(1)} collective-permute-done((bf16[2,8,64,512]{3,2,1,0:T(8,128)(2,1)}, bf16[2,8,64,512]{3,2,1,0:T(8,128)(2,1)S(1)}, u32[]{:S(2)}, u32[]{:S(2)}) %collective-permute-start) | collective-permute-done | bytes 1048608 | tf_op jit(solution)/shard_map/ppermute | solution.py:17
  28.6 1.7 fusion
  30.3 1.9 convert_bitcast_fusion.1
  32.2 3.2 %gather_fusion.5 = f32[8,64,512]{2,1,0:T(8,128)} fusion(f32[16,64,512]{2,1,0:T(8,128)} %get-tuple-element.42, s32[1024]{0:T(1024)S(1)} %get-tuple-element.61), kind=kCustom, calls=%fused_computation.6.clone | custom fusion | bytes 2097184 | tf_op jit(solution)/shard_map/jit(_take)/gather | solution.py:62
  36.9 3.3 %gather_fusion.1 = f32[8,64,512]{2,1,0:T(8,128)} fusion(f32[16,64,512]{2,1,0:T(8,128)} %get-tuple-element.42, s32[1024]{0:T(1024)S(1)} %get-tuple-element.63), kind=kCustom, calls=%fused_computation.2.clone | custom fusion | bytes 2097184 | tf_op jit(solution)/shard_map/jit(_take)/gather | solution.py:62
  41.8 3.2 %gather_fusion.7 = f32[8,64,512]{2,1,0:T(8,128)} fusion(f32[16,64,512]{2,1,0:T(8,128)} %get-tuple-element.42, s32[1024]{0:T(1024)S(1)} %get-tuple-element.60), kind=kCustom, calls=%fused_computation.8.clone | custom fusion | bytes 2097184 | tf_op jit(solution)/shard_map/jit(_take)/gather | solution.py:62
  45.0 1.6 gather_fusion.6
  46.6 3.2 %gather_fusion.3 = f32[8,64,512]{2,1,0:T(8,128)} fusion(f32[16,64,512]{2,1,0:T(8,128)} %get-tuple-element.42, s32[1024]{0:T(1024)S(1)} %get-tuple-element.62), kind=kCustom, calls=%fused_computation.4.clone | custom fusion | bytes 2097184 | tf_op jit(solution)/shard_map/jit(_take)/gather | solution.py:62
  51.4 1.9 add.120
  53.4 4.8 %fusion.7 = (f32[8,64,512]{2,1,0:T(8,128)}, f32[8,64,512]{2,1,0:T(8,128)}, f32[8,64,512]{2,1,0:T(8,128)}, f32[8,64,512]{2,1,0:T(8,128)}) fusion(f32[8,64,512]{2,1,0:T(8,128)} %gather_fusion.5, f32[8,64,512]{2,1,0:T(8,128)} %gather_fusion.4, pred[8]{0:T(512)(128)(4,1)S(1)} %get-tuple-element.52, bf16[2,8,64,512]{3,2,1,0:T(8,128)(2,1)S(1)} %copy-done.1, ...), kind=kLoop, calls=%fused_computation.53 | loop fusion | flops 4718592 | bytes 9437200 | tf_op jit(solution)/shard_map/sub | solution.py:64
  58.2 2.5 %reshape.74 = f32[8,16,4,512]{3,2,1,0:T(4,128)} reshape(f32[8,64,512]{2,1,0:T(8,128)} %get-tuple-element.45) | data formatting | bytes 2097152 | tf_op jit(solution)/shard_map/reshape | solution.py:35
  60.7 2.2 reduce_sum.143
  62.9 1.9 reduce_sum.135
  64.8 2.5 %reshape.75 = f32[8,16,4,512]{3,2,1,0:T(4,128)} reshape(f32[8,64,512]{2,1,0:T(8,128)} %get-tuple-element.46) | data formatting | bytes 2097152 | tf_op jit(solution)/shard_map/reshape | solution.py:35
  67.3 1.9 reduce_sum.136
  69.2 4.8 %fusion.9 = (f32[8,64,512]{2,1,0:T(8,128)}, f32[8,64,512]{2,1,0:T(8,128)}, f32[8,64,512]{2,1,0:T(8,128)}, f32[8,64,512]{2,1,0:T(8,128)}) fusion(f32[8,64,512]{2,1,0:T(8,128)} %gather_fusion.7, f32[8,64,512]{2,1,0:T(8,128)} %gather_fusion.6, pred[8]{0:T(512)(128)(4,1)S(1)} %get-tuple-element.21, bf16[2,8,64,512]{3,2,1,0:T(8,128)(2,1)S(1)} %copy-done.1, ...), kind=kLoop, calls=%fused_computation.55 | loop fusion | flops 4718592 | bytes 9437200 | tf_op jit(solution)/shard_map/sub | solution.py:64
  74.0 2.6 %reshape.76 = f32[8,16,4,512]{3,2,1,0:T(4,128)} reshape(f32[8,64,512]{2,1,0:T(8,128)} %get-tuple-element.43) | data formatting | bytes 2097152 | tf_op jit(solution)/shard_map/reshape | solution.py:35
  76.6 2.6 %reduce_sum.137 = f32[8,16,512]{2,1,0:T(8,128)} reduce(f32[8,16,4,512]{3,2,1,0:T(4,128)} %reshape.76, f32[]{:T(128)} %constant.20.clone.1), dimensions={2}, to_apply=%region_2.4 | reduce | flops 196608 | bytes 1310724 | tf_op jit(solution)/shard_map/reduce_sum | solution.py:35
  80.5 2.7 %reduce_sum.138 = f32[8,16,512]{2,1,0:T(8,128)} reduce(f32[8,16,4,512]{3,2,1,0:T(4,128)} %reshape.77, f32[]{:T(128)} %constant.20.clone.1), dimensions={2}, to_apply=%region_3.5 | reduce | flops 196608 | bytes 1310724 | tf_op jit(solution)/shard_map/reduce_sum | solution.py:35
  83.1 2.5 %reshape.78 = f32[8,16,4,512]{3,2,1,0:T(4,128)} reshape(f32[8,64,512]{2,1,0:T(8,128)} %get-tuple-element.34) | data formatting | bytes 2097152 | tf_op jit(solution)/shard_map/reshape | solution.py:35
  85.6 2.6 %reduce_sum.139 = f32[8,16,512]{2,1,0:T(8,128)} reduce(f32[8,16,4,512]{3,2,1,0:T(4,128)} %reshape.78, f32[]{:T(128)} %constant.20.clone.1), dimensions={2}, to_apply=%region_4.6 | reduce | flops 196608 | bytes 1310724 | tf_op jit(solution)/shard_map/reduce_sum | solution.py:35
  89.5 2.7 %reduce_sum.140 = f32[8,16,512]{2,1,0:T(8,128)} reduce(f32[8,16,4,512]{3,2,1,0:T(4,128)} %reshape.79, f32[]{:T(128)} %constant.20.clone.1), dimensions={2}, to_apply=%region_5.7 | reduce | flops 196608 | bytes 1310724 | tf_op jit(solution)/shard_map/reduce_sum | solution.py:35
  92.1 2.5 %reshape.80 = f32[8,16,4,512]{3,2,1,0:T(4,128)} reshape(f32[8,64,512]{2,1,0:T(8,128)} %get-tuple-element.32) | data formatting | bytes 2097152 | tf_op jit(solution)/shard_map/reshape | solution.py:35
  94.7 2.5 %reduce_sum.141 = f32[8,16,512]{2,1,0:T(8,128)} reduce(f32[8,16,4,512]{3,2,1,0:T(4,128)} %reshape.80, f32[]{:T(128)} %constant.20.clone.1), dimensions={2}, to_apply=%region_6.8 | reduce | flops 196608 | bytes 1310724 | tf_op jit(solution)/shard_map/reduce_sum | solution.py:35
  98.5 2.6 %reduce_sum.142 = f32[8,16,512]{2,1,0:T(8,128)} reduce(f32[8,16,4,512]{3,2,1,0:T(4,128)} %reshape.81, f32[]{:T(128)} %constant.20.clone.1), dimensions={2}, to_apply=%region_7.9 | reduce | flops 196608 | bytes 1310724 | tf_op jit(solution)/shard_map/reduce_sum | solution.py:35
  105.5 5.9 %collective-permute-start.1 = (f32[80,3,512]{2,0,1:T(8,128)}, f32[80,3,512]{2,0,1:T(8,128)}, u32[]{:S(2)}, u32[]{:S(2)}) collective-permute-start(f32[80,3,512]{2,0,1:T(8,128)} %copy.55), channel_id=1, source_target_pairs={{0,2},{1,3},{4,6},{5,7},{8,10},{9,11},{12,14},{13,15},{16,18},{17,... | collective-permute-start | bytes 1474568 | tf_op jit(solution)/shard_map/ppermute | solution.py:25
  111.4 4.2 %collective-permute-start.5 = (f32[8,16,512]{2,1,0:T(8,128)S(1)}, f32[8,16,512]{2,1,0:T(8,128)}, u32[]{:S(2)}, u32[]{:S(2)}) collective-permute-start(f32[8,16,512]{2,1,0:T(8,128)S(1)} %copy-done.8), channel_id=1, source_target_pairs={{0,12},{4,0},{8,4},{12,8},{1,13},{5,1},{9,5},{13,9},{2,14},{6,2},{... | collective-permute-start | bytes 786440 | tf_op jit(solution)/shard_map/ppermute | solution.py:17
  118.5 1.7 collective-permute-done.1
  121.6 1.9 pad_maximum_fusion.4
  123.5 2.2 copy.60
  126.9 2.2 copy.59
  129.1 4.2 %collective-permute-start.3 = (f32[80,22,3]{0,1,2:T(8,128)}, f32[80,22,3]{0,1,2:T(8,128)}, u32[]{:S(2)}, u32[]{:S(2)}) collective-permute-start(f32[80,22,3]{0,1,2:T(8,128)} %copy.59), channel_id=1, source_target_pairs={{0,1},{2,3},{4,5},{6,7},{8,9},{10,11},{12,13},{14,15},{16,17},{18,... | collective-permute-start | bytes 63368 | tf_op jit(solution)/shard_map/ppermute | solution.py:25
  133.3 1.8 pad_maximum_fusion.7
  135.1 2.7 %gather_fusion.9 = f32[32,16,512]{2,1,0:T(8,128)} fusion(f32[16,16,512]{2,1,0:T(8,128)} %pad_maximum_fusion.7, s32[1024]{0:T(1024)S(1)} %pad_clamp_fusion), kind=kCustom, calls=%fused_computation.9.clone | custom fusion | bytes 2097280 | tf_op jit(solution)/shard_map/jit(_take)/gather | solution.py:80
  137.8 2.1 copy.62
  139.9 2.1 copy.61
  142.0 6.8 %pad_maximum_fusion = f32[80,22,518]{2,1,0:T(8,128)S(1)} fusion(f32[80,22,3]{2,1,0:T(8,128)} %copy.62, f32[80,3,512]{2,1,0:T(4,128)S(1)} %copy.58, f32[16,16,512]{2,1,0:T(8,128)S(1)} %copy-done.2, f32[64,16,512]{2,1,0:T(8,128)S(1)} %bitcast.80, f32[80,3,512]{2,1,0:T(4,128)} %copy-done.3, f32[80,22,3]{2,1,0:T(8,128)} %copy.61), kind=kLoop, calls=%fused_computation.12 | loop fusion | flops 4558400 | bytes 7293440 | tf_op jit(solution)/shard_map/concatenate | solution.py:29
  148.8 2.0 slice_add_fusion
  150.7 4.2 %slice_add_fusion.6 = f32[80,16,512]{2,1,0:T(8,128)S(1)} fusion(f32[80,16,518]{2,1,0:T(8,128)S(1)} %slice_add_fusion), kind=kLoop, calls=%fused_computation.39 | loop fusion | flops 3932160 | bytes 20971520 | tf_op jit(solution)/shard_map/add | solution.py:42
  155.0 1.6 slice.190
  157.2 1.6 gather_fusion.8
  158.8 2.8 %fusion.17 = (f32[8,16,512]{2,1,0:T(8,128)S(1)}, f32[8,4,16,512]{3,2,1,0:T(8,128)S(1)}, f32[8,4,16,512]{3,2,1,0:T(8,128)S(1)}) fusion(f32[8,16,512]{2,1,0:T(8,128)S(1)} %copy-done.8, pred[8,4]{1,0:T(8,128)(4,1)S(1)} %copy.63, f32[8,16,512]{2,1,0:T(8,128)S(1)} %slice-done, f32[8,8,16,512]{3,2,1,0:T(8,128)} %bitcast.81, f32[8,4]{1,0:T(8,128)S(1)} %copy.54, ...), kind=kLoop, calls=%fused_computation.116 | loop fusion | flops 3604480 | bytes 7078048 | tf_op jit(solution)/shard_map/reduce_sum | solution.py:90
  163.4 9.1 %collective-permute-done.6 = f32[8,16,512]{2,1,0:T(8,128)S(1)} collective-permute-done((f32[8,16,512]{2,1,0:T(8,128)S(1)}, f32[8,16,512]{2,1,0:T(8,128)S(1)}, u32[]{:S(2)}, u32[]{:S(2)}) %collective-permute-start.6) | collective-permute-done | bytes 262176 | tf_op jit(solution)/shard_map/ppermute | solution.py:17
  173.4 1.7 collective-permute-start.7
  175.8 4.0 %collective-permute-done.7 = bf16[2,8,16,512]{3,2,1,0:T(8,128)(2,1)S(1)} collective-permute-done((bf16[2,8,16,512]{3,2,1,0:T(8,128)(2,1)S(1)}, bf16[2,8,16,512]{3,2,1,0:T(8,128)(2,1)S(1)}, u32[]{:S(2)}, u32[]{:S(2)}) %collective-permute-start.7) | collective-permute-done | bytes 262176 | tf_op jit(solution)/shard_map/ppermute | solution.py:17
  183.9 2.4 %fusion.1 = (f32[]{:T(128)}, f32[]{:T(128)}, f32[]{:T(128)}) fusion(f32[8,4,16,512]{3,2,1,0:T(8,128)S(1)} %get-tuple-element.20, f32[8,4,16,512]{3,2,1,0:T(8,128)S(1)} %bitcast.82, f32[8,16,512]{2,1,0:T(8,128)S(1)} %copy-done.7, pred[8,4]{1,0:T(8,128)(4,1)S(1)} %copy.63, f32[8,4,16,512]{3,2,1,0:T(8,128)} %bitcast.83, f32[8,16,512]{2,1,0:T(8,128)S(1)} %get-tuple-element.17), kind=kLoop, calls=%fused_computation.47 | loop fusion | flops 3145725 | bytes 3670060 | tf_op jit(solution)/shard_map/reduce_sum | solution.py:117
  186.4 31.9 %all-reduce = (f32[]{:T(128)}, f32[]{:T(128)}, f32[]{:T(128)}, f32[]{:T(128)}, f32[]{:T(128)}) all-reduce(f32[]{:T(128)} %get-tuple-element.8, f32[]{:T(128)} %get-tuple-element.7, f32[]{:T(128)} %get-tuple-element.6, f32[]{:T(128)} %get-tuple-element.5, ...), channel_id=1, replica_groups=mesh['groups'=2,'epoch'=4,'space'=2,'sub'=2] {'epoch','space','sub'}, use_global_device_ids=true, to_apply=%region_11.14 | all-reduce | flops 5 | bytes 40 | tf_op jit(solution)/shard_map/psum | solution.py:111
  (89 shorter events, 28.7 us)
Async XLA Ops:
  0.6 27.8 %collective-permute-start = (bf16[2,8,64,512]{3,2,1,0:T(8,128)(2,1)}, bf16[2,8,64,512]{3,2,1,0:T(8,128)(2,1)S(1)}, u32[]{:S(2)}, u32[]{:S(2)}) collective-permute-start(bf16[2,8,64,512]{3,2,1,0:T(8,128)(2,1)} %param.10), channel_id=1, source_target_pairs={{0,12},{4,0},{8,4},{12,8},{1,13},{5,1},{9,5},{13,9},{2,14},{6,2},{... | collective-permute-start | bytes 3145736 | tf_op jit(solution)/shard_map/ppermute | solution.py:17
  51.4 2.0 copy-start.1
  74.0 5.2 %copy-start.6 = (f32[8,64,512]{2,1,0:T(8,128)S(1)}, f32[8,64,512]{2,1,0:T(8,128)}, u32[]{:S(2)}) copy-start(f32[8,64,512]{2,1,0:T(8,128)} %get-tuple-element.44) | copy-start | bytes 3145732
  80.5 7.7 %copy-start.4 = (f32[8,64,512]{2,1,0:T(8,128)S(1)}, f32[8,64,512]{2,1,0:T(8,128)}, u32[]{:S(2)}) copy-start(f32[8,64,512]{2,1,0:T(8,128)} %get-tuple-element.33) | copy-start | bytes 3145732
  89.5 7.7 %copy-start.5 = (f32[8,64,512]{2,1,0:T(8,128)S(1)}, f32[8,64,512]{2,1,0:T(8,128)}, u32[]{:S(2)}) copy-start(f32[8,64,512]{2,1,0:T(8,128)} %get-tuple-element.31) | copy-start | bytes 3145732
  98.5 3.8 %copy-start.9 = (f32[8,16,512]{2,1,0:T(8,128)S(1)}, f32[8,16,512]{2,1,0:T(8,128)}, u32[]{:S(2)}) copy-start(f32[8,16,512]{2,1,0:T(8,128)} %reduce_sum.138) | copy-start | bytes 786436
  98.5 3.8 %copy-start.10 = (f32[8,16,512]{2,1,0:T(8,128)S(1)}, f32[8,16,512]{2,1,0:T(8,128)}, u32[]{:S(2)}) copy-start(f32[8,16,512]{2,1,0:T(8,128)} %reduce_sum.139) | copy-start | bytes 786436
  101.1 1.2 copy-start.11
  101.1 1.2 copy-start.12
  101.1 1.3 copy-start.13
  101.2 1.4 copy-start.2
  102.8 8.6 %copy-start.8 = (f32[8,16,512]{2,1,0:T(8,128)S(1)}, f32[8,16,512]{2,1,0:T(8,128)}, u32[]{:S(2)}) copy-start(f32[8,16,512]{2,1,0:T(8,128)} %param.13) | copy-start | bytes 786436
  102.8 12.8 %copy-start.14 = (s32[8,4]{0,1:T(4,128)S(1)}, s32[8,4]{0,1:T(4,128)}, u32[]{:S(2)}) copy-start(s32[8,4]{0,1:T(4,128)} %param.11) | copy-start | bytes 388
  102.8 12.9 %copy-start.15 = (f32[8,4]{0,1:T(4,128)S(1)}, f32[8,4]{0,1:T(4,128)}, u32[]{:S(2)}) copy-start(f32[8,4]{0,1:T(4,128)} %param.12) | copy-start | bytes 388
  103.0 14.1 %collective-permute-start.2 = (f32[80,3,512]{2,0,1:T(8,128)S(1)}, f32[80,3,512]{2,0,1:T(8,128)}, u32[]{:S(2)}, u32[]{:S(2)}) collective-permute-start(f32[80,3,512]{2,0,1:T(8,128)S(1)} %copy.56), channel_id=1, source_target_pairs={{2,0},{3,1},{6,4},{7,5},{10,8},{11,9},{14,12},{15,13},{18,16},{19,... | collective-permute-start | bytes 1474568 | tf_op jit(solution)/shard_map/ppermute | solution.py:28
  105.5 14.8 %collective-permute-start.1 = (f32[80,3,512]{2,0,1:T(8,128)}, f32[80,3,512]{2,0,1:T(8,128)}, u32[]{:S(2)}, u32[]{:S(2)}) collective-permute-start(f32[80,3,512]{2,0,1:T(8,128)} %copy.55), channel_id=1, source_target_pairs={{0,2},{1,3},{4,6},{5,7},{8,10},{9,11},{12,14},{13,15},{16,18},{17,... | collective-permute-start | bytes 1474568 | tf_op jit(solution)/shard_map/ppermute | solution.py:25
  111.4 21.9 %collective-permute-start.5 = (f32[8,16,512]{2,1,0:T(8,128)S(1)}, f32[8,16,512]{2,1,0:T(8,128)}, u32[]{:S(2)}, u32[]{:S(2)}) collective-permute-start(f32[8,16,512]{2,1,0:T(8,128)S(1)} %copy-done.8), channel_id=1, source_target_pairs={{0,12},{4,0},{8,4},{12,8},{1,13},{5,1},{9,5},{13,9},{2,14},{6,2},{... | collective-permute-start | bytes 786440 | tf_op jit(solution)/shard_map/ppermute | solution.py:17
  121.6 1.9 copy-start.3
  125.6 12.2 %collective-permute-start.4 = (f32[80,22,3]{0,1,2:T(8,128)}, f32[80,22,3]{0,1,2:T(8,128)}, u32[]{:S(2)}, u32[]{:S(2)}) collective-permute-start(f32[80,22,3]{0,1,2:T(8,128)} %copy.60), channel_id=1, source_target_pairs={{1,0},{3,2},{5,4},{7,6},{9,8},{11,10},{13,12},{15,14},{17,16},{19,... | collective-permute-start | bytes 63368 | tf_op jit(solution)/shard_map/ppermute | solution.py:28
  129.1 10.8 %collective-permute-start.3 = (f32[80,22,3]{0,1,2:T(8,128)}, f32[80,22,3]{0,1,2:T(8,128)}, u32[]{:S(2)}, u32[]{:S(2)}) collective-permute-start(f32[80,22,3]{0,1,2:T(8,128)} %copy.59), channel_id=1, source_target_pairs={{0,1},{2,3},{4,5},{6,7},{8,9},{10,11},{12,13},{14,15},{16,17},{18,... | collective-permute-start | bytes 63368 | tf_op jit(solution)/shard_map/ppermute | solution.py:25
  155.0 2.2 copy-start
  157.2 1.6 slice-start
  162.3 10.4 %copy-start.7 = (f32[8,16,512]{2,1,0:T(8,128)S(1)}, f32[8,16,512]{2,1,0:T(8,128)}, u32[]{:S(2)}) copy-start(f32[8,16,512]{2,1,0:T(8,128)} %param.14) | copy-start | bytes 786436
  163.0 9.5 %collective-permute-start.6 = (f32[8,16,512]{2,1,0:T(8,128)S(1)}, f32[8,16,512]{2,1,0:T(8,128)S(1)}, u32[]{:S(2)}, u32[]{:S(2)}) collective-permute-start(f32[8,16,512]{2,1,0:T(8,128)S(1)} %copy.69), channel_id=1, source_target_pairs={{0,4},{4,8},{8,12},{12,0},{1,5},{5,9},{9,13},{13,1},{2,6},{6,10},{... | collective-permute-start | bytes 786440 | tf_op jit(solution)/shard_map/ppermute | solution.py:17
  173.4 6.4 %collective-permute-start.7 = (bf16[2,8,16,512]{3,2,1,0:T(8,128)(2,1)S(1)}, bf16[2,8,16,512]{3,2,1,0:T(8,128)(2,1)S(1)}, u32[]{:S(2)}, u32[]{:S(2)}) collective-permute-start(bf16[2,8,16,512]{3,2,1,0:T(8,128)(2,1)S(1)} %pad_maximum_fusion.10), channel_id=1, source_target_pairs={{0,12},{4,0},{8,4},{12,8},{1,13},{5,1},{9,5},{13,9},{2,14},{6,2},{... | collective-permute-start | bytes 786440 | tf_op jit(solution)/shard_map/ppermute | solution.py:17
where the time goes:
time: 225 us; the launch traced here: 223 us
  local copies, waits for them, and re-layouts  63.5 us (28%)
  other arithmetic  60.6 us (27%)
  waiting for transfers between devices  36.6 us (16%)
  blocking collectives  31.9 us (14%)
  starting transfers between devices  24.3 us (11%)
  between operations  5.64 us (3%)
    ppermute x4, waiting for transfers between devices, passed_along(): return lax.ppermute(x, axis, [(i, (i + by) % size) for i in range(size)])  33.8 us
    psum x1, blocking collectives, on_device(): lax.psum((local_norm, local_crossed, jnp.sum(factor * grad_spread * grad_...  31.9 us
    reduce_sum x9, other arithmetic, looked_sum(): jnp.sum(field.reshape(shape[:-2] + (shape[-2] // LOOK, LOOK, shape[-1])),...  21.5 us
    reshape x8, local copies, waits for them, and re-layouts, looked_sum(): field.reshape(shape[:-2] + (shape[-2] // LOOK, LOOK, shape[-1]))  16.5 us
    gather x4, local copies, waits for them, and re-layouts, on_device(): mate_imag = jnp.take(ext_imag, partner[:, slot_index], axis=0)  12.8 us
    ppermute x4, starting transfers between devices, passed_along(): return lax.ppermute(x, axis, [(i, (i + by) % size) for i in range(size)])  11.4 us
    ppermute x2, starting transfers between devices, extended_2(): lax.ppermute(lax.slice_in_dim(block, block.shape[dim] - width, None, axis...  10.2 us
    sub x2, other arithmetic, on_device(): pieces.append(looked_sum(own_imag * mate_real - own_real * mate_imag))  9.68 us
  transfers between devices with their start and end apart: 8, of which 5 were waited for; matrix products, arithmetic and copies ran while one was open for 8% of the time, Pallas kernels for 0%

commit v1 on v0

--- a/solution.py
+++ b/solution.py
@@ -1,6 +1,10 @@
+import functools
+
 import jax
 import jax.numpy as jnp
 from jax import lax
+from jax.experimental import pallas as pl
+from jax.experimental.pallas import tpu as pltpu
 from jax.sharding import PartitionSpec as P
 
 SLOTS = 4
@@ -43,7 +47,7 @@
     return total
 
 
-def on_device(slc, offsets, weights, estimate, direction, prev_mean):
+def ring_plan(slc, offsets, weights, estimate, direction, prev_mean):
     epochs_here = slc.shape[1]
     look_rows = slc.shape[2] // LOOK
     col_count = slc.shape[3]
@@ -127,6 +131,425 @@
     return (estimate + step_size * new_direction, new_direction)
 
 
+LANES = 128
+SIDES = 2 * RADIUS
+HALO = 16
+PARAM_LANE = 96
+VMEM = pl.BlockSpec(memory_space=pltpu.VMEM)
+SMEM = pl.BlockSpec(memory_space=pltpu.SMEM)
+VMEM_BYTES = 48 * 1024 * 1024
+
+
+def split_two(value):
+    high = value.astype(jnp.bfloat16)
+    low = (value - high.astype(jnp.float32)).astype(jnp.bfloat16)
+    return high, low
+
+
+def pack_kernel(slc, estimate, direction, params, strips, edge, fields):
+    tiles = strips.shape[0]
+    epochs = slc.shape[1]
+    rows = slc.shape[2]
+    look_rows = estimate.shape[1]
+    lane = lax.broadcasted_iota(jnp.int32, (rows, LANES), 1)
+    value = params[...]
+    high = value.astype(jnp.bfloat16).astype(jnp.float32)
+    middle = (value - high).astype(jnp.bfloat16).astype(jnp.float32)
+    low = value - high - middle
+    third = PARAM_LANE + 2 * SLOTS
+    split = jnp.where(lane < third, high, jnp.where(lane < third + SLOTS, middle, low))
+    split = jnp.where(lane >= PARAM_LANE, split, 0.0)
+
+    def tile_of(part, epoch, tile):
+        return slc[part, epoch, :, tile * LANES : (tile + 1) * LANES].astype(jnp.float32)
+
+    def placed(total, source, start, target):
+        moved = pltpu.roll(source, (target - start) % LANES, axis=1)
+        inside = (lane >= target) & (lane < target + RADIUS)
+        return jnp.where(inside, moved, total)
+
+    for tile in range(tiles):
+        total = split
+        for part in range(2):
+            for epoch in range(epochs):
+                at = (part * epochs + epoch) * SIDES
+                if tile > 0:
+                    total = placed(total, tile_of(part, epoch, tile - 1), LANES - RADIUS, at)
+                if tile < tiles - 1:
+                    total = placed(total, tile_of(part, epoch, tile + 1), 0, at + RADIUS)
+        strips[tile] = total.astype(jnp.bfloat16)
+    total = jnp.zeros((rows, LANES), jnp.float32)
+    for part in range(2):
+        for epoch in range(epochs):
+            at = (part * epochs + epoch) * SIDES
+            total = placed(total, tile_of(part, epoch, tiles - 1), LANES - RADIUS, at)
+            total = placed(total, tile_of(part, epoch, 0), 0, at + RADIUS)
+    edge[...] = total.astype(jnp.bfloat16)
+    for tile in range(tiles):
+        columns = slice(tile * LANES, (tile + 1) * LANES)
+        for epoch in range(epochs):
+            here = slice(epoch * look_rows, (epoch + 1) * look_rows)
+            first, second = split_two(estimate[epoch, :, columns])
+            fields[tile, 0, here, :] = first
+            fields[tile, 1, here, :] = second
+            fields[tile, 2, here, :] = direction[epoch, :, columns].astype(jnp.bfloat16)
+
+
+def main_kernel(sizes, partner, weight, present, *refs):
+    tiles, epochs, rows = sizes
+    blocks = refs[:tiles]
+    strips = refs[tiles : 2 * tiles]
+    fields = refs[2 * tiles : 3 * tiles]
+    top, bottom, gradient, sums = refs[3 * tiles : 3 * tiles + 4]
+    full, rim_full, main, rim, looked, power, boxed, power_box, factors, est, old = refs[3 * tiles + 4 :]
+    look_rows = rows // LOOK
+    tall = (rows + 2 * HALO) // LOOK
+    halo_looks = HALO // LOOK
+    total = tiles * epochs
+    group = 2 * SLOTS
+    has_top = present[0]
+    has_bottom = present[1]
+    f32 = jnp.float32
+
+    band_from = lax.broadcasted_iota(jnp.int32, (2 * LANES, LANES), 0)
+    band_to = lax.broadcasted_iota(jnp.int32, (2 * LANES, LANES), 1)
+    rim_lane = band_from - LANES
+    side = rim_lane % SIDES
+    rim_column = jnp.where(side < RADIUS, side - RADIUS, LANES + side - RADIUS)
+    rim_column = jnp.where(rim_lane < LOOK * SIDES, rim_column, 4 * LANES)
+    column = jnp.where(band_from < LANES, band_from, rim_column)
+    band = (jnp.abs(column - band_to) <= RADIUS).astype(f32).astype(jnp.bfloat16)
+    out_at = lax.broadcasted_iota(jnp.int32, (group * look_rows, group * tall), 0)
+    in_at = lax.broadcasted_iota(jnp.int32, (group * look_rows, group * tall), 1)
+    near = jnp.abs(in_at % tall - halo_looks - out_at % look_rows) <= RADIUS
+    near = near & (in_at // tall == out_at // look_rows)
+    sum_rows = near.astype(f32).astype(jnp.bfloat16)
+
+    lane = lax.broadcasted_iota(jnp.int32, (tall, LANES), 1)
+    for block in range(tiles):
+        for part in range(2):
+
+            @pl.loop(0, epochs)
+            def _(epoch):
+                at = part * total + block * epochs + epoch
+                row = pl.multiple_of((part * epochs + epoch) * HALO, HALO)
+                full[at, :HALO] = top[block, pl.ds(row, HALO), :].astype(f32) * has_top
+                full[at, HALO : HALO + rows] = blocks[block][part, epoch].astype(f32)
+                full[at, HALO + rows :] = bottom[block, pl.ds(row, HALO), :].astype(f32) * has_bottom
+
+        last = slice(2 * epochs * HALO, 2 * epochs * HALO + HALO)
+        rim_full[block, :HALO] = top[block, last, :].astype(f32) * has_top
+        rim_full[block, HALO : HALO + rows] = strips[block][...].astype(f32)
+        rim_full[block, HALO + rows :] = bottom[block, last, :].astype(f32) * has_bottom
+
+        @pl.loop(0, epochs)
+        def _(epoch):
+            here = pl.ds(pl.multiple_of(epoch * look_rows, look_rows), look_rows)
+            est[block * epochs + epoch] = fields[block][0, here, :].astype(f32) + fields[block][1, here, :].astype(f32)
+            old[block * epochs + epoch] = fields[block][2, here, :].astype(f32)
+
+    @pl.loop(0, 2 * total)
+    def _(at):
+        for look in range(LOOK):
+            main[at, look] = full[at, pl.ds(look, tall, stride=LOOK), :]
+
+    for block in range(tiles):
+        by_look = [rim_full[block, pl.ds(look, tall, stride=LOOK), :] for look in range(LOOK)]
+        for part in range(2):
+            for epoch in range(epochs):
+                start = (part * epochs + epoch) * SIDES
+                value = jnp.zeros((tall, LANES), f32)
+                for look in range(LOOK):
+                    target = look * SIDES
+                    moved = pltpu.roll(by_look[look], (target - start) % LANES, axis=1)
+                    value = jnp.where((lane >= target) & (lane < target + SIDES), moved, value)
+                rim[part * total + block * epochs + epoch] = value
+
+    @pl.loop(0, total)
+    def _(epoch):
+        for piece in range(0, tall, 8):
+            rows_at = slice(piece, piece + 8)
+            own_re = [main[epoch, look, rows_at] for look in range(LOOK)]
+            own_im = [main[total + epoch, look, rows_at] for look in range(LOOK)]
+            rim_re = rim[epoch, rows_at]
+            rim_im = rim[total + epoch, rows_at]
+            value = own_re[0] * own_re[0] + own_im[0] * own_im[0]
+            for look in range(1, LOOK):
+                value = value + (own_re[look] * own_re[look] + own_im[look] * own_im[look])
+            at = pl.multiple_of(epoch * tall + piece, 8)
+            power[pl.ds(at, 8), :LANES] = value
+            power[pl.ds(at, 8), LANES:] = rim_re * rim_re + rim_im * rim_im
+            for slot in range(SLOTS):
+                mate = partner[epoch * SLOTS + slot]
+                real = None
+                for look in range(LOOK):
+                    mate_re = main[mate, look, rows_at]
+                    mate_im = main[total + mate, look, rows_at]
+                    one = own_re[look] * mate_re + own_im[look] * mate_im
+                    two = own_im[look] * mate_re - own_re[look] * mate_im
+                    real = one if real is None else real + one
+                    imag = two if look == 0 else imag + two
+                mate_re = rim[mate, rows_at]
+                mate_im = rim[total + mate, rows_at]
+                at = pl.multiple_of(epoch * (group * tall) + 2 * slot * tall + piece, 8)
+                looked[pl.ds(at, 8), :LANES] = real
+                looked[pl.ds(at, 8), LANES:] = rim_re * mate_re + rim_im * mate_im
+                at = pl.multiple_of(epoch * (group * tall) + (2 * slot + 1) * tall + piece, 8)
+                looked[pl.ds(at, 8), :LANES] = imag
+                looked[pl.ds(at, 8), LANES:] = rim_im * mate_re - rim_re * mate_im
+
+    def box(value):
+        high, low = split_two(value)
+        wide = jnp.dot(high, band, preferred_element_type=f32) + jnp.dot(low, band, preferred_element_type=f32)
+        high, low = split_two(wide)
+        return jnp.dot(sum_rows, high, preferred_element_type=f32) + jnp.dot(sum_rows, low, preferred_element_type=f32)
+
+    for block in range(total // group):
+        value = box(power[block * group * tall : (block + 1) * group * tall, :])
+        for at in range(group):
+            power_box[block * group + at] = value[at * look_rows : (at + 1) * look_rows]
+
+    @pl.loop(0, total // 4)
+    def _(quad):
+        for extra in range(4):
+            epoch = quad * 4 + extra
+            at = pl.multiple_of(epoch * (group * tall), group * tall)
+            boxed[epoch] = box(looked[pl.ds(at, group * tall), :])
+
+    grad = gradient
+    for block in range(tiles):
+        grad[block] = jnp.zeros(grad.shape[1:], f32)
+
+    def rows_of(epoch):
+        return epoch // epochs, pl.ds(pl.multiple_of((epoch % epochs) * look_rows, look_rows), look_rows)
+
+    @pl.loop(0, total)
+    def _(epoch):
+        own_power = power_box[epoch]
+        own_est = est[epoch]
+        own = jnp.zeros((look_rows, LANES), f32)
+        for slot in range(SLOTS):
+            mate = partner[epoch * SLOTS + slot]
+            coh_re = boxed[epoch, 2 * slot * look_rows : (2 * slot + 1) * look_rows, :]
+            coh_im = boxed[epoch, (2 * slot + 1) * look_rows : (2 * slot + 2) * look_rows, :]
+            inverse = lax.rsqrt(own_power * power_box[mate] + EPSILON)
+            unit_re = coh_re * inverse
+            unit_im = coh_im * inverse
+            factor = weight[epoch * SLOTS + slot] * (unit_re * unit_re + unit_im * unit_im)
+            factors[epoch * SLOTS + slot] = factor
+            weighted = factor * (unit_im - (own_est - est[mate]))
+            own = own + weighted
+            at, here = rows_of(mate)
+            grad[at, here, :] = grad[at, here, :] - weighted
+        at, here = rows_of(epoch)
+        grad[at, here, :] = grad[at, here, :] + own
+
+    def totals(epoch, carry):
+        norm, crossed, grad_term, mixed, old_term = carry
+        at, here = rows_of(epoch)
+        own_grad = grad[at, here, :]
+        own_old = old[epoch]
+        norm = norm + own_grad * own_grad
+        crossed = crossed + own_grad * own_old
+        for slot in range(SLOTS):
+            mate = partner[epoch * SLOTS + slot]
+            factor = factors[epoch * SLOTS + slot]
+            at, here = rows_of(mate)
+            grad_spread = own_grad - grad[at, here, :]
+            old_spread = own_old - old[mate]
+            pulled = factor * grad_spread
+            grad_term = grad_term + pulled * grad_spread
+            mixed = mixed + pulled * old_spread
+            old_term = old_term + factor * old_spread * old_spread
+        return norm, crossed, grad_term, mixed, old_term
+
+    zero = jnp.zeros((look_rows, LANES), f32)
+    results = lax.fori_loop(0, total, totals, (zero,) * 5)
+    sums[...] = jnp.zeros(sums.shape, f32)
+    for at, value in enumerate(results):
+        sums[at : at + 1, :] = jnp.sum(value, axis=0, keepdims=True)
+
+
+def update_kernel(cell_count, me, prev_mean, estimate, direction, *refs):
+    new_estimate, new_direction = refs[-2:]
+    tiles = estimate.shape[2] // LANES
+    pieces = refs[:tiles]
+    scalars = refs[tiles:-2]
+    epochs = estimate.shape[0]
+    look_rows = estimate.shape[1]
+    total = scalars[0][...]
+    for other in scalars[1:]:
+        total = total + other[...]
+    total = jnp.sum(total, axis=1, keepdims=True)
+    grad_norm, crossed, grad_term, mixed, old_term = (total[at : at + 1, :] for at in range(5))
+    momentum = grad_norm / cell_count / prev_mean[0]
+    curvature = grad_term + 2.0 * momentum * mixed + momentum * momentum * old_term
+    step = (grad_norm + momentum * crossed) / curvature
+    momentum = jnp.broadcast_to(momentum, (look_rows, LANES))
+    step = jnp.broadcast_to(step, (look_rows, LANES))
+    for shift, piece in enumerate(pieces):
+        tile = lax.rem(me[0] - shift + tiles, tiles)
+        columns = pl.ds(pl.multiple_of(tile * LANES, LANES), LANES)
+        for epoch in range(epochs):
+            gradient = piece[epoch * look_rows : (epoch + 1) * look_rows, :]
+            moved = gradient + momentum * direction[epoch, :, columns]
+            new_direction[epoch, :, columns] = moved
+            new_estimate[epoch, :, columns] = estimate[epoch, :, columns] + step * moved
+
+
+def swapped(up, down, axis):
+    size = lax.axis_size(axis)
+    if size == 1:
+        return jnp.zeros_like(up), jnp.zeros_like(down)
+    if size == 2:
+        first = lax.axis_index(axis) == 0
+        got = lax.ppermute(jnp.where(first, up, down), axis, [(0, 1), (1, 0)])
+        return got, got
+    forward = [(i, i + 1) for i in range(size - 1)]
+    backward = [(target, source) for source, target in forward]
+    return lax.ppermute(up, axis, forward), lax.ppermute(down, axis, backward)
+
+
+def to_ahead(x, axis, by):
+    size = lax.axis_size(axis)
+    return lax.ppermute(x, axis, [(i, (i + by) % size) for i in range(size)])
+
+
+def transposed_plan(slc, offsets, weights, estimate, direction, prev_mean):
+    f32 = jnp.float32
+    bf16 = jnp.bfloat16
+    tiles = lax.axis_size("epoch")
+    me = lax.axis_index("epoch")
+    epochs, rows, columns = slc.shape[1:]
+    look_rows = rows // LOOK
+    total = tiles * epochs
+    tall = (rows + 2 * HALO) // LOOK
+
+    def for_device(shift):
+        return lax.rem(me + shift, tiles)
+
+    def piece_for(shift):
+        return lax.dynamic_slice_in_dim(slc, for_device(shift) * LANES, LANES, axis=3)
+
+    blocks = [piece_for(0)]
+    order = sorted(range(1, tiles), key=lambda shift: min(shift, tiles - shift))
+    arrived = {}
+    for shift in order:
+        arrived[shift] = to_ahead(piece_for(tiles - shift), "epoch", tiles - shift)
+    blocks += [arrived[shift] for shift in range(1, tiles)]
+
+    params = jnp.zeros((rows, LANES), f32)
+    listed = jnp.concatenate([offsets.astype(f32), weights, weights, weights], axis=1)
+    params = lax.dynamic_update_slice(params, listed, (0, PARAM_LANE))
+    strips, edge, fields = pl.pallas_call(
+        pack_kernel,
+        out_shape=(
+            jax.ShapeDtypeStruct((tiles, rows, LANES), bf16),
+            jax.ShapeDtypeStruct((rows, LANES), bf16),
+            jax.ShapeDtypeStruct((tiles, 3, epochs * look_rows, LANES), bf16),
+        ),
+        in_specs=[VMEM] * 4,
+        out_specs=(VMEM,) * 3,
+        compiler_params=pltpu.CompilerParams(vmem_limit_bytes=VMEM_BYTES),
+        cost_estimate=pl.CostEstimate(flops=4_000_000, bytes_accessed=3_000_000, transcendentals=0),
+    )(slc, estimate, direction, params)
+
+    before, after = swapped(edge, edge, "sub")
+    sub = lax.axis_index("sub")
+    lane = lax.broadcasted_iota(jnp.int32, (rows, LANES), 1)
+    left_side = (lane < 2 * epochs * SIDES) & (lane % SIDES < RADIUS)
+    right_side = (lane < 2 * epochs * SIDES) & (lane % SIDES >= RADIUS)
+    nothing = jnp.zeros_like(edge)
+    left_edge = jnp.where(left_side & (sub > 0), before, nothing)
+    right_edge = jnp.where(right_side & (sub < lax.axis_size("sub") - 1), after, nothing)
+
+    def strip_for(shift):
+        target = for_device(shift)
+        value = lax.dynamic_index_in_dim(strips, target, axis=0, keepdims=False)
+        value = jnp.where(left_side & (target == 0), left_edge, value)
+        return jnp.where(right_side & (target == tiles - 1), right_edge, value)
+
+    def field_for(shift):
+        return lax.dynamic_index_in_dim(fields, for_device(shift), axis=0, keepdims=False)
+
+    strip_blocks = [strip_for(0)]
+    strip_blocks += [to_ahead(strip_for(tiles - shift), "epoch", tiles - shift) for shift in range(1, tiles)]
+    field_blocks = [field_for(0)]
+    field_blocks += [to_ahead(field_for(tiles - shift), "epoch", tiles - shift) for shift in range(1, tiles)]
+
+    def border(from_row):
+        parts = []
+        for block, strip in zip(blocks, strip_blocks):
+            main = lax.dynamic_slice_in_dim(block, from_row, HALO, axis=2).reshape(2 * epochs * HALO, LANES)
+            parts.append(jnp.concatenate([main, lax.dynamic_slice_in_dim(strip, from_row, HALO, axis=0)], axis=0))
+        return jnp.stack(parts)
+
+    space = lax.axis_index("space")
+    spaces = lax.axis_size("space")
+    if spaces == 2:
+        mine = border(jnp.where(space == 0, rows - HALO, 0))
+        top = bottom = lax.ppermute(mine, "space", [(0, 1), (1, 0)])
+    else:
+        top, bottom = swapped(border(rows - HALO), border(0), "space")
+    present = jnp.stack([space > 0, space < spaces - 1]).astype(f32)
+
+    listed = jnp.concatenate([strip[:epochs, PARAM_LANE : PARAM_LANE + 4 * SLOTS] for strip in strip_blocks], axis=0)
+    listed = listed.astype(f32)
+    partner = jnp.arange(total, dtype=jnp.int32)[:, None] + listed[:, :SLOTS].astype(jnp.int32)
+    partner = lax.rem(partner, total).reshape(-1)
+    weight = listed[:, SLOTS : 2 * SLOTS] + listed[:, 2 * SLOTS : 3 * SLOTS] + listed[:, 3 * SLOTS :]
+    group = 2 * SLOTS
+    gradient, sums = pl.pallas_call(
+        functools.partial(main_kernel, (tiles, epochs, rows)),
+        out_shape=(
+            jax.ShapeDtypeStruct((tiles, epochs * look_rows, LANES), f32),
+            jax.ShapeDtypeStruct((8, LANES), f32),
+        ),
+        in_specs=[SMEM] * 3 + [VMEM] * (3 * tiles + 2),
+        out_specs=(VMEM, VMEM),
+        scratch_shapes=[
+            pltpu.VMEM((2 * total, rows + 2 * HALO, LANES), f32),
+            pltpu.VMEM((tiles, rows + 2 * HALO, LANES), f32),
+            pltpu.VMEM((2 * total, LOOK, tall, LANES), f32),
+            pltpu.VMEM((2 * total, tall, LANES), f32),
+            pltpu.VMEM((total * group * tall, 2 * LANES), f32),
+            pltpu.VMEM((total * tall, 2 * LANES), f32),
+            pltpu.VMEM((total, group * look_rows, LANES), f32),
+            pltpu.VMEM((total, look_rows, LANES), f32),
+            pltpu.VMEM((total * SLOTS, look_rows, LANES), f32),
+            pltpu.VMEM((total, look_rows, LANES), f32),
+            pltpu.VMEM((total, look_rows, LANES), f32),
+        ],
+        compiler_params=pltpu.CompilerParams(vmem_limit_bytes=VMEM_BYTES),
+        cost_estimate=pl.CostEstimate(flops=40_000_000, bytes_accessed=4_000_000, transcendentals=0),
+    )(partner, weight.reshape(-1), present, *blocks, *strip_blocks, *field_blocks, top, bottom)
+
+    returned = [gradient[0]]
+    returned += [to_ahead(gradient[shift], "epoch", shift) for shift in range(1, tiles)]
+    place = ("space", "sub")
+    count = spaces * lax.axis_size("sub")
+    shared = [sums] + [lax.ppermute(sums, place, [(i, (i + by) % count) for i in range(count)]) for by in range(1, count)]
+    here = sum(shared[1:], shared[0])
+    scalars = [here] + [to_ahead(here, "epoch", by) for by in range(1, tiles)]
+    cell_count = float(total * look_rows * spaces * columns * lax.axis_size("sub"))
+    return pl.pallas_call(
+        functools.partial(update_kernel, cell_count),
+        out_shape=(jax.ShapeDtypeStruct(estimate.shape, f32),) * 2,
+        in_specs=[SMEM] * 2 + [VMEM] * (2 + 2 * tiles),
+        out_specs=(VMEM, VMEM),
+        compiler_params=pltpu.CompilerParams(vmem_limit_bytes=VMEM_BYTES),
+        cost_estimate=pl.CostEstimate(flops=1_000_000, bytes_accessed=2_000_000, transcendentals=0),
+    )(me.reshape(1), prev_mean, estimate, direction, *returned, *scalars)
+
+
+def on_device(slc, offsets, weights, estimate, direction, prev_mean):
+    epochs, rows, columns = slc.shape[1:]
+    fits = columns == LANES * lax.axis_size("epoch") and lax.axis_size("epoch") > 1
+    fits = fits and 2 * epochs * SIDES <= PARAM_LANE and rows % HALO == 0 and epochs * lax.axis_size("epoch") % (2 * SLOTS) == 0
+    plan = transposed_plan if fits else ring_plan
+    return plan(slc, offsets, weights, estimate, direction, prev_mean)
+
+
 def solution(mesh):
     return jax.shard_map(
         on_device,

time: 225 us -> 95.6 us (0.42)
  other arithmetic: 60.6 us -> 0.39 us
  local copies, waits for them, and re-layouts: 63.5 us -> 5.55 us
  blocking collectives: 31.9 us -> 0 us
  Pallas kernels: 0 us -> 21.1 us
  starting transfers between devices: 24.3 us -> 38.1 us
  waiting for transfers between devices: 36.6 us -> 28.7 us
  between operations: 5.64 us -> 1.48 us
    psum x1 -> x0, blocking collectives: 31.9 us -> none  [on_device(): lax.psum((local_norm, local_crossed, jnp.sum(factor * grad_spread * grad_...]
    reduce_sum x12 -> x0, other arithmetic: 27.4 us -> none  [the longest x9 21.5 us: looked_sum(): jnp.sum(field.reshape(shape[:-2] + (shape[-2] // LOOK, LOOK, shape[-1])),...]
    gather x12 -> x0, local copies, waits for them, and re-layouts: 25.7 us -> none  [the longest x4 12.8 us: on_device(): mate_imag = jnp.take(ext_imag, partner[:, slot_index], axis=0)]
    pallas_call x0 -> x3, Pallas kernels: none -> 21.1 us  [the longest x1 19.5 us: transposed_plan(): pl.pallas_call(functools.partial(main_kernel, (tiles, epochs, rows)), out...]
    reshape x8 -> x2, local copies, waits for them, and re-layouts: 16.5 us -> 0.21 us  [the longest x1 0.1 us: transposed_plan(): partner = lax.rem(partner, total).reshape(-1)]
    ppermute x8 -> x20, starting transfers between devices: 24.3 us -> 38.1 us  [the longest x15 34.3 us: to_ahead(): return lax.ppermute(x, axis, [(i, (i + by) % size) for i in range(size)])]
    sub x2 -> x0, other arithmetic: 9.68 us -> none  [on_device(): pieces.append(looked_sum(own_imag * mate_real - own_real * mate_imag))]
    concatenate x4 -> x1, other arithmetic: 9.61 us -> 0.08 us  [transposed_plan(): jnp.concatenate([offsets.astype(f32), weights, weights, weights], axis=1)]
  transfers between devices with their start and end apart: 8 -> 20, of which waited for: 5 -> 8; matrix products, arithmetic and copies ran while one was open for 8% -> 1% of each run, Pallas kernels for 0% -> 0%
where the time goes in v1:
time: 95.6 us; the launch traced here: 95.3 us
  starting transfers between devices  38.1 us (40%)
  waiting for transfers between devices  28.7 us (30%)
  Pallas kernels  21.1 us (22%)
  local copies, waits for them, and re-layouts  5.55 us (6%)
  between operations  1.48 us (2%)
    ppermute x15, starting transfers between devices, to_ahead(): return lax.ppermute(x, axis, [(i, (i + by) % size) for i in range(size)])  34.3 us
    ppermute x15, waiting for transfers between devices, to_ahead(): return lax.ppermute(x, axis, [(i, (i + by) % size) for i in range(size)])  24 us
    pallas_call x1, Pallas kernels, transposed_plan(): pl.pallas_call(functools.partial(main_kernel, (tiles, epochs, rows)), out...  19.5 us
    ppermute x1, waiting for transfers between devices, transposed_plan(): top = bottom = lax.ppermute(mine, 'space', [(0, 1), (1, 0)])  4.72 us
    unnamed x16, local copies, waits for them, and re-layouts  4.65 us
  transfers between devices with their start and end apart: 20, of which 8 were waited for; matrix products, arithmetic and copies ran while one was open for 1% of the time, Pallas kernels for 0%

profile of v1, /device:TPU:0, one launch (start us, length us, event | category | flops | bytes accessed | tf_op | source)
XLA Modules:
  0.0 95.3 jit_solution(15394919184256373305)
XLA Ops:
  0.6 0.8 copy.12
  1.4 0.7 copy-done.6
  2.1 0.1 copy.13
  2.1 0.1 select_maximum_fusion.params
  2.2 1.2 %copy-done = bf16[2,8,64,512]{3,2,1,0:T(8,128)(2,1)S(1)} copy-done((bf16[2,8,64,512]{3,2,1,0:T(8,128)(2,1)S(1)}, bf16[2,8,64,512]{3,2,1,0:T(8,128)(2,1)}, u32[]{:S(2)}) %copy-start) | copy-done | bytes 1048600
  3.5 0.9 copy-done.2
  4.4 0.9 copy-done.4
  5.4 0.6 shard_map.77
  6.0 0.5 collective-permute-start
  6.5 2.7 %collective-permute-start.9 = (bf16[3,128,128]{2,1,0:T(8,128)(2,1)S(1)}, bf16[3,128,128]{2,1,0:T(8,128)(2,1)S(1)}, u32[]{:S(2)}, u32[]{:S(2)}) collective-permute-start(bf16[3,128,128]{2,1,0:T(8,128)(2,1)S(1)} %get-tuple-element.16), channel_id=1, source_target_pairs={{0,4},{4,8},{8,12},{12,0},{1,5},{5,9},{9,13},{13,1},{2,6},{6,10},{... | collective-permute-start | bytes 294920 | tf_op jit(solution)/shard_map/ppermute | solution.py:415
  9.2 2.6 %collective-permute-start.8 = (bf16[3,128,128]{2,1,0:T(8,128)(2,1)S(1)}, bf16[3,128,128]{2,1,0:T(8,128)(2,1)S(1)}, u32[]{:S(2)}, u32[]{:S(2)}) collective-permute-start(bf16[3,128,128]{2,1,0:T(8,128)(2,1)S(1)} %get-tuple-element.17), channel_id=1, source_target_pairs={{0,8},{4,12},{8,0},{12,4},{1,9},{5,13},{9,1},{13,5},{2,10},{6,14},... | collective-permute-start | bytes 294920 | tf_op jit(solution)/shard_map/ppermute | solution.py:415
  11.8 0.2 constant_dynamic-slice_fusion.8
  12.0 0.1 collective-permute-start.6
  12.1 1.8 %collective-permute-start.5 = (bf16[2,8,64,128]{3,2,1,0:T(8,128)(2,1)S(1)}, bf16[2,8,64,128]{3,2,1,0:T(8,128)(2,1)S(1)}, u32[]{:S(2)}, u32[]{:S(2)}) collective-permute-start(bf16[2,8,64,128]{3,2,1,0:T(8,128)(2,1)S(1)} %get-tuple-element.13), channel_id=1, source_target_pairs={{0,8},{4,12},{8,0},{12,4},{1,9},{5,13},{9,1},{13,5},{2,10},{6,14},... | collective-permute-start | bytes 786440 | tf_op jit(solution)/shard_map/ppermute | solution.py:415
  14.0 0.1 constant_dynamic-slice_fusion.7
  14.1 0.1 add_convert_fusion.present
  14.2 2.5 %collective-permute-start.3 = (bf16[64,128]{1,0:T(8,128)(2,1)S(1)}, bf16[64,128]{1,0:T(8,128)(2,1)S(1)}, u32[]{:S(2)}, u32[]{:S(2)}) collective-permute-start(bf16[64,128]{1,0:T(8,128)(2,1)S(1)} %get-tuple-element.25), channel_id=1, source_target_pairs={{0,4},{4,8},{8,12},{12,0},{1,5},{5,9},{9,13},{13,1},{2,6},{6,10},{... | collective-permute-start | bytes 49160 | tf_op jit(solution)/shard_map/ppermute | solution.py:415
  16.8 0.1 slice.48
  16.9 11.6 %collective-permute-done.3.refs_7_ = bf16[64,128]{1,0:T(8,128)(2,1)S(1)} collective-permute-done((bf16[64,128]{1,0:T(8,128)(2,1)S(1)}, bf16[64,128]{1,0:T(8,128)(2,1)S(1)}, u32[]{:S(2)}, u32[]{:S(2)}) %collective-permute-start.3) | collective-permute-done | bytes 16416 | tf_op jit(solution)/shard_map/ppermute | solution.py:415
  28.4 8.4 %collective-permute-start.2 = (bf16[64,128]{1,0:T(8,128)(2,1)S(1)}, bf16[64,128]{1,0:T(8,128)(2,1)S(1)}, u32[]{:S(2)}, u32[]{:S(2)}) collective-permute-start(bf16[64,128]{1,0:T(8,128)(2,1)S(1)} %get-tuple-element.26), channel_id=1, source_target_pairs={{0,8},{4,12},{8,0},{12,4},{1,9},{5,13},{9,1},{13,5},{2,10},{6,14},... | collective-permute-start | bytes 49160 | tf_op jit(solution)/shard_map/ppermute | solution.py:415
  36.8 1.7 %collective-permute-done.2.refs_6_ = bf16[64,128]{1,0:T(8,128)(2,1)S(1)} collective-permute-done((bf16[64,128]{1,0:T(8,128)(2,1)S(1)}, bf16[64,128]{1,0:T(8,128)(2,1)S(1)}, u32[]{:S(2)}, u32[]{:S(2)}) %collective-permute-start.2) | collective-permute-done | bytes 16416 | tf_op jit(solution)/shard_map/ppermute | solution.py:415
  38.5 0.4 collective-permute-start.1
  39.0 0.1 slice.51
  39.0 0.1 slice.50
  39.1 3.2 %collective-permute-done.1.refs_5_ = bf16[64,128]{1,0:T(8,128)(2,1)S(1)} collective-permute-done((bf16[64,128]{1,0:T(8,128)(2,1)S(1)}, bf16[64,128]{1,0:T(8,128)(2,1)S(1)}, u32[]{:S(2)}, u32[]{:S(2)}) %collective-permute-start.1) | collective-permute-done | bytes 16416 | tf_op jit(solution)/shard_map/ppermute | solution.py:415
  42.3 2.2 %collective-permute-start.7 = (bf16[3,128,128]{2,1,0:T(8,128)(2,1)S(1)}, bf16[3,128,128]{2,1,0:T(8,128)(2,1)S(1)}, u32[]{:S(2)}, u32[]{:S(2)}) collective-permute-start(bf16[3,128,128]{2,1,0:T(8,128)(2,1)S(1)} %get-tuple-element.18), channel_id=1, source_target_pairs={{0,12},{4,0},{8,4},{12,8},{1,13},{5,1},{9,5},{13,9},{2,14},{6,2},{... | collective-permute-start | bytes 294920 | tf_op jit(solution)/shard_map/ppermute | solution.py:415
  44.5 0.1 slice.49
  44.6 2.5 %collective-permute-start.4 = (bf16[2,8,64,128]{3,2,1,0:T(8,128)(2,1)S(1)}, bf16[2,8,64,128]{3,2,1,0:T(8,128)(2,1)S(1)}, u32[]{:S(2)}, u32[]{:S(2)}) collective-permute-start(bf16[2,8,64,128]{3,2,1,0:T(8,128)(2,1)S(1)} %get-tuple-element.14), channel_id=1, source_target_pairs={{0,12},{4,0},{8,4},{12,8},{1,13},{5,1},{9,5},{13,9},{2,14},{6,2},{... | collective-permute-start | bytes 786440 | tf_op jit(solution)/shard_map/ppermute | solution.py:415
  47.1 0.0 collective-permute-done.5.refs_2_
  47.2 4.3 %collective-permute-done.4.refs_1_ = bf16[2,8,64,128]{3,2,1,0:T(8,128)(2,1)S(1)} collective-permute-done((bf16[2,8,64,128]{3,2,1,0:T(8,128)(2,1)S(1)}, bf16[2,8,64,128]{3,2,1,0:T(8,128)(2,1)S(1)}, u32[]{:S(2)}, u32[]{:S(2)}) %collective-permute-start.4) | collective-permute-done | bytes 262176 | tf_op jit(solution)/shard_map/ppermute | solution.py:415
  51.5 1.6 %collective-permute-start.10 = (bf16[4,272,128]{2,1,0:T(8,128)(2,1)S(1)}, bf16[4,272,128]{2,1,0:T(8,128)(2,1)S(1)}, u32[]{:S(2)}, u32[]{:S(2)}) collective-permute-start(bf16[4,272,128]{2,1,0:T(8,128)(2,1)S(1)} %pad_maximum_fusion), channel_id=1, source_target_pairs={{0,2},{2,0},{1,3},{3,1},{4,6},{6,4},{5,7},{7,5},{8,10},{10,8},{9,1... | collective-permute-start | bytes 835592 | tf_op jit(solution)/shard_map/ppermute | solution.py:491
  53.1 0.1 slice_add_fusion
  53.2 0.1 reshape.27.weight
  53.3 0.1 reshape.26.partner
  53.4 4.7 %collective-permute-done.10.refs_12_.refs_13_ = bf16[4,272,128]{2,1,0:T(8,128)(2,1)S(1)} collective-permute-done((bf16[4,272,128]{2,1,0:T(8,128)(2,1)S(1)}, bf16[4,272,128]{2,1,0:T(8,128)(2,1)S(1)}, u32[]{:S(2)}, u32[]{:S(2)}) %collective-permute-start.10) | collective-permute-done | bytes 278560 | tf_op jit(solution)/shard_map/ppermute | solution.py:491
  58.1 19.5 %shard_map.78 = (f32[4,128,128]{2,1,0:T(8,128)S(1)}, f32[8,128]{1,0:T(8,128)S(1)}) custom-call(s32[128]{0:T(128)S(1)} %reshape.26.partner, f32[128]{0:T(128)S(1)} %reshape.27.weight, f32[2]{0:T(128)S(1)} %add_convert_fusion.present, bf16[2,8,64,128]{3,2,1,0:T(8,128)(2,1)S(1)} %get-tuple-element.15.refs_0_, ...), custom_call_target="tpu_custom_call" | custom-call | flops 40000000 | bytes 4000000 | tf_op jit(solution)/shard_map/pallas_call | solution.py:502
  77.6 0.1 collective-permute-start.16
  77.7 1.6 %collective-permute-start.15 = (f32[8,128]{1,0:T(8,128)S(1)}, f32[8,128]{1,0:T(8,128)S(1)}, u32[]{:S(2)}, u32[]{:S(2)}) collective-permute-start(f32[8,128]{1,0:T(8,128)S(1)} %get-tuple-element.11), channel_id=1, source_target_pairs={{0,2},{1,3},{2,0},{3,1},{4,6},{5,7},{6,4},{7,5},{8,10},{9,11},{10,... | collective-permute-start | bytes 12296 | tf_op jit(solution)/shard_map/ppermute | solution.py:531
  79.3 0.2 collective-permute-start.14
  79.5 3.9 %collective-permute-start.13 = (f32[128,128]{1,0:T(8,128)S(1)}, f32[128,128]{1,0:T(8,128)S(1)}, u32[]{:S(2)}, u32[]{:S(2)}) collective-permute-start(f32[128,128]{1,0:T(8,128)S(1)} %get-tuple-element.20), channel_id=1, source_target_pairs={{0,12},{4,0},{8,4},{12,8},{1,13},{5,1},{9,5},{13,9},{2,14},{6,2},{... | collective-permute-start | bytes 196616 | tf_op jit(solution)/shard_map/ppermute | solution.py:415
  83.4 0.6 collective-permute-start.11
  84.0 3.2 %collective-permute-start.19 = (f32[8,128]{1,0:T(8,128)S(1)}, f32[8,128]{1,0:T(8,128)S(1)}, u32[]{:S(2)}, u32[]{:S(2)}) collective-permute-start(f32[8,128]{1,0:T(8,128)S(1)} %add_add_fusion.refs_4_), channel_id=1, source_target_pairs={{0,12},{4,0},{8,4},{12,8},{1,13},{5,1},{9,5},{13,9},{2,14},{6,2},{... | collective-permute-start | bytes 12296 | tf_op jit(solution)/shard_map/ppermute | solution.py:415
  87.3 1.1 %collective-permute-start.18 = (f32[8,128]{1,0:T(8,128)S(1)}, f32[8,128]{1,0:T(8,128)S(1)}, u32[]{:S(2)}, u32[]{:S(2)}) collective-permute-start(f32[8,128]{1,0:T(8,128)S(1)} %add_add_fusion.refs_4_), channel_id=1, source_target_pairs={{0,8},{4,12},{8,0},{12,4},{1,9},{5,13},{9,1},{13,5},{2,10},{6,14},... | collective-permute-start | bytes 12296 | tf_op jit(solution)/shard_map/ppermute | solution.py:415
  88.4 0.5 collective-permute-done.19.refs_7_
  88.9 2.1 %collective-permute-start.17 = (f32[8,128]{1,0:T(8,128)S(1)}, f32[8,128]{1,0:T(8,128)S(1)}, u32[]{:S(2)}, u32[]{:S(2)}) collective-permute-start(f32[8,128]{1,0:T(8,128)S(1)} %add_add_fusion.refs_4_), channel_id=1, source_target_pairs={{0,4},{4,8},{8,12},{12,0},{1,5},{5,9},{9,13},{13,1},{2,6},{6,10},{... | collective-permute-start | bytes 12296 | tf_op jit(solution)/shard_map/ppermute | solution.py:415
  91.7 0.1 collective-permute-done.18.refs_6_
  91.8 2.6 %collective-permute-done.17.refs_5_ = f32[8,128]{1,0:T(8,128)S(1)} collective-permute-done((f32[8,128]{1,0:T(8,128)S(1)}, f32[8,128]{1,0:T(8,128)S(1)}, u32[]{:S(2)}, u32[]{:S(2)}) %collective-permute-start.17) | collective-permute-done | bytes 4128 | tf_op jit(solution)/shard_map/ppermute | solution.py:415
  94.4 0.9 shard_map.79
  (43 shorter events, 0.3 us)
Async XLA Ops:
  1.4 0.7 copy-start.6
  2.2 1.2 %copy-start = (bf16[2,8,64,512]{3,2,1,0:T(8,128)(2,1)S(1)}, bf16[2,8,64,512]{3,2,1,0:T(8,128)(2,1)}, u32[]{:S(2)}) copy-start(bf16[2,8,64,512]{3,2,1,0:T(8,128)(2,1)} %slc.1) | copy-start | bytes 3145732
  3.5 0.9 copy-start.2
  4.4 0.9 copy-start.4
  5.4 6.4 %copy-start.1 = (bf16[2,8,64,512]{3,2,1,0:T(8,128)(2,1)S(1)}, bf16[2,8,64,512]{3,2,1,0:T(8,128)(2,1)}, u32[]{:S(2)}) copy-start(bf16[2,8,64,512]{3,2,1,0:T(8,128)(2,1)} %slc.1) | copy-start | bytes 3145732
  6.0 8.2 %collective-permute-start = (bf16[64,128]{1,0:T(8,128)(2,1)S(1)}, bf16[64,128]{1,0:T(8,128)(2,1)S(1)}, u32[]{:S(2)}, u32[]{:S(2)}) collective-permute-start(bf16[64,128]{1,0:T(8,128)(2,1)S(1)} %get-tuple-element.7), channel_id=1, source_target_pairs={{0,1},{1,0},{2,3},{3,2},{4,5},{5,4},{6,7},{7,6},{8,9},{9,8},{10,11... | collective-permute-start | bytes 49160 | tf_op jit(solution)/shard_map/ppermute | solution.py:406
  6.5 46.8 %collective-permute-start.9 = (bf16[3,128,128]{2,1,0:T(8,128)(2,1)S(1)}, bf16[3,128,128]{2,1,0:T(8,128)(2,1)S(1)}, u32[]{:S(2)}, u32[]{:S(2)}) collective-permute-start(bf16[3,128,128]{2,1,0:T(8,128)(2,1)S(1)} %get-tuple-element.16), channel_id=1, source_target_pairs={{0,4},{4,8},{8,12},{12,0},{1,5},{5,9},{9,13},{13,1},{2,6},{6,10},{... | collective-permute-start | bytes 294920 | tf_op jit(solution)/shard_map/ppermute | solution.py:415
  9.2 44.2 %collective-permute-start.8 = (bf16[3,128,128]{2,1,0:T(8,128)(2,1)S(1)}, bf16[3,128,128]{2,1,0:T(8,128)(2,1)S(1)}, u32[]{:S(2)}, u32[]{:S(2)}) collective-permute-start(bf16[3,128,128]{2,1,0:T(8,128)(2,1)S(1)} %get-tuple-element.17), channel_id=1, source_target_pairs={{0,8},{4,12},{8,0},{12,4},{1,9},{5,13},{9,1},{13,5},{2,10},{6,14},... | collective-permute-start | bytes 294920 | tf_op jit(solution)/shard_map/ppermute | solution.py:415
  12.0 32.6 %collective-permute-start.6 = (bf16[2,8,64,128]{3,2,1,0:T(8,128)(2,1)S(1)}, bf16[2,8,64,128]{3,2,1,0:T(8,128)(2,1)S(1)}, u32[]{:S(2)}, u32[]{:S(2)}) collective-permute-start(bf16[2,8,64,128]{3,2,1,0:T(8,128)(2,1)S(1)} %get-tuple-element.12), channel_id=1, source_target_pairs={{0,4},{4,8},{8,12},{12,0},{1,5},{5,9},{9,13},{13,1},{2,6},{6,10},{... | collective-permute-start | bytes 786440 | tf_op jit(solution)/shard_map/ppermute | solution.py:415
  12.1 35.0 %collective-permute-start.5 = (bf16[2,8,64,128]{3,2,1,0:T(8,128)(2,1)S(1)}, bf16[2,8,64,128]{3,2,1,0:T(8,128)(2,1)S(1)}, u32[]{:S(2)}, u32[]{:S(2)}) collective-permute-start(bf16[2,8,64,128]{3,2,1,0:T(8,128)(2,1)S(1)} %get-tuple-element.13), channel_id=1, source_target_pairs={{0,8},{4,12},{8,0},{12,4},{1,9},{5,13},{9,1},{13,5},{2,10},{6,14},... | collective-permute-start | bytes 786440 | tf_op jit(solution)/shard_map/ppermute | solution.py:415
  14.2 14.2 %collective-permute-start.3 = (bf16[64,128]{1,0:T(8,128)(2,1)S(1)}, bf16[64,128]{1,0:T(8,128)(2,1)S(1)}, u32[]{:S(2)}, u32[]{:S(2)}) collective-permute-start(bf16[64,128]{1,0:T(8,128)(2,1)S(1)} %get-tuple-element.25), channel_id=1, source_target_pairs={{0,4},{4,8},{8,12},{12,0},{1,5},{5,9},{9,13},{13,1},{2,6},{6,10},{... | collective-permute-start | bytes 49160 | tf_op jit(solution)/shard_map/ppermute | solution.py:415
  28.4 10.1 %collective-permute-start.2 = (bf16[64,128]{1,0:T(8,128)(2,1)S(1)}, bf16[64,128]{1,0:T(8,128)(2,1)S(1)}, u32[]{:S(2)}, u32[]{:S(2)}) collective-permute-start(bf16[64,128]{1,0:T(8,128)(2,1)S(1)} %get-tuple-element.26), channel_id=1, source_target_pairs={{0,8},{4,12},{8,0},{12,4},{1,9},{5,13},{9,1},{13,5},{2,10},{6,14},... | collective-permute-start | bytes 49160 | tf_op jit(solution)/shard_map/ppermute | solution.py:415
  38.5 3.8 %collective-permute-start.1 = (bf16[64,128]{1,0:T(8,128)(2,1)S(1)}, bf16[64,128]{1,0:T(8,128)(2,1)S(1)}, u32[]{:S(2)}, u32[]{:S(2)}) collective-permute-start(bf16[64,128]{1,0:T(8,128)(2,1)S(1)} %and_select_fusion.5), channel_id=1, source_target_pairs={{0,12},{4,0},{8,4},{12,8},{1,13},{5,1},{9,5},{13,9},{2,14},{6,2},{... | collective-permute-start | bytes 49160 | tf_op jit(solution)/shard_map/ppermute | solution.py:415
  42.3 11.1 %collective-permute-start.7 = (bf16[3,128,128]{2,1,0:T(8,128)(2,1)S(1)}, bf16[3,128,128]{2,1,0:T(8,128)(2,1)S(1)}, u32[]{:S(2)}, u32[]{:S(2)}) collective-permute-start(bf16[3,128,128]{2,1,0:T(8,128)(2,1)S(1)} %get-tuple-element.18), channel_id=1, source_target_pairs={{0,12},{4,0},{8,4},{12,8},{1,13},{5,1},{9,5},{13,9},{2,14},{6,2},{... | collective-permute-start | bytes 294920 | tf_op jit(solution)/shard_map/ppermute | solution.py:415
  44.6 6.8 %collective-permute-start.4 = (bf16[2,8,64,128]{3,2,1,0:T(8,128)(2,1)S(1)}, bf16[2,8,64,128]{3,2,1,0:T(8,128)(2,1)S(1)}, u32[]{:S(2)}, u32[]{:S(2)}) collective-permute-start(bf16[2,8,64,128]{3,2,1,0:T(8,128)(2,1)S(1)} %get-tuple-element.14), channel_id=1, source_target_pairs={{0,12},{4,0},{8,4},{12,8},{1,13},{5,1},{9,5},{13,9},{2,14},{6,2},{... | collective-permute-start | bytes 786440 | tf_op jit(solution)/shard_map/ppermute | solution.py:415
  51.5 6.6 %collective-permute-start.10 = (bf16[4,272,128]{2,1,0:T(8,128)(2,1)S(1)}, bf16[4,272,128]{2,1,0:T(8,128)(2,1)S(1)}, u32[]{:S(2)}, u32[]{:S(2)}) collective-permute-start(bf16[4,272,128]{2,1,0:T(8,128)(2,1)S(1)} %pad_maximum_fusion), channel_id=1, source_target_pairs={{0,2},{2,0},{1,3},{3,1},{4,6},{6,4},{5,7},{7,5},{8,10},{10,8},{9,1... | collective-permute-start | bytes 835592 | tf_op jit(solution)/shard_map/ppermute | solution.py:491
  77.6 5.7 %collective-permute-start.16 = (f32[8,128]{1,0:T(8,128)S(1)}, f32[8,128]{1,0:T(8,128)S(1)}, u32[]{:S(2)}, u32[]{:S(2)}) collective-permute-start(f32[8,128]{1,0:T(8,128)S(1)} %get-tuple-element.11), channel_id=1, source_target_pairs={{0,3},{1,0},{2,1},{3,2},{4,7},{5,4},{6,5},{7,6},{8,11},{9,8},{10,9... | collective-permute-start | bytes 12296 | tf_op jit(solution)/shard_map/ppermute | solution.py:531
  77.7 6.3 %collective-permute-start.15 = (f32[8,128]{1,0:T(8,128)S(1)}, f32[8,128]{1,0:T(8,128)S(1)}, u32[]{:S(2)}, u32[]{:S(2)}) collective-permute-start(f32[8,128]{1,0:T(8,128)S(1)} %get-tuple-element.11), channel_id=1, source_target_pairs={{0,2},{1,3},{2,0},{3,1},{4,6},{5,7},{6,4},{7,5},{8,10},{9,11},{10,... | collective-permute-start | bytes 12296 | tf_op jit(solution)/shard_map/ppermute | solution.py:531
  79.3 4.8 %collective-permute-start.14 = (f32[8,128]{1,0:T(8,128)S(1)}, f32[8,128]{1,0:T(8,128)S(1)}, u32[]{:S(2)}, u32[]{:S(2)}) collective-permute-start(f32[8,128]{1,0:T(8,128)S(1)} %get-tuple-element.11), channel_id=1, source_target_pairs={{0,1},{1,2},{2,3},{3,0},{4,5},{5,6},{6,7},{7,4},{8,9},{9,10},{10,1... | collective-permute-start | bytes 12296 | tf_op jit(solution)/shard_map/ppermute | solution.py:531
  79.4 14.9 %copy-start.3 = (f32[8,16,512]{2,1,0:T(8,128)S(1)}, f32[8,16,512]{2,1,0:T(8,128)}, u32[]{:S(2)}) copy-start(f32[8,16,512]{2,1,0:T(8,128)} %estimate.3) | copy-start | bytes 786436
  79.4 14.9 %copy-start.5 = (f32[8,16,512]{2,1,0:T(8,128)S(1)}, f32[8,16,512]{2,1,0:T(8,128)}, u32[]{:S(2)}) copy-start(f32[8,16,512]{2,1,0:T(8,128)} %direction.3) | copy-start | bytes 786436
  79.5 14.9 %collective-permute-start.13 = (f32[128,128]{1,0:T(8,128)S(1)}, f32[128,128]{1,0:T(8,128)S(1)}, u32[]{:S(2)}, u32[]{:S(2)}) collective-permute-start(f32[128,128]{1,0:T(8,128)S(1)} %get-tuple-element.20), channel_id=1, source_target_pairs={{0,12},{4,0},{8,4},{12,8},{1,13},{5,1},{9,5},{13,9},{2,14},{6,2},{... | collective-permute-start | bytes 196616 | tf_op jit(solution)/shard_map/ppermute | solution.py:415
  83.4 11.0 %collective-permute-start.12 = (f32[128,128]{1,0:T(8,128)S(1)}, f32[128,128]{1,0:T(8,128)S(1)}, u32[]{:S(2)}, u32[]{:S(2)}) collective-permute-start(f32[128,128]{1,0:T(8,128)S(1)} %get-tuple-element.21), channel_id=1, source_target_pairs={{0,8},{4,12},{8,0},{12,4},{1,9},{5,13},{9,1},{13,5},{2,10},{6,14},... | collective-permute-start | bytes 196616 | tf_op jit(solution)/shard_map/ppermute | solution.py:415
  83.4 11.0 %collective-permute-start.11 = (f32[128,128]{1,0:T(8,128)S(1)}, f32[128,128]{1,0:T(8,128)S(1)}, u32[]{:S(2)}, u32[]{:S(2)}) collective-permute-start(f32[128,128]{1,0:T(8,128)S(1)} %get-tuple-element.22), channel_id=1, source_target_pairs={{0,4},{4,8},{8,12},{12,0},{1,5},{5,9},{9,13},{13,1},{2,6},{6,10},{... | collective-permute-start | bytes 196616 | tf_op jit(solution)/shard_map/ppermute | solution.py:415
  84.0 4.9 %collective-permute-start.19 = (f32[8,128]{1,0:T(8,128)S(1)}, f32[8,128]{1,0:T(8,128)S(1)}, u32[]{:S(2)}, u32[]{:S(2)}) collective-permute-start(f32[8,128]{1,0:T(8,128)S(1)} %add_add_fusion.refs_4_), channel_id=1, source_target_pairs={{0,12},{4,0},{8,4},{12,8},{1,13},{5,1},{9,5},{13,9},{2,14},{6,2},{... | collective-permute-start | bytes 12296 | tf_op jit(solution)/shard_map/ppermute | solution.py:415
  87.3 4.5 %collective-permute-start.18 = (f32[8,128]{1,0:T(8,128)S(1)}, f32[8,128]{1,0:T(8,128)S(1)}, u32[]{:S(2)}, u32[]{:S(2)}) collective-permute-start(f32[8,128]{1,0:T(8,128)S(1)} %add_add_fusion.refs_4_), channel_id=1, source_target_pairs={{0,8},{4,12},{8,0},{12,4},{1,9},{5,13},{9,1},{13,5},{2,10},{6,14},... | collective-permute-start | bytes 12296 | tf_op jit(solution)/shard_map/ppermute | solution.py:415
  88.9 5.4 %collective-permute-start.17 = (f32[8,128]{1,0:T(8,128)S(1)}, f32[8,128]{1,0:T(8,128)S(1)}, u32[]{:S(2)}, u32[]{:S(2)}) collective-permute-start(f32[8,128]{1,0:T(8,128)S(1)} %add_add_fusion.refs_4_), channel_id=1, source_target_pairs={{0,4},{4,8},{8,12},{12,0},{1,5},{5,9},{9,13},{13,1},{2,6},{6,10},{... | collective-permute-start | bytes 12296 | tf_op jit(solution)/shard_map/ppermute | solution.py:415

commit v2 on v1

--- a/solution.py
+++ b/solution.py
@@ -146,44 +146,18 @@
     return high, low
 
 
-def pack_kernel(slc, estimate, direction, params, strips, edge, fields):
-    tiles = strips.shape[0]
+def edge_kernel(slc, estimate, direction, edge, fields):
+    tiles = fields.shape[0]
     epochs = slc.shape[1]
     rows = slc.shape[2]
     look_rows = estimate.shape[1]
     lane = lax.broadcasted_iota(jnp.int32, (rows, LANES), 1)
-    value = params[...]
-    high = value.astype(jnp.bfloat16).astype(jnp.float32)
-    middle = (value - high).astype(jnp.bfloat16).astype(jnp.float32)
-    low = value - high - middle
-    third = PARAM_LANE + 2 * SLOTS
-    split = jnp.where(lane < third, high, jnp.where(lane < third + SLOTS, middle, low))
-    split = jnp.where(lane >= PARAM_LANE, split, 0.0)
-
-    def tile_of(part, epoch, tile):
-        return slc[part, epoch, :, tile * LANES : (tile + 1) * LANES].astype(jnp.float32)
-
-    def placed(total, source, start, target):
-        moved = pltpu.roll(source, (target - start) % LANES, axis=1)
-        inside = (lane >= target) & (lane < target + RADIUS)
-        return jnp.where(inside, moved, total)
-
-    for tile in range(tiles):
-        total = split
-        for part in range(2):
-            for epoch in range(epochs):
-                at = (part * epochs + epoch) * SIDES
-                if tile > 0:
-                    total = placed(total, tile_of(part, epoch, tile - 1), LANES - RADIUS, at)
-                if tile < tiles - 1:
-                    total = placed(total, tile_of(part, epoch, tile + 1), 0, at + RADIUS)
-        strips[tile] = total.astype(jnp.bfloat16)
     total = jnp.zeros((rows, LANES), jnp.float32)
     for part in range(2):
         for epoch in range(epochs):
             at = (part * epochs + epoch) * SIDES
-            total = placed(total, tile_of(part, epoch, tiles - 1), LANES - RADIUS, at)
-            total = placed(total, tile_of(part, epoch, 0), 0, at + RADIUS)
+            total = placed(lane, total, tile_of(slc, part, epoch, tiles - 1), LANES - RADIUS, at)
+            total = placed(lane, total, tile_of(slc, part, epoch, 0), 0, at + RADIUS)
     edge[...] = total.astype(jnp.bfloat16)
     for tile in range(tiles):
         columns = slice(tile * LANES, (tile + 1) * LANES)
@@ -195,13 +169,50 @@
             fields[tile, 2, here, :] = direction[epoch, :, columns].astype(jnp.bfloat16)
 
 
+def tile_of(slc, part, epoch, tile):
+    return slc[part, epoch, :, tile * LANES : (tile + 1) * LANES].astype(jnp.float32)
+
+
+def placed(lane, total, source, start, target):
+    moved = pltpu.roll(source, (target - start) % LANES, axis=1)
+    return jnp.where((lane >= target) & (lane < target + RADIUS), moved, total)
+
+
+def pack_kernel(slc, params, left, right, message):
+    tiles = message.shape[0]
+    epochs = slc.shape[1]
+    rows = slc.shape[2]
+    lane = lax.broadcasted_iota(jnp.int32, (rows, LANES), 1)
+    value = params[...]
+    high = value.astype(jnp.bfloat16).astype(jnp.float32)
+    middle = (value - high).astype(jnp.bfloat16).astype(jnp.float32)
+    low = value - high - middle
+    third = PARAM_LANE + 2 * SLOTS
+    split = jnp.where(lane < third, high, jnp.where(lane < third + SLOTS, middle, low))
+    split = jnp.where(lane >= PARAM_LANE, split, 0.0)
+    for tile in range(tiles):
+        total = split
+        if tile == 0:
+            total = total + left[...].astype(jnp.float32)
+        if tile == tiles - 1:
+            total = total + right[...].astype(jnp.float32)
+        for part in range(2):
+            for epoch in range(epochs):
+                block = part * epochs + epoch
+                at = block * SIDES
+                if tile > 0:
+                    total = placed(lane, total, tile_of(slc, part, epoch, tile - 1), LANES - RADIUS, at)
+                if tile < tiles - 1:
+                    total = placed(lane, total, tile_of(slc, part, epoch, tile + 1), 0, at + RADIUS)
+                own = slc[part, epoch, :, tile * LANES : (tile + 1) * LANES]
+                message[tile, block * rows : (block + 1) * rows, :] = own
+        message[tile, 2 * epochs * rows :, :] = total.astype(jnp.bfloat16)
+
+
 def main_kernel(sizes, partner, weight, present, *refs):
     tiles, epochs, rows = sizes
-    blocks = refs[:tiles]
-    strips = refs[tiles : 2 * tiles]
-    fields = refs[2 * tiles : 3 * tiles]
-    top, bottom, gradient, sums = refs[3 * tiles : 3 * tiles + 4]
-    full, rim_full, main, rim, looked, power, boxed, power_box, factors, est, old = refs[3 * tiles + 4 :]
+    message, fields, top, bottom, gradient, sums = refs[:6]
+    full, rim_full, main, rim, looked, power, boxed, power_box, factors, est, old = refs[6:]
     look_rows = rows // LOOK
     tall = (rows + 2 * HALO) // LOOK
     halo_looks = HALO // LOOK
@@ -234,19 +245,20 @@
                 at = part * total + block * epochs + epoch
                 row = pl.multiple_of((part * epochs + epoch) * HALO, HALO)
                 full[at, :HALO] = top[block, pl.ds(row, HALO), :].astype(f32) * has_top
-                full[at, HALO : HALO + rows] = blocks[block][part, epoch].astype(f32)
+                own = pl.ds(pl.multiple_of((part * epochs + epoch) * rows, rows), rows)
+                full[at, HALO : HALO + rows] = message[block, own, :].astype(f32)
                 full[at, HALO + rows :] = bottom[block, pl.ds(row, HALO), :].astype(f32) * has_bottom
 
         last = slice(2 * epochs * HALO, 2 * epochs * HALO + HALO)
         rim_full[block, :HALO] = top[block, last, :].astype(f32) * has_top
-        rim_full[block, HALO : HALO + rows] = strips[block][...].astype(f32)
+        rim_full[block, HALO : HALO + rows] = message[block, 2 * epochs * rows :, :].astype(f32)
         rim_full[block, HALO + rows :] = bottom[block, last, :].astype(f32) * has_bottom
 
         @pl.loop(0, epochs)
         def _(epoch):
             here = pl.ds(pl.multiple_of(epoch * look_rows, look_rows), look_rows)
-            est[block * epochs + epoch] = fields[block][0, here, :].astype(f32) + fields[block][1, here, :].astype(f32)
-            old[block * epochs + epoch] = fields[block][2, here, :].astype(f32)
+            est[block * epochs + epoch] = fields[block, 0, here, :].astype(f32) + fields[block, 1, here, :].astype(f32)
+            old[block * epochs + epoch] = fields[block, 2, here, :].astype(f32)
 
     @pl.loop(0, 2 * total)
     def _(at):
@@ -370,11 +382,10 @@
         sums[at : at + 1, :] = jnp.sum(value, axis=0, keepdims=True)
 
 
-def update_kernel(cell_count, me, prev_mean, estimate, direction, *refs):
+def update_kernel(cell_count, prev_mean, estimate, direction, pieces, *refs):
     new_estimate, new_direction = refs[-2:]
     tiles = estimate.shape[2] // LANES
-    pieces = refs[:tiles]
-    scalars = refs[tiles:-2]
+    scalars = refs[:-2]
     epochs = estimate.shape[0]
     look_rows = estimate.shape[1]
     total = scalars[0][...]
@@ -387,11 +398,10 @@
     step = (grad_norm + momentum * crossed) / curvature
     momentum = jnp.broadcast_to(momentum, (look_rows, LANES))
     step = jnp.broadcast_to(step, (look_rows, LANES))
-    for shift, piece in enumerate(pieces):
-        tile = lax.rem(me[0] - shift + tiles, tiles)
-        columns = pl.ds(pl.multiple_of(tile * LANES, LANES), LANES)
+    for tile in range(tiles):
+        columns = slice(tile * LANES, (tile + 1) * LANES)
         for epoch in range(epochs):
-            gradient = piece[epoch * look_rows : (epoch + 1) * look_rows, :]
+            gradient = pieces[tile, epoch * look_rows : (epoch + 1) * look_rows, :]
             moved = gradient + momentum * direction[epoch, :, columns]
             new_direction[epoch, :, columns] = moved
             new_estimate[epoch, :, columns] = estimate[epoch, :, columns] + step * moved
@@ -419,70 +429,49 @@
     f32 = jnp.float32
     bf16 = jnp.bfloat16
     tiles = lax.axis_size("epoch")
-    me = lax.axis_index("epoch")
     epochs, rows, columns = slc.shape[1:]
     look_rows = rows // LOOK
     total = tiles * epochs
     tall = (rows + 2 * HALO) // LOOK
 
-    def for_device(shift):
-        return lax.rem(me + shift, tiles)
-
-    def piece_for(shift):
-        return lax.dynamic_slice_in_dim(slc, for_device(shift) * LANES, LANES, axis=3)
-
-    blocks = [piece_for(0)]
-    order = sorted(range(1, tiles), key=lambda shift: min(shift, tiles - shift))
-    arrived = {}
-    for shift in order:
-        arrived[shift] = to_ahead(piece_for(tiles - shift), "epoch", tiles - shift)
-    blocks += [arrived[shift] for shift in range(1, tiles)]
-
     params = jnp.zeros((rows, LANES), f32)
     listed = jnp.concatenate([offsets.astype(f32), weights, weights, weights], axis=1)
     params = lax.dynamic_update_slice(params, listed, (0, PARAM_LANE))
-    strips, edge, fields = pl.pallas_call(
-        pack_kernel,
+    params_of = pltpu.CompilerParams(vmem_limit_bytes=VMEM_BYTES)
+    edge, fields = pl.pallas_call(
+        edge_kernel,
         out_shape=(
-            jax.ShapeDtypeStruct((tiles, rows, LANES), bf16),
             jax.ShapeDtypeStruct((rows, LANES), bf16),
             jax.ShapeDtypeStruct((tiles, 3, epochs * look_rows, LANES), bf16),
         ),
-        in_specs=[VMEM] * 4,
-        out_specs=(VMEM,) * 3,
-        compiler_params=pltpu.CompilerParams(vmem_limit_bytes=VMEM_BYTES),
-        cost_estimate=pl.CostEstimate(flops=4_000_000, bytes_accessed=3_000_000, transcendentals=0),
-    )(slc, estimate, direction, params)
+        in_specs=[VMEM] * 3,
+        out_specs=(VMEM,) * 2,
+        compiler_params=params_of,
+        cost_estimate=pl.CostEstimate(flops=1_000_000, bytes_accessed=2_000_000, transcendentals=0),
+    )(slc, estimate, direction)
 
     before, after = swapped(edge, edge, "sub")
     sub = lax.axis_index("sub")
     lane = lax.broadcasted_iota(jnp.int32, (rows, LANES), 1)
-    left_side = (lane < 2 * epochs * SIDES) & (lane % SIDES < RADIUS)
-    right_side = (lane < 2 * epochs * SIDES) & (lane % SIDES >= RADIUS)
-    nothing = jnp.zeros_like(edge)
-    left_edge = jnp.where(left_side & (sub > 0), before, nothing)
-    right_edge = jnp.where(right_side & (sub < lax.axis_size("sub") - 1), after, nothing)
-
-    def strip_for(shift):
-        target = for_device(shift)
-        value = lax.dynamic_index_in_dim(strips, target, axis=0, keepdims=False)
-        value = jnp.where(left_side & (target == 0), left_edge, value)
-        return jnp.where(right_side & (target == tiles - 1), right_edge, value)
-
-    def field_for(shift):
-        return lax.dynamic_index_in_dim(fields, for_device(shift), axis=0, keepdims=False)
-
-    strip_blocks = [strip_for(0)]
-    strip_blocks += [to_ahead(strip_for(tiles - shift), "epoch", tiles - shift) for shift in range(1, tiles)]
-    field_blocks = [field_for(0)]
-    field_blocks += [to_ahead(field_for(tiles - shift), "epoch", tiles - shift) for shift in range(1, tiles)]
+    inside = lane < 2 * epochs * SIDES
+    left = jnp.where(inside & (lane % SIDES < RADIUS) & (sub > 0), before, jnp.zeros_like(edge))
+    right = inside & (lane % SIDES >= RADIUS) & (sub < lax.axis_size("sub") - 1)
+    right = jnp.where(right, after, jnp.zeros_like(edge))
+    message_rows = 2 * epochs * rows + rows
+    message = pl.pallas_call(
+        pack_kernel,
+        out_shape=jax.ShapeDtypeStruct((tiles, message_rows, LANES), bf16),
+        in_specs=[VMEM] * 4,
+        out_specs=VMEM,
+        compiler_params=params_of,
+        cost_estimate=pl.CostEstimate(flops=3_000_000, bytes_accessed=2_000_000, transcendentals=0),
+    )(slc, params, left, right)
+    message = lax.all_to_all(message, "epoch", 0, 0)
+    fields = lax.all_to_all(fields, "epoch", 0, 0)
 
     def border(from_row):
-        parts = []
-        for block, strip in zip(blocks, strip_blocks):
-            main = lax.dynamic_slice_in_dim(block, from_row, HALO, axis=2).reshape(2 * epochs * HALO, LANES)
-            parts.append(jnp.concatenate([main, lax.dynamic_slice_in_dim(strip, from_row, HALO, axis=0)], axis=0))
-        return jnp.stack(parts)
+        blocks = message.reshape(tiles, 2 * epochs + 1, rows, LANES)
+        return lax.dynamic_slice_in_dim(blocks, from_row, HALO, axis=2).reshape(tiles, (2 * epochs + 1) * HALO, LANES)
 
     space = lax.axis_index("space")
     spaces = lax.axis_size("space")
@@ -493,8 +482,8 @@
         top, bottom = swapped(border(rows - HALO), border(0), "space")
     present = jnp.stack([space > 0, space < spaces - 1]).astype(f32)
 
-    listed = jnp.concatenate([strip[:epochs, PARAM_LANE : PARAM_LANE + 4 * SLOTS] for strip in strip_blocks], axis=0)
-    listed = listed.astype(f32)
+    listed = message[:, 2 * epochs * rows : 2 * epochs * rows + epochs, PARAM_LANE : PARAM_LANE + 4 * SLOTS]
+    listed = listed.reshape(total, 4 * SLOTS).astype(f32)
     partner = jnp.arange(total, dtype=jnp.int32)[:, None] + listed[:, :SLOTS].astype(jnp.int32)
     partner = lax.rem(partner, total).reshape(-1)
     weight = listed[:, SLOTS : 2 * SLOTS] + listed[:, 2 * SLOTS : 3 * SLOTS] + listed[:, 3 * SLOTS :]
@@ -505,7 +494,7 @@
             jax.ShapeDtypeStruct((tiles, epochs * look_rows, LANES), f32),
             jax.ShapeDtypeStruct((8, LANES), f32),
         ),
-        in_specs=[SMEM] * 3 + [VMEM] * (3 * tiles + 2),
+        in_specs=[SMEM] * 3 + [VMEM] * 4,
         out_specs=(VMEM, VMEM),
         scratch_shapes=[
             pltpu.VMEM((2 * total, rows + 2 * HALO, LANES), f32),
@@ -520,12 +509,11 @@
             pltpu.VMEM((total, look_rows, LANES), f32),
             pltpu.VMEM((total, look_rows, LANES), f32),
         ],
-        compiler_params=pltpu.CompilerParams(vmem_limit_bytes=VMEM_BYTES),
+        compiler_params=params_of,
         cost_estimate=pl.CostEstimate(flops=40_000_000, bytes_accessed=4_000_000, transcendentals=0),
-    )(partner, weight.reshape(-1), present, *blocks, *strip_blocks, *field_blocks, top, bottom)
-
-    returned = [gradient[0]]
-    returned += [to_ahead(gradient[shift], "epoch", shift) for shift in range(1, tiles)]
+    )(partner, weight.reshape(-1), present, message, fields, top, bottom)
+
+    returned = lax.all_to_all(gradient, "epoch", 0, 0)
     place = ("space", "sub")
     count = spaces * lax.axis_size("sub")
     shared = [sums] + [lax.ppermute(sums, place, [(i, (i + by) % count) for i in range(count)]) for by in range(1, count)]
@@ -535,11 +523,11 @@
     return pl.pallas_call(
         functools.partial(update_kernel, cell_count),
         out_shape=(jax.ShapeDtypeStruct(estimate.shape, f32),) * 2,
-        in_specs=[SMEM] * 2 + [VMEM] * (2 + 2 * tiles),
+        in_specs=[SMEM] + [VMEM] * (3 + tiles),
         out_specs=(VMEM, VMEM),
-        compiler_params=pltpu.CompilerParams(vmem_limit_bytes=VMEM_BYTES),
+        compiler_params=params_of,
         cost_estimate=pl.CostEstimate(flops=1_000_000, bytes_accessed=2_000_000, transcendentals=0),
-    )(me.reshape(1), prev_mean, estimate, direction, *returned, *scalars)
+    )(prev_mean, estimate, direction, returned, *scalars)
 
 
 def on_device(slc, offsets, weights, estimate, direction, prev_mean):

time: 95.6 us -> 93.3 us (0.976)
  starting transfers between devices: 38.1 us -> 23.8 us
  waiting for transfers between devices: 28.7 us -> 39.9 us
  Pallas kernels: 21.1 us -> 23.7 us
  local copies, waits for them, and re-layouts: 5.55 us -> 3.57 us
    all_to_all x0 -> x3, waiting for transfers between devices: none -> 36.6 us  [the longest x1 27.4 us: transposed_plan(): message = lax.all_to_all(message, 'epoch', 0, 0)]
    ppermute x15 -> x3, starting transfers between devices: 34.3 us -> 5.76 us  [to_ahead(): return lax.ppermute(x, axis, [(i, (i + by) % size) for i in range(size)])]
    ppermute x15 -> x3, waiting for transfers between devices: 24 us -> 1.49 us  [to_ahead(): return lax.ppermute(x, axis, [(i, (i + by) % size) for i in range(size)])]
    all_to_all x0 -> x3, starting transfers between devices: none -> 13.1 us  [the longest x1 6.21 us: transposed_plan(): message = lax.all_to_all(message, 'epoch', 0, 0)]
    ppermute x1, waiting for transfers between devices: 4.72 us -> 0.01 us  [transposed_plan(): top = bottom = lax.ppermute(mine, 'space', [(0, 1), (1, 0)])]
    pallas_call x1 -> x2, Pallas kernels: 0.61 us -> 2.54 us  [the longest x1 1.61 us: transposed_plan(): pl.pallas_call(pack_kernel, out_shape=jax.ShapeDtypeStruct((tiles, messag...]
    unnamed x16 -> x18, local copies, waits for them, and re-layouts: 4.65 us -> 3.3 us
    ppermute x3, waiting for transfers between devices: 0.01 us -> 1.33 us  [transposed_plan(): lax.ppermute(sums, place, [(i, (i + by) % count) for i in range(count)])]
  transfers between devices with their start and end apart: 20 -> 11, of which waited for: 8 -> 7; matrix products, arithmetic and copies ran while one was open for 1% -> 1% of each run, Pallas kernels for 0% -> 0%
where the time goes in v2:
time: 93.3 us; the launch traced here: 92.8 us
  waiting for transfers between devices  39.9 us (43%)
  starting transfers between devices  23.8 us (26%)
  Pallas kernels  23.7 us (25%)
  local copies, waits for them, and re-layouts  3.57 us (4%)
  between operations  1.39 us (1%)
    all_to_all x1, waiting for transfers between devices, transposed_plan(): message = lax.all_to_all(message, 'epoch', 0, 0)  27.4 us
    pallas_call x1, Pallas kernels, transposed_plan(): pl.pallas_call(functools.partial(main_kernel, (tiles, epochs, rows)), out...  20.3 us
    all_to_all x1, waiting for transfers between devices, transposed_plan(): fields = lax.all_to_all(fields, 'epoch', 0, 0)  9.17 us
    all_to_all x1, starting transfers between devices, transposed_plan(): message = lax.all_to_all(message, 'epoch', 0, 0)  6.21 us
    ppermute x3, starting transfers between devices, to_ahead(): return lax.ppermute(x, axis, [(i, (i + by) % size) for i in range(size)])  5.76 us
    all_to_all x1, starting transfers between devices, transposed_plan(): fields = lax.all_to_all(fields, 'epoch', 0, 0)  3.46 us
    all_to_all x1, starting transfers between devices, transposed_plan(): returned = lax.all_to_all(gradient, 'epoch', 0, 0)  3.41 us
    unnamed x18, local copies, waits for them, and re-layouts  3.3 us
  transfers between devices with their start and end apart: 11, of which 7 were waited for; matrix products, arithmetic and copies ran while one was open for 1% of the time, Pallas kernels for 0%

profile of v2, /device:TPU:0, one launch (start us, length us, event | category | flops | bytes accessed | tf_op | source)
XLA Modules:
  0.0 92.8 jit_solution(16183299531787779894)
XLA Ops:
  0.6 0.0 copy-start
  0.6 1.2 %copy-done = bf16[2,8,64,512]{3,2,1,0:T(8,128)(2,1)S(1)} copy-done((bf16[2,8,64,512]{3,2,1,0:T(8,128)(2,1)S(1)}, bf16[2,8,64,512]{3,2,1,0:T(8,128)(2,1)}, u32[]{:S(2)}) %copy-start) | copy-done | bytes 1048600
  1.9 0.0 copy-start.2
  1.9 0.9 %copy-done.2 = f32[8,16,512]{2,1,0:T(8,128)S(1)} copy-done((f32[8,16,512]{2,1,0:T(8,128)S(1)}, f32[8,16,512]{2,1,0:T(8,128)}, u32[]{:S(2)}) %copy-start.2) | copy-done | bytes 262168
  2.8 0.0 copy-start.4
  2.8 0.9 %copy-done.4 = f32[8,16,512]{2,1,0:T(8,128)S(1)} copy-done((f32[8,16,512]{2,1,0:T(8,128)S(1)}, f32[8,16,512]{2,1,0:T(8,128)}, u32[]{:S(2)}) %copy-start.4) | copy-done | bytes 262168
  3.8 0.0 copy-start.6
  3.8 0.9 %shard_map.77 = (bf16[64,128]{1,0:T(8,128)(2,1)S(1)}, bf16[4,3,128,128]{3,2,1,0:T(8,128)(2,1)}) custom-call(bf16[2,8,64,512]{3,2,1,0:T(8,128)(2,1)S(1)} %copy-done, f32[8,16,512]{2,1,0:T(8,128)S(1)} %copy-done.2, f32[8,16,512]{2,1,0:T(8,128)S(1)} %copy-done.4), custom_call_target="tpu_custom_call" | custom-call | flops 1000000 | bytes 2000000 | tf_op jit(solution)/shard_map/pallas_call | solution.py:441
  4.7 0.5 collective-permute-start
  5.2 0.0 copy-done.6
  5.2 0.1 copy.12
  5.2 0.0 copy-done.7
  5.3 0.1 copy.13
  5.3 0.1 select_maximum_fusion.params
  5.4 0.6 collective-permute-done
  6.0 0.0 copy-done.1
  6.0 1.6 %shard_map.78 = bf16[4,1088,128]{2,1,0:T(8,128)(2,1)} custom-call(bf16[2,8,64,512]{3,2,1,0:T(8,128)(2,1)S(1)} %copy-done.1, f32[64,128]{1,0:T(8,128)S(1)} %select_maximum_fusion.params, bf16[64,128]{1,0:T(8,128)(2,1)S(1)} %get-tuple-element.11.left, bf16[64,128]{1,0:T(8,128)(2,1)S(1)} %get-tuple-element.10.right), custom_call_target="tpu_custom_call" | custom-call | flops 3000000 | bytes 2000000 | tf_op jit(solution)/shard_map/pallas_call | solution.py:461
  7.6 6.2 %all-to-all-start = ((bf16[4,1088,128]{2,1,0:T(8,128)(2,1)}), bf16[4,1088,128]{2,1,0:T(8,128)(2,1)S(1)}, u32[]{:S(2)}, u32[]{:S(2)}) async-start(bf16[4,1088,128]{2,1,0:T(8,128)(2,1)} %shard_map.78), calls=%async_computation | async-start | bytes 2228224 | tf_op jit(solution)/shard_map/all_to_all | solution.py:469
  13.8 0.1 add_convert_fusion.present
  13.9 27.4 %all-to-all-done.refs_0_ = bf16[4,1088,128]{2,1,0:T(8,128)(2,1)S(1)} async-done(((bf16[4,1088,128]{2,1,0:T(8,128)(2,1)}), bf16[4,1088,128]{2,1,0:T(8,128)(2,1)S(1)}, u32[]{:S(2)}, u32[]{:S(2)}) %all-to-all-start) | async-done | bytes 1114144 | tf_op jit(solution)/shard_map/all_to_all | solution.py:469
  41.3 3.5 %all-to-all-start.1 = ((bf16[4,3,128,128]{3,2,1,0:T(8,128)(2,1)}), bf16[4,3,128,128]{3,2,1,0:T(8,128)(2,1)S(1)}, u32[]{:S(2)}, u32[]{:S(2)}) async-start(bf16[4,3,128,128]{3,2,1,0:T(8,128)(2,1)} %get-tuple-element.7), calls=%async_computation.1 | async-start | bytes 786432 | tf_op jit(solution)/shard_map/all_to_all | solution.py:470
  44.8 1.6 %collective-permute-start.1 = (bf16[4,272,128]{2,1,0:T(8,128)(2,1)S(1)}, bf16[4,272,128]{2,1,0:T(8,128)(2,1)S(1)}, u32[]{:S(2)}, u32[]{:S(2)}) collective-permute-start(bf16[4,272,128]{2,1,0:T(8,128)(2,1)S(1)} %bitcast.10), channel_id=1, source_target_pairs={{0,2},{2,0},{1,3},{3,1},{4,6},{6,4},{5,7},{7,5},{8,10},{10,8},{9,1... | collective-permute-start | bytes 835592 | tf_op jit(solution)/shard_map/ppermute | solution.py:480
  46.4 0.1 fusion.10
  46.5 0.1 reshape.19.partner
  46.6 0.1 slice_add_fusion
  46.6 0.1 reshape.20.weight
  46.8 0.0 copy-start.3
  46.8 0.0 copy-start.5
  46.8 9.2 %all-to-all-done.1.refs_1_ = bf16[4,3,128,128]{3,2,1,0:T(8,128)(2,1)S(1)} async-done(((bf16[4,3,128,128]{3,2,1,0:T(8,128)(2,1)}), bf16[4,3,128,128]{3,2,1,0:T(8,128)(2,1)S(1)}, u32[]{:S(2)}, u32[]{:S(2)}) %all-to-all-start.1) | async-done | bytes 393248 | tf_op jit(solution)/shard_map/all_to_all | solution.py:470
  56.0 0.0 collective-permute-done.1.refs_2_.refs_3_
  56.0 20.3 %shard_map.79 = (f32[4,128,128]{2,1,0:T(8,128)}, f32[8,128]{1,0:T(8,128)S(1)}) custom-call(s32[128]{0:T(128)S(1)} %reshape.19.partner, f32[128]{0:T(128)S(1)} %reshape.20.weight, f32[2]{0:T(128)S(1)} %add_convert_fusion.present, bf16[4,1088,128]{2,1,0:T(8,128)(2,1)S(1)} %all-to-all-done.refs_0_, bf16[4,3,128,128]{3,2,1,0:T(8,128)(2,1)S(1)} %all-to-all-done.1.refs_1_, ...), custom_call_target="tpu_custom_call" | custom-call | flops 40000000 | bytes 4000000 | tf_op jit(solution)/shard_map/pallas_call | solution.py:491
  76.2 3.4 %all-to-all-start.2 = ((f32[4,128,128]{2,1,0:T(8,128)}), f32[4,128,128]{2,1,0:T(8,128)S(1)}, u32[]{:S(2)}, u32[]{:S(2)}) async-start(f32[4,128,128]{2,1,0:T(8,128)} %get-tuple-element.8), calls=%async_computation.2 | async-start | bytes 524288 | tf_op jit(solution)/shard_map/all_to_all | solution.py:516
  79.6 0.1 collective-permute-start.2
  79.7 1.6 %collective-permute-start.3 = (f32[8,128]{1,0:T(8,128)S(1)}, f32[8,128]{1,0:T(8,128)S(1)}, u32[]{:S(2)}, u32[]{:S(2)}) collective-permute-start(f32[8,128]{1,0:T(8,128)S(1)} %get-tuple-element.9), channel_id=1, source_target_pairs={{0,2},{1,3},{2,0},{3,1},{4,6},{5,7},{6,4},{7,5},{8,10},{9,11},{10,... | collective-permute-start | bytes 12296 | tf_op jit(solution)/shard_map/ppermute | solution.py:519
  81.3 1.4 %collective-permute-start.4 = (f32[8,128]{1,0:T(8,128)S(1)}, f32[8,128]{1,0:T(8,128)S(1)}, u32[]{:S(2)}, u32[]{:S(2)}) collective-permute-start(f32[8,128]{1,0:T(8,128)S(1)} %get-tuple-element.9), channel_id=1, source_target_pairs={{0,3},{1,0},{2,1},{3,2},{4,7},{5,4},{6,5},{7,6},{8,11},{9,8},{10,9... | collective-permute-start | bytes 12296 | tf_op jit(solution)/shard_map/ppermute | solution.py:519
  82.7 0.1 collective-permute-done.2
  82.7 0.7 collective-permute-done.3
  83.4 0.6 collective-permute-done.4
  84.0 1.9 %collective-permute-start.5 = (f32[8,128]{1,0:T(8,128)S(1)}, f32[8,128]{1,0:T(8,128)S(1)}, u32[]{:S(2)}, u32[]{:S(2)}) collective-permute-start(f32[8,128]{1,0:T(8,128)S(1)} %add_add_fusion.refs_0_), channel_id=1, source_target_pairs={{0,4},{4,8},{8,12},{12,0},{1,5},{5,9},{9,13},{13,1},{2,6},{6,10},{... | collective-permute-start | bytes 12296 | tf_op jit(solution)/shard_map/ppermute | solution.py:425
  85.9 2.4 %collective-permute-start.6 = (f32[8,128]{1,0:T(8,128)S(1)}, f32[8,128]{1,0:T(8,128)S(1)}, u32[]{:S(2)}, u32[]{:S(2)}) collective-permute-start(f32[8,128]{1,0:T(8,128)S(1)} %add_add_fusion.refs_0_), channel_id=1, source_target_pairs={{0,8},{4,12},{8,0},{12,4},{1,9},{5,13},{9,1},{13,5},{2,10},{6,14},... | collective-permute-start | bytes 12296 | tf_op jit(solution)/shard_map/ppermute | solution.py:425
  88.3 1.5 %collective-permute-start.7 = (f32[8,128]{1,0:T(8,128)S(1)}, f32[8,128]{1,0:T(8,128)S(1)}, u32[]{:S(2)}, u32[]{:S(2)}) collective-permute-start(f32[8,128]{1,0:T(8,128)S(1)} %add_add_fusion.refs_0_), channel_id=1, source_target_pairs={{0,12},{4,0},{8,4},{12,8},{1,13},{5,1},{9,5},{13,9},{2,14},{6,2},{... | collective-permute-start | bytes 12296 | tf_op jit(solution)/shard_map/ppermute | solution.py:425
  90.4 0.0 collective-permute-done.5.refs_1_
  90.4 0.0 collective-permute-done.6.refs_2_
  90.4 1.5 %collective-permute-done.7.refs_3_ = f32[8,128]{1,0:T(8,128)S(1)} collective-permute-done((f32[8,128]{1,0:T(8,128)S(1)}, f32[8,128]{1,0:T(8,128)S(1)}, u32[]{:S(2)}, u32[]{:S(2)}) %collective-permute-start.7) | collective-permute-done | bytes 4128 | tf_op jit(solution)/shard_map/ppermute | solution.py:425
  91.9 0.0 all-to-all-done.2.pieces
  91.9 0.0 copy-done.3
  91.9 0.0 copy-done.5
  91.9 0.9 shard_map.80
  (9 shorter events, 0.1 us)
Async XLA Ops:
  0.6 1.2 %copy-start = (bf16[2,8,64,512]{3,2,1,0:T(8,128)(2,1)S(1)}, bf16[2,8,64,512]{3,2,1,0:T(8,128)(2,1)}, u32[]{:S(2)}) copy-start(bf16[2,8,64,512]{3,2,1,0:T(8,128)(2,1)} %slc.3) | copy-start | bytes 3145732
  1.9 0.9 %copy-start.2 = (f32[8,16,512]{2,1,0:T(8,128)S(1)}, f32[8,16,512]{2,1,0:T(8,128)}, u32[]{:S(2)}) copy-start(f32[8,16,512]{2,1,0:T(8,128)} %estimate.3) | copy-start | bytes 786436
  2.8 0.9 %copy-start.4 = (f32[8,16,512]{2,1,0:T(8,128)S(1)}, f32[8,16,512]{2,1,0:T(8,128)}, u32[]{:S(2)}) copy-start(f32[8,16,512]{2,1,0:T(8,128)} %direction.3) | copy-start | bytes 786436
  3.8 1.4 %copy-start.6 = (s32[8,4]{0,1:T(4,128)S(1)}, s32[8,4]{0,1:T(4,128)}, u32[]{:S(2)}) copy-start(s32[8,4]{0,1:T(4,128)} %param.7) | copy-start | bytes 388
  3.8 1.5 %copy-start.7 = (f32[8,4]{0,1:T(4,128)S(1)}, f32[8,4]{0,1:T(4,128)}, u32[]{:S(2)}) copy-start(f32[8,4]{0,1:T(4,128)} %param.8) | copy-start | bytes 388
  3.8 2.2 %copy-start.1 = (bf16[2,8,64,512]{3,2,1,0:T(8,128)(2,1)S(1)}, bf16[2,8,64,512]{3,2,1,0:T(8,128)(2,1)}, u32[]{:S(2)}) copy-start(bf16[2,8,64,512]{3,2,1,0:T(8,128)(2,1)} %slc.3) | copy-start | bytes 3145732
  4.7 1.3 %collective-permute-start = (bf16[64,128]{1,0:T(8,128)(2,1)S(1)}, bf16[64,128]{1,0:T(8,128)(2,1)S(1)}, u32[]{:S(2)}, u32[]{:S(2)}) collective-permute-start(bf16[64,128]{1,0:T(8,128)(2,1)S(1)} %get-tuple-element.6), channel_id=1, source_target_pairs={{0,1},{1,0},{2,3},{3,2},{4,5},{5,4},{6,7},{7,6},{8,9},{9,8},{10,11... | collective-permute-start | bytes 49160 | tf_op jit(solution)/shard_map/ppermute | solution.py:416
  7.6 33.7 %all-to-all-start = ((bf16[4,1088,128]{2,1,0:T(8,128)(2,1)}), bf16[4,1088,128]{2,1,0:T(8,128)(2,1)S(1)}, u32[]{:S(2)}, u32[]{:S(2)}) async-start(bf16[4,1088,128]{2,1,0:T(8,128)(2,1)} %shard_map.78), calls=%async_computation | async-start | bytes 2228224 | tf_op jit(solution)/shard_map/all_to_all | solution.py:469
  41.3 14.7 %all-to-all-start.1 = ((bf16[4,3,128,128]{3,2,1,0:T(8,128)(2,1)}), bf16[4,3,128,128]{3,2,1,0:T(8,128)(2,1)S(1)}, u32[]{:S(2)}, u32[]{:S(2)}) async-start(bf16[4,3,128,128]{3,2,1,0:T(8,128)(2,1)} %get-tuple-element.7), calls=%async_computation.1 | async-start | bytes 786432 | tf_op jit(solution)/shard_map/all_to_all | solution.py:470
  44.8 11.1 %collective-permute-start.1 = (bf16[4,272,128]{2,1,0:T(8,128)(2,1)S(1)}, bf16[4,272,128]{2,1,0:T(8,128)(2,1)S(1)}, u32[]{:S(2)}, u32[]{:S(2)}) collective-permute-start(bf16[4,272,128]{2,1,0:T(8,128)(2,1)S(1)} %bitcast.10), channel_id=1, source_target_pairs={{0,2},{2,0},{1,3},{3,1},{4,6},{6,4},{5,7},{7,5},{8,10},{10,8},{9,1... | collective-permute-start | bytes 835592 | tf_op jit(solution)/shard_map/ppermute | solution.py:480
  46.8 45.1 %copy-start.3 = (f32[8,16,512]{2,1,0:T(8,128)S(1)}, f32[8,16,512]{2,1,0:T(8,128)}, u32[]{:S(2)}) copy-start(f32[8,16,512]{2,1,0:T(8,128)} %estimate.3) | copy-start | bytes 786436
  46.8 45.1 %copy-start.5 = (f32[8,16,512]{2,1,0:T(8,128)S(1)}, f32[8,16,512]{2,1,0:T(8,128)}, u32[]{:S(2)}) copy-start(f32[8,16,512]{2,1,0:T(8,128)} %direction.3) | copy-start | bytes 786436
  76.2 15.7 %all-to-all-start.2 = ((f32[4,128,128]{2,1,0:T(8,128)}), f32[4,128,128]{2,1,0:T(8,128)S(1)}, u32[]{:S(2)}, u32[]{:S(2)}) async-start(f32[4,128,128]{2,1,0:T(8,128)} %get-tuple-element.8), calls=%async_computation.2 | async-start | bytes 524288 | tf_op jit(solution)/shard_map/all_to_all | solution.py:516
  79.6 3.1 %collective-permute-start.2 = (f32[8,128]{1,0:T(8,128)S(1)}, f32[8,128]{1,0:T(8,128)S(1)}, u32[]{:S(2)}, u32[]{:S(2)}) collective-permute-start(f32[8,128]{1,0:T(8,128)S(1)} %get-tuple-element.9), channel_id=1, source_target_pairs={{0,1},{1,2},{2,3},{3,0},{4,5},{5,6},{6,7},{7,4},{8,9},{9,10},{10,1... | collective-permute-start | bytes 12296 | tf_op jit(solution)/shard_map/ppermute | solution.py:519
  79.7 3.7 %collective-permute-start.3 = (f32[8,128]{1,0:T(8,128)S(1)}, f32[8,128]{1,0:T(8,128)S(1)}, u32[]{:S(2)}, u32[]{:S(2)}) collective-permute-start(f32[8,128]{1,0:T(8,128)S(1)} %get-tuple-element.9), channel_id=1, source_target_pairs={{0,2},{1,3},{2,0},{3,1},{4,6},{5,7},{6,4},{7,5},{8,10},{9,11},{10,... | collective-permute-start | bytes 12296 | tf_op jit(solution)/shard_map/ppermute | solution.py:519
  81.3 2.7 %collective-permute-start.4 = (f32[8,128]{1,0:T(8,128)S(1)}, f32[8,128]{1,0:T(8,128)S(1)}, u32[]{:S(2)}, u32[]{:S(2)}) collective-permute-start(f32[8,128]{1,0:T(8,128)S(1)} %get-tuple-element.9), channel_id=1, source_target_pairs={{0,3},{1,0},{2,1},{3,2},{4,7},{5,4},{6,5},{7,6},{8,11},{9,8},{10,9... | collective-permute-start | bytes 12296 | tf_op jit(solution)/shard_map/ppermute | solution.py:519
  84.0 6.4 %collective-permute-start.5 = (f32[8,128]{1,0:T(8,128)S(1)}, f32[8,128]{1,0:T(8,128)S(1)}, u32[]{:S(2)}, u32[]{:S(2)}) collective-permute-start(f32[8,128]{1,0:T(8,128)S(1)} %add_add_fusion.refs_0_), channel_id=1, source_target_pairs={{0,4},{4,8},{8,12},{12,0},{1,5},{5,9},{9,13},{13,1},{2,6},{6,10},{... | collective-permute-start | bytes 12296 | tf_op jit(solution)/shard_map/ppermute | solution.py:425
  85.9 4.5 %collective-permute-start.6 = (f32[8,128]{1,0:T(8,128)S(1)}, f32[8,128]{1,0:T(8,128)S(1)}, u32[]{:S(2)}, u32[]{:S(2)}) collective-permute-start(f32[8,128]{1,0:T(8,128)S(1)} %add_add_fusion.refs_0_), channel_id=1, source_target_pairs={{0,8},{4,12},{8,0},{12,4},{1,9},{5,13},{9,1},{13,5},{2,10},{6,14},... | collective-permute-start | bytes 12296 | tf_op jit(solution)/shard_map/ppermute | solution.py:425
  88.3 3.6 %collective-permute-start.7 = (f32[8,128]{1,0:T(8,128)S(1)}, f32[8,128]{1,0:T(8,128)S(1)}, u32[]{:S(2)}, u32[]{:S(2)}) collective-permute-start(f32[8,128]{1,0:T(8,128)S(1)} %add_add_fusion.refs_0_), channel_id=1, source_target_pairs={{0,12},{4,0},{8,4},{12,8},{1,13},{5,1},{9,5},{13,9},{2,14},{6,2},{... | collective-permute-start | bytes 12296 | tf_op jit(solution)/shard_map/ppermute | solution.py:425

commit v3 on v2

--- a/solution.py
+++ b/solution.py
@@ -178,8 +178,8 @@
     return jnp.where((lane >= target) & (lane < target + RADIUS), moved, total)
 
 
-def pack_kernel(slc, params, left, right, message):
-    tiles = message.shape[0]
+def pack_kernel(slc, params, left, right, strips):
+    tiles = strips.shape[0]
     epochs = slc.shape[1]
     rows = slc.shape[2]
     lane = lax.broadcasted_iota(jnp.int32, (rows, LANES), 1)
@@ -198,38 +198,45 @@
             total = total + right[...].astype(jnp.float32)
         for part in range(2):
             for epoch in range(epochs):
-                block = part * epochs + epoch
-                at = block * SIDES
+                at = (part * epochs + epoch) * SIDES
                 if tile > 0:
                     total = placed(lane, total, tile_of(slc, part, epoch, tile - 1), LANES - RADIUS, at)
                 if tile < tiles - 1:
                     total = placed(lane, total, tile_of(slc, part, epoch, tile + 1), 0, at + RADIUS)
-                own = slc[part, epoch, :, tile * LANES : (tile + 1) * LANES]
-                message[tile, block * rows : (block + 1) * rows, :] = own
-        message[tile, 2 * epochs * rows :, :] = total.astype(jnp.bfloat16)
-
-
-def main_kernel(sizes, partner, weight, present, *refs):
-    tiles, epochs, rows = sizes
-    message, fields, top, bottom, gradient, sums = refs[:6]
-    full, rim_full, main, rim, looked, power, boxed, power_box, factors, est, old = refs[6:]
+        strips[tile] = total.astype(jnp.bfloat16)
+
+
+def pair_kernel(sizes, places, partner, weight, present, *refs):
+    epochs, rows, operands = sizes
+    inputs = refs[:operands]
+    factors, pulls = refs[operands : operands + 2]
+    full, rim_full, main, rim, looked, rim_looked, power, rim_power, power_box = refs[operands + 2 :]
+    count = len(places)
     look_rows = rows // LOOK
     tall = (rows + 2 * HALO) // LOOK
     halo_looks = HALO // LOOK
-    total = tiles * epochs
+    total = count * epochs
+    own_total = total - epochs
     group = 2 * SLOTS
+    share = LANES // SLOTS
     has_top = present[0]
     has_bottom = present[1]
     f32 = jnp.float32
 
-    band_from = lax.broadcasted_iota(jnp.int32, (2 * LANES, LANES), 0)
-    band_to = lax.broadcasted_iota(jnp.int32, (2 * LANES, LANES), 1)
-    rim_lane = band_from - LANES
-    side = rim_lane % SIDES
-    rim_column = jnp.where(side < RADIUS, side - RADIUS, LANES + side - RADIUS)
-    rim_column = jnp.where(rim_lane < LOOK * SIDES, rim_column, 4 * LANES)
-    column = jnp.where(band_from < LANES, band_from, rim_column)
-    band = (jnp.abs(column - band_to) <= RADIUS).astype(f32).astype(jnp.bfloat16)
+    def band_of(shape, from_of, to_of):
+        at = lax.broadcasted_iota(jnp.int32, shape, 0)
+        to = lax.broadcasted_iota(jnp.int32, shape, 1)
+        return (jnp.abs(from_of(at, to) - to_of(to)) <= RADIUS).astype(f32).astype(jnp.bfloat16)
+
+    def rim_column(at, to):
+        at = at % LANES
+        side = at % share % SIDES
+        column = jnp.where(side < RADIUS, side - RADIUS, LANES + side - RADIUS)
+        inside = (at // share == to // LANES) & (at % share < LOOK * SIDES)
+        return jnp.where(inside, column, -4 * LANES)
+
+    band = band_of((2 * LANES, LANES), lambda at, to: at % LANES, lambda to: to)
+    rim_band = band_of((2 * LANES, SLOTS * LANES), rim_column, lambda to: to % LANES)
     out_at = lax.broadcasted_iota(jnp.int32, (group * look_rows, group * tall), 0)
     in_at = lax.broadcasted_iota(jnp.int32, (group * look_rows, group * tall), 1)
     near = jnp.abs(in_at % tall - halo_looks - out_at % look_rows) <= RADIUS
@@ -237,35 +244,30 @@
     sum_rows = near.astype(f32).astype(jnp.bfloat16)
 
     lane = lax.broadcasted_iota(jnp.int32, (tall, LANES), 1)
-    for block in range(tiles):
+    for block, (tile_at, strip_at, strip_row, top_at, bottom_at, halo_slot) in enumerate(places):
+        tile, strip, top, bottom = inputs[tile_at], inputs[strip_at], inputs[top_at], inputs[bottom_at]
         for part in range(2):
 
             @pl.loop(0, epochs)
             def _(epoch):
                 at = part * total + block * epochs + epoch
                 row = pl.multiple_of((part * epochs + epoch) * HALO, HALO)
-                full[at, :HALO] = top[block, pl.ds(row, HALO), :].astype(f32) * has_top
-                own = pl.ds(pl.multiple_of((part * epochs + epoch) * rows, rows), rows)
-                full[at, HALO : HALO + rows] = message[block, own, :].astype(f32)
-                full[at, HALO + rows :] = bottom[block, pl.ds(row, HALO), :].astype(f32) * has_bottom
+                own = pl.multiple_of((part * epochs + epoch) * rows, rows)
+                full[at, :HALO] = top[halo_slot, pl.ds(row, HALO), :].astype(f32) * has_top
+                full[at, HALO : HALO + rows] = tile[pl.ds(own, rows), :].astype(f32)
+                full[at, HALO + rows :] = bottom[halo_slot, pl.ds(row, HALO), :].astype(f32) * has_bottom
 
         last = slice(2 * epochs * HALO, 2 * epochs * HALO + HALO)
-        rim_full[block, :HALO] = top[block, last, :].astype(f32) * has_top
-        rim_full[block, HALO : HALO + rows] = message[block, 2 * epochs * rows :, :].astype(f32)
-        rim_full[block, HALO + rows :] = bottom[block, last, :].astype(f32) * has_bottom
-
-        @pl.loop(0, epochs)
-        def _(epoch):
-            here = pl.ds(pl.multiple_of(epoch * look_rows, look_rows), look_rows)
-            est[block * epochs + epoch] = fields[block, 0, here, :].astype(f32) + fields[block, 1, here, :].astype(f32)
-            old[block * epochs + epoch] = fields[block, 2, here, :].astype(f32)
+        rim_full[block, :HALO] = top[halo_slot, last, :].astype(f32) * has_top
+        rim_full[block, HALO : HALO + rows] = strip[strip_row : strip_row + rows, :].astype(f32)
+        rim_full[block, HALO + rows :] = bottom[halo_slot, last, :].astype(f32) * has_bottom
 
     @pl.loop(0, 2 * total)
     def _(at):
         for look in range(LOOK):
             main[at, look] = full[at, pl.ds(look, tall, stride=LOOK), :]
 
-    for block in range(tiles):
+    for block in range(count):
         by_look = [rim_full[block, pl.ds(look, tall, stride=LOOK), :] for look in range(LOOK)]
         for part in range(2):
             for epoch in range(epochs):
@@ -275,24 +277,48 @@
                     target = look * SIDES
                     moved = pltpu.roll(by_look[look], (target - start) % LANES, axis=1)
                     value = jnp.where((lane >= target) & (lane < target + SIDES), moved, value)
+                spread = share
+                while spread < LANES:
+                    value = value + pltpu.roll(value, spread, axis=1)
+                    spread = 2 * spread
                 rim[part * total + block * epochs + epoch] = value
 
-    @pl.loop(0, total)
+    piece_lane = lax.broadcasted_iota(jnp.int32, (8, LANES), 1)
+    slot_lane = [piece_lane // share == slot for slot in range(SLOTS)]
+
+    def mixed(values):
+        result = values[-1]
+        for slot in range(SLOTS - 1):
+            result = jnp.where(slot_lane[slot], values[slot], result)
+        return result
+
+    @pl.loop(0, total // SLOTS)
+    def _(quad):
+        for piece in range(0, tall, 8):
+            rows_at = slice(piece, piece + 8)
+            squares = []
+            for extra in range(SLOTS):
+                epoch = quad * SLOTS + extra
+                value = None
+                for look in range(LOOK):
+                    real = main[epoch, look, rows_at]
+                    imag = main[total + epoch, look, rows_at]
+                    one = real * real + imag * imag
+                    value = one if value is None else value + one
+                power[pl.ds(pl.multiple_of(epoch * tall + piece, 8), 8), :] = value
+                real = rim[epoch, rows_at]
+                imag = rim[total + epoch, rows_at]
+                squares.append(real * real + imag * imag)
+            rim_power[pl.ds(pl.multiple_of(quad * tall + piece, 8), 8), :] = mixed(squares)
+
+    @pl.loop(0, own_total)
     def _(epoch):
+        mates = [partner[epoch * SLOTS + slot] for slot in range(SLOTS)]
         for piece in range(0, tall, 8):
             rows_at = slice(piece, piece + 8)
             own_re = [main[epoch, look, rows_at] for look in range(LOOK)]
             own_im = [main[total + epoch, look, rows_at] for look in range(LOOK)]
-            rim_re = rim[epoch, rows_at]
-            rim_im = rim[total + epoch, rows_at]
-            value = own_re[0] * own_re[0] + own_im[0] * own_im[0]
-            for look in range(1, LOOK):
-                value = value + (own_re[look] * own_re[look] + own_im[look] * own_im[look])
-            at = pl.multiple_of(epoch * tall + piece, 8)
-            power[pl.ds(at, 8), :LANES] = value
-            power[pl.ds(at, 8), LANES:] = rim_re * rim_re + rim_im * rim_im
-            for slot in range(SLOTS):
-                mate = partner[epoch * SLOTS + slot]
+            for slot, mate in enumerate(mates):
                 real = None
                 for look in range(LOOK):
                     mate_re = main[mate, look, rows_at]
@@ -301,91 +327,126 @@
                     two = own_im[look] * mate_re - own_re[look] * mate_im
                     real = one if real is None else real + one
                     imag = two if look == 0 else imag + two
-                mate_re = rim[mate, rows_at]
-                mate_im = rim[total + mate, rows_at]
                 at = pl.multiple_of(epoch * (group * tall) + 2 * slot * tall + piece, 8)
-                looked[pl.ds(at, 8), :LANES] = real
-                looked[pl.ds(at, 8), LANES:] = rim_re * mate_re + rim_im * mate_im
+                looked[pl.ds(at, 8), :] = real
                 at = pl.multiple_of(epoch * (group * tall) + (2 * slot + 1) * tall + piece, 8)
-                looked[pl.ds(at, 8), :LANES] = imag
-                looked[pl.ds(at, 8), LANES:] = rim_im * mate_re - rim_re * mate_im
-
-    def box(value):
-        high, low = split_two(value)
-        wide = jnp.dot(high, band, preferred_element_type=f32) + jnp.dot(low, band, preferred_element_type=f32)
-        high, low = split_two(wide)
+                looked[pl.ds(at, 8), :] = imag
+            rim_re = rim[epoch, rows_at]
+            rim_im = rim[total + epoch, rows_at]
+            mate_re = mixed([rim[mate, rows_at] for mate in mates])
+            mate_im = mixed([rim[total + mate, rows_at] for mate in mates])
+            at = pl.multiple_of(epoch * (2 * tall) + piece, 8)
+            rim_looked[pl.ds(at, 8), :] = rim_re * mate_re + rim_im * mate_im
+            at = pl.multiple_of(epoch * (2 * tall) + tall + piece, 8)
+            rim_looked[pl.ds(at, 8), :] = rim_im * mate_re - rim_re * mate_im
+
+    def box(value, rim_value, by_slot):
+        wide = jnp.dot(jnp.concatenate(split_two(value), axis=1), band, preferred_element_type=f32)
+        outer = jnp.dot(jnp.concatenate(split_two(rim_value), axis=1), rim_band, preferred_element_type=f32)
+        order = []
+        for at in range(group):
+            half, slot = (at % 2, at // 2) if by_slot else (at // SLOTS, at % SLOTS)
+            order.append(outer[half * tall : (half + 1) * tall, slot * LANES : (slot + 1) * LANES])
+        high, low = split_two(wide + jnp.concatenate(order, axis=0))
         return jnp.dot(sum_rows, high, preferred_element_type=f32) + jnp.dot(sum_rows, low, preferred_element_type=f32)
 
     for block in range(total // group):
-        value = box(power[block * group * tall : (block + 1) * group * tall, :])
+        here = slice(block * group * tall, (block + 1) * group * tall)
+        value = box(power[here, :], rim_power[2 * block * tall : 2 * (block + 1) * tall, :], False)
         for at in range(group):
             power_box[block * group + at] = value[at * look_rows : (at + 1) * look_rows]
 
-    @pl.loop(0, total // 4)
+    @pl.loop(0, own_total // 4)
     def _(quad):
         for extra in range(4):
             epoch = quad * 4 + extra
             at = pl.multiple_of(epoch * (group * tall), group * tall)
-            boxed[epoch] = box(looked[pl.ds(at, group * tall), :])
-
-    grad = gradient
+            rim_at = pl.multiple_of(epoch * (2 * tall), 2 * tall)
+            boxed = box(looked[pl.ds(at, group * tall), :], rim_looked[pl.ds(rim_at, 2 * tall), :], True)
+            own_power = power_box[epoch]
+            for slot in range(SLOTS):
+                pair = epoch * SLOTS + slot
+                coh_re = boxed[2 * slot * look_rows : (2 * slot + 1) * look_rows, :]
+                coh_im = boxed[(2 * slot + 1) * look_rows : (2 * slot + 2) * look_rows, :]
+                inverse = lax.rsqrt(own_power * power_box[partner[pair]] + EPSILON)
+                unit_re = coh_re * inverse
+                unit_im = coh_im * inverse
+                factor = weight[pair] * (unit_re * unit_re + unit_im * unit_im)
+                factors[pair] = factor
+                pulls[pair] = factor * unit_im
+
+
+def gradient_kernel(sizes, partner, *refs):
+    tiles, epochs, stages = sizes
+    fields = refs[:tiles]
+    factors = refs[tiles : tiles + len(stages)]
+    pulls = refs[tiles + len(stages) : tiles + 2 * len(stages)]
+    gradient, sums, est, old = refs[tiles + 2 * len(stages) :]
+    look_rows = est.shape[1]
+    total = tiles * epochs
+    f32 = jnp.float32
     for block in range(tiles):
-        grad[block] = jnp.zeros(grad.shape[1:], f32)
-
-    def rows_of(epoch):
-        return epoch // epochs, pl.ds(pl.multiple_of((epoch % epochs) * look_rows, look_rows), look_rows)
+
+        @pl.loop(0, epochs)
+        def _(epoch):
+            here = pl.ds(pl.multiple_of(epoch * look_rows, look_rows), look_rows)
+            est[block * epochs + epoch] = fields[block][0, here, :].astype(f32) + fields[block][1, here, :].astype(f32)
+            old[block * epochs + epoch] = fields[block][2, here, :].astype(f32)
 
     @pl.loop(0, total)
     def _(epoch):
-        own_power = power_box[epoch]
-        own_est = est[epoch]
-        own = jnp.zeros((look_rows, LANES), f32)
-        for slot in range(SLOTS):
-            mate = partner[epoch * SLOTS + slot]
-            coh_re = boxed[epoch, 2 * slot * look_rows : (2 * slot + 1) * look_rows, :]
-            coh_im = boxed[epoch, (2 * slot + 1) * look_rows : (2 * slot + 2) * look_rows, :]
-            inverse = lax.rsqrt(own_power * power_box[mate] + EPSILON)
-            unit_re = coh_re * inverse
-            unit_im = coh_im * inverse
-            factor = weight[epoch * SLOTS + slot] * (unit_re * unit_re + unit_im * unit_im)
-            factors[epoch * SLOTS + slot] = factor
-            weighted = factor * (unit_im - (own_est - est[mate]))
-            own = own + weighted
-            at, here = rows_of(mate)
-            grad[at, here, :] = grad[at, here, :] - weighted
-        at, here = rows_of(epoch)
-        grad[at, here, :] = grad[at, here, :] + own
-
-    def totals(epoch, carry):
-        norm, crossed, grad_term, mixed, old_term = carry
-        at, here = rows_of(epoch)
-        own_grad = grad[at, here, :]
-        own_old = old[epoch]
-        norm = norm + own_grad * own_grad
-        crossed = crossed + own_grad * own_old
-        for slot in range(SLOTS):
-            mate = partner[epoch * SLOTS + slot]
-            factor = factors[epoch * SLOTS + slot]
-            at, here = rows_of(mate)
-            grad_spread = own_grad - grad[at, here, :]
-            old_spread = own_old - old[mate]
-            pulled = factor * grad_spread
-            grad_term = grad_term + pulled * grad_spread
-            mixed = mixed + pulled * old_spread
-            old_term = old_term + factor * old_spread * old_spread
-        return norm, crossed, grad_term, mixed, old_term
+        gradient[epoch] = jnp.zeros((look_rows, LANES), f32)
+
+    for stage, own_blocks in enumerate(stages):
+        for number, block in enumerate(own_blocks):
+
+            @pl.loop(0, epochs)
+            def _(here):
+                epoch = block * epochs + here
+                own_est = est[epoch]
+                own = jnp.zeros((look_rows, LANES), f32)
+                for slot in range(SLOTS):
+                    mate = partner[epoch * SLOTS + slot]
+                    pair = (number * epochs + here) * SLOTS + slot
+                    weighted = pulls[stage][pair] - factors[stage][pair] * (own_est - est[mate])
+                    own = own + weighted
+                    gradient[mate] = gradient[mate] - weighted
+                gradient[epoch] = gradient[epoch] + own
 
     zero = jnp.zeros((look_rows, LANES), f32)
-    results = lax.fori_loop(0, total, totals, (zero,) * 5)
+    results = (zero,) * 5
+    for stage, own_blocks in enumerate(stages):
+        for number, block in enumerate(own_blocks):
+
+            def totals(here, carry):
+                norm, crossed, grad_term, mixed, old_term = carry
+                epoch = block * epochs + here
+                own_grad = gradient[epoch]
+                own_old = old[epoch]
+                norm = norm + own_grad * own_grad
+                crossed = crossed + own_grad * own_old
+                for slot in range(SLOTS):
+                    mate = partner[epoch * SLOTS + slot]
+                    factor = factors[stage][(number * epochs + here) * SLOTS + slot]
+                    grad_spread = own_grad - gradient[mate]
+                    old_spread = own_old - old[mate]
+                    pulled = factor * grad_spread
+                    grad_term = grad_term + pulled * grad_spread
+                    mixed = mixed + pulled * old_spread
+                    old_term = old_term + factor * old_spread * old_spread
+                return norm, crossed, grad_term, mixed, old_term
+
+            results = lax.fori_loop(0, epochs, totals, results)
     sums[...] = jnp.zeros(sums.shape, f32)
     for at, value in enumerate(results):
         sums[at : at + 1, :] = jnp.sum(value, axis=0, keepdims=True)
 
 
-def update_kernel(cell_count, prev_mean, estimate, direction, pieces, *refs):
+def update_kernel(cell_count, me, prev_mean, estimate, direction, *refs):
     new_estimate, new_direction = refs[-2:]
     tiles = estimate.shape[2] // LANES
-    scalars = refs[:-2]
+    pieces = refs[:tiles]
+    scalars = refs[tiles:-2]
     epochs = estimate.shape[0]
     look_rows = estimate.shape[1]
     total = scalars[0][...]
@@ -398,10 +459,11 @@
     step = (grad_norm + momentum * crossed) / curvature
     momentum = jnp.broadcast_to(momentum, (look_rows, LANES))
     step = jnp.broadcast_to(step, (look_rows, LANES))
-    for tile in range(tiles):
-        columns = slice(tile * LANES, (tile + 1) * LANES)
+    for shift, piece in enumerate(pieces):
+        tile = lax.rem(me[0] - shift + tiles, tiles)
+        columns = pl.ds(pl.multiple_of(tile * LANES, LANES), LANES)
         for epoch in range(epochs):
-            gradient = pieces[tile, epoch * look_rows : (epoch + 1) * look_rows, :]
+            gradient = piece[epoch]
             moved = gradient + momentum * direction[epoch, :, columns]
             new_direction[epoch, :, columns] = moved
             new_estimate[epoch, :, columns] = estimate[epoch, :, columns] + step * moved
@@ -429,15 +491,30 @@
     f32 = jnp.float32
     bf16 = jnp.bfloat16
     tiles = lax.axis_size("epoch")
+    me = lax.axis_index("epoch")
     epochs, rows, columns = slc.shape[1:]
     look_rows = rows // LOOK
     total = tiles * epochs
     tall = (rows + 2 * HALO) // LOOK
+    tile_rows = 2 * epochs * rows
+    params_of = pltpu.CompilerParams(vmem_limit_bytes=VMEM_BYTES)
+
+    def for_device(shift):
+        return lax.rem(me + shift, tiles)
+
+    def tile_for(shift):
+        return lax.dynamic_slice_in_dim(slc, for_device(shift) * LANES, LANES, axis=3).reshape(tile_rows, LANES)
+
+    def fetched(send, shift):
+        return to_ahead(send(tiles - shift), "epoch", tiles - shift)
+
+    beside = [tiles - 1, 0, 1]
+    far = list(range(2, tiles - 1))
+    tile = {0: tile_for(0), 1: fetched(tile_for, 1), tiles - 1: fetched(tile_for, tiles - 1)}
 
     params = jnp.zeros((rows, LANES), f32)
     listed = jnp.concatenate([offsets.astype(f32), weights, weights, weights], axis=1)
     params = lax.dynamic_update_slice(params, listed, (0, PARAM_LANE))
-    params_of = pltpu.CompilerParams(vmem_limit_bytes=VMEM_BYTES)
     edge, fields = pl.pallas_call(
         edge_kernel,
         out_shape=(
@@ -449,7 +526,6 @@
         compiler_params=params_of,
         cost_estimate=pl.CostEstimate(flops=1_000_000, bytes_accessed=2_000_000, transcendentals=0),
     )(slc, estimate, direction)
-
     before, after = swapped(edge, edge, "sub")
     sub = lax.axis_index("sub")
     lane = lax.broadcasted_iota(jnp.int32, (rows, LANES), 1)
@@ -457,83 +533,157 @@
     left = jnp.where(inside & (lane % SIDES < RADIUS) & (sub > 0), before, jnp.zeros_like(edge))
     right = inside & (lane % SIDES >= RADIUS) & (sub < lax.axis_size("sub") - 1)
     right = jnp.where(right, after, jnp.zeros_like(edge))
-    message_rows = 2 * epochs * rows + rows
-    message = pl.pallas_call(
+    strips = pl.pallas_call(
         pack_kernel,
-        out_shape=jax.ShapeDtypeStruct((tiles, message_rows, LANES), bf16),
+        out_shape=jax.ShapeDtypeStruct((tiles, rows, LANES), bf16),
         in_specs=[VMEM] * 4,
         out_specs=VMEM,
         compiler_params=params_of,
         cost_estimate=pl.CostEstimate(flops=3_000_000, bytes_accessed=2_000_000, transcendentals=0),
     )(slc, params, left, right)
-    message = lax.all_to_all(message, "epoch", 0, 0)
-    fields = lax.all_to_all(fields, "epoch", 0, 0)
-
-    def border(from_row):
-        blocks = message.reshape(tiles, 2 * epochs + 1, rows, LANES)
-        return lax.dynamic_slice_in_dim(blocks, from_row, HALO, axis=2).reshape(tiles, (2 * epochs + 1) * HALO, LANES)
+
+    def strip_for(shift):
+        return lax.dynamic_index_in_dim(strips, for_device(shift), axis=0, keepdims=False)
+
+    def field_for(shift):
+        return lax.dynamic_index_in_dim(fields, for_device(shift), axis=0, keepdims=False)
+
+    def both_for(shift):
+        return jnp.concatenate([tile_for(shift), strip_for(shift)], axis=0)
+
+    strip = {0: strip_for(0), 1: fetched(strip_for, 1), tiles - 1: fetched(strip_for, tiles - 1)}
+    both = {block: fetched(both_for, block) for block in far}
+    field = {0: field_for(0)}
+    fields = lax.optimization_barrier((fields, tile[1], tile[tiles - 1]))[0]
+    for block in [1, tiles - 1] + far:
+        field[block] = fetched(field_for, block)
 
     space = lax.axis_index("space")
     spaces = lax.axis_size("space")
-    if spaces == 2:
-        mine = border(jnp.where(space == 0, rows - HALO, 0))
-        top = bottom = lax.ppermute(mine, "space", [(0, 1), (1, 0)])
-    else:
-        top, bottom = swapped(border(rows - HALO), border(0), "space")
     present = jnp.stack([space > 0, space < spaces - 1]).astype(f32)
 
-    listed = message[:, 2 * epochs * rows : 2 * epochs * rows + epochs, PARAM_LANE : PARAM_LANE + 4 * SLOTS]
-    listed = listed.reshape(total, 4 * SLOTS).astype(f32)
+    def halo(blocks):
+        def border(from_row):
+            parts = []
+            for block in blocks:
+                if block in tile:
+                    own = tile[block].reshape(2 * epochs, rows, LANES)
+                    rim = strip[block].reshape(1, rows, LANES)
+                    pieces = [own, rim]
+                else:
+                    pieces = [both[block].reshape(2 * epochs + 1, rows, LANES)]
+                for piece in pieces:
+                    cut = lax.dynamic_slice_in_dim(piece, from_row, HALO, axis=1)
+                    parts.append(cut.reshape(-1, LANES))
+            return jnp.concatenate(parts, axis=0).reshape(len(blocks), (2 * epochs + 1) * HALO, LANES)
+
+        if spaces == 2:
+            mine = border(jnp.where(space == 0, rows - HALO, 0))
+            got = lax.ppermute(mine, "space", [(0, 1), (1, 0)])
+            return got, got
+        return swapped(border(rows - HALO), border(0), "space")
+
+    def params_in(block):
+        source = strip[block] if block in strip else both[block][tile_rows:]
+        return source[:epochs, PARAM_LANE : PARAM_LANE + 4 * SLOTS].astype(f32)
+
+    def pairs_of(blocks, loaded):
+        listed = jnp.concatenate([params_in(block) for block in blocks], axis=0)
+        mate = jnp.arange(len(blocks) * epochs, dtype=jnp.int32)[:, None] + listed[:, :SLOTS].astype(jnp.int32)
+        weight = listed[:, SLOTS : 2 * SLOTS] + listed[:, 2 * SLOTS : 3 * SLOTS] + listed[:, 3 * SLOTS :]
+        return mate.reshape(-1), weight.reshape(-1)
+
+    near_halo = halo(beside)
+    def pair_stage(loaded):
+        own = loaded[:-1]
+        mate, weight = pairs_of(own, loaded)
+        operands = []
+
+        def index_of(array):
+            for at, other in enumerate(operands):
+                if other is array:
+                    return at
+            operands.append(array)
+            return len(operands) - 1
+
+        places = []
+        for block in loaded:
+            if block in tile:
+                at = index_of(tile[block]), index_of(strip[block]), 0
+            else:
+                at = index_of(both[block]), index_of(both[block]), tile_rows
+            source, slots = (near_halo, beside) if block in beside else (far_halo, far)
+            places.append(at + (index_of(source[0]), index_of(source[1]), slots.index(block)))
+        here = len(loaded) * epochs
+        owned = len(own) * epochs
+        group = 2 * SLOTS
+        shape = jax.ShapeDtypeStruct((owned * SLOTS, look_rows, LANES), f32)
+        return pl.pallas_call(
+            functools.partial(pair_kernel, (epochs, rows, len(operands)), tuple(places)),
+            out_shape=(shape, shape),
+            in_specs=[SMEM] * 3 + [VMEM] * len(operands),
+            out_specs=(VMEM, VMEM),
+            scratch_shapes=[
+                pltpu.VMEM((2 * here, rows + 2 * HALO, LANES), f32),
+                pltpu.VMEM((len(loaded), rows + 2 * HALO, LANES), f32),
+                pltpu.VMEM((2 * here, LOOK, tall, LANES), f32),
+                pltpu.VMEM((2 * here, tall, LANES), f32),
+                pltpu.VMEM((owned * group * tall, LANES), f32),
+                pltpu.VMEM((owned * 2 * tall, LANES), f32),
+                pltpu.VMEM((here * tall, LANES), f32),
+                pltpu.VMEM((here // SLOTS * tall, LANES), f32),
+                pltpu.VMEM((here, look_rows, LANES), f32),
+            ],
+            compiler_params=params_of,
+            cost_estimate=pl.CostEstimate(flops=20_000_000, bytes_accessed=30_000_000, transcendentals=0),
+        )(mate, weight, present, *operands)
+
+    near_stage = beside
+    far_stage = list(range(1, tiles))
+    near_pairs = pair_stage(near_stage)
+    both, near_pairs = lax.optimization_barrier((both, near_pairs))
+    far_halo = halo(far)
+    far_pairs = pair_stage(far_stage)
+
+    listed = jnp.concatenate([params_in(block) for block in range(tiles)], axis=0)
     partner = jnp.arange(total, dtype=jnp.int32)[:, None] + listed[:, :SLOTS].astype(jnp.int32)
     partner = lax.rem(partner, total).reshape(-1)
-    weight = listed[:, SLOTS : 2 * SLOTS] + listed[:, 2 * SLOTS : 3 * SLOTS] + listed[:, 3 * SLOTS :]
-    group = 2 * SLOTS
+    stages = (tuple(near_stage[:-1]), tuple(far_stage[:-1]))
     gradient, sums = pl.pallas_call(
-        functools.partial(main_kernel, (tiles, epochs, rows)),
+        functools.partial(gradient_kernel, (tiles, epochs, stages)),
         out_shape=(
-            jax.ShapeDtypeStruct((tiles, epochs * look_rows, LANES), f32),
+            jax.ShapeDtypeStruct((total, look_rows, LANES), f32),
             jax.ShapeDtypeStruct((8, LANES), f32),
         ),
-        in_specs=[SMEM] * 3 + [VMEM] * 4,
+        in_specs=[SMEM] + [VMEM] * (tiles + 4),
         out_specs=(VMEM, VMEM),
-        scratch_shapes=[
-            pltpu.VMEM((2 * total, rows + 2 * HALO, LANES), f32),
-            pltpu.VMEM((tiles, rows + 2 * HALO, LANES), f32),
-            pltpu.VMEM((2 * total, LOOK, tall, LANES), f32),
-            pltpu.VMEM((2 * total, tall, LANES), f32),
-            pltpu.VMEM((total * group * tall, 2 * LANES), f32),
-            pltpu.VMEM((total * tall, 2 * LANES), f32),
-            pltpu.VMEM((total, group * look_rows, LANES), f32),
-            pltpu.VMEM((total, look_rows, LANES), f32),
-            pltpu.VMEM((total * SLOTS, look_rows, LANES), f32),
-            pltpu.VMEM((total, look_rows, LANES), f32),
-            pltpu.VMEM((total, look_rows, LANES), f32),
-        ],
+        scratch_shapes=[pltpu.VMEM((total, look_rows, LANES), f32)] * 2,
         compiler_params=params_of,
-        cost_estimate=pl.CostEstimate(flops=40_000_000, bytes_accessed=4_000_000, transcendentals=0),
-    )(partner, weight.reshape(-1), present, message, fields, top, bottom)
-
-    returned = lax.all_to_all(gradient, "epoch", 0, 0)
+        cost_estimate=pl.CostEstimate(flops=10_000_000, bytes_accessed=8_000_000, transcendentals=0),
+    )(partner, *[field[block] for block in range(tiles)], near_pairs[0], far_pairs[0], near_pairs[1], far_pairs[1])
+
     place = ("space", "sub")
     count = spaces * lax.axis_size("sub")
     shared = [sums] + [lax.ppermute(sums, place, [(i, (i + by) % count) for i in range(count)]) for by in range(1, count)]
     here = sum(shared[1:], shared[0])
     scalars = [here] + [to_ahead(here, "epoch", by) for by in range(1, tiles)]
+    returned = [gradient[:epochs]]
+    returned += [to_ahead(gradient[by * epochs : (by + 1) * epochs], "epoch", by) for by in range(1, tiles)]
     cell_count = float(total * look_rows * spaces * columns * lax.axis_size("sub"))
     return pl.pallas_call(
         functools.partial(update_kernel, cell_count),
         out_shape=(jax.ShapeDtypeStruct(estimate.shape, f32),) * 2,
-        in_specs=[SMEM] + [VMEM] * (3 + tiles),
+        in_specs=[SMEM] * 2 + [VMEM] * (2 + 2 * tiles),
         out_specs=(VMEM, VMEM),
         compiler_params=params_of,
         cost_estimate=pl.CostEstimate(flops=1_000_000, bytes_accessed=2_000_000, transcendentals=0),
-    )(prev_mean, estimate, direction, returned, *scalars)
+    )(me.reshape(1), prev_mean, estimate, direction, *returned, *scalars)
 
 
 def on_device(slc, offsets, weights, estimate, direction, prev_mean):
     epochs, rows, columns = slc.shape[1:]
-    fits = columns == LANES * lax.axis_size("epoch") and lax.axis_size("epoch") > 1
-    fits = fits and 2 * epochs * SIDES <= PARAM_LANE and rows % HALO == 0 and epochs * lax.axis_size("epoch") % (2 * SLOTS) == 0
+    fits = columns == LANES * lax.axis_size("epoch") and lax.axis_size("epoch") > 3
+    fits = fits and 2 * epochs * SIDES <= PARAM_LANE and rows % HALO == 0 and epochs % (2 * SLOTS) == 0
     plan = transposed_plan if fits else ring_plan
     return plan(slc, offsets, weights, estimate, direction, prev_mean)
 

time: 93.3 us -> 82.7 us (0.89)
  waiting for transfers between devices: 39.9 us -> 17.2 us
  Pallas kernels: 23.7 us -> 29 us
  starting transfers between devices: 23.8 us -> 27.3 us
  local copies, waits for them, and re-layouts: 3.57 us -> 6.71 us
    all_to_all x3 -> x0, waiting for transfers between devices: 36.6 us -> none  [the longest x1 27.4 us: transposed_plan(): message = lax.all_to_all(message, 'epoch', 0, 0)]
    ppermute x3 -> x14, starting transfers between devices: 5.76 us -> 22 us  [to_ahead(): return lax.ppermute(x, axis, [(i, (i + by) % size) for i in range(size)])]
    all_to_all x3 -> x0, starting transfers between devices: 13.1 us -> none  [the longest x1 6.21 us: transposed_plan(): message = lax.all_to_all(message, 'epoch', 0, 0)]
    ppermute x3 -> x14, waiting for transfers between devices: 1.49 us -> 14.3 us  [to_ahead(): return lax.ppermute(x, axis, [(i, (i + by) % size) for i in range(size)])]
    pallas_call x2 -> x4, Pallas kernels: 21.9 us -> 27.9 us  [the longest x2 25.2 us: pair_stage(): pl.pallas_call(functools.partial(pair_kernel, (epochs, rows, len(operands...]
    ppermute x1 -> x2, waiting for transfers between devices: 0.01 us -> 2.89 us  [halo(): got = lax.ppermute(mine, 'space', [(0, 1), (1, 0)])]
    unnamed x18 -> x23, local copies, waits for them, and re-layouts: 3.3 us -> 5.21 us
    ppermute x1 -> x2, starting transfers between devices: 1.56 us -> 3.19 us  [halo(): got = lax.ppermute(mine, 'space', [(0, 1), (1, 0)])]
  transfers between devices with their start and end apart: 11 -> 20, of which waited for: 7 -> 6; matrix products, arithmetic and copies ran while one was open for 1% -> 3% of each run, Pallas kernels for 0% -> 31%
where the time goes in v3:
time: 82.7 us; the launch traced here: 82.4 us
  Pallas kernels  29 us (35%)
  starting transfers between devices  27.3 us (33%)
  waiting for transfers between devices  17.2 us (21%)
  local copies, waits for them, and re-layouts  6.71 us (8%)
  between operations  1.53 us (2%)
    pallas_call x2, Pallas kernels, pair_stage(): pl.pallas_call(functools.partial(pair_kernel, (epochs, rows, len(operands...  25.2 us
    ppermute x14, starting transfers between devices, to_ahead(): return lax.ppermute(x, axis, [(i, (i + by) % size) for i in range(size)])  22 us
    ppermute x14, waiting for transfers between devices, to_ahead(): return lax.ppermute(x, axis, [(i, (i + by) % size) for i in range(size)])  14.3 us
    unnamed x23, local copies, waits for them, and re-layouts  5.21 us
    ppermute x2, starting transfers between devices, halo(): got = lax.ppermute(mine, 'space', [(0, 1), (1, 0)])  3.19 us
    ppermute x2, waiting for transfers between devices, halo(): got = lax.ppermute(mine, 'space', [(0, 1), (1, 0)])  2.89 us
    pallas_call x1, Pallas kernels, transposed_plan(): pl.pallas_call(functools.partial(gradient_kernel, (tiles, epochs, stages)...  2.24 us
  transfers between devices with their start and end apart: 20, of which 6 were waited for; matrix products, arithmetic and copies ran while one was open for 3% of the time, Pallas kernels for 31%

profile of v3, /device:TPU:0, one launch (start us, length us, event | category | flops | bytes accessed | tf_op | source)
XLA Modules:
  0.0 82.4 jit_solution(7753868548650258200)
XLA Ops:
  0.6 1.2 %copy-done = bf16[2,8,64,512]{3,2,1,0:T(8,128)(2,1)S(1)} copy-done((bf16[2,8,64,512]{3,2,1,0:T(8,128)(2,1)S(1)}, bf16[2,8,64,512]{3,2,1,0:T(8,128)(2,1)}, u32[]{:S(2)}) %copy-start) | copy-done | bytes 1048600
  1.9 0.9 %copy-done.2 = f32[8,16,512]{2,1,0:T(8,128)S(1)} copy-done((f32[8,16,512]{2,1,0:T(8,128)S(1)}, f32[8,16,512]{2,1,0:T(8,128)}, u32[]{:S(2)}) %copy-start.2) | copy-done | bytes 262168
  2.8 0.9 %copy-done.4 = f32[8,16,512]{2,1,0:T(8,128)S(1)} copy-done((f32[8,16,512]{2,1,0:T(8,128)S(1)}, f32[8,16,512]{2,1,0:T(8,128)}, u32[]{:S(2)}) %copy-start.4) | copy-done | bytes 262168
  3.8 0.2 shard_map.77
  4.0 0.5 collective-permute-start
  4.5 0.5 copy-done.1
  5.0 0.9 %constant_dynamic-slice_fusion.3 = (bf16[2,8,64,128]{3,2,1,0:T(8,128)(2,1)S(1)}, bf16[2,8,64,128]{3,2,1,0:T(8,128)(2,1)}, bf16[2,8,64,128]{3,2,1,0:T(8,128)(2,1)S(1)}, bf16[2,8,64,128]{3,2,1,0:T(8,128)(2,1)S(1)}) fusion(bf16[2,8,64,512]{3,2,1,0:T(8,128)(2,1)S(1)} %copy-done.1, s32[]{:T(128)S(6)} %select_n.81, s32[]{:T(128)S(6)} %select_n.76, ...), kind=kLoop, calls=%fused_computation.70 | loop fusion | bytes 2097168 | tf_op jit(solution)/shard_map/dynamic_slice | solution.py:506
  5.9 3.0 %collective-permute-start.4 = (bf16[1024,128]{1,0:T(8,128)(2,1)}, bf16[1024,128]{1,0:T(8,128)(2,1)S(1)}, u32[]{:S(2)}, u32[]{:S(2)}) collective-permute-start(bf16[1024,128]{1,0:T(8,128)(2,1)} %bitcast.8), channel_id=1, source_target_pairs={{0,4},{4,8},{8,12},{12,0},{1,5},{5,9},{9,13},{13,1},{2,6},{6,10},{... | collective-permute-start | bytes 786440 | tf_op jit(solution)/shard_map/ppermute | solution.py:487
  8.9 2.0 %collective-permute-start.5 = (bf16[1024,128]{1,0:T(8,128)(2,1)S(1)}, bf16[1024,128]{1,0:T(8,128)(2,1)S(1)}, u32[]{:S(2)}, u32[]{:S(2)}) collective-permute-start(bf16[1024,128]{1,0:T(8,128)(2,1)S(1)} %bitcast.42), channel_id=1, source_target_pairs={{0,12},{4,0},{8,4},{12,8},{1,13},{5,1},{9,5},{13,9},{2,14},{6,2},{... | collective-permute-start | bytes 786440 | tf_op jit(solution)/shard_map/ppermute | solution.py:487
  10.9 0.7 copy-done.6
  11.6 0.1 copy.12
  11.7 0.7 copy-done.7
  12.4 0.1 copy.13
  12.5 0.1 select_maximum_fusion.params
  12.5 0.1 add_convert_fusion.present
  12.6 0.5 shard_map.78
  13.2 0.1 slice_convert_fusion.2
  13.2 2.0 %collective-permute-start.1 = (bf16[64,128]{1,0:T(8,128)(2,1)S(1)}, bf16[64,128]{1,0:T(8,128)(2,1)S(1)}, u32[]{:S(2)}, u32[]{:S(2)}) collective-permute-start(bf16[64,128]{1,0:T(8,128)(2,1)S(1)} %get-tuple-element.37), channel_id=1, source_target_pairs={{0,12},{4,0},{8,4},{12,8},{1,13},{5,1},{9,5},{13,9},{2,14},{6,2},{... | collective-permute-start | bytes 49160 | tf_op jit(solution)/shard_map/ppermute | solution.py:487
  15.3 1.1 %collective-permute-start.2 = (bf16[1088,128]{1,0:T(8,128)(2,1)S(1)}, bf16[1088,128]{1,0:T(8,128)(2,1)S(1)}, u32[]{:S(2)}, u32[]{:S(2)}) collective-permute-start(bf16[1088,128]{1,0:T(8,128)(2,1)S(1)} %pad_maximum_fusion), channel_id=1, source_target_pairs={{0,8},{4,12},{8,0},{12,4},{1,9},{5,13},{9,1},{13,5},{2,10},{6,14},... | collective-permute-start | bytes 835592 | tf_op jit(solution)/shard_map/ppermute | solution.py:487
  16.4 6.3 %collective-permute-done.1.refs_6_.refs_1_ = bf16[64,128]{1,0:T(8,128)(2,1)S(1)} collective-permute-done((bf16[64,128]{1,0:T(8,128)(2,1)S(1)}, bf16[64,128]{1,0:T(8,128)(2,1)S(1)}, u32[]{:S(2)}, u32[]{:S(2)}) %collective-permute-start.1) | collective-permute-done | bytes 16416 | tf_op jit(solution)/shard_map/ppermute | solution.py:487
  22.7 2.0 %collective-permute-done.3.refs_1_.refs_6_ = bf16[64,128]{1,0:T(8,128)(2,1)S(1)} collective-permute-done((bf16[64,128]{1,0:T(8,128)(2,1)S(1)}, bf16[64,128]{1,0:T(8,128)(2,1)S(1)}, u32[]{:S(2)}, u32[]{:S(2)}) %collective-permute-start.3) | collective-permute-done | bytes 16416 | tf_op jit(solution)/shard_map/ppermute | solution.py:487
  24.8 0.1 reshape.73.partner
  25.1 1.8 %collective-permute-start.6 = (bf16[3,272,128]{2,1,0:T(8,128)(2,1)S(1)}, bf16[3,272,128]{2,1,0:T(8,128)(2,1)S(1)}, u32[]{:S(2)}, u32[]{:S(2)}) collective-permute-start(bf16[3,272,128]{2,1,0:T(8,128)(2,1)S(1)} %bitcast.47), channel_id=1, source_target_pairs={{0,2},{2,0},{1,3},{3,1},{4,6},{6,4},{5,7},{7,5},{8,10},{10,8},{9,1... | collective-permute-start | bytes 626696 | tf_op jit(solution)/shard_map/ppermute | solution.py:582
  26.9 0.1 fusion.20
  27.0 0.1 reshape.74.weight
  27.1 2.6 %collective-permute-start.9 = (bf16[3,128,128]{2,1,0:T(8,128)(2,1)S(1)}, bf16[3,128,128]{2,1,0:T(8,128)(2,1)S(1)}, u32[]{:S(2)}, u32[]{:S(2)}) collective-permute-start(bf16[3,128,128]{2,1,0:T(8,128)(2,1)S(1)} %get-tuple-element.30), channel_id=1, source_target_pairs={{0,4},{4,8},{8,12},{12,0},{1,5},{5,9},{9,13},{13,1},{2,6},{6,10},{... | collective-permute-start | bytes 294920 | tf_op jit(solution)/shard_map/ppermute | solution.py:487
  29.7 2.5 %collective-permute-start.8 = (bf16[3,128,128]{2,1,0:T(8,128)(2,1)S(1)}, bf16[3,128,128]{2,1,0:T(8,128)(2,1)S(1)}, u32[]{:S(2)}, u32[]{:S(2)}) collective-permute-start(bf16[3,128,128]{2,1,0:T(8,128)(2,1)S(1)} %get-tuple-element.31), channel_id=1, source_target_pairs={{0,8},{4,12},{8,0},{12,4},{1,9},{5,13},{9,1},{13,5},{2,10},{6,14},... | collective-permute-start | bytes 294920 | tf_op jit(solution)/shard_map/ppermute | solution.py:487
  32.2 2.8 %collective-permute-start.7 = (bf16[3,128,128]{2,1,0:T(8,128)(2,1)S(1)}, bf16[3,128,128]{2,1,0:T(8,128)(2,1)S(1)}, u32[]{:S(2)}, u32[]{:S(2)}) collective-permute-start(bf16[3,128,128]{2,1,0:T(8,128)(2,1)S(1)} %get-tuple-element.32), channel_id=1, source_target_pairs={{0,12},{4,0},{8,4},{12,8},{1,13},{5,1},{9,5},{13,9},{2,14},{6,2},{... | collective-permute-start | bytes 294920 | tf_op jit(solution)/shard_map/ppermute | solution.py:487
  35.1 12.6 %shard_map.79 = (f32[64,16,128]{2,1,0:T(8,128)S(1)}, f32[64,16,128]{2,1,0:T(8,128)S(1)}) custom-call(s32[64]{0:T(128)S(1)} %reshape.73.partner, f32[64]{0:T(128)S(1)} %reshape.74.weight, f32[2]{0:T(128)S(1)} %add_convert_fusion.present, bf16[1024,128]{1,0:T(8,128)(2,1)S(1)} %collective-permute-done.4.refs_0_.refs_5_, ...), custom_call_target="tpu_custom_call" | custom-call | flops 20000000 | bytes 30000000 | tf_op jit(solution)/shard_map/pallas_call | solution.py:621
  47.7 0.1 slice_convert_fusion.3
  47.8 0.1 fusion.13
  47.8 0.1 reshape.87.partner
  48.0 0.1 reshape.89.weight
  48.1 1.4 %collective-permute-start.10 = (bf16[1,272,128]{2,1,0:T(8,128)(2,1)S(1)}, bf16[1,272,128]{2,1,0:T(8,128)(2,1)S(1)}, u32[]{:S(2)}, u32[]{:S(2)}) collective-permute-start(bf16[1,272,128]{2,1,0:T(8,128)(2,1)S(1)} %bitcast.46), channel_id=1, source_target_pairs={{0,2},{2,0},{1,3},{3,1},{4,6},{6,4},{5,7},{7,5},{8,10},{10,8},{9,1... | collective-permute-start | bytes 208904 | tf_op jit(solution)/shard_map/ppermute | solution.py:582
  49.5 0.1 reshape.88.partner
  49.6 2.9 %collective-permute-done.10.refs_4_ = bf16[1,272,128]{2,1,0:T(8,128)(2,1)S(1)} collective-permute-done((bf16[1,272,128]{2,1,0:T(8,128)(2,1)S(1)}, bf16[1,272,128]{2,1,0:T(8,128)(2,1)S(1)}, u32[]{:S(2)}, u32[]{:S(2)}) %collective-permute-start.10) | collective-permute-done | bytes 69664 | tf_op jit(solution)/shard_map/ppermute | solution.py:582
  52.5 12.6 %shard_map.80 = (f32[64,16,128]{2,1,0:T(8,128)S(1)}, f32[64,16,128]{2,1,0:T(8,128)S(1)}) custom-call(s32[64]{0:T(128)S(1)} %reshape.88.partner, f32[64]{0:T(128)S(1)} %reshape.89.weight, f32[2]{0:T(128)S(1)} %add_convert_fusion.present, bf16[1024,128]{1,0:T(8,128)(2,1)S(1)} %collective-permute-done.5.refs_5_.refs_0_, ...), custom_call_target="tpu_custom_call" | custom-call | flops 20000000 | bytes 30000000 | tf_op jit(solution)/shard_map/pallas_call | solution.py:621
  65.1 2.2 %shard_map.81 = (f32[32,16,128]{2,1,0:T(8,128)S(1)}, f32[8,128]{1,0:T(8,128)S(1)}) custom-call(s32[128]{0:T(128)S(1)} %reshape.87.partner, bf16[3,128,128]{2,1,0:T(8,128)(2,1)S(1)} %dynamic-slice_bitcast_fusion.3.refs_0_, bf16[3,128,128]{2,1,0:T(8,128)(2,1)S(1)} %collective-permute-done.7.refs_1_, bf16[3,128,128]{2,1,0:T(8,128)(2,1)S(1)} %collective-permute-done.8.refs_2_, ...), custom_call_target="tpu_custom_call" | custom-call | flops 10000000 | bytes 8000000 | tf_op jit(solution)/shard_map/pallas_call | solution.py:652
  67.4 1.4 %collective-permute-start.15 = (f32[8,128]{1,0:T(8,128)S(1)}, f32[8,128]{1,0:T(8,128)S(1)}, u32[]{:S(2)}, u32[]{:S(2)}) collective-permute-start(f32[8,128]{1,0:T(8,128)S(1)} %get-tuple-element.25), channel_id=1, source_target_pairs={{0,2},{1,3},{2,0},{3,1},{4,6},{5,7},{6,4},{7,5},{8,10},{9,11},{10,... | collective-permute-start | bytes 12296 | tf_op jit(solution)/shard_map/ppermute | solution.py:667
  68.8 0.2 collective-permute-start.14
  69.0 1.4 %collective-permute-start.12 = (f32[8,16,128]{2,1,0:T(8,128)S(1)}, f32[8,16,128]{2,1,0:T(8,128)S(1)}, u32[]{:S(2)}, u32[]{:S(2)}) collective-permute-start(f32[8,16,128]{2,1,0:T(8,128)S(1)} %get-tuple-element.34), channel_id=1, source_target_pairs={{0,8},{4,12},{8,0},{12,4},{1,9},{5,13},{9,1},{13,5},{2,10},{6,14},... | collective-permute-start | bytes 196616 | tf_op jit(solution)/shard_map/ppermute | solution.py:487
  70.4 1.9 %collective-permute-start.11 = (f32[8,16,128]{2,1,0:T(8,128)S(1)}, f32[8,16,128]{2,1,0:T(8,128)S(1)}, u32[]{:S(2)}, u32[]{:S(2)}) collective-permute-start(f32[8,16,128]{2,1,0:T(8,128)S(1)} %get-tuple-element.35), channel_id=1, source_target_pairs={{0,4},{4,8},{8,12},{12,0},{1,5},{5,9},{9,13},{13,1},{2,6},{6,10},{... | collective-permute-start | bytes 196616 | tf_op jit(solution)/shard_map/ppermute | solution.py:487
  72.4 1.9 %collective-permute-start.19 = (f32[8,128]{1,0:T(8,128)S(1)}, f32[8,128]{1,0:T(8,128)S(1)}, u32[]{:S(2)}, u32[]{:S(2)}) collective-permute-start(f32[8,128]{1,0:T(8,128)S(1)} %add_add_fusion.refs_4_), channel_id=1, source_target_pairs={{0,12},{4,0},{8,4},{12,8},{1,13},{5,1},{9,5},{13,9},{2,14},{6,2},{... | collective-permute-start | bytes 12296 | tf_op jit(solution)/shard_map/ppermute | solution.py:487
  74.3 1.8 %collective-permute-done.19.refs_7_ = f32[8,128]{1,0:T(8,128)S(1)} collective-permute-done((f32[8,128]{1,0:T(8,128)S(1)}, f32[8,128]{1,0:T(8,128)S(1)}, u32[]{:S(2)}, u32[]{:S(2)}) %collective-permute-start.19) | collective-permute-done | bytes 4128 | tf_op jit(solution)/shard_map/ppermute | solution.py:487
  76.1 0.6 collective-permute-start.17
  77.3 1.5 %collective-permute-done.18.refs_6_ = f32[8,128]{1,0:T(8,128)S(1)} collective-permute-done((f32[8,128]{1,0:T(8,128)S(1)}, f32[8,128]{1,0:T(8,128)S(1)}, u32[]{:S(2)}, u32[]{:S(2)}) %collective-permute-start.18) | collective-permute-done | bytes 4128 | tf_op jit(solution)/shard_map/ppermute | solution.py:487
  78.8 2.7 %collective-permute-done.17.refs_5_ = f32[8,128]{1,0:T(8,128)S(1)} collective-permute-done((f32[8,128]{1,0:T(8,128)S(1)}, f32[8,128]{1,0:T(8,128)S(1)}, u32[]{:S(2)}, u32[]{:S(2)}) %collective-permute-start.17) | collective-permute-done | bytes 4128 | tf_op jit(solution)/shard_map/ppermute | solution.py:487
  81.5 0.9 %shard_map.82 = (f32[8,16,512]{2,1,0:T(8,128)}, f32[8,16,512]{2,1,0:T(8,128)}) custom-call(s32[1]{0:T(128)} %bitcast.me, f32[1]{0:T(128)S(6)} %copy.21.prev_mean, f32[8,16,512]{2,1,0:T(8,128)S(1)} %copy-done.3, f32[8,16,512]{2,1,0:T(8,128)S(1)} %copy-done.5, f32[8,16,128]{2,1,0:T(8,128)S(1)} %get-tuple-element.36.refs_0_, ...), custom_call_target="tpu_custom_call" | custom-call | flops 1000000 | bytes 2000000 | tf_op jit(solution)/shard_map/pallas_call | solution.py:673
  (52 shorter events, 0.6 us)
Async XLA Ops:
  0.6 1.2 %copy-start = (bf16[2,8,64,512]{3,2,1,0:T(8,128)(2,1)S(1)}, bf16[2,8,64,512]{3,2,1,0:T(8,128)(2,1)}, u32[]{:S(2)}) copy-start(bf16[2,8,64,512]{3,2,1,0:T(8,128)(2,1)} %slc.3) | copy-start | bytes 3145732
  1.9 0.9 %copy-start.2 = (f32[8,16,512]{2,1,0:T(8,128)S(1)}, f32[8,16,512]{2,1,0:T(8,128)}, u32[]{:S(2)}) copy-start(f32[8,16,512]{2,1,0:T(8,128)} %estimate.3) | copy-start | bytes 786436
  2.8 0.9 %copy-start.4 = (f32[8,16,512]{2,1,0:T(8,128)S(1)}, f32[8,16,512]{2,1,0:T(8,128)}, u32[]{:S(2)}) copy-start(f32[8,16,512]{2,1,0:T(8,128)} %direction.3) | copy-start | bytes 786436
  3.8 1.2 %copy-start.1 = (bf16[2,8,64,512]{3,2,1,0:T(8,128)(2,1)S(1)}, bf16[2,8,64,512]{3,2,1,0:T(8,128)(2,1)}, u32[]{:S(2)}) copy-start(bf16[2,8,64,512]{3,2,1,0:T(8,128)(2,1)} %slc.3) | copy-start | bytes 3145732
  4.0 8.7 %collective-permute-start = (bf16[64,128]{1,0:T(8,128)(2,1)S(1)}, bf16[64,128]{1,0:T(8,128)(2,1)S(1)}, u32[]{:S(2)}, u32[]{:S(2)}) collective-permute-start(bf16[64,128]{1,0:T(8,128)(2,1)S(1)} %get-tuple-element.14), channel_id=1, source_target_pairs={{0,1},{1,0},{2,3},{3,2},{4,5},{5,4},{6,7},{7,6},{8,9},{9,8},{10,11... | collective-permute-start | bytes 49160 | tf_op jit(solution)/shard_map/ppermute | solution.py:478
  5.9 19.0 %collective-permute-start.4 = (bf16[1024,128]{1,0:T(8,128)(2,1)}, bf16[1024,128]{1,0:T(8,128)(2,1)S(1)}, u32[]{:S(2)}, u32[]{:S(2)}) collective-permute-start(bf16[1024,128]{1,0:T(8,128)(2,1)} %bitcast.8), channel_id=1, source_target_pairs={{0,4},{4,8},{8,12},{12,0},{1,5},{5,9},{9,13},{13,1},{2,6},{6,10},{... | collective-permute-start | bytes 786440 | tf_op jit(solution)/shard_map/ppermute | solution.py:487
  8.9 16.1 %collective-permute-start.5 = (bf16[1024,128]{1,0:T(8,128)(2,1)S(1)}, bf16[1024,128]{1,0:T(8,128)(2,1)S(1)}, u32[]{:S(2)}, u32[]{:S(2)}) collective-permute-start(bf16[1024,128]{1,0:T(8,128)(2,1)S(1)} %bitcast.42), channel_id=1, source_target_pairs={{0,12},{4,0},{8,4},{12,8},{1,13},{5,1},{9,5},{13,9},{2,14},{6,2},{... | collective-permute-start | bytes 786440 | tf_op jit(solution)/shard_map/ppermute | solution.py:487
  10.9 0.7 copy-start.6
  11.7 0.7 copy-start.7
  13.2 9.4 %collective-permute-start.1 = (bf16[64,128]{1,0:T(8,128)(2,1)S(1)}, bf16[64,128]{1,0:T(8,128)(2,1)S(1)}, u32[]{:S(2)}, u32[]{:S(2)}) collective-permute-start(bf16[64,128]{1,0:T(8,128)(2,1)S(1)} %get-tuple-element.37), channel_id=1, source_target_pairs={{0,12},{4,0},{8,4},{12,8},{1,13},{5,1},{9,5},{13,9},{2,14},{6,2},{... | collective-permute-start | bytes 49160 | tf_op jit(solution)/shard_map/ppermute | solution.py:487
  15.3 9.5 %collective-permute-start.3 = (bf16[64,128]{1,0:T(8,128)(2,1)S(1)}, bf16[64,128]{1,0:T(8,128)(2,1)S(1)}, u32[]{:S(2)}, u32[]{:S(2)}) collective-permute-start(bf16[64,128]{1,0:T(8,128)(2,1)S(1)} %get-tuple-element.38), channel_id=1, source_target_pairs={{0,4},{4,8},{8,12},{12,0},{1,5},{5,9},{9,13},{13,1},{2,6},{6,10},{... | collective-permute-start | bytes 49160 | tf_op jit(solution)/shard_map/ppermute | solution.py:487
  15.3 32.4 %collective-permute-start.2 = (bf16[1088,128]{1,0:T(8,128)(2,1)S(1)}, bf16[1088,128]{1,0:T(8,128)(2,1)S(1)}, u32[]{:S(2)}, u32[]{:S(2)}) collective-permute-start(bf16[1088,128]{1,0:T(8,128)(2,1)S(1)} %pad_maximum_fusion), channel_id=1, source_target_pairs={{0,8},{4,12},{8,0},{12,4},{1,9},{5,13},{9,1},{13,5},{2,10},{6,14},... | collective-permute-start | bytes 835592 | tf_op jit(solution)/shard_map/ppermute | solution.py:487
  25.1 10.0 %collective-permute-start.6 = (bf16[3,272,128]{2,1,0:T(8,128)(2,1)S(1)}, bf16[3,272,128]{2,1,0:T(8,128)(2,1)S(1)}, u32[]{:S(2)}, u32[]{:S(2)}) collective-permute-start(bf16[3,272,128]{2,1,0:T(8,128)(2,1)S(1)} %bitcast.47), channel_id=1, source_target_pairs={{0,2},{2,0},{1,3},{3,1},{4,6},{6,4},{5,7},{7,5},{8,10},{10,8},{9,1... | collective-permute-start | bytes 626696 | tf_op jit(solution)/shard_map/ppermute | solution.py:582
  27.1 37.9 %collective-permute-start.9 = (bf16[3,128,128]{2,1,0:T(8,128)(2,1)S(1)}, bf16[3,128,128]{2,1,0:T(8,128)(2,1)S(1)}, u32[]{:S(2)}, u32[]{:S(2)}) collective-permute-start(bf16[3,128,128]{2,1,0:T(8,128)(2,1)S(1)} %get-tuple-element.30), channel_id=1, source_target_pairs={{0,4},{4,8},{8,12},{12,0},{1,5},{5,9},{9,13},{13,1},{2,6},{6,10},{... | collective-permute-start | bytes 294920 | tf_op jit(solution)/shard_map/ppermute | solution.py:487
  29.7 35.3 %collective-permute-start.8 = (bf16[3,128,128]{2,1,0:T(8,128)(2,1)S(1)}, bf16[3,128,128]{2,1,0:T(8,128)(2,1)S(1)}, u32[]{:S(2)}, u32[]{:S(2)}) collective-permute-start(bf16[3,128,128]{2,1,0:T(8,128)(2,1)S(1)} %get-tuple-element.31), channel_id=1, source_target_pairs={{0,8},{4,12},{8,0},{12,4},{1,9},{5,13},{9,1},{13,5},{2,10},{6,14},... | collective-permute-start | bytes 294920 | tf_op jit(solution)/shard_map/ppermute | solution.py:487
  32.2 32.8 %collective-permute-start.7 = (bf16[3,128,128]{2,1,0:T(8,128)(2,1)S(1)}, bf16[3,128,128]{2,1,0:T(8,128)(2,1)S(1)}, u32[]{:S(2)}, u32[]{:S(2)}) collective-permute-start(bf16[3,128,128]{2,1,0:T(8,128)(2,1)S(1)} %get-tuple-element.32), channel_id=1, source_target_pairs={{0,12},{4,0},{8,4},{12,8},{1,13},{5,1},{9,5},{13,9},{2,14},{6,2},{... | collective-permute-start | bytes 294920 | tf_op jit(solution)/shard_map/ppermute | solution.py:487
  48.1 4.4 %collective-permute-start.10 = (bf16[1,272,128]{2,1,0:T(8,128)(2,1)S(1)}, bf16[1,272,128]{2,1,0:T(8,128)(2,1)S(1)}, u32[]{:S(2)}, u32[]{:S(2)}) collective-permute-start(bf16[1,272,128]{2,1,0:T(8,128)(2,1)S(1)} %bitcast.46), channel_id=1, source_target_pairs={{0,2},{2,0},{1,3},{3,1},{4,6},{6,4},{5,7},{7,5},{8,10},{10,8},{9,1... | collective-permute-start | bytes 208904 | tf_op jit(solution)/shard_map/ppermute | solution.py:582
  67.3 3.1 %collective-permute-start.16 = (f32[8,128]{1,0:T(8,128)S(1)}, f32[8,128]{1,0:T(8,128)S(1)}, u32[]{:S(2)}, u32[]{:S(2)}) collective-permute-start(f32[8,128]{1,0:T(8,128)S(1)} %get-tuple-element.25), channel_id=1, source_target_pairs={{0,3},{1,0},{2,1},{3,2},{4,7},{5,4},{6,5},{7,6},{8,11},{9,8},{10,9... | collective-permute-start | bytes 12296 | tf_op jit(solution)/shard_map/ppermute | solution.py:667
  67.4 5.0 %collective-permute-start.15 = (f32[8,128]{1,0:T(8,128)S(1)}, f32[8,128]{1,0:T(8,128)S(1)}, u32[]{:S(2)}, u32[]{:S(2)}) collective-permute-start(f32[8,128]{1,0:T(8,128)S(1)} %get-tuple-element.25), channel_id=1, source_target_pairs={{0,2},{1,3},{2,0},{3,1},{4,6},{5,7},{6,4},{7,5},{8,10},{9,11},{10,... | collective-permute-start | bytes 12296 | tf_op jit(solution)/shard_map/ppermute | solution.py:667
  68.8 3.6 %collective-permute-start.14 = (f32[8,128]{1,0:T(8,128)S(1)}, f32[8,128]{1,0:T(8,128)S(1)}, u32[]{:S(2)}, u32[]{:S(2)}) collective-permute-start(f32[8,128]{1,0:T(8,128)S(1)} %get-tuple-element.25), channel_id=1, source_target_pairs={{0,1},{1,2},{2,3},{3,0},{4,5},{5,6},{6,7},{7,4},{8,9},{9,10},{10,1... | collective-permute-start | bytes 12296 | tf_op jit(solution)/shard_map/ppermute | solution.py:667
  68.9 12.5 %copy-start.3 = (f32[8,16,512]{2,1,0:T(8,128)S(1)}, f32[8,16,512]{2,1,0:T(8,128)}, u32[]{:S(2)}) copy-start(f32[8,16,512]{2,1,0:T(8,128)} %estimate.3) | copy-start | bytes 786436
  68.9 12.5 %copy-start.5 = (f32[8,16,512]{2,1,0:T(8,128)S(1)}, f32[8,16,512]{2,1,0:T(8,128)}, u32[]{:S(2)}) copy-start(f32[8,16,512]{2,1,0:T(8,128)} %direction.3) | copy-start | bytes 786436
  69.0 12.5 %collective-permute-start.13 = (f32[8,16,128]{2,1,0:T(8,128)S(1)}, f32[8,16,128]{2,1,0:T(8,128)S(1)}, u32[]{:S(2)}, u32[]{:S(2)}) collective-permute-start(f32[8,16,128]{2,1,0:T(8,128)S(1)} %get-tuple-element.33), channel_id=1, source_target_pairs={{0,12},{4,0},{8,4},{12,8},{1,13},{5,1},{9,5},{13,9},{2,14},{6,2},{... | collective-permute-start | bytes 196616 | tf_op jit(solution)/shard_map/ppermute | solution.py:487
  69.0 12.4 %collective-permute-start.12 = (f32[8,16,128]{2,1,0:T(8,128)S(1)}, f32[8,16,128]{2,1,0:T(8,128)S(1)}, u32[]{:S(2)}, u32[]{:S(2)}) collective-permute-start(f32[8,16,128]{2,1,0:T(8,128)S(1)} %get-tuple-element.34), channel_id=1, source_target_pairs={{0,8},{4,12},{8,0},{12,4},{1,9},{5,13},{9,1},{13,5},{2,10},{6,14},... | collective-permute-start | bytes 196616 | tf_op jit(solution)/shard_map/ppermute | solution.py:487
  70.4 11.1 %collective-permute-start.11 = (f32[8,16,128]{2,1,0:T(8,128)S(1)}, f32[8,16,128]{2,1,0:T(8,128)S(1)}, u32[]{:S(2)}, u32[]{:S(2)}) collective-permute-start(f32[8,16,128]{2,1,0:T(8,128)S(1)} %get-tuple-element.35), channel_id=1, source_target_pairs={{0,4},{4,8},{8,12},{12,0},{1,5},{5,9},{9,13},{13,1},{2,6},{6,10},{... | collective-permute-start | bytes 196616 | tf_op jit(solution)/shard_map/ppermute | solution.py:487
  72.4 3.7 %collective-permute-start.19 = (f32[8,128]{1,0:T(8,128)S(1)}, f32[8,128]{1,0:T(8,128)S(1)}, u32[]{:S(2)}, u32[]{:S(2)}) collective-permute-start(f32[8,128]{1,0:T(8,128)S(1)} %add_add_fusion.refs_4_), channel_id=1, source_target_pairs={{0,12},{4,0},{8,4},{12,8},{1,13},{5,1},{9,5},{13,9},{2,14},{6,2},{... | collective-permute-start | bytes 12296 | tf_op jit(solution)/shard_map/ppermute | solution.py:487
  74.3 4.5 %collective-permute-start.18 = (f32[8,128]{1,0:T(8,128)S(1)}, f32[8,128]{1,0:T(8,128)S(1)}, u32[]{:S(2)}, u32[]{:S(2)}) collective-permute-start(f32[8,128]{1,0:T(8,128)S(1)} %add_add_fusion.refs_4_), channel_id=1, source_target_pairs={{0,8},{4,12},{8,0},{12,4},{1,9},{5,13},{9,1},{13,5},{2,10},{6,14},... | collective-permute-start | bytes 12296 | tf_op jit(solution)/shard_map/ppermute | solution.py:487
  76.1 5.4 %collective-permute-start.17 = (f32[8,128]{1,0:T(8,128)S(1)}, f32[8,128]{1,0:T(8,128)S(1)}, u32[]{:S(2)}, u32[]{:S(2)}) collective-permute-start(f32[8,128]{1,0:T(8,128)S(1)} %add_add_fusion.refs_4_), channel_id=1, source_target_pairs={{0,4},{4,8},{8,12},{12,0},{1,5},{5,9},{9,13},{13,1},{2,6},{6,10},{... | collective-permute-start | bytes 12296 | tf_op jit(solution)/shard_map/ppermute | solution.py:487

commit v4 on v3

--- a/solution.py
+++ b/solution.py
@@ -210,14 +210,15 @@
     epochs, rows, operands = sizes
     inputs = refs[:operands]
     factors, pulls = refs[operands : operands + 2]
-    full, rim_full, main, rim, looked, rim_looked, power, rim_power, power_box = refs[operands + 2 :]
+    full, rim_full, main, rim, looked, rim_looked, wide, outer, boxed, power_box = refs[operands + 2 :]
     count = len(places)
     look_rows = rows // LOOK
     tall = (rows + 2 * HALO) // LOOK
-    halo_looks = HALO // LOOK
+    first_look = HALO // LOOK - RADIUS
     total = count * epochs
     own_total = total - epochs
     group = 2 * SLOTS
+    group_rows = group * tall
     share = LANES // SLOTS
     has_top = present[0]
     has_bottom = present[1]
@@ -237,51 +238,47 @@
 
     band = band_of((2 * LANES, LANES), lambda at, to: at % LANES, lambda to: to)
     rim_band = band_of((2 * LANES, SLOTS * LANES), rim_column, lambda to: to % LANES)
-    out_at = lax.broadcasted_iota(jnp.int32, (group * look_rows, group * tall), 0)
-    in_at = lax.broadcasted_iota(jnp.int32, (group * look_rows, group * tall), 1)
-    near = jnp.abs(in_at % tall - halo_looks - out_at % look_rows) <= RADIUS
-    near = near & (in_at // tall == out_at // look_rows)
-    sum_rows = near.astype(f32).astype(jnp.bfloat16)
 
     lane = lax.broadcasted_iota(jnp.int32, (tall, LANES), 1)
     for block, (tile_at, strip_at, strip_row, top_at, bottom_at, halo_slot) in enumerate(places):
         tile, strip, top, bottom = inputs[tile_at], inputs[strip_at], inputs[top_at], inputs[bottom_at]
-        for part in range(2):
-
-            @pl.loop(0, epochs)
-            def _(epoch):
-                at = part * total + block * epochs + epoch
-                row = pl.multiple_of((part * epochs + epoch) * HALO, HALO)
-                own = pl.multiple_of((part * epochs + epoch) * rows, rows)
-                full[at, :HALO] = top[halo_slot, pl.ds(row, HALO), :].astype(f32) * has_top
-                full[at, HALO : HALO + rows] = tile[pl.ds(own, rows), :].astype(f32)
-                full[at, HALO + rows :] = bottom[halo_slot, pl.ds(row, HALO), :].astype(f32) * has_bottom
+
+        @pl.loop(0, 2 * epochs, unroll=4)
+        def _(at):
+            row = pl.multiple_of(at * HALO, HALO)
+            own = pl.multiple_of(at * rows, rows)
+            at = at + block * 2 * epochs
+            full[at, :HALO] = top[halo_slot, pl.ds(row, HALO), :].astype(f32) * has_top
+            full[at, HALO : HALO + rows] = tile[pl.ds(own, rows), :].astype(f32)
+            full[at, HALO + rows :] = bottom[halo_slot, pl.ds(row, HALO), :].astype(f32) * has_bottom
 
         last = slice(2 * epochs * HALO, 2 * epochs * HALO + HALO)
         rim_full[block, :HALO] = top[halo_slot, last, :].astype(f32) * has_top
         rim_full[block, HALO : HALO + rows] = strip[strip_row : strip_row + rows, :].astype(f32)
         rim_full[block, HALO + rows :] = bottom[halo_slot, last, :].astype(f32) * has_bottom
 
-    @pl.loop(0, 2 * total)
+    def places_of(epoch):
+        at = epoch // epochs * (2 * epochs) + epoch % epochs
+        return at, at + epochs
+
+    @pl.loop(0, 2 * total, unroll=4)
     def _(at):
         for look in range(LOOK):
             main[at, look] = full[at, pl.ds(look, tall, stride=LOOK), :]
 
     for block in range(count):
         by_look = [rim_full[block, pl.ds(look, tall, stride=LOOK), :] for look in range(LOOK)]
-        for part in range(2):
-            for epoch in range(epochs):
-                start = (part * epochs + epoch) * SIDES
-                value = jnp.zeros((tall, LANES), f32)
-                for look in range(LOOK):
-                    target = look * SIDES
-                    moved = pltpu.roll(by_look[look], (target - start) % LANES, axis=1)
-                    value = jnp.where((lane >= target) & (lane < target + SIDES), moved, value)
-                spread = share
-                while spread < LANES:
-                    value = value + pltpu.roll(value, spread, axis=1)
-                    spread = 2 * spread
-                rim[part * total + block * epochs + epoch] = value
+        for at in range(2 * epochs):
+            value = jnp.zeros((tall, LANES), f32)
+            for look in range(LOOK):
+                target = look * SIDES
+                moved = pltpu.roll(by_look[look], (target - at * SIDES) % LANES, axis=1)
+                value = jnp.where((lane >= target) & (lane < target + SIDES), moved, value)
+            spread = share
+            while spread < LANES:
+                value = value + pltpu.roll(value, spread, axis=1)
+                spread = 2 * spread
+            rim[block * 2 * epochs + at] = value
 
     piece_lane = lax.broadcasted_iota(jnp.int32, (8, LANES), 1)
     slot_lane = [piece_lane // share == slot for slot in range(SLOTS)]
@@ -292,88 +289,116 @@
             result = jnp.where(slot_lane[slot], values[slot], result)
         return result
 
-    @pl.loop(0, total // SLOTS)
-    def _(quad):
+    def channel_rows(batch, piece, channel):
+        return pl.ds(batch * group_rows + piece * group + channel, 8, stride=group)
+
+    for block in range(count):
         for piece in range(0, tall, 8):
             rows_at = slice(piece, piece + 8)
-            squares = []
-            for extra in range(SLOTS):
-                epoch = quad * SLOTS + extra
-                value = None
-                for look in range(LOOK):
-                    real = main[epoch, look, rows_at]
-                    imag = main[total + epoch, look, rows_at]
-                    one = real * real + imag * imag
-                    value = one if value is None else value + one
-                power[pl.ds(pl.multiple_of(epoch * tall + piece, 8), 8), :] = value
-                real = rim[epoch, rows_at]
-                imag = rim[total + epoch, rows_at]
-                squares.append(real * real + imag * imag)
-            rim_power[pl.ds(pl.multiple_of(quad * tall + piece, 8), 8), :] = mixed(squares)
+            for half in range(2):
+                squares = []
+                for slot in range(SLOTS):
+                    channel = half * SLOTS + slot
+                    re_at, im_at = places_of(block * epochs + channel)
+                    value = None
+                    for look in range(LOOK):
+                        real = main[re_at, look, rows_at]
+                        imag = main[im_at, look, rows_at]
+                        one = real * real + imag * imag
+                        value = one if value is None else value + one
+                    looked[channel_rows(block, piece, channel), :] = value
+                    real = rim[re_at, rows_at]
+                    imag = rim[im_at, rows_at]
+                    squares.append(real * real + imag * imag)
+                at = block * 2 * tall + half * tall + piece
+                rim_looked[at : at + 8, :] = mixed(squares)
 
     @pl.loop(0, own_total)
     def _(epoch):
-        mates = [partner[epoch * SLOTS + slot] for slot in range(SLOTS)]
+        batch = count + epoch
+        re_at, im_at = places_of(epoch)
+        mates = [places_of(partner[epoch * SLOTS + slot]) for slot in range(SLOTS)]
         for piece in range(0, tall, 8):
             rows_at = slice(piece, piece + 8)
-            own_re = [main[epoch, look, rows_at] for look in range(LOOK)]
-            own_im = [main[total + epoch, look, rows_at] for look in range(LOOK)]
-            for slot, mate in enumerate(mates):
+            own_re = [main[re_at, look, rows_at] for look in range(LOOK)]
+            own_im = [main[im_at, look, rows_at] for look in range(LOOK)]
+            for slot, (mate_re_at, mate_im_at) in enumerate(mates):
                 real = None
                 for look in range(LOOK):
-                    mate_re = main[mate, look, rows_at]
-                    mate_im = main[total + mate, look, rows_at]
+                    mate_re = main[mate_re_at, look, rows_at]
+                    mate_im = main[mate_im_at, look, rows_at]
                     one = own_re[look] * mate_re + own_im[look] * mate_im
                     two = own_im[look] * mate_re - own_re[look] * mate_im
                     real = one if real is None else real + one
                     imag = two if look == 0 else imag + two
-                at = pl.multiple_of(epoch * (group * tall) + 2 * slot * tall + piece, 8)
-                looked[pl.ds(at, 8), :] = real
-                at = pl.multiple_of(epoch * (group * tall) + (2 * slot + 1) * tall + piece, 8)
-                looked[pl.ds(at, 8), :] = imag
-            rim_re = rim[epoch, rows_at]
-            rim_im = rim[total + epoch, rows_at]
-            mate_re = mixed([rim[mate, rows_at] for mate in mates])
-            mate_im = mixed([rim[total + mate, rows_at] for mate in mates])
-            at = pl.multiple_of(epoch * (2 * tall) + piece, 8)
+                looked[channel_rows(batch, piece, slot), :] = real
+                looked[channel_rows(batch, piece, SLOTS + slot), :] = imag
+            rim_re = rim[re_at, rows_at]
+            rim_im = rim[im_at, rows_at]
+            mate_re = mixed([rim[at, rows_at] for at, _ in mates])
+            mate_im = mixed([rim[at, rows_at] for _, at in mates])
+            at = pl.multiple_of(batch * (2 * tall) + piece, 8)
             rim_looked[pl.ds(at, 8), :] = rim_re * mate_re + rim_im * mate_im
-            at = pl.multiple_of(epoch * (2 * tall) + tall + piece, 8)
+            at = pl.multiple_of(batch * (2 * tall) + tall + piece, 8)
             rim_looked[pl.ds(at, 8), :] = rim_im * mate_re - rim_re * mate_im
 
-    def box(value, rim_value, by_slot):
-        wide = jnp.dot(jnp.concatenate(split_two(value), axis=1), band, preferred_element_type=f32)
-        outer = jnp.dot(jnp.concatenate(split_two(rim_value), axis=1), rim_band, preferred_element_type=f32)
-        order = []
-        for at in range(group):
-            half, slot = (at % 2, at // 2) if by_slot else (at // SLOTS, at % SLOTS)
-            order.append(outer[half * tall : (half + 1) * tall, slot * LANES : (slot + 1) * LANES])
-        high, low = split_two(wide + jnp.concatenate(order, axis=0))
-        return jnp.dot(sum_rows, high, preferred_element_type=f32) + jnp.dot(sum_rows, low, preferred_element_type=f32)
-
-    for block in range(total // group):
-        here = slice(block * group * tall, (block + 1) * group * tall)
-        value = box(power[here, :], rim_power[2 * block * tall : 2 * (block + 1) * tall, :], False)
-        for at in range(group):
-            power_box[block * group + at] = value[at * look_rows : (at + 1) * look_rows]
+    def columns_summed(batch, batches):
+        at = pl.ds(pl.multiple_of(batch * group_rows, group_rows), batches * group_rows)
+        halves = jnp.concatenate(split_two(looked[at, :]), axis=1)
+        wide[at, :] = jnp.dot(halves, band, preferred_element_type=f32)
+        rim_at = pl.ds(pl.multiple_of(batch * (2 * tall), 2 * tall), batches * 2 * tall)
+        halves = jnp.concatenate(split_two(rim_looked[rim_at, :]), axis=1)
+        value = jnp.dot(halves, rim_band, preferred_element_type=f32)
+        for one in range(batches):
+            for half in range(2):
+                for piece in range(0, tall, 8):
+                    row = (2 * one + half) * tall + piece
+                    for slot in range(SLOTS):
+                        to = channel_rows(batch + one, piece, half * SLOTS + slot)
+                        outer[to, :] = value[row : row + 8, slot * LANES : (slot + 1) * LANES]
+
+    columns_summed(0, count)
 
     @pl.loop(0, own_total // 4)
     def _(quad):
-        for extra in range(4):
-            epoch = quad * 4 + extra
-            at = pl.multiple_of(epoch * (group * tall), group * tall)
-            rim_at = pl.multiple_of(epoch * (2 * tall), 2 * tall)
-            boxed = box(looked[pl.ds(at, group * tall), :], rim_looked[pl.ds(rim_at, 2 * tall), :], True)
-            own_power = power_box[epoch]
-            for slot in range(SLOTS):
-                pair = epoch * SLOTS + slot
-                coh_re = boxed[2 * slot * look_rows : (2 * slot + 1) * look_rows, :]
-                coh_im = boxed[(2 * slot + 1) * look_rows : (2 * slot + 2) * look_rows, :]
-                inverse = lax.rsqrt(own_power * power_box[partner[pair]] + EPSILON)
-                unit_re = coh_re * inverse
-                unit_im = coh_im * inverse
-                factor = weight[pair] * (unit_re * unit_re + unit_im * unit_im)
-                factors[pair] = factor
-                pulls[pair] = factor * unit_im
+        columns_summed(count + quad * 4, 4)
+
+    def rows_summed(batch):
+        values = []
+        for look in range(tall):
+            at = pl.ds(pl.multiple_of(batch * group_rows + look * group, group), group)
+            values.append(wide[at, :] + outer[at, :])
+        twos = {look: values[look] + values[look + 1] for look in range(first_look, tall - 2)}
+        fours = {look: twos[look] + twos[look + 2] for look in range(first_look, tall - 4)}
+        for out in range(look_rows):
+            at = out + first_look
+            seven = fours[at] + twos[at + 4] + values[at + 6]
+            to = pl.ds(pl.multiple_of((batch * look_rows + out) * group, group), group)
+            boxed[to, :] = seven
+
+    def box_of(batch, channel):
+        return boxed[pl.ds(batch * (look_rows * group) + channel, look_rows, stride=group), :]
+
+    for block in range(count):
+        rows_summed(block)
+        for channel in range(epochs):
+            power_box[block * epochs + channel] = box_of(block, channel)
+
+    @pl.loop(0, own_total, unroll=2)
+    def _(epoch):
+        rows_summed(count + epoch)
+
+    @pl.loop(0, own_total, unroll=2)
+    def _(epoch):
+        own_power = power_box[epoch]
+        for slot in range(SLOTS):
+            pair = epoch * SLOTS + slot
+            inverse = lax.rsqrt(own_power * power_box[partner[pair]] + EPSILON)
+            unit_re = box_of(count + epoch, slot) * inverse
+            unit_im = box_of(count + epoch, SLOTS + slot) * inverse
+            factor = weight[pair] * (unit_re * unit_re + unit_im * unit_im)
+            factors[pair] = factor
+            pulls[pair] = factor * unit_im
 
 
 def gradient_kernel(sizes, partner, *refs):
@@ -617,6 +642,7 @@
         here = len(loaded) * epochs
         owned = len(own) * epochs
         group = 2 * SLOTS
+        batches = len(loaded) + owned
         shape = jax.ShapeDtypeStruct((owned * SLOTS, look_rows, LANES), f32)
         return pl.pallas_call(
             functools.partial(pair_kernel, (epochs, rows, len(operands)), tuple(places)),
@@ -628,10 +654,11 @@
                 pltpu.VMEM((len(loaded), rows + 2 * HALO, LANES), f32),
                 pltpu.VMEM((2 * here, LOOK, tall, LANES), f32),
                 pltpu.VMEM((2 * here, tall, LANES), f32),
-                pltpu.VMEM((owned * group * tall, LANES), f32),
-                pltpu.VMEM((owned * 2 * tall, LANES), f32),
-                pltpu.VMEM((here * tall, LANES), f32),
-                pltpu.VMEM((here // SLOTS * tall, LANES), f32),
+                pltpu.VMEM((batches * group * tall, LANES), f32),
+                pltpu.VMEM((batches * 2 * tall, LANES), f32),
+                pltpu.VMEM((batches * group * tall, LANES), f32),
+                pltpu.VMEM((batches * group * tall, LANES), f32),
+                pltpu.VMEM((batches * group * look_rows, LANES), f32),
                 pltpu.VMEM((here, look_rows, LANES), f32),
             ],
             compiler_params=params_of,
@@ -683,7 +710,7 @@
 def on_device(slc, offsets, weights, estimate, direction, prev_mean):
     epochs, rows, columns = slc.shape[1:]
     fits = columns == LANES * lax.axis_size("epoch") and lax.axis_size("epoch") > 3
-    fits = fits and 2 * epochs * SIDES <= PARAM_LANE and rows % HALO == 0 and epochs % (2 * SLOTS) == 0
+    fits = fits and 2 * epochs * SIDES <= PARAM_LANE and rows % HALO == 0 and epochs == 2 * SLOTS
     plan = transposed_plan if fits else ring_plan
     return plan(slc, offsets, weights, estimate, direction, prev_mean)
 

time: 82.7 us -> 78.3 us (0.947)
  Pallas kernels: 29 us -> 24.6 us
    pallas_call x2, Pallas kernels: 25.2 us -> 20.7 us  [pair_stage(): pl.pallas_call(functools.partial(pair_kernel, (epochs, rows, len(operands...]
  transfers between devices with their start and end apart: 20 -> 20, of which waited for: 6 -> 6; matrix products, arithmetic and copies ran while one was open for 3% -> 3% of each run, Pallas kernels for 31% -> 27%
where the time goes in v4:
time: 78.3 us; the launch traced here: 78 us
  starting transfers between devices  27.3 us (35%)
  Pallas kernels  24.6 us (31%)
  waiting for transfers between devices  17.2 us (22%)
  local copies, waits for them, and re-layouts  6.71 us (9%)
  between operations  1.53 us (2%)
    ppermute x14, starting transfers between devices, to_ahead(): return lax.ppermute(x, axis, [(i, (i + by) % size) for i in range(size)])  22 us
    pallas_call x2, Pallas kernels, pair_stage(): pl.pallas_call(functools.partial(pair_kernel, (epochs, rows, len(operands...  20.7 us
    ppermute x14, waiting for transfers between devices, to_ahead(): return lax.ppermute(x, axis, [(i, (i + by) % size) for i in range(size)])  14.3 us
    unnamed x23, local copies, waits for them, and re-layouts  5.21 us
    ppermute x2, starting transfers between devices, halo(): got = lax.ppermute(mine, 'space', [(0, 1), (1, 0)])  3.2 us
    ppermute x2, waiting for transfers between devices, halo(): got = lax.ppermute(mine, 'space', [(0, 1), (1, 0)])  2.89 us
    pallas_call x1, Pallas kernels, transposed_plan(): pl.pallas_call(functools.partial(gradient_kernel, (tiles, epochs, stages)...  2.24 us
    ppermute x3, starting transfers between devices, transposed_plan(): lax.ppermute(sums, place, [(i, (i + by) % count) for i in range(count)])  1.62 us
  transfers between devices with their start and end apart: 20, of which 6 were waited for; matrix products, arithmetic and copies ran while one was open for 3% of the time, Pallas kernels for 27%

profile of v4, /device:TPU:0, one launch (start us, length us, event | category | flops | bytes accessed | tf_op | source)
XLA Modules:
  0.0 78.0 jit_solution(14191334264214034386)
XLA Ops:
  0.6 1.2 %copy-done = bf16[2,8,64,512]{3,2,1,0:T(8,128)(2,1)S(1)} copy-done((bf16[2,8,64,512]{3,2,1,0:T(8,128)(2,1)S(1)}, bf16[2,8,64,512]{3,2,1,0:T(8,128)(2,1)}, u32[]{:S(2)}) %copy-start) | copy-done | bytes 1048600
  1.9 0.9 %copy-done.2 = f32[8,16,512]{2,1,0:T(8,128)S(1)} copy-done((f32[8,16,512]{2,1,0:T(8,128)S(1)}, f32[8,16,512]{2,1,0:T(8,128)}, u32[]{:S(2)}) %copy-start.2) | copy-done | bytes 262168
  2.8 0.9 %copy-done.4 = f32[8,16,512]{2,1,0:T(8,128)S(1)} copy-done((f32[8,16,512]{2,1,0:T(8,128)S(1)}, f32[8,16,512]{2,1,0:T(8,128)}, u32[]{:S(2)}) %copy-start.4) | copy-done | bytes 262168
  3.8 0.2 shard_map.77
  4.0 0.5 collective-permute-start
  4.5 0.5 copy-done.1
  5.0 0.9 %constant_dynamic-slice_fusion.3 = (bf16[2,8,64,128]{3,2,1,0:T(8,128)(2,1)S(1)}, bf16[2,8,64,128]{3,2,1,0:T(8,128)(2,1)}, bf16[2,8,64,128]{3,2,1,0:T(8,128)(2,1)S(1)}, bf16[2,8,64,128]{3,2,1,0:T(8,128)(2,1)S(1)}) fusion(bf16[2,8,64,512]{3,2,1,0:T(8,128)(2,1)S(1)} %copy-done.1, s32[]{:T(128)S(6)} %select_n.81, s32[]{:T(128)S(6)} %select_n.76, ...), kind=kLoop, calls=%fused_computation.70 | loop fusion | bytes 2097168 | tf_op jit(solution)/shard_map/dynamic_slice | solution.py:531
  5.9 3.0 %collective-permute-start.4 = (bf16[1024,128]{1,0:T(8,128)(2,1)}, bf16[1024,128]{1,0:T(8,128)(2,1)S(1)}, u32[]{:S(2)}, u32[]{:S(2)}) collective-permute-start(bf16[1024,128]{1,0:T(8,128)(2,1)} %bitcast.8), channel_id=1, source_target_pairs={{0,4},{4,8},{8,12},{12,0},{1,5},{5,9},{9,13},{13,1},{2,6},{6,10},{... | collective-permute-start | bytes 786440 | tf_op jit(solution)/shard_map/ppermute | solution.py:512
  8.9 2.0 %collective-permute-start.5 = (bf16[1024,128]{1,0:T(8,128)(2,1)S(1)}, bf16[1024,128]{1,0:T(8,128)(2,1)S(1)}, u32[]{:S(2)}, u32[]{:S(2)}) collective-permute-start(bf16[1024,128]{1,0:T(8,128)(2,1)S(1)} %bitcast.42), channel_id=1, source_target_pairs={{0,12},{4,0},{8,4},{12,8},{1,13},{5,1},{9,5},{13,9},{2,14},{6,2},{... | collective-permute-start | bytes 786440 | tf_op jit(solution)/shard_map/ppermute | solution.py:512
  10.9 0.7 copy-done.6
  11.6 0.1 copy.12
  11.7 0.7 copy-done.7
  12.4 0.1 copy.13
  12.5 0.1 select_maximum_fusion.params
  12.5 0.1 add_convert_fusion.present
  12.6 0.5 shard_map.78
  13.2 0.1 slice_convert_fusion.2
  13.2 2.0 %collective-permute-start.1 = (bf16[64,128]{1,0:T(8,128)(2,1)S(1)}, bf16[64,128]{1,0:T(8,128)(2,1)S(1)}, u32[]{:S(2)}, u32[]{:S(2)}) collective-permute-start(bf16[64,128]{1,0:T(8,128)(2,1)S(1)} %get-tuple-element.37), channel_id=1, source_target_pairs={{0,12},{4,0},{8,4},{12,8},{1,13},{5,1},{9,5},{13,9},{2,14},{6,2},{... | collective-permute-start | bytes 49160 | tf_op jit(solution)/shard_map/ppermute | solution.py:512
  15.3 1.1 %collective-permute-start.2 = (bf16[1088,128]{1,0:T(8,128)(2,1)S(1)}, bf16[1088,128]{1,0:T(8,128)(2,1)S(1)}, u32[]{:S(2)}, u32[]{:S(2)}) collective-permute-start(bf16[1088,128]{1,0:T(8,128)(2,1)S(1)} %pad_maximum_fusion), channel_id=1, source_target_pairs={{0,8},{4,12},{8,0},{12,4},{1,9},{5,13},{9,1},{13,5},{2,10},{6,14},... | collective-permute-start | bytes 835592 | tf_op jit(solution)/shard_map/ppermute | solution.py:512
  16.4 6.3 %collective-permute-done.1.refs_6_.refs_1_ = bf16[64,128]{1,0:T(8,128)(2,1)S(1)} collective-permute-done((bf16[64,128]{1,0:T(8,128)(2,1)S(1)}, bf16[64,128]{1,0:T(8,128)(2,1)S(1)}, u32[]{:S(2)}, u32[]{:S(2)}) %collective-permute-start.1) | collective-permute-done | bytes 16416 | tf_op jit(solution)/shard_map/ppermute | solution.py:512
  22.7 2.0 %collective-permute-done.3.refs_1_.refs_6_ = bf16[64,128]{1,0:T(8,128)(2,1)S(1)} collective-permute-done((bf16[64,128]{1,0:T(8,128)(2,1)S(1)}, bf16[64,128]{1,0:T(8,128)(2,1)S(1)}, u32[]{:S(2)}, u32[]{:S(2)}) %collective-permute-start.3) | collective-permute-done | bytes 16416 | tf_op jit(solution)/shard_map/ppermute | solution.py:512
  24.8 0.1 reshape.73.partner
  25.1 1.8 %collective-permute-start.6 = (bf16[3,272,128]{2,1,0:T(8,128)(2,1)S(1)}, bf16[3,272,128]{2,1,0:T(8,128)(2,1)S(1)}, u32[]{:S(2)}, u32[]{:S(2)}) collective-permute-start(bf16[3,272,128]{2,1,0:T(8,128)(2,1)S(1)} %bitcast.47), channel_id=1, source_target_pairs={{0,2},{2,0},{1,3},{3,1},{4,6},{6,4},{5,7},{7,5},{8,10},{10,8},{9,1... | collective-permute-start | bytes 626696 | tf_op jit(solution)/shard_map/ppermute | solution.py:607
  26.9 0.1 fusion.20
  27.0 0.1 reshape.74.weight
  27.1 2.6 %collective-permute-start.9 = (bf16[3,128,128]{2,1,0:T(8,128)(2,1)S(1)}, bf16[3,128,128]{2,1,0:T(8,128)(2,1)S(1)}, u32[]{:S(2)}, u32[]{:S(2)}) collective-permute-start(bf16[3,128,128]{2,1,0:T(8,128)(2,1)S(1)} %get-tuple-element.30), channel_id=1, source_target_pairs={{0,4},{4,8},{8,12},{12,0},{1,5},{5,9},{9,13},{13,1},{2,6},{6,10},{... | collective-permute-start | bytes 294920 | tf_op jit(solution)/shard_map/ppermute | solution.py:512
  29.7 2.5 %collective-permute-start.8 = (bf16[3,128,128]{2,1,0:T(8,128)(2,1)S(1)}, bf16[3,128,128]{2,1,0:T(8,128)(2,1)S(1)}, u32[]{:S(2)}, u32[]{:S(2)}) collective-permute-start(bf16[3,128,128]{2,1,0:T(8,128)(2,1)S(1)} %get-tuple-element.31), channel_id=1, source_target_pairs={{0,8},{4,12},{8,0},{12,4},{1,9},{5,13},{9,1},{13,5},{2,10},{6,14},... | collective-permute-start | bytes 294920 | tf_op jit(solution)/shard_map/ppermute | solution.py:512
  32.2 2.8 %collective-permute-start.7 = (bf16[3,128,128]{2,1,0:T(8,128)(2,1)S(1)}, bf16[3,128,128]{2,1,0:T(8,128)(2,1)S(1)}, u32[]{:S(2)}, u32[]{:S(2)}) collective-permute-start(bf16[3,128,128]{2,1,0:T(8,128)(2,1)S(1)} %get-tuple-element.32), channel_id=1, source_target_pairs={{0,12},{4,0},{8,4},{12,8},{1,13},{5,1},{9,5},{13,9},{2,14},{6,2},{... | collective-permute-start | bytes 294920 | tf_op jit(solution)/shard_map/ppermute | solution.py:512
  35.1 10.4 %shard_map.79 = (f32[64,16,128]{2,1,0:T(8,128)S(1)}, f32[64,16,128]{2,1,0:T(8,128)S(1)}) custom-call(s32[64]{0:T(128)S(1)} %reshape.73.partner, f32[64]{0:T(128)S(1)} %reshape.74.weight, f32[2]{0:T(128)S(1)} %add_convert_fusion.present, bf16[1024,128]{1,0:T(8,128)(2,1)S(1)} %collective-permute-done.4.refs_0_.refs_5_, ...), custom_call_target="tpu_custom_call" | custom-call | flops 20000000 | bytes 30000000 | tf_op jit(solution)/shard_map/pallas_call | solution.py:647
  45.5 0.1 slice_convert_fusion.3
  45.5 0.1 fusion.13
  45.6 0.1 reshape.87.partner
  45.7 0.1 reshape.89.weight
  45.8 1.4 %collective-permute-start.10 = (bf16[1,272,128]{2,1,0:T(8,128)(2,1)S(1)}, bf16[1,272,128]{2,1,0:T(8,128)(2,1)S(1)}, u32[]{:S(2)}, u32[]{:S(2)}) collective-permute-start(bf16[1,272,128]{2,1,0:T(8,128)(2,1)S(1)} %bitcast.46), channel_id=1, source_target_pairs={{0,2},{2,0},{1,3},{3,1},{4,6},{6,4},{5,7},{7,5},{8,10},{10,8},{9,1... | collective-permute-start | bytes 208904 | tf_op jit(solution)/shard_map/ppermute | solution.py:607
  47.2 0.1 reshape.88.partner
  47.3 2.9 %collective-permute-done.10.refs_4_ = bf16[1,272,128]{2,1,0:T(8,128)(2,1)S(1)} collective-permute-done((bf16[1,272,128]{2,1,0:T(8,128)(2,1)S(1)}, bf16[1,272,128]{2,1,0:T(8,128)(2,1)S(1)}, u32[]{:S(2)}, u32[]{:S(2)}) %collective-permute-start.10) | collective-permute-done | bytes 69664 | tf_op jit(solution)/shard_map/ppermute | solution.py:607
  50.2 10.4 %shard_map.80 = (f32[64,16,128]{2,1,0:T(8,128)S(1)}, f32[64,16,128]{2,1,0:T(8,128)S(1)}) custom-call(s32[64]{0:T(128)S(1)} %reshape.88.partner, f32[64]{0:T(128)S(1)} %reshape.89.weight, f32[2]{0:T(128)S(1)} %add_convert_fusion.present, bf16[1024,128]{1,0:T(8,128)(2,1)S(1)} %collective-permute-done.5.refs_5_.refs_0_, ...), custom_call_target="tpu_custom_call" | custom-call | flops 20000000 | bytes 30000000 | tf_op jit(solution)/shard_map/pallas_call | solution.py:647
  60.6 2.2 %shard_map.81 = (f32[32,16,128]{2,1,0:T(8,128)S(1)}, f32[8,128]{1,0:T(8,128)S(1)}) custom-call(s32[128]{0:T(128)S(1)} %reshape.87.partner, bf16[3,128,128]{2,1,0:T(8,128)(2,1)S(1)} %dynamic-slice_bitcast_fusion.3.refs_0_, bf16[3,128,128]{2,1,0:T(8,128)(2,1)S(1)} %collective-permute-done.7.refs_1_, bf16[3,128,128]{2,1,0:T(8,128)(2,1)S(1)} %collective-permute-done.8.refs_2_, ...), custom_call_target="tpu_custom_call" | custom-call | flops 10000000 | bytes 8000000 | tf_op jit(solution)/shard_map/pallas_call | solution.py:679
  62.9 1.4 %collective-permute-start.15 = (f32[8,128]{1,0:T(8,128)S(1)}, f32[8,128]{1,0:T(8,128)S(1)}, u32[]{:S(2)}, u32[]{:S(2)}) collective-permute-start(f32[8,128]{1,0:T(8,128)S(1)} %get-tuple-element.25), channel_id=1, source_target_pairs={{0,2},{1,3},{2,0},{3,1},{4,6},{5,7},{6,4},{7,5},{8,10},{9,11},{10,... | collective-permute-start | bytes 12296 | tf_op jit(solution)/shard_map/ppermute | solution.py:694
  64.3 0.2 collective-permute-start.14
  64.6 1.4 %collective-permute-start.12 = (f32[8,16,128]{2,1,0:T(8,128)S(1)}, f32[8,16,128]{2,1,0:T(8,128)S(1)}, u32[]{:S(2)}, u32[]{:S(2)}) collective-permute-start(f32[8,16,128]{2,1,0:T(8,128)S(1)} %get-tuple-element.34), channel_id=1, source_target_pairs={{0,8},{4,12},{8,0},{12,4},{1,9},{5,13},{9,1},{13,5},{2,10},{6,14},... | collective-permute-start | bytes 196616 | tf_op jit(solution)/shard_map/ppermute | solution.py:512
  65.9 1.9 %collective-permute-start.11 = (f32[8,16,128]{2,1,0:T(8,128)S(1)}, f32[8,16,128]{2,1,0:T(8,128)S(1)}, u32[]{:S(2)}, u32[]{:S(2)}) collective-permute-start(f32[8,16,128]{2,1,0:T(8,128)S(1)} %get-tuple-element.35), channel_id=1, source_target_pairs={{0,4},{4,8},{8,12},{12,0},{1,5},{5,9},{9,13},{13,1},{2,6},{6,10},{... | collective-permute-start | bytes 196616 | tf_op jit(solution)/shard_map/ppermute | solution.py:512
  67.9 1.9 %collective-permute-start.19 = (f32[8,128]{1,0:T(8,128)S(1)}, f32[8,128]{1,0:T(8,128)S(1)}, u32[]{:S(2)}, u32[]{:S(2)}) collective-permute-start(f32[8,128]{1,0:T(8,128)S(1)} %add_add_fusion.refs_4_), channel_id=1, source_target_pairs={{0,12},{4,0},{8,4},{12,8},{1,13},{5,1},{9,5},{13,9},{2,14},{6,2},{... | collective-permute-start | bytes 12296 | tf_op jit(solution)/shard_map/ppermute | solution.py:512
  69.8 1.8 %collective-permute-done.19.refs_7_ = f32[8,128]{1,0:T(8,128)S(1)} collective-permute-done((f32[8,128]{1,0:T(8,128)S(1)}, f32[8,128]{1,0:T(8,128)S(1)}, u32[]{:S(2)}, u32[]{:S(2)}) %collective-permute-start.19) | collective-permute-done | bytes 4128 | tf_op jit(solution)/shard_map/ppermute | solution.py:512
  71.6 0.6 collective-permute-start.17
  72.8 1.5 %collective-permute-done.18.refs_6_ = f32[8,128]{1,0:T(8,128)S(1)} collective-permute-done((f32[8,128]{1,0:T(8,128)S(1)}, f32[8,128]{1,0:T(8,128)S(1)}, u32[]{:S(2)}, u32[]{:S(2)}) %collective-permute-start.18) | collective-permute-done | bytes 4128 | tf_op jit(solution)/shard_map/ppermute | solution.py:512
  74.3 2.7 %collective-permute-done.17.refs_5_ = f32[8,128]{1,0:T(8,128)S(1)} collective-permute-done((f32[8,128]{1,0:T(8,128)S(1)}, f32[8,128]{1,0:T(8,128)S(1)}, u32[]{:S(2)}, u32[]{:S(2)}) %collective-permute-start.17) | collective-permute-done | bytes 4128 | tf_op jit(solution)/shard_map/ppermute | solution.py:512
  77.0 0.9 %shard_map.82 = (f32[8,16,512]{2,1,0:T(8,128)}, f32[8,16,512]{2,1,0:T(8,128)}) custom-call(s32[1]{0:T(128)} %bitcast.me, f32[1]{0:T(128)S(6)} %copy.21.prev_mean, f32[8,16,512]{2,1,0:T(8,128)S(1)} %copy-done.3, f32[8,16,512]{2,1,0:T(8,128)S(1)} %copy-done.5, f32[8,16,128]{2,1,0:T(8,128)S(1)} %get-tuple-element.36.refs_0_, ...), custom_call_target="tpu_custom_call" | custom-call | flops 1000000 | bytes 2000000 | tf_op jit(solution)/shard_map/pallas_call | solution.py:700
  (52 shorter events, 0.6 us)
Async XLA Ops:
  0.6 1.2 %copy-start = (bf16[2,8,64,512]{3,2,1,0:T(8,128)(2,1)S(1)}, bf16[2,8,64,512]{3,2,1,0:T(8,128)(2,1)}, u32[]{:S(2)}) copy-start(bf16[2,8,64,512]{3,2,1,0:T(8,128)(2,1)} %slc.3) | copy-start | bytes 3145732
  1.9 0.9 %copy-start.2 = (f32[8,16,512]{2,1,0:T(8,128)S(1)}, f32[8,16,512]{2,1,0:T(8,128)}, u32[]{:S(2)}) copy-start(f32[8,16,512]{2,1,0:T(8,128)} %estimate.3) | copy-start | bytes 786436
  2.8 0.9 %copy-start.4 = (f32[8,16,512]{2,1,0:T(8,128)S(1)}, f32[8,16,512]{2,1,0:T(8,128)}, u32[]{:S(2)}) copy-start(f32[8,16,512]{2,1,0:T(8,128)} %direction.3) | copy-start | bytes 786436
  3.8 1.2 %copy-start.1 = (bf16[2,8,64,512]{3,2,1,0:T(8,128)(2,1)S(1)}, bf16[2,8,64,512]{3,2,1,0:T(8,128)(2,1)}, u32[]{:S(2)}) copy-start(bf16[2,8,64,512]{3,2,1,0:T(8,128)(2,1)} %slc.3) | copy-start | bytes 3145732
  4.0 8.7 %collective-permute-start = (bf16[64,128]{1,0:T(8,128)(2,1)S(1)}, bf16[64,128]{1,0:T(8,128)(2,1)S(1)}, u32[]{:S(2)}, u32[]{:S(2)}) collective-permute-start(bf16[64,128]{1,0:T(8,128)(2,1)S(1)} %get-tuple-element.14), channel_id=1, source_target_pairs={{0,1},{1,0},{2,3},{3,2},{4,5},{5,4},{6,7},{7,6},{8,9},{9,8},{10,11... | collective-permute-start | bytes 49160 | tf_op jit(solution)/shard_map/ppermute | solution.py:503
  5.9 19.0 %collective-permute-start.4 = (bf16[1024,128]{1,0:T(8,128)(2,1)}, bf16[1024,128]{1,0:T(8,128)(2,1)S(1)}, u32[]{:S(2)}, u32[]{:S(2)}) collective-permute-start(bf16[1024,128]{1,0:T(8,128)(2,1)} %bitcast.8), channel_id=1, source_target_pairs={{0,4},{4,8},{8,12},{12,0},{1,5},{5,9},{9,13},{13,1},{2,6},{6,10},{... | collective-permute-start | bytes 786440 | tf_op jit(solution)/shard_map/ppermute | solution.py:512
  8.9 16.1 %collective-permute-start.5 = (bf16[1024,128]{1,0:T(8,128)(2,1)S(1)}, bf16[1024,128]{1,0:T(8,128)(2,1)S(1)}, u32[]{:S(2)}, u32[]{:S(2)}) collective-permute-start(bf16[1024,128]{1,0:T(8,128)(2,1)S(1)} %bitcast.42), channel_id=1, source_target_pairs={{0,12},{4,0},{8,4},{12,8},{1,13},{5,1},{9,5},{13,9},{2,14},{6,2},{... | collective-permute-start | bytes 786440 | tf_op jit(solution)/shard_map/ppermute | solution.py:512
  10.9 0.7 copy-start.6
  11.7 0.7 copy-start.7
  13.2 9.4 %collective-permute-start.1 = (bf16[64,128]{1,0:T(8,128)(2,1)S(1)}, bf16[64,128]{1,0:T(8,128)(2,1)S(1)}, u32[]{:S(2)}, u32[]{:S(2)}) collective-permute-start(bf16[64,128]{1,0:T(8,128)(2,1)S(1)} %get-tuple-element.37), channel_id=1, source_target_pairs={{0,12},{4,0},{8,4},{12,8},{1,13},{5,1},{9,5},{13,9},{2,14},{6,2},{... | collective-permute-start | bytes 49160 | tf_op jit(solution)/shard_map/ppermute | solution.py:512
  15.3 9.5 %collective-permute-start.3 = (bf16[64,128]{1,0:T(8,128)(2,1)S(1)}, bf16[64,128]{1,0:T(8,128)(2,1)S(1)}, u32[]{:S(2)}, u32[]{:S(2)}) collective-permute-start(bf16[64,128]{1,0:T(8,128)(2,1)S(1)} %get-tuple-element.38), channel_id=1, source_target_pairs={{0,4},{4,8},{8,12},{12,0},{1,5},{5,9},{9,13},{13,1},{2,6},{6,10},{... | collective-permute-start | bytes 49160 | tf_op jit(solution)/shard_map/ppermute | solution.py:512
  15.3 30.2 %collective-permute-start.2 = (bf16[1088,128]{1,0:T(8,128)(2,1)S(1)}, bf16[1088,128]{1,0:T(8,128)(2,1)S(1)}, u32[]{:S(2)}, u32[]{:S(2)}) collective-permute-start(bf16[1088,128]{1,0:T(8,128)(2,1)S(1)} %pad_maximum_fusion), channel_id=1, source_target_pairs={{0,8},{4,12},{8,0},{12,4},{1,9},{5,13},{9,1},{13,5},{2,10},{6,14},... | collective-permute-start | bytes 835592 | tf_op jit(solution)/shard_map/ppermute | solution.py:512
  25.1 10.0 %collective-permute-start.6 = (bf16[3,272,128]{2,1,0:T(8,128)(2,1)S(1)}, bf16[3,272,128]{2,1,0:T(8,128)(2,1)S(1)}, u32[]{:S(2)}, u32[]{:S(2)}) collective-permute-start(bf16[3,272,128]{2,1,0:T(8,128)(2,1)S(1)} %bitcast.47), channel_id=1, source_target_pairs={{0,2},{2,0},{1,3},{3,1},{4,6},{6,4},{5,7},{7,5},{8,10},{10,8},{9,1... | collective-permute-start | bytes 626696 | tf_op jit(solution)/shard_map/ppermute | solution.py:607
  27.1 33.5 %collective-permute-start.9 = (bf16[3,128,128]{2,1,0:T(8,128)(2,1)S(1)}, bf16[3,128,128]{2,1,0:T(8,128)(2,1)S(1)}, u32[]{:S(2)}, u32[]{:S(2)}) collective-permute-start(bf16[3,128,128]{2,1,0:T(8,128)(2,1)S(1)} %get-tuple-element.30), channel_id=1, source_target_pairs={{0,4},{4,8},{8,12},{12,0},{1,5},{5,9},{9,13},{13,1},{2,6},{6,10},{... | collective-permute-start | bytes 294920 | tf_op jit(solution)/shard_map/ppermute | solution.py:512
  29.7 30.9 %collective-permute-start.8 = (bf16[3,128,128]{2,1,0:T(8,128)(2,1)S(1)}, bf16[3,128,128]{2,1,0:T(8,128)(2,1)S(1)}, u32[]{:S(2)}, u32[]{:S(2)}) collective-permute-start(bf16[3,128,128]{2,1,0:T(8,128)(2,1)S(1)} %get-tuple-element.31), channel_id=1, source_target_pairs={{0,8},{4,12},{8,0},{12,4},{1,9},{5,13},{9,1},{13,5},{2,10},{6,14},... | collective-permute-start | bytes 294920 | tf_op jit(solution)/shard_map/ppermute | solution.py:512
  32.2 28.4 %collective-permute-start.7 = (bf16[3,128,128]{2,1,0:T(8,128)(2,1)S(1)}, bf16[3,128,128]{2,1,0:T(8,128)(2,1)S(1)}, u32[]{:S(2)}, u32[]{:S(2)}) collective-permute-start(bf16[3,128,128]{2,1,0:T(8,128)(2,1)S(1)} %get-tuple-element.32), channel_id=1, source_target_pairs={{0,12},{4,0},{8,4},{12,8},{1,13},{5,1},{9,5},{13,9},{2,14},{6,2},{... | collective-permute-start | bytes 294920 | tf_op jit(solution)/shard_map/ppermute | solution.py:512
  45.8 4.4 %collective-permute-start.10 = (bf16[1,272,128]{2,1,0:T(8,128)(2,1)S(1)}, bf16[1,272,128]{2,1,0:T(8,128)(2,1)S(1)}, u32[]{:S(2)}, u32[]{:S(2)}) collective-permute-start(bf16[1,272,128]{2,1,0:T(8,128)(2,1)S(1)} %bitcast.46), channel_id=1, source_target_pairs={{0,2},{2,0},{1,3},{3,1},{4,6},{6,4},{5,7},{7,5},{8,10},{10,8},{9,1... | collective-permute-start | bytes 208904 | tf_op jit(solution)/shard_map/ppermute | solution.py:607
  62.9 3.1 %collective-permute-start.16 = (f32[8,128]{1,0:T(8,128)S(1)}, f32[8,128]{1,0:T(8,128)S(1)}, u32[]{:S(2)}, u32[]{:S(2)}) collective-permute-start(f32[8,128]{1,0:T(8,128)S(1)} %get-tuple-element.25), channel_id=1, source_target_pairs={{0,3},{1,0},{2,1},{3,2},{4,7},{5,4},{6,5},{7,6},{8,11},{9,8},{10,9... | collective-permute-start | bytes 12296 | tf_op jit(solution)/shard_map/ppermute | solution.py:694
  62.9 5.0 %collective-permute-start.15 = (f32[8,128]{1,0:T(8,128)S(1)}, f32[8,128]{1,0:T(8,128)S(1)}, u32[]{:S(2)}, u32[]{:S(2)}) collective-permute-start(f32[8,128]{1,0:T(8,128)S(1)} %get-tuple-element.25), channel_id=1, source_target_pairs={{0,2},{1,3},{2,0},{3,1},{4,6},{5,7},{6,4},{7,5},{8,10},{9,11},{10,... | collective-permute-start | bytes 12296 | tf_op jit(solution)/shard_map/ppermute | solution.py:694
  64.3 3.6 %collective-permute-start.14 = (f32[8,128]{1,0:T(8,128)S(1)}, f32[8,128]{1,0:T(8,128)S(1)}, u32[]{:S(2)}, u32[]{:S(2)}) collective-permute-start(f32[8,128]{1,0:T(8,128)S(1)} %get-tuple-element.25), channel_id=1, source_target_pairs={{0,1},{1,2},{2,3},{3,0},{4,5},{5,6},{6,7},{7,4},{8,9},{9,10},{10,1... | collective-permute-start | bytes 12296 | tf_op jit(solution)/shard_map/ppermute | solution.py:694
  64.5 12.5 %copy-start.3 = (f32[8,16,512]{2,1,0:T(8,128)S(1)}, f32[8,16,512]{2,1,0:T(8,128)}, u32[]{:S(2)}) copy-start(f32[8,16,512]{2,1,0:T(8,128)} %estimate.3) | copy-start | bytes 786436
  64.5 12.5 %copy-start.5 = (f32[8,16,512]{2,1,0:T(8,128)S(1)}, f32[8,16,512]{2,1,0:T(8,128)}, u32[]{:S(2)}) copy-start(f32[8,16,512]{2,1,0:T(8,128)} %direction.3) | copy-start | bytes 786436
  64.5 12.5 %collective-permute-start.13 = (f32[8,16,128]{2,1,0:T(8,128)S(1)}, f32[8,16,128]{2,1,0:T(8,128)S(1)}, u32[]{:S(2)}, u32[]{:S(2)}) collective-permute-start(f32[8,16,128]{2,1,0:T(8,128)S(1)} %get-tuple-element.33), channel_id=1, source_target_pairs={{0,12},{4,0},{8,4},{12,8},{1,13},{5,1},{9,5},{13,9},{2,14},{6,2},{... | collective-permute-start | bytes 196616 | tf_op jit(solution)/shard_map/ppermute | solution.py:512
  64.6 12.4 %collective-permute-start.12 = (f32[8,16,128]{2,1,0:T(8,128)S(1)}, f32[8,16,128]{2,1,0:T(8,128)S(1)}, u32[]{:S(2)}, u32[]{:S(2)}) collective-permute-start(f32[8,16,128]{2,1,0:T(8,128)S(1)} %get-tuple-element.34), channel_id=1, source_target_pairs={{0,8},{4,12},{8,0},{12,4},{1,9},{5,13},{9,1},{13,5},{2,10},{6,14},... | collective-permute-start | bytes 196616 | tf_op jit(solution)/shard_map/ppermute | solution.py:512
  65.9 11.1 %collective-permute-start.11 = (f32[8,16,128]{2,1,0:T(8,128)S(1)}, f32[8,16,128]{2,1,0:T(8,128)S(1)}, u32[]{:S(2)}, u32[]{:S(2)}) collective-permute-start(f32[8,16,128]{2,1,0:T(8,128)S(1)} %get-tuple-element.35), channel_id=1, source_target_pairs={{0,4},{4,8},{8,12},{12,0},{1,5},{5,9},{9,13},{13,1},{2,6},{6,10},{... | collective-permute-start | bytes 196616 | tf_op jit(solution)/shard_map/ppermute | solution.py:512
  67.9 3.7 %collective-permute-start.19 = (f32[8,128]{1,0:T(8,128)S(1)}, f32[8,128]{1,0:T(8,128)S(1)}, u32[]{:S(2)}, u32[]{:S(2)}) collective-permute-start(f32[8,128]{1,0:T(8,128)S(1)} %add_add_fusion.refs_4_), channel_id=1, source_target_pairs={{0,12},{4,0},{8,4},{12,8},{1,13},{5,1},{9,5},{13,9},{2,14},{6,2},{... | collective-permute-start | bytes 12296 | tf_op jit(solution)/shard_map/ppermute | solution.py:512
  69.8 4.5 %collective-permute-start.18 = (f32[8,128]{1,0:T(8,128)S(1)}, f32[8,128]{1,0:T(8,128)S(1)}, u32[]{:S(2)}, u32[]{:S(2)}) collective-permute-start(f32[8,128]{1,0:T(8,128)S(1)} %add_add_fusion.refs_4_), channel_id=1, source_target_pairs={{0,8},{4,12},{8,0},{12,4},{1,9},{5,13},{9,1},{13,5},{2,10},{6,14},... | collective-permute-start | bytes 12296 | tf_op jit(solution)/shard_map/ppermute | solution.py:512
  71.6 5.4 %collective-permute-start.17 = (f32[8,128]{1,0:T(8,128)S(1)}, f32[8,128]{1,0:T(8,128)S(1)}, u32[]{:S(2)}, u32[]{:S(2)}) collective-permute-start(f32[8,128]{1,0:T(8,128)S(1)} %add_add_fusion.refs_4_), channel_id=1, source_target_pairs={{0,4},{4,8},{8,12},{12,0},{1,5},{5,9},{9,13},{13,1},{2,6},{6,10},{... | collective-permute-start | bytes 12296 | tf_op jit(solution)/shard_map/ppermute | solution.py:512

commit v5 on v4

--- a/solution.py
+++ b/solution.py
@@ -210,11 +210,12 @@
     epochs, rows, operands = sizes
     inputs = refs[:operands]
     factors, pulls = refs[operands : operands + 2]
-    full, rim_full, main, rim, looked, rim_looked, wide, outer, boxed, power_box = refs[operands + 2 :]
+    main, rim, looked, rim_looked, wide, outer, boxed, power_box = refs[operands + 2 :]
     count = len(places)
     look_rows = rows // LOOK
     tall = (rows + 2 * HALO) // LOOK
-    first_look = HALO // LOOK - RADIUS
+    halo_looks = HALO // LOOK
+    full_rows = rows + 2 * HALO
     total = count * epochs
     own_total = total - epochs
     group = 2 * SLOTS
@@ -239,40 +240,47 @@
     band = band_of((2 * LANES, LANES), lambda at, to: at % LANES, lambda to: to)
     rim_band = band_of((2 * LANES, SLOTS * LANES), rim_column, lambda to: to % LANES)
 
+    out_at = lax.broadcasted_iota(jnp.int32, (group * look_rows, group * tall), 0)
+    in_at = lax.broadcasted_iota(jnp.int32, (group * look_rows, group * tall), 1)
+    near = jnp.abs(in_at % tall - halo_looks - out_at % look_rows) <= RADIUS
+    near = near & (in_at // tall == out_at // look_rows)
+    sum_rows = near.astype(f32).astype(jnp.bfloat16)
+
+    out_at = lax.broadcasted_iota(jnp.int32, (full_rows, full_rows), 0)
+    in_at = lax.broadcasted_iota(jnp.int32, (full_rows, full_rows), 1)
+    order = (in_at == out_at % tall * LOOK + out_at // tall).astype(f32)
+    order = jnp.where(in_at < HALO, order * has_top, order)
+    order = jnp.where(in_at >= HALO + rows, order * has_bottom, order).astype(jnp.bfloat16)
+
     lane = lax.broadcasted_iota(jnp.int32, (tall, LANES), 1)
     for block, (tile_at, strip_at, strip_row, top_at, bottom_at, halo_slot) in enumerate(places):
         tile, strip, top, bottom = inputs[tile_at], inputs[strip_at], inputs[top_at], inputs[bottom_at]
 
-        @pl.loop(0, 2 * epochs, unroll=4)
-        def _(at):
-            row = pl.multiple_of(at * HALO, HALO)
-            own = pl.multiple_of(at * rows, rows)
-            at = at + block * 2 * epochs
-            full[at, :HALO] = top[halo_slot, pl.ds(row, HALO), :].astype(f32) * has_top
-            full[at, HALO : HALO + rows] = tile[pl.ds(own, rows), :].astype(f32)
-            full[at, HALO + rows :] = bottom[halo_slot, pl.ds(row, HALO), :].astype(f32) * has_bottom
+        @pl.loop(0, epochs // 2)
+        def _(quad):
+            for couple in range(2):
+                columns = []
+                for one in range(2):
+                    at = quad * 4 + couple * 2 + one
+                    row = pl.multiple_of(at * HALO, HALO)
+                    own = pl.multiple_of(at * rows, rows)
+                    parts = [top[halo_slot, pl.ds(row, HALO), :], tile[pl.ds(own, rows), :], bottom[halo_slot, pl.ds(row, HALO), :]]
+                    columns.append(jnp.concatenate(parts, axis=0))
+                value = jnp.dot(order, jnp.concatenate(columns, axis=1), preferred_element_type=f32)
+                for one in range(2):
+                    at = block * 2 * epochs + quad * 4 + couple * 2 + one
+                    for look in range(LOOK):
+                        main[at, look] = value[look * tall : (look + 1) * tall, one * LANES : (one + 1) * LANES]
 
         last = slice(2 * epochs * HALO, 2 * epochs * HALO + HALO)
-        rim_full[block, :HALO] = top[halo_slot, last, :].astype(f32) * has_top
-        rim_full[block, HALO : HALO + rows] = strip[strip_row : strip_row + rows, :].astype(f32)
-        rim_full[block, HALO + rows :] = bottom[halo_slot, last, :].astype(f32) * has_bottom
-
-    def places_of(epoch):
-        at = epoch // epochs * (2 * epochs) + epoch % epochs
-        return at, at + epochs
-
-    @pl.loop(0, 2 * total, unroll=4)
-    def _(at):
-        for look in range(LOOK):
-            main[at, look] = full[at, pl.ds(look, tall, stride=LOOK), :]
-
-    for block in range(count):
-        by_look = [rim_full[block, pl.ds(look, tall, stride=LOOK), :] for look in range(LOOK)]
+        parts = [top[halo_slot, last, :], strip[strip_row : strip_row + rows, :], bottom[halo_slot, last, :]]
+        by_look = jnp.dot(order, jnp.concatenate(parts, axis=0), preferred_element_type=f32)
         for at in range(2 * epochs):
             value = jnp.zeros((tall, LANES), f32)
             for look in range(LOOK):
                 target = look * SIDES
-                moved = pltpu.roll(by_look[look], (target - at * SIDES) % LANES, axis=1)
+                moved = by_look[look * tall : (look + 1) * tall]
+                moved = pltpu.roll(moved, (target - at * SIDES) % LANES, axis=1)
                 value = jnp.where((lane >= target) & (lane < target + SIDES), moved, value)
             spread = share
             while spread < LANES:
@@ -280,6 +288,10 @@
                 spread = 2 * spread
             rim[block * 2 * epochs + at] = value
 
+    def places_of(epoch):
+        at = epoch // epochs * (2 * epochs) + epoch % epochs
+        return at, at + epochs
+
     piece_lane = lax.broadcasted_iota(jnp.int32, (8, LANES), 1)
     slot_lane = [piece_lane // share == slot for slot in range(SLOTS)]
 
@@ -290,7 +302,7 @@
         return result
 
     def channel_rows(batch, piece, channel):
-        return pl.ds(batch * group_rows + piece * group + channel, 8, stride=group)
+        return pl.ds(pl.multiple_of(batch * group_rows + channel * tall + piece, 8), 8)
 
     for block in range(count):
         for piece in range(0, tall, 8):
@@ -364,41 +376,34 @@
         columns_summed(count + quad * 4, 4)
 
     def rows_summed(batch):
-        values = []
-        for look in range(tall):
-            at = pl.ds(pl.multiple_of(batch * group_rows + look * group, group), group)
-            values.append(wide[at, :] + outer[at, :])
-        twos = {look: values[look] + values[look + 1] for look in range(first_look, tall - 2)}
-        fours = {look: twos[look] + twos[look + 2] for look in range(first_look, tall - 4)}
-        for out in range(look_rows):
-            at = out + first_look
-            seven = fours[at] + twos[at + 4] + values[at + 6]
-            to = pl.ds(pl.multiple_of((batch * look_rows + out) * group, group), group)
-            boxed[to, :] = seven
-
-    def box_of(batch, channel):
-        return boxed[pl.ds(batch * (look_rows * group) + channel, look_rows, stride=group), :]
+        at = pl.ds(pl.multiple_of(batch * group_rows, group_rows), group_rows)
+        halves = jnp.concatenate(split_two(wide[at, :] + outer[at, :]), axis=1)
+        value = jnp.dot(sum_rows, halves, preferred_element_type=f32)
+        return value[:, :LANES] + value[:, LANES:]
 
     for block in range(count):
-        rows_summed(block)
+        value = rows_summed(block)
         for channel in range(epochs):
-            power_box[block * epochs + channel] = box_of(block, channel)
-
-    @pl.loop(0, own_total, unroll=2)
-    def _(epoch):
-        rows_summed(count + epoch)
-
-    @pl.loop(0, own_total, unroll=2)
-    def _(epoch):
-        own_power = power_box[epoch]
-        for slot in range(SLOTS):
-            pair = epoch * SLOTS + slot
-            inverse = lax.rsqrt(own_power * power_box[partner[pair]] + EPSILON)
-            unit_re = box_of(count + epoch, slot) * inverse
-            unit_im = box_of(count + epoch, SLOTS + slot) * inverse
-            factor = weight[pair] * (unit_re * unit_re + unit_im * unit_im)
-            factors[pair] = factor
-            pulls[pair] = factor * unit_im
+            power_box[block * epochs + channel] = value[channel * look_rows : (channel + 1) * look_rows]
+
+    @pl.loop(0, own_total // 4)
+    def _(quad):
+        for one in range(4):
+            boxed[quad * 4 + one] = rows_summed(count + quad * 4 + one)
+
+    @pl.loop(0, own_total // 2)
+    def _(couple):
+        for one in range(2):
+            epoch = couple * 2 + one
+            own_power = power_box[epoch]
+            for slot in range(SLOTS):
+                pair = epoch * SLOTS + slot
+                inverse = lax.rsqrt(own_power * power_box[partner[pair]] + EPSILON)
+                unit_re = boxed[epoch, slot * look_rows : (slot + 1) * look_rows, :] * inverse
+                unit_im = boxed[epoch, (SLOTS + slot) * look_rows : (SLOTS + slot + 1) * look_rows, :] * inverse
+                factor = weight[pair] * (unit_re * unit_re + unit_im * unit_im)
+                factors[pair] = factor
+                pulls[pair] = factor * unit_im
 
 
 def gradient_kernel(sizes, partner, *refs):
@@ -650,15 +655,13 @@
             in_specs=[SMEM] * 3 + [VMEM] * len(operands),
             out_specs=(VMEM, VMEM),
             scratch_shapes=[
-                pltpu.VMEM((2 * here, rows + 2 * HALO, LANES), f32),
-                pltpu.VMEM((len(loaded), rows + 2 * HALO, LANES), f32),
                 pltpu.VMEM((2 * here, LOOK, tall, LANES), f32),
                 pltpu.VMEM((2 * here, tall, LANES), f32),
                 pltpu.VMEM((batches * group * tall, LANES), f32),
                 pltpu.VMEM((batches * 2 * tall, LANES), f32),
                 pltpu.VMEM((batches * group * tall, LANES), f32),
                 pltpu.VMEM((batches * group * tall, LANES), f32),
-                pltpu.VMEM((batches * group * look_rows, LANES), f32),
+                pltpu.VMEM((owned, group * look_rows, LANES), f32),
                 pltpu.VMEM((here, look_rows, LANES), f32),
             ],
             compiler_params=params_of,

time: 78.3 us -> 75 us (0.958)
  Pallas kernels: 24.6 us -> 21.3 us
    pallas_call x2, Pallas kernels: 20.7 us -> 17.5 us  [pair_stage(): pl.pallas_call(functools.partial(pair_kernel, (epochs, rows, len(operands...]
  transfers between devices with their start and end apart: 20 -> 20, of which waited for: 6 -> 6; matrix products, arithmetic and copies ran while one was open for 3% -> 3% of each run, Pallas kernels for 27% -> 24%
where the time goes in v5:
time: 75 us; the launch traced here: 74.7 us
  starting transfers between devices  27.3 us (36%)
  Pallas kernels  21.3 us (28%)
  waiting for transfers between devices  17.2 us (23%)
  local copies, waits for them, and re-layouts  6.71 us (9%)
  between operations  1.53 us (2%)
    ppermute x14, starting transfers between devices, to_ahead(): return lax.ppermute(x, axis, [(i, (i + by) % size) for i in range(size)])  22 us
    pallas_call x2, Pallas kernels, pair_stage(): pl.pallas_call(functools.partial(pair_kernel, (epochs, rows, len(operands...  17.5 us
    ppermute x14, waiting for transfers between devices, to_ahead(): return lax.ppermute(x, axis, [(i, (i + by) % size) for i in range(size)])  14.3 us
    unnamed x23, local copies, waits for them, and re-layouts  5.21 us
    ppermute x2, starting transfers between devices, halo(): got = lax.ppermute(mine, 'space', [(0, 1), (1, 0)])  3.2 us
    ppermute x2, waiting for transfers between devices, halo(): got = lax.ppermute(mine, 'space', [(0, 1), (1, 0)])  2.89 us
    pallas_call x1, Pallas kernels, transposed_plan(): pl.pallas_call(functools.partial(gradient_kernel, (tiles, epochs, stages)...  2.24 us
    ppermute x3, starting transfers between devices, transposed_plan(): lax.ppermute(sums, place, [(i, (i + by) % count) for i in range(count)])  1.62 us
  transfers between devices with their start and end apart: 20, of which 6 were waited for; matrix products, arithmetic and copies ran while one was open for 3% of the time, Pallas kernels for 24%

profile of v5, /device:TPU:0, one launch (start us, length us, event | category | flops | bytes accessed | tf_op | source)
XLA Modules:
  0.0 74.7 jit_solution(16789818010083775152)
XLA Ops:
  0.6 1.2 %copy-done = bf16[2,8,64,512]{3,2,1,0:T(8,128)(2,1)S(1)} copy-done((bf16[2,8,64,512]{3,2,1,0:T(8,128)(2,1)S(1)}, bf16[2,8,64,512]{3,2,1,0:T(8,128)(2,1)}, u32[]{:S(2)}) %copy-start) | copy-done | bytes 1048600
  1.9 0.9 %copy-done.2 = f32[8,16,512]{2,1,0:T(8,128)S(1)} copy-done((f32[8,16,512]{2,1,0:T(8,128)S(1)}, f32[8,16,512]{2,1,0:T(8,128)}, u32[]{:S(2)}) %copy-start.2) | copy-done | bytes 262168
  2.8 0.9 %copy-done.4 = f32[8,16,512]{2,1,0:T(8,128)S(1)} copy-done((f32[8,16,512]{2,1,0:T(8,128)S(1)}, f32[8,16,512]{2,1,0:T(8,128)}, u32[]{:S(2)}) %copy-start.4) | copy-done | bytes 262168
  3.8 0.2 shard_map.77
  4.0 0.5 collective-permute-start
  4.5 0.5 copy-done.1
  5.0 0.9 %constant_dynamic-slice_fusion.3 = (bf16[2,8,64,128]{3,2,1,0:T(8,128)(2,1)S(1)}, bf16[2,8,64,128]{3,2,1,0:T(8,128)(2,1)}, bf16[2,8,64,128]{3,2,1,0:T(8,128)(2,1)S(1)}, bf16[2,8,64,128]{3,2,1,0:T(8,128)(2,1)S(1)}) fusion(bf16[2,8,64,512]{3,2,1,0:T(8,128)(2,1)S(1)} %copy-done.1, s32[]{:T(128)S(6)} %select_n.81, s32[]{:T(128)S(6)} %select_n.76, ...), kind=kLoop, calls=%fused_computation.70 | loop fusion | bytes 2097168 | tf_op jit(solution)/shard_map/dynamic_slice | solution.py:536
  5.9 3.0 %collective-permute-start.4 = (bf16[1024,128]{1,0:T(8,128)(2,1)}, bf16[1024,128]{1,0:T(8,128)(2,1)S(1)}, u32[]{:S(2)}, u32[]{:S(2)}) collective-permute-start(bf16[1024,128]{1,0:T(8,128)(2,1)} %bitcast.8), channel_id=1, source_target_pairs={{0,4},{4,8},{8,12},{12,0},{1,5},{5,9},{9,13},{13,1},{2,6},{6,10},{... | collective-permute-start | bytes 786440 | tf_op jit(solution)/shard_map/ppermute | solution.py:517
  8.9 2.0 %collective-permute-start.5 = (bf16[1024,128]{1,0:T(8,128)(2,1)S(1)}, bf16[1024,128]{1,0:T(8,128)(2,1)S(1)}, u32[]{:S(2)}, u32[]{:S(2)}) collective-permute-start(bf16[1024,128]{1,0:T(8,128)(2,1)S(1)} %bitcast.42), channel_id=1, source_target_pairs={{0,12},{4,0},{8,4},{12,8},{1,13},{5,1},{9,5},{13,9},{2,14},{6,2},{... | collective-permute-start | bytes 786440 | tf_op jit(solution)/shard_map/ppermute | solution.py:517
  10.9 0.7 copy-done.6
  11.6 0.1 copy.12
  11.7 0.7 copy-done.7
  12.4 0.1 copy.13
  12.5 0.1 select_maximum_fusion.params
  12.5 0.1 add_convert_fusion.present
  12.6 0.5 shard_map.78
  13.2 0.1 slice_convert_fusion.2
  13.2 2.0 %collective-permute-start.1 = (bf16[64,128]{1,0:T(8,128)(2,1)S(1)}, bf16[64,128]{1,0:T(8,128)(2,1)S(1)}, u32[]{:S(2)}, u32[]{:S(2)}) collective-permute-start(bf16[64,128]{1,0:T(8,128)(2,1)S(1)} %get-tuple-element.37), channel_id=1, source_target_pairs={{0,12},{4,0},{8,4},{12,8},{1,13},{5,1},{9,5},{13,9},{2,14},{6,2},{... | collective-permute-start | bytes 49160 | tf_op jit(solution)/shard_map/ppermute | solution.py:517
  15.3 1.1 %collective-permute-start.2 = (bf16[1088,128]{1,0:T(8,128)(2,1)S(1)}, bf16[1088,128]{1,0:T(8,128)(2,1)S(1)}, u32[]{:S(2)}, u32[]{:S(2)}) collective-permute-start(bf16[1088,128]{1,0:T(8,128)(2,1)S(1)} %pad_maximum_fusion), channel_id=1, source_target_pairs={{0,8},{4,12},{8,0},{12,4},{1,9},{5,13},{9,1},{13,5},{2,10},{6,14},... | collective-permute-start | bytes 835592 | tf_op jit(solution)/shard_map/ppermute | solution.py:517
  16.4 6.3 %collective-permute-done.1.refs_6_.refs_1_ = bf16[64,128]{1,0:T(8,128)(2,1)S(1)} collective-permute-done((bf16[64,128]{1,0:T(8,128)(2,1)S(1)}, bf16[64,128]{1,0:T(8,128)(2,1)S(1)}, u32[]{:S(2)}, u32[]{:S(2)}) %collective-permute-start.1) | collective-permute-done | bytes 16416 | tf_op jit(solution)/shard_map/ppermute | solution.py:517
  22.7 2.0 %collective-permute-done.3.refs_1_.refs_6_ = bf16[64,128]{1,0:T(8,128)(2,1)S(1)} collective-permute-done((bf16[64,128]{1,0:T(8,128)(2,1)S(1)}, bf16[64,128]{1,0:T(8,128)(2,1)S(1)}, u32[]{:S(2)}, u32[]{:S(2)}) %collective-permute-start.3) | collective-permute-done | bytes 16416 | tf_op jit(solution)/shard_map/ppermute | solution.py:517
  24.8 0.1 reshape.73.partner
  25.1 1.8 %collective-permute-start.6 = (bf16[3,272,128]{2,1,0:T(8,128)(2,1)S(1)}, bf16[3,272,128]{2,1,0:T(8,128)(2,1)S(1)}, u32[]{:S(2)}, u32[]{:S(2)}) collective-permute-start(bf16[3,272,128]{2,1,0:T(8,128)(2,1)S(1)} %bitcast.47), channel_id=1, source_target_pairs={{0,2},{2,0},{1,3},{3,1},{4,6},{6,4},{5,7},{7,5},{8,10},{10,8},{9,1... | collective-permute-start | bytes 626696 | tf_op jit(solution)/shard_map/ppermute | solution.py:612
  26.9 0.1 fusion.20
  27.0 0.1 reshape.74.weight
  27.1 2.6 %collective-permute-start.9 = (bf16[3,128,128]{2,1,0:T(8,128)(2,1)S(1)}, bf16[3,128,128]{2,1,0:T(8,128)(2,1)S(1)}, u32[]{:S(2)}, u32[]{:S(2)}) collective-permute-start(bf16[3,128,128]{2,1,0:T(8,128)(2,1)S(1)} %get-tuple-element.30), channel_id=1, source_target_pairs={{0,4},{4,8},{8,12},{12,0},{1,5},{5,9},{9,13},{13,1},{2,6},{6,10},{... | collective-permute-start | bytes 294920 | tf_op jit(solution)/shard_map/ppermute | solution.py:517
  29.7 2.5 %collective-permute-start.8 = (bf16[3,128,128]{2,1,0:T(8,128)(2,1)S(1)}, bf16[3,128,128]{2,1,0:T(8,128)(2,1)S(1)}, u32[]{:S(2)}, u32[]{:S(2)}) collective-permute-start(bf16[3,128,128]{2,1,0:T(8,128)(2,1)S(1)} %get-tuple-element.31), channel_id=1, source_target_pairs={{0,8},{4,12},{8,0},{12,4},{1,9},{5,13},{9,1},{13,5},{2,10},{6,14},... | collective-permute-start | bytes 294920 | tf_op jit(solution)/shard_map/ppermute | solution.py:517
  32.2 2.8 %collective-permute-start.7 = (bf16[3,128,128]{2,1,0:T(8,128)(2,1)S(1)}, bf16[3,128,128]{2,1,0:T(8,128)(2,1)S(1)}, u32[]{:S(2)}, u32[]{:S(2)}) collective-permute-start(bf16[3,128,128]{2,1,0:T(8,128)(2,1)S(1)} %get-tuple-element.32), channel_id=1, source_target_pairs={{0,12},{4,0},{8,4},{12,8},{1,13},{5,1},{9,5},{13,9},{2,14},{6,2},{... | collective-permute-start | bytes 294920 | tf_op jit(solution)/shard_map/ppermute | solution.py:517
  35.1 8.7 %shard_map.79 = (f32[64,16,128]{2,1,0:T(8,128)S(1)}, f32[64,16,128]{2,1,0:T(8,128)S(1)}) custom-call(s32[64]{0:T(128)S(1)} %reshape.73.partner, f32[64]{0:T(128)S(1)} %reshape.74.weight, f32[2]{0:T(128)S(1)} %add_convert_fusion.present, bf16[1024,128]{1,0:T(8,128)(2,1)S(1)} %collective-permute-done.4.refs_0_.refs_5_, ...), custom_call_target="tpu_custom_call" | custom-call | flops 20000000 | bytes 30000000 | tf_op jit(solution)/shard_map/pallas_call | solution.py:652
  43.8 0.1 slice_convert_fusion.3
  43.9 0.1 fusion.13
  44.0 0.1 reshape.87.partner
  44.1 0.1 reshape.89.weight
  44.2 1.4 %collective-permute-start.10 = (bf16[1,272,128]{2,1,0:T(8,128)(2,1)S(1)}, bf16[1,272,128]{2,1,0:T(8,128)(2,1)S(1)}, u32[]{:S(2)}, u32[]{:S(2)}) collective-permute-start(bf16[1,272,128]{2,1,0:T(8,128)(2,1)S(1)} %bitcast.46), channel_id=1, source_target_pairs={{0,2},{2,0},{1,3},{3,1},{4,6},{6,4},{5,7},{7,5},{8,10},{10,8},{9,1... | collective-permute-start | bytes 208904 | tf_op jit(solution)/shard_map/ppermute | solution.py:612
  45.6 0.1 reshape.88.partner
  45.7 2.9 %collective-permute-done.10.refs_4_ = bf16[1,272,128]{2,1,0:T(8,128)(2,1)S(1)} collective-permute-done((bf16[1,272,128]{2,1,0:T(8,128)(2,1)S(1)}, bf16[1,272,128]{2,1,0:T(8,128)(2,1)S(1)}, u32[]{:S(2)}, u32[]{:S(2)}) %collective-permute-start.10) | collective-permute-done | bytes 69664 | tf_op jit(solution)/shard_map/ppermute | solution.py:612
  48.6 8.7 %shard_map.80 = (f32[64,16,128]{2,1,0:T(8,128)S(1)}, f32[64,16,128]{2,1,0:T(8,128)S(1)}) custom-call(s32[64]{0:T(128)S(1)} %reshape.88.partner, f32[64]{0:T(128)S(1)} %reshape.89.weight, f32[2]{0:T(128)S(1)} %add_convert_fusion.present, bf16[1024,128]{1,0:T(8,128)(2,1)S(1)} %collective-permute-done.5.refs_5_.refs_0_, ...), custom_call_target="tpu_custom_call" | custom-call | flops 20000000 | bytes 30000000 | tf_op jit(solution)/shard_map/pallas_call | solution.py:652
  57.4 2.2 %shard_map.81 = (f32[32,16,128]{2,1,0:T(8,128)S(1)}, f32[8,128]{1,0:T(8,128)S(1)}) custom-call(s32[128]{0:T(128)S(1)} %reshape.87.partner, bf16[3,128,128]{2,1,0:T(8,128)(2,1)S(1)} %dynamic-slice_bitcast_fusion.3.refs_0_, bf16[3,128,128]{2,1,0:T(8,128)(2,1)S(1)} %collective-permute-done.7.refs_1_, bf16[3,128,128]{2,1,0:T(8,128)(2,1)S(1)} %collective-permute-done.8.refs_2_, ...), custom_call_target="tpu_custom_call" | custom-call | flops 10000000 | bytes 8000000 | tf_op jit(solution)/shard_map/pallas_call | solution.py:682
  59.7 1.4 %collective-permute-start.15 = (f32[8,128]{1,0:T(8,128)S(1)}, f32[8,128]{1,0:T(8,128)S(1)}, u32[]{:S(2)}, u32[]{:S(2)}) collective-permute-start(f32[8,128]{1,0:T(8,128)S(1)} %get-tuple-element.25), channel_id=1, source_target_pairs={{0,2},{1,3},{2,0},{3,1},{4,6},{5,7},{6,4},{7,5},{8,10},{9,11},{10,... | collective-permute-start | bytes 12296 | tf_op jit(solution)/shard_map/ppermute | solution.py:697
  61.1 0.2 collective-permute-start.14
  61.3 1.4 %collective-permute-start.12 = (f32[8,16,128]{2,1,0:T(8,128)S(1)}, f32[8,16,128]{2,1,0:T(8,128)S(1)}, u32[]{:S(2)}, u32[]{:S(2)}) collective-permute-start(f32[8,16,128]{2,1,0:T(8,128)S(1)} %get-tuple-element.34), channel_id=1, source_target_pairs={{0,8},{4,12},{8,0},{12,4},{1,9},{5,13},{9,1},{13,5},{2,10},{6,14},... | collective-permute-start | bytes 196616 | tf_op jit(solution)/shard_map/ppermute | solution.py:517
  62.7 1.9 %collective-permute-start.11 = (f32[8,16,128]{2,1,0:T(8,128)S(1)}, f32[8,16,128]{2,1,0:T(8,128)S(1)}, u32[]{:S(2)}, u32[]{:S(2)}) collective-permute-start(f32[8,16,128]{2,1,0:T(8,128)S(1)} %get-tuple-element.35), channel_id=1, source_target_pairs={{0,4},{4,8},{8,12},{12,0},{1,5},{5,9},{9,13},{13,1},{2,6},{6,10},{... | collective-permute-start | bytes 196616 | tf_op jit(solution)/shard_map/ppermute | solution.py:517
  64.7 1.9 %collective-permute-start.19 = (f32[8,128]{1,0:T(8,128)S(1)}, f32[8,128]{1,0:T(8,128)S(1)}, u32[]{:S(2)}, u32[]{:S(2)}) collective-permute-start(f32[8,128]{1,0:T(8,128)S(1)} %add_add_fusion.refs_4_), channel_id=1, source_target_pairs={{0,12},{4,0},{8,4},{12,8},{1,13},{5,1},{9,5},{13,9},{2,14},{6,2},{... | collective-permute-start | bytes 12296 | tf_op jit(solution)/shard_map/ppermute | solution.py:517
  66.6 1.8 %collective-permute-done.19.refs_7_ = f32[8,128]{1,0:T(8,128)S(1)} collective-permute-done((f32[8,128]{1,0:T(8,128)S(1)}, f32[8,128]{1,0:T(8,128)S(1)}, u32[]{:S(2)}, u32[]{:S(2)}) %collective-permute-start.19) | collective-permute-done | bytes 4128 | tf_op jit(solution)/shard_map/ppermute | solution.py:517
  68.4 0.6 collective-permute-start.17
  69.6 1.5 %collective-permute-done.18.refs_6_ = f32[8,128]{1,0:T(8,128)S(1)} collective-permute-done((f32[8,128]{1,0:T(8,128)S(1)}, f32[8,128]{1,0:T(8,128)S(1)}, u32[]{:S(2)}, u32[]{:S(2)}) %collective-permute-start.18) | collective-permute-done | bytes 4128 | tf_op jit(solution)/shard_map/ppermute | solution.py:517
  71.1 2.7 %collective-permute-done.17.refs_5_ = f32[8,128]{1,0:T(8,128)S(1)} collective-permute-done((f32[8,128]{1,0:T(8,128)S(1)}, f32[8,128]{1,0:T(8,128)S(1)}, u32[]{:S(2)}, u32[]{:S(2)}) %collective-permute-start.17) | collective-permute-done | bytes 4128 | tf_op jit(solution)/shard_map/ppermute | solution.py:517
  73.8 0.9 %shard_map.82 = (f32[8,16,512]{2,1,0:T(8,128)}, f32[8,16,512]{2,1,0:T(8,128)}) custom-call(s32[1]{0:T(128)} %bitcast.me, f32[1]{0:T(128)S(6)} %copy.21.prev_mean, f32[8,16,512]{2,1,0:T(8,128)S(1)} %copy-done.3, f32[8,16,512]{2,1,0:T(8,128)S(1)} %copy-done.5, f32[8,16,128]{2,1,0:T(8,128)S(1)} %get-tuple-element.36.refs_0_, ...), custom_call_target="tpu_custom_call" | custom-call | flops 1000000 | bytes 2000000 | tf_op jit(solution)/shard_map/pallas_call | solution.py:703
  (52 shorter events, 0.6 us)
Async XLA Ops:
  0.6 1.2 %copy-start = (bf16[2,8,64,512]{3,2,1,0:T(8,128)(2,1)S(1)}, bf16[2,8,64,512]{3,2,1,0:T(8,128)(2,1)}, u32[]{:S(2)}) copy-start(bf16[2,8,64,512]{3,2,1,0:T(8,128)(2,1)} %slc.3) | copy-start | bytes 3145732
  1.9 0.9 %copy-start.2 = (f32[8,16,512]{2,1,0:T(8,128)S(1)}, f32[8,16,512]{2,1,0:T(8,128)}, u32[]{:S(2)}) copy-start(f32[8,16,512]{2,1,0:T(8,128)} %estimate.3) | copy-start | bytes 786436
  2.8 0.9 %copy-start.4 = (f32[8,16,512]{2,1,0:T(8,128)S(1)}, f32[8,16,512]{2,1,0:T(8,128)}, u32[]{:S(2)}) copy-start(f32[8,16,512]{2,1,0:T(8,128)} %direction.3) | copy-start | bytes 786436
  3.8 1.2 %copy-start.1 = (bf16[2,8,64,512]{3,2,1,0:T(8,128)(2,1)S(1)}, bf16[2,8,64,512]{3,2,1,0:T(8,128)(2,1)}, u32[]{:S(2)}) copy-start(bf16[2,8,64,512]{3,2,1,0:T(8,128)(2,1)} %slc.3) | copy-start | bytes 3145732
  4.0 8.7 %collective-permute-start = (bf16[64,128]{1,0:T(8,128)(2,1)S(1)}, bf16[64,128]{1,0:T(8,128)(2,1)S(1)}, u32[]{:S(2)}, u32[]{:S(2)}) collective-permute-start(bf16[64,128]{1,0:T(8,128)(2,1)S(1)} %get-tuple-element.14), channel_id=1, source_target_pairs={{0,1},{1,0},{2,3},{3,2},{4,5},{5,4},{6,7},{7,6},{8,9},{9,8},{10,11... | collective-permute-start | bytes 49160 | tf_op jit(solution)/shard_map/ppermute | solution.py:508
  5.9 19.0 %collective-permute-start.4 = (bf16[1024,128]{1,0:T(8,128)(2,1)}, bf16[1024,128]{1,0:T(8,128)(2,1)S(1)}, u32[]{:S(2)}, u32[]{:S(2)}) collective-permute-start(bf16[1024,128]{1,0:T(8,128)(2,1)} %bitcast.8), channel_id=1, source_target_pairs={{0,4},{4,8},{8,12},{12,0},{1,5},{5,9},{9,13},{13,1},{2,6},{6,10},{... | collective-permute-start | bytes 786440 | tf_op jit(solution)/shard_map/ppermute | solution.py:517
  8.9 16.1 %collective-permute-start.5 = (bf16[1024,128]{1,0:T(8,128)(2,1)S(1)}, bf16[1024,128]{1,0:T(8,128)(2,1)S(1)}, u32[]{:S(2)}, u32[]{:S(2)}) collective-permute-start(bf16[1024,128]{1,0:T(8,128)(2,1)S(1)} %bitcast.42), channel_id=1, source_target_pairs={{0,12},{4,0},{8,4},{12,8},{1,13},{5,1},{9,5},{13,9},{2,14},{6,2},{... | collective-permute-start | bytes 786440 | tf_op jit(solution)/shard_map/ppermute | solution.py:517
  10.9 0.7 copy-start.6
  11.7 0.7 copy-start.7
  13.2 9.4 %collective-permute-start.1 = (bf16[64,128]{1,0:T(8,128)(2,1)S(1)}, bf16[64,128]{1,0:T(8,128)(2,1)S(1)}, u32[]{:S(2)}, u32[]{:S(2)}) collective-permute-start(bf16[64,128]{1,0:T(8,128)(2,1)S(1)} %get-tuple-element.37), channel_id=1, source_target_pairs={{0,12},{4,0},{8,4},{12,8},{1,13},{5,1},{9,5},{13,9},{2,14},{6,2},{... | collective-permute-start | bytes 49160 | tf_op jit(solution)/shard_map/ppermute | solution.py:517
  15.3 9.5 %collective-permute-start.3 = (bf16[64,128]{1,0:T(8,128)(2,1)S(1)}, bf16[64,128]{1,0:T(8,128)(2,1)S(1)}, u32[]{:S(2)}, u32[]{:S(2)}) collective-permute-start(bf16[64,128]{1,0:T(8,128)(2,1)S(1)} %get-tuple-element.38), channel_id=1, source_target_pairs={{0,4},{4,8},{8,12},{12,0},{1,5},{5,9},{9,13},{13,1},{2,6},{6,10},{... | collective-permute-start | bytes 49160 | tf_op jit(solution)/shard_map/ppermute | solution.py:517
  15.3 28.5 %collective-permute-start.2 = (bf16[1088,128]{1,0:T(8,128)(2,1)S(1)}, bf16[1088,128]{1,0:T(8,128)(2,1)S(1)}, u32[]{:S(2)}, u32[]{:S(2)}) collective-permute-start(bf16[1088,128]{1,0:T(8,128)(2,1)S(1)} %pad_maximum_fusion), channel_id=1, source_target_pairs={{0,8},{4,12},{8,0},{12,4},{1,9},{5,13},{9,1},{13,5},{2,10},{6,14},... | collective-permute-start | bytes 835592 | tf_op jit(solution)/shard_map/ppermute | solution.py:517
  25.1 10.0 %collective-permute-start.6 = (bf16[3,272,128]{2,1,0:T(8,128)(2,1)S(1)}, bf16[3,272,128]{2,1,0:T(8,128)(2,1)S(1)}, u32[]{:S(2)}, u32[]{:S(2)}) collective-permute-start(bf16[3,272,128]{2,1,0:T(8,128)(2,1)S(1)} %bitcast.47), channel_id=1, source_target_pairs={{0,2},{2,0},{1,3},{3,1},{4,6},{6,4},{5,7},{7,5},{8,10},{10,8},{9,1... | collective-permute-start | bytes 626696 | tf_op jit(solution)/shard_map/ppermute | solution.py:612
  27.1 30.2 %collective-permute-start.9 = (bf16[3,128,128]{2,1,0:T(8,128)(2,1)S(1)}, bf16[3,128,128]{2,1,0:T(8,128)(2,1)S(1)}, u32[]{:S(2)}, u32[]{:S(2)}) collective-permute-start(bf16[3,128,128]{2,1,0:T(8,128)(2,1)S(1)} %get-tuple-element.30), channel_id=1, source_target_pairs={{0,4},{4,8},{8,12},{12,0},{1,5},{5,9},{9,13},{13,1},{2,6},{6,10},{... | collective-permute-start | bytes 294920 | tf_op jit(solution)/shard_map/ppermute | solution.py:517
  29.7 27.6 %collective-permute-start.8 = (bf16[3,128,128]{2,1,0:T(8,128)(2,1)S(1)}, bf16[3,128,128]{2,1,0:T(8,128)(2,1)S(1)}, u32[]{:S(2)}, u32[]{:S(2)}) collective-permute-start(bf16[3,128,128]{2,1,0:T(8,128)(2,1)S(1)} %get-tuple-element.31), channel_id=1, source_target_pairs={{0,8},{4,12},{8,0},{12,4},{1,9},{5,13},{9,1},{13,5},{2,10},{6,14},... | collective-permute-start | bytes 294920 | tf_op jit(solution)/shard_map/ppermute | solution.py:517
  32.2 25.1 %collective-permute-start.7 = (bf16[3,128,128]{2,1,0:T(8,128)(2,1)S(1)}, bf16[3,128,128]{2,1,0:T(8,128)(2,1)S(1)}, u32[]{:S(2)}, u32[]{:S(2)}) collective-permute-start(bf16[3,128,128]{2,1,0:T(8,128)(2,1)S(1)} %get-tuple-element.32), channel_id=1, source_target_pairs={{0,12},{4,0},{8,4},{12,8},{1,13},{5,1},{9,5},{13,9},{2,14},{6,2},{... | collective-permute-start | bytes 294920 | tf_op jit(solution)/shard_map/ppermute | solution.py:517
  44.2 4.4 %collective-permute-start.10 = (bf16[1,272,128]{2,1,0:T(8,128)(2,1)S(1)}, bf16[1,272,128]{2,1,0:T(8,128)(2,1)S(1)}, u32[]{:S(2)}, u32[]{:S(2)}) collective-permute-start(bf16[1,272,128]{2,1,0:T(8,128)(2,1)S(1)} %bitcast.46), channel_id=1, source_target_pairs={{0,2},{2,0},{1,3},{3,1},{4,6},{6,4},{5,7},{7,5},{8,10},{10,8},{9,1... | collective-permute-start | bytes 208904 | tf_op jit(solution)/shard_map/ppermute | solution.py:612
  59.6 3.1 %collective-permute-start.16 = (f32[8,128]{1,0:T(8,128)S(1)}, f32[8,128]{1,0:T(8,128)S(1)}, u32[]{:S(2)}, u32[]{:S(2)}) collective-permute-start(f32[8,128]{1,0:T(8,128)S(1)} %get-tuple-element.25), channel_id=1, source_target_pairs={{0,3},{1,0},{2,1},{3,2},{4,7},{5,4},{6,5},{7,6},{8,11},{9,8},{10,9... | collective-permute-start | bytes 12296 | tf_op jit(solution)/shard_map/ppermute | solution.py:697
  59.7 5.0 %collective-permute-start.15 = (f32[8,128]{1,0:T(8,128)S(1)}, f32[8,128]{1,0:T(8,128)S(1)}, u32[]{:S(2)}, u32[]{:S(2)}) collective-permute-start(f32[8,128]{1,0:T(8,128)S(1)} %get-tuple-element.25), channel_id=1, source_target_pairs={{0,2},{1,3},{2,0},{3,1},{4,6},{5,7},{6,4},{7,5},{8,10},{9,11},{10,... | collective-permute-start | bytes 12296 | tf_op jit(solution)/shard_map/ppermute | solution.py:697
  61.1 3.6 %collective-permute-start.14 = (f32[8,128]{1,0:T(8,128)S(1)}, f32[8,128]{1,0:T(8,128)S(1)}, u32[]{:S(2)}, u32[]{:S(2)}) collective-permute-start(f32[8,128]{1,0:T(8,128)S(1)} %get-tuple-element.25), channel_id=1, source_target_pairs={{0,1},{1,2},{2,3},{3,0},{4,5},{5,6},{6,7},{7,4},{8,9},{9,10},{10,1... | collective-permute-start | bytes 12296 | tf_op jit(solution)/shard_map/ppermute | solution.py:697
  61.2 12.5 %copy-start.3 = (f32[8,16,512]{2,1,0:T(8,128)S(1)}, f32[8,16,512]{2,1,0:T(8,128)}, u32[]{:S(2)}) copy-start(f32[8,16,512]{2,1,0:T(8,128)} %estimate.3) | copy-start | bytes 786436
  61.2 12.5 %copy-start.5 = (f32[8,16,512]{2,1,0:T(8,128)S(1)}, f32[8,16,512]{2,1,0:T(8,128)}, u32[]{:S(2)}) copy-start(f32[8,16,512]{2,1,0:T(8,128)} %direction.3) | copy-start | bytes 786436
  61.3 12.5 %collective-permute-start.13 = (f32[8,16,128]{2,1,0:T(8,128)S(1)}, f32[8,16,128]{2,1,0:T(8,128)S(1)}, u32[]{:S(2)}, u32[]{:S(2)}) collective-permute-start(f32[8,16,128]{2,1,0:T(8,128)S(1)} %get-tuple-element.33), channel_id=1, source_target_pairs={{0,12},{4,0},{8,4},{12,8},{1,13},{5,1},{9,5},{13,9},{2,14},{6,2},{... | collective-permute-start | bytes 196616 | tf_op jit(solution)/shard_map/ppermute | solution.py:517
  61.3 12.4 %collective-permute-start.12 = (f32[8,16,128]{2,1,0:T(8,128)S(1)}, f32[8,16,128]{2,1,0:T(8,128)S(1)}, u32[]{:S(2)}, u32[]{:S(2)}) collective-permute-start(f32[8,16,128]{2,1,0:T(8,128)S(1)} %get-tuple-element.34), channel_id=1, source_target_pairs={{0,8},{4,12},{8,0},{12,4},{1,9},{5,13},{9,1},{13,5},{2,10},{6,14},... | collective-permute-start | bytes 196616 | tf_op jit(solution)/shard_map/ppermute | solution.py:517
  62.7 11.1 %collective-permute-start.11 = (f32[8,16,128]{2,1,0:T(8,128)S(1)}, f32[8,16,128]{2,1,0:T(8,128)S(1)}, u32[]{:S(2)}, u32[]{:S(2)}) collective-permute-start(f32[8,16,128]{2,1,0:T(8,128)S(1)} %get-tuple-element.35), channel_id=1, source_target_pairs={{0,4},{4,8},{8,12},{12,0},{1,5},{5,9},{9,13},{13,1},{2,6},{6,10},{... | collective-permute-start | bytes 196616 | tf_op jit(solution)/shard_map/ppermute | solution.py:517
  64.7 3.7 %collective-permute-start.19 = (f32[8,128]{1,0:T(8,128)S(1)}, f32[8,128]{1,0:T(8,128)S(1)}, u32[]{:S(2)}, u32[]{:S(2)}) collective-permute-start(f32[8,128]{1,0:T(8,128)S(1)} %add_add_fusion.refs_4_), channel_id=1, source_target_pairs={{0,12},{4,0},{8,4},{12,8},{1,13},{5,1},{9,5},{13,9},{2,14},{6,2},{... | collective-permute-start | bytes 12296 | tf_op jit(solution)/shard_map/ppermute | solution.py:517
  66.6 4.5 %collective-permute-start.18 = (f32[8,128]{1,0:T(8,128)S(1)}, f32[8,128]{1,0:T(8,128)S(1)}, u32[]{:S(2)}, u32[]{:S(2)}) collective-permute-start(f32[8,128]{1,0:T(8,128)S(1)} %add_add_fusion.refs_4_), channel_id=1, source_target_pairs={{0,8},{4,12},{8,0},{12,4},{1,9},{5,13},{9,1},{13,5},{2,10},{6,14},... | collective-permute-start | bytes 12296 | tf_op jit(solution)/shard_map/ppermute | solution.py:517
  68.4 5.4 %collective-permute-start.17 = (f32[8,128]{1,0:T(8,128)S(1)}, f32[8,128]{1,0:T(8,128)S(1)}, u32[]{:S(2)}, u32[]{:S(2)}) collective-permute-start(f32[8,128]{1,0:T(8,128)S(1)} %add_add_fusion.refs_4_), channel_id=1, source_target_pairs={{0,4},{4,8},{8,12},{12,0},{1,5},{5,9},{9,13},{13,1},{2,6},{6,10},{... | collective-permute-start | bytes 12296 | tf_op jit(solution)/shard_map/ppermute | solution.py:517

commit v6 on v5

--- a/solution.py
+++ b/solution.py
@@ -146,22 +146,23 @@
     return high, low
 
 
-def edge_kernel(slc, estimate, direction, edge, fields):
-    tiles = fields.shape[0]
-    epochs = slc.shape[1]
-    rows = slc.shape[2]
-    look_rows = estimate.shape[1]
-    lane = lax.broadcasted_iota(jnp.int32, (rows, LANES), 1)
-    total = jnp.zeros((rows, LANES), jnp.float32)
+def edge_kernel(first, last, edge):
+    epochs = first.shape[1]
+    lane = lax.broadcasted_iota(jnp.int32, edge.shape, 1)
+    total = jnp.zeros(edge.shape, jnp.float32)
     for part in range(2):
         for epoch in range(epochs):
             at = (part * epochs + epoch) * SIDES
-            total = placed(lane, total, tile_of(slc, part, epoch, tiles - 1), LANES - RADIUS, at)
-            total = placed(lane, total, tile_of(slc, part, epoch, 0), 0, at + RADIUS)
+            total = placed(lane, total, tile_of(last, part, epoch, 0), LANES - RADIUS, at)
+            total = placed(lane, total, tile_of(first, part, epoch, 0), 0, at + RADIUS)
     edge[...] = total.astype(jnp.bfloat16)
-    for tile in range(tiles):
+
+
+def fields_kernel(estimate, direction, fields):
+    look_rows = estimate.shape[1]
+    for tile in range(fields.shape[0]):
         columns = slice(tile * LANES, (tile + 1) * LANES)
-        for epoch in range(epochs):
+        for epoch in range(estimate.shape[0]):
             here = slice(epoch * look_rows, (epoch + 1) * look_rows)
             first, second = split_two(estimate[epoch, :, columns])
             fields[tile, 0, here, :] = first
@@ -253,7 +254,7 @@
     order = jnp.where(in_at >= HALO + rows, order * has_bottom, order).astype(jnp.bfloat16)
 
     lane = lax.broadcasted_iota(jnp.int32, (tall, LANES), 1)
-    for block, (tile_at, strip_at, strip_row, top_at, bottom_at, halo_slot) in enumerate(places):
+    for block, (tile_at, strip_at, strip_row, top_at, bottom_at, halo_row) in enumerate(places):
         tile, strip, top, bottom = inputs[tile_at], inputs[strip_at], inputs[top_at], inputs[bottom_at]
 
         @pl.loop(0, epochs // 2)
@@ -262,9 +263,9 @@
                 columns = []
                 for one in range(2):
                     at = quad * 4 + couple * 2 + one
-                    row = pl.multiple_of(at * HALO, HALO)
+                    row = pl.multiple_of(halo_row + at * HALO, HALO)
                     own = pl.multiple_of(at * rows, rows)
-                    parts = [top[halo_slot, pl.ds(row, HALO), :], tile[pl.ds(own, rows), :], bottom[halo_slot, pl.ds(row, HALO), :]]
+                    parts = [top[pl.ds(row, HALO), :], tile[pl.ds(own, rows), :], bottom[pl.ds(row, HALO), :]]
                     columns.append(jnp.concatenate(parts, axis=0))
                 value = jnp.dot(order, jnp.concatenate(columns, axis=1), preferred_element_type=f32)
                 for one in range(2):
@@ -272,8 +273,8 @@
                     for look in range(LOOK):
                         main[at, look] = value[look * tall : (look + 1) * tall, one * LANES : (one + 1) * LANES]
 
-        last = slice(2 * epochs * HALO, 2 * epochs * HALO + HALO)
-        parts = [top[halo_slot, last, :], strip[strip_row : strip_row + rows, :], bottom[halo_slot, last, :]]
+        last = slice(halo_row + 2 * epochs * HALO, halo_row + 2 * epochs * HALO + HALO)
+        parts = [top[last, :], strip[strip_row : strip_row + rows, :], bottom[last, :]]
         by_look = jnp.dot(order, jnp.concatenate(parts, axis=0), preferred_element_type=f32)
         for at in range(2 * epochs):
             value = jnp.zeros((tall, LANES), f32)
@@ -540,22 +541,34 @@
 
     beside = [tiles - 1, 0, 1]
     far = list(range(2, tiles - 1))
-    tile = {0: tile_for(0), 1: fetched(tile_for, 1), tiles - 1: fetched(tile_for, tiles - 1)}
+    cut = {shift: tile_for(shift) for shift in beside}
+    tile = {0: cut[0], 1: fetched(cut.get, 1), tiles - 1: fetched(cut.get, tiles - 1)}
+    slc, estimate, direction, cut = lax.optimization_barrier((slc, estimate, direction, cut))
 
     params = jnp.zeros((rows, LANES), f32)
     listed = jnp.concatenate([offsets.astype(f32), weights, weights, weights], axis=1)
     params = lax.dynamic_update_slice(params, listed, (0, PARAM_LANE))
-    edge, fields = pl.pallas_call(
+    outer_tile = (2, epochs, rows, LANES)
+    edge = pl.pallas_call(
         edge_kernel,
-        out_shape=(
-            jax.ShapeDtypeStruct((rows, LANES), bf16),
-            jax.ShapeDtypeStruct((tiles, 3, epochs * look_rows, LANES), bf16),
-        ),
-        in_specs=[VMEM] * 3,
-        out_specs=(VMEM,) * 2,
+        out_shape=jax.ShapeDtypeStruct((rows, LANES), bf16),
+        grid=(1,),
+        in_specs=[
+            pl.BlockSpec(outer_tile, lambda _: (0, 0, 0, 0)),
+            pl.BlockSpec(outer_tile, lambda _: (0, 0, 0, tiles - 1)),
+        ],
+        out_specs=pl.BlockSpec((rows, LANES), lambda _: (0, 0)),
+        compiler_params=params_of,
+        cost_estimate=pl.CostEstimate(flops=1_000_000, bytes_accessed=1_000_000, transcendentals=0),
+    )(slc, slc)
+    fields = pl.pallas_call(
+        fields_kernel,
+        out_shape=jax.ShapeDtypeStruct((tiles, 3, epochs * look_rows, LANES), bf16),
+        in_specs=[VMEM] * 2,
+        out_specs=VMEM,
         compiler_params=params_of,
         cost_estimate=pl.CostEstimate(flops=1_000_000, bytes_accessed=2_000_000, transcendentals=0),
-    )(slc, estimate, direction)
+    )(estimate, direction)
     before, after = swapped(edge, edge, "sub")
     sub = lax.axis_index("sub")
     lane = lax.broadcasted_iota(jnp.int32, (rows, LANES), 1)
@@ -592,26 +605,18 @@
     spaces = lax.axis_size("space")
     present = jnp.stack([space > 0, space < spaces - 1]).astype(f32)
 
-    def halo(blocks):
+    def halo(pieces):
         def border(from_row):
-            parts = []
-            for block in blocks:
-                if block in tile:
-                    own = tile[block].reshape(2 * epochs, rows, LANES)
-                    rim = strip[block].reshape(1, rows, LANES)
-                    pieces = [own, rim]
-                else:
-                    pieces = [both[block].reshape(2 * epochs + 1, rows, LANES)]
-                for piece in pieces:
-                    cut = lax.dynamic_slice_in_dim(piece, from_row, HALO, axis=1)
-                    parts.append(cut.reshape(-1, LANES))
-            return jnp.concatenate(parts, axis=0).reshape(len(blocks), (2 * epochs + 1) * HALO, LANES)
+            cuts = [lax.dynamic_slice_in_dim(piece, from_row, HALO, axis=1).reshape(-1, LANES) for piece in pieces]
+            return jnp.concatenate(cuts, axis=0)
 
         if spaces == 2:
-            mine = border(jnp.where(space == 0, rows - HALO, 0))
-            got = lax.ppermute(mine, "space", [(0, 1), (1, 0)])
+            got = lax.ppermute(border(jnp.where(space == 0, rows - HALO, 0)), "space", [(0, 1), (1, 0)])
             return got, got
         return swapped(border(rows - HALO), border(0), "space")
+
+    def by_rows(array):
+        return array.reshape(-1, rows, LANES)
 
     def params_in(block):
         source = strip[block] if block in strip else both[block][tile_rows:]
@@ -623,7 +628,9 @@
         weight = listed[:, SLOTS : 2 * SLOTS] + listed[:, 2 * SLOTS : 3 * SLOTS] + listed[:, 3 * SLOTS :]
         return mate.reshape(-1), weight.reshape(-1)
 
-    near_halo = halo(beside)
+    mine = lax.optimization_barrier((tile[0], strip[0], strip[1], strip[tiles - 1]))
+    own_halo = halo([by_rows(mine[0]), by_rows(mine[1])])
+    near_halo = halo([by_rows(array[block]) for block in (1, tiles - 1) for array in (tile, strip)])
     def pair_stage(loaded):
         own = loaded[:-1]
         mate, weight = pairs_of(own, loaded)
@@ -642,8 +649,11 @@
                 at = index_of(tile[block]), index_of(strip[block]), 0
             else:
                 at = index_of(both[block]), index_of(both[block]), tile_rows
-            source, slots = (near_halo, beside) if block in beside else (far_halo, far)
-            places.append(at + (index_of(source[0]), index_of(source[1]), slots.index(block)))
+            source, slots = (near_halo, [1, tiles - 1]) if block in beside else (far_halo, far)
+            if block == 0:
+                source, slots = own_halo, [0]
+            halo_row = slots.index(block) * (2 * epochs + 1) * HALO
+            places.append(at + (index_of(source[0]), index_of(source[1]), halo_row))
         here = len(loaded) * epochs
         owned = len(own) * epochs
         group = 2 * SLOTS
@@ -672,7 +682,7 @@
     far_stage = list(range(1, tiles))
     near_pairs = pair_stage(near_stage)
     both, near_pairs = lax.optimization_barrier((both, near_pairs))
-    far_halo = halo(far)
+    far_halo = halo([by_rows(both[block]) for block in far])
     far_pairs = pair_stage(far_stage)
 
     listed = jnp.concatenate([params_in(block) for block in range(tiles)], axis=0)
@@ -692,18 +702,18 @@
         cost_estimate=pl.CostEstimate(flops=10_000_000, bytes_accessed=8_000_000, transcendentals=0),
     )(partner, *[field[block] for block in range(tiles)], near_pairs[0], far_pairs[0], near_pairs[1], far_pairs[1])
 
+    along = [sums] + [to_ahead(sums, "epoch", by) for by in range(1, tiles)]
+    here = sum(along[1:], along[0])
     place = ("space", "sub")
     count = spaces * lax.axis_size("sub")
-    shared = [sums] + [lax.ppermute(sums, place, [(i, (i + by) % count) for i in range(count)]) for by in range(1, count)]
-    here = sum(shared[1:], shared[0])
-    scalars = [here] + [to_ahead(here, "epoch", by) for by in range(1, tiles)]
+    scalars = [here] + [lax.ppermute(here, place, [(i, (i + by) % count) for i in range(count)]) for by in range(1, count)]
     returned = [gradient[:epochs]]
     returned += [to_ahead(gradient[by * epochs : (by + 1) * epochs], "epoch", by) for by in range(1, tiles)]
     cell_count = float(total * look_rows * spaces * columns * lax.axis_size("sub"))
     return pl.pallas_call(
         functools.partial(update_kernel, cell_count),
         out_shape=(jax.ShapeDtypeStruct(estimate.shape, f32),) * 2,
-        in_specs=[SMEM] * 2 + [VMEM] * (2 + 2 * tiles),
+        in_specs=[SMEM] * 2 + [VMEM] * (2 + tiles + count),
         out_specs=(VMEM, VMEM),
         compiler_params=params_of,
         cost_estimate=pl.CostEstimate(flops=1_000_000, bytes_accessed=2_000_000, transcendentals=0),

time: 75 us -> 70.7 us (0.943); the launches traced: 74.7 us -> 69.4 us
  waiting for transfers between devices: 17.2 us -> 9.08 us
  starting transfers between devices: 27.3 us -> 28.8 us
  other arithmetic: 0.68 us -> 1.98 us
    ppermute x14, waiting for transfers between devices: 14.3 us -> 4.26 us  [to_ahead(): return lax.ppermute(x, axis, [(i, (i + by) % size) for i in range(size)])]
    unnamed x23 -> x24, local copies, waits for them, and re-layouts: 5.21 us -> 2.42 us
    ppermute x5 -> x6, waiting for transfers between devices: 2.89 us -> 4.82 us  [the longest x3 2.69 us: halo(): lax.ppermute(border(jnp.where(space == 0, rows - HALO, 0)), 'space', [(0,...]
    dynamic_slice x1 -> x2, local copies, waits for them, and re-layouts: 0.89 us -> 2.82 us  [tile_for(): lax.dynamic_slice_in_dim(slc, for_device(shift) * LANES, LANES, axis=3)]
    ppermute x14, starting transfers between devices: 22 us -> 23.4 us  [to_ahead(): return lax.ppermute(x, axis, [(i, (i + by) % size) for i in range(size)])]
    ppermute x5 -> x6, starting transfers between devices: 4.81 us -> 5.33 us  [the longest x3 3.72 us: halo(): lax.ppermute(border(jnp.where(space == 0, rows - HALO, 0)), 'space', [(0,...]
  transfers between devices with their start and end apart: 20 -> 21, of which waited for: 6 -> 5; matrix products, arithmetic and copies ran while one was open for 3% -> 6% of each run, Pallas kernels for 24% -> 26%
where the time goes in v6:
time: 70.7 us; the launch traced here: 69.4 us
  starting transfers between devices  28.8 us (41%)
  Pallas kernels  21.4 us (30%)
  waiting for transfers between devices  9.08 us (13%)
  local copies, waits for them, and re-layouts  6.5 us (9%)
  other arithmetic  1.98 us (3%)
  between operations  1.62 us (2%)
    ppermute x14, starting transfers between devices, to_ahead(): return lax.ppermute(x, axis, [(i, (i + by) % size) for i in range(size)])  23.4 us
    pallas_call x2, Pallas kernels, pair_stage(): pl.pallas_call(functools.partial(pair_kernel, (epochs, rows, len(operands...  17.5 us
    ppermute x14, waiting for transfers between devices, to_ahead(): return lax.ppermute(x, axis, [(i, (i + by) % size) for i in range(size)])  4.26 us
    ppermute x3, starting transfers between devices, halo(): lax.ppermute(border(jnp.where(space == 0, rows - HALO, 0)), 'space', [(0,...  3.72 us
    dynamic_slice x2, local copies, waits for them, and re-layouts, tile_for(): lax.dynamic_slice_in_dim(slc, for_device(shift) * LANES, LANES, axis=3)  2.82 us
    ppermute x3, waiting for transfers between devices, halo(): lax.ppermute(border(jnp.where(space == 0, rows - HALO, 0)), 'space', [(0,...  2.69 us
    unnamed x24, local copies, waits for them, and re-layouts  2.42 us
    pallas_call x1, Pallas kernels, transposed_plan(): pl.pallas_call(functools.partial(gradient_kernel, (tiles, epochs, stages)...  2.24 us
  transfers between devices with their start and end apart: 21, of which 5 were waited for; matrix products, arithmetic and copies ran while one was open for 6% of the time, Pallas kernels for 26%

profile of v6, /device:TPU:0, one launch (start us, length us, event | category | flops | bytes accessed | tf_op | source)
XLA Modules:
  0.0 69.4 jit_solution(6744635980842197191)
XLA Ops:
  0.7 2.1 %constant_dynamic-slice_fusion.8 = (bf16[2,8,64,128]{3,2,1,0:T(8,128)(2,1)}, bf16[2,8,64,128]{3,2,1,0:T(8,128)(2,1)}, bf16[2,8,64,128]{3,2,1,0:T(8,128)(2,1)S(1)}) fusion(bf16[2,8,64,512]{3,2,1,0:T(8,128)(2,1)} %slc, s32[]{:T(128)S(6)} %select_n.67, s32[]{:T(128)S(6)} %select_n.66, s32[]{:T(128)S(6)} %select_n.65), kind=kLoop, calls=%fused_computation.71 | loop fusion | bytes 1572876 | tf_op jit(solution)/shard_map/dynamic_slice | solution.py:537
  2.7 5.0 %collective-permute-start.5 = (bf16[1024,128]{1,0:T(8,128)(2,1)}, bf16[1024,128]{1,0:T(8,128)(2,1)S(1)}, u32[]{:S(2)}, u32[]{:S(2)}) collective-permute-start(bf16[1024,128]{1,0:T(8,128)(2,1)} %bitcast.3), channel_id=1, source_target_pairs={{0,12},{4,0},{8,4},{12,8},{1,13},{5,1},{9,5},{13,9},{2,14},{6,2},{... | collective-permute-start | bytes 786440 | tf_op jit(solution)/shard_map/ppermute | solution.py:518
  7.8 0.2 shard_map.77
  8.2 0.7 copy-done.9
  8.8 0.1 copy.12
  8.9 0.7 copy-done.10
  9.6 0.1 copy.13
  9.7 0.8 %constant_dynamic-slice_fusion.7 = bf16[2,8,64,128]{3,2,1,0:T(8,128)(2,1)} fusion(bf16[2,8,64,512]{3,2,1,0:T(8,128)(2,1)S(1)} %copy-done, s32[]{:T(128)S(6)} %select_n.73), kind=kLoop, calls=%fused_computation.70 | loop fusion | bytes 524292 | tf_op jit(solution)/shard_map/dynamic_slice | solution.py:537
  10.4 0.1 select_maximum_fusion.params
  10.5 0.1 copy-done.1
  10.7 0.1 copy-done.2
  10.9 0.1 add_convert_fusion.present
  11.0 0.5 shard_map.78
  11.5 3.9 %collective-permute-start.1 = (bf16[64,128]{1,0:T(8,128)(2,1)S(1)}, bf16[64,128]{1,0:T(8,128)(2,1)S(1)}, u32[]{:S(2)}, u32[]{:S(2)}) collective-permute-start(bf16[64,128]{1,0:T(8,128)(2,1)S(1)} %get-tuple-element.42), channel_id=1, source_target_pairs={{0,12},{4,0},{8,4},{12,8},{1,13},{5,1},{9,5},{13,9},{2,14},{6,2},{... | collective-permute-start | bytes 49160 | tf_op jit(solution)/shard_map/ppermute | solution.py:518
  15.4 0.7 %pad_maximum_fusion = bf16[1088,128]{1,0:T(8,128)(2,1)} fusion(bf16[64,128]{1,0:T(8,128)(2,1)S(1)} %get-tuple-element.44, bf16[1024,128]{1,0:T(8,128)(2,1)S(1)} %bitcast.36), kind=kLoop, calls=%fused_computation | loop fusion | flops 557056 | bytes 557056 | tf_op jit(solution)/shard_map/concatenate | solution.py:595
  16.2 0.6 collective-permute-start.2
  16.8 3.9 %collective-permute-done.1.refs_7_.refs_1_ = bf16[64,128]{1,0:T(8,128)(2,1)S(1)} collective-permute-done((bf16[64,128]{1,0:T(8,128)(2,1)S(1)}, bf16[64,128]{1,0:T(8,128)(2,1)S(1)}, u32[]{:S(2)}, u32[]{:S(2)}) %collective-permute-start.1) | collective-permute-done | bytes 16416 | tf_op jit(solution)/shard_map/ppermute | solution.py:518
  20.7 0.4 collective-permute-done.3.refs_1_.refs_6_
  21.1 1.6 %collective-permute-start.7 = (bf16[272,128]{1,0:T(8,128)(2,1)S(1)}, bf16[272,128]{1,0:T(8,128)(2,1)S(1)}, u32[]{:S(2)}, u32[]{:S(2)}) collective-permute-start(bf16[272,128]{1,0:T(8,128)(2,1)S(1)} %pad_maximum_fusion.2), channel_id=1, source_target_pairs={{0,2},{2,0},{1,3},{3,1},{4,6},{6,4},{5,7},{7,5},{8,10},{10,8},{9,1... | collective-permute-start | bytes 208904 | tf_op jit(solution)/shard_map/ppermute | solution.py:614
  22.7 0.7 slice_convert_fusion.1
  23.5 0.6 collective-permute-start.6
  24.1 0.1 fusion.20
  24.1 0.1 reshape.82.weight
  24.2 0.1 reshape.81.partner
  24.3 0.7 dynamic-slice_bitcast_fusion
  25.0 2.5 %collective-permute-start.10 = (bf16[3,128,128]{2,1,0:T(8,128)(2,1)}, bf16[3,128,128]{2,1,0:T(8,128)(2,1)S(1)}, u32[]{:S(2)}, u32[]{:S(2)}) collective-permute-start(bf16[3,128,128]{2,1,0:T(8,128)(2,1)} %get-tuple-element.35), channel_id=1, source_target_pairs={{0,4},{4,8},{8,12},{12,0},{1,5},{5,9},{9,13},{13,1},{2,6},{6,10},{... | collective-permute-start | bytes 294920 | tf_op jit(solution)/shard_map/ppermute | solution.py:518
  27.5 1.6 %collective-permute-start.8 = (bf16[3,128,128]{2,1,0:T(8,128)(2,1)S(1)}, bf16[3,128,128]{2,1,0:T(8,128)(2,1)S(1)}, u32[]{:S(2)}, u32[]{:S(2)}) collective-permute-start(bf16[3,128,128]{2,1,0:T(8,128)(2,1)S(1)} %get-tuple-element.37), channel_id=1, source_target_pairs={{0,12},{4,0},{8,4},{12,8},{1,13},{5,1},{9,5},{13,9},{2,14},{6,2},{... | collective-permute-start | bytes 294920 | tf_op jit(solution)/shard_map/ppermute | solution.py:518
  29.0 0.6 collective-permute-start.9
  29.6 8.7 %shard_map.79 = (f32[64,16,128]{2,1,0:T(8,128)S(1)}, f32[64,16,128]{2,1,0:T(8,128)S(1)}) custom-call(s32[64]{0:T(128)S(1)} %reshape.81.partner, f32[64]{0:T(128)S(1)} %reshape.82.weight, f32[2]{0:T(128)S(1)} %add_convert_fusion.present, bf16[1024,128]{1,0:T(8,128)(2,1)S(1)} %collective-permute-done.4.refs_0_.refs_5_, ...), custom_call_target="tpu_custom_call" | custom-call | flops 20000000 | bytes 30000000 | tf_op jit(solution)/shard_map/pallas_call | solution.py:662
  38.4 0.1 slice_convert_fusion.3
  38.4 0.6 copy-done.8
  39.1 0.1 reshape.93.partner
  39.2 0.1 reshape.94.weight
  39.3 1.6 %collective-permute-start.11 = (bf16[272,128]{1,0:T(8,128)(2,1)S(1)}, bf16[272,128]{1,0:T(8,128)(2,1)S(1)}, u32[]{:S(2)}, u32[]{:S(2)}) collective-permute-start(bf16[272,128]{1,0:T(8,128)(2,1)S(1)} %bitcast.40), channel_id=1, source_target_pairs={{0,2},{2,0},{1,3},{3,1},{4,6},{6,4},{5,7},{7,5},{8,10},{10,8},{9,1... | collective-permute-start | bytes 208904 | tf_op jit(solution)/shard_map/ppermute | solution.py:614
  40.9 0.1 reshape.92.partner
  41.0 2.7 %collective-permute-done.11.refs_4_ = bf16[272,128]{1,0:T(8,128)(2,1)S(1)} collective-permute-done((bf16[272,128]{1,0:T(8,128)(2,1)S(1)}, bf16[272,128]{1,0:T(8,128)(2,1)S(1)}, u32[]{:S(2)}, u32[]{:S(2)}) %collective-permute-start.11) | collective-permute-done | bytes 69664 | tf_op jit(solution)/shard_map/ppermute | solution.py:614
  43.7 8.7 %shard_map.81 = (f32[64,16,128]{2,1,0:T(8,128)S(1)}, f32[64,16,128]{2,1,0:T(8,128)S(1)}) custom-call(s32[64]{0:T(128)S(1)} %reshape.93.partner, f32[64]{0:T(128)S(1)} %reshape.94.weight, f32[2]{0:T(128)S(1)} %add_convert_fusion.present, bf16[1024,128]{1,0:T(8,128)(2,1)S(1)} %collective-permute-done.5.refs_6_.refs_0_, ...), custom_call_target="tpu_custom_call" | custom-call | flops 20000000 | bytes 30000000 | tf_op jit(solution)/shard_map/pallas_call | solution.py:662
  52.5 2.2 %shard_map.82 = (f32[32,16,128]{2,1,0:T(8,128)S(1)}, f32[8,128]{1,0:T(8,128)S(1)}) custom-call(s32[128]{0:T(128)S(1)} %reshape.92.partner, bf16[3,128,128]{2,1,0:T(8,128)(2,1)S(1)} %dynamic-slice_bitcast_fusion.3.refs_0_, bf16[3,128,128]{2,1,0:T(8,128)(2,1)S(1)} %collective-permute-done.8.refs_1_, bf16[3,128,128]{2,1,0:T(8,128)(2,1)S(1)} %collective-permute-done.9.refs_2_, ...), custom_call_target="tpu_custom_call" | custom-call | flops 10000000 | bytes 8000000 | tf_op jit(solution)/shard_map/pallas_call | solution.py:692
  54.8 2.1 %collective-permute-start.15 = (f32[8,128]{1,0:T(8,128)S(1)}, f32[8,128]{1,0:T(8,128)S(1)}, u32[]{:S(2)}, u32[]{:S(2)}) collective-permute-start(f32[8,128]{1,0:T(8,128)S(1)} %get-tuple-element.31), channel_id=1, source_target_pairs={{0,4},{4,8},{8,12},{12,0},{1,5},{5,9},{9,13},{13,1},{2,6},{6,10},{... | collective-permute-start | bytes 12296 | tf_op jit(solution)/shard_map/ppermute | solution.py:518
  56.8 1.5 %collective-permute-start.16 = (f32[8,128]{1,0:T(8,128)S(1)}, f32[8,128]{1,0:T(8,128)S(1)}, u32[]{:S(2)}, u32[]{:S(2)}) collective-permute-start(f32[8,128]{1,0:T(8,128)S(1)} %get-tuple-element.31), channel_id=1, source_target_pairs={{0,8},{4,12},{8,0},{12,4},{1,9},{5,13},{9,1},{13,5},{2,10},{6,14},... | collective-permute-start | bytes 12296 | tf_op jit(solution)/shard_map/ppermute | solution.py:518
  58.4 1.7 %collective-permute-start.17 = (f32[8,128]{1,0:T(8,128)S(1)}, f32[8,128]{1,0:T(8,128)S(1)}, u32[]{:S(2)}, u32[]{:S(2)}) collective-permute-start(f32[8,128]{1,0:T(8,128)S(1)} %get-tuple-element.31), channel_id=1, source_target_pairs={{0,12},{4,0},{8,4},{12,8},{1,13},{5,1},{9,5},{13,9},{2,14},{6,2},{... | collective-permute-start | bytes 12296 | tf_op jit(solution)/shard_map/ppermute | solution.py:518
  60.1 0.4 collective-permute-start.12
  60.5 1.4 %collective-permute-start.13 = (f32[8,16,128]{2,1,0:T(8,128)S(1)}, f32[8,16,128]{2,1,0:T(8,128)S(1)}, u32[]{:S(2)}, u32[]{:S(2)}) collective-permute-start(f32[8,16,128]{2,1,0:T(8,128)S(1)} %get-tuple-element.39), channel_id=1, source_target_pairs={{0,8},{4,12},{8,0},{12,4},{1,9},{5,13},{9,1},{13,5},{2,10},{6,14},... | collective-permute-start | bytes 196616 | tf_op jit(solution)/shard_map/ppermute | solution.py:518
  61.9 2.1 %collective-permute-start.14 = (f32[8,16,128]{2,1,0:T(8,128)S(1)}, f32[8,16,128]{2,1,0:T(8,128)S(1)}, u32[]{:S(2)}, u32[]{:S(2)}) collective-permute-start(f32[8,16,128]{2,1,0:T(8,128)S(1)} %get-tuple-element.38), channel_id=1, source_target_pairs={{0,12},{4,0},{8,4},{12,8},{1,13},{5,1},{9,5},{13,9},{2,14},{6,2},{... | collective-permute-start | bytes 196616 | tf_op jit(solution)/shard_map/ppermute | solution.py:518
  64.1 1.6 %collective-permute-start.19 = (f32[8,128]{1,0:T(8,128)S(1)}, f32[8,128]{1,0:T(8,128)S(1)}, u32[]{:S(2)}, u32[]{:S(2)}) collective-permute-start(f32[8,128]{1,0:T(8,128)S(1)} %add_add_fusion.refs_4_), channel_id=1, source_target_pairs={{0,2},{1,3},{2,0},{3,1},{4,6},{5,7},{6,4},{7,5},{8,10},{9,11},{10,... | collective-permute-start | bytes 12296 | tf_op jit(solution)/shard_map/ppermute | solution.py:709
  65.6 1.5 %collective-permute-done.18.refs_5_ = f32[8,128]{1,0:T(8,128)S(1)} collective-permute-done((f32[8,128]{1,0:T(8,128)S(1)}, f32[8,128]{1,0:T(8,128)S(1)}, u32[]{:S(2)}, u32[]{:S(2)}) %collective-permute-start.18) | collective-permute-done | bytes 4128 | tf_op jit(solution)/shard_map/ppermute | solution.py:709
  67.8 0.7 collective-permute-done.20.refs_7_
  68.4 0.9 %shard_map.83 = (f32[8,16,512]{2,1,0:T(8,128)}, f32[8,16,512]{2,1,0:T(8,128)}) custom-call(s32[1]{0:T(128)} %bitcast.me, f32[1]{0:T(128)S(6)} %copy.16.prev_mean, f32[8,16,512]{2,1,0:T(8,128)S(1)} %copy-done.1, f32[8,16,512]{2,1,0:T(8,128)S(1)} %copy-done.2, f32[8,16,128]{2,1,0:T(8,128)S(1)} %get-tuple-element.41.refs_0_, ...), custom_call_target="tpu_custom_call" | custom-call | flops 1000000 | bytes 2000000 | tf_op jit(solution)/shard_map/pallas_call | solution.py:713
  (62 shorter events, 0.7 us)
Async XLA Ops:
  0.6 7.2 %copy-start = (bf16[2,8,64,512]{3,2,1,0:T(8,128)(2,1)S(1)}, bf16[2,8,64,512]{3,2,1,0:T(8,128)(2,1)}, u32[]{:S(2)}) copy-start(bf16[2,8,64,512]{3,2,1,0:T(8,128)(2,1)} %slc) | copy-start | bytes 3145732
  2.7 20.6 %collective-permute-start.5 = (bf16[1024,128]{1,0:T(8,128)(2,1)}, bf16[1024,128]{1,0:T(8,128)(2,1)S(1)}, u32[]{:S(2)}, u32[]{:S(2)}) collective-permute-start(bf16[1024,128]{1,0:T(8,128)(2,1)} %bitcast.3), channel_id=1, source_target_pairs={{0,12},{4,0},{8,4},{12,8},{1,13},{5,1},{9,5},{13,9},{2,14},{6,2},{... | collective-permute-start | bytes 786440 | tf_op jit(solution)/shard_map/ppermute | solution.py:518
  7.8 15.6 %collective-permute-start.4 = (bf16[1024,128]{1,0:T(8,128)(2,1)}, bf16[1024,128]{1,0:T(8,128)(2,1)S(1)}, u32[]{:S(2)}, u32[]{:S(2)}) collective-permute-start(bf16[1024,128]{1,0:T(8,128)(2,1)} %bitcast.2), channel_id=1, source_target_pairs={{0,4},{4,8},{8,12},{12,0},{1,5},{5,9},{9,13},{13,1},{2,6},{6,10},{... | collective-permute-start | bytes 786440 | tf_op jit(solution)/shard_map/ppermute | solution.py:518
  8.0 2.9 %collective-permute-start = (bf16[64,128]{1,0:T(8,128)(2,1)S(1)}, bf16[64,128]{1,0:T(8,128)(2,1)S(1)}, u32[]{:S(2)}, u32[]{:S(2)}) collective-permute-start(bf16[64,128]{1,0:T(8,128)(2,1)S(1)} %shard_map.77), channel_id=1, source_target_pairs={{0,1},{1,0},{2,3},{3,2},{4,5},{5,4},{6,7},{7,6},{8,9},{9,8},{10,11... | collective-permute-start | bytes 49160 | tf_op jit(solution)/shard_map/ppermute | solution.py:509
  8.1 0.7 copy-start.9
  8.9 0.7 copy-start.10
  9.7 1.0 %copy-start.1 = (f32[8,16,512]{2,1,0:T(8,128)S(1)}, f32[8,16,512]{2,1,0:T(8,128)}, u32[]{:S(2)}) copy-start(f32[8,16,512]{2,1,0:T(8,128)} %estimate.1) | copy-start | bytes 786436
  9.7 1.1 %copy-start.2 = (f32[8,16,512]{2,1,0:T(8,128)S(1)}, f32[8,16,512]{2,1,0:T(8,128)}, u32[]{:S(2)}) copy-start(f32[8,16,512]{2,1,0:T(8,128)} %direction.1) | copy-start | bytes 786436
  11.0 4.4 %copy-start.3 = (bf16[2,8,64,128]{3,2,1,0:T(8,128)(2,1)S(1)}, bf16[2,8,64,128]{3,2,1,0:T(8,128)(2,1)}, u32[]{:S(2)}) copy-start(bf16[2,8,64,128]{3,2,1,0:T(8,128)(2,1)} %constant_dynamic-slice_fusion.7) | copy-start | bytes 786436
  11.5 9.2 %collective-permute-start.1 = (bf16[64,128]{1,0:T(8,128)(2,1)S(1)}, bf16[64,128]{1,0:T(8,128)(2,1)S(1)}, u32[]{:S(2)}, u32[]{:S(2)}) collective-permute-start(bf16[64,128]{1,0:T(8,128)(2,1)S(1)} %get-tuple-element.42), channel_id=1, source_target_pairs={{0,12},{4,0},{8,4},{12,8},{1,13},{5,1},{9,5},{13,9},{2,14},{6,2},{... | collective-permute-start | bytes 49160 | tf_op jit(solution)/shard_map/ppermute | solution.py:518
  15.4 5.7 %collective-permute-start.3 = (bf16[64,128]{1,0:T(8,128)(2,1)S(1)}, bf16[64,128]{1,0:T(8,128)(2,1)S(1)}, u32[]{:S(2)}, u32[]{:S(2)}) collective-permute-start(bf16[64,128]{1,0:T(8,128)(2,1)S(1)} %get-tuple-element.43), channel_id=1, source_target_pairs={{0,4},{4,8},{8,12},{12,0},{1,5},{5,9},{9,13},{13,1},{2,6},{6,10},{... | collective-permute-start | bytes 49160 | tf_op jit(solution)/shard_map/ppermute | solution.py:518
  16.2 7.9 %copy-start.4 = (f32[8,16]{1,0:T(8,128)}, f32[8,16]{1,0:T(8,128)S(1)}, u32[]{:S(2)}) copy-start(f32[8,16]{1,0:T(8,128)S(1)} %slice_convert_fusion.2) | copy-start | bytes 1540
  16.2 22.2 %collective-permute-start.2 = (bf16[1088,128]{1,0:T(8,128)(2,1)}, bf16[1088,128]{1,0:T(8,128)(2,1)S(1)}, u32[]{:S(2)}, u32[]{:S(2)}) collective-permute-start(bf16[1088,128]{1,0:T(8,128)(2,1)} %pad_maximum_fusion), channel_id=1, source_target_pairs={{0,8},{4,12},{8,0},{12,4},{1,9},{5,13},{9,1},{13,5},{2,10},{6,14},... | collective-permute-start | bytes 835592 | tf_op jit(solution)/shard_map/ppermute | solution.py:518
  21.1 8.0 %collective-permute-start.7 = (bf16[272,128]{1,0:T(8,128)(2,1)S(1)}, bf16[272,128]{1,0:T(8,128)(2,1)S(1)}, u32[]{:S(2)}, u32[]{:S(2)}) collective-permute-start(bf16[272,128]{1,0:T(8,128)(2,1)S(1)} %pad_maximum_fusion.2), channel_id=1, source_target_pairs={{0,2},{2,0},{1,3},{3,1},{4,6},{6,4},{5,7},{7,5},{8,10},{10,8},{9,1... | collective-permute-start | bytes 208904 | tf_op jit(solution)/shard_map/ppermute | solution.py:614
  22.7 1.4 %copy-start.6 = (f32[8,16]{1,0:T(8,128)}, f32[8,16]{1,0:T(8,128)S(1)}, u32[]{:S(2)}) copy-start(f32[8,16]{1,0:T(8,128)S(1)} %slice_convert_fusion) | copy-start | bytes 1540
  23.5 6.1 %collective-permute-start.6 = (bf16[544,128]{1,0:T(8,128)(2,1)S(1)}, bf16[544,128]{1,0:T(8,128)(2,1)S(1)}, u32[]{:S(2)}, u32[]{:S(2)}) collective-permute-start(bf16[544,128]{1,0:T(8,128)(2,1)S(1)} %pad_maximum_fusion.1), channel_id=1, source_target_pairs={{0,2},{2,0},{1,3},{3,1},{4,6},{6,4},{5,7},{7,5},{8,10},{10,8},{9,1... | collective-permute-start | bytes 417800 | tf_op jit(solution)/shard_map/ppermute | solution.py:614
  25.0 27.5 %collective-permute-start.10 = (bf16[3,128,128]{2,1,0:T(8,128)(2,1)}, bf16[3,128,128]{2,1,0:T(8,128)(2,1)S(1)}, u32[]{:S(2)}, u32[]{:S(2)}) collective-permute-start(bf16[3,128,128]{2,1,0:T(8,128)(2,1)} %get-tuple-element.35), channel_id=1, source_target_pairs={{0,4},{4,8},{8,12},{12,0},{1,5},{5,9},{9,13},{13,1},{2,6},{6,10},{... | collective-permute-start | bytes 294920 | tf_op jit(solution)/shard_map/ppermute | solution.py:518
  27.5 25.0 %collective-permute-start.8 = (bf16[3,128,128]{2,1,0:T(8,128)(2,1)S(1)}, bf16[3,128,128]{2,1,0:T(8,128)(2,1)S(1)}, u32[]{:S(2)}, u32[]{:S(2)}) collective-permute-start(bf16[3,128,128]{2,1,0:T(8,128)(2,1)S(1)} %get-tuple-element.37), channel_id=1, source_target_pairs={{0,12},{4,0},{8,4},{12,8},{1,13},{5,1},{9,5},{13,9},{2,14},{6,2},{... | collective-permute-start | bytes 294920 | tf_op jit(solution)/shard_map/ppermute | solution.py:518
  29.0 23.5 %collective-permute-start.9 = (bf16[3,128,128]{2,1,0:T(8,128)(2,1)S(1)}, bf16[3,128,128]{2,1,0:T(8,128)(2,1)S(1)}, u32[]{:S(2)}, u32[]{:S(2)}) collective-permute-start(bf16[3,128,128]{2,1,0:T(8,128)(2,1)S(1)} %get-tuple-element.36), channel_id=1, source_target_pairs={{0,8},{4,12},{8,0},{12,4},{1,9},{5,13},{9,1},{13,5},{2,10},{6,14},... | collective-permute-start | bytes 294920 | tf_op jit(solution)/shard_map/ppermute | solution.py:518
  38.4 0.7 copy-start.8
  39.3 1.6 %copy-start.5 = (f32[8,16]{1,0:T(8,128)S(1)}, f32[8,16]{1,0:T(8,128)}, u32[]{:S(2)}) copy-start(f32[8,16]{1,0:T(8,128)} %copy-done.4) | copy-start | bytes 1540
  39.3 1.6 %copy-start.7 = (f32[8,16]{1,0:T(8,128)S(1)}, f32[8,16]{1,0:T(8,128)}, u32[]{:S(2)}) copy-start(f32[8,16]{1,0:T(8,128)} %copy-done.6) | copy-start | bytes 1540
  39.3 4.4 %collective-permute-start.11 = (bf16[272,128]{1,0:T(8,128)(2,1)S(1)}, bf16[272,128]{1,0:T(8,128)(2,1)S(1)}, u32[]{:S(2)}, u32[]{:S(2)}) collective-permute-start(bf16[272,128]{1,0:T(8,128)(2,1)S(1)} %bitcast.40), channel_id=1, source_target_pairs={{0,2},{2,0},{1,3},{3,1},{4,6},{6,4},{5,7},{7,5},{8,10},{10,8},{9,1... | collective-permute-start | bytes 208904 | tf_op jit(solution)/shard_map/ppermute | solution.py:614
  54.8 7.1 %collective-permute-start.15 = (f32[8,128]{1,0:T(8,128)S(1)}, f32[8,128]{1,0:T(8,128)S(1)}, u32[]{:S(2)}, u32[]{:S(2)}) collective-permute-start(f32[8,128]{1,0:T(8,128)S(1)} %get-tuple-element.31), channel_id=1, source_target_pairs={{0,4},{4,8},{8,12},{12,0},{1,5},{5,9},{9,13},{13,1},{2,6},{6,10},{... | collective-permute-start | bytes 12296 | tf_op jit(solution)/shard_map/ppermute | solution.py:518
  56.8 7.2 %collective-permute-start.16 = (f32[8,128]{1,0:T(8,128)S(1)}, f32[8,128]{1,0:T(8,128)S(1)}, u32[]{:S(2)}, u32[]{:S(2)}) collective-permute-start(f32[8,128]{1,0:T(8,128)S(1)} %get-tuple-element.31), channel_id=1, source_target_pairs={{0,8},{4,12},{8,0},{12,4},{1,9},{5,13},{9,1},{13,5},{2,10},{6,14},... | collective-permute-start | bytes 12296 | tf_op jit(solution)/shard_map/ppermute | solution.py:518
  58.4 5.6 %collective-permute-start.17 = (f32[8,128]{1,0:T(8,128)S(1)}, f32[8,128]{1,0:T(8,128)S(1)}, u32[]{:S(2)}, u32[]{:S(2)}) collective-permute-start(f32[8,128]{1,0:T(8,128)S(1)} %get-tuple-element.31), channel_id=1, source_target_pairs={{0,12},{4,0},{8,4},{12,8},{1,13},{5,1},{9,5},{13,9},{2,14},{6,2},{... | collective-permute-start | bytes 12296 | tf_op jit(solution)/shard_map/ppermute | solution.py:518
  60.1 8.3 %collective-permute-start.12 = (f32[8,16,128]{2,1,0:T(8,128)S(1)}, f32[8,16,128]{2,1,0:T(8,128)S(1)}, u32[]{:S(2)}, u32[]{:S(2)}) collective-permute-start(f32[8,16,128]{2,1,0:T(8,128)S(1)} %get-tuple-element.40), channel_id=1, source_target_pairs={{0,4},{4,8},{8,12},{12,0},{1,5},{5,9},{9,13},{13,1},{2,6},{6,10},{... | collective-permute-start | bytes 196616 | tf_op jit(solution)/shard_map/ppermute | solution.py:518
  60.5 8.0 %collective-permute-start.13 = (f32[8,16,128]{2,1,0:T(8,128)S(1)}, f32[8,16,128]{2,1,0:T(8,128)S(1)}, u32[]{:S(2)}, u32[]{:S(2)}) collective-permute-start(f32[8,16,128]{2,1,0:T(8,128)S(1)} %get-tuple-element.39), channel_id=1, source_target_pairs={{0,8},{4,12},{8,0},{12,4},{1,9},{5,13},{9,1},{13,5},{2,10},{6,14},... | collective-permute-start | bytes 196616 | tf_op jit(solution)/shard_map/ppermute | solution.py:518
  61.9 6.6 %collective-permute-start.14 = (f32[8,16,128]{2,1,0:T(8,128)S(1)}, f32[8,16,128]{2,1,0:T(8,128)S(1)}, u32[]{:S(2)}, u32[]{:S(2)}) collective-permute-start(f32[8,16,128]{2,1,0:T(8,128)S(1)} %get-tuple-element.38), channel_id=1, source_target_pairs={{0,12},{4,0},{8,4},{12,8},{1,13},{5,1},{9,5},{13,9},{2,14},{6,2},{... | collective-permute-start | bytes 196616 | tf_op jit(solution)/shard_map/ppermute | solution.py:518
  64.0 3.1 %collective-permute-start.18 = (f32[8,128]{1,0:T(8,128)S(1)}, f32[8,128]{1,0:T(8,128)S(1)}, u32[]{:S(2)}, u32[]{:S(2)}) collective-permute-start(f32[8,128]{1,0:T(8,128)S(1)} %add_add_fusion.refs_4_), channel_id=1, source_target_pairs={{0,1},{1,2},{2,3},{3,0},{4,5},{5,6},{6,7},{7,4},{8,9},{9,10},{10,1... | collective-permute-start | bytes 12296 | tf_op jit(solution)/shard_map/ppermute | solution.py:709
  64.1 3.7 %collective-permute-start.19 = (f32[8,128]{1,0:T(8,128)S(1)}, f32[8,128]{1,0:T(8,128)S(1)}, u32[]{:S(2)}, u32[]{:S(2)}) collective-permute-start(f32[8,128]{1,0:T(8,128)S(1)} %add_add_fusion.refs_4_), channel_id=1, source_target_pairs={{0,2},{1,3},{2,0},{3,1},{4,6},{5,7},{6,4},{7,5},{8,10},{9,11},{10,... | collective-permute-start | bytes 12296 | tf_op jit(solution)/shard_map/ppermute | solution.py:709
  67.1 1.3 %collective-permute-start.20 = (f32[8,128]{1,0:T(8,128)S(1)}, f32[8,128]{1,0:T(8,128)S(1)}, u32[]{:S(2)}, u32[]{:S(2)}) collective-permute-start(f32[8,128]{1,0:T(8,128)S(1)} %add_add_fusion.refs_4_), channel_id=1, source_target_pairs={{0,3},{1,0},{2,1},{3,2},{4,7},{5,4},{6,5},{7,6},{8,11},{9,8},{10,9... | collective-permute-start | bytes 12296 | tf_op jit(solution)/shard_map/ppermute | solution.py:709

commit v7 on v6

--- a/solution.py
+++ b/solution.py
@@ -158,16 +158,18 @@
     edge[...] = total.astype(jnp.bfloat16)
 
 
-def fields_kernel(estimate, direction, fields):
+def fields_kernel(me, estimate, direction, *fields):
     look_rows = estimate.shape[1]
-    for tile in range(fields.shape[0]):
-        columns = slice(tile * LANES, (tile + 1) * LANES)
+    tiles = len(fields)
+    for shift, out in enumerate(fields):
+        tile = lax.rem(me[0] + shift, tiles)
+        columns = pl.ds(pl.multiple_of(tile * LANES, LANES), LANES)
         for epoch in range(estimate.shape[0]):
             here = slice(epoch * look_rows, (epoch + 1) * look_rows)
             first, second = split_two(estimate[epoch, :, columns])
-            fields[tile, 0, here, :] = first
-            fields[tile, 1, here, :] = second
-            fields[tile, 2, here, :] = direction[epoch, :, columns].astype(jnp.bfloat16)
+            out[0, here, :] = first
+            out[1, here, :] = second
+            out[2, here, :] = direction[epoch, :, columns].astype(jnp.bfloat16)
 
 
 def tile_of(slc, part, epoch, tile):
@@ -179,8 +181,9 @@
     return jnp.where((lane >= target) & (lane < target + RADIUS), moved, total)
 
 
-def pack_kernel(slc, params, left, right, strips):
-    tiles = strips.shape[0]
+def pack_kernel(me, present, slc, params, before, after, *refs):
+    messages, strips = refs[:-1], refs[-1]
+    tiles = len(messages)
     epochs = slc.shape[1]
     rows = slc.shape[2]
     lane = lax.broadcasted_iota(jnp.int32, (rows, LANES), 1)
@@ -191,12 +194,15 @@
     third = PARAM_LANE + 2 * SLOTS
     split = jnp.where(lane < third, high, jnp.where(lane < third + SLOTS, middle, low))
     split = jnp.where(lane >= PARAM_LANE, split, 0.0)
+    inside = lane < 2 * epochs * SIDES
     for tile in range(tiles):
         total = split
         if tile == 0:
-            total = total + left[...].astype(jnp.float32)
+            edge = before[...].astype(jnp.float32) * present[0]
+            total = jnp.where(inside & (lane % SIDES < RADIUS), edge, total)
         if tile == tiles - 1:
-            total = total + right[...].astype(jnp.float32)
+            edge = after[...].astype(jnp.float32) * present[1]
+            total = jnp.where(inside & (lane % SIDES >= RADIUS), edge, total)
         for part in range(2):
             for epoch in range(epochs):
                 at = (part * epochs + epoch) * SIDES
@@ -205,6 +211,14 @@
                 if tile < tiles - 1:
                     total = placed(lane, total, tile_of(slc, part, epoch, tile + 1), 0, at + RADIUS)
         strips[tile] = total.astype(jnp.bfloat16)
+    for shift, message in enumerate(messages):
+        tile = lax.rem(me[0] + shift, tiles)
+        columns = pl.ds(pl.multiple_of(tile * LANES, LANES), LANES)
+        for part in range(2):
+            for epoch in range(epochs):
+                at = (part * epochs + epoch) * rows
+                message[at : at + rows, :] = slc[part, epoch, :, columns]
+        message[2 * epochs * rows :, :] = strips[tile]
 
 
 def pair_kernel(sizes, places, partner, weight, present, *refs):
@@ -254,8 +268,8 @@
     order = jnp.where(in_at >= HALO + rows, order * has_bottom, order).astype(jnp.bfloat16)
 
     lane = lax.broadcasted_iota(jnp.int32, (tall, LANES), 1)
-    for block, (tile_at, strip_at, strip_row, top_at, bottom_at, halo_row) in enumerate(places):
-        tile, strip, top, bottom = inputs[tile_at], inputs[strip_at], inputs[top_at], inputs[bottom_at]
+    for block, (tile_at, top_at, bottom_at, halo_row) in enumerate(places):
+        tile, top, bottom = inputs[tile_at], inputs[top_at], inputs[bottom_at]
 
         @pl.loop(0, epochs // 2)
         def _(quad):
@@ -274,7 +288,7 @@
                         main[at, look] = value[look * tall : (look + 1) * tall, one * LANES : (one + 1) * LANES]
 
         last = slice(halo_row + 2 * epochs * HALO, halo_row + 2 * epochs * HALO + HALO)
-        parts = [top[last, :], strip[strip_row : strip_row + rows, :], bottom[last, :]]
+        parts = [top[last, :], tile[2 * epochs * rows :, :], bottom[last, :]]
         by_look = jnp.dot(order, jnp.concatenate(parts, axis=0), preferred_element_type=f32)
         for at in range(2 * epochs):
             value = jnp.zeros((tall, LANES), f32)
@@ -412,37 +426,50 @@
     fields = refs[:tiles]
     factors = refs[tiles : tiles + len(stages)]
     pulls = refs[tiles + len(stages) : tiles + 2 * len(stages)]
-    gradient, sums, est, old = refs[tiles + 2 * len(stages) :]
+    gradient, est = refs[tiles + 2 * len(stages) :]
     look_rows = est.shape[1]
-    total = tiles * epochs
     f32 = jnp.float32
     for block in range(tiles):
 
-        @pl.loop(0, epochs)
+        @pl.loop(0, epochs, unroll=4)
         def _(epoch):
             here = pl.ds(pl.multiple_of(epoch * look_rows, look_rows), look_rows)
             est[block * epochs + epoch] = fields[block][0, here, :].astype(f32) + fields[block][1, here, :].astype(f32)
-            old[block * epochs + epoch] = fields[block][2, here, :].astype(f32)
-
-    @pl.loop(0, total)
-    def _(epoch):
-        gradient[epoch] = jnp.zeros((look_rows, LANES), f32)
+            gradient[block * epochs + epoch] = jnp.zeros((look_rows, LANES), f32)
 
     for stage, own_blocks in enumerate(stages):
         for number, block in enumerate(own_blocks):
 
-            @pl.loop(0, epochs)
+            @pl.loop(0, epochs, unroll=2)
             def _(here):
                 epoch = block * epochs + here
                 own_est = est[epoch]
                 own = jnp.zeros((look_rows, LANES), f32)
-                for slot in range(SLOTS):
-                    mate = partner[epoch * SLOTS + slot]
+                mates = [partner[epoch * SLOTS + slot] for slot in range(SLOTS)]
+                values = []
+                for slot, mate in enumerate(mates):
                     pair = (number * epochs + here) * SLOTS + slot
                     weighted = pulls[stage][pair] - factors[stage][pair] * (own_est - est[mate])
                     own = own + weighted
+                    values.append(weighted)
+                for mate, weighted in zip(mates, values):
                     gradient[mate] = gradient[mate] - weighted
                 gradient[epoch] = gradient[epoch] + own
+
+
+def sums_kernel(sizes, partner, gradient, *refs):
+    tiles, epochs, stages = sizes
+    fields = refs[:tiles]
+    factors = refs[tiles : tiles + len(stages)]
+    sums, old = refs[tiles + len(stages) :]
+    look_rows = old.shape[1]
+    f32 = jnp.float32
+    for block in range(tiles):
+
+        @pl.loop(0, epochs, unroll=4)
+        def _(epoch):
+            here = pl.ds(pl.multiple_of(epoch * look_rows, look_rows), look_rows)
+            old[block * epochs + epoch] = fields[block][2, here, :].astype(f32)
 
     zero = jnp.zeros((look_rows, LANES), f32)
     results = (zero,) * 5
@@ -467,7 +494,7 @@
                     old_term = old_term + factor * old_spread * old_spread
                 return norm, crossed, grad_term, mixed, old_term
 
-            results = lax.fori_loop(0, epochs, totals, results)
+            results = lax.fori_loop(0, epochs, totals, results, unroll=2)
     sums[...] = jnp.zeros(sums.shape, f32)
     for at, value in enumerate(results):
         sums[at : at + 1, :] = jnp.sum(value, axis=0, keepdims=True)
@@ -530,24 +557,12 @@
     tile_rows = 2 * epochs * rows
     params_of = pltpu.CompilerParams(vmem_limit_bytes=VMEM_BYTES)
 
-    def for_device(shift):
-        return lax.rem(me + shift, tiles)
-
-    def tile_for(shift):
-        return lax.dynamic_slice_in_dim(slc, for_device(shift) * LANES, LANES, axis=3).reshape(tile_rows, LANES)
-
-    def fetched(send, shift):
-        return to_ahead(send(tiles - shift), "epoch", tiles - shift)
+    def fetched(messages, shift):
+        return to_ahead(messages[tiles - shift], "epoch", tiles - shift)
 
     beside = [tiles - 1, 0, 1]
     far = list(range(2, tiles - 1))
-    cut = {shift: tile_for(shift) for shift in beside}
-    tile = {0: cut[0], 1: fetched(cut.get, 1), tiles - 1: fetched(cut.get, tiles - 1)}
-    slc, estimate, direction, cut = lax.optimization_barrier((slc, estimate, direction, cut))
-
-    params = jnp.zeros((rows, LANES), f32)
-    listed = jnp.concatenate([offsets.astype(f32), weights, weights, weights], axis=1)
-    params = lax.dynamic_update_slice(params, listed, (0, PARAM_LANE))
+    sub = lax.axis_index("sub")
     outer_tile = (2, epochs, rows, LANES)
     edge = pl.pallas_call(
         edge_kernel,
@@ -561,45 +576,35 @@
         compiler_params=params_of,
         cost_estimate=pl.CostEstimate(flops=1_000_000, bytes_accessed=1_000_000, transcendentals=0),
     )(slc, slc)
+    before, after = swapped(edge, edge, "sub")
+    params = jnp.zeros((rows, LANES), f32)
+    listed = jnp.concatenate([offsets.astype(f32), weights, weights, weights], axis=1)
+    params = lax.dynamic_update_slice(params, listed, (0, PARAM_LANE))
+    sub_present = jnp.stack([sub > 0, sub < lax.axis_size("sub") - 1]).astype(f32)
+    messages = pl.pallas_call(
+        pack_kernel,
+        out_shape=(jax.ShapeDtypeStruct((tile_rows + rows, LANES), bf16),) * tiles,
+        in_specs=[SMEM] * 2 + [VMEM] * 4,
+        out_specs=(VMEM,) * tiles,
+        scratch_shapes=[pltpu.VMEM((tiles, rows, LANES), bf16)],
+        compiler_params=params_of,
+        cost_estimate=pl.CostEstimate(flops=3_000_000, bytes_accessed=4_000_000, transcendentals=0),
+    )(me.reshape(1), sub_present, slc, params, before, after)
+    block = {0: messages[0], 1: fetched(messages, 1), tiles - 1: fetched(messages, tiles - 1)}
+
+    estimate, direction, _ = lax.optimization_barrier((estimate, direction, messages))
     fields = pl.pallas_call(
         fields_kernel,
-        out_shape=jax.ShapeDtypeStruct((tiles, 3, epochs * look_rows, LANES), bf16),
-        in_specs=[VMEM] * 2,
-        out_specs=VMEM,
+        out_shape=(jax.ShapeDtypeStruct((3, epochs * look_rows, LANES), bf16),) * tiles,
+        in_specs=[SMEM] + [VMEM] * 2,
+        out_specs=(VMEM,) * tiles,
         compiler_params=params_of,
         cost_estimate=pl.CostEstimate(flops=1_000_000, bytes_accessed=2_000_000, transcendentals=0),
-    )(estimate, direction)
-    before, after = swapped(edge, edge, "sub")
-    sub = lax.axis_index("sub")
-    lane = lax.broadcasted_iota(jnp.int32, (rows, LANES), 1)
-    inside = lane < 2 * epochs * SIDES
-    left = jnp.where(inside & (lane % SIDES < RADIUS) & (sub > 0), before, jnp.zeros_like(edge))
-    right = inside & (lane % SIDES >= RADIUS) & (sub < lax.axis_size("sub") - 1)
-    right = jnp.where(right, after, jnp.zeros_like(edge))
-    strips = pl.pallas_call(
-        pack_kernel,
-        out_shape=jax.ShapeDtypeStruct((tiles, rows, LANES), bf16),
-        in_specs=[VMEM] * 4,
-        out_specs=VMEM,
-        compiler_params=params_of,
-        cost_estimate=pl.CostEstimate(flops=3_000_000, bytes_accessed=2_000_000, transcendentals=0),
-    )(slc, params, left, right)
-
-    def strip_for(shift):
-        return lax.dynamic_index_in_dim(strips, for_device(shift), axis=0, keepdims=False)
-
-    def field_for(shift):
-        return lax.dynamic_index_in_dim(fields, for_device(shift), axis=0, keepdims=False)
-
-    def both_for(shift):
-        return jnp.concatenate([tile_for(shift), strip_for(shift)], axis=0)
-
-    strip = {0: strip_for(0), 1: fetched(strip_for, 1), tiles - 1: fetched(strip_for, tiles - 1)}
-    both = {block: fetched(both_for, block) for block in far}
-    field = {0: field_for(0)}
-    fields = lax.optimization_barrier((fields, tile[1], tile[tiles - 1]))[0]
-    for block in [1, tiles - 1] + far:
-        field[block] = fetched(field_for, block)
+    )(me.reshape(1), estimate, direction)
+    late = lax.optimization_barrier((fields, block[1], block[tiles - 1]))[0]
+    field = {0: fields[0]}
+    for shift in [1, tiles - 1] + far:
+        field[shift] = fetched(late, shift)
 
     space = lax.axis_index("space")
     spaces = lax.axis_size("space")
@@ -615,12 +620,11 @@
             return got, got
         return swapped(border(rows - HALO), border(0), "space")
 
-    def by_rows(array):
-        return array.reshape(-1, rows, LANES)
-
-    def params_in(block):
-        source = strip[block] if block in strip else both[block][tile_rows:]
-        return source[:epochs, PARAM_LANE : PARAM_LANE + 4 * SLOTS].astype(f32)
+    def by_rows(shift):
+        return block[shift].reshape(-1, rows, LANES)
+
+    def params_in(shift):
+        return block[shift][tile_rows : tile_rows + epochs, PARAM_LANE : PARAM_LANE + 4 * SLOTS].astype(f32)
 
     def pairs_of(blocks, loaded):
         listed = jnp.concatenate([params_in(block) for block in blocks], axis=0)
@@ -628,9 +632,11 @@
         weight = listed[:, SLOTS : 2 * SLOTS] + listed[:, 2 * SLOTS : 3 * SLOTS] + listed[:, 3 * SLOTS :]
         return mate.reshape(-1), weight.reshape(-1)
 
-    mine = lax.optimization_barrier((tile[0], strip[0], strip[1], strip[tiles - 1]))
-    own_halo = halo([by_rows(mine[0]), by_rows(mine[1])])
-    near_halo = halo([by_rows(array[block]) for block in (1, tiles - 1) for array in (tile, strip)])
+    own_halo = halo([by_rows(0)])
+    after_halo = lax.optimization_barrier((messages, own_halo))[0]
+    block.update({shift: fetched(after_halo, shift) for shift in far})
+    near_halo = halo([by_rows(1), by_rows(tiles - 1)])
+
     def pair_stage(loaded):
         own = loaded[:-1]
         mate, weight = pairs_of(own, loaded)
@@ -644,16 +650,12 @@
             return len(operands) - 1
 
         places = []
-        for block in loaded:
-            if block in tile:
-                at = index_of(tile[block]), index_of(strip[block]), 0
-            else:
-                at = index_of(both[block]), index_of(both[block]), tile_rows
-            source, slots = (near_halo, [1, tiles - 1]) if block in beside else (far_halo, far)
-            if block == 0:
+        for shift in loaded:
+            source, slots = (near_halo, [1, tiles - 1]) if shift in beside else (far_halo, far)
+            if shift == 0:
                 source, slots = own_halo, [0]
-            halo_row = slots.index(block) * (2 * epochs + 1) * HALO
-            places.append(at + (index_of(source[0]), index_of(source[1]), halo_row))
+            halo_row = slots.index(shift) * (2 * epochs + 1) * HALO
+            places.append((index_of(block[shift]), index_of(source[0]), index_of(source[1]), halo_row))
         here = len(loaded) * epochs
         owned = len(own) * epochs
         group = 2 * SLOTS
@@ -681,39 +683,48 @@
     near_stage = beside
     far_stage = list(range(1, tiles))
     near_pairs = pair_stage(near_stage)
-    both, near_pairs = lax.optimization_barrier((both, near_pairs))
-    far_halo = halo([by_rows(both[block]) for block in far])
+    held, near_pairs = lax.optimization_barrier(([block[shift] for shift in far], near_pairs))
+    block.update(zip(far, held))
+    far_halo = halo([by_rows(shift) for shift in far])
     far_pairs = pair_stage(far_stage)
 
-    listed = jnp.concatenate([params_in(block) for block in range(tiles)], axis=0)
+    listed = jnp.concatenate([params_in(shift) for shift in range(tiles)], axis=0)
     partner = jnp.arange(total, dtype=jnp.int32)[:, None] + listed[:, :SLOTS].astype(jnp.int32)
     partner = lax.rem(partner, total).reshape(-1)
     stages = (tuple(near_stage[:-1]), tuple(far_stage[:-1]))
-    gradient, sums = pl.pallas_call(
-        functools.partial(gradient_kernel, (tiles, epochs, stages)),
-        out_shape=(
-            jax.ShapeDtypeStruct((total, look_rows, LANES), f32),
-            jax.ShapeDtypeStruct((8, LANES), f32),
-        ),
+    block_fields = [field[shift] for shift in range(tiles)]
+    sizes = (tiles, epochs, stages)
+    gradient = pl.pallas_call(
+        functools.partial(gradient_kernel, sizes),
+        out_shape=jax.ShapeDtypeStruct((total, look_rows, LANES), f32),
         in_specs=[SMEM] + [VMEM] * (tiles + 4),
-        out_specs=(VMEM, VMEM),
-        scratch_shapes=[pltpu.VMEM((total, look_rows, LANES), f32)] * 2,
+        out_specs=VMEM,
+        scratch_shapes=[pltpu.VMEM((total, look_rows, LANES), f32)],
+        compiler_params=params_of,
+        cost_estimate=pl.CostEstimate(flops=10_000_000, bytes_accessed=4_000_000, transcendentals=0),
+    )(partner, *block_fields, near_pairs[0], far_pairs[0], near_pairs[1], far_pairs[1])
+    returned = [gradient[:epochs]]
+    returned += [to_ahead(gradient[by * epochs : (by + 1) * epochs], "epoch", by) for by in range(1, tiles)]
+    gradient = lax.optimization_barrier((gradient, returned[1]))[0]
+    sums = pl.pallas_call(
+        functools.partial(sums_kernel, sizes),
+        out_shape=jax.ShapeDtypeStruct((8, LANES), f32),
+        in_specs=[SMEM] + [VMEM] * (tiles + 3),
+        out_specs=VMEM,
+        scratch_shapes=[pltpu.VMEM((total, look_rows, LANES), f32)],
         compiler_params=params_of,
         cost_estimate=pl.CostEstimate(flops=10_000_000, bytes_accessed=8_000_000, transcendentals=0),
-    )(partner, *[field[block] for block in range(tiles)], near_pairs[0], far_pairs[0], near_pairs[1], far_pairs[1])
-
-    along = [sums] + [to_ahead(sums, "epoch", by) for by in range(1, tiles)]
-    here = sum(along[1:], along[0])
+    )(partner, gradient, *block_fields, near_pairs[0], far_pairs[0])
     place = ("space", "sub")
     count = spaces * lax.axis_size("sub")
-    scalars = [here] + [lax.ppermute(here, place, [(i, (i + by) % count) for i in range(count)]) for by in range(1, count)]
-    returned = [gradient[:epochs]]
-    returned += [to_ahead(gradient[by * epochs : (by + 1) * epochs], "epoch", by) for by in range(1, tiles)]
+    along = [sums] + [lax.ppermute(sums, place, [(i, (i + by) % count) for i in range(count)]) for by in range(1, count)]
+    here = sum(along[1:], along[0])
+    scalars = [here] + [to_ahead(here, "epoch", by) for by in range(1, tiles)]
     cell_count = float(total * look_rows * spaces * columns * lax.axis_size("sub"))
     return pl.pallas_call(
         functools.partial(update_kernel, cell_count),
         out_shape=(jax.ShapeDtypeStruct(estimate.shape, f32),) * 2,
-        in_specs=[SMEM] * 2 + [VMEM] * (2 + tiles + count),
+        in_specs=[SMEM] * 2 + [VMEM] * (2 + 2 * tiles),
         out_specs=(VMEM, VMEM),
         compiler_params=params_of,
         cost_estimate=pl.CostEstimate(flops=1_000_000, bytes_accessed=2_000_000, transcendentals=0),

time: 70.7 us -> 80.8 us (1.14); the launches traced: 69.4 us -> 80.6 us
  waiting for transfers between devices: 9.08 us -> 24.2 us
  local copies, waits for them, and re-layouts: 6.5 us -> 3.28 us
  Pallas kernels: 21.4 us -> 23.5 us
  starting transfers between devices: 28.8 us -> 27.4 us
  other arithmetic: 1.98 us -> 0.71 us
    ppermute x14 -> x12, waiting for transfers between devices: 4.26 us -> 17.8 us  [to_ahead(): return lax.ppermute(x, axis, [(i, (i + by) % size) for i in range(size)])]
    dynamic_slice x2 -> x0, local copies, waits for them, and re-layouts: 2.82 us -> none  [tile_for(): lax.dynamic_slice_in_dim(slc, for_device(shift) * LANES, LANES, axis=3)]
    pallas_call x3 -> x4, Pallas kernels: 2.77 us -> 4.88 us  [the longest x1 1.86 us: transposed_plan(): pl.pallas_call(pack_kernel, out_shape=(jax.ShapeDtypeStruct((tile_rows +...]
    ppermute x3, waiting for transfers between devices: 2.69 us -> 4.15 us  [halo(): lax.ppermute(border(jnp.where(space == 0, rows - HALO, 0)), 'space', [(0,...]
    ppermute x3, starting transfers between devices: 1.61 us -> 0.56 us  [transposed_plan(): lax.ppermute(sums, place, [(i, (i + by) % count) for i in range(count)])]
    unnamed x24 -> x14, local copies, waits for them, and re-layouts: 2.42 us -> 2.75 us
    ppermute x14 -> x12, starting transfers between devices: 23.4 us -> 23.3 us  [to_ahead(): return lax.ppermute(x, axis, [(i, (i + by) % size) for i in range(size)])]
  transfers between devices with their start and end apart: 21 -> 19, of which waited for: 5 -> 8; matrix products, arithmetic and copies ran while one was open for 6% -> 2% of each run, Pallas kernels for 26% -> 23%
where the time goes in v7:
time: 80.8 us; the launch traced here: 80.6 us
  starting transfers between devices  27.4 us (34%)
  waiting for transfers between devices  24.2 us (30%)
  Pallas kernels  23.5 us (29%)
  local copies, waits for them, and re-layouts  3.28 us (4%)
  between operations  1.46 us (2%)
    ppermute x12, starting transfers between devices, to_ahead(): return lax.ppermute(x, axis, [(i, (i + by) % size) for i in range(size)])  23.3 us
    ppermute x12, waiting for transfers between devices, to_ahead(): return lax.ppermute(x, axis, [(i, (i + by) % size) for i in range(size)])  17.8 us
    pallas_call x2, Pallas kernels, pair_stage(): pl.pallas_call(functools.partial(pair_kernel, (epochs, rows, len(operands...  17.5 us
    ppermute x3, waiting for transfers between devices, halo(): lax.ppermute(border(jnp.where(space == 0, rows - HALO, 0)), 'space', [(0,...  4.15 us
    ppermute x3, starting transfers between devices, halo(): lax.ppermute(border(jnp.where(space == 0, rows - HALO, 0)), 'space', [(0,...  3 us
    unnamed x14, local copies, waits for them, and re-layouts  2.75 us
    ppermute x3, waiting for transfers between devices, transposed_plan(): lax.ppermute(sums, place, [(i, (i + by) % count) for i in range(count)])  2.28 us
    pallas_call x1, Pallas kernels, transposed_plan(): pl.pallas_call(pack_kernel, out_shape=(jax.ShapeDtypeStruct((tile_rows +...  1.86 us
  transfers between devices with their start and end apart: 19, of which 8 were waited for; matrix products, arithmetic and copies ran while one was open for 2% of the time, Pallas kernels for 23%

profile of v7, /device:TPU:0, one launch (start us, length us, event | category | flops | bytes accessed | tf_op | source)
XLA Modules:
  0.0 80.6 jit_solution(16113576010631218461)
XLA Ops:
  0.6 1.2 %copy-done = bf16[2,8,64,512]{3,2,1,0:T(8,128)(2,1)S(1)} copy-done((bf16[2,8,64,512]{3,2,1,0:T(8,128)(2,1)S(1)}, bf16[2,8,64,512]{3,2,1,0:T(8,128)(2,1)}, u32[]{:S(2)}) %copy-start) | copy-done | bytes 1048600
  1.9 0.2 shard_map.77
  2.1 0.5 collective-permute-start
  2.6 0.7 copy-done.4
  3.3 0.1 copy.12
  3.4 0.7 copy-done.5
  4.1 0.1 copy.13
  4.1 0.1 add_convert_fusion.1.present
  4.2 0.1 select_maximum_fusion.params
  4.3 0.1 add_convert_fusion.present
  4.4 1.9 %shard_map.78 = (bf16[1088,128]{1,0:T(8,128)(2,1)S(1)}, bf16[1088,128]{1,0:T(8,128)(2,1)S(1)}, bf16[1088,128]{1,0:T(8,128)(2,1)}, bf16[1088,128]{1,0:T(8,128)(2,1)S(1)}) custom-call(s32[1]{0:T(128)} %bitcast.me, f32[2]{0:T(128)S(1)} %add_convert_fusion.present, bf16[2,8,64,512]{3,2,1,0:T(8,128)(2,1)S(1)} %copy-done.1, ...), custom_call_target="tpu_custom_call" | custom-call | flops 3000000 | bytes 4000000 | tf_op jit(solution)/shard_map/pallas_call | solution.py:584
  6.3 2.6 %collective-permute-start.4 = (bf16[1088,128]{1,0:T(8,128)(2,1)S(1)}, bf16[1088,128]{1,0:T(8,128)(2,1)S(1)}, u32[]{:S(2)}, u32[]{:S(2)}) collective-permute-start(bf16[1088,128]{1,0:T(8,128)(2,1)S(1)} %get-tuple-element.25), channel_id=1, source_target_pairs={{0,4},{4,8},{8,12},{12,0},{1,5},{5,9},{9,13},{13,1},{2,6},{6,10},{... | collective-permute-start | bytes 835592 | tf_op jit(solution)/shard_map/ppermute | solution.py:545
  8.9 1.6 %collective-permute-start.2 = (bf16[272,128]{1,0:T(8,128)(2,1)S(1)}, bf16[272,128]{1,0:T(8,128)(2,1)S(1)}, u32[]{:S(2)}, u32[]{:S(2)}) collective-permute-start(bf16[272,128]{1,0:T(8,128)(2,1)S(1)} %bitcast.19), channel_id=1, source_target_pairs={{0,2},{2,0},{1,3},{3,1},{4,6},{6,4},{5,7},{7,5},{8,10},{10,8},{9,1... | collective-permute-start | bytes 208904 | tf_op jit(solution)/shard_map/ppermute | solution.py:619
  10.4 2.2 %collective-permute-start.1 = (bf16[1088,128]{1,0:T(8,128)(2,1)S(1)}, bf16[1088,128]{1,0:T(8,128)(2,1)S(1)}, u32[]{:S(2)}, u32[]{:S(2)}) collective-permute-start(bf16[1088,128]{1,0:T(8,128)(2,1)S(1)} %get-tuple-element.27), channel_id=1, source_target_pairs={{0,12},{4,0},{8,4},{12,8},{1,13},{5,1},{9,5},{13,9},{2,14},{6,2},{... | collective-permute-start | bytes 835592 | tf_op jit(solution)/shard_map/ppermute | solution.py:545
  12.8 0.7 shard_map.80
  13.5 2.4 %collective-permute-start.3 = (bf16[1088,128]{1,0:T(8,128)(2,1)}, bf16[1088,128]{1,0:T(8,128)(2,1)S(1)}, u32[]{:S(2)}, u32[]{:S(2)}) collective-permute-start(bf16[1088,128]{1,0:T(8,128)(2,1)} %get-tuple-element.30), channel_id=1, source_target_pairs={{0,8},{4,12},{8,0},{12,4},{1,9},{5,13},{9,1},{13,5},{2,10},{6,14},... | collective-permute-start | bytes 835592 | tf_op jit(solution)/shard_map/ppermute | solution.py:545
  15.8 2.6 %collective-permute-done.4.refs_0_.refs_4_ = bf16[1088,128]{1,0:T(8,128)(2,1)S(1)} collective-permute-done((bf16[1088,128]{1,0:T(8,128)(2,1)S(1)}, bf16[1088,128]{1,0:T(8,128)(2,1)S(1)}, u32[]{:S(2)}, u32[]{:S(2)}) %collective-permute-start.4) | collective-permute-done | bytes 278560 | tf_op jit(solution)/shard_map/ppermute | solution.py:545
  18.4 5.7 %collective-permute-done.1.refs_4_.refs_0_ = bf16[1088,128]{1,0:T(8,128)(2,1)S(1)} collective-permute-done((bf16[1088,128]{1,0:T(8,128)(2,1)S(1)}, bf16[1088,128]{1,0:T(8,128)(2,1)S(1)}, u32[]{:S(2)}, u32[]{:S(2)}) %collective-permute-start.1) | collective-permute-done | bytes 278560 | tf_op jit(solution)/shard_map/ppermute | solution.py:545
  24.2 0.1 slice_convert_fusion
  24.3 0.1 fusion.14
  24.3 0.1 reshape.51.partner
  24.4 0.1 reshape.52.weight
  24.5 1.3 %collective-permute-start.5 = (bf16[544,128]{1,0:T(8,128)(2,1)S(1)}, bf16[544,128]{1,0:T(8,128)(2,1)S(1)}, u32[]{:S(2)}, u32[]{:S(2)}) collective-permute-start(bf16[544,128]{1,0:T(8,128)(2,1)S(1)} %pad_maximum_fusion), channel_id=1, source_target_pairs={{0,2},{2,0},{1,3},{3,1},{4,6},{6,4},{5,7},{7,5},{8,10},{10,8},{9,1... | collective-permute-start | bytes 417800 | tf_op jit(solution)/shard_map/ppermute | solution.py:619
  25.8 2.3 %collective-permute-start.6 = (bf16[3,128,128]{2,1,0:T(8,128)(2,1)}, bf16[3,128,128]{2,1,0:T(8,128)(2,1)S(1)}, u32[]{:S(2)}, u32[]{:S(2)}) collective-permute-start(bf16[3,128,128]{2,1,0:T(8,128)(2,1)} %get-tuple-element.38), channel_id=1, source_target_pairs={{0,12},{4,0},{8,4},{12,8},{1,13},{5,1},{9,5},{13,9},{2,14},{6,2},{... | collective-permute-start | bytes 294920 | tf_op jit(solution)/shard_map/ppermute | solution.py:545
  28.1 8.3 %collective-permute-start.7 = (bf16[3,128,128]{2,1,0:T(8,128)(2,1)S(1)}, bf16[3,128,128]{2,1,0:T(8,128)(2,1)S(1)}, u32[]{:S(2)}, u32[]{:S(2)}) collective-permute-start(bf16[3,128,128]{2,1,0:T(8,128)(2,1)S(1)} %get-tuple-element.39), channel_id=1, source_target_pairs={{0,8},{4,12},{8,0},{12,4},{1,9},{5,13},{9,1},{13,5},{2,10},{6,14},... | collective-permute-start | bytes 294920 | tf_op jit(solution)/shard_map/ppermute | solution.py:545
  36.4 2.0 %collective-permute-start.8 = (bf16[3,128,128]{2,1,0:T(8,128)(2,1)S(1)}, bf16[3,128,128]{2,1,0:T(8,128)(2,1)S(1)}, u32[]{:S(2)}, u32[]{:S(2)}) collective-permute-start(bf16[3,128,128]{2,1,0:T(8,128)(2,1)S(1)} %get-tuple-element.40), channel_id=1, source_target_pairs={{0,4},{4,8},{8,12},{12,0},{1,5},{5,9},{9,13},{13,1},{2,6},{6,10},{... | collective-permute-start | bytes 294920 | tf_op jit(solution)/shard_map/ppermute | solution.py:545
  38.5 8.7 %shard_map.79 = (f32[64,16,128]{2,1,0:T(8,128)S(1)}, f32[64,16,128]{2,1,0:T(8,128)S(1)}) custom-call(s32[64]{0:T(128)S(1)} %reshape.51.partner, f32[64]{0:T(128)S(1)} %reshape.52.weight, f32[2]{0:T(128)S(1)} %add_convert_fusion.1.present, bf16[1088,128]{1,0:T(8,128)(2,1)S(1)} %collective-permute-done.4.refs_0_.refs_4_, ...), custom_call_target="tpu_custom_call" | custom-call | flops 20000000 | bytes 30000000 | tf_op jit(solution)/shard_map/pallas_call | solution.py:664
  47.2 0.1 slice_convert_fusion.2
  47.4 0.1 reshape.57.partner
  47.5 0.1 reshape.59.weight
  47.6 0.1 collective-permute-start.9
  47.8 0.1 reshape.58.partner
  47.9 4.1 %collective-permute-done.9.refs_3_ = bf16[272,128]{1,0:T(8,128)(2,1)S(1)} collective-permute-done((bf16[272,128]{1,0:T(8,128)(2,1)S(1)}, bf16[272,128]{1,0:T(8,128)(2,1)S(1)}, u32[]{:S(2)}, u32[]{:S(2)}) %collective-permute-start.9) | collective-permute-done | bytes 69664 | tf_op jit(solution)/shard_map/ppermute | solution.py:619
  52.0 8.7 %shard_map.81 = (f32[64,16,128]{2,1,0:T(8,128)S(1)}, f32[64,16,128]{2,1,0:T(8,128)S(1)}) custom-call(s32[64]{0:T(128)S(1)} %reshape.58.partner, f32[64]{0:T(128)S(1)} %reshape.59.weight, f32[2]{0:T(128)S(1)} %add_convert_fusion.1.present, bf16[1088,128]{1,0:T(8,128)(2,1)S(1)} %collective-permute-done.1.refs_4_.refs_0_, ...), custom_call_target="tpu_custom_call" | custom-call | flops 20000000 | bytes 30000000 | tf_op jit(solution)/shard_map/pallas_call | solution.py:664
  60.8 1.2 %shard_map.82.gradient = f32[32,16,128]{2,1,0:T(8,128)S(1)} custom-call(s32[128]{0:T(128)S(1)} %reshape.57.partner, bf16[3,128,128]{2,1,0:T(8,128)(2,1)S(1)} %get-tuple-element.34.refs_0_, bf16[3,128,128]{2,1,0:T(8,128)(2,1)S(1)} %collective-permute-done.6.refs_1_, bf16[3,128,128]{2,1,0:T(8,128)(2,1)S(1)} %collective-permute-done.7.refs_2_, ...), custom_call_target="tpu_custom_call" | custom-call | flops 10000000 | bytes 4000000 | tf_op jit(solution)/shard_map/pallas_call | solution.py:697
  62.1 6.0 %collective-permute-done.10.refs_1_ = f32[8,16,128]{2,1,0:T(8,128)S(1)} collective-permute-done((f32[8,16,128]{2,1,0:T(8,128)S(1)}, f32[8,16,128]{2,1,0:T(8,128)S(1)}, u32[]{:S(2)}, u32[]{:S(2)}) %collective-permute-start.10) | collective-permute-done | bytes 65568 | tf_op jit(solution)/shard_map/ppermute | solution.py:545
  68.2 1.1 %shard_map.83 = f32[8,128]{1,0:T(8,128)S(1)} custom-call(s32[128]{0:T(128)S(1)} %reshape.57.partner, f32[32,16,128]{2,1,0:T(8,128)S(1)} %shard_map.82.gradient, bf16[3,128,128]{2,1,0:T(8,128)(2,1)S(1)} %get-tuple-element.34.refs_0_, bf16[3,128,128]{2,1,0:T(8,128)(2,1)S(1)} %collective-permute-done.6.refs_1_, ...), custom_call_target="tpu_custom_call" | custom-call | flops 10000000 | bytes 8000000 | tf_op jit(solution)/shard_map/pallas_call | solution.py:709
  69.3 0.1 collective-permute-start.14
  69.5 0.4 collective-permute-start.13
  69.8 0.3 collective-permute-start.12
  70.1 0.6 collective-permute-start.11
  70.7 2.3 %collective-permute-done.14 = f32[8,128]{1,0:T(8,128)S(1)} collective-permute-done((f32[8,128]{1,0:T(8,128)S(1)}, f32[8,128]{1,0:T(8,128)S(1)}, u32[]{:S(2)}, u32[]{:S(2)}) %collective-permute-start.14) | collective-permute-done | bytes 4128 | tf_op jit(solution)/shard_map/ppermute | solution.py:720
  73.0 1.3 %collective-permute-start.18 = (f32[8,128]{1,0:T(8,128)S(1)}, f32[8,128]{1,0:T(8,128)S(1)}, u32[]{:S(2)}, u32[]{:S(2)}) collective-permute-start(f32[8,128]{1,0:T(8,128)S(1)} %add_add_fusion.refs_4_), channel_id=1, source_target_pairs={{0,12},{4,0},{8,4},{12,8},{1,13},{5,1},{9,5},{13,9},{2,14},{6,2},{... | collective-permute-start | bytes 12296 | tf_op jit(solution)/shard_map/ppermute | solution.py:545
  74.3 1.3 %collective-permute-start.16 = (f32[8,128]{1,0:T(8,128)S(1)}, f32[8,128]{1,0:T(8,128)S(1)}, u32[]{:S(2)}, u32[]{:S(2)}) collective-permute-start(f32[8,128]{1,0:T(8,128)S(1)} %add_add_fusion.refs_4_), channel_id=1, source_target_pairs={{0,4},{4,8},{8,12},{12,0},{1,5},{5,9},{9,13},{13,1},{2,6},{6,10},{... | collective-permute-start | bytes 12296 | tf_op jit(solution)/shard_map/ppermute | solution.py:545
  76.3 0.4 collective-permute-done.18.refs_7_
  76.7 2.1 %collective-permute-done.17.refs_6_ = f32[8,128]{1,0:T(8,128)S(1)} collective-permute-done((f32[8,128]{1,0:T(8,128)S(1)}, f32[8,128]{1,0:T(8,128)S(1)}, u32[]{:S(2)}, u32[]{:S(2)}) %collective-permute-start.17) | collective-permute-done | bytes 4128 | tf_op jit(solution)/shard_map/ppermute | solution.py:545
  78.8 0.9 %collective-permute-done.16.refs_5_ = f32[8,128]{1,0:T(8,128)S(1)} collective-permute-done((f32[8,128]{1,0:T(8,128)S(1)}, f32[8,128]{1,0:T(8,128)S(1)}, u32[]{:S(2)}, u32[]{:S(2)}) %collective-permute-start.16) | collective-permute-done | bytes 4128 | tf_op jit(solution)/shard_map/ppermute | solution.py:545
  79.7 0.9 %shard_map.84 = (f32[8,16,512]{2,1,0:T(8,128)}, f32[8,16,512]{2,1,0:T(8,128)}) custom-call(s32[1]{0:T(128)} %bitcast.me, f32[1]{0:T(128)S(6)} %copy.16.prev_mean, f32[8,16,512]{2,1,0:T(8,128)S(1)} %copy-done.2, f32[8,16,512]{2,1,0:T(8,128)S(1)} %copy-done.3, f32[8,16,128]{2,1,0:T(8,128)S(1)} %get-tuple-element.49.refs_0_, ...), custom_call_target="tpu_custom_call" | custom-call | flops 1000000 | bytes 2000000 | tf_op jit(solution)/shard_map/pallas_call | solution.py:724
  (37 shorter events, 0.5 us)
Async XLA Ops:
  0.6 1.2 %copy-start = (bf16[2,8,64,512]{3,2,1,0:T(8,128)(2,1)S(1)}, bf16[2,8,64,512]{3,2,1,0:T(8,128)(2,1)}, u32[]{:S(2)}) copy-start(bf16[2,8,64,512]{3,2,1,0:T(8,128)(2,1)} %slc.1) | copy-start | bytes 3145732
  1.9 2.5 %copy-start.1 = (bf16[2,8,64,512]{3,2,1,0:T(8,128)(2,1)S(1)}, bf16[2,8,64,512]{3,2,1,0:T(8,128)(2,1)}, u32[]{:S(2)}) copy-start(bf16[2,8,64,512]{3,2,1,0:T(8,128)(2,1)} %slc.1) | copy-start | bytes 3145732
  2.1 2.3 %collective-permute-start = (bf16[64,128]{1,0:T(8,128)(2,1)S(1)}, bf16[64,128]{1,0:T(8,128)(2,1)S(1)}, u32[]{:S(2)}, u32[]{:S(2)}) collective-permute-start(bf16[64,128]{1,0:T(8,128)(2,1)S(1)} %shard_map.77), channel_id=1, source_target_pairs={{0,1},{1,0},{2,3},{3,2},{4,5},{5,4},{6,7},{7,6},{8,9},{9,8},{10,11... | collective-permute-start | bytes 49160 | tf_op jit(solution)/shard_map/ppermute | solution.py:536
  2.6 0.7 copy-start.4
  3.4 0.7 copy-start.5
  4.4 8.4 %copy-start.2 = (f32[8,16,512]{2,1,0:T(8,128)S(1)}, f32[8,16,512]{2,1,0:T(8,128)}, u32[]{:S(2)}) copy-start(f32[8,16,512]{2,1,0:T(8,128)} %estimate.1) | copy-start | bytes 786436
  4.4 8.4 %copy-start.3 = (f32[8,16,512]{2,1,0:T(8,128)S(1)}, f32[8,16,512]{2,1,0:T(8,128)}, u32[]{:S(2)}) copy-start(f32[8,16,512]{2,1,0:T(8,128)} %direction.1) | copy-start | bytes 786436
  6.3 12.2 %collective-permute-start.4 = (bf16[1088,128]{1,0:T(8,128)(2,1)S(1)}, bf16[1088,128]{1,0:T(8,128)(2,1)S(1)}, u32[]{:S(2)}, u32[]{:S(2)}) collective-permute-start(bf16[1088,128]{1,0:T(8,128)(2,1)S(1)} %get-tuple-element.25), channel_id=1, source_target_pairs={{0,4},{4,8},{8,12},{12,0},{1,5},{5,9},{9,13},{13,1},{2,6},{6,10},{... | collective-permute-start | bytes 835592 | tf_op jit(solution)/shard_map/ppermute | solution.py:545
  8.9 4.6 %collective-permute-start.2 = (bf16[272,128]{1,0:T(8,128)(2,1)S(1)}, bf16[272,128]{1,0:T(8,128)(2,1)S(1)}, u32[]{:S(2)}, u32[]{:S(2)}) collective-permute-start(bf16[272,128]{1,0:T(8,128)(2,1)S(1)} %bitcast.19), channel_id=1, source_target_pairs={{0,2},{2,0},{1,3},{3,1},{4,6},{6,4},{5,7},{7,5},{8,10},{10,8},{9,1... | collective-permute-start | bytes 208904 | tf_op jit(solution)/shard_map/ppermute | solution.py:619
  10.4 13.7 %collective-permute-start.1 = (bf16[1088,128]{1,0:T(8,128)(2,1)S(1)}, bf16[1088,128]{1,0:T(8,128)(2,1)S(1)}, u32[]{:S(2)}, u32[]{:S(2)}) collective-permute-start(bf16[1088,128]{1,0:T(8,128)(2,1)S(1)} %get-tuple-element.27), channel_id=1, source_target_pairs={{0,12},{4,0},{8,4},{12,8},{1,13},{5,1},{9,5},{13,9},{2,14},{6,2},{... | collective-permute-start | bytes 835592 | tf_op jit(solution)/shard_map/ppermute | solution.py:545
  13.5 33.8 %collective-permute-start.3 = (bf16[1088,128]{1,0:T(8,128)(2,1)}, bf16[1088,128]{1,0:T(8,128)(2,1)S(1)}, u32[]{:S(2)}, u32[]{:S(2)}) collective-permute-start(bf16[1088,128]{1,0:T(8,128)(2,1)} %get-tuple-element.30), channel_id=1, source_target_pairs={{0,8},{4,12},{8,0},{12,4},{1,9},{5,13},{9,1},{13,5},{2,10},{6,14},... | collective-permute-start | bytes 835592 | tf_op jit(solution)/shard_map/ppermute | solution.py:545
  24.5 14.0 %collective-permute-start.5 = (bf16[544,128]{1,0:T(8,128)(2,1)S(1)}, bf16[544,128]{1,0:T(8,128)(2,1)S(1)}, u32[]{:S(2)}, u32[]{:S(2)}) collective-permute-start(bf16[544,128]{1,0:T(8,128)(2,1)S(1)} %pad_maximum_fusion), channel_id=1, source_target_pairs={{0,2},{2,0},{1,3},{3,1},{4,6},{6,4},{5,7},{7,5},{8,10},{10,8},{9,1... | collective-permute-start | bytes 417800 | tf_op jit(solution)/shard_map/ppermute | solution.py:619
  25.8 34.9 %collective-permute-start.6 = (bf16[3,128,128]{2,1,0:T(8,128)(2,1)}, bf16[3,128,128]{2,1,0:T(8,128)(2,1)S(1)}, u32[]{:S(2)}, u32[]{:S(2)}) collective-permute-start(bf16[3,128,128]{2,1,0:T(8,128)(2,1)} %get-tuple-element.38), channel_id=1, source_target_pairs={{0,12},{4,0},{8,4},{12,8},{1,13},{5,1},{9,5},{13,9},{2,14},{6,2},{... | collective-permute-start | bytes 294920 | tf_op jit(solution)/shard_map/ppermute | solution.py:545
  28.1 32.7 %collective-permute-start.7 = (bf16[3,128,128]{2,1,0:T(8,128)(2,1)S(1)}, bf16[3,128,128]{2,1,0:T(8,128)(2,1)S(1)}, u32[]{:S(2)}, u32[]{:S(2)}) collective-permute-start(bf16[3,128,128]{2,1,0:T(8,128)(2,1)S(1)} %get-tuple-element.39), channel_id=1, source_target_pairs={{0,8},{4,12},{8,0},{12,4},{1,9},{5,13},{9,1},{13,5},{2,10},{6,14},... | collective-permute-start | bytes 294920 | tf_op jit(solution)/shard_map/ppermute | solution.py:545
  36.4 24.4 %collective-permute-start.8 = (bf16[3,128,128]{2,1,0:T(8,128)(2,1)S(1)}, bf16[3,128,128]{2,1,0:T(8,128)(2,1)S(1)}, u32[]{:S(2)}, u32[]{:S(2)}) collective-permute-start(bf16[3,128,128]{2,1,0:T(8,128)(2,1)S(1)} %get-tuple-element.40), channel_id=1, source_target_pairs={{0,4},{4,8},{8,12},{12,0},{1,5},{5,9},{9,13},{13,1},{2,6},{6,10},{... | collective-permute-start | bytes 294920 | tf_op jit(solution)/shard_map/ppermute | solution.py:545
  47.6 4.4 %collective-permute-start.9 = (bf16[272,128]{1,0:T(8,128)(2,1)S(1)}, bf16[272,128]{1,0:T(8,128)(2,1)S(1)}, u32[]{:S(2)}, u32[]{:S(2)}) collective-permute-start(bf16[272,128]{1,0:T(8,128)(2,1)S(1)} %bitcast.20), channel_id=1, source_target_pairs={{0,2},{2,0},{1,3},{3,1},{4,6},{6,4},{5,7},{7,5},{8,10},{10,8},{9,1... | collective-permute-start | bytes 208904 | tf_op jit(solution)/shard_map/ppermute | solution.py:619
  62.0 6.1 %collective-permute-start.10 = (f32[8,16,128]{2,1,0:T(8,128)S(1)}, f32[8,16,128]{2,1,0:T(8,128)S(1)}, u32[]{:S(2)}, u32[]{:S(2)}) collective-permute-start(f32[8,16,128]{2,1,0:T(8,128)S(1)} %get-tuple-element.48), channel_id=1, source_target_pairs={{0,4},{4,8},{8,12},{12,0},{1,5},{5,9},{9,13},{13,1},{2,6},{6,10},{... | collective-permute-start | bytes 196616 | tf_op jit(solution)/shard_map/ppermute | solution.py:545
  69.3 1.5 %collective-permute-start.15 = (f32[8,128]{1,0:T(8,128)S(1)}, f32[8,128]{1,0:T(8,128)S(1)}, u32[]{:S(2)}, u32[]{:S(2)}) collective-permute-start(f32[8,128]{1,0:T(8,128)S(1)} %shard_map.83), channel_id=1, source_target_pairs={{0,3},{1,0},{2,1},{3,2},{4,7},{5,4},{6,5},{7,6},{8,11},{9,8},{10,9... | collective-permute-start | bytes 12296 | tf_op jit(solution)/shard_map/ppermute | solution.py:720
  69.3 3.7 %collective-permute-start.14 = (f32[8,128]{1,0:T(8,128)S(1)}, f32[8,128]{1,0:T(8,128)S(1)}, u32[]{:S(2)}, u32[]{:S(2)}) collective-permute-start(f32[8,128]{1,0:T(8,128)S(1)} %shard_map.83), channel_id=1, source_target_pairs={{0,2},{1,3},{2,0},{3,1},{4,6},{5,7},{6,4},{7,5},{8,10},{9,11},{10,... | collective-permute-start | bytes 12296 | tf_op jit(solution)/shard_map/ppermute | solution.py:720
  69.5 3.5 %collective-permute-start.13 = (f32[8,128]{1,0:T(8,128)S(1)}, f32[8,128]{1,0:T(8,128)S(1)}, u32[]{:S(2)}, u32[]{:S(2)}) collective-permute-start(f32[8,128]{1,0:T(8,128)S(1)} %shard_map.83), channel_id=1, source_target_pairs={{0,1},{1,2},{2,3},{3,0},{4,5},{5,6},{6,7},{7,4},{8,9},{9,10},{10,1... | collective-permute-start | bytes 12296 | tf_op jit(solution)/shard_map/ppermute | solution.py:720
  69.8 6.4 %collective-permute-start.12 = (f32[8,16,128]{2,1,0:T(8,128)S(1)}, f32[8,16,128]{2,1,0:T(8,128)S(1)}, u32[]{:S(2)}, u32[]{:S(2)}) collective-permute-start(f32[8,16,128]{2,1,0:T(8,128)S(1)} %get-tuple-element.46), channel_id=1, source_target_pairs={{0,12},{4,0},{8,4},{12,8},{1,13},{5,1},{9,5},{13,9},{2,14},{6,2},{... | collective-permute-start | bytes 196616 | tf_op jit(solution)/shard_map/ppermute | solution.py:545
  70.1 6.1 %collective-permute-start.11 = (f32[8,16,128]{2,1,0:T(8,128)S(1)}, f32[8,16,128]{2,1,0:T(8,128)S(1)}, u32[]{:S(2)}, u32[]{:S(2)}) collective-permute-start(f32[8,16,128]{2,1,0:T(8,128)S(1)} %get-tuple-element.47), channel_id=1, source_target_pairs={{0,8},{4,12},{8,0},{12,4},{1,9},{5,13},{9,1},{13,5},{2,10},{6,14},... | collective-permute-start | bytes 196616 | tf_op jit(solution)/shard_map/ppermute | solution.py:545
  73.0 3.7 %collective-permute-start.18 = (f32[8,128]{1,0:T(8,128)S(1)}, f32[8,128]{1,0:T(8,128)S(1)}, u32[]{:S(2)}, u32[]{:S(2)}) collective-permute-start(f32[8,128]{1,0:T(8,128)S(1)} %add_add_fusion.refs_4_), channel_id=1, source_target_pairs={{0,12},{4,0},{8,4},{12,8},{1,13},{5,1},{9,5},{13,9},{2,14},{6,2},{... | collective-permute-start | bytes 12296 | tf_op jit(solution)/shard_map/ppermute | solution.py:545
  74.3 4.5 %collective-permute-start.17 = (f32[8,128]{1,0:T(8,128)S(1)}, f32[8,128]{1,0:T(8,128)S(1)}, u32[]{:S(2)}, u32[]{:S(2)}) collective-permute-start(f32[8,128]{1,0:T(8,128)S(1)} %add_add_fusion.refs_4_), channel_id=1, source_target_pairs={{0,8},{4,12},{8,0},{12,4},{1,9},{5,13},{9,1},{13,5},{2,10},{6,14},... | collective-permute-start | bytes 12296 | tf_op jit(solution)/shard_map/ppermute | solution.py:545
  74.3 5.4 %collective-permute-start.16 = (f32[8,128]{1,0:T(8,128)S(1)}, f32[8,128]{1,0:T(8,128)S(1)}, u32[]{:S(2)}, u32[]{:S(2)}) collective-permute-start(f32[8,128]{1,0:T(8,128)S(1)} %add_add_fusion.refs_4_), channel_id=1, source_target_pairs={{0,4},{4,8},{8,12},{12,0},{1,5},{5,9},{9,13},{13,1},{2,6},{6,10},{... | collective-permute-start | bytes 12296 | tf_op jit(solution)/shard_map/ppermute | solution.py:545

commit v8 on v0

--- a/solution.py
+++ b/solution.py
@@ -1,6 +1,10 @@
+import functools
+
 import jax
 import jax.numpy as jnp
 from jax import lax
+from jax.experimental import pallas as pl
+from jax.experimental.pallas import tpu as pltpu
 from jax.sharding import PartitionSpec as P
 
 SLOTS = 4
@@ -43,7 +47,7 @@
     return total
 
 
-def on_device(slc, offsets, weights, estimate, direction, prev_mean):
+def ring_plan(slc, offsets, weights, estimate, direction, prev_mean):
     epochs_here = slc.shape[1]
     look_rows = slc.shape[2] // LOOK
     col_count = slc.shape[3]
@@ -127,6 +131,624 @@
     return (estimate + step_size * new_direction, new_direction)
 
 
+LANES = 128
+SIDES = 2 * RADIUS
+HALO = 16
+PARAM_LANE = 96
+VMEM = pl.BlockSpec(memory_space=pltpu.VMEM)
+SMEM = pl.BlockSpec(memory_space=pltpu.SMEM)
+VMEM_BYTES = 48 * 1024 * 1024
+
+
+def split_two(value):
+    high = value.astype(jnp.bfloat16)
+    low = (value - high.astype(jnp.float32)).astype(jnp.bfloat16)
+    return high, low
+
+
+def edge_kernel(first, last, edge):
+    epochs = first.shape[1]
+    lane = lax.broadcasted_iota(jnp.int32, edge.shape, 1)
+    total = jnp.zeros(edge.shape, jnp.float32)
+    for part in range(2):
+        for epoch in range(epochs):
+            at = (part * epochs + epoch) * SIDES
+            total = placed(lane, total, tile_of(last, part, epoch, 0), LANES - RADIUS, at)
+            total = placed(lane, total, tile_of(first, part, epoch, 0), 0, at + RADIUS)
+    edge[...] = total.astype(jnp.bfloat16)
+
+
+def fields_kernel(me, estimate, direction, *fields):
+    look_rows = estimate.shape[1]
+    tiles = len(fields)
+    for shift, out in enumerate(fields):
+        tile = lax.rem(me[0] + shift, tiles)
+        columns = pl.ds(pl.multiple_of(tile * LANES, LANES), LANES)
+        for epoch in range(estimate.shape[0]):
+            here = slice(epoch * look_rows, (epoch + 1) * look_rows)
+            first, second = split_two(estimate[epoch, :, columns])
+            out[0, here, :] = first
+            out[1, here, :] = second
+            out[2, here, :] = direction[epoch, :, columns].astype(jnp.bfloat16)
+
+
+def tile_of(slc, part, epoch, tile):
+    return slc[part, epoch, :, tile * LANES : (tile + 1) * LANES].astype(jnp.float32)
+
+
+def placed(lane, total, source, start, target):
+    moved = pltpu.roll(source, (target - start) % LANES, axis=1)
+    return jnp.where((lane >= target) & (lane < target + RADIUS), moved, total)
+
+
+def pack_kernel(me, present, slc, params, before, after, *refs):
+    messages, strips = refs[:-1], refs[-1]
+    tiles = len(messages)
+    epochs = slc.shape[1]
+    rows = slc.shape[2]
+    lane = lax.broadcasted_iota(jnp.int32, (rows, LANES), 1)
+    value = params[...]
+    high = value.astype(jnp.bfloat16).astype(jnp.float32)
+    middle = (value - high).astype(jnp.bfloat16).astype(jnp.float32)
+    low = value - high - middle
+    third = PARAM_LANE + 2 * SLOTS
+    split = jnp.where(lane < third, high, jnp.where(lane < third + SLOTS, middle, low))
+    split = jnp.where(lane >= PARAM_LANE, split, 0.0)
+    inside = lane < 2 * epochs * SIDES
+    for tile in range(tiles):
+        total = split
+        if tile == 0:
+            edge = before[...].astype(jnp.float32) * present[0]
+            total = jnp.where(inside & (lane % SIDES < RADIUS), edge, total)
+        if tile == tiles - 1:
+            edge = after[...].astype(jnp.float32) * present[1]
+            total = jnp.where(inside & (lane % SIDES >= RADIUS), edge, total)
+        for part in range(2):
+            for epoch in range(epochs):
+                at = (part * epochs + epoch) * SIDES
+                if tile > 0:
+                    total = placed(lane, total, tile_of(slc, part, epoch, tile - 1), LANES - RADIUS, at)
+                if tile < tiles - 1:
+                    total = placed(lane, total, tile_of(slc, part, epoch, tile + 1), 0, at + RADIUS)
+        strips[tile] = total.astype(jnp.bfloat16)
+    for tile in range(tiles):
+        shift = lax.rem(tile - me[0] + tiles, tiles)
+        for number, message in enumerate(messages):
+
+            @pl.when(shift == number)
+            def _():
+                for part in range(2):
+                    for epoch in range(epochs):
+                        at = (part * epochs + epoch) * rows
+                        message[at : at + rows, :] = slc[part, epoch, :, tile * LANES : (tile + 1) * LANES]
+                message[2 * epochs * rows :, :] = strips[tile]
+
+
+def look_order(from_rows, keep):
+    looks = from_rows // LOOK
+    to = lax.broadcasted_iota(jnp.int32, (from_rows, from_rows), 0)
+    at = lax.broadcasted_iota(jnp.int32, (from_rows, from_rows), 1)
+    order = (at == to % looks * LOOK + to // looks).astype(jnp.float32)
+    return (order * keep(at)).astype(jnp.bfloat16)
+
+
+def unpack_tiles(order, sources, main, first, columns_of):
+    looks = order.shape[0] // LOOK
+    for start in range(0, len(sources), 4):
+        parts = jnp.concatenate([columns_of(source) for source in sources[start : start + 4]], axis=1)
+        value = jnp.dot(order, parts, preferred_element_type=jnp.float32)
+        for one in range(4):
+            for look in range(LOOK):
+                main[first[start + one], look] = value[look * looks : (look + 1) * looks, one * LANES : (one + 1) * LANES]
+
+
+def unpack_rims(by_look, looks, rim, first):
+    share = LANES // SLOTS
+    lane = lax.broadcasted_iota(jnp.int32, (looks, LANES), 1)
+    for at, place in enumerate(first):
+        value = jnp.zeros((looks, LANES), jnp.float32)
+        for look in range(LOOK):
+            target = look * SIDES
+            moved = pltpu.roll(by_look[look * looks : (look + 1) * looks], (target - at * SIDES) % LANES, axis=1)
+            value = jnp.where((lane >= target) & (lane < target + SIDES), moved, value)
+        spread = share
+        while spread < LANES:
+            value = value + pltpu.roll(value, spread, axis=1)
+            spread = 2 * spread
+        rim[place] = value
+
+
+def band_of(shape, from_of, to_of):
+    at = lax.broadcasted_iota(jnp.int32, shape, 0)
+    to = lax.broadcasted_iota(jnp.int32, shape, 1)
+    return (jnp.abs(from_of(at, to) - to_of(at, to)) <= RADIUS).astype(jnp.float32).astype(jnp.bfloat16)
+
+
+def column_bands():
+    share = LANES // SLOTS
+
+    def rim_from(at, to):
+        side = at % share % SIDES
+        return jnp.where(side < RADIUS, side - RADIUS, LANES + side - RADIUS)
+
+    def rim_to(at, to):
+        column = (to - at % LANES // share * share + LANES) % LANES
+        inside = (column < RADIUS) | (column >= LANES - RADIUS)
+        inside = inside & (at % share < LOOK * SIDES)
+        return jnp.where(inside, column, 4 * LANES)
+
+    band = band_of((2 * LANES, LANES), lambda at, to: at % LANES, lambda at, to: to)
+    return band, band_of((2 * LANES, LANES), rim_from, rim_to)
+
+
+def row_sums(look_rows, looks, look_of):
+    group = 2 * SLOTS
+    out_at = lax.broadcasted_iota(jnp.int32, (group * look_rows, group * looks), 0)
+    in_at = lax.broadcasted_iota(jnp.int32, (group * look_rows, group * looks), 1)
+    near = jnp.abs(look_of(in_at % looks) - out_at % look_rows) <= RADIUS
+    near = near & (in_at // looks == out_at // look_rows)
+    return near.astype(jnp.float32).astype(jnp.bfloat16)
+
+
+def mixed(values):
+    lane = lax.broadcasted_iota(jnp.int32, values[0].shape, 1)
+    result = values[-1]
+    for slot in range(SLOTS - 1):
+        result = jnp.where(lane // (LANES // SLOTS) == slot, values[slot], result)
+    return result
+
+
+def power_batches(blocks, epochs, looks, main, rim, looked, rim_looked):
+    total = blocks * epochs
+    group = 2 * SLOTS
+    for block in range(blocks):
+        for piece in range(0, looks, 8):
+            rows_at = slice(piece, piece + 8)
+            for half in range(2):
+                squares = []
+                for slot in range(SLOTS):
+                    channel = half * SLOTS + slot
+                    epoch = block * epochs + channel
+                    value = None
+                    for look in range(LOOK):
+                        real = main[epoch, look, rows_at]
+                        imag = main[total + epoch, look, rows_at]
+                        one = real * real + imag * imag
+                        value = one if value is None else value + one
+                    at = (block * group + channel) * looks + piece
+                    looked[at : at + 8, :] = value
+                    real = rim[epoch, rows_at]
+                    imag = rim[total + epoch, rows_at]
+                    squares.append(real * real + imag * imag)
+                at = (block * 2 + half) * looks + piece
+                rim_looked[at : at + 8, :] = mixed(squares)
+
+
+def pair_batch(batch, epoch, mates, total, looks, main, rim, looked, rim_looked):
+    group = 2 * SLOTS
+    for piece in range(0, looks, 8):
+        rows_at = slice(piece, piece + 8)
+        own_re = [main[epoch, look, rows_at] for look in range(LOOK)]
+        own_im = [main[total + epoch, look, rows_at] for look in range(LOOK)]
+        for slot, mate in enumerate(mates):
+            real = None
+            for look in range(LOOK):
+                mate_re = main[mate, look, rows_at]
+                mate_im = main[total + mate, look, rows_at]
+                one = own_re[look] * mate_re + own_im[look] * mate_im
+                two = own_im[look] * mate_re - own_re[look] * mate_im
+                real = one if real is None else real + one
+                imag = two if look == 0 else imag + two
+            at = pl.multiple_of((batch * group + slot) * looks + piece, 8)
+            looked[pl.ds(at, 8), :] = real
+            at = pl.multiple_of((batch * group + SLOTS + slot) * looks + piece, 8)
+            looked[pl.ds(at, 8), :] = imag
+        rim_re = rim[epoch, rows_at]
+        rim_im = rim[total + epoch, rows_at]
+        mate_re = mixed([rim[mate, rows_at] for mate in mates])
+        mate_im = mixed([rim[total + mate, rows_at] for mate in mates])
+        at = pl.multiple_of(batch * 2 * looks + piece, 8)
+        rim_looked[pl.ds(at, 8), :] = rim_re * mate_re + rim_im * mate_im
+        at = pl.multiple_of((batch * 2 + 1) * looks + piece, 8)
+        rim_looked[pl.ds(at, 8), :] = rim_im * mate_re - rim_re * mate_im
+
+
+def columns_summed(couple, looks, bands, looked, rim_looked, wide):
+    group = 2 * SLOTS
+    f32 = jnp.float32
+    at = pl.ds(pl.multiple_of(couple * (2 * group * looks), 2 * group * looks), 2 * group * looks)
+    halves = jnp.concatenate(split_two(looked[at, :]), axis=1)
+    value = jnp.dot(halves, bands[0], preferred_element_type=f32)
+    at = pl.ds(pl.multiple_of(couple * (4 * looks), 4 * looks), 4 * looks)
+    halves = jnp.concatenate(split_two(rim_looked[at, :]), axis=1)
+    outer = jnp.dot(halves, bands[1], preferred_element_type=f32)
+    lane = lax.broadcasted_iota(jnp.int32, (looks, LANES), 1)
+    outside = (lane < RADIUS) | (lane >= LANES - RADIUS)
+    for channel in range(2 * group):
+        batch, half, slot = channel // group, channel % group // SLOTS, channel % SLOTS
+        row = (batch * 2 + half) * looks
+        part = outer[row : row + looks]
+        if slot > 0:
+            part = pltpu.roll(part, LANES - slot * (LANES // SLOTS), axis=1)
+        row = channel * looks
+        to = pl.ds(pl.multiple_of(couple * (2 * group * looks) + row, 8), looks)
+        wide[to, :] = value[row : row + looks] + jnp.where(outside, part, 0.0)
+
+
+def rows_summed(batch, looks, sum_rows, wide):
+    rows = 2 * SLOTS * looks
+    at = pl.ds(pl.multiple_of(batch * rows, rows), rows)
+    halves = jnp.concatenate(split_two(wide[at, :]), axis=1)
+    value = jnp.dot(sum_rows, halves, preferred_element_type=jnp.float32)
+    return value[:, :LANES] + value[:, LANES:]
+
+
+def clipped(value, last):
+    return jnp.minimum(jnp.maximum(value, 0), last)
+
+
+def inner_kernel(sizes, partner, *refs):
+    tiles, epochs, rows = sizes
+    messages = refs[:tiles]
+    boxed, main, rim, looked, rim_looked, wide = refs[tiles:]
+    total = tiles * epochs
+    look_rows = rows // LOOK
+    order = look_order(rows, lambda at: 1.0)
+    bands = column_bands()
+    sum_rows = row_sums(look_rows, look_rows, lambda look: look)
+    for block, message in enumerate(messages):
+        first = [part * total + block * epochs + epoch for part in range(2) for epoch in range(epochs)]
+        unpack_tiles(order, range(2 * epochs), main, first, lambda at: message[at * rows : (at + 1) * rows, :])
+        by_look = jnp.dot(order, message[2 * epochs * rows :, :], preferred_element_type=jnp.float32)
+        unpack_rims(by_look, look_rows, rim, first)
+    power_batches(tiles, epochs, look_rows, main, rim, looked, rim_looked)
+    last = (tiles + total) // 2 - 1
+
+    @pl.loop(0, last + 2)
+    def _(turn):
+        here = clipped(turn, total // 2 - 1)
+        for one in range(2):
+            epoch = here * 2 + one
+            mates = [partner[epoch * SLOTS + slot] for slot in range(SLOTS)]
+            pair_batch(tiles + epoch, epoch, mates, total, look_rows, main, rim, looked, rim_looked)
+        columns_summed(clipped(turn, last), look_rows, bands, looked, rim_looked, wide)
+        here = clipped(turn - 1, last)
+        for one in range(2):
+            boxed[here * 2 + one] = rows_summed(here * 2 + one, look_rows, sum_rows, wide)
+
+
+def border_kernel(sizes, partner, weight, present, *refs):
+    tiles, epochs, look_rows = sizes
+    top, bottom, inner, factors, pulls, boxed, main, rim, looked, rim_looked, wide = refs
+    total = tiles * epochs
+    looks = 2 * HALO // LOOK
+    halo_looks = HALO // LOOK
+    tile_rows = (2 * epochs + 1) * HALO
+    order = look_order(2 * HALO, lambda at: jnp.where(at < HALO, present[0], present[1]))
+    bands = column_bands()
+    sum_rows = row_sums(look_rows, looks, lambda at: jnp.where(at < halo_looks, at - halo_looks, at - halo_looks + look_rows))
+    for block in range(tiles):
+
+        def border_of(at):
+            here = slice(block * tile_rows + at * HALO, block * tile_rows + (at + 1) * HALO)
+            return jnp.concatenate([top[here, :], bottom[here, :]], axis=0)
+
+        first = [part * total + block * epochs + epoch for part in range(2) for epoch in range(epochs)]
+        unpack_tiles(order, range(2 * epochs), main, first, border_of)
+        by_look = jnp.dot(order, border_of(2 * epochs), preferred_element_type=jnp.float32)
+        unpack_rims(by_look, looks, rim, first)
+    power_batches(tiles, epochs, looks, main, rim, looked, rim_looked)
+    last = (tiles + total) // 2 - 1
+
+    def power_of(epoch):
+        at = pl.ds(pl.multiple_of(epoch % epochs * look_rows, look_rows), look_rows)
+        return boxed[epoch // epochs, at, :]
+
+    @pl.loop(0, last + 3)
+    def _(turn):
+        here = clipped(turn, total // 2 - 1)
+        for one in range(2):
+            epoch = here * 2 + one
+            mates = [partner[epoch * SLOTS + slot] for slot in range(SLOTS)]
+            pair_batch(tiles + epoch, epoch, mates, total, looks, main, rim, looked, rim_looked)
+        columns_summed(clipped(turn, last), looks, bands, looked, rim_looked, wide)
+        here = clipped(turn - 2 - tiles // 2, total // 2 - 1)
+        for one in range(2):
+            epoch = here * 2 + one
+            batch = tiles + epoch
+            own_power = power_of(epoch)
+            for slot in range(SLOTS):
+                pair = epoch * SLOTS + slot
+                inverse = lax.rsqrt(own_power * power_of(partner[pair]) + EPSILON)
+                unit_re = boxed[batch, slot * look_rows : (slot + 1) * look_rows, :] * inverse
+                unit_im = boxed[batch, (SLOTS + slot) * look_rows : (SLOTS + slot + 1) * look_rows, :] * inverse
+                factor = weight[pair] * (unit_re * unit_re + unit_im * unit_im)
+                factors[pair] = factor
+                pulls[pair] = factor * unit_im
+        here = clipped(turn - 1, last)
+        for one in range(2):
+            batch = here * 2 + one
+            boxed[batch] = inner[batch] + rows_summed(batch, looks, sum_rows, wide)
+
+
+def gradient_kernel(sizes, partner, *refs):
+    tiles, epochs = sizes
+    fields = refs[:tiles]
+    factors, pulls, gradient, sums, est, old = refs[tiles:]
+    look_rows = est.shape[1]
+    total = tiles * epochs
+    f32 = jnp.float32
+    for block in range(tiles):
+
+        @pl.loop(0, epochs, unroll=4)
+        def _(epoch):
+            here = pl.ds(pl.multiple_of(epoch * look_rows, look_rows), look_rows)
+            est[block * epochs + epoch] = fields[block][0, here, :].astype(f32) + fields[block][1, here, :].astype(f32)
+            old[block * epochs + epoch] = fields[block][2, here, :].astype(f32)
+            gradient[block * epochs + epoch] = jnp.zeros((look_rows, LANES), f32)
+
+    @pl.loop(0, total, unroll=2)
+    def _(epoch):
+        own_est = est[epoch]
+        own = jnp.zeros((look_rows, LANES), f32)
+        mates = [partner[epoch * SLOTS + slot] for slot in range(SLOTS)]
+        values = []
+        for slot, mate in enumerate(mates):
+            pair = epoch * SLOTS + slot
+            weighted = pulls[pair] - factors[pair] * (own_est - est[mate])
+            own = own + weighted
+            values.append(weighted)
+        for mate, weighted in zip(mates, values):
+            gradient[mate] = gradient[mate] - weighted
+        gradient[epoch] = gradient[epoch] + own
+
+    def totals(epoch, carry):
+        norm, crossed, grad_term, mixed_term, old_term = carry
+        own_grad = gradient[epoch]
+        own_old = old[epoch]
+        norm = norm + own_grad * own_grad
+        crossed = crossed + own_grad * own_old
+        for slot in range(SLOTS):
+            mate = partner[epoch * SLOTS + slot]
+            factor = factors[epoch * SLOTS + slot]
+            grad_spread = own_grad - gradient[mate]
+            old_spread = own_old - old[mate]
+            pulled = factor * grad_spread
+            grad_term = grad_term + pulled * grad_spread
+            mixed_term = mixed_term + pulled * old_spread
+            old_term = old_term + factor * old_spread * old_spread
+        return norm, crossed, grad_term, mixed_term, old_term
+
+    zero = jnp.zeros((look_rows, LANES), f32)
+    results = lax.fori_loop(0, total, totals, (zero,) * 5, unroll=2)
+    sums[...] = jnp.zeros(sums.shape, f32)
+    for at, value in enumerate(results):
+        sums[at : at + 1, :] = jnp.sum(value, axis=0, keepdims=True)
+
+
+def return_kernel(tiles, gradient, *refs):
+    pieces = refs[-tiles:]
+    shared = refs[:-tiles]
+    total = shared[0][...]
+    for other in shared[1:]:
+        total = total + other[...]
+    epochs = gradient.shape[0] // len(pieces)
+    look_rows = gradient.shape[1]
+    for number, piece in enumerate(pieces):
+        for epoch in range(epochs):
+            piece[epoch * look_rows : (epoch + 1) * look_rows, :] = gradient[number * epochs + epoch]
+        piece[epochs * look_rows :, :] = total
+
+
+def update_kernel(cell_count, me, prev_mean, estimate, direction, *refs):
+    new_estimate, new_direction = refs[-2:]
+    pieces = refs[:-2]
+    tiles = len(pieces)
+    epochs = estimate.shape[0]
+    look_rows = estimate.shape[1]
+    total = pieces[0][epochs * look_rows :, :]
+    for piece in pieces[1:]:
+        total = total + piece[epochs * look_rows :, :]
+    total = jnp.sum(total, axis=1, keepdims=True)
+    grad_norm, crossed, grad_term, mixed, old_term = (total[at : at + 1, :] for at in range(5))
+    momentum = grad_norm / cell_count / prev_mean[0]
+    curvature = grad_term + 2.0 * momentum * mixed + momentum * momentum * old_term
+    step = (grad_norm + momentum * crossed) / curvature
+    momentum = jnp.broadcast_to(momentum, (look_rows, LANES))
+    step = jnp.broadcast_to(step, (look_rows, LANES))
+    for shift, piece in enumerate(pieces):
+        tile = lax.rem(me[0] - shift + tiles, tiles)
+        columns = pl.ds(pl.multiple_of(tile * LANES, LANES), LANES)
+        for epoch in range(epochs):
+            gradient = piece[epoch * look_rows : (epoch + 1) * look_rows, :]
+            moved = gradient + momentum * direction[epoch, :, columns]
+            new_direction[epoch, :, columns] = moved
+            new_estimate[epoch, :, columns] = estimate[epoch, :, columns] + step * moved
+
+
+def swapped(up, down, axis):
+    size = lax.axis_size(axis)
+    if size == 1:
+        return jnp.zeros_like(up), jnp.zeros_like(down)
+    if size == 2:
+        first = lax.axis_index(axis) == 0
+        got = lax.ppermute(jnp.where(first, up, down), axis, [(0, 1), (1, 0)])
+        return got, got
+    forward = [(i, i + 1) for i in range(size - 1)]
+    backward = [(target, source) for source, target in forward]
+    return lax.ppermute(up, axis, forward), lax.ppermute(down, axis, backward)
+
+
+def to_ahead(x, axis, by):
+    size = lax.axis_size(axis)
+    return lax.ppermute(x, axis, [(i, (i + by) % size) for i in range(size)])
+
+
+def transposed_plan(slc, offsets, weights, estimate, direction, prev_mean):
+    f32 = jnp.float32
+    bf16 = jnp.bfloat16
+    tiles = lax.axis_size("epoch")
+    me = lax.axis_index("epoch")
+    epochs, rows, columns = slc.shape[1:]
+    look_rows = rows // LOOK
+    total = tiles * epochs
+    tile_rows = 2 * epochs * rows
+    params_of = pltpu.CompilerParams(vmem_limit_bytes=VMEM_BYTES)
+
+    def fetched(messages, shift):
+        return to_ahead(messages[tiles - shift], "epoch", tiles - shift)
+
+    sub = lax.axis_index("sub")
+    outer_tile = (2, epochs, rows, LANES)
+    edge = pl.pallas_call(
+        edge_kernel,
+        out_shape=jax.ShapeDtypeStruct((rows, LANES), bf16),
+        grid=(1,),
+        in_specs=[
+            pl.BlockSpec(outer_tile, lambda _: (0, 0, 0, 0)),
+            pl.BlockSpec(outer_tile, lambda _: (0, 0, 0, tiles - 1)),
+        ],
+        out_specs=pl.BlockSpec((rows, LANES), lambda _: (0, 0)),
+        compiler_params=params_of,
+        cost_estimate=pl.CostEstimate(flops=1_000_000, bytes_accessed=1_000_000, transcendentals=0),
+    )(slc, slc)
+    before, after = swapped(edge, edge, "sub")
+    params = jnp.zeros((rows, LANES), f32)
+    listed = jnp.concatenate([offsets.astype(f32), weights, weights, weights], axis=1)
+    params = lax.dynamic_update_slice(params, listed, (0, PARAM_LANE))
+    sub_present = jnp.stack([sub > 0, sub < lax.axis_size("sub") - 1]).astype(f32)
+    messages = pl.pallas_call(
+        pack_kernel,
+        out_shape=(jax.ShapeDtypeStruct((tile_rows + rows, LANES), bf16),) * tiles,
+        in_specs=[SMEM] * 2 + [VMEM] * 4,
+        out_specs=(VMEM,) * tiles,
+        scratch_shapes=[pltpu.VMEM((tiles, rows, LANES), bf16)],
+        compiler_params=params_of,
+        cost_estimate=pl.CostEstimate(flops=3_000_000, bytes_accessed=4_000_000, transcendentals=0),
+    )(me.reshape(1), sub_present, slc, params, before, after)
+    block = [messages[0]] + [fetched(messages, shift) for shift in range(1, tiles)]
+
+    estimate, direction, _ = lax.optimization_barrier((estimate, direction, messages))
+    fields = pl.pallas_call(
+        fields_kernel,
+        out_shape=(jax.ShapeDtypeStruct((3, epochs * look_rows, LANES), bf16),) * tiles,
+        in_specs=[SMEM] + [VMEM] * 2,
+        out_specs=(VMEM,) * tiles,
+        compiler_params=params_of,
+        cost_estimate=pl.CostEstimate(flops=1_000_000, bytes_accessed=2_000_000, transcendentals=0),
+    )(me.reshape(1), estimate, direction)
+    late = lax.optimization_barrier((fields, block))[0]
+    field = [fields[0]] + [fetched(late, shift) for shift in range(1, tiles)]
+
+    space = lax.axis_index("space")
+    spaces = lax.axis_size("space")
+    present = jnp.stack([space > 0, space < spaces - 1]).astype(f32)
+
+    def halo(pieces):
+        def border(from_row):
+            cuts = [lax.dynamic_slice_in_dim(piece, from_row, HALO, axis=1).reshape(-1, LANES) for piece in pieces]
+            return jnp.concatenate(cuts, axis=0)
+
+        if spaces == 2:
+            got = lax.ppermute(border(jnp.where(space == 0, rows - HALO, 0)), "space", [(0, 1), (1, 0)])
+            return got, got
+        return swapped(border(rows - HALO), border(0), "space")
+
+    def by_rows(shift):
+        return block[shift].reshape(-1, rows, LANES)
+
+    def params_in(shift):
+        return block[shift][tile_rows : tile_rows + epochs, PARAM_LANE : PARAM_LANE + 4 * SLOTS].astype(f32)
+
+    def pairs_of(blocks, loaded):
+        listed = jnp.concatenate([params_in(block) for block in blocks], axis=0)
+        mate = jnp.arange(len(blocks) * epochs, dtype=jnp.int32)[:, None] + listed[:, :SLOTS].astype(jnp.int32)
+        weight = listed[:, SLOTS : 2 * SLOTS] + listed[:, 2 * SLOTS : 3 * SLOTS] + listed[:, 3 * SLOTS :]
+        return mate.reshape(-1), weight.reshape(-1)
+
+    top, bottom = halo([by_rows(shift) for shift in range(tiles)])
+    listed = jnp.concatenate([params_in(shift) for shift in range(tiles)], axis=0)
+    partner = jnp.arange(total, dtype=jnp.int32)[:, None] + listed[:, :SLOTS].astype(jnp.int32)
+    partner = lax.rem(partner, total).reshape(-1)
+    weight = listed[:, SLOTS : 2 * SLOTS] + listed[:, 2 * SLOTS : 3 * SLOTS] + listed[:, 3 * SLOTS :]
+    weight = weight.reshape(-1)
+
+    group = 2 * SLOTS
+    batches = tiles + total
+
+    def scratch(looks):
+        return [
+            pltpu.VMEM((2 * total, LOOK, looks, LANES), f32),
+            pltpu.VMEM((2 * total, looks, LANES), f32),
+            pltpu.VMEM((batches * group * looks, LANES), f32),
+            pltpu.VMEM((batches * 2 * looks, LANES), f32),
+            pltpu.VMEM((batches * group * looks, LANES), f32),
+        ]
+
+    boxed_shape = (batches, group * look_rows, LANES)
+    inner = pl.pallas_call(
+        functools.partial(inner_kernel, (tiles, epochs, rows)),
+        out_shape=jax.ShapeDtypeStruct(boxed_shape, f32),
+        in_specs=[SMEM] + [VMEM] * tiles,
+        out_specs=VMEM,
+        scratch_shapes=scratch(look_rows),
+        compiler_params=params_of,
+        cost_estimate=pl.CostEstimate(flops=20_000_000, bytes_accessed=20_000_000, transcendentals=0),
+    )(partner, *block)
+    pair_shape = jax.ShapeDtypeStruct((total * SLOTS, look_rows, LANES), f32)
+    factors, pulls = pl.pallas_call(
+        functools.partial(border_kernel, (tiles, epochs, look_rows)),
+        out_shape=(pair_shape, pair_shape),
+        in_specs=[SMEM] * 3 + [VMEM] * 3,
+        out_specs=(VMEM, VMEM),
+        scratch_shapes=[pltpu.VMEM(boxed_shape, f32)] + scratch(2 * HALO // LOOK),
+        compiler_params=params_of,
+        cost_estimate=pl.CostEstimate(flops=20_000_000, bytes_accessed=15_000_000, transcendentals=0),
+    )(partner, weight, present, top, bottom, inner)
+    gradient, sums = pl.pallas_call(
+        functools.partial(gradient_kernel, (tiles, epochs)),
+        out_shape=(
+            jax.ShapeDtypeStruct((total, look_rows, LANES), f32),
+            jax.ShapeDtypeStruct((8, LANES), f32),
+        ),
+        in_specs=[SMEM] + [VMEM] * (tiles + 2),
+        out_specs=(VMEM, VMEM),
+        scratch_shapes=[pltpu.VMEM((total, look_rows, LANES), f32)] * 2,
+        compiler_params=params_of,
+        cost_estimate=pl.CostEstimate(flops=10_000_000, bytes_accessed=8_000_000, transcendentals=0),
+    )(partner, *field, factors, pulls)
+
+    place = ("space", "sub")
+    count = spaces * lax.axis_size("sub")
+    shared = [sums] + [lax.ppermute(sums, place, [(i, (i + by) % count) for i in range(count)]) for by in range(1, count)]
+    pieces = pl.pallas_call(
+        functools.partial(return_kernel, tiles),
+        out_shape=(jax.ShapeDtypeStruct((epochs * look_rows + 8, LANES), f32),) * tiles,
+        in_specs=[VMEM] * (1 + count),
+        out_specs=(VMEM,) * tiles,
+        compiler_params=params_of,
+        cost_estimate=pl.CostEstimate(flops=10_000, bytes_accessed=1_000_000, transcendentals=0),
+    )(gradient, *shared)
+    returned = [pieces[0]] + [to_ahead(pieces[by], "epoch", by) for by in range(1, tiles)]
+    cell_count = float(total * look_rows * spaces * columns * lax.axis_size("sub"))
+    return pl.pallas_call(
+        functools.partial(update_kernel, cell_count),
+        out_shape=(jax.ShapeDtypeStruct(estimate.shape, f32),) * 2,
+        in_specs=[SMEM] * 2 + [VMEM] * (2 + tiles),
+        out_specs=(VMEM, VMEM),
+        compiler_params=params_of,
+        cost_estimate=pl.CostEstimate(flops=1_000_000, bytes_accessed=2_000_000, transcendentals=0),
+    )(me.reshape(1), prev_mean, estimate, direction, *returned)
+
+
+def on_device(slc, offsets, weights, estimate, direction, prev_mean):
+    epochs, rows, columns = slc.shape[1:]
+    fits = columns == LANES * lax.axis_size("epoch") and lax.axis_size("epoch") % 2 == 0
+    fits = fits and 2 * epochs * SIDES <= PARAM_LANE and rows % HALO == 0 and epochs == 2 * SLOTS
+    plan = transposed_plan if fits else ring_plan
+    return plan(slc, offsets, weights, estimate, direction, prev_mean)
+
+
 def solution(mesh):
     return jax.shard_map(
         on_device,

time: 225 us -> 80.1 us (0.36)
  other arithmetic: 60.6 us -> 0.35 us
  local copies, waits for them, and re-layouts: 63.5 us -> 3.29 us
  blocking collectives: 31.9 us -> 0 us
  Pallas kernels: 0 us -> 28.3 us
  waiting for transfers between devices: 36.6 us -> 23.4 us
  between operations: 5.64 us -> 1.43 us
    psum x1 -> x0, blocking collectives: 31.9 us -> none  [on_device(): lax.psum((local_norm, local_crossed, jnp.sum(factor * grad_spread * grad_...]
    pallas_call x0 -> x8, Pallas kernels: none -> 28.3 us  [the longest x1 14.1 us: transposed_plan(): pl.pallas_call(functools.partial(inner_kernel, (tiles, epochs, rows)), ou...]
    reduce_sum x12 -> x0, other arithmetic: 27.4 us -> none  [the longest x9 21.5 us: looked_sum(): jnp.sum(field.reshape(shape[:-2] + (shape[-2] // LOOK, LOOK, shape[-1])),...]
    gather x12 -> x0, local copies, waits for them, and re-layouts: 25.7 us -> none  [the longest x4 12.8 us: on_device(): mate_imag = jnp.take(ext_imag, partner[:, slot_index], axis=0)]
    reshape x8 -> x2, local copies, waits for them, and re-layouts: 16.5 us -> 0.21 us  [the longest x1 0.1 us: transposed_plan(): partner = lax.rem(partner, total).reshape(-1)]
    ppermute x8 -> x14, waiting for transfers between devices: 36.6 us -> 23.4 us  [the longest x9 20.5 us: to_ahead(): return lax.ppermute(x, axis, [(i, (i + by) % size) for i in range(size)])]
    sub x2 -> x0, other arithmetic: 9.68 us -> none  [on_device(): pieces.append(looked_sum(own_imag * mate_real - own_real * mate_imag))]
    concatenate x4 -> x3, other arithmetic: 9.61 us -> 0.11 us  [the longest x1 0.08 us: transposed_plan(): jnp.concatenate([offsets.astype(f32), weights, weights, weights], axis=1)]
  transfers between devices with their start and end apart: 8 -> 14, of which waited for: 5 -> 6; matrix products, arithmetic and copies ran while one was open for 8% -> 3% of each run, Pallas kernels for 0% -> 30%
where the time goes in v8:
time: 80.1 us; the launch traced here: 79.9 us
  Pallas kernels  28.3 us (35%)
  waiting for transfers between devices  23.4 us (29%)
  starting transfers between devices  23.1 us (29%)
  local copies, waits for them, and re-layouts  3.29 us (4%)
  between operations  1.43 us (2%)
    ppermute x9, waiting for transfers between devices, to_ahead(): return lax.ppermute(x, axis, [(i, (i + by) % size) for i in range(size)])  20.5 us
    ppermute x9, starting transfers between devices, to_ahead(): return lax.ppermute(x, axis, [(i, (i + by) % size) for i in range(size)])  20.2 us
    pallas_call x1, Pallas kernels, transposed_plan(): pl.pallas_call(functools.partial(inner_kernel, (tiles, epochs, rows)), ou...  14.1 us
    pallas_call x1, Pallas kernels, transposed_plan(): pl.pallas_call(functools.partial(border_kernel, (tiles, epochs, look_rows...  10.1 us
    ppermute x3, waiting for transfers between devices, transposed_plan(): lax.ppermute(sums, place, [(i, (i + by) % count) for i in range(count)])  2.91 us
    unnamed x10, local copies, waits for them, and re-layouts  2.74 us
    pallas_call x1, Pallas kernels, transposed_plan(): pl.pallas_call(functools.partial(gradient_kernel, (tiles, epochs)), out_s...  1.67 us
  transfers between devices with their start and end apart: 14, of which 6 were waited for; matrix products, arithmetic and copies ran while one was open for 3% of the time, Pallas kernels for 30%

profile of v8, /device:TPU:0, one launch (start us, length us, event | category | flops | bytes accessed | tf_op | source)
XLA Modules:
  0.0 79.9 jit_solution(5493677798554637861)
XLA Ops:
  0.6 1.2 %copy-done = bf16[2,8,64,512]{3,2,1,0:T(8,128)(2,1)S(1)} copy-done((bf16[2,8,64,512]{3,2,1,0:T(8,128)(2,1)S(1)}, bf16[2,8,64,512]{3,2,1,0:T(8,128)(2,1)}, u32[]{:S(2)}) %copy-start) | copy-done | bytes 1048600
  1.9 0.2 shard_map.77
  2.1 0.5 collective-permute-start
  2.6 0.8 copy.12
  3.4 0.8 copy.13
  4.1 0.1 select_maximum_fusion.params
  4.2 0.1 add_convert_fusion.present
  4.3 0.0 collective-permute-done.before.after
  4.3 1.3 %shard_map.78 = (bf16[1088,128]{1,0:T(8,128)(2,1)S(1)}, bf16[1088,128]{1,0:T(8,128)(2,1)S(1)}, bf16[1088,128]{1,0:T(8,128)(2,1)S(1)}, bf16[1088,128]{1,0:T(8,128)(2,1)S(1)}) custom-call(s32[1]{0:T(128)} %bitcast.me, f32[2]{0:T(128)S(1)} %add_convert_fusion.present, bf16[2,8,64,512]{3,2,1,0:T(8,128)(2,1)S(1)} %copy-done.1, ...), custom_call_target="tpu_custom_call" | custom-call | flops 3000000 | bytes 4000000 | tf_op jit(solution)/shard_map/pallas_call | solution.py:620
  5.6 2.8 %collective-permute-start.3 = (bf16[1088,128]{1,0:T(8,128)(2,1)S(1)}, bf16[1088,128]{1,0:T(8,128)(2,1)S(1)}, u32[]{:S(2)}, u32[]{:S(2)}) collective-permute-start(bf16[1088,128]{1,0:T(8,128)(2,1)S(1)} %get-tuple-element.24), channel_id=1, source_target_pairs={{0,4},{4,8},{8,12},{12,0},{1,5},{5,9},{9,13},{13,1},{2,6},{6,10},{... | collective-permute-start | bytes 835592 | tf_op jit(solution)/shard_map/ppermute | solution.py:584
  8.4 2.6 %collective-permute-start.2 = (bf16[1088,128]{1,0:T(8,128)(2,1)S(1)}, bf16[1088,128]{1,0:T(8,128)(2,1)S(1)}, u32[]{:S(2)}, u32[]{:S(2)}) collective-permute-start(bf16[1088,128]{1,0:T(8,128)(2,1)S(1)} %get-tuple-element.25), channel_id=1, source_target_pairs={{0,8},{4,12},{8,0},{12,4},{1,9},{5,13},{9,1},{13,5},{2,10},{6,14},... | collective-permute-start | bytes 835592 | tf_op jit(solution)/shard_map/ppermute | solution.py:584
  11.0 0.1 add_convert_fusion.1.present
  11.0 1.3 %collective-permute-start.1 = (bf16[1088,128]{1,0:T(8,128)(2,1)S(1)}, bf16[1088,128]{1,0:T(8,128)(2,1)S(1)}, u32[]{:S(2)}, u32[]{:S(2)}) collective-permute-start(bf16[1088,128]{1,0:T(8,128)(2,1)S(1)} %get-tuple-element.26), channel_id=1, source_target_pairs={{0,12},{4,0},{8,4},{12,8},{1,13},{5,1},{9,5},{13,9},{2,14},{6,2},{... | collective-permute-start | bytes 835592 | tf_op jit(solution)/shard_map/ppermute | solution.py:584
  12.4 0.1 slice.24
  12.5 0.1 shard_map.79
  12.6 5.5 %collective-permute-done.3.refs_3_ = bf16[1088,128]{1,0:T(8,128)(2,1)S(1)} collective-permute-done((bf16[1088,128]{1,0:T(8,128)(2,1)S(1)}, bf16[1088,128]{1,0:T(8,128)(2,1)S(1)}, u32[]{:S(2)}, u32[]{:S(2)}) %collective-permute-start.3) | collective-permute-done | bytes 278560 | tf_op jit(solution)/shard_map/ppermute | solution.py:584
  18.1 11.6 %collective-permute-done.2.refs_2_ = bf16[1088,128]{1,0:T(8,128)(2,1)S(1)} collective-permute-done((bf16[1088,128]{1,0:T(8,128)(2,1)S(1)}, bf16[1088,128]{1,0:T(8,128)(2,1)S(1)}, u32[]{:S(2)}, u32[]{:S(2)}) %collective-permute-start.2) | collective-permute-done | bytes 278560 | tf_op jit(solution)/shard_map/ppermute | solution.py:584
  29.6 0.0 collective-permute-done.1.refs_1_
  29.7 1.6 %collective-permute-start.7 = (bf16[1088,128]{1,0:T(8,128)(2,1)S(1)}, bf16[1088,128]{1,0:T(8,128)(2,1)S(1)}, u32[]{:S(2)}, u32[]{:S(2)}) collective-permute-start(bf16[1088,128]{1,0:T(8,128)(2,1)S(1)} %pad_maximum_fusion), channel_id=1, source_target_pairs={{0,2},{2,0},{1,3},{3,1},{4,6},{6,4},{5,7},{7,5},{8,10},{10,8},{9,1... | collective-permute-start | bytes 835592 | tf_op jit(solution)/shard_map/ppermute | solution.py:653
  31.3 0.1 slice.34
  31.3 0.1 slice.33
  31.4 0.1 slice.32
  31.5 0.1 slice_add_fusion
  31.6 7.5 %collective-permute-start.4 = (bf16[3,128,128]{2,1,0:T(8,128)(2,1)S(1)}, bf16[3,128,128]{2,1,0:T(8,128)(2,1)S(1)}, u32[]{:S(2)}, u32[]{:S(2)}) collective-permute-start(bf16[3,128,128]{2,1,0:T(8,128)(2,1)S(1)} %get-tuple-element.33), channel_id=1, source_target_pairs={{0,12},{4,0},{8,4},{12,8},{1,13},{5,1},{9,5},{13,9},{2,14},{6,2},{... | collective-permute-start | bytes 294920 | tf_op jit(solution)/shard_map/ppermute | solution.py:584
  39.0 0.4 collective-permute-start.5
  39.5 0.2 collective-permute-start.6
  39.7 0.1 reshape.41.weight
  39.8 0.1 reshape.40.partner
  39.9 14.1 %shard_map.80.refs_2_ = f32[36,128,128]{2,1,0:T(8,128)S(1)} custom-call(s32[128]{0:T(128)S(1)} %reshape.40.partner, bf16[1088,128]{1,0:T(8,128)(2,1)S(1)} %get-tuple-element.23.refs_0_, bf16[1088,128]{1,0:T(8,128)(2,1)S(1)} %collective-permute-done.1.refs_1_, bf16[1088,128]{1,0:T(8,128)(2,1)S(1)} %collective-permute-done.2.refs_2_, ...), custom_call_target="tpu_custom_call" | custom-call | flops 20000000 | bytes 20000000 | tf_op jit(solution)/shard_map/pallas_call | solution.py:689
  54.0 0.0 collective-permute-done.7.refs_0_.refs_1_
  54.0 10.1 %shard_map.81 = (f32[128,16,128]{2,1,0:T(8,128)S(1)}, f32[128,16,128]{2,1,0:T(8,128)S(1)}) custom-call(s32[128]{0:T(128)S(1)} %reshape.40.partner, f32[128]{0:T(128)S(1)} %reshape.41.weight, f32[2]{0:T(128)S(1)} %add_convert_fusion.1.present, bf16[1088,128]{1,0:T(8,128)(2,1)S(1)} %collective-permute-done.7.refs_0_.refs_1_, ...), custom_call_target="tpu_custom_call" | custom-call | flops 20000000 | bytes 15000000 | tf_op jit(solution)/shard_map/pallas_call | solution.py:699
  64.1 0.0 collective-permute-done.4.refs_1_
  64.1 0.0 collective-permute-done.5.refs_2_
  64.1 0.0 collective-permute-done.6.refs_3_
  64.1 1.7 %shard_map.82 = (f32[32,16,128]{2,1,0:T(8,128)S(1)}, f32[8,128]{1,0:T(8,128)S(1)}) custom-call(s32[128]{0:T(128)S(1)} %reshape.40.partner, bf16[3,128,128]{2,1,0:T(8,128)(2,1)S(1)} %get-tuple-element.29.refs_0_, bf16[3,128,128]{2,1,0:T(8,128)(2,1)S(1)} %collective-permute-done.4.refs_1_, bf16[3,128,128]{2,1,0:T(8,128)(2,1)S(1)} %collective-permute-done.5.refs_2_, ...), custom_call_target="tpu_custom_call" | custom-call | flops 10000000 | bytes 8000000 | tf_op jit(solution)/shard_map/pallas_call | solution.py:708
  65.8 0.1 collective-permute-start.10
  65.9 0.6 collective-permute-start.9
  66.5 0.2 collective-permute-start.8
  66.6 0.6 collective-permute-done.10.refs_3_
  67.2 2.4 %collective-permute-done.9.refs_2_ = f32[8,128]{1,0:T(8,128)S(1)} collective-permute-done((f32[8,128]{1,0:T(8,128)S(1)}, f32[8,128]{1,0:T(8,128)S(1)}, u32[]{:S(2)}, u32[]{:S(2)}) %collective-permute-start.9) | collective-permute-done | bytes 4128 | tf_op jit(solution)/shard_map/ppermute | solution.py:723
  69.5 0.0 collective-permute-done.8.refs_1_
  69.6 2.9 %collective-permute-start.11 = (f32[136,128]{1,0:T(8,128)S(1)}, f32[136,128]{1,0:T(8,128)S(1)}, u32[]{:S(2)}, u32[]{:S(2)}) collective-permute-start(f32[136,128]{1,0:T(8,128)S(1)} %get-tuple-element.41), channel_id=1, source_target_pairs={{0,4},{4,8},{8,12},{12,0},{1,5},{5,9},{9,13},{13,1},{2,6},{6,10},{... | collective-permute-start | bytes 208904 | tf_op jit(solution)/shard_map/ppermute | solution.py:584
  72.5 1.3 %collective-permute-start.12 = (f32[136,128]{1,0:T(8,128)S(1)}, f32[136,128]{1,0:T(8,128)S(1)}, u32[]{:S(2)}, u32[]{:S(2)}) collective-permute-start(f32[136,128]{1,0:T(8,128)S(1)} %get-tuple-element.42), channel_id=1, source_target_pairs={{0,8},{4,12},{8,0},{12,4},{1,9},{5,13},{9,1},{13,5},{2,10},{6,14},... | collective-permute-start | bytes 208904 | tf_op jit(solution)/shard_map/ppermute | solution.py:584
  73.8 1.1 %collective-permute-start.13 = (f32[136,128]{1,0:T(8,128)S(1)}, f32[136,128]{1,0:T(8,128)S(1)}, u32[]{:S(2)}, u32[]{:S(2)}) collective-permute-start(f32[136,128]{1,0:T(8,128)S(1)} %get-tuple-element.43), channel_id=1, source_target_pairs={{0,12},{4,0},{8,4},{12,8},{1,13},{5,1},{9,5},{13,9},{2,14},{6,2},{... | collective-permute-start | bytes 208904 | tf_op jit(solution)/shard_map/ppermute | solution.py:584
  75.6 0.8 %collective-permute-done.11.refs_1_ = f32[136,128]{1,0:T(8,128)S(1)} collective-permute-done((f32[136,128]{1,0:T(8,128)S(1)}, f32[136,128]{1,0:T(8,128)S(1)}, u32[]{:S(2)}, u32[]{:S(2)}) %collective-permute-start.11) | collective-permute-done | bytes 69664 | tf_op jit(solution)/shard_map/ppermute | solution.py:584
  76.4 2.6 %collective-permute-done.12.refs_2_ = f32[136,128]{1,0:T(8,128)S(1)} collective-permute-done((f32[136,128]{1,0:T(8,128)S(1)}, f32[136,128]{1,0:T(8,128)S(1)}, u32[]{:S(2)}, u32[]{:S(2)}) %collective-permute-start.12) | collective-permute-done | bytes 69664 | tf_op jit(solution)/shard_map/ppermute | solution.py:584
  79.0 0.0 collective-permute-done.13.refs_3_
  79.0 0.9 %shard_map.84 = (f32[8,16,512]{2,1,0:T(8,128)}, f32[8,16,512]{2,1,0:T(8,128)}) custom-call(s32[1]{0:T(128)} %bitcast.me, f32[1]{0:T(128)S(6)} %copy.16.prev_mean, f32[8,16,512]{2,1,0:T(8,128)S(1)} %copy-done.2, f32[8,16,512]{2,1,0:T(8,128)S(1)} %copy-done.3, f32[136,128]{1,0:T(8,128)S(1)} %get-tuple-element.40.refs_0_, ...), custom_call_target="tpu_custom_call" | custom-call | flops 1000000 | bytes 2000000 | tf_op jit(solution)/shard_map/pallas_call | solution.py:734
  (16 shorter events, 0.1 us)
Async XLA Ops:
  0.6 1.2 %copy-start = (bf16[2,8,64,512]{3,2,1,0:T(8,128)(2,1)S(1)}, bf16[2,8,64,512]{3,2,1,0:T(8,128)(2,1)}, u32[]{:S(2)}) copy-start(bf16[2,8,64,512]{3,2,1,0:T(8,128)(2,1)} %slc.1) | copy-start | bytes 3145732
  1.9 2.4 %copy-start.1 = (bf16[2,8,64,512]{3,2,1,0:T(8,128)(2,1)S(1)}, bf16[2,8,64,512]{3,2,1,0:T(8,128)(2,1)}, u32[]{:S(2)}) copy-start(bf16[2,8,64,512]{3,2,1,0:T(8,128)(2,1)} %slc.1) | copy-start | bytes 3145732
  1.9 10.6 %copy-start.2 = (f32[8,16,512]{2,1,0:T(8,128)S(1)}, f32[8,16,512]{2,1,0:T(8,128)}, u32[]{:S(2)}) copy-start(f32[8,16,512]{2,1,0:T(8,128)} %estimate.1) | copy-start | bytes 786436
  1.9 10.6 %copy-start.3 = (f32[8,16,512]{2,1,0:T(8,128)S(1)}, f32[8,16,512]{2,1,0:T(8,128)}, u32[]{:S(2)}) copy-start(f32[8,16,512]{2,1,0:T(8,128)} %direction.1) | copy-start | bytes 786436
  2.1 2.2 %collective-permute-start = (bf16[64,128]{1,0:T(8,128)(2,1)S(1)}, bf16[64,128]{1,0:T(8,128)(2,1)S(1)}, u32[]{:S(2)}, u32[]{:S(2)}) collective-permute-start(bf16[64,128]{1,0:T(8,128)(2,1)S(1)} %shard_map.77), channel_id=1, source_target_pairs={{0,1},{1,0},{2,3},{3,2},{4,5},{5,4},{6,7},{7,6},{8,9},{9,8},{10,11... | collective-permute-start | bytes 49160 | tf_op jit(solution)/shard_map/ppermute | solution.py:575
  5.6 12.5 %collective-permute-start.3 = (bf16[1088,128]{1,0:T(8,128)(2,1)S(1)}, bf16[1088,128]{1,0:T(8,128)(2,1)S(1)}, u32[]{:S(2)}, u32[]{:S(2)}) collective-permute-start(bf16[1088,128]{1,0:T(8,128)(2,1)S(1)} %get-tuple-element.24), channel_id=1, source_target_pairs={{0,4},{4,8},{8,12},{12,0},{1,5},{5,9},{9,13},{13,1},{2,6},{6,10},{... | collective-permute-start | bytes 835592 | tf_op jit(solution)/shard_map/ppermute | solution.py:584
  8.4 21.3 %collective-permute-start.2 = (bf16[1088,128]{1,0:T(8,128)(2,1)S(1)}, bf16[1088,128]{1,0:T(8,128)(2,1)S(1)}, u32[]{:S(2)}, u32[]{:S(2)}) collective-permute-start(bf16[1088,128]{1,0:T(8,128)(2,1)S(1)} %get-tuple-element.25), channel_id=1, source_target_pairs={{0,8},{4,12},{8,0},{12,4},{1,9},{5,13},{9,1},{13,5},{2,10},{6,14},... | collective-permute-start | bytes 835592 | tf_op jit(solution)/shard_map/ppermute | solution.py:584
  11.0 18.6 %collective-permute-start.1 = (bf16[1088,128]{1,0:T(8,128)(2,1)S(1)}, bf16[1088,128]{1,0:T(8,128)(2,1)S(1)}, u32[]{:S(2)}, u32[]{:S(2)}) collective-permute-start(bf16[1088,128]{1,0:T(8,128)(2,1)S(1)} %get-tuple-element.26), channel_id=1, source_target_pairs={{0,12},{4,0},{8,4},{12,8},{1,13},{5,1},{9,5},{13,9},{2,14},{6,2},{... | collective-permute-start | bytes 835592 | tf_op jit(solution)/shard_map/ppermute | solution.py:584
  29.7 24.3 %collective-permute-start.7 = (bf16[1088,128]{1,0:T(8,128)(2,1)S(1)}, bf16[1088,128]{1,0:T(8,128)(2,1)S(1)}, u32[]{:S(2)}, u32[]{:S(2)}) collective-permute-start(bf16[1088,128]{1,0:T(8,128)(2,1)S(1)} %pad_maximum_fusion), channel_id=1, source_target_pairs={{0,2},{2,0},{1,3},{3,1},{4,6},{6,4},{5,7},{7,5},{8,10},{10,8},{9,1... | collective-permute-start | bytes 835592 | tf_op jit(solution)/shard_map/ppermute | solution.py:653
  31.6 32.5 %collective-permute-start.4 = (bf16[3,128,128]{2,1,0:T(8,128)(2,1)S(1)}, bf16[3,128,128]{2,1,0:T(8,128)(2,1)S(1)}, u32[]{:S(2)}, u32[]{:S(2)}) collective-permute-start(bf16[3,128,128]{2,1,0:T(8,128)(2,1)S(1)} %get-tuple-element.33), channel_id=1, source_target_pairs={{0,12},{4,0},{8,4},{12,8},{1,13},{5,1},{9,5},{13,9},{2,14},{6,2},{... | collective-permute-start | bytes 294920 | tf_op jit(solution)/shard_map/ppermute | solution.py:584
  39.0 25.1 %collective-permute-start.5 = (bf16[3,128,128]{2,1,0:T(8,128)(2,1)S(1)}, bf16[3,128,128]{2,1,0:T(8,128)(2,1)S(1)}, u32[]{:S(2)}, u32[]{:S(2)}) collective-permute-start(bf16[3,128,128]{2,1,0:T(8,128)(2,1)S(1)} %get-tuple-element.34), channel_id=1, source_target_pairs={{0,8},{4,12},{8,0},{12,4},{1,9},{5,13},{9,1},{13,5},{2,10},{6,14},... | collective-permute-start | bytes 294920 | tf_op jit(solution)/shard_map/ppermute | solution.py:584
  39.5 24.7 %collective-permute-start.6 = (bf16[3,128,128]{2,1,0:T(8,128)(2,1)S(1)}, bf16[3,128,128]{2,1,0:T(8,128)(2,1)S(1)}, u32[]{:S(2)}, u32[]{:S(2)}) collective-permute-start(bf16[3,128,128]{2,1,0:T(8,128)(2,1)S(1)} %get-tuple-element.35), channel_id=1, source_target_pairs={{0,4},{4,8},{8,12},{12,0},{1,5},{5,9},{9,13},{13,1},{2,6},{6,10},{... | collective-permute-start | bytes 294920 | tf_op jit(solution)/shard_map/ppermute | solution.py:584
  65.8 1.4 %collective-permute-start.10 = (f32[8,128]{1,0:T(8,128)S(1)}, f32[8,128]{1,0:T(8,128)S(1)}, u32[]{:S(2)}, u32[]{:S(2)}) collective-permute-start(f32[8,128]{1,0:T(8,128)S(1)} %get-tuple-element.39.refs_0_), channel_id=1, source_target_pairs={{0,3},{1,0},{2,1},{3,2},{4,7},{5,4},{6,5},{7,6},{8,11},{9,8},{10,9... | collective-permute-start | bytes 12296 | tf_op jit(solution)/shard_map/ppermute | solution.py:723
  65.9 3.7 %collective-permute-start.9 = (f32[8,128]{1,0:T(8,128)S(1)}, f32[8,128]{1,0:T(8,128)S(1)}, u32[]{:S(2)}, u32[]{:S(2)}) collective-permute-start(f32[8,128]{1,0:T(8,128)S(1)} %get-tuple-element.39.refs_0_), channel_id=1, source_target_pairs={{0,2},{1,3},{2,0},{3,1},{4,6},{5,7},{6,4},{7,5},{8,10},{9,11},{10,... | collective-permute-start | bytes 12296 | tf_op jit(solution)/shard_map/ppermute | solution.py:723
  66.5 3.1 %collective-permute-start.8 = (f32[8,128]{1,0:T(8,128)S(1)}, f32[8,128]{1,0:T(8,128)S(1)}, u32[]{:S(2)}, u32[]{:S(2)}) collective-permute-start(f32[8,128]{1,0:T(8,128)S(1)} %get-tuple-element.39.refs_0_), channel_id=1, source_target_pairs={{0,1},{1,2},{2,3},{3,0},{4,5},{5,6},{6,7},{7,4},{8,9},{9,10},{10,1... | collective-permute-start | bytes 12296 | tf_op jit(solution)/shard_map/ppermute | solution.py:723
  69.6 6.8 %collective-permute-start.11 = (f32[136,128]{1,0:T(8,128)S(1)}, f32[136,128]{1,0:T(8,128)S(1)}, u32[]{:S(2)}, u32[]{:S(2)}) collective-permute-start(f32[136,128]{1,0:T(8,128)S(1)} %get-tuple-element.41), channel_id=1, source_target_pairs={{0,4},{4,8},{8,12},{12,0},{1,5},{5,9},{9,13},{13,1},{2,6},{6,10},{... | collective-permute-start | bytes 208904 | tf_op jit(solution)/shard_map/ppermute | solution.py:584
  72.5 6.5 %collective-permute-start.12 = (f32[136,128]{1,0:T(8,128)S(1)}, f32[136,128]{1,0:T(8,128)S(1)}, u32[]{:S(2)}, u32[]{:S(2)}) collective-permute-start(f32[136,128]{1,0:T(8,128)S(1)} %get-tuple-element.42), channel_id=1, source_target_pairs={{0,8},{4,12},{8,0},{12,4},{1,9},{5,13},{9,1},{13,5},{2,10},{6,14},... | collective-permute-start | bytes 208904 | tf_op jit(solution)/shard_map/ppermute | solution.py:584
  73.8 5.2 %collective-permute-start.13 = (f32[136,128]{1,0:T(8,128)S(1)}, f32[136,128]{1,0:T(8,128)S(1)}, u32[]{:S(2)}, u32[]{:S(2)}) collective-permute-start(f32[136,128]{1,0:T(8,128)S(1)} %get-tuple-element.43), channel_id=1, source_target_pairs={{0,12},{4,0},{8,4},{12,8},{1,13},{5,1},{9,5},{13,9},{2,14},{6,2},{... | collective-permute-start | bytes 208904 | tf_op jit(solution)/shard_map/ppermute | solution.py:584

commit v9 on v8

--- a/solution.py
+++ b/solution.py
@@ -406,15 +406,15 @@
 
     @pl.loop(0, last + 2)
     def _(turn):
+        here = clipped(turn - 1, last)
+        for one in range(2):
+            boxed[here * 2 + one] = rows_summed(here * 2 + one, look_rows, sum_rows, wide)
+        columns_summed(clipped(turn, last), look_rows, bands, looked, rim_looked, wide)
         here = clipped(turn, total // 2 - 1)
         for one in range(2):
             epoch = here * 2 + one
             mates = [partner[epoch * SLOTS + slot] for slot in range(SLOTS)]
             pair_batch(tiles + epoch, epoch, mates, total, look_rows, main, rim, looked, rim_looked)
-        columns_summed(clipped(turn, last), look_rows, bands, looked, rim_looked, wide)
-        here = clipped(turn - 1, last)
-        for one in range(2):
-            boxed[here * 2 + one] = rows_summed(here * 2 + one, look_rows, sum_rows, wide)
 
 
 def border_kernel(sizes, partner, weight, present, *refs):
@@ -446,12 +446,6 @@
 
     @pl.loop(0, last + 3)
     def _(turn):
-        here = clipped(turn, total // 2 - 1)
-        for one in range(2):
-            epoch = here * 2 + one
-            mates = [partner[epoch * SLOTS + slot] for slot in range(SLOTS)]
-            pair_batch(tiles + epoch, epoch, mates, total, looks, main, rim, looked, rim_looked)
-        columns_summed(clipped(turn, last), looks, bands, looked, rim_looked, wide)
         here = clipped(turn - 2 - tiles // 2, total // 2 - 1)
         for one in range(2):
             epoch = here * 2 + one
@@ -466,9 +460,15 @@
                 factors[pair] = factor
                 pulls[pair] = factor * unit_im
         here = clipped(turn - 1, last)
+        values = [inner[here * 2 + one] + rows_summed(here * 2 + one, looks, sum_rows, wide) for one in range(2)]
         for one in range(2):
-            batch = here * 2 + one
-            boxed[batch] = inner[batch] + rows_summed(batch, looks, sum_rows, wide)
+            boxed[here * 2 + one] = values[one]
+        columns_summed(clipped(turn, last), looks, bands, looked, rim_looked, wide)
+        here = clipped(turn, total // 2 - 1)
+        for one in range(2):
+            epoch = here * 2 + one
+            mates = [partner[epoch * SLOTS + slot] for slot in range(SLOTS)]
+            pair_batch(tiles + epoch, epoch, mates, total, looks, main, rim, looked, rim_looked)
 
 
 def gradient_kernel(sizes, partner, *refs):

time: 80.1 us -> 74.8 us (0.934)
  Pallas kernels: 28.3 us -> 23 us
    pallas_call x1, Pallas kernels: 14.1 us -> 10.7 us  [transposed_plan(): pl.pallas_call(functools.partial(inner_kernel, (tiles, epochs, rows)), ou...]
    pallas_call x1, Pallas kernels: 10.1 us -> 8.16 us  [transposed_plan(): pl.pallas_call(functools.partial(border_kernel, (tiles, epochs, look_rows...]
  transfers between devices with their start and end apart: 14 -> 14, of which waited for: 6 -> 6; matrix products, arithmetic and copies ran while one was open for 3% -> 3% of each run, Pallas kernels for 30% -> 25%
where the time goes in v9:
time: 74.8 us; the launch traced here: 74.6 us
  waiting for transfers between devices  23.4 us (31%)
  starting transfers between devices  23.1 us (31%)
  Pallas kernels  23 us (31%)
  local copies, waits for them, and re-layouts  3.29 us (4%)
  between operations  1.43 us (2%)
    ppermute x9, waiting for transfers between devices, to_ahead(): return lax.ppermute(x, axis, [(i, (i + by) % size) for i in range(size)])  20.5 us
    ppermute x9, starting transfers between devices, to_ahead(): return lax.ppermute(x, axis, [(i, (i + by) % size) for i in range(size)])  20.2 us
    pallas_call x1, Pallas kernels, transposed_plan(): pl.pallas_call(functools.partial(inner_kernel, (tiles, epochs, rows)), ou...  10.7 us
    pallas_call x1, Pallas kernels, transposed_plan(): pl.pallas_call(functools.partial(border_kernel, (tiles, epochs, look_rows...  8.16 us
    ppermute x3, waiting for transfers between devices, transposed_plan(): lax.ppermute(sums, place, [(i, (i + by) % count) for i in range(count)])  2.91 us
    unnamed x10, local copies, waits for them, and re-layouts  2.74 us
    pallas_call x1, Pallas kernels, transposed_plan(): pl.pallas_call(functools.partial(gradient_kernel, (tiles, epochs)), out_s...  1.67 us
    ppermute x1, starting transfers between devices, halo(): lax.ppermute(border(jnp.where(space == 0, rows - HALO, 0)), 'space', [(0,...  1.56 us
  transfers between devices with their start and end apart: 14, of which 6 were waited for; matrix products, arithmetic and copies ran while one was open for 3% of the time, Pallas kernels for 25%

profile of v9, /device:TPU:0, one launch (start us, length us, event | category | flops | bytes accessed | tf_op | source)
XLA Modules:
  0.0 74.6 jit_solution(9082071612844075947)
XLA Ops:
  0.6 1.2 %copy-done = bf16[2,8,64,512]{3,2,1,0:T(8,128)(2,1)S(1)} copy-done((bf16[2,8,64,512]{3,2,1,0:T(8,128)(2,1)S(1)}, bf16[2,8,64,512]{3,2,1,0:T(8,128)(2,1)}, u32[]{:S(2)}) %copy-start) | copy-done | bytes 1048600
  1.9 0.2 shard_map.77
  2.1 0.5 collective-permute-start
  2.6 0.8 %copy.12 = s32[8,4]{1,0:T(8,128)S(1)} copy(s32[8,4]{0,1:T(4,128)} %param.7) | data formatting | bytes 256 | tf_op args[1]
  3.4 0.8 %copy.13 = f32[8,4]{1,0:T(8,128)S(1)} copy(f32[8,4]{0,1:T(4,128)} %param.8) | data formatting | bytes 256 | tf_op args[2]
  4.1 0.1 select_maximum_fusion.params
  4.2 0.1 add_convert_fusion.present
  4.3 0.0 collective-permute-done.before.after
  4.3 1.3 %shard_map.78 = (bf16[1088,128]{1,0:T(8,128)(2,1)S(1)}, bf16[1088,128]{1,0:T(8,128)(2,1)S(1)}, bf16[1088,128]{1,0:T(8,128)(2,1)S(1)}, bf16[1088,128]{1,0:T(8,128)(2,1)S(1)}) custom-call(s32[1]{0:T(128)} %bitcast.me, f32[2]{0:T(128)S(1)} %add_convert_fusion.present, bf16[2,8,64,512]{3,2,1,0:T(8,128)(2,1)S(1)} %copy-done.1, ...), custom_call_target="tpu_custom_call" | custom-call | flops 3000000 | bytes 4000000 | tf_op jit(solution)/shard_map/pallas_call | solution.py:620
  5.6 2.8 %collective-permute-start.3 = (bf16[1088,128]{1,0:T(8,128)(2,1)S(1)}, bf16[1088,128]{1,0:T(8,128)(2,1)S(1)}, u32[]{:S(2)}, u32[]{:S(2)}) collective-permute-start(bf16[1088,128]{1,0:T(8,128)(2,1)S(1)} %get-tuple-element.24), channel_id=1, source_target_pairs={{0,4},{4,8},{8,12},{12,0},{1,5},{5,9},{9,13},{13,1},{2,6},{6,10},{... | collective-permute-start | bytes 835592 | tf_op jit(solution)/shard_map/ppermute | solution.py:584
  8.4 2.6 %collective-permute-start.2 = (bf16[1088,128]{1,0:T(8,128)(2,1)S(1)}, bf16[1088,128]{1,0:T(8,128)(2,1)S(1)}, u32[]{:S(2)}, u32[]{:S(2)}) collective-permute-start(bf16[1088,128]{1,0:T(8,128)(2,1)S(1)} %get-tuple-element.25), channel_id=1, source_target_pairs={{0,8},{4,12},{8,0},{12,4},{1,9},{5,13},{9,1},{13,5},{2,10},{6,14},... | collective-permute-start | bytes 835592 | tf_op jit(solution)/shard_map/ppermute | solution.py:584
  11.0 0.1 add_convert_fusion.1.present
  11.0 1.3 %collective-permute-start.1 = (bf16[1088,128]{1,0:T(8,128)(2,1)S(1)}, bf16[1088,128]{1,0:T(8,128)(2,1)S(1)}, u32[]{:S(2)}, u32[]{:S(2)}) collective-permute-start(bf16[1088,128]{1,0:T(8,128)(2,1)S(1)} %get-tuple-element.26), channel_id=1, source_target_pairs={{0,12},{4,0},{8,4},{12,8},{1,13},{5,1},{9,5},{13,9},{2,14},{6,2},{... | collective-permute-start | bytes 835592 | tf_op jit(solution)/shard_map/ppermute | solution.py:584
  12.4 0.1 slice.24
  12.5 0.1 shard_map.79
  12.6 5.5 %collective-permute-done.3.refs_3_ = bf16[1088,128]{1,0:T(8,128)(2,1)S(1)} collective-permute-done((bf16[1088,128]{1,0:T(8,128)(2,1)S(1)}, bf16[1088,128]{1,0:T(8,128)(2,1)S(1)}, u32[]{:S(2)}, u32[]{:S(2)}) %collective-permute-start.3) | collective-permute-done | bytes 278560 | tf_op jit(solution)/shard_map/ppermute | solution.py:584
  18.1 11.6 %collective-permute-done.2.refs_2_ = bf16[1088,128]{1,0:T(8,128)(2,1)S(1)} collective-permute-done((bf16[1088,128]{1,0:T(8,128)(2,1)S(1)}, bf16[1088,128]{1,0:T(8,128)(2,1)S(1)}, u32[]{:S(2)}, u32[]{:S(2)}) %collective-permute-start.2) | collective-permute-done | bytes 278560 | tf_op jit(solution)/shard_map/ppermute | solution.py:584
  29.6 0.0 collective-permute-done.1.refs_1_
  29.7 1.6 %collective-permute-start.7 = (bf16[1088,128]{1,0:T(8,128)(2,1)S(1)}, bf16[1088,128]{1,0:T(8,128)(2,1)S(1)}, u32[]{:S(2)}, u32[]{:S(2)}) collective-permute-start(bf16[1088,128]{1,0:T(8,128)(2,1)S(1)} %pad_maximum_fusion), channel_id=1, source_target_pairs={{0,2},{2,0},{1,3},{3,1},{4,6},{6,4},{5,7},{7,5},{8,10},{10,8},{9,1... | collective-permute-start | bytes 835592 | tf_op jit(solution)/shard_map/ppermute | solution.py:653
  31.3 0.1 slice.34
  31.3 0.1 slice.33
  31.4 0.1 slice.32
  31.5 0.1 slice_add_fusion
  31.6 7.5 %collective-permute-start.4 = (bf16[3,128,128]{2,1,0:T(8,128)(2,1)S(1)}, bf16[3,128,128]{2,1,0:T(8,128)(2,1)S(1)}, u32[]{:S(2)}, u32[]{:S(2)}) collective-permute-start(bf16[3,128,128]{2,1,0:T(8,128)(2,1)S(1)} %get-tuple-element.33), channel_id=1, source_target_pairs={{0,12},{4,0},{8,4},{12,8},{1,13},{5,1},{9,5},{13,9},{2,14},{6,2},{... | collective-permute-start | bytes 294920 | tf_op jit(solution)/shard_map/ppermute | solution.py:584
  39.0 0.4 collective-permute-start.5
  39.5 0.2 collective-permute-start.6
  39.7 0.1 reshape.41.weight
  39.8 0.1 reshape.40.partner
  39.9 10.7 %shard_map.80.refs_2_ = f32[36,128,128]{2,1,0:T(8,128)S(1)} custom-call(s32[128]{0:T(128)S(1)} %reshape.40.partner, bf16[1088,128]{1,0:T(8,128)(2,1)S(1)} %get-tuple-element.23.refs_0_, bf16[1088,128]{1,0:T(8,128)(2,1)S(1)} %collective-permute-done.1.refs_1_, bf16[1088,128]{1,0:T(8,128)(2,1)S(1)} %collective-permute-done.2.refs_2_, ...), custom_call_target="tpu_custom_call" | custom-call | flops 20000000 | bytes 20000000 | tf_op jit(solution)/shard_map/pallas_call | solution.py:689
  50.6 0.0 collective-permute-done.7.refs_0_.refs_1_
  50.6 8.2 %shard_map.81 = (f32[128,16,128]{2,1,0:T(8,128)S(1)}, f32[128,16,128]{2,1,0:T(8,128)S(1)}) custom-call(s32[128]{0:T(128)S(1)} %reshape.40.partner, f32[128]{0:T(128)S(1)} %reshape.41.weight, f32[2]{0:T(128)S(1)} %add_convert_fusion.1.present, bf16[1088,128]{1,0:T(8,128)(2,1)S(1)} %collective-permute-done.7.refs_0_.refs_1_, ...), custom_call_target="tpu_custom_call" | custom-call | flops 20000000 | bytes 15000000 | tf_op jit(solution)/shard_map/pallas_call | solution.py:699
  58.8 0.0 collective-permute-done.4.refs_1_
  58.8 0.0 collective-permute-done.5.refs_2_
  58.8 0.0 collective-permute-done.6.refs_3_
  58.8 1.7 %shard_map.82 = (f32[32,16,128]{2,1,0:T(8,128)S(1)}, f32[8,128]{1,0:T(8,128)S(1)}) custom-call(s32[128]{0:T(128)S(1)} %reshape.40.partner, bf16[3,128,128]{2,1,0:T(8,128)(2,1)S(1)} %get-tuple-element.29.refs_0_, bf16[3,128,128]{2,1,0:T(8,128)(2,1)S(1)} %collective-permute-done.4.refs_1_, bf16[3,128,128]{2,1,0:T(8,128)(2,1)S(1)} %collective-permute-done.5.refs_2_, ...), custom_call_target="tpu_custom_call" | custom-call | flops 10000000 | bytes 8000000 | tf_op jit(solution)/shard_map/pallas_call | solution.py:708
  60.5 0.1 collective-permute-start.10
  60.5 0.6 collective-permute-start.9
  61.1 0.2 collective-permute-start.8
  61.3 0.6 collective-permute-done.10.refs_3_
  61.9 2.4 %collective-permute-done.9.refs_2_ = f32[8,128]{1,0:T(8,128)S(1)} collective-permute-done((f32[8,128]{1,0:T(8,128)S(1)}, f32[8,128]{1,0:T(8,128)S(1)}, u32[]{:S(2)}, u32[]{:S(2)}) %collective-permute-start.9) | collective-permute-done | bytes 4128 | tf_op jit(solution)/shard_map/ppermute | solution.py:723
  64.2 0.0 collective-permute-done.8.refs_1_
  64.2 2.9 %collective-permute-start.11 = (f32[136,128]{1,0:T(8,128)S(1)}, f32[136,128]{1,0:T(8,128)S(1)}, u32[]{:S(2)}, u32[]{:S(2)}) collective-permute-start(f32[136,128]{1,0:T(8,128)S(1)} %get-tuple-element.41), channel_id=1, source_target_pairs={{0,4},{4,8},{8,12},{12,0},{1,5},{5,9},{9,13},{13,1},{2,6},{6,10},{... | collective-permute-start | bytes 208904 | tf_op jit(solution)/shard_map/ppermute | solution.py:584
  67.2 1.3 %collective-permute-start.12 = (f32[136,128]{1,0:T(8,128)S(1)}, f32[136,128]{1,0:T(8,128)S(1)}, u32[]{:S(2)}, u32[]{:S(2)}) collective-permute-start(f32[136,128]{1,0:T(8,128)S(1)} %get-tuple-element.42), channel_id=1, source_target_pairs={{0,8},{4,12},{8,0},{12,4},{1,9},{5,13},{9,1},{13,5},{2,10},{6,14},... | collective-permute-start | bytes 208904 | tf_op jit(solution)/shard_map/ppermute | solution.py:584
  68.5 1.1 %collective-permute-start.13 = (f32[136,128]{1,0:T(8,128)S(1)}, f32[136,128]{1,0:T(8,128)S(1)}, u32[]{:S(2)}, u32[]{:S(2)}) collective-permute-start(f32[136,128]{1,0:T(8,128)S(1)} %get-tuple-element.43), channel_id=1, source_target_pairs={{0,12},{4,0},{8,4},{12,8},{1,13},{5,1},{9,5},{13,9},{2,14},{6,2},{... | collective-permute-start | bytes 208904 | tf_op jit(solution)/shard_map/ppermute | solution.py:584
  70.2 0.8 %collective-permute-done.11.refs_1_ = f32[136,128]{1,0:T(8,128)S(1)} collective-permute-done((f32[136,128]{1,0:T(8,128)S(1)}, f32[136,128]{1,0:T(8,128)S(1)}, u32[]{:S(2)}, u32[]{:S(2)}) %collective-permute-start.11) | collective-permute-done | bytes 69664 | tf_op jit(solution)/shard_map/ppermute | solution.py:584
  71.1 2.6 %collective-permute-done.12.refs_2_ = f32[136,128]{1,0:T(8,128)S(1)} collective-permute-done((f32[136,128]{1,0:T(8,128)S(1)}, f32[136,128]{1,0:T(8,128)S(1)}, u32[]{:S(2)}, u32[]{:S(2)}) %collective-permute-start.12) | collective-permute-done | bytes 69664 | tf_op jit(solution)/shard_map/ppermute | solution.py:584
  73.7 0.0 collective-permute-done.13.refs_3_
  73.7 0.9 %shard_map.84 = (f32[8,16,512]{2,1,0:T(8,128)}, f32[8,16,512]{2,1,0:T(8,128)}) custom-call(s32[1]{0:T(128)} %bitcast.me, f32[1]{0:T(128)S(6)} %copy.16.prev_mean, f32[8,16,512]{2,1,0:T(8,128)S(1)} %copy-done.2, f32[8,16,512]{2,1,0:T(8,128)S(1)} %copy-done.3, f32[136,128]{1,0:T(8,128)S(1)} %get-tuple-element.40.refs_0_, ...), custom_call_target="tpu_custom_call" | custom-call | flops 1000000 | bytes 2000000 | tf_op jit(solution)/shard_map/pallas_call | solution.py:734
  (16 shorter events, 0.1 us)
Async XLA Ops:
  0.6 1.2 %copy-start = (bf16[2,8,64,512]{3,2,1,0:T(8,128)(2,1)S(1)}, bf16[2,8,64,512]{3,2,1,0:T(8,128)(2,1)}, u32[]{:S(2)}) copy-start(bf16[2,8,64,512]{3,2,1,0:T(8,128)(2,1)} %slc.1) | copy-start | bytes 3145732
  1.9 2.4 %copy-start.1 = (bf16[2,8,64,512]{3,2,1,0:T(8,128)(2,1)S(1)}, bf16[2,8,64,512]{3,2,1,0:T(8,128)(2,1)}, u32[]{:S(2)}) copy-start(bf16[2,8,64,512]{3,2,1,0:T(8,128)(2,1)} %slc.1) | copy-start | bytes 3145732
  1.9 10.6 %copy-start.2 = (f32[8,16,512]{2,1,0:T(8,128)S(1)}, f32[8,16,512]{2,1,0:T(8,128)}, u32[]{:S(2)}) copy-start(f32[8,16,512]{2,1,0:T(8,128)} %estimate.1) | copy-start | bytes 786436
  1.9 10.6 %copy-start.3 = (f32[8,16,512]{2,1,0:T(8,128)S(1)}, f32[8,16,512]{2,1,0:T(8,128)}, u32[]{:S(2)}) copy-start(f32[8,16,512]{2,1,0:T(8,128)} %direction.1) | copy-start | bytes 786436
  2.1 2.2 %collective-permute-start = (bf16[64,128]{1,0:T(8,128)(2,1)S(1)}, bf16[64,128]{1,0:T(8,128)(2,1)S(1)}, u32[]{:S(2)}, u32[]{:S(2)}) collective-permute-start(bf16[64,128]{1,0:T(8,128)(2,1)S(1)} %shard_map.77), channel_id=1, source_target_pairs={{0,1},{1,0},{2,3},{3,2},{4,5},{5,4},{6,7},{7,6},{8,9},{9,8},{10,11... | collective-permute-start | bytes 49160 | tf_op jit(solution)/shard_map/ppermute | solution.py:575
  5.6 12.5 %collective-permute-start.3 = (bf16[1088,128]{1,0:T(8,128)(2,1)S(1)}, bf16[1088,128]{1,0:T(8,128)(2,1)S(1)}, u32[]{:S(2)}, u32[]{:S(2)}) collective-permute-start(bf16[1088,128]{1,0:T(8,128)(2,1)S(1)} %get-tuple-element.24), channel_id=1, source_target_pairs={{0,4},{4,8},{8,12},{12,0},{1,5},{5,9},{9,13},{13,1},{2,6},{6,10},{... | collective-permute-start | bytes 835592 | tf_op jit(solution)/shard_map/ppermute | solution.py:584
  8.4 21.3 %collective-permute-start.2 = (bf16[1088,128]{1,0:T(8,128)(2,1)S(1)}, bf16[1088,128]{1,0:T(8,128)(2,1)S(1)}, u32[]{:S(2)}, u32[]{:S(2)}) collective-permute-start(bf16[1088,128]{1,0:T(8,128)(2,1)S(1)} %get-tuple-element.25), channel_id=1, source_target_pairs={{0,8},{4,12},{8,0},{12,4},{1,9},{5,13},{9,1},{13,5},{2,10},{6,14},... | collective-permute-start | bytes 835592 | tf_op jit(solution)/shard_map/ppermute | solution.py:584
  11.0 18.6 %collective-permute-start.1 = (bf16[1088,128]{1,0:T(8,128)(2,1)S(1)}, bf16[1088,128]{1,0:T(8,128)(2,1)S(1)}, u32[]{:S(2)}, u32[]{:S(2)}) collective-permute-start(bf16[1088,128]{1,0:T(8,128)(2,1)S(1)} %get-tuple-element.26), channel_id=1, source_target_pairs={{0,12},{4,0},{8,4},{12,8},{1,13},{5,1},{9,5},{13,9},{2,14},{6,2},{... | collective-permute-start | bytes 835592 | tf_op jit(solution)/shard_map/ppermute | solution.py:584
  29.7 20.9 %collective-permute-start.7 = (bf16[1088,128]{1,0:T(8,128)(2,1)S(1)}, bf16[1088,128]{1,0:T(8,128)(2,1)S(1)}, u32[]{:S(2)}, u32[]{:S(2)}) collective-permute-start(bf16[1088,128]{1,0:T(8,128)(2,1)S(1)} %pad_maximum_fusion), channel_id=1, source_target_pairs={{0,2},{2,0},{1,3},{3,1},{4,6},{6,4},{5,7},{7,5},{8,10},{10,8},{9,1... | collective-permute-start | bytes 835592 | tf_op jit(solution)/shard_map/ppermute | solution.py:653
  31.6 27.2 %collective-permute-start.4 = (bf16[3,128,128]{2,1,0:T(8,128)(2,1)S(1)}, bf16[3,128,128]{2,1,0:T(8,128)(2,1)S(1)}, u32[]{:S(2)}, u32[]{:S(2)}) collective-permute-start(bf16[3,128,128]{2,1,0:T(8,128)(2,1)S(1)} %get-tuple-element.33), channel_id=1, source_target_pairs={{0,12},{4,0},{8,4},{12,8},{1,13},{5,1},{9,5},{13,9},{2,14},{6,2},{... | collective-permute-start | bytes 294920 | tf_op jit(solution)/shard_map/ppermute | solution.py:584
  39.0 19.7 %collective-permute-start.5 = (bf16[3,128,128]{2,1,0:T(8,128)(2,1)S(1)}, bf16[3,128,128]{2,1,0:T(8,128)(2,1)S(1)}, u32[]{:S(2)}, u32[]{:S(2)}) collective-permute-start(bf16[3,128,128]{2,1,0:T(8,128)(2,1)S(1)} %get-tuple-element.34), channel_id=1, source_target_pairs={{0,8},{4,12},{8,0},{12,4},{1,9},{5,13},{9,1},{13,5},{2,10},{6,14},... | collective-permute-start | bytes 294920 | tf_op jit(solution)/shard_map/ppermute | solution.py:584
  39.5 19.3 %collective-permute-start.6 = (bf16[3,128,128]{2,1,0:T(8,128)(2,1)S(1)}, bf16[3,128,128]{2,1,0:T(8,128)(2,1)S(1)}, u32[]{:S(2)}, u32[]{:S(2)}) collective-permute-start(bf16[3,128,128]{2,1,0:T(8,128)(2,1)S(1)} %get-tuple-element.35), channel_id=1, source_target_pairs={{0,4},{4,8},{8,12},{12,0},{1,5},{5,9},{9,13},{13,1},{2,6},{6,10},{... | collective-permute-start | bytes 294920 | tf_op jit(solution)/shard_map/ppermute | solution.py:584
  60.5 1.4 %collective-permute-start.10 = (f32[8,128]{1,0:T(8,128)S(1)}, f32[8,128]{1,0:T(8,128)S(1)}, u32[]{:S(2)}, u32[]{:S(2)}) collective-permute-start(f32[8,128]{1,0:T(8,128)S(1)} %get-tuple-element.39.refs_0_), channel_id=1, source_target_pairs={{0,3},{1,0},{2,1},{3,2},{4,7},{5,4},{6,5},{7,6},{8,11},{9,8},{10,9... | collective-permute-start | bytes 12296 | tf_op jit(solution)/shard_map/ppermute | solution.py:723
  60.5 3.7 %collective-permute-start.9 = (f32[8,128]{1,0:T(8,128)S(1)}, f32[8,128]{1,0:T(8,128)S(1)}, u32[]{:S(2)}, u32[]{:S(2)}) collective-permute-start(f32[8,128]{1,0:T(8,128)S(1)} %get-tuple-element.39.refs_0_), channel_id=1, source_target_pairs={{0,2},{1,3},{2,0},{3,1},{4,6},{5,7},{6,4},{7,5},{8,10},{9,11},{10,... | collective-permute-start | bytes 12296 | tf_op jit(solution)/shard_map/ppermute | solution.py:723
  61.1 3.1 %collective-permute-start.8 = (f32[8,128]{1,0:T(8,128)S(1)}, f32[8,128]{1,0:T(8,128)S(1)}, u32[]{:S(2)}, u32[]{:S(2)}) collective-permute-start(f32[8,128]{1,0:T(8,128)S(1)} %get-tuple-element.39.refs_0_), channel_id=1, source_target_pairs={{0,1},{1,2},{2,3},{3,0},{4,5},{5,6},{6,7},{7,4},{8,9},{9,10},{10,1... | collective-permute-start | bytes 12296 | tf_op jit(solution)/shard_map/ppermute | solution.py:723
  64.2 6.8 %collective-permute-start.11 = (f32[136,128]{1,0:T(8,128)S(1)}, f32[136,128]{1,0:T(8,128)S(1)}, u32[]{:S(2)}, u32[]{:S(2)}) collective-permute-start(f32[136,128]{1,0:T(8,128)S(1)} %get-tuple-element.41), channel_id=1, source_target_pairs={{0,4},{4,8},{8,12},{12,0},{1,5},{5,9},{9,13},{13,1},{2,6},{6,10},{... | collective-permute-start | bytes 208904 | tf_op jit(solution)/shard_map/ppermute | solution.py:584
  67.2 6.5 %collective-permute-start.12 = (f32[136,128]{1,0:T(8,128)S(1)}, f32[136,128]{1,0:T(8,128)S(1)}, u32[]{:S(2)}, u32[]{:S(2)}) collective-permute-start(f32[136,128]{1,0:T(8,128)S(1)} %get-tuple-element.42), channel_id=1, source_target_pairs={{0,8},{4,12},{8,0},{12,4},{1,9},{5,13},{9,1},{13,5},{2,10},{6,14},... | collective-permute-start | bytes 208904 | tf_op jit(solution)/shard_map/ppermute | solution.py:584
  68.5 5.2 %collective-permute-start.13 = (f32[136,128]{1,0:T(8,128)S(1)}, f32[136,128]{1,0:T(8,128)S(1)}, u32[]{:S(2)}, u32[]{:S(2)}) collective-permute-start(f32[136,128]{1,0:T(8,128)S(1)} %get-tuple-element.43), channel_id=1, source_target_pairs={{0,12},{4,0},{8,4},{12,8},{1,13},{5,1},{9,5},{13,9},{2,14},{6,2},{... | collective-permute-start | bytes 208904 | tf_op jit(solution)/shard_map/ppermute | solution.py:584

commit v10 on v9

--- a/solution.py
+++ b/solution.py
@@ -324,8 +324,9 @@
                 rim_looked[at : at + 8, :] = mixed(squares)
 
 
-def pair_batch(batch, epoch, mates, total, looks, main, rim, looked, rim_looked):
+def pair_batch(batch, epoch, mates, total, looks, main, rim):
     group = 2 * SLOTS
+    products, rims = [], []
     for piece in range(0, looks, 8):
         rows_at = slice(piece, piece + 8)
         own_re = [main[epoch, look, rows_at] for look in range(LOOK)]
@@ -339,21 +340,23 @@
                 two = own_im[look] * mate_re - own_re[look] * mate_im
                 real = one if real is None else real + one
                 imag = two if look == 0 else imag + two
-            at = pl.multiple_of((batch * group + slot) * looks + piece, 8)
-            looked[pl.ds(at, 8), :] = real
-            at = pl.multiple_of((batch * group + SLOTS + slot) * looks + piece, 8)
-            looked[pl.ds(at, 8), :] = imag
+            products.append(((batch * group + slot) * looks + piece, real))
+            products.append(((batch * group + SLOTS + slot) * looks + piece, imag))
         rim_re = rim[epoch, rows_at]
         rim_im = rim[total + epoch, rows_at]
         mate_re = mixed([rim[mate, rows_at] for mate in mates])
         mate_im = mixed([rim[total + mate, rows_at] for mate in mates])
-        at = pl.multiple_of(batch * 2 * looks + piece, 8)
-        rim_looked[pl.ds(at, 8), :] = rim_re * mate_re + rim_im * mate_im
-        at = pl.multiple_of((batch * 2 + 1) * looks + piece, 8)
-        rim_looked[pl.ds(at, 8), :] = rim_im * mate_re - rim_re * mate_im
-
-
-def columns_summed(couple, looks, bands, looked, rim_looked, wide):
+        rims.append((batch * 2 * looks + piece, rim_re * mate_re + rim_im * mate_im))
+        rims.append(((batch * 2 + 1) * looks + piece, rim_im * mate_re - rim_re * mate_im))
+    return products, rims
+
+
+def put(ref, parts):
+    for at, value in parts:
+        ref[pl.ds(pl.multiple_of(at, 8), value.shape[0]), :] = value
+
+
+def columns_summed(couple, looks, bands, looked, rim_looked):
     group = 2 * SLOTS
     f32 = jnp.float32
     at = pl.ds(pl.multiple_of(couple * (2 * group * looks), 2 * group * looks), 2 * group * looks)
@@ -364,6 +367,7 @@
     outer = jnp.dot(halves, bands[1], preferred_element_type=f32)
     lane = lax.broadcasted_iota(jnp.int32, (looks, LANES), 1)
     outside = (lane < RADIUS) | (lane >= LANES - RADIUS)
+    results = []
     for channel in range(2 * group):
         batch, half, slot = channel // group, channel % group // SLOTS, channel % SLOTS
         row = (batch * 2 + half) * looks
@@ -371,8 +375,8 @@
         if slot > 0:
             part = pltpu.roll(part, LANES - slot * (LANES // SLOTS), axis=1)
         row = channel * looks
-        to = pl.ds(pl.multiple_of(couple * (2 * group * looks) + row, 8), looks)
-        wide[to, :] = value[row : row + looks] + jnp.where(outside, part, 0.0)
+        results.append((couple * (2 * group * looks) + row, value[row : row + looks] + jnp.where(outside, part, 0.0)))
+    return results
 
 
 def rows_summed(batch, looks, sum_rows, wide):
@@ -381,6 +385,18 @@
     halves = jnp.concatenate(split_two(wide[at, :]), axis=1)
     value = jnp.dot(sum_rows, halves, preferred_element_type=jnp.float32)
     return value[:, :LANES] + value[:, LANES:]
+
+
+def pair_couple(turn, tiles, total, partner, looks, main, rim):
+    here = clipped(turn, total // 2 - 1)
+    products, rims = [], []
+    for one in range(2):
+        epoch = here * 2 + one
+        mates = [partner[epoch * SLOTS + slot] for slot in range(SLOTS)]
+        more, more_rims = pair_batch(tiles + epoch, epoch, mates, total, looks, main, rim)
+        products += more
+        rims += more_rims
+    return products, rims
 
 
 def clipped(value, last):
@@ -407,14 +423,14 @@
     @pl.loop(0, last + 2)
     def _(turn):
         here = clipped(turn - 1, last)
+        sums = [rows_summed(here * 2 + one, look_rows, sum_rows, wide) for one in range(2)]
+        columns = columns_summed(clipped(turn, last), look_rows, bands, looked, rim_looked)
+        products, rims = pair_couple(turn, tiles, total, partner, look_rows, main, rim)
         for one in range(2):
-            boxed[here * 2 + one] = rows_summed(here * 2 + one, look_rows, sum_rows, wide)
-        columns_summed(clipped(turn, last), look_rows, bands, looked, rim_looked, wide)
-        here = clipped(turn, total // 2 - 1)
-        for one in range(2):
-            epoch = here * 2 + one
-            mates = [partner[epoch * SLOTS + slot] for slot in range(SLOTS)]
-            pair_batch(tiles + epoch, epoch, mates, total, look_rows, main, rim, looked, rim_looked)
+            boxed[here * 2 + one] = sums[one]
+        put(wide, columns)
+        put(looked, products)
+        put(rim_looked, rims)
 
 
 def border_kernel(sizes, partner, weight, present, *refs):
@@ -446,9 +462,10 @@
 
     @pl.loop(0, last + 3)
     def _(turn):
-        here = clipped(turn - 2 - tiles // 2, total // 2 - 1)
+        done = clipped(turn - 2 - tiles // 2, total // 2 - 1)
+        results = []
         for one in range(2):
-            epoch = here * 2 + one
+            epoch = done * 2 + one
             batch = tiles + epoch
             own_power = power_of(epoch)
             for slot in range(SLOTS):
@@ -457,18 +474,19 @@
                 unit_re = boxed[batch, slot * look_rows : (slot + 1) * look_rows, :] * inverse
                 unit_im = boxed[batch, (SLOTS + slot) * look_rows : (SLOTS + slot + 1) * look_rows, :] * inverse
                 factor = weight[pair] * (unit_re * unit_re + unit_im * unit_im)
-                factors[pair] = factor
-                pulls[pair] = factor * unit_im
+                results.append((pair, factor, factor * unit_im))
         here = clipped(turn - 1, last)
-        values = [inner[here * 2 + one] + rows_summed(here * 2 + one, looks, sum_rows, wide) for one in range(2)]
+        sums = [inner[here * 2 + one] + rows_summed(here * 2 + one, looks, sum_rows, wide) for one in range(2)]
+        columns = columns_summed(clipped(turn, last), looks, bands, looked, rim_looked)
+        products, rims = pair_couple(turn, tiles, total, partner, looks, main, rim)
+        for pair, factor, pull in results:
+            factors[pair] = factor
+            pulls[pair] = pull
         for one in range(2):
-            boxed[here * 2 + one] = values[one]
-        columns_summed(clipped(turn, last), looks, bands, looked, rim_looked, wide)
-        here = clipped(turn, total // 2 - 1)
-        for one in range(2):
-            epoch = here * 2 + one
-            mates = [partner[epoch * SLOTS + slot] for slot in range(SLOTS)]
-            pair_batch(tiles + epoch, epoch, mates, total, looks, main, rim, looked, rim_looked)
+            boxed[here * 2 + one] = sums[one]
+        put(wide, columns)
+        put(looked, products)
+        put(rim_looked, rims)
 
 
 def gradient_kernel(sizes, partner, *refs):

time: 74.8 us -> 74.8 us (level)
  no operation moved by 1% of the time
where the time goes in v10:
time: 74.8 us; the launch traced here: 74.6 us
  waiting for transfers between devices  23.4 us (31%)
  starting transfers between devices  23.1 us (31%)
  Pallas kernels  23 us (31%)
  local copies, waits for them, and re-layouts  3.29 us (4%)
  between operations  1.43 us (2%)
    ppermute x9, waiting for transfers between devices, to_ahead(): return lax.ppermute(x, axis, [(i, (i + by) % size) for i in range(size)])  20.5 us
    ppermute x9, starting transfers between devices, to_ahead(): return lax.ppermute(x, axis, [(i, (i + by) % size) for i in range(size)])  20.2 us
    pallas_call x1, Pallas kernels, transposed_plan(): pl.pallas_call(functools.partial(inner_kernel, (tiles, epochs, rows)), ou...  10.7 us
    pallas_call x1, Pallas kernels, transposed_plan(): pl.pallas_call(functools.partial(border_kernel, (tiles, epochs, look_rows...  8.17 us
    ppermute x3, waiting for transfers between devices, transposed_plan(): lax.ppermute(sums, place, [(i, (i + by) % count) for i in range(count)])  2.91 us
    unnamed x10, local copies, waits for them, and re-layouts  2.74 us
    pallas_call x1, Pallas kernels, transposed_plan(): pl.pallas_call(functools.partial(gradient_kernel, (tiles, epochs)), out_s...  1.67 us
    ppermute x1, starting transfers between devices, halo(): lax.ppermute(border(jnp.where(space == 0, rows - HALO, 0)), 'space', [(0,...  1.56 us
  transfers between devices with their start and end apart: 14, of which 6 were waited for; matrix products, arithmetic and copies ran while one was open for 3% of the time, Pallas kernels for 25%

profile of v10, /device:TPU:0, one launch (start us, length us, event | category | flops | bytes accessed | tf_op | source)
XLA Modules:
  0.0 74.6 jit_solution(10345303104132905665)
XLA Ops:
  0.6 1.2 %copy-done = bf16[2,8,64,512]{3,2,1,0:T(8,128)(2,1)S(1)} copy-done((bf16[2,8,64,512]{3,2,1,0:T(8,128)(2,1)S(1)}, bf16[2,8,64,512]{3,2,1,0:T(8,128)(2,1)}, u32[]{:S(2)}) %copy-start) | copy-done | bytes 1048600
  1.9 0.2 shard_map.77
  2.1 0.5 collective-permute-start
  2.6 0.8 %copy.12 = s32[8,4]{1,0:T(8,128)S(1)} copy(s32[8,4]{0,1:T(4,128)} %param.7) | data formatting | bytes 256 | tf_op args[1]
  3.4 0.8 %copy.13 = f32[8,4]{1,0:T(8,128)S(1)} copy(f32[8,4]{0,1:T(4,128)} %param.8) | data formatting | bytes 256 | tf_op args[2]
  4.1 0.1 select_maximum_fusion.params
  4.2 0.1 add_convert_fusion.present
  4.3 0.0 collective-permute-done.before.after
  4.3 1.3 %shard_map.78 = (bf16[1088,128]{1,0:T(8,128)(2,1)S(1)}, bf16[1088,128]{1,0:T(8,128)(2,1)S(1)}, bf16[1088,128]{1,0:T(8,128)(2,1)S(1)}, bf16[1088,128]{1,0:T(8,128)(2,1)S(1)}) custom-call(s32[1]{0:T(128)} %bitcast.me, f32[2]{0:T(128)S(1)} %add_convert_fusion.present, bf16[2,8,64,512]{3,2,1,0:T(8,128)(2,1)S(1)} %copy-done.1, ...), custom_call_target="tpu_custom_call" | custom-call | flops 3000000 | bytes 4000000 | tf_op jit(solution)/shard_map/pallas_call | solution.py:638
  5.6 2.8 %collective-permute-start.3 = (bf16[1088,128]{1,0:T(8,128)(2,1)S(1)}, bf16[1088,128]{1,0:T(8,128)(2,1)S(1)}, u32[]{:S(2)}, u32[]{:S(2)}) collective-permute-start(bf16[1088,128]{1,0:T(8,128)(2,1)S(1)} %get-tuple-element.24), channel_id=1, source_target_pairs={{0,4},{4,8},{8,12},{12,0},{1,5},{5,9},{9,13},{13,1},{2,6},{6,10},{... | collective-permute-start | bytes 835592 | tf_op jit(solution)/shard_map/ppermute | solution.py:602
  8.4 2.6 %collective-permute-start.2 = (bf16[1088,128]{1,0:T(8,128)(2,1)S(1)}, bf16[1088,128]{1,0:T(8,128)(2,1)S(1)}, u32[]{:S(2)}, u32[]{:S(2)}) collective-permute-start(bf16[1088,128]{1,0:T(8,128)(2,1)S(1)} %get-tuple-element.25), channel_id=1, source_target_pairs={{0,8},{4,12},{8,0},{12,4},{1,9},{5,13},{9,1},{13,5},{2,10},{6,14},... | collective-permute-start | bytes 835592 | tf_op jit(solution)/shard_map/ppermute | solution.py:602
  11.0 0.1 add_convert_fusion.1.present
  11.0 1.3 %collective-permute-start.1 = (bf16[1088,128]{1,0:T(8,128)(2,1)S(1)}, bf16[1088,128]{1,0:T(8,128)(2,1)S(1)}, u32[]{:S(2)}, u32[]{:S(2)}) collective-permute-start(bf16[1088,128]{1,0:T(8,128)(2,1)S(1)} %get-tuple-element.26), channel_id=1, source_target_pairs={{0,12},{4,0},{8,4},{12,8},{1,13},{5,1},{9,5},{13,9},{2,14},{6,2},{... | collective-permute-start | bytes 835592 | tf_op jit(solution)/shard_map/ppermute | solution.py:602
  12.4 0.1 slice.24
  12.5 0.1 shard_map.79
  12.6 5.5 %collective-permute-done.3.refs_3_ = bf16[1088,128]{1,0:T(8,128)(2,1)S(1)} collective-permute-done((bf16[1088,128]{1,0:T(8,128)(2,1)S(1)}, bf16[1088,128]{1,0:T(8,128)(2,1)S(1)}, u32[]{:S(2)}, u32[]{:S(2)}) %collective-permute-start.3) | collective-permute-done | bytes 278560 | tf_op jit(solution)/shard_map/ppermute | solution.py:602
  18.1 11.6 %collective-permute-done.2.refs_2_ = bf16[1088,128]{1,0:T(8,128)(2,1)S(1)} collective-permute-done((bf16[1088,128]{1,0:T(8,128)(2,1)S(1)}, bf16[1088,128]{1,0:T(8,128)(2,1)S(1)}, u32[]{:S(2)}, u32[]{:S(2)}) %collective-permute-start.2) | collective-permute-done | bytes 278560 | tf_op jit(solution)/shard_map/ppermute | solution.py:602
  29.6 0.0 collective-permute-done.1.refs_1_
  29.7 1.6 %collective-permute-start.7 = (bf16[1088,128]{1,0:T(8,128)(2,1)S(1)}, bf16[1088,128]{1,0:T(8,128)(2,1)S(1)}, u32[]{:S(2)}, u32[]{:S(2)}) collective-permute-start(bf16[1088,128]{1,0:T(8,128)(2,1)S(1)} %pad_maximum_fusion), channel_id=1, source_target_pairs={{0,2},{2,0},{1,3},{3,1},{4,6},{6,4},{5,7},{7,5},{8,10},{10,8},{9,1... | collective-permute-start | bytes 835592 | tf_op jit(solution)/shard_map/ppermute | solution.py:671
  31.3 0.1 slice.34
  31.3 0.1 slice.33
  31.4 0.1 slice.32
  31.5 0.1 slice_add_fusion
  31.6 7.5 %collective-permute-start.4 = (bf16[3,128,128]{2,1,0:T(8,128)(2,1)S(1)}, bf16[3,128,128]{2,1,0:T(8,128)(2,1)S(1)}, u32[]{:S(2)}, u32[]{:S(2)}) collective-permute-start(bf16[3,128,128]{2,1,0:T(8,128)(2,1)S(1)} %get-tuple-element.33), channel_id=1, source_target_pairs={{0,12},{4,0},{8,4},{12,8},{1,13},{5,1},{9,5},{13,9},{2,14},{6,2},{... | collective-permute-start | bytes 294920 | tf_op jit(solution)/shard_map/ppermute | solution.py:602
  39.0 0.4 collective-permute-start.5
  39.5 0.2 collective-permute-start.6
  39.7 0.1 reshape.41.weight
  39.8 0.1 reshape.40.partner
  39.9 10.7 %shard_map.80.refs_2_ = f32[36,128,128]{2,1,0:T(8,128)S(1)} custom-call(s32[128]{0:T(128)S(1)} %reshape.40.partner, bf16[1088,128]{1,0:T(8,128)(2,1)S(1)} %get-tuple-element.23.refs_0_, bf16[1088,128]{1,0:T(8,128)(2,1)S(1)} %collective-permute-done.1.refs_1_, bf16[1088,128]{1,0:T(8,128)(2,1)S(1)} %collective-permute-done.2.refs_2_, ...), custom_call_target="tpu_custom_call" | custom-call | flops 20000000 | bytes 20000000 | tf_op jit(solution)/shard_map/pallas_call | solution.py:707
  50.6 0.0 collective-permute-done.7.refs_0_.refs_1_
  50.6 8.2 %shard_map.81 = (f32[128,16,128]{2,1,0:T(8,128)S(1)}, f32[128,16,128]{2,1,0:T(8,128)S(1)}) custom-call(s32[128]{0:T(128)S(1)} %reshape.40.partner, f32[128]{0:T(128)S(1)} %reshape.41.weight, f32[2]{0:T(128)S(1)} %add_convert_fusion.1.present, bf16[1088,128]{1,0:T(8,128)(2,1)S(1)} %collective-permute-done.7.refs_0_.refs_1_, ...), custom_call_target="tpu_custom_call" | custom-call | flops 20000000 | bytes 15000000 | tf_op jit(solution)/shard_map/pallas_call | solution.py:717
  58.8 0.0 collective-permute-done.4.refs_1_
  58.8 0.0 collective-permute-done.5.refs_2_
  58.8 0.0 collective-permute-done.6.refs_3_
  58.8 1.7 %shard_map.82 = (f32[32,16,128]{2,1,0:T(8,128)S(1)}, f32[8,128]{1,0:T(8,128)S(1)}) custom-call(s32[128]{0:T(128)S(1)} %reshape.40.partner, bf16[3,128,128]{2,1,0:T(8,128)(2,1)S(1)} %get-tuple-element.29.refs_0_, bf16[3,128,128]{2,1,0:T(8,128)(2,1)S(1)} %collective-permute-done.4.refs_1_, bf16[3,128,128]{2,1,0:T(8,128)(2,1)S(1)} %collective-permute-done.5.refs_2_, ...), custom_call_target="tpu_custom_call" | custom-call | flops 10000000 | bytes 8000000 | tf_op jit(solution)/shard_map/pallas_call | solution.py:726
  60.5 0.1 collective-permute-start.10
  60.6 0.6 collective-permute-start.9
  61.2 0.2 collective-permute-start.8
  61.3 0.6 collective-permute-done.10.refs_3_
  61.9 2.4 %collective-permute-done.9.refs_2_ = f32[8,128]{1,0:T(8,128)S(1)} collective-permute-done((f32[8,128]{1,0:T(8,128)S(1)}, f32[8,128]{1,0:T(8,128)S(1)}, u32[]{:S(2)}, u32[]{:S(2)}) %collective-permute-start.9) | collective-permute-done | bytes 4128 | tf_op jit(solution)/shard_map/ppermute | solution.py:741
  64.2 0.0 collective-permute-done.8.refs_1_
  64.3 2.9 %collective-permute-start.11 = (f32[136,128]{1,0:T(8,128)S(1)}, f32[136,128]{1,0:T(8,128)S(1)}, u32[]{:S(2)}, u32[]{:S(2)}) collective-permute-start(f32[136,128]{1,0:T(8,128)S(1)} %get-tuple-element.41), channel_id=1, source_target_pairs={{0,4},{4,8},{8,12},{12,0},{1,5},{5,9},{9,13},{13,1},{2,6},{6,10},{... | collective-permute-start | bytes 208904 | tf_op jit(solution)/shard_map/ppermute | solution.py:602
  67.2 1.3 %collective-permute-start.12 = (f32[136,128]{1,0:T(8,128)S(1)}, f32[136,128]{1,0:T(8,128)S(1)}, u32[]{:S(2)}, u32[]{:S(2)}) collective-permute-start(f32[136,128]{1,0:T(8,128)S(1)} %get-tuple-element.42), channel_id=1, source_target_pairs={{0,8},{4,12},{8,0},{12,4},{1,9},{5,13},{9,1},{13,5},{2,10},{6,14},... | collective-permute-start | bytes 208904 | tf_op jit(solution)/shard_map/ppermute | solution.py:602
  68.5 1.1 %collective-permute-start.13 = (f32[136,128]{1,0:T(8,128)S(1)}, f32[136,128]{1,0:T(8,128)S(1)}, u32[]{:S(2)}, u32[]{:S(2)}) collective-permute-start(f32[136,128]{1,0:T(8,128)S(1)} %get-tuple-element.43), channel_id=1, source_target_pairs={{0,12},{4,0},{8,4},{12,8},{1,13},{5,1},{9,5},{13,9},{2,14},{6,2},{... | collective-permute-start | bytes 208904 | tf_op jit(solution)/shard_map/ppermute | solution.py:602
  70.3 0.8 %collective-permute-done.11.refs_1_ = f32[136,128]{1,0:T(8,128)S(1)} collective-permute-done((f32[136,128]{1,0:T(8,128)S(1)}, f32[136,128]{1,0:T(8,128)S(1)}, u32[]{:S(2)}, u32[]{:S(2)}) %collective-permute-start.11) | collective-permute-done | bytes 69664 | tf_op jit(solution)/shard_map/ppermute | solution.py:602
  71.1 2.6 %collective-permute-done.12.refs_2_ = f32[136,128]{1,0:T(8,128)S(1)} collective-permute-done((f32[136,128]{1,0:T(8,128)S(1)}, f32[136,128]{1,0:T(8,128)S(1)}, u32[]{:S(2)}, u32[]{:S(2)}) %collective-permute-start.12) | collective-permute-done | bytes 69664 | tf_op jit(solution)/shard_map/ppermute | solution.py:602
  73.7 0.0 collective-permute-done.13.refs_3_
  73.7 0.9 %shard_map.84 = (f32[8,16,512]{2,1,0:T(8,128)}, f32[8,16,512]{2,1,0:T(8,128)}) custom-call(s32[1]{0:T(128)} %bitcast.me, f32[1]{0:T(128)S(6)} %copy.16.prev_mean, f32[8,16,512]{2,1,0:T(8,128)S(1)} %copy-done.2, f32[8,16,512]{2,1,0:T(8,128)S(1)} %copy-done.3, f32[136,128]{1,0:T(8,128)S(1)} %get-tuple-element.40.refs_0_, ...), custom_call_target="tpu_custom_call" | custom-call | flops 1000000 | bytes 2000000 | tf_op jit(solution)/shard_map/pallas_call | solution.py:752
  (16 shorter events, 0.1 us)
Async XLA Ops:
  0.6 1.2 %copy-start = (bf16[2,8,64,512]{3,2,1,0:T(8,128)(2,1)S(1)}, bf16[2,8,64,512]{3,2,1,0:T(8,128)(2,1)}, u32[]{:S(2)}) copy-start(bf16[2,8,64,512]{3,2,1,0:T(8,128)(2,1)} %slc.1) | copy-start | bytes 3145732
  1.9 2.4 %copy-start.1 = (bf16[2,8,64,512]{3,2,1,0:T(8,128)(2,1)S(1)}, bf16[2,8,64,512]{3,2,1,0:T(8,128)(2,1)}, u32[]{:S(2)}) copy-start(bf16[2,8,64,512]{3,2,1,0:T(8,128)(2,1)} %slc.1) | copy-start | bytes 3145732
  1.9 10.6 %copy-start.2 = (f32[8,16,512]{2,1,0:T(8,128)S(1)}, f32[8,16,512]{2,1,0:T(8,128)}, u32[]{:S(2)}) copy-start(f32[8,16,512]{2,1,0:T(8,128)} %estimate.1) | copy-start | bytes 786436
  1.9 10.6 %copy-start.3 = (f32[8,16,512]{2,1,0:T(8,128)S(1)}, f32[8,16,512]{2,1,0:T(8,128)}, u32[]{:S(2)}) copy-start(f32[8,16,512]{2,1,0:T(8,128)} %direction.1) | copy-start | bytes 786436
  2.1 2.2 %collective-permute-start = (bf16[64,128]{1,0:T(8,128)(2,1)S(1)}, bf16[64,128]{1,0:T(8,128)(2,1)S(1)}, u32[]{:S(2)}, u32[]{:S(2)}) collective-permute-start(bf16[64,128]{1,0:T(8,128)(2,1)S(1)} %shard_map.77), channel_id=1, source_target_pairs={{0,1},{1,0},{2,3},{3,2},{4,5},{5,4},{6,7},{7,6},{8,9},{9,8},{10,11... | collective-permute-start | bytes 49160 | tf_op jit(solution)/shard_map/ppermute | solution.py:593
  5.6 12.5 %collective-permute-start.3 = (bf16[1088,128]{1,0:T(8,128)(2,1)S(1)}, bf16[1088,128]{1,0:T(8,128)(2,1)S(1)}, u32[]{:S(2)}, u32[]{:S(2)}) collective-permute-start(bf16[1088,128]{1,0:T(8,128)(2,1)S(1)} %get-tuple-element.24), channel_id=1, source_target_pairs={{0,4},{4,8},{8,12},{12,0},{1,5},{5,9},{9,13},{13,1},{2,6},{6,10},{... | collective-permute-start | bytes 835592 | tf_op jit(solution)/shard_map/ppermute | solution.py:602
  8.4 21.3 %collective-permute-start.2 = (bf16[1088,128]{1,0:T(8,128)(2,1)S(1)}, bf16[1088,128]{1,0:T(8,128)(2,1)S(1)}, u32[]{:S(2)}, u32[]{:S(2)}) collective-permute-start(bf16[1088,128]{1,0:T(8,128)(2,1)S(1)} %get-tuple-element.25), channel_id=1, source_target_pairs={{0,8},{4,12},{8,0},{12,4},{1,9},{5,13},{9,1},{13,5},{2,10},{6,14},... | collective-permute-start | bytes 835592 | tf_op jit(solution)/shard_map/ppermute | solution.py:602
  11.0 18.6 %collective-permute-start.1 = (bf16[1088,128]{1,0:T(8,128)(2,1)S(1)}, bf16[1088,128]{1,0:T(8,128)(2,1)S(1)}, u32[]{:S(2)}, u32[]{:S(2)}) collective-permute-start(bf16[1088,128]{1,0:T(8,128)(2,1)S(1)} %get-tuple-element.26), channel_id=1, source_target_pairs={{0,12},{4,0},{8,4},{12,8},{1,13},{5,1},{9,5},{13,9},{2,14},{6,2},{... | collective-permute-start | bytes 835592 | tf_op jit(solution)/shard_map/ppermute | solution.py:602
  29.7 20.9 %collective-permute-start.7 = (bf16[1088,128]{1,0:T(8,128)(2,1)S(1)}, bf16[1088,128]{1,0:T(8,128)(2,1)S(1)}, u32[]{:S(2)}, u32[]{:S(2)}) collective-permute-start(bf16[1088,128]{1,0:T(8,128)(2,1)S(1)} %pad_maximum_fusion), channel_id=1, source_target_pairs={{0,2},{2,0},{1,3},{3,1},{4,6},{6,4},{5,7},{7,5},{8,10},{10,8},{9,1... | collective-permute-start | bytes 835592 | tf_op jit(solution)/shard_map/ppermute | solution.py:671
  31.6 27.2 %collective-permute-start.4 = (bf16[3,128,128]{2,1,0:T(8,128)(2,1)S(1)}, bf16[3,128,128]{2,1,0:T(8,128)(2,1)S(1)}, u32[]{:S(2)}, u32[]{:S(2)}) collective-permute-start(bf16[3,128,128]{2,1,0:T(8,128)(2,1)S(1)} %get-tuple-element.33), channel_id=1, source_target_pairs={{0,12},{4,0},{8,4},{12,8},{1,13},{5,1},{9,5},{13,9},{2,14},{6,2},{... | collective-permute-start | bytes 294920 | tf_op jit(solution)/shard_map/ppermute | solution.py:602
  39.0 19.8 %collective-permute-start.5 = (bf16[3,128,128]{2,1,0:T(8,128)(2,1)S(1)}, bf16[3,128,128]{2,1,0:T(8,128)(2,1)S(1)}, u32[]{:S(2)}, u32[]{:S(2)}) collective-permute-start(bf16[3,128,128]{2,1,0:T(8,128)(2,1)S(1)} %get-tuple-element.34), channel_id=1, source_target_pairs={{0,8},{4,12},{8,0},{12,4},{1,9},{5,13},{9,1},{13,5},{2,10},{6,14},... | collective-permute-start | bytes 294920 | tf_op jit(solution)/shard_map/ppermute | solution.py:602
  39.5 19.4 %collective-permute-start.6 = (bf16[3,128,128]{2,1,0:T(8,128)(2,1)S(1)}, bf16[3,128,128]{2,1,0:T(8,128)(2,1)S(1)}, u32[]{:S(2)}, u32[]{:S(2)}) collective-permute-start(bf16[3,128,128]{2,1,0:T(8,128)(2,1)S(1)} %get-tuple-element.35), channel_id=1, source_target_pairs={{0,4},{4,8},{8,12},{12,0},{1,5},{5,9},{9,13},{13,1},{2,6},{6,10},{... | collective-permute-start | bytes 294920 | tf_op jit(solution)/shard_map/ppermute | solution.py:602
  60.5 1.4 %collective-permute-start.10 = (f32[8,128]{1,0:T(8,128)S(1)}, f32[8,128]{1,0:T(8,128)S(1)}, u32[]{:S(2)}, u32[]{:S(2)}) collective-permute-start(f32[8,128]{1,0:T(8,128)S(1)} %get-tuple-element.39.refs_0_), channel_id=1, source_target_pairs={{0,3},{1,0},{2,1},{3,2},{4,7},{5,4},{6,5},{7,6},{8,11},{9,8},{10,9... | collective-permute-start | bytes 12296 | tf_op jit(solution)/shard_map/ppermute | solution.py:741
  60.6 3.7 %collective-permute-start.9 = (f32[8,128]{1,0:T(8,128)S(1)}, f32[8,128]{1,0:T(8,128)S(1)}, u32[]{:S(2)}, u32[]{:S(2)}) collective-permute-start(f32[8,128]{1,0:T(8,128)S(1)} %get-tuple-element.39.refs_0_), channel_id=1, source_target_pairs={{0,2},{1,3},{2,0},{3,1},{4,6},{5,7},{6,4},{7,5},{8,10},{9,11},{10,... | collective-permute-start | bytes 12296 | tf_op jit(solution)/shard_map/ppermute | solution.py:741
  61.2 3.1 %collective-permute-start.8 = (f32[8,128]{1,0:T(8,128)S(1)}, f32[8,128]{1,0:T(8,128)S(1)}, u32[]{:S(2)}, u32[]{:S(2)}) collective-permute-start(f32[8,128]{1,0:T(8,128)S(1)} %get-tuple-element.39.refs_0_), channel_id=1, source_target_pairs={{0,1},{1,2},{2,3},{3,0},{4,5},{5,6},{6,7},{7,4},{8,9},{9,10},{10,1... | collective-permute-start | bytes 12296 | tf_op jit(solution)/shard_map/ppermute | solution.py:741
  64.3 6.8 %collective-permute-start.11 = (f32[136,128]{1,0:T(8,128)S(1)}, f32[136,128]{1,0:T(8,128)S(1)}, u32[]{:S(2)}, u32[]{:S(2)}) collective-permute-start(f32[136,128]{1,0:T(8,128)S(1)} %get-tuple-element.41), channel_id=1, source_target_pairs={{0,4},{4,8},{8,12},{12,0},{1,5},{5,9},{9,13},{13,1},{2,6},{6,10},{... | collective-permute-start | bytes 208904 | tf_op jit(solution)/shard_map/ppermute | solution.py:602
  67.2 6.5 %collective-permute-start.12 = (f32[136,128]{1,0:T(8,128)S(1)}, f32[136,128]{1,0:T(8,128)S(1)}, u32[]{:S(2)}, u32[]{:S(2)}) collective-permute-start(f32[136,128]{1,0:T(8,128)S(1)} %get-tuple-element.42), channel_id=1, source_target_pairs={{0,8},{4,12},{8,0},{12,4},{1,9},{5,13},{9,1},{13,5},{2,10},{6,14},... | collective-permute-start | bytes 208904 | tf_op jit(solution)/shard_map/ppermute | solution.py:602
  68.5 5.2 %collective-permute-start.13 = (f32[136,128]{1,0:T(8,128)S(1)}, f32[136,128]{1,0:T(8,128)S(1)}, u32[]{:S(2)}, u32[]{:S(2)}) collective-permute-start(f32[136,128]{1,0:T(8,128)S(1)} %get-tuple-element.43), channel_id=1, source_target_pairs={{0,12},{4,0},{8,4},{12,8},{1,13},{5,1},{9,5},{13,9},{2,14},{6,2},{... | collective-permute-start | bytes 208904 | tf_op jit(solution)/shard_map/ppermute | solution.py:602

commit v11 on v10

--- a/solution.py
+++ b/solution.py
@@ -324,36 +324,28 @@
                 rim_looked[at : at + 8, :] = mixed(squares)
 
 
-def pair_batch(batch, epoch, mates, total, looks, main, rim):
-    group = 2 * SLOTS
-    products, rims = [], []
-    for piece in range(0, looks, 8):
-        rows_at = slice(piece, piece + 8)
-        own_re = [main[epoch, look, rows_at] for look in range(LOOK)]
-        own_im = [main[total + epoch, look, rows_at] for look in range(LOOK)]
-        for slot, mate in enumerate(mates):
-            real = None
-            for look in range(LOOK):
-                mate_re = main[mate, look, rows_at]
-                mate_im = main[total + mate, look, rows_at]
-                one = own_re[look] * mate_re + own_im[look] * mate_im
-                two = own_im[look] * mate_re - own_re[look] * mate_im
-                real = one if real is None else real + one
-                imag = two if look == 0 else imag + two
-            products.append(((batch * group + slot) * looks + piece, real))
-            products.append(((batch * group + SLOTS + slot) * looks + piece, imag))
-        rim_re = rim[epoch, rows_at]
-        rim_im = rim[total + epoch, rows_at]
-        mate_re = mixed([rim[mate, rows_at] for mate in mates])
-        mate_im = mixed([rim[total + mate, rows_at] for mate in mates])
-        rims.append((batch * 2 * looks + piece, rim_re * mate_re + rim_im * mate_im))
-        rims.append(((batch * 2 + 1) * looks + piece, rim_im * mate_re - rim_re * mate_im))
-    return products, rims
-
-
-def put(ref, parts):
-    for at, value in parts:
-        ref[pl.ds(pl.multiple_of(at, 8), value.shape[0]), :] = value
+def pair_batch(epoch, mates, total, main, rim):
+    own_re, own_im = main[epoch], main[total + epoch]
+    reals, imags = [], []
+    for mate in mates:
+        mate_re, mate_im = main[mate], main[total + mate]
+        real = own_re[0] * mate_re[0] + own_im[0] * mate_im[0]
+        imag = own_im[0] * mate_re[0] - own_re[0] * mate_im[0]
+        for look in range(1, LOOK):
+            real = real + (own_re[look] * mate_re[look] + own_im[look] * mate_im[look])
+            imag = imag + (own_im[look] * mate_re[look] - own_re[look] * mate_im[look])
+        reals.append(real)
+        imags.append(imag)
+    own_re, own_im = rim[epoch], rim[total + epoch]
+    mate_re = mixed([rim[mate] for mate in mates])
+    mate_im = mixed([rim[total + mate] for mate in mates])
+    rims = [own_re * mate_re + own_im * mate_im, own_im * mate_re - own_re * mate_im]
+    return reals + imags, rims
+
+
+def put(ref, block, values):
+    rows = sum(value.shape[0] for value in values)
+    ref[pl.ds(pl.multiple_of(block * rows, rows), rows), :] = jnp.concatenate(values, axis=0)
 
 
 def columns_summed(couple, looks, bands, looked, rim_looked):
@@ -375,7 +367,7 @@
         if slot > 0:
             part = pltpu.roll(part, LANES - slot * (LANES // SLOTS), axis=1)
         row = channel * looks
-        results.append((couple * (2 * group * looks) + row, value[row : row + looks] + jnp.where(outside, part, 0.0)))
+        results.append(value[row : row + looks] + jnp.where(outside, part, 0.0))
     return results
 
 
@@ -387,13 +379,12 @@
     return value[:, :LANES] + value[:, LANES:]
 
 
-def pair_couple(turn, tiles, total, partner, looks, main, rim):
-    here = clipped(turn, total // 2 - 1)
+def pair_couple(couple, total, partner, main, rim):
     products, rims = [], []
     for one in range(2):
-        epoch = here * 2 + one
+        epoch = couple * 2 + one
         mates = [partner[epoch * SLOTS + slot] for slot in range(SLOTS)]
-        more, more_rims = pair_batch(tiles + epoch, epoch, mates, total, looks, main, rim)
+        more, more_rims = pair_batch(epoch, mates, total, main, rim)
         products += more
         rims += more_rims
     return products, rims
@@ -422,15 +413,16 @@
 
     @pl.loop(0, last + 2)
     def _(turn):
-        here = clipped(turn - 1, last)
-        sums = [rows_summed(here * 2 + one, look_rows, sum_rows, wide) for one in range(2)]
-        columns = columns_summed(clipped(turn, last), look_rows, bands, looked, rim_looked)
-        products, rims = pair_couple(turn, tiles, total, partner, look_rows, main, rim)
-        for one in range(2):
-            boxed[here * 2 + one] = sums[one]
-        put(wide, columns)
-        put(looked, products)
-        put(rim_looked, rims)
+        summed = clipped(turn - 1, last)
+        sums = [rows_summed(summed * 2 + one, look_rows, sum_rows, wide) for one in range(2)]
+        couple = clipped(turn, last)
+        columns = columns_summed(couple, look_rows, bands, looked, rim_looked)
+        here = clipped(turn, total // 2 - 1)
+        products, rims = pair_couple(here, total, partner, main, rim)
+        put(boxed, summed, sums)
+        put(wide, couple, columns)
+        put(looked, tiles // 2 + here, products)
+        put(rim_looked, tiles // 2 + here, rims)
 
 
 def border_kernel(sizes, partner, weight, present, *refs):
@@ -456,9 +448,8 @@
     power_batches(tiles, epochs, looks, main, rim, looked, rim_looked)
     last = (tiles + total) // 2 - 1
 
-    def power_of(epoch):
-        at = pl.ds(pl.multiple_of(epoch % epochs * look_rows, look_rows), look_rows)
-        return boxed[epoch // epochs, at, :]
+    def boxed_of(channel):
+        return boxed[pl.ds(pl.multiple_of(channel * look_rows, look_rows), look_rows), :]
 
     @pl.loop(0, last + 3)
     def _(turn):
@@ -466,27 +457,31 @@
         results = []
         for one in range(2):
             epoch = done * 2 + one
-            batch = tiles + epoch
-            own_power = power_of(epoch)
+            own_power = boxed_of(epoch)
+            first = (tiles + epoch) * (2 * SLOTS * look_rows)
+            parts = boxed[pl.ds(pl.multiple_of(first, 2 * SLOTS * look_rows), 2 * SLOTS * look_rows), :]
+            parts = parts.reshape(2 * SLOTS, look_rows, LANES)
             for slot in range(SLOTS):
                 pair = epoch * SLOTS + slot
-                inverse = lax.rsqrt(own_power * power_of(partner[pair]) + EPSILON)
-                unit_re = boxed[batch, slot * look_rows : (slot + 1) * look_rows, :] * inverse
-                unit_im = boxed[batch, (SLOTS + slot) * look_rows : (SLOTS + slot + 1) * look_rows, :] * inverse
+                inverse = lax.rsqrt(own_power * boxed_of(partner[pair]) + EPSILON)
+                unit_re = parts[slot] * inverse
+                unit_im = parts[SLOTS + slot] * inverse
                 factor = weight[pair] * (unit_re * unit_re + unit_im * unit_im)
-                results.append((pair, factor, factor * unit_im))
-        here = clipped(turn - 1, last)
-        sums = [inner[here * 2 + one] + rows_summed(here * 2 + one, looks, sum_rows, wide) for one in range(2)]
-        columns = columns_summed(clipped(turn, last), looks, bands, looked, rim_looked)
-        products, rims = pair_couple(turn, tiles, total, partner, looks, main, rim)
-        for pair, factor, pull in results:
-            factors[pair] = factor
-            pulls[pair] = pull
-        for one in range(2):
-            boxed[here * 2 + one] = sums[one]
-        put(wide, columns)
-        put(looked, products)
-        put(rim_looked, rims)
+                results.append((factor, factor * unit_im))
+        summed = clipped(turn - 1, last)
+        half = 2 * SLOTS * look_rows
+        share = inner[pl.ds(pl.multiple_of(summed * 2 * half, 2 * half), 2 * half), :]
+        sums = [share[one * half : (one + 1) * half] + rows_summed(summed * 2 + one, looks, sum_rows, wide) for one in range(2)]
+        couple = clipped(turn, last)
+        columns = columns_summed(couple, looks, bands, looked, rim_looked)
+        here = clipped(turn, total // 2 - 1)
+        products, rims = pair_couple(here, total, partner, main, rim)
+        for ref, values in zip((factors, pulls), zip(*results)):
+            ref[pl.ds(done * 2 * SLOTS, 2 * SLOTS)] = jnp.stack(values)
+        put(boxed, summed, sums)
+        put(wide, couple, columns)
+        put(looked, tiles // 2 + here, products)
+        put(rim_looked, tiles // 2 + here, rims)
 
 
 def gradient_kernel(sizes, partner, *refs):
@@ -703,7 +698,7 @@
             pltpu.VMEM((batches * group * looks, LANES), f32),
         ]
 
-    boxed_shape = (batches, group * look_rows, LANES)
+    boxed_shape = (batches * group * look_rows, LANES)
     inner = pl.pallas_call(
         functools.partial(inner_kernel, (tiles, epochs, rows)),
         out_shape=jax.ShapeDtypeStruct(boxed_shape, f32),

time: 74.8 us -> 74 us (0.989)
  Pallas kernels: 23 us -> 22.2 us
    pallas_call x1, Pallas kernels: 8.17 us -> 7.38 us  [transposed_plan(): pl.pallas_call(functools.partial(border_kernel, (tiles, epochs, look_rows...]
  transfers between devices with their start and end apart: 14 -> 14, of which waited for: 6 -> 6; matrix products, arithmetic and copies ran while one was open for 3% -> 3% of each run, Pallas kernels for 25% -> 24%
where the time goes in v11:
time: 74 us; the launch traced here: 73.8 us
  waiting for transfers between devices  23.4 us (32%)
  starting transfers between devices  23.1 us (31%)
  Pallas kernels  22.2 us (30%)
  local copies, waits for them, and re-layouts  3.29 us (4%)
  between operations  1.43 us (2%)
    ppermute x9, waiting for transfers between devices, to_ahead(): return lax.ppermute(x, axis, [(i, (i + by) % size) for i in range(size)])  20.5 us
    ppermute x9, starting transfers between devices, to_ahead(): return lax.ppermute(x, axis, [(i, (i + by) % size) for i in range(size)])  20.2 us
    pallas_call x1, Pallas kernels, transposed_plan(): pl.pallas_call(functools.partial(inner_kernel, (tiles, epochs, rows)), ou...  10.6 us
    pallas_call x1, Pallas kernels, transposed_plan(): pl.pallas_call(functools.partial(border_kernel, (tiles, epochs, look_rows...  7.38 us
    ppermute x3, waiting for transfers between devices, transposed_plan(): lax.ppermute(sums, place, [(i, (i + by) % count) for i in range(count)])  2.91 us
    unnamed x10, local copies, waits for them, and re-layouts  2.74 us
    pallas_call x1, Pallas kernels, transposed_plan(): pl.pallas_call(functools.partial(gradient_kernel, (tiles, epochs)), out_s...  1.67 us
    ppermute x1, starting transfers between devices, halo(): lax.ppermute(border(jnp.where(space == 0, rows - HALO, 0)), 'space', [(0,...  1.56 us
  transfers between devices with their start and end apart: 14, of which 6 were waited for; matrix products, arithmetic and copies ran while one was open for 3% of the time, Pallas kernels for 24%

profile of v11, /device:TPU:0, one launch (start us, length us, event | category | flops | bytes accessed | tf_op | source)
XLA Modules:
  0.0 73.8 jit_solution(6411474058660640923)
XLA Ops:
  0.6 1.2 %copy-done = bf16[2,8,64,512]{3,2,1,0:T(8,128)(2,1)S(1)} copy-done((bf16[2,8,64,512]{3,2,1,0:T(8,128)(2,1)S(1)}, bf16[2,8,64,512]{3,2,1,0:T(8,128)(2,1)}, u32[]{:S(2)}) %copy-start) | copy-done | bytes 1048600
  1.9 0.2 shard_map.77
  2.1 0.5 collective-permute-start
  2.6 0.8 %copy.12 = s32[8,4]{1,0:T(8,128)S(1)} copy(s32[8,4]{0,1:T(4,128)} %param.7) | data formatting | bytes 256 | tf_op args[1]
  3.4 0.8 %copy.13 = f32[8,4]{1,0:T(8,128)S(1)} copy(f32[8,4]{0,1:T(4,128)} %param.8) | data formatting | bytes 256 | tf_op args[2]
  4.1 0.1 select_maximum_fusion.params
  4.2 0.1 add_convert_fusion.present
  4.3 0.0 collective-permute-done.before.after
  4.3 1.3 %shard_map.78 = (bf16[1088,128]{1,0:T(8,128)(2,1)S(1)}, bf16[1088,128]{1,0:T(8,128)(2,1)S(1)}, bf16[1088,128]{1,0:T(8,128)(2,1)S(1)}, bf16[1088,128]{1,0:T(8,128)(2,1)S(1)}) custom-call(s32[1]{0:T(128)} %bitcast.me, f32[2]{0:T(128)S(1)} %add_convert_fusion.present, bf16[2,8,64,512]{3,2,1,0:T(8,128)(2,1)S(1)} %copy-done.1, ...), custom_call_target="tpu_custom_call" | custom-call | flops 3000000 | bytes 4000000 | tf_op jit(solution)/shard_map/pallas_call | solution.py:633
  5.6 2.8 %collective-permute-start.3 = (bf16[1088,128]{1,0:T(8,128)(2,1)S(1)}, bf16[1088,128]{1,0:T(8,128)(2,1)S(1)}, u32[]{:S(2)}, u32[]{:S(2)}) collective-permute-start(bf16[1088,128]{1,0:T(8,128)(2,1)S(1)} %get-tuple-element.24), channel_id=1, source_target_pairs={{0,4},{4,8},{8,12},{12,0},{1,5},{5,9},{9,13},{13,1},{2,6},{6,10},{... | collective-permute-start | bytes 835592 | tf_op jit(solution)/shard_map/ppermute | solution.py:597
  8.4 2.6 %collective-permute-start.2 = (bf16[1088,128]{1,0:T(8,128)(2,1)S(1)}, bf16[1088,128]{1,0:T(8,128)(2,1)S(1)}, u32[]{:S(2)}, u32[]{:S(2)}) collective-permute-start(bf16[1088,128]{1,0:T(8,128)(2,1)S(1)} %get-tuple-element.25), channel_id=1, source_target_pairs={{0,8},{4,12},{8,0},{12,4},{1,9},{5,13},{9,1},{13,5},{2,10},{6,14},... | collective-permute-start | bytes 835592 | tf_op jit(solution)/shard_map/ppermute | solution.py:597
  11.0 0.1 add_convert_fusion.1.present
  11.0 1.3 %collective-permute-start.1 = (bf16[1088,128]{1,0:T(8,128)(2,1)S(1)}, bf16[1088,128]{1,0:T(8,128)(2,1)S(1)}, u32[]{:S(2)}, u32[]{:S(2)}) collective-permute-start(bf16[1088,128]{1,0:T(8,128)(2,1)S(1)} %get-tuple-element.26), channel_id=1, source_target_pairs={{0,12},{4,0},{8,4},{12,8},{1,13},{5,1},{9,5},{13,9},{2,14},{6,2},{... | collective-permute-start | bytes 835592 | tf_op jit(solution)/shard_map/ppermute | solution.py:597
  12.4 0.1 slice.24
  12.5 0.1 shard_map.79
  12.6 5.5 %collective-permute-done.3.refs_3_ = bf16[1088,128]{1,0:T(8,128)(2,1)S(1)} collective-permute-done((bf16[1088,128]{1,0:T(8,128)(2,1)S(1)}, bf16[1088,128]{1,0:T(8,128)(2,1)S(1)}, u32[]{:S(2)}, u32[]{:S(2)}) %collective-permute-start.3) | collective-permute-done | bytes 278560 | tf_op jit(solution)/shard_map/ppermute | solution.py:597
  18.1 11.6 %collective-permute-done.2.refs_2_ = bf16[1088,128]{1,0:T(8,128)(2,1)S(1)} collective-permute-done((bf16[1088,128]{1,0:T(8,128)(2,1)S(1)}, bf16[1088,128]{1,0:T(8,128)(2,1)S(1)}, u32[]{:S(2)}, u32[]{:S(2)}) %collective-permute-start.2) | collective-permute-done | bytes 278560 | tf_op jit(solution)/shard_map/ppermute | solution.py:597
  29.6 0.0 collective-permute-done.1.refs_1_
  29.7 1.6 %collective-permute-start.7 = (bf16[1088,128]{1,0:T(8,128)(2,1)S(1)}, bf16[1088,128]{1,0:T(8,128)(2,1)S(1)}, u32[]{:S(2)}, u32[]{:S(2)}) collective-permute-start(bf16[1088,128]{1,0:T(8,128)(2,1)S(1)} %pad_maximum_fusion), channel_id=1, source_target_pairs={{0,2},{2,0},{1,3},{3,1},{4,6},{6,4},{5,7},{7,5},{8,10},{10,8},{9,1... | collective-permute-start | bytes 835592 | tf_op jit(solution)/shard_map/ppermute | solution.py:666
  31.3 0.1 slice.34
  31.3 0.1 slice.33
  31.4 0.1 slice.32
  31.5 0.1 slice_add_fusion
  31.6 7.5 %collective-permute-start.4 = (bf16[3,128,128]{2,1,0:T(8,128)(2,1)S(1)}, bf16[3,128,128]{2,1,0:T(8,128)(2,1)S(1)}, u32[]{:S(2)}, u32[]{:S(2)}) collective-permute-start(bf16[3,128,128]{2,1,0:T(8,128)(2,1)S(1)} %get-tuple-element.33), channel_id=1, source_target_pairs={{0,12},{4,0},{8,4},{12,8},{1,13},{5,1},{9,5},{13,9},{2,14},{6,2},{... | collective-permute-start | bytes 294920 | tf_op jit(solution)/shard_map/ppermute | solution.py:597
  39.0 0.4 collective-permute-start.5
  39.5 0.2 collective-permute-start.6
  39.7 0.1 reshape.41.weight
  39.8 0.1 reshape.40.partner
  39.9 10.6 %shard_map.80.refs_2_ = f32[4608,128]{1,0:T(8,128)S(1)} custom-call(s32[128]{0:T(128)S(1)} %reshape.40.partner, bf16[1088,128]{1,0:T(8,128)(2,1)S(1)} %get-tuple-element.23.refs_0_, bf16[1088,128]{1,0:T(8,128)(2,1)S(1)} %collective-permute-done.1.refs_1_, bf16[1088,128]{1,0:T(8,128)(2,1)S(1)} %collective-permute-done.2.refs_2_, ...), custom_call_target="tpu_custom_call" | custom-call | flops 20000000 | bytes 20000000 | tf_op jit(solution)/shard_map/pallas_call | solution.py:702
  50.5 0.0 collective-permute-done.7.refs_0_.refs_1_
  50.5 7.4 %shard_map.81 = (f32[128,16,128]{2,1,0:T(8,128)S(1)}, f32[128,16,128]{2,1,0:T(8,128)S(1)}) custom-call(s32[128]{0:T(128)S(1)} %reshape.40.partner, f32[128]{0:T(128)S(1)} %reshape.41.weight, f32[2]{0:T(128)S(1)} %add_convert_fusion.1.present, bf16[1088,128]{1,0:T(8,128)(2,1)S(1)} %collective-permute-done.7.refs_0_.refs_1_, ...), custom_call_target="tpu_custom_call" | custom-call | flops 20000000 | bytes 15000000 | tf_op jit(solution)/shard_map/pallas_call | solution.py:712
  57.9 0.0 collective-permute-done.4.refs_1_
  57.9 0.0 collective-permute-done.5.refs_2_
  57.9 0.0 collective-permute-done.6.refs_3_
  58.0 1.7 %shard_map.82 = (f32[32,16,128]{2,1,0:T(8,128)S(1)}, f32[8,128]{1,0:T(8,128)S(1)}) custom-call(s32[128]{0:T(128)S(1)} %reshape.40.partner, bf16[3,128,128]{2,1,0:T(8,128)(2,1)S(1)} %get-tuple-element.29.refs_0_, bf16[3,128,128]{2,1,0:T(8,128)(2,1)S(1)} %collective-permute-done.4.refs_1_, bf16[3,128,128]{2,1,0:T(8,128)(2,1)S(1)} %collective-permute-done.5.refs_2_, ...), custom_call_target="tpu_custom_call" | custom-call | flops 10000000 | bytes 8000000 | tf_op jit(solution)/shard_map/pallas_call | solution.py:721
  59.6 0.1 collective-permute-start.10
  59.7 0.6 collective-permute-start.9
  60.3 0.2 collective-permute-start.8
  60.5 0.6 collective-permute-done.10.refs_3_
  61.0 2.4 %collective-permute-done.9.refs_2_ = f32[8,128]{1,0:T(8,128)S(1)} collective-permute-done((f32[8,128]{1,0:T(8,128)S(1)}, f32[8,128]{1,0:T(8,128)S(1)}, u32[]{:S(2)}, u32[]{:S(2)}) %collective-permute-start.9) | collective-permute-done | bytes 4128 | tf_op jit(solution)/shard_map/ppermute | solution.py:736
  63.4 0.0 collective-permute-done.8.refs_1_
  63.4 2.9 %collective-permute-start.11 = (f32[136,128]{1,0:T(8,128)S(1)}, f32[136,128]{1,0:T(8,128)S(1)}, u32[]{:S(2)}, u32[]{:S(2)}) collective-permute-start(f32[136,128]{1,0:T(8,128)S(1)} %get-tuple-element.41), channel_id=1, source_target_pairs={{0,4},{4,8},{8,12},{12,0},{1,5},{5,9},{9,13},{13,1},{2,6},{6,10},{... | collective-permute-start | bytes 208904 | tf_op jit(solution)/shard_map/ppermute | solution.py:597
  66.3 1.3 %collective-permute-start.12 = (f32[136,128]{1,0:T(8,128)S(1)}, f32[136,128]{1,0:T(8,128)S(1)}, u32[]{:S(2)}, u32[]{:S(2)}) collective-permute-start(f32[136,128]{1,0:T(8,128)S(1)} %get-tuple-element.42), channel_id=1, source_target_pairs={{0,8},{4,12},{8,0},{12,4},{1,9},{5,13},{9,1},{13,5},{2,10},{6,14},... | collective-permute-start | bytes 208904 | tf_op jit(solution)/shard_map/ppermute | solution.py:597
  67.6 1.1 %collective-permute-start.13 = (f32[136,128]{1,0:T(8,128)S(1)}, f32[136,128]{1,0:T(8,128)S(1)}, u32[]{:S(2)}, u32[]{:S(2)}) collective-permute-start(f32[136,128]{1,0:T(8,128)S(1)} %get-tuple-element.43), channel_id=1, source_target_pairs={{0,12},{4,0},{8,4},{12,8},{1,13},{5,1},{9,5},{13,9},{2,14},{6,2},{... | collective-permute-start | bytes 208904 | tf_op jit(solution)/shard_map/ppermute | solution.py:597
  69.4 0.8 %collective-permute-done.11.refs_1_ = f32[136,128]{1,0:T(8,128)S(1)} collective-permute-done((f32[136,128]{1,0:T(8,128)S(1)}, f32[136,128]{1,0:T(8,128)S(1)}, u32[]{:S(2)}, u32[]{:S(2)}) %collective-permute-start.11) | collective-permute-done | bytes 69664 | tf_op jit(solution)/shard_map/ppermute | solution.py:597
  70.2 2.6 %collective-permute-done.12.refs_2_ = f32[136,128]{1,0:T(8,128)S(1)} collective-permute-done((f32[136,128]{1,0:T(8,128)S(1)}, f32[136,128]{1,0:T(8,128)S(1)}, u32[]{:S(2)}, u32[]{:S(2)}) %collective-permute-start.12) | collective-permute-done | bytes 69664 | tf_op jit(solution)/shard_map/ppermute | solution.py:597
  72.8 0.0 collective-permute-done.13.refs_3_
  72.8 0.9 %shard_map.84 = (f32[8,16,512]{2,1,0:T(8,128)}, f32[8,16,512]{2,1,0:T(8,128)}) custom-call(s32[1]{0:T(128)} %bitcast.me, f32[1]{0:T(128)S(6)} %copy.16.prev_mean, f32[8,16,512]{2,1,0:T(8,128)S(1)} %copy-done.2, f32[8,16,512]{2,1,0:T(8,128)S(1)} %copy-done.3, f32[136,128]{1,0:T(8,128)S(1)} %get-tuple-element.40.refs_0_, ...), custom_call_target="tpu_custom_call" | custom-call | flops 1000000 | bytes 2000000 | tf_op jit(solution)/shard_map/pallas_call | solution.py:747
  (16 shorter events, 0.1 us)
Async XLA Ops:
  0.6 1.2 %copy-start = (bf16[2,8,64,512]{3,2,1,0:T(8,128)(2,1)S(1)}, bf16[2,8,64,512]{3,2,1,0:T(8,128)(2,1)}, u32[]{:S(2)}) copy-start(bf16[2,8,64,512]{3,2,1,0:T(8,128)(2,1)} %slc.1) | copy-start | bytes 3145732
  1.9 2.4 %copy-start.1 = (bf16[2,8,64,512]{3,2,1,0:T(8,128)(2,1)S(1)}, bf16[2,8,64,512]{3,2,1,0:T(8,128)(2,1)}, u32[]{:S(2)}) copy-start(bf16[2,8,64,512]{3,2,1,0:T(8,128)(2,1)} %slc.1) | copy-start | bytes 3145732
  1.9 10.6 %copy-start.2 = (f32[8,16,512]{2,1,0:T(8,128)S(1)}, f32[8,16,512]{2,1,0:T(8,128)}, u32[]{:S(2)}) copy-start(f32[8,16,512]{2,1,0:T(8,128)} %estimate.1) | copy-start | bytes 786436
  1.9 10.6 %copy-start.3 = (f32[8,16,512]{2,1,0:T(8,128)S(1)}, f32[8,16,512]{2,1,0:T(8,128)}, u32[]{:S(2)}) copy-start(f32[8,16,512]{2,1,0:T(8,128)} %direction.1) | copy-start | bytes 786436
  2.1 2.2 %collective-permute-start = (bf16[64,128]{1,0:T(8,128)(2,1)S(1)}, bf16[64,128]{1,0:T(8,128)(2,1)S(1)}, u32[]{:S(2)}, u32[]{:S(2)}) collective-permute-start(bf16[64,128]{1,0:T(8,128)(2,1)S(1)} %shard_map.77), channel_id=1, source_target_pairs={{0,1},{1,0},{2,3},{3,2},{4,5},{5,4},{6,7},{7,6},{8,9},{9,8},{10,11... | collective-permute-start | bytes 49160 | tf_op jit(solution)/shard_map/ppermute | solution.py:588
  5.6 12.5 %collective-permute-start.3 = (bf16[1088,128]{1,0:T(8,128)(2,1)S(1)}, bf16[1088,128]{1,0:T(8,128)(2,1)S(1)}, u32[]{:S(2)}, u32[]{:S(2)}) collective-permute-start(bf16[1088,128]{1,0:T(8,128)(2,1)S(1)} %get-tuple-element.24), channel_id=1, source_target_pairs={{0,4},{4,8},{8,12},{12,0},{1,5},{5,9},{9,13},{13,1},{2,6},{6,10},{... | collective-permute-start | bytes 835592 | tf_op jit(solution)/shard_map/ppermute | solution.py:597
  8.4 21.3 %collective-permute-start.2 = (bf16[1088,128]{1,0:T(8,128)(2,1)S(1)}, bf16[1088,128]{1,0:T(8,128)(2,1)S(1)}, u32[]{:S(2)}, u32[]{:S(2)}) collective-permute-start(bf16[1088,128]{1,0:T(8,128)(2,1)S(1)} %get-tuple-element.25), channel_id=1, source_target_pairs={{0,8},{4,12},{8,0},{12,4},{1,9},{5,13},{9,1},{13,5},{2,10},{6,14},... | collective-permute-start | bytes 835592 | tf_op jit(solution)/shard_map/ppermute | solution.py:597
  11.0 18.6 %collective-permute-start.1 = (bf16[1088,128]{1,0:T(8,128)(2,1)S(1)}, bf16[1088,128]{1,0:T(8,128)(2,1)S(1)}, u32[]{:S(2)}, u32[]{:S(2)}) collective-permute-start(bf16[1088,128]{1,0:T(8,128)(2,1)S(1)} %get-tuple-element.26), channel_id=1, source_target_pairs={{0,12},{4,0},{8,4},{12,8},{1,13},{5,1},{9,5},{13,9},{2,14},{6,2},{... | collective-permute-start | bytes 835592 | tf_op jit(solution)/shard_map/ppermute | solution.py:597
  29.7 20.8 %collective-permute-start.7 = (bf16[1088,128]{1,0:T(8,128)(2,1)S(1)}, bf16[1088,128]{1,0:T(8,128)(2,1)S(1)}, u32[]{:S(2)}, u32[]{:S(2)}) collective-permute-start(bf16[1088,128]{1,0:T(8,128)(2,1)S(1)} %pad_maximum_fusion), channel_id=1, source_target_pairs={{0,2},{2,0},{1,3},{3,1},{4,6},{6,4},{5,7},{7,5},{8,10},{10,8},{9,1... | collective-permute-start | bytes 835592 | tf_op jit(solution)/shard_map/ppermute | solution.py:666
  31.6 26.4 %collective-permute-start.4 = (bf16[3,128,128]{2,1,0:T(8,128)(2,1)S(1)}, bf16[3,128,128]{2,1,0:T(8,128)(2,1)S(1)}, u32[]{:S(2)}, u32[]{:S(2)}) collective-permute-start(bf16[3,128,128]{2,1,0:T(8,128)(2,1)S(1)} %get-tuple-element.33), channel_id=1, source_target_pairs={{0,12},{4,0},{8,4},{12,8},{1,13},{5,1},{9,5},{13,9},{2,14},{6,2},{... | collective-permute-start | bytes 294920 | tf_op jit(solution)/shard_map/ppermute | solution.py:597
  39.0 18.9 %collective-permute-start.5 = (bf16[3,128,128]{2,1,0:T(8,128)(2,1)S(1)}, bf16[3,128,128]{2,1,0:T(8,128)(2,1)S(1)}, u32[]{:S(2)}, u32[]{:S(2)}) collective-permute-start(bf16[3,128,128]{2,1,0:T(8,128)(2,1)S(1)} %get-tuple-element.34), channel_id=1, source_target_pairs={{0,8},{4,12},{8,0},{12,4},{1,9},{5,13},{9,1},{13,5},{2,10},{6,14},... | collective-permute-start | bytes 294920 | tf_op jit(solution)/shard_map/ppermute | solution.py:597
  39.5 18.5 %collective-permute-start.6 = (bf16[3,128,128]{2,1,0:T(8,128)(2,1)S(1)}, bf16[3,128,128]{2,1,0:T(8,128)(2,1)S(1)}, u32[]{:S(2)}, u32[]{:S(2)}) collective-permute-start(bf16[3,128,128]{2,1,0:T(8,128)(2,1)S(1)} %get-tuple-element.35), channel_id=1, source_target_pairs={{0,4},{4,8},{8,12},{12,0},{1,5},{5,9},{9,13},{13,1},{2,6},{6,10},{... | collective-permute-start | bytes 294920 | tf_op jit(solution)/shard_map/ppermute | solution.py:597
  59.6 1.4 %collective-permute-start.10 = (f32[8,128]{1,0:T(8,128)S(1)}, f32[8,128]{1,0:T(8,128)S(1)}, u32[]{:S(2)}, u32[]{:S(2)}) collective-permute-start(f32[8,128]{1,0:T(8,128)S(1)} %get-tuple-element.39.refs_0_), channel_id=1, source_target_pairs={{0,3},{1,0},{2,1},{3,2},{4,7},{5,4},{6,5},{7,6},{8,11},{9,8},{10,9... | collective-permute-start | bytes 12296 | tf_op jit(solution)/shard_map/ppermute | solution.py:736
  59.7 3.7 %collective-permute-start.9 = (f32[8,128]{1,0:T(8,128)S(1)}, f32[8,128]{1,0:T(8,128)S(1)}, u32[]{:S(2)}, u32[]{:S(2)}) collective-permute-start(f32[8,128]{1,0:T(8,128)S(1)} %get-tuple-element.39.refs_0_), channel_id=1, source_target_pairs={{0,2},{1,3},{2,0},{3,1},{4,6},{5,7},{6,4},{7,5},{8,10},{9,11},{10,... | collective-permute-start | bytes 12296 | tf_op jit(solution)/shard_map/ppermute | solution.py:736
  60.3 3.1 %collective-permute-start.8 = (f32[8,128]{1,0:T(8,128)S(1)}, f32[8,128]{1,0:T(8,128)S(1)}, u32[]{:S(2)}, u32[]{:S(2)}) collective-permute-start(f32[8,128]{1,0:T(8,128)S(1)} %get-tuple-element.39.refs_0_), channel_id=1, source_target_pairs={{0,1},{1,2},{2,3},{3,0},{4,5},{5,6},{6,7},{7,4},{8,9},{9,10},{10,1... | collective-permute-start | bytes 12296 | tf_op jit(solution)/shard_map/ppermute | solution.py:736
  63.4 6.8 %collective-permute-start.11 = (f32[136,128]{1,0:T(8,128)S(1)}, f32[136,128]{1,0:T(8,128)S(1)}, u32[]{:S(2)}, u32[]{:S(2)}) collective-permute-start(f32[136,128]{1,0:T(8,128)S(1)} %get-tuple-element.41), channel_id=1, source_target_pairs={{0,4},{4,8},{8,12},{12,0},{1,5},{5,9},{9,13},{13,1},{2,6},{6,10},{... | collective-permute-start | bytes 208904 | tf_op jit(solution)/shard_map/ppermute | solution.py:597
  66.3 6.5 %collective-permute-start.12 = (f32[136,128]{1,0:T(8,128)S(1)}, f32[136,128]{1,0:T(8,128)S(1)}, u32[]{:S(2)}, u32[]{:S(2)}) collective-permute-start(f32[136,128]{1,0:T(8,128)S(1)} %get-tuple-element.42), channel_id=1, source_target_pairs={{0,8},{4,12},{8,0},{12,4},{1,9},{5,13},{9,1},{13,5},{2,10},{6,14},... | collective-permute-start | bytes 208904 | tf_op jit(solution)/shard_map/ppermute | solution.py:597
  67.6 5.2 %collective-permute-start.13 = (f32[136,128]{1,0:T(8,128)S(1)}, f32[136,128]{1,0:T(8,128)S(1)}, u32[]{:S(2)}, u32[]{:S(2)}) collective-permute-start(f32[136,128]{1,0:T(8,128)S(1)} %get-tuple-element.43), channel_id=1, source_target_pairs={{0,12},{4,0},{8,4},{12,8},{1,13},{5,1},{9,5},{13,9},{2,14},{6,2},{... | collective-permute-start | bytes 208904 | tf_op jit(solution)/shard_map/ppermute | solution.py:597

commit v12 on v11

--- a/solution.py
+++ b/solution.py
@@ -394,73 +394,53 @@
     return jnp.minimum(jnp.maximum(value, 0), last)
 
 
-def inner_kernel(sizes, partner, *refs):
-    tiles, epochs, rows = sizes
-    messages = refs[:tiles]
-    boxed, main, rim, looked, rim_looked, wide = refs[tiles:]
-    total = tiles * epochs
+def pair_kernel(sizes, places, partner, weight, present, *refs):
+    epochs, rows, operands = sizes
+    inputs = refs[:operands]
+    factors, pulls, boxed, main, rim, looked, rim_looked, wide = refs[operands:]
+    count = len(places)
+    total = count * epochs
+    own_total = total - epochs
     look_rows = rows // LOOK
-    order = look_order(rows, lambda at: 1.0)
+    halo_looks = HALO // LOOK
+    looks = look_rows + 2 * halo_looks
+    full_rows = rows + 2 * HALO
+    group = 2 * SLOTS
+
+    def keep(at):
+        return jnp.where(at < HALO, present[0], jnp.where(at >= HALO + rows, present[1], 1.0))
+
+    order = look_order(full_rows, keep)
     bands = column_bands()
-    sum_rows = row_sums(look_rows, look_rows, lambda look: look)
-    for block, message in enumerate(messages):
+    sum_rows = row_sums(look_rows, looks, lambda at: at - halo_looks)
+    for block, (tile_at, top_at, bottom_at, halo_row) in enumerate(places):
+        tile, top, bottom = inputs[tile_at], inputs[top_at], inputs[bottom_at]
+
+        def rows_of(at):
+            border = slice(halo_row + at * HALO, halo_row + (at + 1) * HALO)
+            return jnp.concatenate([top[border, :], tile[at * rows : (at + 1) * rows, :], bottom[border, :]], axis=0)
+
         first = [part * total + block * epochs + epoch for part in range(2) for epoch in range(epochs)]
-        unpack_tiles(order, range(2 * epochs), main, first, lambda at: message[at * rows : (at + 1) * rows, :])
-        by_look = jnp.dot(order, message[2 * epochs * rows :, :], preferred_element_type=jnp.float32)
-        unpack_rims(by_look, look_rows, rim, first)
-    power_batches(tiles, epochs, look_rows, main, rim, looked, rim_looked)
-    last = (tiles + total) // 2 - 1
-
-    @pl.loop(0, last + 2)
-    def _(turn):
-        summed = clipped(turn - 1, last)
-        sums = [rows_summed(summed * 2 + one, look_rows, sum_rows, wide) for one in range(2)]
-        couple = clipped(turn, last)
-        columns = columns_summed(couple, look_rows, bands, looked, rim_looked)
-        here = clipped(turn, total // 2 - 1)
-        products, rims = pair_couple(here, total, partner, main, rim)
-        put(boxed, summed, sums)
-        put(wide, couple, columns)
-        put(looked, tiles // 2 + here, products)
-        put(rim_looked, tiles // 2 + here, rims)
-
-
-def border_kernel(sizes, partner, weight, present, *refs):
-    tiles, epochs, look_rows = sizes
-    top, bottom, inner, factors, pulls, boxed, main, rim, looked, rim_looked, wide = refs
-    total = tiles * epochs
-    looks = 2 * HALO // LOOK
-    halo_looks = HALO // LOOK
-    tile_rows = (2 * epochs + 1) * HALO
-    order = look_order(2 * HALO, lambda at: jnp.where(at < HALO, present[0], present[1]))
-    bands = column_bands()
-    sum_rows = row_sums(look_rows, looks, lambda at: jnp.where(at < halo_looks, at - halo_looks, at - halo_looks + look_rows))
-    for block in range(tiles):
-
-        def border_of(at):
-            here = slice(block * tile_rows + at * HALO, block * tile_rows + (at + 1) * HALO)
-            return jnp.concatenate([top[here, :], bottom[here, :]], axis=0)
-
-        first = [part * total + block * epochs + epoch for part in range(2) for epoch in range(epochs)]
-        unpack_tiles(order, range(2 * epochs), main, first, border_of)
-        by_look = jnp.dot(order, border_of(2 * epochs), preferred_element_type=jnp.float32)
+        unpack_tiles(order, range(2 * epochs), main, first, rows_of)
+        by_look = jnp.dot(order, rows_of(2 * epochs), preferred_element_type=jnp.float32)
         unpack_rims(by_look, looks, rim, first)
-    power_batches(tiles, epochs, looks, main, rim, looked, rim_looked)
-    last = (tiles + total) // 2 - 1
+    power_batches(count, epochs, looks, main, rim, looked, rim_looked)
+    powers = (count + 1) // 2
+    last = powers + own_total // 2 - 1
 
     def boxed_of(channel):
         return boxed[pl.ds(pl.multiple_of(channel * look_rows, look_rows), look_rows), :]
 
     @pl.loop(0, last + 3)
     def _(turn):
-        done = clipped(turn - 2 - tiles // 2, total // 2 - 1)
+        done = clipped(turn - 2 - powers, own_total // 2 - 1)
         results = []
         for one in range(2):
             epoch = done * 2 + one
             own_power = boxed_of(epoch)
-            first = (tiles + epoch) * (2 * SLOTS * look_rows)
-            parts = boxed[pl.ds(pl.multiple_of(first, 2 * SLOTS * look_rows), 2 * SLOTS * look_rows), :]
-            parts = parts.reshape(2 * SLOTS, look_rows, LANES)
+            first = (2 * powers + epoch) * (group * look_rows)
+            parts = boxed[pl.ds(pl.multiple_of(first, group * look_rows), group * look_rows), :]
+            parts = parts.reshape(group, look_rows, LANES)
             for slot in range(SLOTS):
                 pair = epoch * SLOTS + slot
                 inverse = lax.rsqrt(own_power * boxed_of(partner[pair]) + EPSILON)
@@ -469,25 +449,25 @@
                 factor = weight[pair] * (unit_re * unit_re + unit_im * unit_im)
                 results.append((factor, factor * unit_im))
         summed = clipped(turn - 1, last)
-        half = 2 * SLOTS * look_rows
-        share = inner[pl.ds(pl.multiple_of(summed * 2 * half, 2 * half), 2 * half), :]
-        sums = [share[one * half : (one + 1) * half] + rows_summed(summed * 2 + one, looks, sum_rows, wide) for one in range(2)]
+        sums = [rows_summed(summed * 2 + one, looks, sum_rows, wide) for one in range(2)]
         couple = clipped(turn, last)
         columns = columns_summed(couple, looks, bands, looked, rim_looked)
-        here = clipped(turn, total // 2 - 1)
+        here = clipped(turn, own_total // 2 - 1)
         products, rims = pair_couple(here, total, partner, main, rim)
         for ref, values in zip((factors, pulls), zip(*results)):
             ref[pl.ds(done * 2 * SLOTS, 2 * SLOTS)] = jnp.stack(values)
         put(boxed, summed, sums)
         put(wide, couple, columns)
-        put(looked, tiles // 2 + here, products)
-        put(rim_looked, tiles // 2 + here, rims)
+        put(looked, powers + here, products)
+        put(rim_looked, powers + here, rims)
 
 
 def gradient_kernel(sizes, partner, *refs):
-    tiles, epochs = sizes
+    tiles, epochs, stages = sizes
     fields = refs[:tiles]
-    factors, pulls, gradient, sums, est, old = refs[tiles:]
+    factors = refs[tiles : tiles + len(stages)]
+    pulls = refs[tiles + len(stages) : tiles + 2 * len(stages)]
+    gradient, sums, est, old = refs[tiles + 2 * len(stages) :]
     look_rows = est.shape[1]
     total = tiles * epochs
     f32 = jnp.float32
@@ -500,40 +480,47 @@
             old[block * epochs + epoch] = fields[block][2, here, :].astype(f32)
             gradient[block * epochs + epoch] = jnp.zeros((look_rows, LANES), f32)
 
-    @pl.loop(0, total, unroll=2)
-    def _(epoch):
-        own_est = est[epoch]
-        own = jnp.zeros((look_rows, LANES), f32)
-        mates = [partner[epoch * SLOTS + slot] for slot in range(SLOTS)]
-        values = []
-        for slot, mate in enumerate(mates):
-            pair = epoch * SLOTS + slot
-            weighted = pulls[pair] - factors[pair] * (own_est - est[mate])
-            own = own + weighted
-            values.append(weighted)
-        for mate, weighted in zip(mates, values):
-            gradient[mate] = gradient[mate] - weighted
-        gradient[epoch] = gradient[epoch] + own
-
-    def totals(epoch, carry):
-        norm, crossed, grad_term, mixed_term, old_term = carry
-        own_grad = gradient[epoch]
-        own_old = old[epoch]
-        norm = norm + own_grad * own_grad
-        crossed = crossed + own_grad * own_old
-        for slot in range(SLOTS):
-            mate = partner[epoch * SLOTS + slot]
-            factor = factors[epoch * SLOTS + slot]
-            grad_spread = own_grad - gradient[mate]
-            old_spread = own_old - old[mate]
-            pulled = factor * grad_spread
-            grad_term = grad_term + pulled * grad_spread
-            mixed_term = mixed_term + pulled * old_spread
-            old_term = old_term + factor * old_spread * old_spread
-        return norm, crossed, grad_term, mixed_term, old_term
+    for stage, (first, own_total) in enumerate(stages):
+
+        @pl.loop(0, own_total, unroll=2)
+        def _(here):
+            epoch = lax.rem(first + here, total)
+            own_est = est[epoch]
+            own = jnp.zeros((look_rows, LANES), f32)
+            mates = [partner[epoch * SLOTS + slot] for slot in range(SLOTS)]
+            values = []
+            for slot, mate in enumerate(mates):
+                pair = here * SLOTS + slot
+                weighted = pulls[stage][pair] - factors[stage][pair] * (own_est - est[mate])
+                own = own + weighted
+                values.append(weighted)
+            for mate, weighted in zip(mates, values):
+                gradient[mate] = gradient[mate] - weighted
+            gradient[epoch] = gradient[epoch] + own
 
     zero = jnp.zeros((look_rows, LANES), f32)
-    results = lax.fori_loop(0, total, totals, (zero,) * 5, unroll=2)
+    results = (zero,) * 5
+    for stage, (first, own_total) in enumerate(stages):
+
+        def totals(here, carry):
+            norm, crossed, grad_term, mixed_term, old_term = carry
+            epoch = lax.rem(first + here, total)
+            own_grad = gradient[epoch]
+            own_old = old[epoch]
+            norm = norm + own_grad * own_grad
+            crossed = crossed + own_grad * own_old
+            for slot in range(SLOTS):
+                mate = partner[epoch * SLOTS + slot]
+                factor = factors[stage][here * SLOTS + slot]
+                grad_spread = own_grad - gradient[mate]
+                old_spread = own_old - old[mate]
+                pulled = factor * grad_spread
+                grad_term = grad_term + pulled * grad_spread
+                mixed_term = mixed_term + pulled * old_spread
+                old_term = old_term + factor * old_spread * old_spread
+            return norm, crossed, grad_term, mixed_term, old_term
+
+        results = lax.fori_loop(0, own_total, totals, results, unroll=2)
     sums[...] = jnp.zeros(sums.shape, f32)
     for at, value in enumerate(results):
         sums[at : at + 1, :] = jnp.sum(value, axis=0, keepdims=True)
@@ -639,7 +626,11 @@
         compiler_params=params_of,
         cost_estimate=pl.CostEstimate(flops=3_000_000, bytes_accessed=4_000_000, transcendentals=0),
     )(me.reshape(1), sub_present, slc, params, before, after)
-    block = [messages[0]] + [fetched(messages, shift) for shift in range(1, tiles)]
+    beside = [tiles - 1, 0, 1]
+    far = list(range(2, tiles - 1))
+    block = {0: messages[0], 1: fetched(messages, 1), tiles - 1: fetched(messages, tiles - 1)}
+    held = lax.optimization_barrier((messages, block[1], block[tiles - 1]))[0]
+    block.update({shift: fetched(held, shift) for shift in far})
 
     estimate, direction, _ = lax.optimization_barrier((estimate, direction, messages))
     fields = pl.pallas_call(
@@ -650,9 +641,6 @@
         compiler_params=params_of,
         cost_estimate=pl.CostEstimate(flops=1_000_000, bytes_accessed=2_000_000, transcendentals=0),
     )(me.reshape(1), estimate, direction)
-    late = lax.optimization_barrier((fields, block))[0]
-    field = [fields[0]] + [fetched(late, shift) for shift in range(1, tiles)]
-
     space = lax.axis_index("space")
     spaces = lax.axis_size("space")
     present = jnp.stack([space > 0, space < spaces - 1]).astype(f32)
@@ -679,57 +667,78 @@
         weight = listed[:, SLOTS : 2 * SLOTS] + listed[:, 2 * SLOTS : 3 * SLOTS] + listed[:, 3 * SLOTS :]
         return mate.reshape(-1), weight.reshape(-1)
 
-    top, bottom = halo([by_rows(shift) for shift in range(tiles)])
+    own_halo = halo([by_rows(0)])
+    near_halo = halo([by_rows(1), by_rows(tiles - 1)])
+    halos = {0: (own_halo, 0), 1: (near_halo, 0), tiles - 1: (near_halo, 1)}
+
+    def pair_stage(loaded):
+        own = loaded[:-1]
+        listed = jnp.concatenate([params_in(shift) for shift in own], axis=0)
+        mate = jnp.arange(len(own) * epochs, dtype=jnp.int32)[:, None] + listed[:, :SLOTS].astype(jnp.int32)
+        weight = listed[:, SLOTS : 2 * SLOTS] + listed[:, 2 * SLOTS : 3 * SLOTS] + listed[:, 3 * SLOTS :]
+        operands = []
+
+        def index_of(array):
+            for at, other in enumerate(operands):
+                if other is array:
+                    return at
+            operands.append(array)
+            return len(operands) - 1
+
+        places = []
+        for shift in loaded:
+            (top, bottom), slot = halos[shift]
+            place = index_of(block[shift]), index_of(top), index_of(bottom), slot * (2 * epochs + 1) * HALO
+            places.append(place)
+        here = len(loaded) * epochs
+        owned = len(own) * epochs
+        looks = (rows + 2 * HALO) // LOOK
+        group = 2 * SLOTS
+        batches = (len(loaded) + 1) // 2 * 2 + owned
+        shape = jax.ShapeDtypeStruct((owned * SLOTS, look_rows, LANES), f32)
+        return pl.pallas_call(
+            functools.partial(pair_kernel, (epochs, rows, len(operands)), tuple(places)),
+            out_shape=(shape, shape),
+            in_specs=[SMEM] * 3 + [VMEM] * len(operands),
+            out_specs=(VMEM, VMEM),
+            scratch_shapes=[
+                pltpu.VMEM((batches * group * look_rows, LANES), f32),
+                pltpu.VMEM((2 * here, LOOK, looks, LANES), f32),
+                pltpu.VMEM((2 * here, looks, LANES), f32),
+                pltpu.VMEM((batches * group * looks, LANES), f32),
+                pltpu.VMEM((batches * 2 * looks, LANES), f32),
+                pltpu.VMEM((batches * group * looks, LANES), f32),
+            ],
+            compiler_params=params_of,
+            cost_estimate=pl.CostEstimate(flops=20_000_000, bytes_accessed=30_000_000, transcendentals=0),
+        )(mate.reshape(-1), weight.reshape(-1), present, *operands)
+
+    near_stage = beside
+    far_stage = list(range(1, tiles))
+    near_pairs = pair_stage(near_stage)
+    held, fields, near_pairs = lax.optimization_barrier(([block[shift] for shift in far], fields, near_pairs))
+    block.update(zip(far, held))
+    far_halo = halo([by_rows(shift) for shift in far])
+    halos.update({shift: (far_halo, at) for at, shift in enumerate(far)})
+    field = [fields[0]] + [fetched(fields, shift) for shift in range(1, tiles)]
+    far_pairs = pair_stage(far_stage)
+
     listed = jnp.concatenate([params_in(shift) for shift in range(tiles)], axis=0)
     partner = jnp.arange(total, dtype=jnp.int32)[:, None] + listed[:, :SLOTS].astype(jnp.int32)
     partner = lax.rem(partner, total).reshape(-1)
-    weight = listed[:, SLOTS : 2 * SLOTS] + listed[:, 2 * SLOTS : 3 * SLOTS] + listed[:, 3 * SLOTS :]
-    weight = weight.reshape(-1)
-
-    group = 2 * SLOTS
-    batches = tiles + total
-
-    def scratch(looks):
-        return [
-            pltpu.VMEM((2 * total, LOOK, looks, LANES), f32),
-            pltpu.VMEM((2 * total, looks, LANES), f32),
-            pltpu.VMEM((batches * group * looks, LANES), f32),
-            pltpu.VMEM((batches * 2 * looks, LANES), f32),
-            pltpu.VMEM((batches * group * looks, LANES), f32),
-        ]
-
-    boxed_shape = (batches * group * look_rows, LANES)
-    inner = pl.pallas_call(
-        functools.partial(inner_kernel, (tiles, epochs, rows)),
-        out_shape=jax.ShapeDtypeStruct(boxed_shape, f32),
-        in_specs=[SMEM] + [VMEM] * tiles,
-        out_specs=VMEM,
-        scratch_shapes=scratch(look_rows),
-        compiler_params=params_of,
-        cost_estimate=pl.CostEstimate(flops=20_000_000, bytes_accessed=20_000_000, transcendentals=0),
-    )(partner, *block)
-    pair_shape = jax.ShapeDtypeStruct((total * SLOTS, look_rows, LANES), f32)
-    factors, pulls = pl.pallas_call(
-        functools.partial(border_kernel, (tiles, epochs, look_rows)),
-        out_shape=(pair_shape, pair_shape),
-        in_specs=[SMEM] * 3 + [VMEM] * 3,
-        out_specs=(VMEM, VMEM),
-        scratch_shapes=[pltpu.VMEM(boxed_shape, f32)] + scratch(2 * HALO // LOOK),
-        compiler_params=params_of,
-        cost_estimate=pl.CostEstimate(flops=20_000_000, bytes_accessed=15_000_000, transcendentals=0),
-    )(partner, weight, present, top, bottom, inner)
+    stages = tuple((stage[0] * epochs, (len(stage) - 1) * epochs) for stage in (near_stage, far_stage))
     gradient, sums = pl.pallas_call(
-        functools.partial(gradient_kernel, (tiles, epochs)),
+        functools.partial(gradient_kernel, (tiles, epochs, stages)),
         out_shape=(
             jax.ShapeDtypeStruct((total, look_rows, LANES), f32),
             jax.ShapeDtypeStruct((8, LANES), f32),
         ),
-        in_specs=[SMEM] + [VMEM] * (tiles + 2),
+        in_specs=[SMEM] + [VMEM] * (tiles + 4),
         out_specs=(VMEM, VMEM),
         scratch_shapes=[pltpu.VMEM((total, look_rows, LANES), f32)] * 2,
         compiler_params=params_of,
         cost_estimate=pl.CostEstimate(flops=10_000_000, bytes_accessed=8_000_000, transcendentals=0),
-    )(partner, *field, factors, pulls)
+    )(partner, *field, near_pairs[0], far_pairs[0], near_pairs[1], far_pairs[1])
 
     place = ("space", "sub")
     count = spaces * lax.axis_size("sub")
@@ -756,7 +765,7 @@
 
 def on_device(slc, offsets, weights, estimate, direction, prev_mean):
     epochs, rows, columns = slc.shape[1:]
-    fits = columns == LANES * lax.axis_size("epoch") and lax.axis_size("epoch") % 2 == 0
+    fits = columns == LANES * lax.axis_size("epoch") and lax.axis_size("epoch") > 3
     fits = fits and 2 * epochs * SIDES <= PARAM_LANE and rows % HALO == 0 and epochs == 2 * SLOTS
     plan = transposed_plan if fits else ring_plan
     return plan(slc, offsets, weights, estimate, direction, prev_mean)

time: 74 us -> 68.9 us (0.931)
  starting transfers between devices: 23.1 us -> 19.9 us
  waiting for transfers between devices: 23.4 us -> 21 us
    ppermute x9, starting transfers between devices: 20.2 us -> 14.4 us  [to_ahead(): return lax.ppermute(x, axis, [(i, (i + by) % size) for i in range(size)])]
    ppermute x9, waiting for transfers between devices: 20.5 us -> 15.6 us  [to_ahead(): return lax.ppermute(x, axis, [(i, (i + by) % size) for i in range(size)])]
    ppermute x1 -> x3, waiting for transfers between devices: 0.01 us -> 2.51 us  [halo(): lax.ppermute(border(jnp.where(space == 0, rows - HALO, 0)), 'space', [(0,...]
    ppermute x1 -> x3, starting transfers between devices: 1.56 us -> 3.86 us  [halo(): lax.ppermute(border(jnp.where(space == 0, rows - HALO, 0)), 'space', [(0,...]
    unnamed x10 -> x22, local copies, waits for them, and re-layouts: 2.74 us -> 2.77 us
  transfers between devices with their start and end apart: 14 -> 16, of which waited for: 6 -> 10; matrix products, arithmetic and copies ran while one was open for 3% -> 1% of each run, Pallas kernels for 24% -> 26%
where the time goes in v12:
time: 68.9 us; the launch traced here: 68.7 us
  Pallas kernels  22.4 us (33%)
  waiting for transfers between devices  21 us (30%)
  starting transfers between devices  19.9 us (29%)
  local copies, waits for them, and re-layouts  3.28 us (5%)
  between operations  1.48 us (2%)
  other arithmetic  0.71 us (1%)
    pallas_call x2, Pallas kernels, pair_stage(): pl.pallas_call(functools.partial(pair_kernel, (epochs, rows, len(operands...  18.1 us
    ppermute x9, waiting for transfers between devices, to_ahead(): return lax.ppermute(x, axis, [(i, (i + by) % size) for i in range(size)])  15.6 us
    ppermute x9, starting transfers between devices, to_ahead(): return lax.ppermute(x, axis, [(i, (i + by) % size) for i in range(size)])  14.4 us
    ppermute x3, starting transfers between devices, halo(): lax.ppermute(border(jnp.where(space == 0, rows - HALO, 0)), 'space', [(0,...  3.86 us
    ppermute x3, waiting for transfers between devices, transposed_plan(): lax.ppermute(sums, place, [(i, (i + by) % count) for i in range(count)])  2.87 us
    unnamed x22, local copies, waits for them, and re-layouts  2.77 us
    ppermute x3, waiting for transfers between devices, halo(): lax.ppermute(border(jnp.where(space == 0, rows - HALO, 0)), 'space', [(0,...  2.51 us
    pallas_call x1, Pallas kernels, transposed_plan(): pl.pallas_call(functools.partial(gradient_kernel, (tiles, epochs, stages)...  1.76 us
  transfers between devices with their start and end apart: 16, of which 10 were waited for; matrix products, arithmetic and copies ran while one was open for 1% of the time, Pallas kernels for 26%

profile of v12, /device:TPU:0, one launch (start us, length us, event | category | flops | bytes accessed | tf_op | source)
XLA Modules:
  0.0 68.7 jit_solution(7256920634574802066)
XLA Ops:
  0.6 1.2 %copy-done = bf16[2,8,64,512]{3,2,1,0:T(8,128)(2,1)S(1)} copy-done((bf16[2,8,64,512]{3,2,1,0:T(8,128)(2,1)S(1)}, bf16[2,8,64,512]{3,2,1,0:T(8,128)(2,1)}, u32[]{:S(2)}) %copy-start) | copy-done | bytes 1048600
  1.9 0.2 shard_map.77
  2.1 0.5 collective-permute-start
  2.6 0.7 copy-done.8
  3.3 0.1 copy.12
  3.4 0.7 copy-done.9
  4.1 0.1 copy.13
  4.1 0.1 add_convert_fusion.1.present
  4.2 0.1 select_maximum_fusion.params
  4.3 0.1 add_convert_fusion.present
  4.4 1.3 %shard_map.78 = (bf16[1088,128]{1,0:T(8,128)(2,1)S(1)}, bf16[1088,128]{1,0:T(8,128)(2,1)S(1)}, bf16[1088,128]{1,0:T(8,128)(2,1)S(1)}, bf16[1088,128]{1,0:T(8,128)(2,1)S(1)}) custom-call(s32[1]{0:T(128)} %bitcast.me, f32[2]{0:T(128)S(1)} %add_convert_fusion.present, bf16[2,8,64,512]{3,2,1,0:T(8,128)(2,1)S(1)} %copy-done.1, ...), custom_call_target="tpu_custom_call" | custom-call | flops 3000000 | bytes 4000000 | tf_op jit(solution)/shard_map/pallas_call | solution.py:620
  5.7 2.7 %collective-permute-start.2 = (bf16[1088,128]{1,0:T(8,128)(2,1)S(1)}, bf16[1088,128]{1,0:T(8,128)(2,1)S(1)}, u32[]{:S(2)}, u32[]{:S(2)}) collective-permute-start(bf16[1088,128]{1,0:T(8,128)(2,1)S(1)} %get-tuple-element.31), channel_id=1, source_target_pairs={{0,4},{4,8},{8,12},{12,0},{1,5},{5,9},{9,13},{13,1},{2,6},{6,10},{... | collective-permute-start | bytes 835592 | tf_op jit(solution)/shard_map/ppermute | solution.py:584
  8.3 2.1 %collective-permute-start.1 = (bf16[1088,128]{1,0:T(8,128)(2,1)S(1)}, bf16[1088,128]{1,0:T(8,128)(2,1)S(1)}, u32[]{:S(2)}, u32[]{:S(2)}) collective-permute-start(bf16[1088,128]{1,0:T(8,128)(2,1)S(1)} %get-tuple-element.33), channel_id=1, source_target_pairs={{0,12},{4,0},{8,4},{12,8},{1,13},{5,1},{9,5},{13,9},{2,14},{6,2},{... | collective-permute-start | bytes 835592 | tf_op jit(solution)/shard_map/ppermute | solution.py:584
  10.4 1.7 %collective-permute-start.5 = (bf16[272,128]{1,0:T(8,128)(2,1)S(1)}, bf16[272,128]{1,0:T(8,128)(2,1)S(1)}, u32[]{:S(2)}, u32[]{:S(2)}) collective-permute-start(bf16[272,128]{1,0:T(8,128)(2,1)S(1)} %bitcast.19), channel_id=1, source_target_pairs={{0,2},{2,0},{1,3},{3,1},{4,6},{6,4},{5,7},{7,5},{8,10},{10,8},{9,1... | collective-permute-start | bytes 208904 | tf_op jit(solution)/shard_map/ppermute | solution.py:654
  12.1 0.1 shard_map.79
  12.2 0.1 slice_convert_fusion.3
  12.3 5.6 %collective-permute-done.2.refs_0_.refs_4_ = bf16[1088,128]{1,0:T(8,128)(2,1)S(1)} collective-permute-done((bf16[1088,128]{1,0:T(8,128)(2,1)S(1)}, bf16[1088,128]{1,0:T(8,128)(2,1)S(1)}, u32[]{:S(2)}, u32[]{:S(2)}) %collective-permute-start.2) | collective-permute-done | bytes 278560 | tf_op jit(solution)/shard_map/ppermute | solution.py:584
  17.9 5.1 %collective-permute-done.1.refs_4_.refs_0_ = bf16[1088,128]{1,0:T(8,128)(2,1)S(1)} collective-permute-done((bf16[1088,128]{1,0:T(8,128)(2,1)S(1)}, bf16[1088,128]{1,0:T(8,128)(2,1)S(1)}, u32[]{:S(2)}, u32[]{:S(2)}) %collective-permute-start.1) | collective-permute-done | bytes 278560 | tf_op jit(solution)/shard_map/ppermute | solution.py:584
  23.1 1.6 %collective-permute-start.4 = (bf16[544,128]{1,0:T(8,128)(2,1)S(1)}, bf16[544,128]{1,0:T(8,128)(2,1)S(1)}, u32[]{:S(2)}, u32[]{:S(2)}) collective-permute-start(bf16[544,128]{1,0:T(8,128)(2,1)S(1)} %pad_maximum_fusion), channel_id=1, source_target_pairs={{0,2},{2,0},{1,3},{3,1},{4,6},{6,4},{5,7},{7,5},{8,10},{10,8},{9,1... | collective-permute-start | bytes 417800 | tf_op jit(solution)/shard_map/ppermute | solution.py:654
  24.7 1.3 %collective-permute-start.3 = (bf16[1088,128]{1,0:T(8,128)(2,1)S(1)}, bf16[1088,128]{1,0:T(8,128)(2,1)S(1)}, u32[]{:S(2)}, u32[]{:S(2)}) collective-permute-start(bf16[1088,128]{1,0:T(8,128)(2,1)S(1)} %get-tuple-element.36), channel_id=1, source_target_pairs={{0,8},{4,12},{8,0},{12,4},{1,9},{5,13},{9,1},{13,5},{2,10},{6,14},... | collective-permute-start | bytes 835592 | tf_op jit(solution)/shard_map/ppermute | solution.py:584
  26.0 0.1 slice_convert_fusion
  26.2 0.1 reshape.49.partner
  26.2 0.1 fusion.14
  26.3 0.1 reshape.50.weight
  26.4 1.8 %collective-permute-done.4.refs_1_ = bf16[544,128]{1,0:T(8,128)(2,1)S(1)} collective-permute-done((bf16[544,128]{1,0:T(8,128)(2,1)S(1)}, bf16[544,128]{1,0:T(8,128)(2,1)S(1)}, u32[]{:S(2)}, u32[]{:S(2)}) %collective-permute-start.4) | collective-permute-done | bytes 139296 | tf_op jit(solution)/shard_map/ppermute | solution.py:654
  28.2 9.0 %shard_map.80 = (f32[64,16,128]{2,1,0:T(8,128)S(1)}, f32[64,16,128]{2,1,0:T(8,128)S(1)}) custom-call(s32[64]{0:T(128)S(1)} %reshape.49.partner, f32[64]{0:T(128)S(1)} %reshape.50.weight, f32[2]{0:T(128)S(1)} %add_convert_fusion.1.present, bf16[1088,128]{1,0:T(8,128)(2,1)S(1)} %collective-permute-done.2.refs_0_.refs_4_, ...), custom_call_target="tpu_custom_call" | custom-call | flops 20000000 | bytes 30000000 | tf_op jit(solution)/shard_map/pallas_call | solution.py:699
  37.3 2.0 %collective-permute-done.3.refs_2_ = bf16[1088,128]{1,0:T(8,128)(2,1)S(1)} collective-permute-done((bf16[1088,128]{1,0:T(8,128)(2,1)S(1)}, bf16[1088,128]{1,0:T(8,128)(2,1)S(1)}, u32[]{:S(2)}, u32[]{:S(2)}) %collective-permute-start.3) | collective-permute-done | bytes 278560 | tf_op jit(solution)/shard_map/ppermute | solution.py:584
  39.4 0.1 fusion.7
  39.5 0.1 reshape.57.partner
  39.6 0.1 reshape.59.weight
  39.7 0.6 collective-permute-start.9
  40.3 2.3 %collective-permute-start.6 = (bf16[3,128,128]{2,1,0:T(8,128)(2,1)S(1)}, bf16[3,128,128]{2,1,0:T(8,128)(2,1)S(1)}, u32[]{:S(2)}, u32[]{:S(2)}) collective-permute-start(bf16[3,128,128]{2,1,0:T(8,128)(2,1)S(1)} %copy-done.7), channel_id=1, source_target_pairs={{0,12},{4,0},{8,4},{12,8},{1,13},{5,1},{9,5},{13,9},{2,14},{6,2},{... | collective-permute-start | bytes 294920 | tf_op jit(solution)/shard_map/ppermute | solution.py:584
  42.7 0.6 collective-permute-start.8
  43.3 0.1 reshape.58.partner
  43.4 0.7 %collective-permute-done.9.refs_3_ = bf16[272,128]{1,0:T(8,128)(2,1)S(1)} collective-permute-done((bf16[272,128]{1,0:T(8,128)(2,1)S(1)}, bf16[272,128]{1,0:T(8,128)(2,1)S(1)}, u32[]{:S(2)}, u32[]{:S(2)}) %collective-permute-start.9) | collective-permute-done | bytes 69664 | tf_op jit(solution)/shard_map/ppermute | solution.py:654
  44.1 9.0 %shard_map.81 = (f32[64,16,128]{2,1,0:T(8,128)S(1)}, f32[64,16,128]{2,1,0:T(8,128)S(1)}) custom-call(s32[64]{0:T(128)S(1)} %reshape.58.partner, f32[64]{0:T(128)S(1)} %reshape.59.weight, f32[2]{0:T(128)S(1)} %add_convert_fusion.1.present, bf16[1088,128]{1,0:T(8,128)(2,1)S(1)} %collective-permute-done.1.refs_4_.refs_0_, ...), custom_call_target="tpu_custom_call" | custom-call | flops 20000000 | bytes 30000000 | tf_op jit(solution)/shard_map/pallas_call | solution.py:699
  53.2 1.8 %shard_map.82 = (f32[32,16,128]{2,1,0:T(8,128)S(1)}, f32[8,128]{1,0:T(8,128)S(1)}) custom-call(s32[128]{0:T(128)S(1)} %reshape.57.partner, bf16[3,128,128]{2,1,0:T(8,128)(2,1)S(1)} %get-tuple-element.44.refs_0_, bf16[3,128,128]{2,1,0:T(8,128)(2,1)S(1)} %collective-permute-done.6.refs_1_, bf16[3,128,128]{2,1,0:T(8,128)(2,1)S(1)} %collective-permute-done.7.refs_2_, ...), custom_call_target="tpu_custom_call" | custom-call | flops 10000000 | bytes 8000000 | tf_op jit(solution)/shard_map/pallas_call | solution.py:730
  55.0 0.9 %collective-permute-start.11 = (f32[8,128]{1,0:T(8,128)S(1)}, f32[8,128]{1,0:T(8,128)S(1)}, u32[]{:S(2)}, u32[]{:S(2)}) collective-permute-start(f32[8,128]{1,0:T(8,128)S(1)} %get-tuple-element.53.refs_0_), channel_id=1, source_target_pairs={{0,2},{1,3},{2,0},{3,1},{4,6},{5,7},{6,4},{7,5},{8,10},{9,11},{10,... | collective-permute-start | bytes 12296 | tf_op jit(solution)/shard_map/ppermute | solution.py:745
  55.9 0.2 collective-permute-start.10
  56.0 0.3 collective-permute-done.12.refs_3_
  56.3 2.4 %collective-permute-done.11.refs_2_ = f32[8,128]{1,0:T(8,128)S(1)} collective-permute-done((f32[8,128]{1,0:T(8,128)S(1)}, f32[8,128]{1,0:T(8,128)S(1)}, u32[]{:S(2)}, u32[]{:S(2)}) %collective-permute-start.11) | collective-permute-done | bytes 4128 | tf_op jit(solution)/shard_map/ppermute | solution.py:745
  58.7 0.2 collective-permute-done.10.refs_1_
  58.9 2.9 %collective-permute-start.13 = (f32[136,128]{1,0:T(8,128)S(1)}, f32[136,128]{1,0:T(8,128)S(1)}, u32[]{:S(2)}, u32[]{:S(2)}) collective-permute-start(f32[136,128]{1,0:T(8,128)S(1)} %get-tuple-element.55), channel_id=1, source_target_pairs={{0,4},{4,8},{8,12},{12,0},{1,5},{5,9},{9,13},{13,1},{2,6},{6,10},{... | collective-permute-start | bytes 208904 | tf_op jit(solution)/shard_map/ppermute | solution.py:584
  61.8 0.9 %collective-permute-start.14 = (f32[136,128]{1,0:T(8,128)S(1)}, f32[136,128]{1,0:T(8,128)S(1)}, u32[]{:S(2)}, u32[]{:S(2)}) collective-permute-start(f32[136,128]{1,0:T(8,128)S(1)} %get-tuple-element.56), channel_id=1, source_target_pairs={{0,8},{4,12},{8,0},{12,4},{1,9},{5,13},{9,1},{13,5},{2,10},{6,14},... | collective-permute-start | bytes 208904 | tf_op jit(solution)/shard_map/ppermute | solution.py:584
  62.7 1.5 %collective-permute-start.15 = (f32[136,128]{1,0:T(8,128)S(1)}, f32[136,128]{1,0:T(8,128)S(1)}, u32[]{:S(2)}, u32[]{:S(2)}) collective-permute-start(f32[136,128]{1,0:T(8,128)S(1)} %get-tuple-element.57), channel_id=1, source_target_pairs={{0,12},{4,0},{8,4},{12,8},{1,13},{5,1},{9,5},{13,9},{2,14},{6,2},{... | collective-permute-start | bytes 208904 | tf_op jit(solution)/shard_map/ppermute | solution.py:584
  64.9 0.6 collective-permute-done.13.refs_1_
  65.5 2.3 %collective-permute-done.14.refs_2_ = f32[136,128]{1,0:T(8,128)S(1)} collective-permute-done((f32[136,128]{1,0:T(8,128)S(1)}, f32[136,128]{1,0:T(8,128)S(1)}, u32[]{:S(2)}, u32[]{:S(2)}) %collective-permute-start.14) | collective-permute-done | bytes 69664 | tf_op jit(solution)/shard_map/ppermute | solution.py:584
  67.8 0.9 %shard_map.84 = (f32[8,16,512]{2,1,0:T(8,128)}, f32[8,16,512]{2,1,0:T(8,128)}) custom-call(s32[1]{0:T(128)} %bitcast.me, f32[1]{0:T(128)S(6)} %copy.16.prev_mean, f32[8,16,512]{2,1,0:T(8,128)S(1)} %copy-done.2, f32[8,16,512]{2,1,0:T(8,128)S(1)} %copy-done.3, f32[136,128]{1,0:T(8,128)S(1)} %get-tuple-element.54.refs_0_, ...), custom_call_target="tpu_custom_call" | custom-call | flops 1000000 | bytes 2000000 | tf_op jit(solution)/shard_map/pallas_call | solution.py:756
  (37 shorter events, 0.4 us)
Async XLA Ops:
  0.6 1.2 %copy-start = (bf16[2,8,64,512]{3,2,1,0:T(8,128)(2,1)S(1)}, bf16[2,8,64,512]{3,2,1,0:T(8,128)(2,1)}, u32[]{:S(2)}) copy-start(bf16[2,8,64,512]{3,2,1,0:T(8,128)(2,1)} %slc.1) | copy-start | bytes 3145732
  1.9 2.5 %copy-start.1 = (bf16[2,8,64,512]{3,2,1,0:T(8,128)(2,1)S(1)}, bf16[2,8,64,512]{3,2,1,0:T(8,128)(2,1)}, u32[]{:S(2)}) copy-start(bf16[2,8,64,512]{3,2,1,0:T(8,128)(2,1)} %slc.1) | copy-start | bytes 3145732
  2.1 2.3 %collective-permute-start = (bf16[64,128]{1,0:T(8,128)(2,1)S(1)}, bf16[64,128]{1,0:T(8,128)(2,1)S(1)}, u32[]{:S(2)}, u32[]{:S(2)}) collective-permute-start(bf16[64,128]{1,0:T(8,128)(2,1)S(1)} %shard_map.77), channel_id=1, source_target_pairs={{0,1},{1,0},{2,3},{3,2},{4,5},{5,4},{6,7},{7,6},{8,9},{9,8},{10,11... | collective-permute-start | bytes 49160 | tf_op jit(solution)/shard_map/ppermute | solution.py:575
  2.6 0.7 copy-start.8
  3.4 0.7 copy-start.9
  4.4 7.8 %copy-start.2 = (f32[8,16,512]{2,1,0:T(8,128)S(1)}, f32[8,16,512]{2,1,0:T(8,128)}, u32[]{:S(2)}) copy-start(f32[8,16,512]{2,1,0:T(8,128)} %estimate.1) | copy-start | bytes 786436
  4.4 7.8 %copy-start.3 = (f32[8,16,512]{2,1,0:T(8,128)S(1)}, f32[8,16,512]{2,1,0:T(8,128)}, u32[]{:S(2)}) copy-start(f32[8,16,512]{2,1,0:T(8,128)} %direction.1) | copy-start | bytes 786436
  5.7 12.2 %collective-permute-start.2 = (bf16[1088,128]{1,0:T(8,128)(2,1)S(1)}, bf16[1088,128]{1,0:T(8,128)(2,1)S(1)}, u32[]{:S(2)}, u32[]{:S(2)}) collective-permute-start(bf16[1088,128]{1,0:T(8,128)(2,1)S(1)} %get-tuple-element.31), channel_id=1, source_target_pairs={{0,4},{4,8},{8,12},{12,0},{1,5},{5,9},{9,13},{13,1},{2,6},{6,10},{... | collective-permute-start | bytes 835592 | tf_op jit(solution)/shard_map/ppermute | solution.py:584
  8.3 14.7 %collective-permute-start.1 = (bf16[1088,128]{1,0:T(8,128)(2,1)S(1)}, bf16[1088,128]{1,0:T(8,128)(2,1)S(1)}, u32[]{:S(2)}, u32[]{:S(2)}) collective-permute-start(bf16[1088,128]{1,0:T(8,128)(2,1)S(1)} %get-tuple-element.33), channel_id=1, source_target_pairs={{0,12},{4,0},{8,4},{12,8},{1,13},{5,1},{9,5},{13,9},{2,14},{6,2},{... | collective-permute-start | bytes 835592 | tf_op jit(solution)/shard_map/ppermute | solution.py:584
  10.4 16.0 %collective-permute-start.5 = (bf16[272,128]{1,0:T(8,128)(2,1)S(1)}, bf16[272,128]{1,0:T(8,128)(2,1)S(1)}, u32[]{:S(2)}, u32[]{:S(2)}) collective-permute-start(bf16[272,128]{1,0:T(8,128)(2,1)S(1)} %bitcast.19), channel_id=1, source_target_pairs={{0,2},{2,0},{1,3},{3,1},{4,6},{6,4},{5,7},{7,5},{8,10},{10,8},{9,1... | collective-permute-start | bytes 208904 | tf_op jit(solution)/shard_map/ppermute | solution.py:654
  12.2 10.9 %copy-start.4 = (bf16[3,128,128]{2,1,0:T(8,128)(2,1)}, bf16[3,128,128]{2,1,0:T(8,128)(2,1)S(1)}, u32[]{:S(2)}) copy-start(bf16[3,128,128]{2,1,0:T(8,128)(2,1)S(1)} %get-tuple-element.46) | copy-start | bytes 294916
  12.2 10.9 %copy-start.6 = (bf16[3,128,128]{2,1,0:T(8,128)(2,1)}, bf16[3,128,128]{2,1,0:T(8,128)(2,1)S(1)}, u32[]{:S(2)}) copy-start(bf16[3,128,128]{2,1,0:T(8,128)(2,1)S(1)} %get-tuple-element.45) | copy-start | bytes 294916
  23.1 5.1 %collective-permute-start.4 = (bf16[544,128]{1,0:T(8,128)(2,1)S(1)}, bf16[544,128]{1,0:T(8,128)(2,1)S(1)}, u32[]{:S(2)}, u32[]{:S(2)}) collective-permute-start(bf16[544,128]{1,0:T(8,128)(2,1)S(1)} %pad_maximum_fusion), channel_id=1, source_target_pairs={{0,2},{2,0},{1,3},{3,1},{4,6},{6,4},{5,7},{7,5},{8,10},{10,8},{9,1... | collective-permute-start | bytes 417800 | tf_op jit(solution)/shard_map/ppermute | solution.py:654
  24.7 14.6 %collective-permute-start.3 = (bf16[1088,128]{1,0:T(8,128)(2,1)S(1)}, bf16[1088,128]{1,0:T(8,128)(2,1)S(1)}, u32[]{:S(2)}, u32[]{:S(2)}) collective-permute-start(bf16[1088,128]{1,0:T(8,128)(2,1)S(1)} %get-tuple-element.36), channel_id=1, source_target_pairs={{0,8},{4,12},{8,0},{12,4},{1,9},{5,13},{9,1},{13,5},{2,10},{6,14},... | collective-permute-start | bytes 835592 | tf_op jit(solution)/shard_map/ppermute | solution.py:584
  39.4 0.9 %copy-start.7 = (bf16[3,128,128]{2,1,0:T(8,128)(2,1)S(1)}, bf16[3,128,128]{2,1,0:T(8,128)(2,1)}, u32[]{:S(2)}) copy-start(bf16[3,128,128]{2,1,0:T(8,128)(2,1)} %copy-done.6) | copy-start | bytes 294916
  39.4 3.3 %copy-start.5 = (bf16[3,128,128]{2,1,0:T(8,128)(2,1)S(1)}, bf16[3,128,128]{2,1,0:T(8,128)(2,1)}, u32[]{:S(2)}) copy-start(bf16[3,128,128]{2,1,0:T(8,128)(2,1)} %copy-done.4) | copy-start | bytes 294916
  39.7 4.4 %collective-permute-start.9 = (bf16[272,128]{1,0:T(8,128)(2,1)S(1)}, bf16[272,128]{1,0:T(8,128)(2,1)S(1)}, u32[]{:S(2)}, u32[]{:S(2)}) collective-permute-start(bf16[272,128]{1,0:T(8,128)(2,1)S(1)} %bitcast.20), channel_id=1, source_target_pairs={{0,2},{2,0},{1,3},{3,1},{4,6},{6,4},{5,7},{7,5},{8,10},{10,8},{9,1... | collective-permute-start | bytes 208904 | tf_op jit(solution)/shard_map/ppermute | solution.py:654
  40.3 12.8 %collective-permute-start.6 = (bf16[3,128,128]{2,1,0:T(8,128)(2,1)S(1)}, bf16[3,128,128]{2,1,0:T(8,128)(2,1)S(1)}, u32[]{:S(2)}, u32[]{:S(2)}) collective-permute-start(bf16[3,128,128]{2,1,0:T(8,128)(2,1)S(1)} %copy-done.7), channel_id=1, source_target_pairs={{0,12},{4,0},{8,4},{12,8},{1,13},{5,1},{9,5},{13,9},{2,14},{6,2},{... | collective-permute-start | bytes 294920 | tf_op jit(solution)/shard_map/ppermute | solution.py:584
  42.6 10.5 %collective-permute-start.7 = (bf16[3,128,128]{2,1,0:T(8,128)(2,1)S(1)}, bf16[3,128,128]{2,1,0:T(8,128)(2,1)S(1)}, u32[]{:S(2)}, u32[]{:S(2)}) collective-permute-start(bf16[3,128,128]{2,1,0:T(8,128)(2,1)S(1)} %copy-done.5), channel_id=1, source_target_pairs={{0,8},{4,12},{8,0},{12,4},{1,9},{5,13},{9,1},{13,5},{2,10},{6,14},... | collective-permute-start | bytes 294920 | tf_op jit(solution)/shard_map/ppermute | solution.py:584
  42.7 10.5 %collective-permute-start.8 = (bf16[3,128,128]{2,1,0:T(8,128)(2,1)S(1)}, bf16[3,128,128]{2,1,0:T(8,128)(2,1)S(1)}, u32[]{:S(2)}, u32[]{:S(2)}) collective-permute-start(bf16[3,128,128]{2,1,0:T(8,128)(2,1)S(1)} %get-tuple-element.47), channel_id=1, source_target_pairs={{0,4},{4,8},{8,12},{12,0},{1,5},{5,9},{9,13},{13,1},{2,6},{6,10},{... | collective-permute-start | bytes 294920 | tf_op jit(solution)/shard_map/ppermute | solution.py:584
  54.9 1.4 %collective-permute-start.12 = (f32[8,128]{1,0:T(8,128)S(1)}, f32[8,128]{1,0:T(8,128)S(1)}, u32[]{:S(2)}, u32[]{:S(2)}) collective-permute-start(f32[8,128]{1,0:T(8,128)S(1)} %get-tuple-element.53.refs_0_), channel_id=1, source_target_pairs={{0,3},{1,0},{2,1},{3,2},{4,7},{5,4},{6,5},{7,6},{8,11},{9,8},{10,9... | collective-permute-start | bytes 12296 | tf_op jit(solution)/shard_map/ppermute | solution.py:745
  55.0 3.7 %collective-permute-start.11 = (f32[8,128]{1,0:T(8,128)S(1)}, f32[8,128]{1,0:T(8,128)S(1)}, u32[]{:S(2)}, u32[]{:S(2)}) collective-permute-start(f32[8,128]{1,0:T(8,128)S(1)} %get-tuple-element.53.refs_0_), channel_id=1, source_target_pairs={{0,2},{1,3},{2,0},{3,1},{4,6},{5,7},{6,4},{7,5},{8,10},{9,11},{10,... | collective-permute-start | bytes 12296 | tf_op jit(solution)/shard_map/ppermute | solution.py:745
  55.9 3.0 %collective-permute-start.10 = (f32[8,128]{1,0:T(8,128)S(1)}, f32[8,128]{1,0:T(8,128)S(1)}, u32[]{:S(2)}, u32[]{:S(2)}) collective-permute-start(f32[8,128]{1,0:T(8,128)S(1)} %get-tuple-element.53.refs_0_), channel_id=1, source_target_pairs={{0,1},{1,2},{2,3},{3,0},{4,5},{5,6},{6,7},{7,4},{8,9},{9,10},{10,1... | collective-permute-start | bytes 12296 | tf_op jit(solution)/shard_map/ppermute | solution.py:745
  58.9 6.6 %collective-permute-start.13 = (f32[136,128]{1,0:T(8,128)S(1)}, f32[136,128]{1,0:T(8,128)S(1)}, u32[]{:S(2)}, u32[]{:S(2)}) collective-permute-start(f32[136,128]{1,0:T(8,128)S(1)} %get-tuple-element.55), channel_id=1, source_target_pairs={{0,4},{4,8},{8,12},{12,0},{1,5},{5,9},{9,13},{13,1},{2,6},{6,10},{... | collective-permute-start | bytes 208904 | tf_op jit(solution)/shard_map/ppermute | solution.py:584
  61.8 6.0 %collective-permute-start.14 = (f32[136,128]{1,0:T(8,128)S(1)}, f32[136,128]{1,0:T(8,128)S(1)}, u32[]{:S(2)}, u32[]{:S(2)}) collective-permute-start(f32[136,128]{1,0:T(8,128)S(1)} %get-tuple-element.56), channel_id=1, source_target_pairs={{0,8},{4,12},{8,0},{12,4},{1,9},{5,13},{9,1},{13,5},{2,10},{6,14},... | collective-permute-start | bytes 208904 | tf_op jit(solution)/shard_map/ppermute | solution.py:584
  62.7 5.1 %collective-permute-start.15 = (f32[136,128]{1,0:T(8,128)S(1)}, f32[136,128]{1,0:T(8,128)S(1)}, u32[]{:S(2)}, u32[]{:S(2)}) collective-permute-start(f32[136,128]{1,0:T(8,128)S(1)} %get-tuple-element.57), channel_id=1, source_target_pairs={{0,12},{4,0},{8,4},{12,8},{1,13},{5,1},{9,5},{13,9},{2,14},{6,2},{... | collective-permute-start | bytes 208904 | tf_op jit(solution)/shard_map/ppermute | solution.py:584

commit v13 on v12

--- a/solution.py
+++ b/solution.py
@@ -224,11 +224,11 @@
                 message[2 * epochs * rows :, :] = strips[tile]
 
 
-def look_order(from_rows, keep):
+def look_order(from_rows, first, keep):
     looks = from_rows // LOOK
     to = lax.broadcasted_iota(jnp.int32, (from_rows, from_rows), 0)
     at = lax.broadcasted_iota(jnp.int32, (from_rows, from_rows), 1)
-    order = (at == to % looks * LOOK + to // looks).astype(jnp.float32)
+    order = (at == (to + first) % looks * LOOK + to // looks).astype(jnp.float32)
     return (order * keep(at)).astype(jnp.bfloat16)
 
 
@@ -279,15 +279,6 @@
 
     band = band_of((2 * LANES, LANES), lambda at, to: at % LANES, lambda at, to: to)
     return band, band_of((2 * LANES, LANES), rim_from, rim_to)
-
-
-def row_sums(look_rows, looks, look_of):
-    group = 2 * SLOTS
-    out_at = lax.broadcasted_iota(jnp.int32, (group * look_rows, group * looks), 0)
-    in_at = lax.broadcasted_iota(jnp.int32, (group * look_rows, group * looks), 1)
-    near = jnp.abs(look_of(in_at % looks) - out_at % look_rows) <= RADIUS
-    near = near & (in_at // looks == out_at // look_rows)
-    return near.astype(jnp.float32).astype(jnp.bfloat16)
 
 
 def mixed(values):
@@ -371,12 +362,12 @@
     return results
 
 
-def rows_summed(batch, looks, sum_rows, wide):
-    rows = 2 * SLOTS * looks
-    at = pl.ds(pl.multiple_of(batch * rows, rows), rows)
-    halves = jnp.concatenate(split_two(wide[at, :]), axis=1)
-    value = jnp.dot(sum_rows, halves, preferred_element_type=jnp.float32)
-    return value[:, :LANES] + value[:, LANES:]
+def rows_summed(channel, looks, look_rows, wide):
+    first = channel * looks
+    total = wide[pl.ds(first, look_rows), :]
+    for shift in range(1, 2 * RADIUS + 1):
+        total = total + wide[pl.ds(first + shift, look_rows), :]
+    return total
 
 
 def pair_couple(couple, total, partner, main, rim):
@@ -410,9 +401,8 @@
     def keep(at):
         return jnp.where(at < HALO, present[0], jnp.where(at >= HALO + rows, present[1], 1.0))
 
-    order = look_order(full_rows, keep)
+    order = look_order(full_rows, halo_looks - RADIUS, keep)
     bands = column_bands()
-    sum_rows = row_sums(look_rows, looks, lambda at: at - halo_looks)
     for block, (tile_at, top_at, bottom_at, halo_row) in enumerate(places):
         tile, top, bottom = inputs[tile_at], inputs[top_at], inputs[bottom_at]
 
@@ -449,7 +439,7 @@
                 factor = weight[pair] * (unit_re * unit_re + unit_im * unit_im)
                 results.append((factor, factor * unit_im))
         summed = clipped(turn - 1, last)
-        sums = [rows_summed(summed * 2 + one, looks, sum_rows, wide) for one in range(2)]
+        sums = [rows_summed(summed * 2 * group + one, looks, look_rows, wide) for one in range(2 * group)]
         couple = clipped(turn, last)
         columns = columns_summed(couple, looks, bands, looked, rim_looked)
         here = clipped(turn, own_total // 2 - 1)

time: 68.9 us -> 68.6 us (level)
  Pallas kernels: 22.4 us -> 21.7 us
where the time goes in v13:
time: 68.6 us; the launch traced here: 68.4 us
  Pallas kernels  21.7 us (32%)
  waiting for transfers between devices  21.3 us (31%)
  starting transfers between devices  19.9 us (29%)
  local copies, waits for them, and re-layouts  3.28 us (5%)
  between operations  1.48 us (2%)
  other arithmetic  0.71 us (1%)
    pallas_call x2, Pallas kernels, pair_stage(): pl.pallas_call(functools.partial(pair_kernel, (epochs, rows, len(operands...  17.4 us
    ppermute x9, waiting for transfers between devices, to_ahead(): return lax.ppermute(x, axis, [(i, (i + by) % size) for i in range(size)])  16 us
    ppermute x9, starting transfers between devices, to_ahead(): return lax.ppermute(x, axis, [(i, (i + by) % size) for i in range(size)])  14.4 us
    ppermute x3, starting transfers between devices, halo(): lax.ppermute(border(jnp.where(space == 0, rows - HALO, 0)), 'space', [(0,...  3.86 us
    ppermute x3, waiting for transfers between devices, transposed_plan(): lax.ppermute(sums, place, [(i, (i + by) % count) for i in range(count)])  2.87 us
    unnamed x22, local copies, waits for them, and re-layouts  2.77 us
    ppermute x3, waiting for transfers between devices, halo(): lax.ppermute(border(jnp.where(space == 0, rows - HALO, 0)), 'space', [(0,...  2.51 us
    pallas_call x1, Pallas kernels, transposed_plan(): pl.pallas_call(functools.partial(gradient_kernel, (tiles, epochs, stages)...  1.76 us
  transfers between devices with their start and end apart: 16, of which 10 were waited for; matrix products, arithmetic and copies ran while one was open for 1% of the time, Pallas kernels for 26%

profile of v13, /device:TPU:0, one launch (start us, length us, event | category | flops | bytes accessed | tf_op | source)
XLA Modules:
  0.0 68.4 jit_solution(2108784772886174577)
XLA Ops:
  0.6 1.2 %copy-done = bf16[2,8,64,512]{3,2,1,0:T(8,128)(2,1)S(1)} copy-done((bf16[2,8,64,512]{3,2,1,0:T(8,128)(2,1)S(1)}, bf16[2,8,64,512]{3,2,1,0:T(8,128)(2,1)}, u32[]{:S(2)}) %copy-start) | copy-done | bytes 1048600
  1.9 0.2 shard_map.77
  2.1 0.5 collective-permute-start
  2.6 0.7 copy-done.8
  3.3 0.1 copy.12
  3.4 0.7 copy-done.9
  4.1 0.1 copy.13
  4.1 0.1 add_convert_fusion.1.present
  4.2 0.1 select_maximum_fusion.params
  4.3 0.1 add_convert_fusion.present
  4.4 1.3 %shard_map.78 = (bf16[1088,128]{1,0:T(8,128)(2,1)S(1)}, bf16[1088,128]{1,0:T(8,128)(2,1)S(1)}, bf16[1088,128]{1,0:T(8,128)(2,1)S(1)}, bf16[1088,128]{1,0:T(8,128)(2,1)S(1)}) custom-call(s32[1]{0:T(128)} %bitcast.me, f32[2]{0:T(128)S(1)} %add_convert_fusion.present, bf16[2,8,64,512]{3,2,1,0:T(8,128)(2,1)S(1)} %copy-done.1, ...), custom_call_target="tpu_custom_call" | custom-call | flops 3000000 | bytes 4000000 | tf_op jit(solution)/shard_map/pallas_call | solution.py:610
  5.7 2.7 %collective-permute-start.2 = (bf16[1088,128]{1,0:T(8,128)(2,1)S(1)}, bf16[1088,128]{1,0:T(8,128)(2,1)S(1)}, u32[]{:S(2)}, u32[]{:S(2)}) collective-permute-start(bf16[1088,128]{1,0:T(8,128)(2,1)S(1)} %get-tuple-element.31), channel_id=1, source_target_pairs={{0,4},{4,8},{8,12},{12,0},{1,5},{5,9},{9,13},{13,1},{2,6},{6,10},{... | collective-permute-start | bytes 835592 | tf_op jit(solution)/shard_map/ppermute | solution.py:574
  8.3 2.1 %collective-permute-start.1 = (bf16[1088,128]{1,0:T(8,128)(2,1)S(1)}, bf16[1088,128]{1,0:T(8,128)(2,1)S(1)}, u32[]{:S(2)}, u32[]{:S(2)}) collective-permute-start(bf16[1088,128]{1,0:T(8,128)(2,1)S(1)} %get-tuple-element.33), channel_id=1, source_target_pairs={{0,12},{4,0},{8,4},{12,8},{1,13},{5,1},{9,5},{13,9},{2,14},{6,2},{... | collective-permute-start | bytes 835592 | tf_op jit(solution)/shard_map/ppermute | solution.py:574
  10.4 1.7 %collective-permute-start.5 = (bf16[272,128]{1,0:T(8,128)(2,1)S(1)}, bf16[272,128]{1,0:T(8,128)(2,1)S(1)}, u32[]{:S(2)}, u32[]{:S(2)}) collective-permute-start(bf16[272,128]{1,0:T(8,128)(2,1)S(1)} %bitcast.19), channel_id=1, source_target_pairs={{0,2},{2,0},{1,3},{3,1},{4,6},{6,4},{5,7},{7,5},{8,10},{10,8},{9,1... | collective-permute-start | bytes 208904 | tf_op jit(solution)/shard_map/ppermute | solution.py:644
  12.1 0.1 shard_map.79
  12.2 0.1 slice_convert_fusion.3
  12.3 5.6 %collective-permute-done.2.refs_0_.refs_4_ = bf16[1088,128]{1,0:T(8,128)(2,1)S(1)} collective-permute-done((bf16[1088,128]{1,0:T(8,128)(2,1)S(1)}, bf16[1088,128]{1,0:T(8,128)(2,1)S(1)}, u32[]{:S(2)}, u32[]{:S(2)}) %collective-permute-start.2) | collective-permute-done | bytes 278560 | tf_op jit(solution)/shard_map/ppermute | solution.py:574
  17.9 5.1 %collective-permute-done.1.refs_4_.refs_0_ = bf16[1088,128]{1,0:T(8,128)(2,1)S(1)} collective-permute-done((bf16[1088,128]{1,0:T(8,128)(2,1)S(1)}, bf16[1088,128]{1,0:T(8,128)(2,1)S(1)}, u32[]{:S(2)}, u32[]{:S(2)}) %collective-permute-start.1) | collective-permute-done | bytes 278560 | tf_op jit(solution)/shard_map/ppermute | solution.py:574
  23.1 1.6 %collective-permute-start.4 = (bf16[544,128]{1,0:T(8,128)(2,1)S(1)}, bf16[544,128]{1,0:T(8,128)(2,1)S(1)}, u32[]{:S(2)}, u32[]{:S(2)}) collective-permute-start(bf16[544,128]{1,0:T(8,128)(2,1)S(1)} %pad_maximum_fusion), channel_id=1, source_target_pairs={{0,2},{2,0},{1,3},{3,1},{4,6},{6,4},{5,7},{7,5},{8,10},{10,8},{9,1... | collective-permute-start | bytes 417800 | tf_op jit(solution)/shard_map/ppermute | solution.py:644
  24.7 1.3 %collective-permute-start.3 = (bf16[1088,128]{1,0:T(8,128)(2,1)S(1)}, bf16[1088,128]{1,0:T(8,128)(2,1)S(1)}, u32[]{:S(2)}, u32[]{:S(2)}) collective-permute-start(bf16[1088,128]{1,0:T(8,128)(2,1)S(1)} %get-tuple-element.36), channel_id=1, source_target_pairs={{0,8},{4,12},{8,0},{12,4},{1,9},{5,13},{9,1},{13,5},{2,10},{6,14},... | collective-permute-start | bytes 835592 | tf_op jit(solution)/shard_map/ppermute | solution.py:574
  26.0 0.1 slice_convert_fusion
  26.2 0.1 reshape.49.partner
  26.2 0.1 fusion.14
  26.3 0.1 reshape.50.weight
  26.4 1.8 %collective-permute-done.4.refs_1_ = bf16[544,128]{1,0:T(8,128)(2,1)S(1)} collective-permute-done((bf16[544,128]{1,0:T(8,128)(2,1)S(1)}, bf16[544,128]{1,0:T(8,128)(2,1)S(1)}, u32[]{:S(2)}, u32[]{:S(2)}) %collective-permute-start.4) | collective-permute-done | bytes 139296 | tf_op jit(solution)/shard_map/ppermute | solution.py:644
  28.2 8.7 %shard_map.80 = (f32[64,16,128]{2,1,0:T(8,128)S(1)}, f32[64,16,128]{2,1,0:T(8,128)S(1)}) custom-call(s32[64]{0:T(128)S(1)} %reshape.49.partner, f32[64]{0:T(128)S(1)} %reshape.50.weight, f32[2]{0:T(128)S(1)} %add_convert_fusion.1.present, bf16[1088,128]{1,0:T(8,128)(2,1)S(1)} %collective-permute-done.2.refs_0_.refs_4_, ...), custom_call_target="tpu_custom_call" | custom-call | flops 20000000 | bytes 30000000 | tf_op jit(solution)/shard_map/pallas_call | solution.py:689
  37.0 2.4 %collective-permute-done.3.refs_2_ = bf16[1088,128]{1,0:T(8,128)(2,1)S(1)} collective-permute-done((bf16[1088,128]{1,0:T(8,128)(2,1)S(1)}, bf16[1088,128]{1,0:T(8,128)(2,1)S(1)}, u32[]{:S(2)}, u32[]{:S(2)}) %collective-permute-start.3) | collective-permute-done | bytes 278560 | tf_op jit(solution)/shard_map/ppermute | solution.py:574
  39.4 0.1 fusion.7
  39.5 0.1 reshape.57.partner
  39.6 0.1 reshape.59.weight
  39.7 0.6 collective-permute-start.9
  40.3 2.3 %collective-permute-start.6 = (bf16[3,128,128]{2,1,0:T(8,128)(2,1)S(1)}, bf16[3,128,128]{2,1,0:T(8,128)(2,1)S(1)}, u32[]{:S(2)}, u32[]{:S(2)}) collective-permute-start(bf16[3,128,128]{2,1,0:T(8,128)(2,1)S(1)} %copy-done.7), channel_id=1, source_target_pairs={{0,12},{4,0},{8,4},{12,8},{1,13},{5,1},{9,5},{13,9},{2,14},{6,2},{... | collective-permute-start | bytes 294920 | tf_op jit(solution)/shard_map/ppermute | solution.py:574
  42.7 0.6 collective-permute-start.8
  43.3 0.1 reshape.58.partner
  43.4 0.7 %collective-permute-done.9.refs_3_ = bf16[272,128]{1,0:T(8,128)(2,1)S(1)} collective-permute-done((bf16[272,128]{1,0:T(8,128)(2,1)S(1)}, bf16[272,128]{1,0:T(8,128)(2,1)S(1)}, u32[]{:S(2)}, u32[]{:S(2)}) %collective-permute-start.9) | collective-permute-done | bytes 69664 | tf_op jit(solution)/shard_map/ppermute | solution.py:644
  44.1 8.7 %shard_map.81 = (f32[64,16,128]{2,1,0:T(8,128)S(1)}, f32[64,16,128]{2,1,0:T(8,128)S(1)}) custom-call(s32[64]{0:T(128)S(1)} %reshape.58.partner, f32[64]{0:T(128)S(1)} %reshape.59.weight, f32[2]{0:T(128)S(1)} %add_convert_fusion.1.present, bf16[1088,128]{1,0:T(8,128)(2,1)S(1)} %collective-permute-done.1.refs_4_.refs_0_, ...), custom_call_target="tpu_custom_call" | custom-call | flops 20000000 | bytes 30000000 | tf_op jit(solution)/shard_map/pallas_call | solution.py:689
  52.8 1.8 %shard_map.82 = (f32[32,16,128]{2,1,0:T(8,128)S(1)}, f32[8,128]{1,0:T(8,128)S(1)}) custom-call(s32[128]{0:T(128)S(1)} %reshape.57.partner, bf16[3,128,128]{2,1,0:T(8,128)(2,1)S(1)} %get-tuple-element.44.refs_0_, bf16[3,128,128]{2,1,0:T(8,128)(2,1)S(1)} %collective-permute-done.6.refs_1_, bf16[3,128,128]{2,1,0:T(8,128)(2,1)S(1)} %collective-permute-done.7.refs_2_, ...), custom_call_target="tpu_custom_call" | custom-call | flops 10000000 | bytes 8000000 | tf_op jit(solution)/shard_map/pallas_call | solution.py:720
  54.6 0.9 %collective-permute-start.11 = (f32[8,128]{1,0:T(8,128)S(1)}, f32[8,128]{1,0:T(8,128)S(1)}, u32[]{:S(2)}, u32[]{:S(2)}) collective-permute-start(f32[8,128]{1,0:T(8,128)S(1)} %get-tuple-element.53.refs_0_), channel_id=1, source_target_pairs={{0,2},{1,3},{2,0},{3,1},{4,6},{5,7},{6,4},{7,5},{8,10},{9,11},{10,... | collective-permute-start | bytes 12296 | tf_op jit(solution)/shard_map/ppermute | solution.py:735
  55.5 0.2 collective-permute-start.10
  55.7 0.3 collective-permute-done.12.refs_3_
  56.0 2.4 %collective-permute-done.11.refs_2_ = f32[8,128]{1,0:T(8,128)S(1)} collective-permute-done((f32[8,128]{1,0:T(8,128)S(1)}, f32[8,128]{1,0:T(8,128)S(1)}, u32[]{:S(2)}, u32[]{:S(2)}) %collective-permute-start.11) | collective-permute-done | bytes 4128 | tf_op jit(solution)/shard_map/ppermute | solution.py:735
  58.3 0.2 collective-permute-done.10.refs_1_
  58.6 2.9 %collective-permute-start.13 = (f32[136,128]{1,0:T(8,128)S(1)}, f32[136,128]{1,0:T(8,128)S(1)}, u32[]{:S(2)}, u32[]{:S(2)}) collective-permute-start(f32[136,128]{1,0:T(8,128)S(1)} %get-tuple-element.55), channel_id=1, source_target_pairs={{0,4},{4,8},{8,12},{12,0},{1,5},{5,9},{9,13},{13,1},{2,6},{6,10},{... | collective-permute-start | bytes 208904 | tf_op jit(solution)/shard_map/ppermute | solution.py:574
  61.5 0.9 %collective-permute-start.14 = (f32[136,128]{1,0:T(8,128)S(1)}, f32[136,128]{1,0:T(8,128)S(1)}, u32[]{:S(2)}, u32[]{:S(2)}) collective-permute-start(f32[136,128]{1,0:T(8,128)S(1)} %get-tuple-element.56), channel_id=1, source_target_pairs={{0,8},{4,12},{8,0},{12,4},{1,9},{5,13},{9,1},{13,5},{2,10},{6,14},... | collective-permute-start | bytes 208904 | tf_op jit(solution)/shard_map/ppermute | solution.py:574
  62.4 1.5 %collective-permute-start.15 = (f32[136,128]{1,0:T(8,128)S(1)}, f32[136,128]{1,0:T(8,128)S(1)}, u32[]{:S(2)}, u32[]{:S(2)}) collective-permute-start(f32[136,128]{1,0:T(8,128)S(1)} %get-tuple-element.57), channel_id=1, source_target_pairs={{0,12},{4,0},{8,4},{12,8},{1,13},{5,1},{9,5},{13,9},{2,14},{6,2},{... | collective-permute-start | bytes 208904 | tf_op jit(solution)/shard_map/ppermute | solution.py:574
  64.6 0.6 collective-permute-done.13.refs_1_
  65.2 2.2 %collective-permute-done.14.refs_2_ = f32[136,128]{1,0:T(8,128)S(1)} collective-permute-done((f32[136,128]{1,0:T(8,128)S(1)}, f32[136,128]{1,0:T(8,128)S(1)}, u32[]{:S(2)}, u32[]{:S(2)}) %collective-permute-start.14) | collective-permute-done | bytes 69664 | tf_op jit(solution)/shard_map/ppermute | solution.py:574
  67.5 0.9 %shard_map.84 = (f32[8,16,512]{2,1,0:T(8,128)}, f32[8,16,512]{2,1,0:T(8,128)}) custom-call(s32[1]{0:T(128)} %bitcast.me, f32[1]{0:T(128)S(6)} %copy.16.prev_mean, f32[8,16,512]{2,1,0:T(8,128)S(1)} %copy-done.2, f32[8,16,512]{2,1,0:T(8,128)S(1)} %copy-done.3, f32[136,128]{1,0:T(8,128)S(1)} %get-tuple-element.54.refs_0_, ...), custom_call_target="tpu_custom_call" | custom-call | flops 1000000 | bytes 2000000 | tf_op jit(solution)/shard_map/pallas_call | solution.py:746
  (37 shorter events, 0.4 us)
Async XLA Ops:
  0.6 1.2 %copy-start = (bf16[2,8,64,512]{3,2,1,0:T(8,128)(2,1)S(1)}, bf16[2,8,64,512]{3,2,1,0:T(8,128)(2,1)}, u32[]{:S(2)}) copy-start(bf16[2,8,64,512]{3,2,1,0:T(8,128)(2,1)} %slc.1) | copy-start | bytes 3145732
  1.9 2.5 %copy-start.1 = (bf16[2,8,64,512]{3,2,1,0:T(8,128)(2,1)S(1)}, bf16[2,8,64,512]{3,2,1,0:T(8,128)(2,1)}, u32[]{:S(2)}) copy-start(bf16[2,8,64,512]{3,2,1,0:T(8,128)(2,1)} %slc.1) | copy-start | bytes 3145732
  2.1 2.3 %collective-permute-start = (bf16[64,128]{1,0:T(8,128)(2,1)S(1)}, bf16[64,128]{1,0:T(8,128)(2,1)S(1)}, u32[]{:S(2)}, u32[]{:S(2)}) collective-permute-start(bf16[64,128]{1,0:T(8,128)(2,1)S(1)} %shard_map.77), channel_id=1, source_target_pairs={{0,1},{1,0},{2,3},{3,2},{4,5},{5,4},{6,7},{7,6},{8,9},{9,8},{10,11... | collective-permute-start | bytes 49160 | tf_op jit(solution)/shard_map/ppermute | solution.py:565
  2.6 0.7 copy-start.8
  3.4 0.7 copy-start.9
  4.4 7.8 %copy-start.2 = (f32[8,16,512]{2,1,0:T(8,128)S(1)}, f32[8,16,512]{2,1,0:T(8,128)}, u32[]{:S(2)}) copy-start(f32[8,16,512]{2,1,0:T(8,128)} %estimate.1) | copy-start | bytes 786436
  4.4 7.8 %copy-start.3 = (f32[8,16,512]{2,1,0:T(8,128)S(1)}, f32[8,16,512]{2,1,0:T(8,128)}, u32[]{:S(2)}) copy-start(f32[8,16,512]{2,1,0:T(8,128)} %direction.1) | copy-start | bytes 786436
  5.7 12.2 %collective-permute-start.2 = (bf16[1088,128]{1,0:T(8,128)(2,1)S(1)}, bf16[1088,128]{1,0:T(8,128)(2,1)S(1)}, u32[]{:S(2)}, u32[]{:S(2)}) collective-permute-start(bf16[1088,128]{1,0:T(8,128)(2,1)S(1)} %get-tuple-element.31), channel_id=1, source_target_pairs={{0,4},{4,8},{8,12},{12,0},{1,5},{5,9},{9,13},{13,1},{2,6},{6,10},{... | collective-permute-start | bytes 835592 | tf_op jit(solution)/shard_map/ppermute | solution.py:574
  8.3 14.7 %collective-permute-start.1 = (bf16[1088,128]{1,0:T(8,128)(2,1)S(1)}, bf16[1088,128]{1,0:T(8,128)(2,1)S(1)}, u32[]{:S(2)}, u32[]{:S(2)}) collective-permute-start(bf16[1088,128]{1,0:T(8,128)(2,1)S(1)} %get-tuple-element.33), channel_id=1, source_target_pairs={{0,12},{4,0},{8,4},{12,8},{1,13},{5,1},{9,5},{13,9},{2,14},{6,2},{... | collective-permute-start | bytes 835592 | tf_op jit(solution)/shard_map/ppermute | solution.py:574
  10.4 16.0 %collective-permute-start.5 = (bf16[272,128]{1,0:T(8,128)(2,1)S(1)}, bf16[272,128]{1,0:T(8,128)(2,1)S(1)}, u32[]{:S(2)}, u32[]{:S(2)}) collective-permute-start(bf16[272,128]{1,0:T(8,128)(2,1)S(1)} %bitcast.19), channel_id=1, source_target_pairs={{0,2},{2,0},{1,3},{3,1},{4,6},{6,4},{5,7},{7,5},{8,10},{10,8},{9,1... | collective-permute-start | bytes 208904 | tf_op jit(solution)/shard_map/ppermute | solution.py:644
  12.2 10.9 %copy-start.4 = (bf16[3,128,128]{2,1,0:T(8,128)(2,1)}, bf16[3,128,128]{2,1,0:T(8,128)(2,1)S(1)}, u32[]{:S(2)}) copy-start(bf16[3,128,128]{2,1,0:T(8,128)(2,1)S(1)} %get-tuple-element.46) | copy-start | bytes 294916
  12.2 10.9 %copy-start.6 = (bf16[3,128,128]{2,1,0:T(8,128)(2,1)}, bf16[3,128,128]{2,1,0:T(8,128)(2,1)S(1)}, u32[]{:S(2)}) copy-start(bf16[3,128,128]{2,1,0:T(8,128)(2,1)S(1)} %get-tuple-element.45) | copy-start | bytes 294916
  23.1 5.1 %collective-permute-start.4 = (bf16[544,128]{1,0:T(8,128)(2,1)S(1)}, bf16[544,128]{1,0:T(8,128)(2,1)S(1)}, u32[]{:S(2)}, u32[]{:S(2)}) collective-permute-start(bf16[544,128]{1,0:T(8,128)(2,1)S(1)} %pad_maximum_fusion), channel_id=1, source_target_pairs={{0,2},{2,0},{1,3},{3,1},{4,6},{6,4},{5,7},{7,5},{8,10},{10,8},{9,1... | collective-permute-start | bytes 417800 | tf_op jit(solution)/shard_map/ppermute | solution.py:644
  24.7 14.6 %collective-permute-start.3 = (bf16[1088,128]{1,0:T(8,128)(2,1)S(1)}, bf16[1088,128]{1,0:T(8,128)(2,1)S(1)}, u32[]{:S(2)}, u32[]{:S(2)}) collective-permute-start(bf16[1088,128]{1,0:T(8,128)(2,1)S(1)} %get-tuple-element.36), channel_id=1, source_target_pairs={{0,8},{4,12},{8,0},{12,4},{1,9},{5,13},{9,1},{13,5},{2,10},{6,14},... | collective-permute-start | bytes 835592 | tf_op jit(solution)/shard_map/ppermute | solution.py:574
  39.4 0.9 %copy-start.7 = (bf16[3,128,128]{2,1,0:T(8,128)(2,1)S(1)}, bf16[3,128,128]{2,1,0:T(8,128)(2,1)}, u32[]{:S(2)}) copy-start(bf16[3,128,128]{2,1,0:T(8,128)(2,1)} %copy-done.6) | copy-start | bytes 294916
  39.4 3.3 %copy-start.5 = (bf16[3,128,128]{2,1,0:T(8,128)(2,1)S(1)}, bf16[3,128,128]{2,1,0:T(8,128)(2,1)}, u32[]{:S(2)}) copy-start(bf16[3,128,128]{2,1,0:T(8,128)(2,1)} %copy-done.4) | copy-start | bytes 294916
  39.7 4.4 %collective-permute-start.9 = (bf16[272,128]{1,0:T(8,128)(2,1)S(1)}, bf16[272,128]{1,0:T(8,128)(2,1)S(1)}, u32[]{:S(2)}, u32[]{:S(2)}) collective-permute-start(bf16[272,128]{1,0:T(8,128)(2,1)S(1)} %bitcast.20), channel_id=1, source_target_pairs={{0,2},{2,0},{1,3},{3,1},{4,6},{6,4},{5,7},{7,5},{8,10},{10,8},{9,1... | collective-permute-start | bytes 208904 | tf_op jit(solution)/shard_map/ppermute | solution.py:644
  40.3 12.5 %collective-permute-start.6 = (bf16[3,128,128]{2,1,0:T(8,128)(2,1)S(1)}, bf16[3,128,128]{2,1,0:T(8,128)(2,1)S(1)}, u32[]{:S(2)}, u32[]{:S(2)}) collective-permute-start(bf16[3,128,128]{2,1,0:T(8,128)(2,1)S(1)} %copy-done.7), channel_id=1, source_target_pairs={{0,12},{4,0},{8,4},{12,8},{1,13},{5,1},{9,5},{13,9},{2,14},{6,2},{... | collective-permute-start | bytes 294920 | tf_op jit(solution)/shard_map/ppermute | solution.py:574
  42.6 10.2 %collective-permute-start.7 = (bf16[3,128,128]{2,1,0:T(8,128)(2,1)S(1)}, bf16[3,128,128]{2,1,0:T(8,128)(2,1)S(1)}, u32[]{:S(2)}, u32[]{:S(2)}) collective-permute-start(bf16[3,128,128]{2,1,0:T(8,128)(2,1)S(1)} %copy-done.5), channel_id=1, source_target_pairs={{0,8},{4,12},{8,0},{12,4},{1,9},{5,13},{9,1},{13,5},{2,10},{6,14},... | collective-permute-start | bytes 294920 | tf_op jit(solution)/shard_map/ppermute | solution.py:574
  42.7 10.2 %collective-permute-start.8 = (bf16[3,128,128]{2,1,0:T(8,128)(2,1)S(1)}, bf16[3,128,128]{2,1,0:T(8,128)(2,1)S(1)}, u32[]{:S(2)}, u32[]{:S(2)}) collective-permute-start(bf16[3,128,128]{2,1,0:T(8,128)(2,1)S(1)} %get-tuple-element.47), channel_id=1, source_target_pairs={{0,4},{4,8},{8,12},{12,0},{1,5},{5,9},{9,13},{13,1},{2,6},{6,10},{... | collective-permute-start | bytes 294920 | tf_op jit(solution)/shard_map/ppermute | solution.py:574
  54.6 1.4 %collective-permute-start.12 = (f32[8,128]{1,0:T(8,128)S(1)}, f32[8,128]{1,0:T(8,128)S(1)}, u32[]{:S(2)}, u32[]{:S(2)}) collective-permute-start(f32[8,128]{1,0:T(8,128)S(1)} %get-tuple-element.53.refs_0_), channel_id=1, source_target_pairs={{0,3},{1,0},{2,1},{3,2},{4,7},{5,4},{6,5},{7,6},{8,11},{9,8},{10,9... | collective-permute-start | bytes 12296 | tf_op jit(solution)/shard_map/ppermute | solution.py:735
  54.6 3.7 %collective-permute-start.11 = (f32[8,128]{1,0:T(8,128)S(1)}, f32[8,128]{1,0:T(8,128)S(1)}, u32[]{:S(2)}, u32[]{:S(2)}) collective-permute-start(f32[8,128]{1,0:T(8,128)S(1)} %get-tuple-element.53.refs_0_), channel_id=1, source_target_pairs={{0,2},{1,3},{2,0},{3,1},{4,6},{5,7},{6,4},{7,5},{8,10},{9,11},{10,... | collective-permute-start | bytes 12296 | tf_op jit(solution)/shard_map/ppermute | solution.py:735
  55.5 3.0 %collective-permute-start.10 = (f32[8,128]{1,0:T(8,128)S(1)}, f32[8,128]{1,0:T(8,128)S(1)}, u32[]{:S(2)}, u32[]{:S(2)}) collective-permute-start(f32[8,128]{1,0:T(8,128)S(1)} %get-tuple-element.53.refs_0_), channel_id=1, source_target_pairs={{0,1},{1,2},{2,3},{3,0},{4,5},{5,6},{6,7},{7,4},{8,9},{9,10},{10,1... | collective-permute-start | bytes 12296 | tf_op jit(solution)/shard_map/ppermute | solution.py:735
  58.6 6.6 %collective-permute-start.13 = (f32[136,128]{1,0:T(8,128)S(1)}, f32[136,128]{1,0:T(8,128)S(1)}, u32[]{:S(2)}, u32[]{:S(2)}) collective-permute-start(f32[136,128]{1,0:T(8,128)S(1)} %get-tuple-element.55), channel_id=1, source_target_pairs={{0,4},{4,8},{8,12},{12,0},{1,5},{5,9},{9,13},{13,1},{2,6},{6,10},{... | collective-permute-start | bytes 208904 | tf_op jit(solution)/shard_map/ppermute | solution.py:574
  61.5 6.0 %collective-permute-start.14 = (f32[136,128]{1,0:T(8,128)S(1)}, f32[136,128]{1,0:T(8,128)S(1)}, u32[]{:S(2)}, u32[]{:S(2)}) collective-permute-start(f32[136,128]{1,0:T(8,128)S(1)} %get-tuple-element.56), channel_id=1, source_target_pairs={{0,8},{4,12},{8,0},{12,4},{1,9},{5,13},{9,1},{13,5},{2,10},{6,14},... | collective-permute-start | bytes 208904 | tf_op jit(solution)/shard_map/ppermute | solution.py:574
  62.4 5.1 %collective-permute-start.15 = (f32[136,128]{1,0:T(8,128)S(1)}, f32[136,128]{1,0:T(8,128)S(1)}, u32[]{:S(2)}, u32[]{:S(2)}) collective-permute-start(f32[136,128]{1,0:T(8,128)S(1)} %get-tuple-element.57), channel_id=1, source_target_pairs={{0,12},{4,0},{8,4},{12,8},{1,13},{5,1},{9,5},{13,9},{2,14},{6,2},{... | collective-permute-start | bytes 208904 | tf_op jit(solution)/shard_map/ppermute | solution.py:574

commit v14 on v13

--- a/solution.py
+++ b/solution.py
@@ -2,6 +2,7 @@
 
 import jax
 import jax.numpy as jnp
+import numpy as np
 from jax import lax
 from jax.experimental import pallas as pl
 from jax.experimental.pallas import tpu as pltpu
@@ -181,7 +182,7 @@
     return jnp.where((lane >= target) & (lane < target + RADIUS), moved, total)
 
 
-def pack_kernel(me, present, slc, params, before, after, *refs):
+def pack_kernel(me, present, slc, params, outer, before, after, *refs):
     messages, strips = refs[:-1], refs[-1]
     tiles = len(messages)
     epochs = slc.shape[1]
@@ -194,15 +195,15 @@
     third = PARAM_LANE + 2 * SLOTS
     split = jnp.where(lane < third, high, jnp.where(lane < third + SLOTS, middle, low))
     split = jnp.where(lane >= PARAM_LANE, split, 0.0)
-    inside = lane < 2 * epochs * SIDES
+    sides = outer[...]
     for tile in range(tiles):
         total = split
         if tile == 0:
             edge = before[...].astype(jnp.float32) * present[0]
-            total = jnp.where(inside & (lane % SIDES < RADIUS), edge, total)
+            total = jnp.where(sides == 1.0, edge, total)
         if tile == tiles - 1:
             edge = after[...].astype(jnp.float32) * present[1]
-            total = jnp.where(inside & (lane % SIDES >= RADIUS), edge, total)
+            total = jnp.where(sides == 2.0, edge, total)
         for part in range(2):
             for epoch in range(epochs):
                 at = (part * epochs + epoch) * SIDES
@@ -224,12 +225,11 @@
                 message[2 * epochs * rows :, :] = strips[tile]
 
 
-def look_order(from_rows, first, keep):
+def look_order(from_rows, first):
     looks = from_rows // LOOK
-    to = lax.broadcasted_iota(jnp.int32, (from_rows, from_rows), 0)
-    at = lax.broadcasted_iota(jnp.int32, (from_rows, from_rows), 1)
-    order = (at == (to + first) % looks * LOOK + to // looks).astype(jnp.float32)
-    return (order * keep(at)).astype(jnp.bfloat16)
+    to = np.arange(from_rows)[:, None]
+    at = np.arange(from_rows)[None, :]
+    return jnp.asarray(at == (to + first) % looks * LOOK + to // looks, jnp.bfloat16)
 
 
 def unpack_tiles(order, sources, main, first, columns_of):
@@ -258,34 +258,25 @@
         rim[place] = value
 
 
-def band_of(shape, from_of, to_of):
-    at = lax.broadcasted_iota(jnp.int32, shape, 0)
-    to = lax.broadcasted_iota(jnp.int32, shape, 1)
-    return (jnp.abs(from_of(at, to) - to_of(at, to)) <= RADIUS).astype(jnp.float32).astype(jnp.bfloat16)
-
-
 def column_bands():
     share = LANES // SLOTS
-
-    def rim_from(at, to):
-        side = at % share % SIDES
-        return jnp.where(side < RADIUS, side - RADIUS, LANES + side - RADIUS)
-
-    def rim_to(at, to):
-        column = (to - at % LANES // share * share + LANES) % LANES
-        inside = (column < RADIUS) | (column >= LANES - RADIUS)
-        inside = inside & (at % share < LOOK * SIDES)
-        return jnp.where(inside, column, 4 * LANES)
-
-    band = band_of((2 * LANES, LANES), lambda at, to: at % LANES, lambda at, to: to)
-    return band, band_of((2 * LANES, LANES), rim_from, rim_to)
+    at = np.arange(2 * LANES)[:, None] % LANES
+    to = np.arange(LANES)[None, :]
+    side = at % share % SIDES
+    source = np.where(side < RADIUS, side - RADIUS, LANES + side - RADIUS)
+    column = (to - at // share * share) % LANES
+    inside = (column < RADIUS) | (column >= LANES - RADIUS)
+    inside = inside & (at % share < LOOK * SIDES)
+    band = np.abs(at - to) <= RADIUS
+    rim_band = inside & (np.abs(source - column) <= RADIUS)
+    return jnp.asarray(band, jnp.bfloat16), jnp.asarray(rim_band, jnp.bfloat16)
 
 
 def mixed(values):
     lane = lax.broadcasted_iota(jnp.int32, values[0].shape, 1)
     result = values[-1]
     for slot in range(SLOTS - 1):
-        result = jnp.where(lane // (LANES // SLOTS) == slot, values[slot], result)
+        result = jnp.where(lane < (SLOTS - 1 - slot) * (LANES // SLOTS), values[SLOTS - 2 - slot], result)
     return result
 
 
@@ -385,7 +376,7 @@
     return jnp.minimum(jnp.maximum(value, 0), last)
 
 
-def pair_kernel(sizes, places, partner, weight, present, *refs):
+def pair_kernel(sizes, places, partner, weight, present, order, band, rim_band, *refs):
     epochs, rows, operands = sizes
     inputs = refs[:operands]
     factors, pulls, boxed, main, rim, looked, rim_looked, wide = refs[operands:]
@@ -398,11 +389,10 @@
     full_rows = rows + 2 * HALO
     group = 2 * SLOTS
 
-    def keep(at):
-        return jnp.where(at < HALO, present[0], jnp.where(at >= HALO + rows, present[1], 1.0))
-
-    order = look_order(full_rows, halo_looks - RADIUS, keep)
-    bands = column_bands()
+    at = lax.broadcasted_iota(jnp.int32, (full_rows, full_rows), 1)
+    keep = jnp.where(at < HALO, present[0], jnp.where(at >= HALO + rows, present[1], 1.0))
+    order = (order[...].astype(jnp.float32) * keep).astype(jnp.bfloat16)
+    bands = band[...], rim_band[...]
     for block, (tile_at, top_at, bottom_at, halo_row) in enumerate(places):
         tile, top, bottom = inputs[tile_at], inputs[top_at], inputs[bottom_at]
 
@@ -474,7 +464,8 @@
 
         @pl.loop(0, own_total, unroll=2)
         def _(here):
-            epoch = lax.rem(first + here, total)
+            epoch = first + here
+            epoch = jnp.where(epoch < total, epoch, epoch - total)
             own_est = est[epoch]
             own = jnp.zeros((look_rows, LANES), f32)
             mates = [partner[epoch * SLOTS + slot] for slot in range(SLOTS)]
@@ -494,7 +485,8 @@
 
         def totals(here, carry):
             norm, crossed, grad_term, mixed_term, old_term = carry
-            epoch = lax.rem(first + here, total)
+            epoch = first + here
+            epoch = jnp.where(epoch < total, epoch, epoch - total)
             own_grad = gradient[epoch]
             own_old = old[epoch]
             norm = norm + own_grad * own_grad
@@ -606,16 +598,19 @@
     params = jnp.zeros((rows, LANES), f32)
     listed = jnp.concatenate([offsets.astype(f32), weights, weights, weights], axis=1)
     params = lax.dynamic_update_slice(params, listed, (0, PARAM_LANE))
+    lane = np.arange(LANES)
+    sides = np.where(lane < 2 * epochs * SIDES, np.where(lane % SIDES < RADIUS, 1.0, 2.0), 0.0)
+    sides = jnp.asarray(np.broadcast_to(sides, (rows, LANES)), f32)
     sub_present = jnp.stack([sub > 0, sub < lax.axis_size("sub") - 1]).astype(f32)
     messages = pl.pallas_call(
         pack_kernel,
         out_shape=(jax.ShapeDtypeStruct((tile_rows + rows, LANES), bf16),) * tiles,
-        in_specs=[SMEM] * 2 + [VMEM] * 4,
+        in_specs=[SMEM] * 2 + [VMEM] * 5,
         out_specs=(VMEM,) * tiles,
         scratch_shapes=[pltpu.VMEM((tiles, rows, LANES), bf16)],
         compiler_params=params_of,
         cost_estimate=pl.CostEstimate(flops=3_000_000, bytes_accessed=4_000_000, transcendentals=0),
-    )(me.reshape(1), sub_present, slc, params, before, after)
+    )(me.reshape(1), sub_present, slc, params, sides, before, after)
     beside = [tiles - 1, 0, 1]
     far = list(range(2, tiles - 1))
     block = {0: messages[0], 1: fetched(messages, 1), tiles - 1: fetched(messages, tiles - 1)}
@@ -660,6 +655,9 @@
     own_halo = halo([by_rows(0)])
     near_halo = halo([by_rows(1), by_rows(tiles - 1)])
     halos = {0: (own_halo, 0), 1: (near_halo, 0), tiles - 1: (near_halo, 1)}
+
+    order = look_order(rows + 2 * HALO, HALO // LOOK - RADIUS)
+    bands = column_bands()
 
     def pair_stage(loaded):
         own = loaded[:-1]
@@ -689,7 +687,7 @@
         return pl.pallas_call(
             functools.partial(pair_kernel, (epochs, rows, len(operands)), tuple(places)),
             out_shape=(shape, shape),
-            in_specs=[SMEM] * 3 + [VMEM] * len(operands),
+            in_specs=[SMEM] * 3 + [VMEM] * (3 + len(operands)),
             out_specs=(VMEM, VMEM),
             scratch_shapes=[
                 pltpu.VMEM((batches * group * look_rows, LANES), f32),
@@ -701,7 +699,7 @@
             ],
             compiler_params=params_of,
             cost_estimate=pl.CostEstimate(flops=20_000_000, bytes_accessed=30_000_000, transcendentals=0),
-        )(mate.reshape(-1), weight.reshape(-1), present, *operands)
+        )(mate.reshape(-1), weight.reshape(-1), present, order, *bands, *operands)
 
     near_stage = beside
     far_stage = list(range(1, tiles))

time: 68.6 us -> 69.2 us (level)
    unnamed x22 -> x30, local copies, waits for them, and re-layouts: 2.77 us -> 3.3 us
where the time goes in v14:
time: 69.2 us; the launch traced here: 68.9 us
  Pallas kernels  22.2 us (32%)
  waiting for transfers between devices  20.9 us (30%)
  starting transfers between devices  19.8 us (29%)
  local copies, waits for them, and re-layouts  3.81 us (6%)
  between operations  1.48 us (2%)
  other arithmetic  0.71 us (1%)
    pallas_call x2, Pallas kernels, pair_stage(): pl.pallas_call(functools.partial(pair_kernel, (epochs, rows, len(operands...  17.4 us
    ppermute x9, waiting for transfers between devices, to_ahead(): return lax.ppermute(x, axis, [(i, (i + by) % size) for i in range(size)])  15.4 us
    ppermute x9, starting transfers between devices, to_ahead(): return lax.ppermute(x, axis, [(i, (i + by) % size) for i in range(size)])  14.4 us
    ppermute x3, starting transfers between devices, halo(): lax.ppermute(border(jnp.where(space == 0, rows - HALO, 0)), 'space', [(0,...  3.86 us
    unnamed x30, local copies, waits for them, and re-layouts  3.3 us
    ppermute x3, waiting for transfers between devices, transposed_plan(): lax.ppermute(sums, place, [(i, (i + by) % count) for i in range(count)])  2.87 us
    ppermute x3, waiting for transfers between devices, halo(): lax.ppermute(border(jnp.where(space == 0, rows - HALO, 0)), 'space', [(0,...  2.58 us
    pallas_call x1, Pallas kernels, transposed_plan(): pl.pallas_call(functools.partial(gradient_kernel, (tiles, epochs, stages)...  1.73 us
  transfers between devices with their start and end apart: 16, of which 10 were waited for; matrix products, arithmetic and copies ran while one was open for 1% of the time, Pallas kernels for 26%

profile of v14, /device:TPU:0, one launch (start us, length us, event | category | flops | bytes accessed | tf_op | source)
XLA Modules:
  0.0 68.9 jit_solution(9680706331092072709)
XLA Ops:
  0.6 1.2 %copy-done = bf16[2,8,64,512]{3,2,1,0:T(8,128)(2,1)S(1)} copy-done((bf16[2,8,64,512]{3,2,1,0:T(8,128)(2,1)S(1)}, bf16[2,8,64,512]{3,2,1,0:T(8,128)(2,1)}, u32[]{:S(2)}) %copy-start) | copy-done | bytes 1048600
  1.9 0.2 shard_map.113
  2.1 0.5 collective-permute-start
  2.6 0.7 copy-done.12
  3.3 0.1 copy.16
  3.4 0.7 copy-done.13
  4.1 0.1 copy.17
  4.1 0.1 add_convert_fusion.1.present
  4.2 0.1 select_maximum_fusion.params
  4.3 0.1 add_convert_fusion.present
  4.4 0.5 copy-done.7
  4.9 1.3 %shard_map.114 = (bf16[1088,128]{1,0:T(8,128)(2,1)S(1)}, bf16[1088,128]{1,0:T(8,128)(2,1)S(1)}, bf16[1088,128]{1,0:T(8,128)(2,1)S(1)}, bf16[1088,128]{1,0:T(8,128)(2,1)S(1)}) custom-call(s32[1]{0:T(128)} %bitcast.me, f32[2]{0:T(128)S(1)} %add_convert_fusion.present, bf16[2,8,64,512]{3,2,1,0:T(8,128)(2,1)S(1)} %copy-done.1, ...), custom_call_target="tpu_custom_call" | custom-call | flops 3000000 | bytes 4000000 | tf_op jit(solution)/shard_map/pallas_call | solution.py:605
  6.2 2.7 %collective-permute-start.2 = (bf16[1088,128]{1,0:T(8,128)(2,1)S(1)}, bf16[1088,128]{1,0:T(8,128)(2,1)S(1)}, u32[]{:S(2)}, u32[]{:S(2)}) collective-permute-start(bf16[1088,128]{1,0:T(8,128)(2,1)S(1)} %get-tuple-element.31), channel_id=1, source_target_pairs={{0,4},{4,8},{8,12},{12,0},{1,5},{5,9},{9,13},{13,1},{2,6},{6,10},{... | collective-permute-start | bytes 835592 | tf_op jit(solution)/shard_map/ppermute | solution.py:566
  8.9 2.1 %collective-permute-start.1 = (bf16[1088,128]{1,0:T(8,128)(2,1)S(1)}, bf16[1088,128]{1,0:T(8,128)(2,1)S(1)}, u32[]{:S(2)}, u32[]{:S(2)}) collective-permute-start(bf16[1088,128]{1,0:T(8,128)(2,1)S(1)} %get-tuple-element.33), channel_id=1, source_target_pairs={{0,12},{4,0},{8,4},{12,8},{1,13},{5,1},{9,5},{13,9},{2,14},{6,2},{... | collective-permute-start | bytes 835592 | tf_op jit(solution)/shard_map/ppermute | solution.py:566
  11.0 1.7 %collective-permute-start.5 = (bf16[272,128]{1,0:T(8,128)(2,1)S(1)}, bf16[272,128]{1,0:T(8,128)(2,1)S(1)}, u32[]{:S(2)}, u32[]{:S(2)}) collective-permute-start(bf16[272,128]{1,0:T(8,128)(2,1)S(1)} %bitcast.19), channel_id=1, source_target_pairs={{0,2},{2,0},{1,3},{3,1},{4,6},{6,4},{5,7},{7,5},{8,10},{10,8},{9,1... | collective-permute-start | bytes 208904 | tf_op jit(solution)/shard_map/ppermute | solution.py:639
  12.7 0.7 %shard_map.115 = (bf16[3,128,128]{2,1,0:T(8,128)(2,1)S(1)}, bf16[3,128,128]{2,1,0:T(8,128)(2,1)S(1)}, bf16[3,128,128]{2,1,0:T(8,128)(2,1)S(1)}, bf16[3,128,128]{2,1,0:T(8,128)(2,1)}) custom-call(s32[1]{0:T(128)} %bitcast.me, f32[8,16,512]{2,1,0:T(8,128)S(1)} %copy-done.2, f32[8,16,512]{2,1,0:T(8,128)S(1)} %copy-done.3), custom_call_target="tpu_custom_call" | custom-call | flops 1000000 | bytes 2000000 | tf_op jit(solution)/shard_map/pallas_call | solution.py:621
  13.4 0.1 slice_convert_fusion.3
  13.4 5.0 %collective-permute-done.2.refs_0_.refs_4_ = bf16[1088,128]{1,0:T(8,128)(2,1)S(1)} collective-permute-done((bf16[1088,128]{1,0:T(8,128)(2,1)S(1)}, bf16[1088,128]{1,0:T(8,128)(2,1)S(1)}, u32[]{:S(2)}, u32[]{:S(2)}) %collective-permute-start.2) | collective-permute-done | bytes 278560 | tf_op jit(solution)/shard_map/ppermute | solution.py:566
  18.5 5.1 %collective-permute-done.1.refs_4_.refs_0_ = bf16[1088,128]{1,0:T(8,128)(2,1)S(1)} collective-permute-done((bf16[1088,128]{1,0:T(8,128)(2,1)S(1)}, bf16[1088,128]{1,0:T(8,128)(2,1)S(1)}, u32[]{:S(2)}, u32[]{:S(2)}) %collective-permute-start.1) | collective-permute-done | bytes 278560 | tf_op jit(solution)/shard_map/ppermute | solution.py:566
  23.7 1.6 %collective-permute-start.4 = (bf16[544,128]{1,0:T(8,128)(2,1)S(1)}, bf16[544,128]{1,0:T(8,128)(2,1)S(1)}, u32[]{:S(2)}, u32[]{:S(2)}) collective-permute-start(bf16[544,128]{1,0:T(8,128)(2,1)S(1)} %pad_maximum_fusion), channel_id=1, source_target_pairs={{0,2},{2,0},{1,3},{3,1},{4,6},{6,4},{5,7},{7,5},{8,10},{10,8},{9,1... | collective-permute-start | bytes 417800 | tf_op jit(solution)/shard_map/ppermute | solution.py:639
  25.2 1.3 %collective-permute-start.3 = (bf16[1088,128]{1,0:T(8,128)(2,1)S(1)}, bf16[1088,128]{1,0:T(8,128)(2,1)S(1)}, u32[]{:S(2)}, u32[]{:S(2)}) collective-permute-start(bf16[1088,128]{1,0:T(8,128)(2,1)S(1)} %get-tuple-element.36), channel_id=1, source_target_pairs={{0,8},{4,12},{8,0},{12,4},{1,9},{5,13},{9,1},{13,5},{2,10},{6,14},... | collective-permute-start | bytes 835592 | tf_op jit(solution)/shard_map/ppermute | solution.py:566
  26.7 0.1 reshape.49.partner
  26.8 0.1 fusion.14
  26.9 0.1 reshape.50.weight
  27.0 1.8 %collective-permute-done.4.refs_1_ = bf16[544,128]{1,0:T(8,128)(2,1)S(1)} collective-permute-done((bf16[544,128]{1,0:T(8,128)(2,1)S(1)}, bf16[544,128]{1,0:T(8,128)(2,1)S(1)}, u32[]{:S(2)}, u32[]{:S(2)}) %collective-permute-start.4) | collective-permute-done | bytes 139296 | tf_op jit(solution)/shard_map/ppermute | solution.py:639
  28.8 8.7 %shard_map.116 = (f32[64,16,128]{2,1,0:T(8,128)S(1)}, f32[64,16,128]{2,1,0:T(8,128)S(1)}) custom-call(s32[64]{0:T(128)S(1)} %reshape.49.partner, f32[64]{0:T(128)S(1)} %reshape.50.weight, f32[2]{0:T(128)S(1)} %add_convert_fusion.1.present, bf16[96,96]{1,0:T(8,128)(2,1)S(1)} %copy-done.6, bf16[256,128]{1,0:T(8,128)(2,1)S(1)} %copy-done.5, ...), custom_call_target="tpu_custom_call" | custom-call | flops 20000000 | bytes 30000000 | tf_op jit(solution)/shard_map/pallas_call | solution.py:687
  37.5 2.4 %collective-permute-done.3.refs_2_ = bf16[1088,128]{1,0:T(8,128)(2,1)S(1)} collective-permute-done((bf16[1088,128]{1,0:T(8,128)(2,1)S(1)}, bf16[1088,128]{1,0:T(8,128)(2,1)S(1)}, u32[]{:S(2)}, u32[]{:S(2)}) %collective-permute-start.3) | collective-permute-done | bytes 278560 | tf_op jit(solution)/shard_map/ppermute | solution.py:566
  40.0 0.1 fusion.7
  40.0 0.1 reshape.57.partner
  40.1 0.1 reshape.59.weight
  40.3 0.6 collective-permute-start.9
  40.9 2.3 %collective-permute-start.6 = (bf16[3,128,128]{2,1,0:T(8,128)(2,1)}, bf16[3,128,128]{2,1,0:T(8,128)(2,1)S(1)}, u32[]{:S(2)}, u32[]{:S(2)}) collective-permute-start(bf16[3,128,128]{2,1,0:T(8,128)(2,1)} %get-tuple-element.45), channel_id=1, source_target_pairs={{0,12},{4,0},{8,4},{12,8},{1,13},{5,1},{9,5},{13,9},{2,14},{6,2},{... | collective-permute-start | bytes 294920 | tf_op jit(solution)/shard_map/ppermute | solution.py:566
  43.2 0.6 collective-permute-start.8
  43.8 0.1 reshape.58.partner
  43.9 0.8 %collective-permute-done.9.refs_3_ = bf16[272,128]{1,0:T(8,128)(2,1)S(1)} collective-permute-done((bf16[272,128]{1,0:T(8,128)(2,1)S(1)}, bf16[272,128]{1,0:T(8,128)(2,1)S(1)}, u32[]{:S(2)}, u32[]{:S(2)}) %collective-permute-start.9) | collective-permute-done | bytes 69664 | tf_op jit(solution)/shard_map/ppermute | solution.py:639
  44.6 8.7 %shard_map.117 = (f32[64,16,128]{2,1,0:T(8,128)S(1)}, f32[64,16,128]{2,1,0:T(8,128)S(1)}) custom-call(s32[64]{0:T(128)S(1)} %reshape.58.partner, f32[64]{0:T(128)S(1)} %reshape.59.weight, f32[2]{0:T(128)S(1)} %add_convert_fusion.1.present, bf16[96,96]{1,0:T(8,128)(2,1)S(1)} %copy-done.6, bf16[256,128]{1,0:T(8,128)(2,1)S(1)} %copy-done.5, ...), custom_call_target="tpu_custom_call" | custom-call | flops 20000000 | bytes 30000000 | tf_op jit(solution)/shard_map/pallas_call | solution.py:687
  53.3 1.7 %shard_map.118 = (f32[32,16,128]{2,1,0:T(8,128)S(1)}, f32[8,128]{1,0:T(8,128)S(1)}) custom-call(s32[128]{0:T(128)S(1)} %reshape.57.partner, bf16[3,128,128]{2,1,0:T(8,128)(2,1)S(1)} %get-tuple-element.44.refs_0_, bf16[3,128,128]{2,1,0:T(8,128)(2,1)S(1)} %collective-permute-done.6.refs_1_, bf16[3,128,128]{2,1,0:T(8,128)(2,1)S(1)} %collective-permute-done.7.refs_2_, ...), custom_call_target="tpu_custom_call" | custom-call | flops 10000000 | bytes 8000000 | tf_op jit(solution)/shard_map/pallas_call | solution.py:718
  55.1 0.8 %collective-permute-start.11 = (f32[8,128]{1,0:T(8,128)S(1)}, f32[8,128]{1,0:T(8,128)S(1)}, u32[]{:S(2)}, u32[]{:S(2)}) collective-permute-start(f32[8,128]{1,0:T(8,128)S(1)} %get-tuple-element.53.refs_0_), channel_id=1, source_target_pairs={{0,2},{1,3},{2,0},{3,1},{4,6},{5,7},{6,4},{7,5},{8,10},{9,11},{10,... | collective-permute-start | bytes 12296 | tf_op jit(solution)/shard_map/ppermute | solution.py:733
  55.9 0.2 collective-permute-start.10
  56.1 0.3 collective-permute-done.12.refs_3_
  56.5 2.4 %collective-permute-done.11.refs_2_ = f32[8,128]{1,0:T(8,128)S(1)} collective-permute-done((f32[8,128]{1,0:T(8,128)S(1)}, f32[8,128]{1,0:T(8,128)S(1)}, u32[]{:S(2)}, u32[]{:S(2)}) %collective-permute-start.11) | collective-permute-done | bytes 4128 | tf_op jit(solution)/shard_map/ppermute | solution.py:733
  58.8 0.2 collective-permute-done.10.refs_1_
  59.0 3.0 %collective-permute-start.13 = (f32[136,128]{1,0:T(8,128)S(1)}, f32[136,128]{1,0:T(8,128)S(1)}, u32[]{:S(2)}, u32[]{:S(2)}) collective-permute-start(f32[136,128]{1,0:T(8,128)S(1)} %get-tuple-element.55), channel_id=1, source_target_pairs={{0,4},{4,8},{8,12},{12,0},{1,5},{5,9},{9,13},{13,1},{2,6},{6,10},{... | collective-permute-start | bytes 208904 | tf_op jit(solution)/shard_map/ppermute | solution.py:566
  62.0 1.0 %collective-permute-start.14 = (f32[136,128]{1,0:T(8,128)S(1)}, f32[136,128]{1,0:T(8,128)S(1)}, u32[]{:S(2)}, u32[]{:S(2)}) collective-permute-start(f32[136,128]{1,0:T(8,128)S(1)} %get-tuple-element.56), channel_id=1, source_target_pairs={{0,8},{4,12},{8,0},{12,4},{1,9},{5,13},{9,1},{13,5},{2,10},{6,14},... | collective-permute-start | bytes 208904 | tf_op jit(solution)/shard_map/ppermute | solution.py:566
  62.9 1.5 %collective-permute-start.15 = (f32[136,128]{1,0:T(8,128)S(1)}, f32[136,128]{1,0:T(8,128)S(1)}, u32[]{:S(2)}, u32[]{:S(2)}) collective-permute-start(f32[136,128]{1,0:T(8,128)S(1)} %get-tuple-element.57), channel_id=1, source_target_pairs={{0,12},{4,0},{8,4},{12,8},{1,13},{5,1},{9,5},{13,9},{2,14},{6,2},{... | collective-permute-start | bytes 208904 | tf_op jit(solution)/shard_map/ppermute | solution.py:566
  65.1 0.6 collective-permute-done.13.refs_1_
  65.7 2.3 %collective-permute-done.14.refs_2_ = f32[136,128]{1,0:T(8,128)S(1)} collective-permute-done((f32[136,128]{1,0:T(8,128)S(1)}, f32[136,128]{1,0:T(8,128)S(1)}, u32[]{:S(2)}, u32[]{:S(2)}) %collective-permute-start.14) | collective-permute-done | bytes 69664 | tf_op jit(solution)/shard_map/ppermute | solution.py:566
  68.0 0.9 %shard_map.120 = (f32[8,16,512]{2,1,0:T(8,128)}, f32[8,16,512]{2,1,0:T(8,128)}) custom-call(s32[1]{0:T(128)} %bitcast.me, f32[1]{0:T(128)S(6)} %copy.20.prev_mean, f32[8,16,512]{2,1,0:T(8,128)S(1)} %copy-done.2, f32[8,16,512]{2,1,0:T(8,128)S(1)} %copy-done.3, f32[136,128]{1,0:T(8,128)S(1)} %get-tuple-element.54.refs_0_, ...), custom_call_target="tpu_custom_call" | custom-call | flops 1000000 | bytes 2000000 | tf_op jit(solution)/shard_map/pallas_call | solution.py:744
  (45 shorter events, 0.5 us)
Async XLA Ops:
  0.6 1.2 %copy-start = (bf16[2,8,64,512]{3,2,1,0:T(8,128)(2,1)S(1)}, bf16[2,8,64,512]{3,2,1,0:T(8,128)(2,1)}, u32[]{:S(2)}) copy-start(bf16[2,8,64,512]{3,2,1,0:T(8,128)(2,1)} %slc.1) | copy-start | bytes 3145732
  1.9 2.5 %copy-start.1 = (bf16[2,8,64,512]{3,2,1,0:T(8,128)(2,1)S(1)}, bf16[2,8,64,512]{3,2,1,0:T(8,128)(2,1)}, u32[]{:S(2)}) copy-start(bf16[2,8,64,512]{3,2,1,0:T(8,128)(2,1)} %slc.1) | copy-start | bytes 3145732
  2.1 2.3 %collective-permute-start = (bf16[64,128]{1,0:T(8,128)(2,1)S(1)}, bf16[64,128]{1,0:T(8,128)(2,1)S(1)}, u32[]{:S(2)}, u32[]{:S(2)}) collective-permute-start(bf16[64,128]{1,0:T(8,128)(2,1)S(1)} %shard_map.113), channel_id=1, source_target_pairs={{0,1},{1,0},{2,3},{3,2},{4,5},{5,4},{6,7},{7,6},{8,9},{9,8},{10,11... | collective-permute-start | bytes 49160 | tf_op jit(solution)/shard_map/ppermute | solution.py:557
  2.6 0.7 copy-start.12
  3.4 0.7 copy-start.13
  4.1 0.8 %copy-start.7 = (f32[64,128]{1,0:T(8,128)S(1)}, f32[64,128]{1,0:T(8,128)}, u32[]{:S(2)}) copy-start(f32[64,128]{1,0:T(8,128)} %constant.34.clone.outer) | copy-start | bytes 98308
  4.9 7.8 %copy-start.2 = (f32[8,16,512]{2,1,0:T(8,128)S(1)}, f32[8,16,512]{2,1,0:T(8,128)}, u32[]{:S(2)}) copy-start(f32[8,16,512]{2,1,0:T(8,128)} %estimate.1) | copy-start | bytes 786436
  4.9 7.8 %copy-start.3 = (f32[8,16,512]{2,1,0:T(8,128)S(1)}, f32[8,16,512]{2,1,0:T(8,128)}, u32[]{:S(2)}) copy-start(f32[8,16,512]{2,1,0:T(8,128)} %direction.1) | copy-start | bytes 786436
  6.2 12.2 %collective-permute-start.2 = (bf16[1088,128]{1,0:T(8,128)(2,1)S(1)}, bf16[1088,128]{1,0:T(8,128)(2,1)S(1)}, u32[]{:S(2)}, u32[]{:S(2)}) collective-permute-start(bf16[1088,128]{1,0:T(8,128)(2,1)S(1)} %get-tuple-element.31), channel_id=1, source_target_pairs={{0,4},{4,8},{8,12},{12,0},{1,5},{5,9},{9,13},{13,1},{2,6},{6,10},{... | collective-permute-start | bytes 835592 | tf_op jit(solution)/shard_map/ppermute | solution.py:566
  8.9 14.7 %collective-permute-start.1 = (bf16[1088,128]{1,0:T(8,128)(2,1)S(1)}, bf16[1088,128]{1,0:T(8,128)(2,1)S(1)}, u32[]{:S(2)}, u32[]{:S(2)}) collective-permute-start(bf16[1088,128]{1,0:T(8,128)(2,1)S(1)} %get-tuple-element.33), channel_id=1, source_target_pairs={{0,12},{4,0},{8,4},{12,8},{1,13},{5,1},{9,5},{13,9},{2,14},{6,2},{... | collective-permute-start | bytes 835592 | tf_op jit(solution)/shard_map/ppermute | solution.py:566
  11.0 16.0 %collective-permute-start.5 = (bf16[272,128]{1,0:T(8,128)(2,1)S(1)}, bf16[272,128]{1,0:T(8,128)(2,1)S(1)}, u32[]{:S(2)}, u32[]{:S(2)}) collective-permute-start(bf16[272,128]{1,0:T(8,128)(2,1)S(1)} %bitcast.19), channel_id=1, source_target_pairs={{0,2},{2,0},{1,3},{3,1},{4,6},{6,4},{5,7},{7,5},{8,10},{10,8},{9,1... | collective-permute-start | bytes 208904 | tf_op jit(solution)/shard_map/ppermute | solution.py:639
  13.4 10.2 %copy-start.8 = (bf16[3,128,128]{2,1,0:T(8,128)(2,1)}, bf16[3,128,128]{2,1,0:T(8,128)(2,1)S(1)}, u32[]{:S(2)}) copy-start(bf16[3,128,128]{2,1,0:T(8,128)(2,1)S(1)} %get-tuple-element.47) | copy-start | bytes 294916
  13.4 10.2 %copy-start.10 = (bf16[3,128,128]{2,1,0:T(8,128)(2,1)}, bf16[3,128,128]{2,1,0:T(8,128)(2,1)S(1)}, u32[]{:S(2)}) copy-start(bf16[3,128,128]{2,1,0:T(8,128)(2,1)S(1)} %get-tuple-element.46) | copy-start | bytes 294916
  23.6 5.2 %copy-start.4 = (bf16[256,128]{1,0:T(8,128)(2,1)S(1)}, bf16[256,128]{1,0:T(8,128)(2,1)}, u32[]{:S(2)}) copy-start(bf16[256,128]{1,0:T(8,128)(2,1)} %constant.37.clone.rim_band) | copy-start | bytes 196612
  23.6 5.2 %copy-start.5 = (bf16[256,128]{1,0:T(8,128)(2,1)S(1)}, bf16[256,128]{1,0:T(8,128)(2,1)}, u32[]{:S(2)}) copy-start(bf16[256,128]{1,0:T(8,128)(2,1)} %constant.36.clone.band) | copy-start | bytes 196612
  23.7 5.1 %collective-permute-start.4 = (bf16[544,128]{1,0:T(8,128)(2,1)S(1)}, bf16[544,128]{1,0:T(8,128)(2,1)S(1)}, u32[]{:S(2)}, u32[]{:S(2)}) collective-permute-start(bf16[544,128]{1,0:T(8,128)(2,1)S(1)} %pad_maximum_fusion), channel_id=1, source_target_pairs={{0,2},{2,0},{1,3},{3,1},{4,6},{6,4},{5,7},{7,5},{8,10},{10,8},{9,1... | collective-permute-start | bytes 417800 | tf_op jit(solution)/shard_map/ppermute | solution.py:639
  25.2 14.6 %collective-permute-start.3 = (bf16[1088,128]{1,0:T(8,128)(2,1)S(1)}, bf16[1088,128]{1,0:T(8,128)(2,1)S(1)}, u32[]{:S(2)}, u32[]{:S(2)}) collective-permute-start(bf16[1088,128]{1,0:T(8,128)(2,1)S(1)} %get-tuple-element.36), channel_id=1, source_target_pairs={{0,8},{4,12},{8,0},{12,4},{1,9},{5,13},{9,1},{13,5},{2,10},{6,14},... | collective-permute-start | bytes 835592 | tf_op jit(solution)/shard_map/ppermute | solution.py:566
  26.7 2.1 %copy-start.6 = (bf16[96,96]{1,0:T(8,128)(2,1)S(1)}, bf16[96,96]{1,0:T(8,128)(2,1)}, u32[]{:S(2)}) copy-start(bf16[96,96]{1,0:T(8,128)(2,1)} %constant.35.clone.order) | copy-start | bytes 55300
  39.9 3.3 %copy-start.11 = (bf16[3,128,128]{2,1,0:T(8,128)(2,1)S(1)}, bf16[3,128,128]{2,1,0:T(8,128)(2,1)}, u32[]{:S(2)}) copy-start(bf16[3,128,128]{2,1,0:T(8,128)(2,1)} %copy-done.10) | copy-start | bytes 294916
  39.9 3.3 %copy-start.9 = (bf16[3,128,128]{2,1,0:T(8,128)(2,1)S(1)}, bf16[3,128,128]{2,1,0:T(8,128)(2,1)}, u32[]{:S(2)}) copy-start(bf16[3,128,128]{2,1,0:T(8,128)(2,1)} %copy-done.8) | copy-start | bytes 294916
  40.3 4.4 %collective-permute-start.9 = (bf16[272,128]{1,0:T(8,128)(2,1)S(1)}, bf16[272,128]{1,0:T(8,128)(2,1)S(1)}, u32[]{:S(2)}, u32[]{:S(2)}) collective-permute-start(bf16[272,128]{1,0:T(8,128)(2,1)S(1)} %bitcast.20), channel_id=1, source_target_pairs={{0,2},{2,0},{1,3},{3,1},{4,6},{6,4},{5,7},{7,5},{8,10},{10,8},{9,1... | collective-permute-start | bytes 208904 | tf_op jit(solution)/shard_map/ppermute | solution.py:639
  40.9 12.5 %collective-permute-start.6 = (bf16[3,128,128]{2,1,0:T(8,128)(2,1)}, bf16[3,128,128]{2,1,0:T(8,128)(2,1)S(1)}, u32[]{:S(2)}, u32[]{:S(2)}) collective-permute-start(bf16[3,128,128]{2,1,0:T(8,128)(2,1)} %get-tuple-element.45), channel_id=1, source_target_pairs={{0,12},{4,0},{8,4},{12,8},{1,13},{5,1},{9,5},{13,9},{2,14},{6,2},{... | collective-permute-start | bytes 294920 | tf_op jit(solution)/shard_map/ppermute | solution.py:566
  43.2 10.1 %collective-permute-start.7 = (bf16[3,128,128]{2,1,0:T(8,128)(2,1)S(1)}, bf16[3,128,128]{2,1,0:T(8,128)(2,1)S(1)}, u32[]{:S(2)}, u32[]{:S(2)}) collective-permute-start(bf16[3,128,128]{2,1,0:T(8,128)(2,1)S(1)} %copy-done.11), channel_id=1, source_target_pairs={{0,8},{4,12},{8,0},{12,4},{1,9},{5,13},{9,1},{13,5},{2,10},{6,14},... | collective-permute-start | bytes 294920 | tf_op jit(solution)/shard_map/ppermute | solution.py:566
  43.2 10.1 %collective-permute-start.8 = (bf16[3,128,128]{2,1,0:T(8,128)(2,1)S(1)}, bf16[3,128,128]{2,1,0:T(8,128)(2,1)S(1)}, u32[]{:S(2)}, u32[]{:S(2)}) collective-permute-start(bf16[3,128,128]{2,1,0:T(8,128)(2,1)S(1)} %copy-done.9), channel_id=1, source_target_pairs={{0,4},{4,8},{8,12},{12,0},{1,5},{5,9},{9,13},{13,1},{2,6},{6,10},{... | collective-permute-start | bytes 294920 | tf_op jit(solution)/shard_map/ppermute | solution.py:566
  55.1 1.4 %collective-permute-start.12 = (f32[8,128]{1,0:T(8,128)S(1)}, f32[8,128]{1,0:T(8,128)S(1)}, u32[]{:S(2)}, u32[]{:S(2)}) collective-permute-start(f32[8,128]{1,0:T(8,128)S(1)} %get-tuple-element.53.refs_0_), channel_id=1, source_target_pairs={{0,3},{1,0},{2,1},{3,2},{4,7},{5,4},{6,5},{7,6},{8,11},{9,8},{10,9... | collective-permute-start | bytes 12296 | tf_op jit(solution)/shard_map/ppermute | solution.py:733
  55.1 3.7 %collective-permute-start.11 = (f32[8,128]{1,0:T(8,128)S(1)}, f32[8,128]{1,0:T(8,128)S(1)}, u32[]{:S(2)}, u32[]{:S(2)}) collective-permute-start(f32[8,128]{1,0:T(8,128)S(1)} %get-tuple-element.53.refs_0_), channel_id=1, source_target_pairs={{0,2},{1,3},{2,0},{3,1},{4,6},{5,7},{6,4},{7,5},{8,10},{9,11},{10,... | collective-permute-start | bytes 12296 | tf_op jit(solution)/shard_map/ppermute | solution.py:733
  55.9 3.0 %collective-permute-start.10 = (f32[8,128]{1,0:T(8,128)S(1)}, f32[8,128]{1,0:T(8,128)S(1)}, u32[]{:S(2)}, u32[]{:S(2)}) collective-permute-start(f32[8,128]{1,0:T(8,128)S(1)} %get-tuple-element.53.refs_0_), channel_id=1, source_target_pairs={{0,1},{1,2},{2,3},{3,0},{4,5},{5,6},{6,7},{7,4},{8,9},{9,10},{10,1... | collective-permute-start | bytes 12296 | tf_op jit(solution)/shard_map/ppermute | solution.py:733
  59.0 6.7 %collective-permute-start.13 = (f32[136,128]{1,0:T(8,128)S(1)}, f32[136,128]{1,0:T(8,128)S(1)}, u32[]{:S(2)}, u32[]{:S(2)}) collective-permute-start(f32[136,128]{1,0:T(8,128)S(1)} %get-tuple-element.55), channel_id=1, source_target_pairs={{0,4},{4,8},{8,12},{12,0},{1,5},{5,9},{9,13},{13,1},{2,6},{6,10},{... | collective-permute-start | bytes 208904 | tf_op jit(solution)/shard_map/ppermute | solution.py:566
  62.0 6.0 %collective-permute-start.14 = (f32[136,128]{1,0:T(8,128)S(1)}, f32[136,128]{1,0:T(8,128)S(1)}, u32[]{:S(2)}, u32[]{:S(2)}) collective-permute-start(f32[136,128]{1,0:T(8,128)S(1)} %get-tuple-element.56), channel_id=1, source_target_pairs={{0,8},{4,12},{8,0},{12,4},{1,9},{5,13},{9,1},{13,5},{2,10},{6,14},... | collective-permute-start | bytes 208904 | tf_op jit(solution)/shard_map/ppermute | solution.py:566
  62.9 5.1 %collective-permute-start.15 = (f32[136,128]{1,0:T(8,128)S(1)}, f32[136,128]{1,0:T(8,128)S(1)}, u32[]{:S(2)}, u32[]{:S(2)}) collective-permute-start(f32[136,128]{1,0:T(8,128)S(1)} %get-tuple-element.57), channel_id=1, source_target_pairs={{0,12},{4,0},{8,4},{12,8},{1,13},{5,1},{9,5},{13,9},{2,14},{6,2},{... | collective-permute-start | bytes 208904 | tf_op jit(solution)/shard_map/ppermute | solution.py:566

commit v15 on v14

--- a/solution.py
+++ b/solution.py
@@ -182,7 +182,7 @@
     return jnp.where((lane >= target) & (lane < target + RADIUS), moved, total)
 
 
-def pack_kernel(me, present, slc, params, outer, before, after, *refs):
+def pack_kernel(me, present, slc, params, before, after, *refs):
     messages, strips = refs[:-1], refs[-1]
     tiles = len(messages)
     epochs = slc.shape[1]
@@ -195,15 +195,15 @@
     third = PARAM_LANE + 2 * SLOTS
     split = jnp.where(lane < third, high, jnp.where(lane < third + SLOTS, middle, low))
     split = jnp.where(lane >= PARAM_LANE, split, 0.0)
-    sides = outer[...]
+    inside = lane < 2 * epochs * SIDES
     for tile in range(tiles):
         total = split
         if tile == 0:
             edge = before[...].astype(jnp.float32) * present[0]
-            total = jnp.where(sides == 1.0, edge, total)
+            total = jnp.where(inside & (lane % SIDES < RADIUS), edge, total)
         if tile == tiles - 1:
             edge = after[...].astype(jnp.float32) * present[1]
-            total = jnp.where(sides == 2.0, edge, total)
+            total = jnp.where(inside & (lane % SIDES >= RADIUS), edge, total)
         for part in range(2):
             for epoch in range(epochs):
                 at = (part * epochs + epoch) * SIDES
@@ -393,12 +393,13 @@
     keep = jnp.where(at < HALO, present[0], jnp.where(at >= HALO + rows, present[1], 1.0))
     order = (order[...].astype(jnp.float32) * keep).astype(jnp.bfloat16)
     bands = band[...], rim_band[...]
-    for block, (tile_at, top_at, bottom_at, halo_row) in enumerate(places):
+    for block, (tile_at, top_at, bottom_at, top_row, bottom_row) in enumerate(places):
         tile, top, bottom = inputs[tile_at], inputs[top_at], inputs[bottom_at]
 
         def rows_of(at):
-            border = slice(halo_row + at * HALO, halo_row + (at + 1) * HALO)
-            return jnp.concatenate([top[border, :], tile[at * rows : (at + 1) * rows, :], bottom[border, :]], axis=0)
+            above = top[top_row + at * HALO : top_row + (at + 1) * HALO, :]
+            below = bottom[bottom_row + at * HALO : bottom_row + (at + 1) * HALO, :]
+            return jnp.concatenate([above, tile[at * rows : (at + 1) * rows, :], below], axis=0)
 
         first = [part * total + block * epochs + epoch for part in range(2) for epoch in range(epochs)]
         unpack_tiles(order, range(2 * epochs), main, first, rows_of)
@@ -406,17 +407,15 @@
         unpack_rims(by_look, looks, rim, first)
     power_batches(count, epochs, looks, main, rim, looked, rim_looked)
     powers = (count + 1) // 2
-    last = powers + own_total // 2 - 1
+    couples = own_total // 2
 
     def boxed_of(channel):
         return boxed[pl.ds(pl.multiple_of(channel * look_rows, look_rows), look_rows), :]
 
-    @pl.loop(0, last + 3)
-    def _(turn):
-        done = clipped(turn - 2 - powers, own_total // 2 - 1)
+    def finished(couple):
         results = []
         for one in range(2):
-            epoch = done * 2 + one
+            epoch = couple * 2 + one
             own_power = boxed_of(epoch)
             first = (2 * powers + epoch) * (group * look_rows)
             parts = boxed[pl.ds(pl.multiple_of(first, group * look_rows), group * look_rows), :]
@@ -428,18 +427,42 @@
                 unit_im = parts[SLOTS + slot] * inverse
                 factor = weight[pair] * (unit_re * unit_re + unit_im * unit_im)
                 results.append((factor, factor * unit_im))
-        summed = clipped(turn - 1, last)
-        sums = [rows_summed(summed * 2 * group + one, looks, look_rows, wide) for one in range(2 * group)]
-        couple = clipped(turn, last)
-        columns = columns_summed(couple, looks, bands, looked, rim_looked)
-        here = clipped(turn, own_total // 2 - 1)
-        products, rims = pair_couple(here, total, partner, main, rim)
-        for ref, values in zip((factors, pulls), zip(*results)):
-            ref[pl.ds(done * 2 * SLOTS, 2 * SLOTS)] = jnp.stack(values)
-        put(boxed, summed, sums)
-        put(wide, couple, columns)
-        put(looked, powers + here, products)
-        put(rim_looked, powers + here, rims)
+        return results
+
+    def boxes(couple):
+        return [rows_summed(couple * 2 * group + one, looks, look_rows, wide) for one in range(2 * group)]
+
+    def turn(number, steps):
+        if 3 in steps:
+            results = finished(number - 3)
+        if 2 in steps:
+            sums = boxes(powers + number - 2)
+        if 1 in steps:
+            columns = columns_summed(powers + number - 1, looks, bands, looked, rim_looked)
+        if 0 in steps:
+            products, rims = pair_couple(number, total, partner, main, rim)
+        if 3 in steps:
+            for ref, values in zip((factors, pulls), zip(*results)):
+                ref[pl.ds((number - 3) * 2 * SLOTS, 2 * SLOTS)] = jnp.stack(values)
+        if 2 in steps:
+            put(boxed, powers + number - 2, sums)
+        if 1 in steps:
+            put(wide, powers + number - 1, columns)
+        if 0 in steps:
+            put(looked, powers + number, products)
+            put(rim_looked, powers + number, rims)
+
+    for couple in range(powers):
+        put(wide, couple, columns_summed(couple, looks, bands, looked, rim_looked))
+    turn(0, (0,))
+    for couple in range(powers):
+        put(boxed, couple, boxes(couple))
+    turn(1, (0, 1))
+    turn(2, (0, 1, 2))
+    pl.loop(3, couples)(lambda number: turn(number, (0, 1, 2, 3)))
+    turn(couples, (1, 2, 3))
+    turn(couples + 1, (2, 3))
+    turn(couples + 2, (3,))
 
 
 def gradient_kernel(sizes, partner, *refs):
@@ -598,24 +621,42 @@
     params = jnp.zeros((rows, LANES), f32)
     listed = jnp.concatenate([offsets.astype(f32), weights, weights, weights], axis=1)
     params = lax.dynamic_update_slice(params, listed, (0, PARAM_LANE))
-    lane = np.arange(LANES)
-    sides = np.where(lane < 2 * epochs * SIDES, np.where(lane % SIDES < RADIUS, 1.0, 2.0), 0.0)
-    sides = jnp.asarray(np.broadcast_to(sides, (rows, LANES)), f32)
     sub_present = jnp.stack([sub > 0, sub < lax.axis_size("sub") - 1]).astype(f32)
     messages = pl.pallas_call(
         pack_kernel,
         out_shape=(jax.ShapeDtypeStruct((tile_rows + rows, LANES), bf16),) * tiles,
-        in_specs=[SMEM] * 2 + [VMEM] * 5,
+        in_specs=[SMEM] * 2 + [VMEM] * 4,
         out_specs=(VMEM,) * tiles,
         scratch_shapes=[pltpu.VMEM((tiles, rows, LANES), bf16)],
         compiler_params=params_of,
         cost_estimate=pl.CostEstimate(flops=3_000_000, bytes_accessed=4_000_000, transcendentals=0),
-    )(me.reshape(1), sub_present, slc, params, sides, before, after)
+    )(me.reshape(1), sub_present, slc, params, before, after)
+    space = lax.axis_index("space")
+    spaces = lax.axis_size("space")
+    present = jnp.stack([space > 0, space < spaces - 1]).astype(f32)
+
+    def halo(pieces):
+        def border(from_row):
+            cuts = [lax.dynamic_slice_in_dim(piece, from_row, HALO, axis=1).reshape(-1, LANES) for piece in pieces]
+            return jnp.concatenate(cuts, axis=0)
+
+        if spaces == 2:
+            got = lax.ppermute(border(jnp.where(space == 0, rows - HALO, 0)), "space", [(0, 1), (1, 0)])
+            return got, got
+        return swapped(border(rows - HALO), border(0), "space")
+
     beside = [tiles - 1, 0, 1]
     far = list(range(2, tiles - 1))
     block = {0: messages[0], 1: fetched(messages, 1), tiles - 1: fetched(messages, tiles - 1)}
-    held = lax.optimization_barrier((messages, block[1], block[tiles - 1]))[0]
-    block.update({shift: fetched(held, shift) for shift in far})
+    early = {0: halo([messages[0].reshape(-1, rows, LANES)])}
+    ready = lax.optimization_barrier((messages, block[1]))[0]
+    early.update({shift: halo([ready[shift].reshape(-1, rows, LANES)]) for shift in far})
+    sent = {shift: messages[shift] for shift in far}
+    for shift in far:
+        borders = early[shift][:1] if spaces == 2 else early[shift]
+        sent[shift] = jnp.concatenate((messages[shift],) + borders, axis=0)
+    sent = lax.optimization_barrier((sent, block[1], block[tiles - 1]))[0]
+    block.update({shift: fetched(sent, shift) for shift in far})
 
     estimate, direction, _ = lax.optimization_barrier((estimate, direction, messages))
     fields = pl.pallas_call(
@@ -626,20 +667,6 @@
         compiler_params=params_of,
         cost_estimate=pl.CostEstimate(flops=1_000_000, bytes_accessed=2_000_000, transcendentals=0),
     )(me.reshape(1), estimate, direction)
-    space = lax.axis_index("space")
-    spaces = lax.axis_size("space")
-    present = jnp.stack([space > 0, space < spaces - 1]).astype(f32)
-
-    def halo(pieces):
-        def border(from_row):
-            cuts = [lax.dynamic_slice_in_dim(piece, from_row, HALO, axis=1).reshape(-1, LANES) for piece in pieces]
-            return jnp.concatenate(cuts, axis=0)
-
-        if spaces == 2:
-            got = lax.ppermute(border(jnp.where(space == 0, rows - HALO, 0)), "space", [(0, 1), (1, 0)])
-            return got, got
-        return swapped(border(rows - HALO), border(0), "space")
-
     def by_rows(shift):
         return block[shift].reshape(-1, rows, LANES)
 
@@ -652,9 +679,12 @@
         weight = listed[:, SLOTS : 2 * SLOTS] + listed[:, 2 * SLOTS : 3 * SLOTS] + listed[:, 3 * SLOTS :]
         return mate.reshape(-1), weight.reshape(-1)
 
-    own_halo = halo([by_rows(0)])
+    border_rows = (2 * epochs + 1) * HALO
     near_halo = halo([by_rows(1), by_rows(tiles - 1)])
-    halos = {0: (own_halo, 0), 1: (near_halo, 0), tiles - 1: (near_halo, 1)}
+    halos = {0: early[0] + (0, 0), 1: near_halo + (0, 0), tiles - 1: near_halo + (border_rows, border_rows)}
+    for shift in far:
+        bottom_at = tile_rows + rows if spaces == 2 else tile_rows + rows + border_rows
+        halos[shift] = block[shift], block[shift], tile_rows + rows, bottom_at
 
     order = look_order(rows + 2 * HALO, HALO // LOOK - RADIUS)
     bands = column_bands()
@@ -675,9 +705,8 @@
 
         places = []
         for shift in loaded:
-            (top, bottom), slot = halos[shift]
-            place = index_of(block[shift]), index_of(top), index_of(bottom), slot * (2 * epochs + 1) * HALO
-            places.append(place)
+            top, bottom, top_row, bottom_row = halos[shift]
+            places.append((index_of(block[shift]), index_of(top), index_of(bottom), top_row, bottom_row))
         here = len(loaded) * epochs
         owned = len(own) * epochs
         looks = (rows + 2 * HALO) // LOOK
@@ -704,10 +733,7 @@
     near_stage = beside
     far_stage = list(range(1, tiles))
     near_pairs = pair_stage(near_stage)
-    held, fields, near_pairs = lax.optimization_barrier(([block[shift] for shift in far], fields, near_pairs))
-    block.update(zip(far, held))
-    far_halo = halo([by_rows(shift) for shift in far])
-    halos.update({shift: (far_halo, at) for at, shift in enumerate(far)})
+    fields, near_pairs = lax.optimization_barrier((fields, near_pairs))
     field = [fields[0]] + [fetched(fields, shift) for shift in range(1, tiles)]
     far_pairs = pair_stage(far_stage)
 

time: 69.2 us -> 71.8 us (1.038)
  waiting for transfers between devices: 20.9 us -> 29 us
  Pallas kernels: 22.2 us -> 15.5 us
  other arithmetic: 0.71 us -> 2.06 us
    ppermute x9, waiting for transfers between devices: 15.4 us -> 23.3 us  [to_ahead(): return lax.ppermute(x, axis, [(i, (i + by) % size) for i in range(size)])]
    pallas_call x2, Pallas kernels: 17.4 us -> 11.2 us  [pair_stage(): pl.pallas_call(functools.partial(pair_kernel, (epochs, rows, len(operands...]
    ppermute x9, starting transfers between devices: 14.4 us -> 13.6 us  [to_ahead(): return lax.ppermute(x, axis, [(i, (i + by) % size) for i in range(size)])]
    concatenate x0 -> x1, other arithmetic: none -> 0.76 us  [transposed_plan(): sent[shift] = jnp.concatenate((messages[shift],) + borders, axis=0)]
    ppermute x3, starting transfers between devices: 1.03 us -> 1.77 us  [transposed_plan(): lax.ppermute(sums, place, [(i, (i + by) % count) for i in range(count)])]
    unnamed x30 -> x26, local copies, waits for them, and re-layouts: 3.3 us -> 3.19 us
  transfers between devices with their start and end apart: 16 -> 16, of which waited for: 10 -> 8; matrix products, arithmetic and copies ran while one was open for 1% -> 4% of each run, Pallas kernels for 26% -> 16%
where the time goes in v15:
time: 71.8 us; the launch traced here: 71.5 us
  waiting for transfers between devices  29 us (40%)
  starting transfers between devices  19.8 us (28%)
  Pallas kernels  15.5 us (22%)
  local copies, waits for them, and re-layouts  3.69 us (5%)
  other arithmetic  2.06 us (3%)
  between operations  1.5 us (2%)
    ppermute x9, waiting for transfers between devices, to_ahead(): return lax.ppermute(x, axis, [(i, (i + by) % size) for i in range(size)])  23.3 us
    ppermute x9, starting transfers between devices, to_ahead(): return lax.ppermute(x, axis, [(i, (i + by) % size) for i in range(size)])  13.6 us
    pallas_call x2, Pallas kernels, pair_stage(): pl.pallas_call(functools.partial(pair_kernel, (epochs, rows, len(operands...  11.2 us
    ppermute x3, starting transfers between devices, halo(): lax.ppermute(border(jnp.where(space == 0, rows - HALO, 0)), 'space', [(0,...  3.86 us
    unnamed x26, local copies, waits for them, and re-layouts  3.19 us
    ppermute x3, waiting for transfers between devices, halo(): lax.ppermute(border(jnp.where(space == 0, rows - HALO, 0)), 'space', [(0,...  2.88 us
    ppermute x3, waiting for transfers between devices, transposed_plan(): lax.ppermute(sums, place, [(i, (i + by) % count) for i in range(count)])  2.87 us
    ppermute x3, starting transfers between devices, transposed_plan(): lax.ppermute(sums, place, [(i, (i + by) % count) for i in range(count)])  1.77 us
  transfers between devices with their start and end apart: 16, of which 8 were waited for; matrix products, arithmetic and copies ran while one was open for 4% of the time, Pallas kernels for 16%

profile of v15, /device:TPU:0, one launch (start us, length us, event | category | flops | bytes accessed | tf_op | source)
XLA Modules:
  0.0 71.5 jit_solution(8822054217248755156)
XLA Ops:
  0.6 1.2 %copy-done = bf16[2,8,64,512]{3,2,1,0:T(8,128)(2,1)S(1)} copy-done((bf16[2,8,64,512]{3,2,1,0:T(8,128)(2,1)S(1)}, bf16[2,8,64,512]{3,2,1,0:T(8,128)(2,1)}, u32[]{:S(2)}) %copy-start) | copy-done | bytes 1048600
  1.9 0.2 shard_map.104
  2.1 0.5 collective-permute-start
  2.6 0.7 copy-done.10
  3.3 0.1 copy.15
  3.4 0.7 copy-done.11
  4.1 0.1 copy.16
  4.1 0.1 add_convert_fusion.1.present
  4.2 0.1 select_maximum_fusion.params
  4.3 0.1 add_convert_fusion.present
  4.4 1.3 %shard_map.105 = (bf16[1088,128]{1,0:T(8,128)(2,1)S(1)}, bf16[1088,128]{1,0:T(8,128)(2,1)S(1)}, bf16[1088,128]{1,0:T(8,128)(2,1)S(1)}, bf16[1088,128]{1,0:T(8,128)(2,1)S(1)}) custom-call(s32[1]{0:T(128)} %bitcast.me, f32[2]{0:T(128)S(1)} %add_convert_fusion.present, bf16[2,8,64,512]{3,2,1,0:T(8,128)(2,1)S(1)} %copy-done.1, ...), custom_call_target="tpu_custom_call" | custom-call | flops 3000000 | bytes 4000000 | tf_op jit(solution)/shard_map/pallas_call | solution.py:625
  5.7 2.7 %collective-permute-start.3 = (bf16[1088,128]{1,0:T(8,128)(2,1)S(1)}, bf16[1088,128]{1,0:T(8,128)(2,1)S(1)}, u32[]{:S(2)}, u32[]{:S(2)}) collective-permute-start(bf16[1088,128]{1,0:T(8,128)(2,1)S(1)} %get-tuple-element.31), channel_id=1, source_target_pairs={{0,4},{4,8},{8,12},{12,0},{1,5},{5,9},{9,13},{13,1},{2,6},{6,10},{... | collective-permute-start | bytes 835592 | tf_op jit(solution)/shard_map/ppermute | solution.py:589
  8.3 2.1 %collective-permute-start.1 = (bf16[1088,128]{1,0:T(8,128)(2,1)S(1)}, bf16[1088,128]{1,0:T(8,128)(2,1)S(1)}, u32[]{:S(2)}, u32[]{:S(2)}) collective-permute-start(bf16[1088,128]{1,0:T(8,128)(2,1)S(1)} %get-tuple-element.33), channel_id=1, source_target_pairs={{0,12},{4,0},{8,4},{12,8},{1,13},{5,1},{9,5},{13,9},{2,14},{6,2},{... | collective-permute-start | bytes 835592 | tf_op jit(solution)/shard_map/ppermute | solution.py:589
  10.4 1.7 %collective-permute-start.6 = (bf16[272,128]{1,0:T(8,128)(2,1)S(1)}, bf16[272,128]{1,0:T(8,128)(2,1)S(1)}, u32[]{:S(2)}, u32[]{:S(2)}) collective-permute-start(bf16[272,128]{1,0:T(8,128)(2,1)S(1)} %bitcast.19), channel_id=1, source_target_pairs={{0,2},{2,0},{1,3},{3,1},{4,6},{6,4},{5,7},{7,5},{8,10},{10,8},{9,1... | collective-permute-start | bytes 208904 | tf_op jit(solution)/shard_map/ppermute | solution.py:644
  12.1 0.1 shard_map.106
  12.2 0.1 slice_convert_fusion.3
  12.3 5.6 %collective-permute-done.3.refs_0_.refs_3_ = bf16[1088,128]{1,0:T(8,128)(2,1)S(1)} collective-permute-done((bf16[1088,128]{1,0:T(8,128)(2,1)S(1)}, bf16[1088,128]{1,0:T(8,128)(2,1)S(1)}, u32[]{:S(2)}, u32[]{:S(2)}) %collective-permute-start.3) | collective-permute-done | bytes 278560 | tf_op jit(solution)/shard_map/ppermute | solution.py:589
  17.9 5.1 %collective-permute-done.1.refs_4_.refs_0_ = bf16[1088,128]{1,0:T(8,128)(2,1)S(1)} collective-permute-done((bf16[1088,128]{1,0:T(8,128)(2,1)S(1)}, bf16[1088,128]{1,0:T(8,128)(2,1)S(1)}, u32[]{:S(2)}, u32[]{:S(2)}) %collective-permute-start.1) | collective-permute-done | bytes 278560 | tf_op jit(solution)/shard_map/ppermute | solution.py:589
  23.1 1.6 %collective-permute-start.2 = (bf16[272,128]{1,0:T(8,128)(2,1)S(1)}, bf16[272,128]{1,0:T(8,128)(2,1)S(1)}, u32[]{:S(2)}, u32[]{:S(2)}) collective-permute-start(bf16[272,128]{1,0:T(8,128)(2,1)S(1)} %bitcast.20), channel_id=1, source_target_pairs={{0,2},{2,0},{1,3},{3,1},{4,6},{6,4},{5,7},{7,5},{8,10},{10,8},{9,1... | collective-permute-start | bytes 208904 | tf_op jit(solution)/shard_map/ppermute | solution.py:644
  24.7 0.6 collective-permute-start.5
  25.4 2.9 %collective-permute-done.2 = bf16[272,128]{1,0:T(8,128)(2,1)S(1)} collective-permute-done((bf16[272,128]{1,0:T(8,128)(2,1)S(1)}, bf16[272,128]{1,0:T(8,128)(2,1)S(1)}, u32[]{:S(2)}, u32[]{:S(2)}) %collective-permute-start.2) | collective-permute-done | bytes 69664 | tf_op jit(solution)/shard_map/ppermute | solution.py:644
  28.2 0.8 %pad_maximum_fusion = bf16[1360,128]{1,0:T(8,128)(2,1)} fusion(bf16[272,128]{1,0:T(8,128)(2,1)S(1)} %collective-permute-done.2, bf16[1088,128]{1,0:T(8,128)(2,1)S(1)} %get-tuple-element.36), kind=kLoop, calls=%fused_computation | loop fusion | flops 696320 | bytes 696320 | tf_op jit(solution)/shard_map/concatenate | solution.py:657
  29.0 1.3 %collective-permute-start.4 = (bf16[1360,128]{1,0:T(8,128)(2,1)}, bf16[1360,128]{1,0:T(8,128)(2,1)S(1)}, u32[]{:S(2)}, u32[]{:S(2)}) collective-permute-start(bf16[1360,128]{1,0:T(8,128)(2,1)} %pad_maximum_fusion), channel_id=1, source_target_pairs={{0,8},{4,12},{8,0},{12,4},{1,9},{5,13},{9,1},{13,5},{2,10},{6,14},... | collective-permute-start | bytes 1044488 | tf_op jit(solution)/shard_map/ppermute | solution.py:589
  30.3 0.7 slice_convert_fusion.2
  31.0 0.1 fusion.14
  31.1 0.1 reshape.53.weight
  31.2 0.1 reshape.52.partner
  31.3 0.4 copy-done.6
  31.7 5.6 %shard_map.107 = (f32[64,16,128]{2,1,0:T(8,128)S(1)}, f32[64,16,128]{2,1,0:T(8,128)S(1)}) custom-call(s32[64]{0:T(128)S(1)} %reshape.52.partner, f32[64]{0:T(128)S(1)} %reshape.53.weight, f32[2]{0:T(128)S(1)} %add_convert_fusion.1.present, bf16[96,96]{1,0:T(8,128)(2,1)S(1)} %copy-done.6, bf16[256,128]{1,0:T(8,128)(2,1)S(1)} %copy-done.5, ...), custom_call_target="tpu_custom_call" | custom-call | flops 20000000 | bytes 30000000 | tf_op jit(solution)/shard_map/pallas_call | solution.py:716
  37.4 1.9 %collective-permute-start.7 = (bf16[3,128,128]{2,1,0:T(8,128)(2,1)S(1)}, bf16[3,128,128]{2,1,0:T(8,128)(2,1)S(1)}, u32[]{:S(2)}, u32[]{:S(2)}) collective-permute-start(bf16[3,128,128]{2,1,0:T(8,128)(2,1)S(1)} %get-tuple-element.45), channel_id=1, source_target_pairs={{0,12},{4,0},{8,4},{12,8},{1,13},{5,1},{9,5},{13,9},{2,14},{6,2},{... | collective-permute-start | bytes 294920 | tf_op jit(solution)/shard_map/ppermute | solution.py:589
  39.3 1.1 %collective-permute-start.8 = (bf16[3,128,128]{2,1,0:T(8,128)(2,1)S(1)}, bf16[3,128,128]{2,1,0:T(8,128)(2,1)S(1)}, u32[]{:S(2)}, u32[]{:S(2)}) collective-permute-start(bf16[3,128,128]{2,1,0:T(8,128)(2,1)S(1)} %get-tuple-element.46), channel_id=1, source_target_pairs={{0,8},{4,12},{8,0},{12,4},{1,9},{5,13},{9,1},{13,5},{2,10},{6,14},... | collective-permute-start | bytes 294920 | tf_op jit(solution)/shard_map/ppermute | solution.py:589
  40.4 0.6 collective-permute-start.9
  41.0 9.7 %collective-permute-done.4.refs_2_ = bf16[1360,128]{1,0:T(8,128)(2,1)S(1)} collective-permute-done((bf16[1360,128]{1,0:T(8,128)(2,1)}, bf16[1360,128]{1,0:T(8,128)(2,1)S(1)}, u32[]{:S(2)}, u32[]{:S(2)}) %collective-permute-start.4) | collective-permute-done | bytes 348192 | tf_op jit(solution)/shard_map/ppermute | solution.py:589
  50.8 0.1 fusion.7
  50.9 0.1 reshape.51.partner
  51.0 0.1 reshape.61.weight
  51.1 0.1 reshape.60.partner
  51.2 5.6 %shard_map.108 = (f32[64,16,128]{2,1,0:T(8,128)S(1)}, f32[64,16,128]{2,1,0:T(8,128)S(1)}) custom-call(s32[64]{0:T(128)S(1)} %reshape.60.partner, f32[64]{0:T(128)S(1)} %reshape.61.weight, f32[2]{0:T(128)S(1)} %add_convert_fusion.1.present, bf16[96,96]{1,0:T(8,128)(2,1)S(1)} %copy-done.6, bf16[256,128]{1,0:T(8,128)(2,1)S(1)} %copy-done.5, ...), custom_call_target="tpu_custom_call" | custom-call | flops 20000000 | bytes 30000000 | tf_op jit(solution)/shard_map/pallas_call | solution.py:716
  56.9 1.7 %shard_map.109 = (f32[32,16,128]{2,1,0:T(8,128)S(1)}, f32[8,128]{1,0:T(8,128)S(1)}) custom-call(s32[128]{0:T(128)S(1)} %reshape.51.partner, bf16[3,128,128]{2,1,0:T(8,128)(2,1)S(1)} %get-tuple-element.44.refs_0_, bf16[3,128,128]{2,1,0:T(8,128)(2,1)S(1)} %collective-permute-done.7.refs_1_, bf16[3,128,128]{2,1,0:T(8,128)(2,1)S(1)} %collective-permute-done.8.refs_2_, ...), custom_call_target="tpu_custom_call" | custom-call | flops 10000000 | bytes 8000000 | tf_op jit(solution)/shard_map/pallas_call | solution.py:744
  58.7 1.5 %collective-permute-start.11 = (f32[8,128]{1,0:T(8,128)S(1)}, f32[8,128]{1,0:T(8,128)S(1)}, u32[]{:S(2)}, u32[]{:S(2)}) collective-permute-start(f32[8,128]{1,0:T(8,128)S(1)} %get-tuple-element.53.refs_0_), channel_id=1, source_target_pairs={{0,2},{1,3},{2,0},{3,1},{4,6},{5,7},{6,4},{7,5},{8,10},{9,11},{10,... | collective-permute-start | bytes 12296 | tf_op jit(solution)/shard_map/ppermute | solution.py:759
  60.2 0.2 collective-permute-start.10
  60.4 2.0 %collective-permute-done.11.refs_2_ = f32[8,128]{1,0:T(8,128)S(1)} collective-permute-done((f32[8,128]{1,0:T(8,128)S(1)}, f32[8,128]{1,0:T(8,128)S(1)}, u32[]{:S(2)}, u32[]{:S(2)}) %collective-permute-start.11) | collective-permute-done | bytes 4128 | tf_op jit(solution)/shard_map/ppermute | solution.py:759
  62.3 0.9 %collective-permute-done.10.refs_1_ = f32[8,128]{1,0:T(8,128)S(1)} collective-permute-done((f32[8,128]{1,0:T(8,128)S(1)}, f32[8,128]{1,0:T(8,128)S(1)}, u32[]{:S(2)}, u32[]{:S(2)}) %collective-permute-start.10) | collective-permute-done | bytes 4128 | tf_op jit(solution)/shard_map/ppermute | solution.py:759
  63.3 1.7 %collective-permute-start.14 = (f32[136,128]{1,0:T(8,128)S(1)}, f32[136,128]{1,0:T(8,128)S(1)}, u32[]{:S(2)}, u32[]{:S(2)}) collective-permute-start(f32[136,128]{1,0:T(8,128)S(1)} %get-tuple-element.56), channel_id=1, source_target_pairs={{0,8},{4,12},{8,0},{12,4},{1,9},{5,13},{9,1},{13,5},{2,10},{6,14},... | collective-permute-start | bytes 208904 | tf_op jit(solution)/shard_map/ppermute | solution.py:589
  65.0 2.1 %collective-permute-start.15 = (f32[136,128]{1,0:T(8,128)S(1)}, f32[136,128]{1,0:T(8,128)S(1)}, u32[]{:S(2)}, u32[]{:S(2)}) collective-permute-start(f32[136,128]{1,0:T(8,128)S(1)} %get-tuple-element.57), channel_id=1, source_target_pairs={{0,12},{4,0},{8,4},{12,8},{1,13},{5,1},{9,5},{13,9},{2,14},{6,2},{... | collective-permute-start | bytes 208904 | tf_op jit(solution)/shard_map/ppermute | solution.py:589
  67.8 1.8 %collective-permute-done.13.refs_1_ = f32[136,128]{1,0:T(8,128)S(1)} collective-permute-done((f32[136,128]{1,0:T(8,128)S(1)}, f32[136,128]{1,0:T(8,128)S(1)}, u32[]{:S(2)}, u32[]{:S(2)}) %collective-permute-start.13) | collective-permute-done | bytes 69664 | tf_op jit(solution)/shard_map/ppermute | solution.py:589
  69.6 1.0 %collective-permute-done.14.refs_2_ = f32[136,128]{1,0:T(8,128)S(1)} collective-permute-done((f32[136,128]{1,0:T(8,128)S(1)}, f32[136,128]{1,0:T(8,128)S(1)}, u32[]{:S(2)}, u32[]{:S(2)}) %collective-permute-start.14) | collective-permute-done | bytes 69664 | tf_op jit(solution)/shard_map/ppermute | solution.py:589
  70.6 0.9 %shard_map.111 = (f32[8,16,512]{2,1,0:T(8,128)}, f32[8,16,512]{2,1,0:T(8,128)}) custom-call(s32[1]{0:T(128)} %bitcast.me, f32[1]{0:T(128)S(6)} %copy.19.prev_mean, f32[8,16,512]{2,1,0:T(8,128)S(1)} %copy-done.2, f32[8,16,512]{2,1,0:T(8,128)S(1)} %copy-done.3, f32[136,128]{1,0:T(8,128)S(1)} %get-tuple-element.54.refs_0_, ...), custom_call_target="tpu_custom_call" | custom-call | flops 1000000 | bytes 2000000 | tf_op jit(solution)/shard_map/pallas_call | solution.py:770
  (42 shorter events, 0.4 us)
Async XLA Ops:
  0.6 1.2 %copy-start = (bf16[2,8,64,512]{3,2,1,0:T(8,128)(2,1)S(1)}, bf16[2,8,64,512]{3,2,1,0:T(8,128)(2,1)}, u32[]{:S(2)}) copy-start(bf16[2,8,64,512]{3,2,1,0:T(8,128)(2,1)} %slc.1) | copy-start | bytes 3145732
  1.9 2.5 %copy-start.1 = (bf16[2,8,64,512]{3,2,1,0:T(8,128)(2,1)S(1)}, bf16[2,8,64,512]{3,2,1,0:T(8,128)(2,1)}, u32[]{:S(2)}) copy-start(bf16[2,8,64,512]{3,2,1,0:T(8,128)(2,1)} %slc.1) | copy-start | bytes 3145732
  2.1 2.3 %collective-permute-start = (bf16[64,128]{1,0:T(8,128)(2,1)S(1)}, bf16[64,128]{1,0:T(8,128)(2,1)S(1)}, u32[]{:S(2)}, u32[]{:S(2)}) collective-permute-start(bf16[64,128]{1,0:T(8,128)(2,1)S(1)} %shard_map.104), channel_id=1, source_target_pairs={{0,1},{1,0},{2,3},{3,2},{4,5},{5,4},{6,7},{7,6},{8,9},{9,8},{10,11... | collective-permute-start | bytes 49160 | tf_op jit(solution)/shard_map/ppermute | solution.py:580
  2.6 0.7 copy-start.10
  3.4 0.7 copy-start.11
  4.4 7.8 %copy-start.2 = (f32[8,16,512]{2,1,0:T(8,128)S(1)}, f32[8,16,512]{2,1,0:T(8,128)}, u32[]{:S(2)}) copy-start(f32[8,16,512]{2,1,0:T(8,128)} %estimate.1) | copy-start | bytes 786436
  4.4 7.8 %copy-start.3 = (f32[8,16,512]{2,1,0:T(8,128)S(1)}, f32[8,16,512]{2,1,0:T(8,128)}, u32[]{:S(2)}) copy-start(f32[8,16,512]{2,1,0:T(8,128)} %direction.1) | copy-start | bytes 786436
  5.7 12.2 %collective-permute-start.3 = (bf16[1088,128]{1,0:T(8,128)(2,1)S(1)}, bf16[1088,128]{1,0:T(8,128)(2,1)S(1)}, u32[]{:S(2)}, u32[]{:S(2)}) collective-permute-start(bf16[1088,128]{1,0:T(8,128)(2,1)S(1)} %get-tuple-element.31), channel_id=1, source_target_pairs={{0,4},{4,8},{8,12},{12,0},{1,5},{5,9},{9,13},{13,1},{2,6},{6,10},{... | collective-permute-start | bytes 835592 | tf_op jit(solution)/shard_map/ppermute | solution.py:589
  8.3 14.7 %collective-permute-start.1 = (bf16[1088,128]{1,0:T(8,128)(2,1)S(1)}, bf16[1088,128]{1,0:T(8,128)(2,1)S(1)}, u32[]{:S(2)}, u32[]{:S(2)}) collective-permute-start(bf16[1088,128]{1,0:T(8,128)(2,1)S(1)} %get-tuple-element.33), channel_id=1, source_target_pairs={{0,12},{4,0},{8,4},{12,8},{1,13},{5,1},{9,5},{13,9},{2,14},{6,2},{... | collective-permute-start | bytes 835592 | tf_op jit(solution)/shard_map/ppermute | solution.py:589
  10.4 20.8 %collective-permute-start.6 = (bf16[272,128]{1,0:T(8,128)(2,1)S(1)}, bf16[272,128]{1,0:T(8,128)(2,1)S(1)}, u32[]{:S(2)}, u32[]{:S(2)}) collective-permute-start(bf16[272,128]{1,0:T(8,128)(2,1)S(1)} %bitcast.19), channel_id=1, source_target_pairs={{0,2},{2,0},{1,3},{3,1},{4,6},{6,4},{5,7},{7,5},{8,10},{10,8},{9,1... | collective-permute-start | bytes 208904 | tf_op jit(solution)/shard_map/ppermute | solution.py:644
  23.1 5.1 %collective-permute-start.2 = (bf16[272,128]{1,0:T(8,128)(2,1)S(1)}, bf16[272,128]{1,0:T(8,128)(2,1)S(1)}, u32[]{:S(2)}, u32[]{:S(2)}) collective-permute-start(bf16[272,128]{1,0:T(8,128)(2,1)S(1)} %bitcast.20), channel_id=1, source_target_pairs={{0,2},{2,0},{1,3},{3,1},{4,6},{6,4},{5,7},{7,5},{8,10},{10,8},{9,1... | collective-permute-start | bytes 208904 | tf_op jit(solution)/shard_map/ppermute | solution.py:644
  24.7 6.6 %collective-permute-start.5 = (bf16[544,128]{1,0:T(8,128)(2,1)S(1)}, bf16[544,128]{1,0:T(8,128)(2,1)S(1)}, u32[]{:S(2)}, u32[]{:S(2)}) collective-permute-start(bf16[544,128]{1,0:T(8,128)(2,1)S(1)} %pad_maximum_fusion.1), channel_id=1, source_target_pairs={{0,2},{2,0},{1,3},{3,1},{4,6},{6,4},{5,7},{7,5},{8,10},{10,8},{9,1... | collective-permute-start | bytes 417800 | tf_op jit(solution)/shard_map/ppermute | solution.py:644
  25.4 5.8 %copy-start.7 = (f32[8,16]{1,0:T(8,128)}, f32[8,16]{1,0:T(8,128)S(1)}, u32[]{:S(2)}) copy-start(f32[8,16]{1,0:T(8,128)S(1)} %slice_convert_fusion) | copy-start | bytes 1540
  28.2 3.1 %copy-start.4 = (bf16[256,128]{1,0:T(8,128)(2,1)S(1)}, bf16[256,128]{1,0:T(8,128)(2,1)}, u32[]{:S(2)}) copy-start(bf16[256,128]{1,0:T(8,128)(2,1)} %constant.34.clone.rim_band) | copy-start | bytes 196612
  28.2 3.1 %copy-start.5 = (bf16[256,128]{1,0:T(8,128)(2,1)S(1)}, bf16[256,128]{1,0:T(8,128)(2,1)}, u32[]{:S(2)}) copy-start(bf16[256,128]{1,0:T(8,128)(2,1)} %constant.33.clone.band) | copy-start | bytes 196612
  29.0 21.8 %collective-permute-start.4 = (bf16[1360,128]{1,0:T(8,128)(2,1)}, bf16[1360,128]{1,0:T(8,128)(2,1)S(1)}, u32[]{:S(2)}, u32[]{:S(2)}) collective-permute-start(bf16[1360,128]{1,0:T(8,128)(2,1)} %pad_maximum_fusion), channel_id=1, source_target_pairs={{0,8},{4,12},{8,0},{12,4},{1,9},{5,13},{9,1},{13,5},{2,10},{6,14},... | collective-permute-start | bytes 1044488 | tf_op jit(solution)/shard_map/ppermute | solution.py:589
  31.0 0.7 %copy-start.6 = (bf16[96,96]{1,0:T(8,128)(2,1)S(1)}, bf16[96,96]{1,0:T(8,128)(2,1)}, u32[]{:S(2)}) copy-start(bf16[96,96]{1,0:T(8,128)(2,1)} %constant.32.clone.order) | copy-start | bytes 55300
  37.3 13.5 %copy-start.9 = (f32[8,16]{1,0:T(8,128)S(1)}, f32[8,16]{1,0:T(8,128)}, u32[]{:S(2)}) copy-start(f32[8,16]{1,0:T(8,128)} %slice_convert_fusion.2) | copy-start | bytes 1540
  37.3 13.5 %copy-start.8 = (f32[8,16]{1,0:T(8,128)S(1)}, f32[8,16]{1,0:T(8,128)}, u32[]{:S(2)}) copy-start(f32[8,16]{1,0:T(8,128)} %copy-done.7) | copy-start | bytes 1540
  37.4 19.5 %collective-permute-start.7 = (bf16[3,128,128]{2,1,0:T(8,128)(2,1)S(1)}, bf16[3,128,128]{2,1,0:T(8,128)(2,1)S(1)}, u32[]{:S(2)}, u32[]{:S(2)}) collective-permute-start(bf16[3,128,128]{2,1,0:T(8,128)(2,1)S(1)} %get-tuple-element.45), channel_id=1, source_target_pairs={{0,12},{4,0},{8,4},{12,8},{1,13},{5,1},{9,5},{13,9},{2,14},{6,2},{... | collective-permute-start | bytes 294920 | tf_op jit(solution)/shard_map/ppermute | solution.py:589
  39.3 17.5 %collective-permute-start.8 = (bf16[3,128,128]{2,1,0:T(8,128)(2,1)S(1)}, bf16[3,128,128]{2,1,0:T(8,128)(2,1)S(1)}, u32[]{:S(2)}, u32[]{:S(2)}) collective-permute-start(bf16[3,128,128]{2,1,0:T(8,128)(2,1)S(1)} %get-tuple-element.46), channel_id=1, source_target_pairs={{0,8},{4,12},{8,0},{12,4},{1,9},{5,13},{9,1},{13,5},{2,10},{6,14},... | collective-permute-start | bytes 294920 | tf_op jit(solution)/shard_map/ppermute | solution.py:589
  40.4 16.4 %collective-permute-start.9 = (bf16[3,128,128]{2,1,0:T(8,128)(2,1)S(1)}, bf16[3,128,128]{2,1,0:T(8,128)(2,1)S(1)}, u32[]{:S(2)}, u32[]{:S(2)}) collective-permute-start(bf16[3,128,128]{2,1,0:T(8,128)(2,1)S(1)} %get-tuple-element.47), channel_id=1, source_target_pairs={{0,4},{4,8},{8,12},{12,0},{1,5},{5,9},{9,13},{13,1},{2,6},{6,10},{... | collective-permute-start | bytes 294920 | tf_op jit(solution)/shard_map/ppermute | solution.py:589
  58.6 1.8 %collective-permute-start.12 = (f32[8,128]{1,0:T(8,128)S(1)}, f32[8,128]{1,0:T(8,128)S(1)}, u32[]{:S(2)}, u32[]{:S(2)}) collective-permute-start(f32[8,128]{1,0:T(8,128)S(1)} %get-tuple-element.53.refs_0_), channel_id=1, source_target_pairs={{0,3},{1,0},{2,1},{3,2},{4,7},{5,4},{6,5},{7,6},{8,11},{9,8},{10,9... | collective-permute-start | bytes 12296 | tf_op jit(solution)/shard_map/ppermute | solution.py:759
  58.7 3.7 %collective-permute-start.11 = (f32[8,128]{1,0:T(8,128)S(1)}, f32[8,128]{1,0:T(8,128)S(1)}, u32[]{:S(2)}, u32[]{:S(2)}) collective-permute-start(f32[8,128]{1,0:T(8,128)S(1)} %get-tuple-element.53.refs_0_), channel_id=1, source_target_pairs={{0,2},{1,3},{2,0},{3,1},{4,6},{5,7},{6,4},{7,5},{8,10},{9,11},{10,... | collective-permute-start | bytes 12296 | tf_op jit(solution)/shard_map/ppermute | solution.py:759
  60.2 3.0 %collective-permute-start.10 = (f32[8,128]{1,0:T(8,128)S(1)}, f32[8,128]{1,0:T(8,128)S(1)}, u32[]{:S(2)}, u32[]{:S(2)}) collective-permute-start(f32[8,128]{1,0:T(8,128)S(1)} %get-tuple-element.53.refs_0_), channel_id=1, source_target_pairs={{0,1},{1,2},{2,3},{3,0},{4,5},{5,6},{6,7},{7,4},{8,9},{9,10},{10,1... | collective-permute-start | bytes 12296 | tf_op jit(solution)/shard_map/ppermute | solution.py:759
  63.3 6.3 %collective-permute-start.13 = (f32[136,128]{1,0:T(8,128)S(1)}, f32[136,128]{1,0:T(8,128)S(1)}, u32[]{:S(2)}, u32[]{:S(2)}) collective-permute-start(f32[136,128]{1,0:T(8,128)S(1)} %get-tuple-element.55), channel_id=1, source_target_pairs={{0,4},{4,8},{8,12},{12,0},{1,5},{5,9},{9,13},{13,1},{2,6},{6,10},{... | collective-permute-start | bytes 208904 | tf_op jit(solution)/shard_map/ppermute | solution.py:589
  63.3 7.2 %collective-permute-start.14 = (f32[136,128]{1,0:T(8,128)S(1)}, f32[136,128]{1,0:T(8,128)S(1)}, u32[]{:S(2)}, u32[]{:S(2)}) collective-permute-start(f32[136,128]{1,0:T(8,128)S(1)} %get-tuple-element.56), channel_id=1, source_target_pairs={{0,8},{4,12},{8,0},{12,4},{1,9},{5,13},{9,1},{13,5},{2,10},{6,14},... | collective-permute-start | bytes 208904 | tf_op jit(solution)/shard_map/ppermute | solution.py:589
  65.0 5.6 %collective-permute-start.15 = (f32[136,128]{1,0:T(8,128)S(1)}, f32[136,128]{1,0:T(8,128)S(1)}, u32[]{:S(2)}, u32[]{:S(2)}) collective-permute-start(f32[136,128]{1,0:T(8,128)S(1)} %get-tuple-element.57), channel_id=1, source_target_pairs={{0,12},{4,0},{8,4},{12,8},{1,13},{5,1},{9,5},{13,9},{2,14},{6,2},{... | collective-permute-start | bytes 208904 | tf_op jit(solution)/shard_map/ppermute | solution.py:589

commit v16 on v15

--- a/solution.py
+++ b/solution.py
@@ -382,7 +382,6 @@
     factors, pulls, boxed, main, rim, looked, rim_looked, wide = refs[operands:]
     count = len(places)
     total = count * epochs
-    own_total = total - epochs
     look_rows = rows // LOOK
     halo_looks = HALO // LOOK
     looks = look_rows + 2 * halo_looks
@@ -406,8 +405,8 @@
         by_look = jnp.dot(order, rows_of(2 * epochs), preferred_element_type=jnp.float32)
         unpack_rims(by_look, looks, rim, first)
     power_batches(count, epochs, looks, main, rim, looked, rim_looked)
-    powers = (count + 1) // 2
-    couples = own_total // 2
+    powers = count // 2
+    couples = total // 2
 
     def boxed_of(channel):
         return boxed[pl.ds(pl.multiple_of(channel * look_rows, look_rows), look_rows), :]
@@ -466,11 +465,9 @@
 
 
 def gradient_kernel(sizes, partner, *refs):
-    tiles, epochs, stages = sizes
+    tiles, epochs = sizes
     fields = refs[:tiles]
-    factors = refs[tiles : tiles + len(stages)]
-    pulls = refs[tiles + len(stages) : tiles + 2 * len(stages)]
-    gradient, sums, est, old = refs[tiles + 2 * len(stages) :]
+    factors, pulls, gradient, sums, est, old = refs[tiles:]
     look_rows = est.shape[1]
     total = tiles * epochs
     f32 = jnp.float32
@@ -483,49 +480,40 @@
             old[block * epochs + epoch] = fields[block][2, here, :].astype(f32)
             gradient[block * epochs + epoch] = jnp.zeros((look_rows, LANES), f32)
 
-    for stage, (first, own_total) in enumerate(stages):
-
-        @pl.loop(0, own_total, unroll=2)
-        def _(here):
-            epoch = first + here
-            epoch = jnp.where(epoch < total, epoch, epoch - total)
-            own_est = est[epoch]
-            own = jnp.zeros((look_rows, LANES), f32)
-            mates = [partner[epoch * SLOTS + slot] for slot in range(SLOTS)]
-            values = []
-            for slot, mate in enumerate(mates):
-                pair = here * SLOTS + slot
-                weighted = pulls[stage][pair] - factors[stage][pair] * (own_est - est[mate])
-                own = own + weighted
-                values.append(weighted)
-            for mate, weighted in zip(mates, values):
-                gradient[mate] = gradient[mate] - weighted
-            gradient[epoch] = gradient[epoch] + own
+    @pl.loop(0, total, unroll=2)
+    def _(epoch):
+        own_est = est[epoch]
+        own = jnp.zeros((look_rows, LANES), f32)
+        mates = [partner[epoch * SLOTS + slot] for slot in range(SLOTS)]
+        values = []
+        for slot, mate in enumerate(mates):
+            pair = epoch * SLOTS + slot
+            weighted = pulls[pair] - factors[pair] * (own_est - est[mate])
+            own = own + weighted
+            values.append(weighted)
+        for mate, weighted in zip(mates, values):
+            gradient[mate] = gradient[mate] - weighted
+        gradient[epoch] = gradient[epoch] + own
+
+    def totals(epoch, carry):
+        norm, crossed, grad_term, mixed_term, old_term = carry
+        own_grad = gradient[epoch]
+        own_old = old[epoch]
+        norm = norm + own_grad * own_grad
+        crossed = crossed + own_grad * own_old
+        for slot in range(SLOTS):
+            mate = partner[epoch * SLOTS + slot]
+            factor = factors[epoch * SLOTS + slot]
+            grad_spread = own_grad - gradient[mate]
+            old_spread = own_old - old[mate]
+            pulled = factor * grad_spread
+            grad_term = grad_term + pulled * grad_spread
+            mixed_term = mixed_term + pulled * old_spread
+            old_term = old_term + factor * old_spread * old_spread
+        return norm, crossed, grad_term, mixed_term, old_term
 
     zero = jnp.zeros((look_rows, LANES), f32)
-    results = (zero,) * 5
-    for stage, (first, own_total) in enumerate(stages):
-
-        def totals(here, carry):
-            norm, crossed, grad_term, mixed_term, old_term = carry
-            epoch = first + here
-            epoch = jnp.where(epoch < total, epoch, epoch - total)
-            own_grad = gradient[epoch]
-            own_old = old[epoch]
-            norm = norm + own_grad * own_grad
-            crossed = crossed + own_grad * own_old
-            for slot in range(SLOTS):
-                mate = partner[epoch * SLOTS + slot]
-                factor = factors[stage][here * SLOTS + slot]
-                grad_spread = own_grad - gradient[mate]
-                old_spread = own_old - old[mate]
-                pulled = factor * grad_spread
-                grad_term = grad_term + pulled * grad_spread
-                mixed_term = mixed_term + pulled * old_spread
-                old_term = old_term + factor * old_spread * old_spread
-            return norm, crossed, grad_term, mixed_term, old_term
-
-        results = lax.fori_loop(0, own_total, totals, results, unroll=2)
+    results = lax.fori_loop(0, total, totals, (zero,) * 5, unroll=2)
     sums[...] = jnp.zeros(sums.shape, f32)
     for at, value in enumerate(results):
         sums[at : at + 1, :] = jnp.sum(value, axis=0, keepdims=True)
@@ -645,19 +633,7 @@
             return got, got
         return swapped(border(rows - HALO), border(0), "space")
 
-    beside = [tiles - 1, 0, 1]
-    far = list(range(2, tiles - 1))
-    block = {0: messages[0], 1: fetched(messages, 1), tiles - 1: fetched(messages, tiles - 1)}
-    early = {0: halo([messages[0].reshape(-1, rows, LANES)])}
-    ready = lax.optimization_barrier((messages, block[1]))[0]
-    early.update({shift: halo([ready[shift].reshape(-1, rows, LANES)]) for shift in far})
-    sent = {shift: messages[shift] for shift in far}
-    for shift in far:
-        borders = early[shift][:1] if spaces == 2 else early[shift]
-        sent[shift] = jnp.concatenate((messages[shift],) + borders, axis=0)
-    sent = lax.optimization_barrier((sent, block[1], block[tiles - 1]))[0]
-    block.update({shift: fetched(sent, shift) for shift in far})
-
+    block = [messages[0]] + [fetched(messages, shift) for shift in range(1, tiles)]
     estimate, direction, _ = lax.optimization_barrier((estimate, direction, messages))
     fields = pl.pallas_call(
         fields_kernel,
@@ -667,9 +643,6 @@
         compiler_params=params_of,
         cost_estimate=pl.CostEstimate(flops=1_000_000, bytes_accessed=2_000_000, transcendentals=0),
     )(me.reshape(1), estimate, direction)
-    def by_rows(shift):
-        return block[shift].reshape(-1, rows, LANES)
-
     def params_in(shift):
         return block[shift][tile_rows : tile_rows + epochs, PARAM_LANE : PARAM_LANE + 4 * SLOTS].astype(f32)
 
@@ -679,80 +652,58 @@
         weight = listed[:, SLOTS : 2 * SLOTS] + listed[:, 2 * SLOTS : 3 * SLOTS] + listed[:, 3 * SLOTS :]
         return mate.reshape(-1), weight.reshape(-1)
 
-    border_rows = (2 * epochs + 1) * HALO
-    near_halo = halo([by_rows(1), by_rows(tiles - 1)])
-    halos = {0: early[0] + (0, 0), 1: near_halo + (0, 0), tiles - 1: near_halo + (border_rows, border_rows)}
-    for shift in far:
-        bottom_at = tile_rows + rows if spaces == 2 else tile_rows + rows + border_rows
-        halos[shift] = block[shift], block[shift], tile_rows + rows, bottom_at
-
-    order = look_order(rows + 2 * HALO, HALO // LOOK - RADIUS)
-    bands = column_bands()
-
-    def pair_stage(loaded):
-        own = loaded[:-1]
-        listed = jnp.concatenate([params_in(shift) for shift in own], axis=0)
-        mate = jnp.arange(len(own) * epochs, dtype=jnp.int32)[:, None] + listed[:, :SLOTS].astype(jnp.int32)
-        weight = listed[:, SLOTS : 2 * SLOTS] + listed[:, 2 * SLOTS : 3 * SLOTS] + listed[:, 3 * SLOTS :]
-        operands = []
-
-        def index_of(array):
-            for at, other in enumerate(operands):
-                if other is array:
-                    return at
-            operands.append(array)
-            return len(operands) - 1
-
-        places = []
-        for shift in loaded:
-            top, bottom, top_row, bottom_row = halos[shift]
-            places.append((index_of(block[shift]), index_of(top), index_of(bottom), top_row, bottom_row))
-        here = len(loaded) * epochs
-        owned = len(own) * epochs
-        looks = (rows + 2 * HALO) // LOOK
-        group = 2 * SLOTS
-        batches = (len(loaded) + 1) // 2 * 2 + owned
-        shape = jax.ShapeDtypeStruct((owned * SLOTS, look_rows, LANES), f32)
-        return pl.pallas_call(
-            functools.partial(pair_kernel, (epochs, rows, len(operands)), tuple(places)),
-            out_shape=(shape, shape),
-            in_specs=[SMEM] * 3 + [VMEM] * (3 + len(operands)),
-            out_specs=(VMEM, VMEM),
-            scratch_shapes=[
-                pltpu.VMEM((batches * group * look_rows, LANES), f32),
-                pltpu.VMEM((2 * here, LOOK, looks, LANES), f32),
-                pltpu.VMEM((2 * here, looks, LANES), f32),
-                pltpu.VMEM((batches * group * looks, LANES), f32),
-                pltpu.VMEM((batches * 2 * looks, LANES), f32),
-                pltpu.VMEM((batches * group * looks, LANES), f32),
-            ],
-            compiler_params=params_of,
-            cost_estimate=pl.CostEstimate(flops=20_000_000, bytes_accessed=30_000_000, transcendentals=0),
-        )(mate.reshape(-1), weight.reshape(-1), present, order, *bands, *operands)
-
-    near_stage = beside
-    far_stage = list(range(1, tiles))
-    near_pairs = pair_stage(near_stage)
-    fields, near_pairs = lax.optimization_barrier((fields, near_pairs))
-    field = [fields[0]] + [fetched(fields, shift) for shift in range(1, tiles)]
-    far_pairs = pair_stage(far_stage)
+    halos = [halo([array.reshape(-1, rows, LANES)]) for array in block]
+    late = lax.optimization_barrier((fields, block))[0]
+    field = [fields[0]] + [fetched(late, shift) for shift in range(1, tiles)]
 
     listed = jnp.concatenate([params_in(shift) for shift in range(tiles)], axis=0)
     partner = jnp.arange(total, dtype=jnp.int32)[:, None] + listed[:, :SLOTS].astype(jnp.int32)
     partner = lax.rem(partner, total).reshape(-1)
-    stages = tuple((stage[0] * epochs, (len(stage) - 1) * epochs) for stage in (near_stage, far_stage))
+    weight = listed[:, SLOTS : 2 * SLOTS] + listed[:, 2 * SLOTS : 3 * SLOTS] + listed[:, 3 * SLOTS :]
+    order = look_order(rows + 2 * HALO, HALO // LOOK - RADIUS)
+    bands = column_bands()
+    operands = list(block)
+    places = []
+    for shift in range(tiles):
+        top, bottom = halos[shift]
+        operands.append(top)
+        top_at = bottom_at = len(operands) - 1
+        if bottom is not top:
+            operands.append(bottom)
+            bottom_at = len(operands) - 1
+        places.append((shift, top_at, bottom_at, 0, 0))
+    looks = (rows + 2 * HALO) // LOOK
+    group = 2 * SLOTS
+    batches = tiles + total
+    shape = jax.ShapeDtypeStruct((total * SLOTS, look_rows, LANES), f32)
+    factors, pulls = pl.pallas_call(
+        functools.partial(pair_kernel, (epochs, rows, len(operands)), tuple(places)),
+        out_shape=(shape, shape),
+        in_specs=[SMEM] * 3 + [VMEM] * (3 + len(operands)),
+        out_specs=(VMEM, VMEM),
+        scratch_shapes=[
+            pltpu.VMEM((batches * group * look_rows, LANES), f32),
+            pltpu.VMEM((2 * total, LOOK, looks, LANES), f32),
+            pltpu.VMEM((2 * total, looks, LANES), f32),
+            pltpu.VMEM((batches * group * looks, LANES), f32),
+            pltpu.VMEM((batches * 2 * looks, LANES), f32),
+            pltpu.VMEM((batches * group * looks, LANES), f32),
+        ],
+        compiler_params=params_of,
+        cost_estimate=pl.CostEstimate(flops=20_000_000, bytes_accessed=30_000_000, transcendentals=0),
+    )(partner, weight.reshape(-1), present, order, *bands, *operands)
     gradient, sums = pl.pallas_call(
-        functools.partial(gradient_kernel, (tiles, epochs, stages)),
+        functools.partial(gradient_kernel, (tiles, epochs)),
         out_shape=(
             jax.ShapeDtypeStruct((total, look_rows, LANES), f32),
             jax.ShapeDtypeStruct((8, LANES), f32),
         ),
-        in_specs=[SMEM] + [VMEM] * (tiles + 4),
+        in_specs=[SMEM] + [VMEM] * (tiles + 2),
         out_specs=(VMEM, VMEM),
         scratch_shapes=[pltpu.VMEM((total, look_rows, LANES), f32)] * 2,
         compiler_params=params_of,
         cost_estimate=pl.CostEstimate(flops=10_000_000, bytes_accessed=8_000_000, transcendentals=0),
-    )(partner, *field, near_pairs[0], far_pairs[0], near_pairs[1], far_pairs[1])
+    )(partner, *field, factors, pulls)
 
     place = ("space", "sub")
     count = spaces * lax.axis_size("sub")
@@ -779,7 +730,7 @@
 
 def on_device(slc, offsets, weights, estimate, direction, prev_mean):
     epochs, rows, columns = slc.shape[1:]
-    fits = columns == LANES * lax.axis_size("epoch") and lax.axis_size("epoch") > 3
+    fits = columns == LANES * lax.axis_size("epoch") and lax.axis_size("epoch") % 2 == 0
     fits = fits and 2 * epochs * SIDES <= PARAM_LANE and rows % HALO == 0 and epochs == 2 * SLOTS
     plan = transposed_plan if fits else ring_plan
     return plan(slc, offsets, weights, estimate, direction, prev_mean)

time: 71.8 us -> 69.4 us (0.967)
  waiting for transfers between devices: 29 us -> 19.8 us
  starting transfers between devices: 19.8 us -> 27.7 us
  other arithmetic: 2.06 us -> 0.33 us
  Pallas kernels: 15.5 us -> 16.5 us
    ppermute x9, starting transfers between devices: 13.6 us -> 20.1 us  [to_ahead(): return lax.ppermute(x, axis, [(i, (i + by) % size) for i in range(size)])]
    ppermute x9, waiting for transfers between devices: 23.3 us -> 16.9 us  [to_ahead(): return lax.ppermute(x, axis, [(i, (i + by) % size) for i in range(size)])]
    ppermute x3 -> x4, waiting for transfers between devices: 2.88 us -> 0.01 us  [halo(): lax.ppermute(border(jnp.where(space == 0, rows - HALO, 0)), 'space', [(0,...]
    ppermute x3 -> x4, starting transfers between devices: 3.86 us -> 5.33 us  [halo(): lax.ppermute(border(jnp.where(space == 0, rows - HALO, 0)), 'space', [(0,...]
    pallas_call x3 -> x2, Pallas kernels: 12.9 us -> 14 us  [the longest x1 12.3 us: transposed_plan(): pl.pallas_call(functools.partial(pair_kernel, (epochs, rows, len(operands...]
    convert_element_type x4 -> x0, other arithmetic: 0.88 us -> none  [params_in(): block[shift]]
    concatenate x2 -> x1, other arithmetic: 0.77 us -> 0.01 us  [transposed_plan(): jnp.concatenate([params_in(shift) for shift in range(tiles)], axis=0)]
    unnamed x26 -> x20, local copies, waits for them, and re-layouts: 3.19 us -> 2.77 us
  transfers between devices with their start and end apart: 16 -> 17, of which waited for: 8 -> 7; matrix products, arithmetic and copies ran while one was open for 4% -> 2% of each run, Pallas kernels for 16% -> 18%
where the time goes in v16:
time: 69.4 us; the launch traced here: 69.2 us
  starting transfers between devices  27.7 us (40%)
  waiting for transfers between devices  19.8 us (29%)
  Pallas kernels  16.5 us (24%)
  local copies, waits for them, and re-layouts  3.31 us (5%)
  between operations  1.47 us (2%)
    ppermute x9, starting transfers between devices, to_ahead(): return lax.ppermute(x, axis, [(i, (i + by) % size) for i in range(size)])  20.1 us
    ppermute x9, waiting for transfers between devices, to_ahead(): return lax.ppermute(x, axis, [(i, (i + by) % size) for i in range(size)])  16.9 us
    pallas_call x1, Pallas kernels, transposed_plan(): pl.pallas_call(functools.partial(pair_kernel, (epochs, rows, len(operands...  12.3 us
    ppermute x4, starting transfers between devices, halo(): lax.ppermute(border(jnp.where(space == 0, rows - HALO, 0)), 'space', [(0,...  5.33 us
    ppermute x3, waiting for transfers between devices, transposed_plan(): lax.ppermute(sums, place, [(i, (i + by) % count) for i in range(count)])  2.87 us
    unnamed x20, local copies, waits for them, and re-layouts  2.77 us
    ppermute x3, starting transfers between devices, transposed_plan(): lax.ppermute(sums, place, [(i, (i + by) % count) for i in range(count)])  1.81 us
    pallas_call x1, Pallas kernels, transposed_plan(): pl.pallas_call(functools.partial(gradient_kernel, (tiles, epochs)), out_s...  1.67 us
  transfers between devices with their start and end apart: 17, of which 7 were waited for; matrix products, arithmetic and copies ran while one was open for 2% of the time, Pallas kernels for 18%

profile of v16, /device:TPU:0, one launch (start us, length us, event | category | flops | bytes accessed | tf_op | source)
XLA Modules:
  0.0 69.2 jit_solution(2132479559540171940)
XLA Ops:
  0.6 1.2 %copy-done = bf16[2,8,64,512]{3,2,1,0:T(8,128)(2,1)S(1)} copy-done((bf16[2,8,64,512]{3,2,1,0:T(8,128)(2,1)S(1)}, bf16[2,8,64,512]{3,2,1,0:T(8,128)(2,1)}, u32[]{:S(2)}) %copy-start) | copy-done | bytes 1048600
  1.9 0.2 shard_map.104
  2.1 0.5 collective-permute-start
  2.6 0.7 copy-done.7
  3.3 0.1 copy.15
  3.4 0.7 copy-done.8
  4.1 0.1 copy.16
  4.1 0.1 select_maximum_fusion.params
  4.2 0.1 add_convert_fusion.present
  4.3 0.0 collective-permute-done.before.after
  4.3 0.0 copy-start.3
  4.3 1.3 %shard_map.105 = (bf16[1088,128]{1,0:T(8,128)(2,1)S(1)}, bf16[1088,128]{1,0:T(8,128)(2,1)S(1)}, bf16[1088,128]{1,0:T(8,128)(2,1)S(1)}, bf16[1088,128]{1,0:T(8,128)(2,1)S(1)}) custom-call(s32[1]{0:T(128)} %bitcast.me, f32[2]{0:T(128)S(1)} %add_convert_fusion.present, bf16[2,8,64,512]{3,2,1,0:T(8,128)(2,1)S(1)} %copy-done.1, ...), custom_call_target="tpu_custom_call" | custom-call | flops 3000000 | bytes 4000000 | tf_op jit(solution)/shard_map/pallas_call | solution.py:613
  5.6 2.7 %collective-permute-start.3 = (bf16[1088,128]{1,0:T(8,128)(2,1)S(1)}, bf16[1088,128]{1,0:T(8,128)(2,1)S(1)}, u32[]{:S(2)}, u32[]{:S(2)}) collective-permute-start(bf16[1088,128]{1,0:T(8,128)(2,1)S(1)} %get-tuple-element.24), channel_id=1, source_target_pairs={{0,4},{4,8},{8,12},{12,0},{1,5},{5,9},{9,13},{13,1},{2,6},{6,10},{... | collective-permute-start | bytes 835592 | tf_op jit(solution)/shard_map/ppermute | solution.py:577
  8.3 2.6 %collective-permute-start.2 = (bf16[1088,128]{1,0:T(8,128)(2,1)S(1)}, bf16[1088,128]{1,0:T(8,128)(2,1)S(1)}, u32[]{:S(2)}, u32[]{:S(2)}) collective-permute-start(bf16[1088,128]{1,0:T(8,128)(2,1)S(1)} %get-tuple-element.25), channel_id=1, source_target_pairs={{0,8},{4,12},{8,0},{12,4},{1,9},{5,13},{9,1},{13,5},{2,10},{6,14},... | collective-permute-start | bytes 835592 | tf_op jit(solution)/shard_map/ppermute | solution.py:577
  10.8 0.1 add_convert_fusion.1.present
  10.9 1.3 %collective-permute-start.1 = (bf16[1088,128]{1,0:T(8,128)(2,1)S(1)}, bf16[1088,128]{1,0:T(8,128)(2,1)S(1)}, u32[]{:S(2)}, u32[]{:S(2)}) collective-permute-start(bf16[1088,128]{1,0:T(8,128)(2,1)S(1)} %get-tuple-element.26), channel_id=1, source_target_pairs={{0,12},{4,0},{8,4},{12,8},{1,13},{5,1},{9,5},{13,9},{2,14},{6,2},{... | collective-permute-start | bytes 835592 | tf_op jit(solution)/shard_map/ppermute | solution.py:577
  12.3 0.1 slice.24
  12.4 1.5 %collective-permute-start.7 = (bf16[272,128]{1,0:T(8,128)(2,1)S(1)}, bf16[272,128]{1,0:T(8,128)(2,1)S(1)}, u32[]{:S(2)}, u32[]{:S(2)}) collective-permute-start(bf16[272,128]{1,0:T(8,128)(2,1)S(1)} %bitcast.17), channel_id=1, source_target_pairs={{0,2},{2,0},{1,3},{3,1},{4,6},{6,4},{5,7},{7,5},{8,10},{10,8},{9,1... | collective-permute-start | bytes 208904 | tf_op jit(solution)/shard_map/ppermute | solution.py:632
  13.9 0.1 shard_map.106
  13.9 4.0 %collective-permute-done.3.refs_3_ = bf16[1088,128]{1,0:T(8,128)(2,1)S(1)} collective-permute-done((bf16[1088,128]{1,0:T(8,128)(2,1)S(1)}, bf16[1088,128]{1,0:T(8,128)(2,1)S(1)}, u32[]{:S(2)}, u32[]{:S(2)}) %collective-permute-start.3) | collective-permute-done | bytes 278560 | tf_op jit(solution)/shard_map/ppermute | solution.py:577
  17.9 1.7 %collective-permute-start.10 = (bf16[272,128]{1,0:T(8,128)(2,1)S(1)}, bf16[272,128]{1,0:T(8,128)(2,1)S(1)}, u32[]{:S(2)}, u32[]{:S(2)}) collective-permute-start(bf16[272,128]{1,0:T(8,128)(2,1)S(1)} %bitcast.19), channel_id=1, source_target_pairs={{0,2},{2,0},{1,3},{3,1},{4,6},{6,4},{5,7},{7,5},{8,10},{10,8},{9,1... | collective-permute-start | bytes 208904 | tf_op jit(solution)/shard_map/ppermute | solution.py:632
  19.6 10.0 %collective-permute-done.2.refs_2_ = bf16[1088,128]{1,0:T(8,128)(2,1)S(1)} collective-permute-done((bf16[1088,128]{1,0:T(8,128)(2,1)S(1)}, bf16[1088,128]{1,0:T(8,128)(2,1)S(1)}, u32[]{:S(2)}, u32[]{:S(2)}) %collective-permute-start.2) | collective-permute-done | bytes 278560 | tf_op jit(solution)/shard_map/ppermute | solution.py:577
  29.6 1.6 %collective-permute-start.9 = (bf16[272,128]{1,0:T(8,128)(2,1)S(1)}, bf16[272,128]{1,0:T(8,128)(2,1)S(1)}, u32[]{:S(2)}, u32[]{:S(2)}) collective-permute-start(bf16[272,128]{1,0:T(8,128)(2,1)S(1)} %bitcast.18), channel_id=1, source_target_pairs={{0,2},{2,0},{1,3},{3,1},{4,6},{6,4},{5,7},{7,5},{8,10},{10,8},{9,1... | collective-permute-start | bytes 208904 | tf_op jit(solution)/shard_map/ppermute | solution.py:632
  31.2 0.1 slice.34
  31.3 0.1 slice.33
  31.4 0.1 slice.32
  31.4 0.1 slice_add_fusion
  31.5 0.0 copy-start.6
  31.6 0.0 copy-start.4
  31.6 0.6 collective-permute-start.8
  32.2 7.5 %collective-permute-start.4 = (bf16[3,128,128]{2,1,0:T(8,128)(2,1)S(1)}, bf16[3,128,128]{2,1,0:T(8,128)(2,1)S(1)}, u32[]{:S(2)}, u32[]{:S(2)}) collective-permute-start(bf16[3,128,128]{2,1,0:T(8,128)(2,1)S(1)} %get-tuple-element.33), channel_id=1, source_target_pairs={{0,12},{4,0},{8,4},{12,8},{1,13},{5,1},{9,5},{13,9},{2,14},{6,2},{... | collective-permute-start | bytes 294920 | tf_op jit(solution)/shard_map/ppermute | solution.py:577
  39.7 0.6 collective-permute-start.6
  40.2 0.1 reshape.41.weight
  40.3 0.1 reshape.40.partner
  40.5 12.3 %shard_map.107 = (f32[128,16,128]{2,1,0:T(8,128)S(1)}, f32[128,16,128]{2,1,0:T(8,128)S(1)}) custom-call(s32[128]{0:T(128)S(1)} %reshape.40.partner, f32[128]{0:T(128)S(1)} %reshape.41.weight, f32[2]{0:T(128)S(1)} %add_convert_fusion.1.present, bf16[96,96]{1,0:T(8,128)(2,1)S(1)} %copy-done.6, bf16[256,128]{1,0:T(8,128)(2,1)S(1)} %copy-done.5, ...), custom_call_target="tpu_custom_call" | custom-call | flops 20000000 | bytes 30000000 | tf_op jit(solution)/shard_map/pallas_call | solution.py:679
  52.9 1.7 %shard_map.108 = (f32[32,16,128]{2,1,0:T(8,128)S(1)}, f32[8,128]{1,0:T(8,128)S(1)}) custom-call(s32[128]{0:T(128)S(1)} %reshape.40.partner, bf16[3,128,128]{2,1,0:T(8,128)(2,1)S(1)} %get-tuple-element.29.refs_0_, bf16[3,128,128]{2,1,0:T(8,128)(2,1)S(1)} %collective-permute-done.4.refs_1_, bf16[3,128,128]{2,1,0:T(8,128)(2,1)S(1)} %collective-permute-done.5.refs_2_, ...), custom_call_target="tpu_custom_call" | custom-call | flops 10000000 | bytes 8000000 | tf_op jit(solution)/shard_map/pallas_call | solution.py:695
  54.5 0.1 collective-permute-start.13
  54.6 1.6 %collective-permute-start.12 = (f32[8,128]{1,0:T(8,128)S(1)}, f32[8,128]{1,0:T(8,128)S(1)}, u32[]{:S(2)}, u32[]{:S(2)}) collective-permute-start(f32[8,128]{1,0:T(8,128)S(1)} %get-tuple-element.39.refs_0_), channel_id=1, source_target_pairs={{0,2},{1,3},{2,0},{3,1},{4,6},{5,7},{6,4},{7,5},{8,10},{9,11},{10,... | collective-permute-start | bytes 12296 | tf_op jit(solution)/shard_map/ppermute | solution.py:710
  56.2 0.2 collective-permute-start.11
  56.4 1.9 %collective-permute-done.12.refs_2_ = f32[8,128]{1,0:T(8,128)S(1)} collective-permute-done((f32[8,128]{1,0:T(8,128)S(1)}, f32[8,128]{1,0:T(8,128)S(1)}, u32[]{:S(2)}, u32[]{:S(2)}) %collective-permute-start.12) | collective-permute-done | bytes 4128 | tf_op jit(solution)/shard_map/ppermute | solution.py:710
  58.3 0.9 %collective-permute-done.11.refs_1_ = f32[8,128]{1,0:T(8,128)S(1)} collective-permute-done((f32[8,128]{1,0:T(8,128)S(1)}, f32[8,128]{1,0:T(8,128)S(1)}, u32[]{:S(2)}, u32[]{:S(2)}) %collective-permute-start.11) | collective-permute-done | bytes 4128 | tf_op jit(solution)/shard_map/ppermute | solution.py:710
  59.3 3.0 %collective-permute-start.14 = (f32[136,128]{1,0:T(8,128)S(1)}, f32[136,128]{1,0:T(8,128)S(1)}, u32[]{:S(2)}, u32[]{:S(2)}) collective-permute-start(f32[136,128]{1,0:T(8,128)S(1)} %get-tuple-element.41), channel_id=1, source_target_pairs={{0,4},{4,8},{8,12},{12,0},{1,5},{5,9},{9,13},{13,1},{2,6},{6,10},{... | collective-permute-start | bytes 208904 | tf_op jit(solution)/shard_map/ppermute | solution.py:577
  62.2 1.0 %collective-permute-start.15 = (f32[136,128]{1,0:T(8,128)S(1)}, f32[136,128]{1,0:T(8,128)S(1)}, u32[]{:S(2)}, u32[]{:S(2)}) collective-permute-start(f32[136,128]{1,0:T(8,128)S(1)} %get-tuple-element.42), channel_id=1, source_target_pairs={{0,8},{4,12},{8,0},{12,4},{1,9},{5,13},{9,1},{13,5},{2,10},{6,14},... | collective-permute-start | bytes 208904 | tf_op jit(solution)/shard_map/ppermute | solution.py:577
  63.2 1.5 %collective-permute-start.16 = (f32[136,128]{1,0:T(8,128)S(1)}, f32[136,128]{1,0:T(8,128)S(1)}, u32[]{:S(2)}, u32[]{:S(2)}) collective-permute-start(f32[136,128]{1,0:T(8,128)S(1)} %get-tuple-element.43), channel_id=1, source_target_pairs={{0,12},{4,0},{8,4},{12,8},{1,13},{5,1},{9,5},{13,9},{2,14},{6,2},{... | collective-permute-start | bytes 208904 | tf_op jit(solution)/shard_map/ppermute | solution.py:577
  65.3 0.5 collective-permute-done.14.refs_1_
  65.8 2.3 %collective-permute-done.15.refs_2_ = f32[136,128]{1,0:T(8,128)S(1)} collective-permute-done((f32[136,128]{1,0:T(8,128)S(1)}, f32[136,128]{1,0:T(8,128)S(1)}, u32[]{:S(2)}, u32[]{:S(2)}) %collective-permute-start.15) | collective-permute-done | bytes 69664 | tf_op jit(solution)/shard_map/ppermute | solution.py:577
  68.2 0.1 collective-permute-done.16.refs_3_
  68.2 0.9 %shard_map.110 = (f32[8,16,512]{2,1,0:T(8,128)}, f32[8,16,512]{2,1,0:T(8,128)}) custom-call(s32[1]{0:T(128)} %bitcast.me, f32[1]{0:T(128)S(6)} %copy.19.prev_mean, f32[8,16,512]{2,1,0:T(8,128)S(1)} %copy-done.2, f32[8,16,512]{2,1,0:T(8,128)S(1)} %copy-done.3, f32[136,128]{1,0:T(8,128)S(1)} %get-tuple-element.40.refs_0_, ...), custom_call_target="tpu_custom_call" | custom-call | flops 1000000 | bytes 2000000 | tf_op jit(solution)/shard_map/pallas_call | solution.py:721
  (30 shorter events, 0.1 us)
Async XLA Ops:
  0.6 1.2 %copy-start = (bf16[2,8,64,512]{3,2,1,0:T(8,128)(2,1)S(1)}, bf16[2,8,64,512]{3,2,1,0:T(8,128)(2,1)}, u32[]{:S(2)}) copy-start(bf16[2,8,64,512]{3,2,1,0:T(8,128)(2,1)} %slc.1) | copy-start | bytes 3145732
  1.9 2.4 %copy-start.1 = (bf16[2,8,64,512]{3,2,1,0:T(8,128)(2,1)S(1)}, bf16[2,8,64,512]{3,2,1,0:T(8,128)(2,1)}, u32[]{:S(2)}) copy-start(bf16[2,8,64,512]{3,2,1,0:T(8,128)(2,1)} %slc.1) | copy-start | bytes 3145732
  2.1 2.2 %collective-permute-start = (bf16[64,128]{1,0:T(8,128)(2,1)S(1)}, bf16[64,128]{1,0:T(8,128)(2,1)S(1)}, u32[]{:S(2)}, u32[]{:S(2)}) collective-permute-start(bf16[64,128]{1,0:T(8,128)(2,1)S(1)} %shard_map.104), channel_id=1, source_target_pairs={{0,1},{1,0},{2,3},{3,2},{4,5},{5,4},{6,7},{7,6},{8,9},{9,8},{10,11... | collective-permute-start | bytes 49160 | tf_op jit(solution)/shard_map/ppermute | solution.py:568
  2.6 0.7 copy-start.7
  3.4 0.7 copy-start.8
  4.3 9.6 %copy-start.2 = (f32[8,16,512]{2,1,0:T(8,128)S(1)}, f32[8,16,512]{2,1,0:T(8,128)}, u32[]{:S(2)}) copy-start(f32[8,16,512]{2,1,0:T(8,128)} %estimate.1) | copy-start | bytes 786436
  4.3 9.5 %copy-start.3 = (f32[8,16,512]{2,1,0:T(8,128)S(1)}, f32[8,16,512]{2,1,0:T(8,128)}, u32[]{:S(2)}) copy-start(f32[8,16,512]{2,1,0:T(8,128)} %direction.1) | copy-start | bytes 786436
  5.6 12.3 %collective-permute-start.3 = (bf16[1088,128]{1,0:T(8,128)(2,1)S(1)}, bf16[1088,128]{1,0:T(8,128)(2,1)S(1)}, u32[]{:S(2)}, u32[]{:S(2)}) collective-permute-start(bf16[1088,128]{1,0:T(8,128)(2,1)S(1)} %get-tuple-element.24), channel_id=1, source_target_pairs={{0,4},{4,8},{8,12},{12,0},{1,5},{5,9},{9,13},{13,1},{2,6},{6,10},{... | collective-permute-start | bytes 835592 | tf_op jit(solution)/shard_map/ppermute | solution.py:577
  8.3 21.4 %collective-permute-start.2 = (bf16[1088,128]{1,0:T(8,128)(2,1)S(1)}, bf16[1088,128]{1,0:T(8,128)(2,1)S(1)}, u32[]{:S(2)}, u32[]{:S(2)}) collective-permute-start(bf16[1088,128]{1,0:T(8,128)(2,1)S(1)} %get-tuple-element.25), channel_id=1, source_target_pairs={{0,8},{4,12},{8,0},{12,4},{1,9},{5,13},{9,1},{13,5},{2,10},{6,14},... | collective-permute-start | bytes 835592 | tf_op jit(solution)/shard_map/ppermute | solution.py:577
  10.9 20.4 %collective-permute-start.1 = (bf16[1088,128]{1,0:T(8,128)(2,1)S(1)}, bf16[1088,128]{1,0:T(8,128)(2,1)S(1)}, u32[]{:S(2)}, u32[]{:S(2)}) collective-permute-start(bf16[1088,128]{1,0:T(8,128)(2,1)S(1)} %get-tuple-element.26), channel_id=1, source_target_pairs={{0,12},{4,0},{8,4},{12,8},{1,13},{5,1},{9,5},{13,9},{2,14},{6,2},{... | collective-permute-start | bytes 835592 | tf_op jit(solution)/shard_map/ppermute | solution.py:577
  12.4 27.3 %collective-permute-start.7 = (bf16[272,128]{1,0:T(8,128)(2,1)S(1)}, bf16[272,128]{1,0:T(8,128)(2,1)S(1)}, u32[]{:S(2)}, u32[]{:S(2)}) collective-permute-start(bf16[272,128]{1,0:T(8,128)(2,1)S(1)} %bitcast.17), channel_id=1, source_target_pairs={{0,2},{2,0},{1,3},{3,1},{4,6},{6,4},{5,7},{7,5},{8,10},{10,8},{9,1... | collective-permute-start | bytes 208904 | tf_op jit(solution)/shard_map/ppermute | solution.py:632
  17.9 21.7 %collective-permute-start.10 = (bf16[272,128]{1,0:T(8,128)(2,1)S(1)}, bf16[272,128]{1,0:T(8,128)(2,1)S(1)}, u32[]{:S(2)}, u32[]{:S(2)}) collective-permute-start(bf16[272,128]{1,0:T(8,128)(2,1)S(1)} %bitcast.19), channel_id=1, source_target_pairs={{0,2},{2,0},{1,3},{3,1},{4,6},{6,4},{5,7},{7,5},{8,10},{10,8},{9,1... | collective-permute-start | bytes 208904 | tf_op jit(solution)/shard_map/ppermute | solution.py:632
  29.6 10.8 %collective-permute-start.9 = (bf16[272,128]{1,0:T(8,128)(2,1)S(1)}, bf16[272,128]{1,0:T(8,128)(2,1)S(1)}, u32[]{:S(2)}, u32[]{:S(2)}) collective-permute-start(bf16[272,128]{1,0:T(8,128)(2,1)S(1)} %bitcast.18), channel_id=1, source_target_pairs={{0,2},{2,0},{1,3},{3,1},{4,6},{6,4},{5,7},{7,5},{8,10},{10,8},{9,1... | collective-permute-start | bytes 208904 | tf_op jit(solution)/shard_map/ppermute | solution.py:632
  31.5 9.0 %copy-start.5 = (bf16[256,128]{1,0:T(8,128)(2,1)S(1)}, bf16[256,128]{1,0:T(8,128)(2,1)}, u32[]{:S(2)}) copy-start(bf16[256,128]{1,0:T(8,128)(2,1)} %constant.33.clone.band) | copy-start | bytes 196612
  31.5 9.0 %copy-start.6 = (bf16[96,96]{1,0:T(8,128)(2,1)S(1)}, bf16[96,96]{1,0:T(8,128)(2,1)}, u32[]{:S(2)}) copy-start(bf16[96,96]{1,0:T(8,128)(2,1)} %constant.32.clone.order) | copy-start | bytes 55300
  31.6 8.9 %copy-start.4 = (bf16[256,128]{1,0:T(8,128)(2,1)S(1)}, bf16[256,128]{1,0:T(8,128)(2,1)}, u32[]{:S(2)}) copy-start(bf16[256,128]{1,0:T(8,128)(2,1)} %constant.34.clone.rim_band) | copy-start | bytes 196612
  31.6 8.9 %collective-permute-start.8 = (bf16[272,128]{1,0:T(8,128)(2,1)S(1)}, bf16[272,128]{1,0:T(8,128)(2,1)S(1)}, u32[]{:S(2)}, u32[]{:S(2)}) collective-permute-start(bf16[272,128]{1,0:T(8,128)(2,1)S(1)} %bitcast.20), channel_id=1, source_target_pairs={{0,2},{2,0},{1,3},{3,1},{4,6},{6,4},{5,7},{7,5},{8,10},{10,8},{9,1... | collective-permute-start | bytes 208904 | tf_op jit(solution)/shard_map/ppermute | solution.py:632
  32.2 20.7 %collective-permute-start.4 = (bf16[3,128,128]{2,1,0:T(8,128)(2,1)S(1)}, bf16[3,128,128]{2,1,0:T(8,128)(2,1)S(1)}, u32[]{:S(2)}, u32[]{:S(2)}) collective-permute-start(bf16[3,128,128]{2,1,0:T(8,128)(2,1)S(1)} %get-tuple-element.33), channel_id=1, source_target_pairs={{0,12},{4,0},{8,4},{12,8},{1,13},{5,1},{9,5},{13,9},{2,14},{6,2},{... | collective-permute-start | bytes 294920 | tf_op jit(solution)/shard_map/ppermute | solution.py:577
  39.7 13.2 %collective-permute-start.5 = (bf16[3,128,128]{2,1,0:T(8,128)(2,1)S(1)}, bf16[3,128,128]{2,1,0:T(8,128)(2,1)S(1)}, u32[]{:S(2)}, u32[]{:S(2)}) collective-permute-start(bf16[3,128,128]{2,1,0:T(8,128)(2,1)S(1)} %get-tuple-element.34), channel_id=1, source_target_pairs={{0,8},{4,12},{8,0},{12,4},{1,9},{5,13},{9,1},{13,5},{2,10},{6,14},... | collective-permute-start | bytes 294920 | tf_op jit(solution)/shard_map/ppermute | solution.py:577
  39.7 13.2 %collective-permute-start.6 = (bf16[3,128,128]{2,1,0:T(8,128)(2,1)S(1)}, bf16[3,128,128]{2,1,0:T(8,128)(2,1)S(1)}, u32[]{:S(2)}, u32[]{:S(2)}) collective-permute-start(bf16[3,128,128]{2,1,0:T(8,128)(2,1)S(1)} %get-tuple-element.35), channel_id=1, source_target_pairs={{0,4},{4,8},{8,12},{12,0},{1,5},{5,9},{9,13},{13,1},{2,6},{6,10},{... | collective-permute-start | bytes 294920 | tf_op jit(solution)/shard_map/ppermute | solution.py:577
  54.5 1.8 %collective-permute-start.13 = (f32[8,128]{1,0:T(8,128)S(1)}, f32[8,128]{1,0:T(8,128)S(1)}, u32[]{:S(2)}, u32[]{:S(2)}) collective-permute-start(f32[8,128]{1,0:T(8,128)S(1)} %get-tuple-element.39.refs_0_), channel_id=1, source_target_pairs={{0,3},{1,0},{2,1},{3,2},{4,7},{5,4},{6,5},{7,6},{8,11},{9,8},{10,9... | collective-permute-start | bytes 12296 | tf_op jit(solution)/shard_map/ppermute | solution.py:710
  54.6 3.7 %collective-permute-start.12 = (f32[8,128]{1,0:T(8,128)S(1)}, f32[8,128]{1,0:T(8,128)S(1)}, u32[]{:S(2)}, u32[]{:S(2)}) collective-permute-start(f32[8,128]{1,0:T(8,128)S(1)} %get-tuple-element.39.refs_0_), channel_id=1, source_target_pairs={{0,2},{1,3},{2,0},{3,1},{4,6},{5,7},{6,4},{7,5},{8,10},{9,11},{10,... | collective-permute-start | bytes 12296 | tf_op jit(solution)/shard_map/ppermute | solution.py:710
  56.2 3.0 %collective-permute-start.11 = (f32[8,128]{1,0:T(8,128)S(1)}, f32[8,128]{1,0:T(8,128)S(1)}, u32[]{:S(2)}, u32[]{:S(2)}) collective-permute-start(f32[8,128]{1,0:T(8,128)S(1)} %get-tuple-element.39.refs_0_), channel_id=1, source_target_pairs={{0,1},{1,2},{2,3},{3,0},{4,5},{5,6},{6,7},{7,4},{8,9},{9,10},{10,1... | collective-permute-start | bytes 12296 | tf_op jit(solution)/shard_map/ppermute | solution.py:710
  59.3 6.6 %collective-permute-start.14 = (f32[136,128]{1,0:T(8,128)S(1)}, f32[136,128]{1,0:T(8,128)S(1)}, u32[]{:S(2)}, u32[]{:S(2)}) collective-permute-start(f32[136,128]{1,0:T(8,128)S(1)} %get-tuple-element.41), channel_id=1, source_target_pairs={{0,4},{4,8},{8,12},{12,0},{1,5},{5,9},{9,13},{13,1},{2,6},{6,10},{... | collective-permute-start | bytes 208904 | tf_op jit(solution)/shard_map/ppermute | solution.py:577
  62.2 5.9 %collective-permute-start.15 = (f32[136,128]{1,0:T(8,128)S(1)}, f32[136,128]{1,0:T(8,128)S(1)}, u32[]{:S(2)}, u32[]{:S(2)}) collective-permute-start(f32[136,128]{1,0:T(8,128)S(1)} %get-tuple-element.42), channel_id=1, source_target_pairs={{0,8},{4,12},{8,0},{12,4},{1,9},{5,13},{9,1},{13,5},{2,10},{6,14},... | collective-permute-start | bytes 208904 | tf_op jit(solution)/shard_map/ppermute | solution.py:577
  63.2 5.1 %collective-permute-start.16 = (f32[136,128]{1,0:T(8,128)S(1)}, f32[136,128]{1,0:T(8,128)S(1)}, u32[]{:S(2)}, u32[]{:S(2)}) collective-permute-start(f32[136,128]{1,0:T(8,128)S(1)} %get-tuple-element.43), channel_id=1, source_target_pairs={{0,12},{4,0},{8,4},{12,8},{1,13},{5,1},{9,5},{13,9},{2,14},{6,2},{... | collective-permute-start | bytes 208904 | tf_op jit(solution)/shard_map/ppermute | solution.py:577

commit v17 on v16

--- a/solution.py
+++ b/solution.py
@@ -327,16 +327,16 @@
 
 def put(ref, block, values):
     rows = sum(value.shape[0] for value in values)
-    ref[pl.ds(pl.multiple_of(block * rows, rows), rows), :] = jnp.concatenate(values, axis=0)
+    ref[block * rows : (block + 1) * rows, :] = jnp.concatenate(values, axis=0)
 
 
 def columns_summed(couple, looks, bands, looked, rim_looked):
     group = 2 * SLOTS
     f32 = jnp.float32
-    at = pl.ds(pl.multiple_of(couple * (2 * group * looks), 2 * group * looks), 2 * group * looks)
+    at = slice(couple * 2 * group * looks, (couple + 1) * 2 * group * looks)
     halves = jnp.concatenate(split_two(looked[at, :]), axis=1)
     value = jnp.dot(halves, bands[0], preferred_element_type=f32)
-    at = pl.ds(pl.multiple_of(couple * (4 * looks), 4 * looks), 4 * looks)
+    at = slice(couple * 4 * looks, (couple + 1) * 4 * looks)
     halves = jnp.concatenate(split_two(rim_looked[at, :]), axis=1)
     outer = jnp.dot(halves, bands[1], preferred_element_type=f32)
     lane = lax.broadcasted_iota(jnp.int32, (looks, LANES), 1)
@@ -417,7 +417,7 @@
             epoch = couple * 2 + one
             own_power = boxed_of(epoch)
             first = (2 * powers + epoch) * (group * look_rows)
-            parts = boxed[pl.ds(pl.multiple_of(first, group * look_rows), group * look_rows), :]
+            parts = boxed[first : first + group * look_rows, :]
             parts = parts.reshape(group, look_rows, LANES)
             for slot in range(SLOTS):
                 pair = epoch * SLOTS + slot
@@ -458,7 +458,8 @@
         put(boxed, couple, boxes(couple))
     turn(1, (0, 1))
     turn(2, (0, 1, 2))
-    pl.loop(3, couples)(lambda number: turn(number, (0, 1, 2, 3)))
+    for number in range(3, couples):
+        turn(number, (0, 1, 2, 3))
     turn(couples, (1, 2, 3))
     turn(couples + 1, (2, 3))
     turn(couples + 2, (3,))

time: 69.4 us -> 63.6 us (0.916)
  Pallas kernels: 16.5 us -> 10.1 us
  waiting for transfers between devices: 19.8 us -> 21.4 us
  starting transfers between devices: 27.7 us -> 26.8 us
    pallas_call x1, Pallas kernels: 12.3 us -> 5.94 us  [transposed_plan(): pl.pallas_call(functools.partial(pair_kernel, (epochs, rows, len(operands...]
    ppermute x9, waiting for transfers between devices: 16.9 us -> 18.3 us  [to_ahead(): return lax.ppermute(x, axis, [(i, (i + by) % size) for i in range(size)])]
  transfers between devices with their start and end apart: 17 -> 17, of which waited for: 7 -> 8; matrix products, arithmetic and copies ran while one was open for 2% -> 2% of each run, Pallas kernels for 18% -> 9%
where the time goes in v17:
time: 63.6 us; the launch traced here: 63.4 us
  starting transfers between devices  26.8 us (42%)
  waiting for transfers between devices  21.4 us (34%)
  Pallas kernels  10.1 us (16%)
  local copies, waits for them, and re-layouts  3.31 us (5%)
  between operations  1.45 us (2%)
    ppermute x9, starting transfers between devices, to_ahead(): return lax.ppermute(x, axis, [(i, (i + by) % size) for i in range(size)])  19.8 us
    ppermute x9, waiting for transfers between devices, to_ahead(): return lax.ppermute(x, axis, [(i, (i + by) % size) for i in range(size)])  18.3 us
    pallas_call x1, Pallas kernels, transposed_plan(): pl.pallas_call(functools.partial(pair_kernel, (epochs, rows, len(operands...  5.94 us
    ppermute x4, starting transfers between devices, halo(): lax.ppermute(border(jnp.where(space == 0, rows - HALO, 0)), 'space', [(0,...  5.33 us
    ppermute x3, waiting for transfers between devices, transposed_plan(): lax.ppermute(sums, place, [(i, (i + by) % count) for i in range(count)])  3.03 us
    unnamed x20, local copies, waits for them, and re-layouts  2.77 us
    pallas_call x1, Pallas kernels, transposed_plan(): pl.pallas_call(functools.partial(gradient_kernel, (tiles, epochs)), out_s...  1.66 us
  transfers between devices with their start and end apart: 17, of which 8 were waited for; matrix products, arithmetic and copies ran while one was open for 2% of the time, Pallas kernels for 9%

profile of v17, /device:TPU:0, one launch (start us, length us, event | category | flops | bytes accessed | tf_op | source)
XLA Modules:
  0.0 63.4 jit_solution(5250410663769108133)
XLA Ops:
  0.6 1.2 %copy-done = bf16[2,8,64,512]{3,2,1,0:T(8,128)(2,1)S(1)} copy-done((bf16[2,8,64,512]{3,2,1,0:T(8,128)(2,1)S(1)}, bf16[2,8,64,512]{3,2,1,0:T(8,128)(2,1)}, u32[]{:S(2)}) %copy-start) | copy-done | bytes 1048600
  1.9 0.2 shard_map.104
  2.1 0.5 collective-permute-start
  2.6 0.7 %copy-done.7 = s32[8,4]{0,1:T(4,128)S(1)} copy-done((s32[8,4]{0,1:T(4,128)S(1)}, s32[8,4]{0,1:T(4,128)}, u32[]{:S(2)}) %copy-start.7) | copy-done | bytes 152
  3.3 0.1 copy.15
  3.4 0.7 %copy-done.8 = f32[8,4]{0,1:T(4,128)S(1)} copy-done((f32[8,4]{0,1:T(4,128)S(1)}, f32[8,4]{0,1:T(4,128)}, u32[]{:S(2)}) %copy-start.8) | copy-done | bytes 152
  4.1 0.1 copy.16
  4.1 0.1 select_maximum_fusion.params
  4.2 0.1 add_convert_fusion.present
  4.3 0.0 collective-permute-done.before.after
  4.3 0.0 copy-start.3
  4.3 1.3 %shard_map.105 = (bf16[1088,128]{1,0:T(8,128)(2,1)S(1)}, bf16[1088,128]{1,0:T(8,128)(2,1)S(1)}, bf16[1088,128]{1,0:T(8,128)(2,1)S(1)}, bf16[1088,128]{1,0:T(8,128)(2,1)S(1)}) custom-call(s32[1]{0:T(128)} %bitcast.me, f32[2]{0:T(128)S(1)} %add_convert_fusion.present, bf16[2,8,64,512]{3,2,1,0:T(8,128)(2,1)S(1)} %copy-done.1, ...), custom_call_target="tpu_custom_call" | custom-call | flops 3000000 | bytes 4000000 | tf_op jit(solution)/shard_map/pallas_call | solution.py:614
  5.6 2.7 %collective-permute-start.3 = (bf16[1088,128]{1,0:T(8,128)(2,1)S(1)}, bf16[1088,128]{1,0:T(8,128)(2,1)S(1)}, u32[]{:S(2)}, u32[]{:S(2)}) collective-permute-start(bf16[1088,128]{1,0:T(8,128)(2,1)S(1)} %get-tuple-element.24), channel_id=1, source_target_pairs={{0,4},{4,8},{8,12},{12,0},{1,5},{5,9},{9,13},{13,1},{2,6},{6,10},{... | collective-permute-start | bytes 835592 | tf_op jit(solution)/shard_map/ppermute | solution.py:578
  8.3 2.6 %collective-permute-start.2 = (bf16[1088,128]{1,0:T(8,128)(2,1)S(1)}, bf16[1088,128]{1,0:T(8,128)(2,1)S(1)}, u32[]{:S(2)}, u32[]{:S(2)}) collective-permute-start(bf16[1088,128]{1,0:T(8,128)(2,1)S(1)} %get-tuple-element.25), channel_id=1, source_target_pairs={{0,8},{4,12},{8,0},{12,4},{1,9},{5,13},{9,1},{13,5},{2,10},{6,14},... | collective-permute-start | bytes 835592 | tf_op jit(solution)/shard_map/ppermute | solution.py:578
  10.8 0.1 add_convert_fusion.1.present
  10.9 1.3 %collective-permute-start.1 = (bf16[1088,128]{1,0:T(8,128)(2,1)S(1)}, bf16[1088,128]{1,0:T(8,128)(2,1)S(1)}, u32[]{:S(2)}, u32[]{:S(2)}) collective-permute-start(bf16[1088,128]{1,0:T(8,128)(2,1)S(1)} %get-tuple-element.26), channel_id=1, source_target_pairs={{0,12},{4,0},{8,4},{12,8},{1,13},{5,1},{9,5},{13,9},{2,14},{6,2},{... | collective-permute-start | bytes 835592 | tf_op jit(solution)/shard_map/ppermute | solution.py:578
  12.3 0.1 slice.24
  12.4 1.5 %collective-permute-start.7 = (bf16[272,128]{1,0:T(8,128)(2,1)S(1)}, bf16[272,128]{1,0:T(8,128)(2,1)S(1)}, u32[]{:S(2)}, u32[]{:S(2)}) collective-permute-start(bf16[272,128]{1,0:T(8,128)(2,1)S(1)} %bitcast.17), channel_id=1, source_target_pairs={{0,2},{2,0},{1,3},{3,1},{4,6},{6,4},{5,7},{7,5},{8,10},{10,8},{9,1... | collective-permute-start | bytes 208904 | tf_op jit(solution)/shard_map/ppermute | solution.py:633
  13.9 0.1 shard_map.106
  13.9 4.0 %collective-permute-done.3.refs_3_ = bf16[1088,128]{1,0:T(8,128)(2,1)S(1)} collective-permute-done((bf16[1088,128]{1,0:T(8,128)(2,1)S(1)}, bf16[1088,128]{1,0:T(8,128)(2,1)S(1)}, u32[]{:S(2)}, u32[]{:S(2)}) %collective-permute-start.3) | collective-permute-done | bytes 278560 | tf_op jit(solution)/shard_map/ppermute | solution.py:578
  17.9 1.7 %collective-permute-start.10 = (bf16[272,128]{1,0:T(8,128)(2,1)S(1)}, bf16[272,128]{1,0:T(8,128)(2,1)S(1)}, u32[]{:S(2)}, u32[]{:S(2)}) collective-permute-start(bf16[272,128]{1,0:T(8,128)(2,1)S(1)} %bitcast.19), channel_id=1, source_target_pairs={{0,2},{2,0},{1,3},{3,1},{4,6},{6,4},{5,7},{7,5},{8,10},{10,8},{9,1... | collective-permute-start | bytes 208904 | tf_op jit(solution)/shard_map/ppermute | solution.py:633
  19.6 10.0 %collective-permute-done.2.refs_2_ = bf16[1088,128]{1,0:T(8,128)(2,1)S(1)} collective-permute-done((bf16[1088,128]{1,0:T(8,128)(2,1)S(1)}, bf16[1088,128]{1,0:T(8,128)(2,1)S(1)}, u32[]{:S(2)}, u32[]{:S(2)}) %collective-permute-start.2) | collective-permute-done | bytes 278560 | tf_op jit(solution)/shard_map/ppermute | solution.py:578
  29.6 1.6 %collective-permute-start.9 = (bf16[272,128]{1,0:T(8,128)(2,1)S(1)}, bf16[272,128]{1,0:T(8,128)(2,1)S(1)}, u32[]{:S(2)}, u32[]{:S(2)}) collective-permute-start(bf16[272,128]{1,0:T(8,128)(2,1)S(1)} %bitcast.18), channel_id=1, source_target_pairs={{0,2},{2,0},{1,3},{3,1},{4,6},{6,4},{5,7},{7,5},{8,10},{10,8},{9,1... | collective-permute-start | bytes 208904 | tf_op jit(solution)/shard_map/ppermute | solution.py:633
  31.2 0.1 slice.34
  31.3 0.1 slice.33
  31.4 0.1 slice.32
  31.4 0.1 slice_add_fusion
  31.5 0.0 copy-start.6
  31.6 0.0 copy-start.4
  31.6 0.6 collective-permute-start.8
  32.2 7.5 %collective-permute-start.4 = (bf16[3,128,128]{2,1,0:T(8,128)(2,1)S(1)}, bf16[3,128,128]{2,1,0:T(8,128)(2,1)S(1)}, u32[]{:S(2)}, u32[]{:S(2)}) collective-permute-start(bf16[3,128,128]{2,1,0:T(8,128)(2,1)S(1)} %get-tuple-element.33), channel_id=1, source_target_pairs={{0,12},{4,0},{8,4},{12,8},{1,13},{5,1},{9,5},{13,9},{2,14},{6,2},{... | collective-permute-start | bytes 294920 | tf_op jit(solution)/shard_map/ppermute | solution.py:578
  39.7 0.6 collective-permute-start.6
  40.2 0.1 reshape.41.weight
  40.3 0.1 reshape.40.partner
  40.5 5.9 %shard_map.107 = (f32[128,16,128]{2,1,0:T(8,128)S(1)}, f32[128,16,128]{2,1,0:T(8,128)S(1)}) custom-call(s32[128]{0:T(128)S(1)} %reshape.40.partner, f32[128]{0:T(128)S(1)} %reshape.41.weight, f32[2]{0:T(128)S(1)} %add_convert_fusion.1.present, bf16[96,96]{1,0:T(8,128)(2,1)S(1)} %copy-done.6, bf16[256,128]{1,0:T(8,128)(2,1)S(1)} %copy-done.5, ...), custom_call_target="tpu_custom_call" | custom-call | flops 20000000 | bytes 30000000 | tf_op jit(solution)/shard_map/pallas_call | solution.py:680
  46.5 1.6 %collective-permute-done.5.refs_2_ = bf16[3,128,128]{2,1,0:T(8,128)(2,1)S(1)} collective-permute-done((bf16[3,128,128]{2,1,0:T(8,128)(2,1)S(1)}, bf16[3,128,128]{2,1,0:T(8,128)(2,1)S(1)}, u32[]{:S(2)}, u32[]{:S(2)}) %collective-permute-start.5) | collective-permute-done | bytes 98336 | tf_op jit(solution)/shard_map/ppermute | solution.py:578
  48.1 1.7 %shard_map.108 = (f32[32,16,128]{2,1,0:T(8,128)S(1)}, f32[8,128]{1,0:T(8,128)S(1)}) custom-call(s32[128]{0:T(128)S(1)} %reshape.40.partner, bf16[3,128,128]{2,1,0:T(8,128)(2,1)S(1)} %get-tuple-element.29.refs_0_, bf16[3,128,128]{2,1,0:T(8,128)(2,1)S(1)} %collective-permute-done.4.refs_1_, bf16[3,128,128]{2,1,0:T(8,128)(2,1)S(1)} %collective-permute-done.5.refs_2_, ...), custom_call_target="tpu_custom_call" | custom-call | flops 10000000 | bytes 8000000 | tf_op jit(solution)/shard_map/pallas_call | solution.py:696
  49.8 0.1 collective-permute-start.13
  49.8 1.1 %collective-permute-start.12 = (f32[8,128]{1,0:T(8,128)S(1)}, f32[8,128]{1,0:T(8,128)S(1)}, u32[]{:S(2)}, u32[]{:S(2)}) collective-permute-start(f32[8,128]{1,0:T(8,128)S(1)} %get-tuple-element.39.refs_0_), channel_id=1, source_target_pairs={{0,2},{1,3},{2,0},{3,1},{4,6},{5,7},{6,4},{7,5},{8,10},{9,11},{10,... | collective-permute-start | bytes 12296 | tf_op jit(solution)/shard_map/ppermute | solution.py:711
  50.9 0.3 collective-permute-done.13.refs_3_
  51.1 2.4 %collective-permute-done.12.refs_2_ = f32[8,128]{1,0:T(8,128)S(1)} collective-permute-done((f32[8,128]{1,0:T(8,128)S(1)}, f32[8,128]{1,0:T(8,128)S(1)}, u32[]{:S(2)}, u32[]{:S(2)}) %collective-permute-start.12) | collective-permute-done | bytes 4128 | tf_op jit(solution)/shard_map/ppermute | solution.py:711
  53.5 0.4 collective-permute-done.11.refs_1_
  53.9 1.9 %collective-permute-start.14 = (f32[136,128]{1,0:T(8,128)S(1)}, f32[136,128]{1,0:T(8,128)S(1)}, u32[]{:S(2)}, u32[]{:S(2)}) collective-permute-start(f32[136,128]{1,0:T(8,128)S(1)} %get-tuple-element.41), channel_id=1, source_target_pairs={{0,4},{4,8},{8,12},{12,0},{1,5},{5,9},{9,13},{13,1},{2,6},{6,10},{... | collective-permute-start | bytes 208904 | tf_op jit(solution)/shard_map/ppermute | solution.py:578
  55.9 0.9 %collective-permute-start.15 = (f32[136,128]{1,0:T(8,128)S(1)}, f32[136,128]{1,0:T(8,128)S(1)}, u32[]{:S(2)}, u32[]{:S(2)}) collective-permute-start(f32[136,128]{1,0:T(8,128)S(1)} %get-tuple-element.42), channel_id=1, source_target_pairs={{0,8},{4,12},{8,0},{12,4},{1,9},{5,13},{9,1},{13,5},{2,10},{6,14},... | collective-permute-start | bytes 208904 | tf_op jit(solution)/shard_map/ppermute | solution.py:578
  56.8 2.4 %collective-permute-start.16 = (f32[136,128]{1,0:T(8,128)S(1)}, f32[136,128]{1,0:T(8,128)S(1)}, u32[]{:S(2)}, u32[]{:S(2)}) collective-permute-start(f32[136,128]{1,0:T(8,128)S(1)} %get-tuple-element.43), channel_id=1, source_target_pairs={{0,12},{4,0},{8,4},{12,8},{1,13},{5,1},{9,5},{13,9},{2,14},{6,2},{... | collective-permute-start | bytes 208904 | tf_op jit(solution)/shard_map/ppermute | solution.py:578
  59.8 0.5 collective-permute-done.14.refs_1_
  60.4 2.1 %collective-permute-done.15.refs_2_ = f32[136,128]{1,0:T(8,128)S(1)} collective-permute-done((f32[136,128]{1,0:T(8,128)S(1)}, f32[136,128]{1,0:T(8,128)S(1)}, u32[]{:S(2)}, u32[]{:S(2)}) %collective-permute-start.15) | collective-permute-done | bytes 69664 | tf_op jit(solution)/shard_map/ppermute | solution.py:578
  62.5 0.9 %shard_map.110 = (f32[8,16,512]{2,1,0:T(8,128)}, f32[8,16,512]{2,1,0:T(8,128)}) custom-call(s32[1]{0:T(128)} %bitcast.me, f32[1]{0:T(128)S(6)} %copy.19.prev_mean, f32[8,16,512]{2,1,0:T(8,128)S(1)} %copy-done.2, f32[8,16,512]{2,1,0:T(8,128)S(1)} %copy-done.3, f32[136,128]{1,0:T(8,128)S(1)} %get-tuple-element.40.refs_0_, ...), custom_call_target="tpu_custom_call" | custom-call | flops 1000000 | bytes 2000000 | tf_op jit(solution)/shard_map/pallas_call | solution.py:722
  (30 shorter events, 0.1 us)
Async XLA Ops:
  0.6 1.2 %copy-start = (bf16[2,8,64,512]{3,2,1,0:T(8,128)(2,1)S(1)}, bf16[2,8,64,512]{3,2,1,0:T(8,128)(2,1)}, u32[]{:S(2)}) copy-start(bf16[2,8,64,512]{3,2,1,0:T(8,128)(2,1)} %slc.1) | copy-start | bytes 3145732
  1.9 2.4 %copy-start.1 = (bf16[2,8,64,512]{3,2,1,0:T(8,128)(2,1)S(1)}, bf16[2,8,64,512]{3,2,1,0:T(8,128)(2,1)}, u32[]{:S(2)}) copy-start(bf16[2,8,64,512]{3,2,1,0:T(8,128)(2,1)} %slc.1) | copy-start | bytes 3145732
  2.1 2.2 %collective-permute-start = (bf16[64,128]{1,0:T(8,128)(2,1)S(1)}, bf16[64,128]{1,0:T(8,128)(2,1)S(1)}, u32[]{:S(2)}, u32[]{:S(2)}) collective-permute-start(bf16[64,128]{1,0:T(8,128)(2,1)S(1)} %shard_map.104), channel_id=1, source_target_pairs={{0,1},{1,0},{2,3},{3,2},{4,5},{5,4},{6,7},{7,6},{8,9},{9,8},{10,11... | collective-permute-start | bytes 49160 | tf_op jit(solution)/shard_map/ppermute | solution.py:569
  2.6 0.7 %copy-start.7 = (s32[8,4]{0,1:T(4,128)S(1)}, s32[8,4]{0,1:T(4,128)}, u32[]{:S(2)}) copy-start(s32[8,4]{0,1:T(4,128)} %param.10) | copy-start | bytes 388
  3.4 0.7 %copy-start.8 = (f32[8,4]{0,1:T(4,128)S(1)}, f32[8,4]{0,1:T(4,128)}, u32[]{:S(2)}) copy-start(f32[8,4]{0,1:T(4,128)} %param.11) | copy-start | bytes 388
  4.3 9.6 %copy-start.2 = (f32[8,16,512]{2,1,0:T(8,128)S(1)}, f32[8,16,512]{2,1,0:T(8,128)}, u32[]{:S(2)}) copy-start(f32[8,16,512]{2,1,0:T(8,128)} %estimate.1) | copy-start | bytes 786436
  4.3 9.5 %copy-start.3 = (f32[8,16,512]{2,1,0:T(8,128)S(1)}, f32[8,16,512]{2,1,0:T(8,128)}, u32[]{:S(2)}) copy-start(f32[8,16,512]{2,1,0:T(8,128)} %direction.1) | copy-start | bytes 786436
  5.6 12.3 %collective-permute-start.3 = (bf16[1088,128]{1,0:T(8,128)(2,1)S(1)}, bf16[1088,128]{1,0:T(8,128)(2,1)S(1)}, u32[]{:S(2)}, u32[]{:S(2)}) collective-permute-start(bf16[1088,128]{1,0:T(8,128)(2,1)S(1)} %get-tuple-element.24), channel_id=1, source_target_pairs={{0,4},{4,8},{8,12},{12,0},{1,5},{5,9},{9,13},{13,1},{2,6},{6,10},{... | collective-permute-start | bytes 835592 | tf_op jit(solution)/shard_map/ppermute | solution.py:578
  8.3 21.4 %collective-permute-start.2 = (bf16[1088,128]{1,0:T(8,128)(2,1)S(1)}, bf16[1088,128]{1,0:T(8,128)(2,1)S(1)}, u32[]{:S(2)}, u32[]{:S(2)}) collective-permute-start(bf16[1088,128]{1,0:T(8,128)(2,1)S(1)} %get-tuple-element.25), channel_id=1, source_target_pairs={{0,8},{4,12},{8,0},{12,4},{1,9},{5,13},{9,1},{13,5},{2,10},{6,14},... | collective-permute-start | bytes 835592 | tf_op jit(solution)/shard_map/ppermute | solution.py:578
  10.9 20.4 %collective-permute-start.1 = (bf16[1088,128]{1,0:T(8,128)(2,1)S(1)}, bf16[1088,128]{1,0:T(8,128)(2,1)S(1)}, u32[]{:S(2)}, u32[]{:S(2)}) collective-permute-start(bf16[1088,128]{1,0:T(8,128)(2,1)S(1)} %get-tuple-element.26), channel_id=1, source_target_pairs={{0,12},{4,0},{8,4},{12,8},{1,13},{5,1},{9,5},{13,9},{2,14},{6,2},{... | collective-permute-start | bytes 835592 | tf_op jit(solution)/shard_map/ppermute | solution.py:578
  12.4 27.3 %collective-permute-start.7 = (bf16[272,128]{1,0:T(8,128)(2,1)S(1)}, bf16[272,128]{1,0:T(8,128)(2,1)S(1)}, u32[]{:S(2)}, u32[]{:S(2)}) collective-permute-start(bf16[272,128]{1,0:T(8,128)(2,1)S(1)} %bitcast.17), channel_id=1, source_target_pairs={{0,2},{2,0},{1,3},{3,1},{4,6},{6,4},{5,7},{7,5},{8,10},{10,8},{9,1... | collective-permute-start | bytes 208904 | tf_op jit(solution)/shard_map/ppermute | solution.py:633
  17.9 21.7 %collective-permute-start.10 = (bf16[272,128]{1,0:T(8,128)(2,1)S(1)}, bf16[272,128]{1,0:T(8,128)(2,1)S(1)}, u32[]{:S(2)}, u32[]{:S(2)}) collective-permute-start(bf16[272,128]{1,0:T(8,128)(2,1)S(1)} %bitcast.19), channel_id=1, source_target_pairs={{0,2},{2,0},{1,3},{3,1},{4,6},{6,4},{5,7},{7,5},{8,10},{10,8},{9,1... | collective-permute-start | bytes 208904 | tf_op jit(solution)/shard_map/ppermute | solution.py:633
  29.6 10.8 %collective-permute-start.9 = (bf16[272,128]{1,0:T(8,128)(2,1)S(1)}, bf16[272,128]{1,0:T(8,128)(2,1)S(1)}, u32[]{:S(2)}, u32[]{:S(2)}) collective-permute-start(bf16[272,128]{1,0:T(8,128)(2,1)S(1)} %bitcast.18), channel_id=1, source_target_pairs={{0,2},{2,0},{1,3},{3,1},{4,6},{6,4},{5,7},{7,5},{8,10},{10,8},{9,1... | collective-permute-start | bytes 208904 | tf_op jit(solution)/shard_map/ppermute | solution.py:633
  31.5 9.0 %copy-start.5 = (bf16[256,128]{1,0:T(8,128)(2,1)S(1)}, bf16[256,128]{1,0:T(8,128)(2,1)}, u32[]{:S(2)}) copy-start(bf16[256,128]{1,0:T(8,128)(2,1)} %constant.33.clone.band) | copy-start | bytes 196612
  31.5 9.0 %copy-start.6 = (bf16[96,96]{1,0:T(8,128)(2,1)S(1)}, bf16[96,96]{1,0:T(8,128)(2,1)}, u32[]{:S(2)}) copy-start(bf16[96,96]{1,0:T(8,128)(2,1)} %constant.32.clone.order) | copy-start | bytes 55300
  31.6 8.9 %copy-start.4 = (bf16[256,128]{1,0:T(8,128)(2,1)S(1)}, bf16[256,128]{1,0:T(8,128)(2,1)}, u32[]{:S(2)}) copy-start(bf16[256,128]{1,0:T(8,128)(2,1)} %constant.34.clone.rim_band) | copy-start | bytes 196612
  31.6 8.9 %collective-permute-start.8 = (bf16[272,128]{1,0:T(8,128)(2,1)S(1)}, bf16[272,128]{1,0:T(8,128)(2,1)S(1)}, u32[]{:S(2)}, u32[]{:S(2)}) collective-permute-start(bf16[272,128]{1,0:T(8,128)(2,1)S(1)} %bitcast.20), channel_id=1, source_target_pairs={{0,2},{2,0},{1,3},{3,1},{4,6},{6,4},{5,7},{7,5},{8,10},{10,8},{9,1... | collective-permute-start | bytes 208904 | tf_op jit(solution)/shard_map/ppermute | solution.py:633
  32.2 14.3 %collective-permute-start.4 = (bf16[3,128,128]{2,1,0:T(8,128)(2,1)S(1)}, bf16[3,128,128]{2,1,0:T(8,128)(2,1)S(1)}, u32[]{:S(2)}, u32[]{:S(2)}) collective-permute-start(bf16[3,128,128]{2,1,0:T(8,128)(2,1)S(1)} %get-tuple-element.33), channel_id=1, source_target_pairs={{0,12},{4,0},{8,4},{12,8},{1,13},{5,1},{9,5},{13,9},{2,14},{6,2},{... | collective-permute-start | bytes 294920 | tf_op jit(solution)/shard_map/ppermute | solution.py:578
  39.7 8.4 %collective-permute-start.5 = (bf16[3,128,128]{2,1,0:T(8,128)(2,1)S(1)}, bf16[3,128,128]{2,1,0:T(8,128)(2,1)S(1)}, u32[]{:S(2)}, u32[]{:S(2)}) collective-permute-start(bf16[3,128,128]{2,1,0:T(8,128)(2,1)S(1)} %get-tuple-element.34), channel_id=1, source_target_pairs={{0,8},{4,12},{8,0},{12,4},{1,9},{5,13},{9,1},{13,5},{2,10},{6,14},... | collective-permute-start | bytes 294920 | tf_op jit(solution)/shard_map/ppermute | solution.py:578
  39.7 8.4 %collective-permute-start.6 = (bf16[3,128,128]{2,1,0:T(8,128)(2,1)S(1)}, bf16[3,128,128]{2,1,0:T(8,128)(2,1)S(1)}, u32[]{:S(2)}, u32[]{:S(2)}) collective-permute-start(bf16[3,128,128]{2,1,0:T(8,128)(2,1)S(1)} %get-tuple-element.35), channel_id=1, source_target_pairs={{0,4},{4,8},{8,12},{12,0},{1,5},{5,9},{9,13},{13,1},{2,6},{6,10},{... | collective-permute-start | bytes 294920 | tf_op jit(solution)/shard_map/ppermute | solution.py:578
  49.8 1.4 %collective-permute-start.13 = (f32[8,128]{1,0:T(8,128)S(1)}, f32[8,128]{1,0:T(8,128)S(1)}, u32[]{:S(2)}, u32[]{:S(2)}) collective-permute-start(f32[8,128]{1,0:T(8,128)S(1)} %get-tuple-element.39.refs_0_), channel_id=1, source_target_pairs={{0,3},{1,0},{2,1},{3,2},{4,7},{5,4},{6,5},{7,6},{8,11},{9,8},{10,9... | collective-permute-start | bytes 12296 | tf_op jit(solution)/shard_map/ppermute | solution.py:711
  49.8 3.7 %collective-permute-start.12 = (f32[8,128]{1,0:T(8,128)S(1)}, f32[8,128]{1,0:T(8,128)S(1)}, u32[]{:S(2)}, u32[]{:S(2)}) collective-permute-start(f32[8,128]{1,0:T(8,128)S(1)} %get-tuple-element.39.refs_0_), channel_id=1, source_target_pairs={{0,2},{1,3},{2,0},{3,1},{4,6},{5,7},{6,4},{7,5},{8,10},{9,11},{10,... | collective-permute-start | bytes 12296 | tf_op jit(solution)/shard_map/ppermute | solution.py:711
  50.9 3.0 %collective-permute-start.11 = (f32[8,128]{1,0:T(8,128)S(1)}, f32[8,128]{1,0:T(8,128)S(1)}, u32[]{:S(2)}, u32[]{:S(2)}) collective-permute-start(f32[8,128]{1,0:T(8,128)S(1)} %get-tuple-element.39.refs_0_), channel_id=1, source_target_pairs={{0,1},{1,2},{2,3},{3,0},{4,5},{5,6},{6,7},{7,4},{8,9},{9,10},{10,1... | collective-permute-start | bytes 12296 | tf_op jit(solution)/shard_map/ppermute | solution.py:711
  53.9 6.4 %collective-permute-start.14 = (f32[136,128]{1,0:T(8,128)S(1)}, f32[136,128]{1,0:T(8,128)S(1)}, u32[]{:S(2)}, u32[]{:S(2)}) collective-permute-start(f32[136,128]{1,0:T(8,128)S(1)} %get-tuple-element.41), channel_id=1, source_target_pairs={{0,4},{4,8},{8,12},{12,0},{1,5},{5,9},{9,13},{13,1},{2,6},{6,10},{... | collective-permute-start | bytes 208904 | tf_op jit(solution)/shard_map/ppermute | solution.py:578
  55.9 6.6 %collective-permute-start.15 = (f32[136,128]{1,0:T(8,128)S(1)}, f32[136,128]{1,0:T(8,128)S(1)}, u32[]{:S(2)}, u32[]{:S(2)}) collective-permute-start(f32[136,128]{1,0:T(8,128)S(1)} %get-tuple-element.42), channel_id=1, source_target_pairs={{0,8},{4,12},{8,0},{12,4},{1,9},{5,13},{9,1},{13,5},{2,10},{6,14},... | collective-permute-start | bytes 208904 | tf_op jit(solution)/shard_map/ppermute | solution.py:578
  56.8 5.7 %collective-permute-start.16 = (f32[136,128]{1,0:T(8,128)S(1)}, f32[136,128]{1,0:T(8,128)S(1)}, u32[]{:S(2)}, u32[]{:S(2)}) collective-permute-start(f32[136,128]{1,0:T(8,128)S(1)} %get-tuple-element.43), channel_id=1, source_target_pairs={{0,12},{4,0},{8,4},{12,8},{1,13},{5,1},{9,5},{13,9},{2,14},{6,2},{... | collective-permute-start | bytes 208904 | tf_op jit(solution)/shard_map/ppermute | solution.py:578

commit v18 on v17

--- a/solution.py
+++ b/solution.py
@@ -135,6 +135,7 @@
 LANES = 128
 SIDES = 2 * RADIUS
 HALO = 16
+FIELD_STEPS = 16383.0
 PARAM_LANE = 96
 VMEM = pl.BlockSpec(memory_space=pltpu.VMEM)
 SMEM = pl.BlockSpec(memory_space=pltpu.SMEM)
@@ -159,6 +160,14 @@
     edge[...] = total.astype(jnp.bfloat16)
 
 
+def fixed_point(value):
+    return jnp.floor(value * FIELD_STEPS + 0.5).astype(jnp.int32).astype(jnp.int16)
+
+
+def from_fixed_point(value):
+    return value.astype(jnp.int32).astype(jnp.float32) * (1.0 / FIELD_STEPS)
+
+
 def fields_kernel(me, estimate, direction, *fields):
     look_rows = estimate.shape[1]
     tiles = len(fields)
@@ -167,10 +176,8 @@
         columns = pl.ds(pl.multiple_of(tile * LANES, LANES), LANES)
         for epoch in range(estimate.shape[0]):
             here = slice(epoch * look_rows, (epoch + 1) * look_rows)
-            first, second = split_two(estimate[epoch, :, columns])
-            out[0, here, :] = first
-            out[1, here, :] = second
-            out[2, here, :] = direction[epoch, :, columns].astype(jnp.bfloat16)
+            out[0, here, :] = fixed_point(estimate[epoch, :, columns])
+            out[1, here, :] = fixed_point(direction[epoch, :, columns])
 
 
 def tile_of(slc, part, epoch, tile):
@@ -468,42 +475,38 @@
 def gradient_kernel(sizes, partner, *refs):
     tiles, epochs = sizes
     fields = refs[:tiles]
-    factors, pulls, gradient, sums, est, old = refs[tiles:]
+    factors, pulls, gradient, sums, est, old, shares = refs[tiles:]
     look_rows = est.shape[1]
     total = tiles * epochs
     f32 = jnp.float32
     for block in range(tiles):
-
-        @pl.loop(0, epochs, unroll=4)
-        def _(epoch):
-            here = pl.ds(pl.multiple_of(epoch * look_rows, look_rows), look_rows)
-            est[block * epochs + epoch] = fields[block][0, here, :].astype(f32) + fields[block][1, here, :].astype(f32)
-            old[block * epochs + epoch] = fields[block][2, here, :].astype(f32)
-            gradient[block * epochs + epoch] = jnp.zeros((look_rows, LANES), f32)
-
-    @pl.loop(0, total, unroll=2)
-    def _(epoch):
+        for epoch in range(epochs):
+            here = slice(epoch * look_rows, (epoch + 1) * look_rows)
+            est[block * epochs + epoch] = from_fixed_point(fields[block][0, here, :])
+            old[block * epochs + epoch] = from_fixed_point(fields[block][1, here, :])
+    mates = [[partner[epoch * SLOTS + slot] for slot in range(SLOTS)] for epoch in range(total)]
+    for epoch in range(total):
         own_est = est[epoch]
-        own = jnp.zeros((look_rows, LANES), f32)
-        mates = [partner[epoch * SLOTS + slot] for slot in range(SLOTS)]
-        values = []
-        for slot, mate in enumerate(mates):
+        own = None
+        for slot, mate in enumerate(mates[epoch]):
             pair = epoch * SLOTS + slot
             weighted = pulls[pair] - factors[pair] * (own_est - est[mate])
-            own = own + weighted
-            values.append(weighted)
-        for mate, weighted in zip(mates, values):
-            gradient[mate] = gradient[mate] - weighted
-        gradient[epoch] = gradient[epoch] + own
-
-    def totals(epoch, carry):
-        norm, crossed, grad_term, mixed_term, old_term = carry
+            own = weighted if own is None else own + weighted
+            shares[pair] = weighted
+        gradient[epoch] = own
+    for epoch in range(total):
+        values = [gradient[mate] - shares[epoch * SLOTS + slot] for slot, mate in enumerate(mates[epoch])]
+        for mate, value in zip(mates[epoch], values):
+            gradient[mate] = value
+
+    zero = jnp.zeros((look_rows, LANES), f32)
+    norm, crossed, grad_term, mixed_term, old_term = (zero,) * 5
+    for epoch in range(total):
         own_grad = gradient[epoch]
         own_old = old[epoch]
         norm = norm + own_grad * own_grad
         crossed = crossed + own_grad * own_old
-        for slot in range(SLOTS):
-            mate = partner[epoch * SLOTS + slot]
+        for slot, mate in enumerate(mates[epoch]):
             factor = factors[epoch * SLOTS + slot]
             grad_spread = own_grad - gradient[mate]
             old_spread = own_old - old[mate]
@@ -511,12 +514,8 @@
             grad_term = grad_term + pulled * grad_spread
             mixed_term = mixed_term + pulled * old_spread
             old_term = old_term + factor * old_spread * old_spread
-        return norm, crossed, grad_term, mixed_term, old_term
-
-    zero = jnp.zeros((look_rows, LANES), f32)
-    results = lax.fori_loop(0, total, totals, (zero,) * 5, unroll=2)
     sums[...] = jnp.zeros(sums.shape, f32)
-    for at, value in enumerate(results):
+    for at, value in enumerate((norm, crossed, grad_term, mixed_term, old_term)):
         sums[at : at + 1, :] = jnp.sum(value, axis=0, keepdims=True)
 
 
@@ -638,7 +637,7 @@
     estimate, direction, _ = lax.optimization_barrier((estimate, direction, messages))
     fields = pl.pallas_call(
         fields_kernel,
-        out_shape=(jax.ShapeDtypeStruct((3, epochs * look_rows, LANES), bf16),) * tiles,
+        out_shape=(jax.ShapeDtypeStruct((2, epochs * look_rows, LANES), jnp.int16),) * tiles,
         in_specs=[SMEM] + [VMEM] * 2,
         out_specs=(VMEM,) * tiles,
         compiler_params=params_of,
@@ -701,7 +700,8 @@
         ),
         in_specs=[SMEM] + [VMEM] * (tiles + 2),
         out_specs=(VMEM, VMEM),
-        scratch_shapes=[pltpu.VMEM((total, look_rows, LANES), f32)] * 2,
+        scratch_shapes=[pltpu.VMEM((total, look_rows, LANES), f32)] * 2
+        + [pltpu.VMEM((total * SLOTS, look_rows, LANES), f32)],
         compiler_params=params_of,
         cost_estimate=pl.CostEstimate(flops=10_000_000, bytes_accessed=8_000_000, transcendentals=0),
     )(partner, *field, factors, pulls)

time: 63.6 us -> 65.9 us (1.036)
  waiting for transfers between devices: 21.4 us -> 23.9 us
    ppermute x4, waiting for transfers between devices: 0.01 us -> 3.55 us  [halo(): lax.ppermute(border(jnp.where(space == 0, rows - HALO, 0)), 'space', [(0,...]
    ppermute x9, waiting for transfers between devices: 18.3 us -> 17.4 us  [to_ahead(): return lax.ppermute(x, axis, [(i, (i + by) % size) for i in range(size)])]
  transfers between devices with their start and end apart: 17 -> 17, of which waited for: 8 -> 7; matrix products, arithmetic and copies ran while one was open for 2% -> 2% of each run, Pallas kernels for 9% -> 9%
where the time goes in v18:
time: 65.9 us; the launch traced here: 65.8 us
  starting transfers between devices  26.7 us (41%)
  waiting for transfers between devices  23.9 us (36%)
  Pallas kernels  10.1 us (15%)
  local copies, waits for them, and re-layouts  3.3 us (5%)
  between operations  1.43 us (2%)
    ppermute x9, starting transfers between devices, to_ahead(): return lax.ppermute(x, axis, [(i, (i + by) % size) for i in range(size)])  20.1 us
    ppermute x9, waiting for transfers between devices, to_ahead(): return lax.ppermute(x, axis, [(i, (i + by) % size) for i in range(size)])  17.4 us
    pallas_call x1, Pallas kernels, transposed_plan(): pl.pallas_call(functools.partial(pair_kernel, (epochs, rows, len(operands...  6.06 us
    ppermute x4, starting transfers between devices, halo(): lax.ppermute(border(jnp.where(space == 0, rows - HALO, 0)), 'space', [(0,...  5.27 us
    ppermute x4, waiting for transfers between devices, halo(): lax.ppermute(border(jnp.where(space == 0, rows - HALO, 0)), 'space', [(0,...  3.55 us
    ppermute x3, waiting for transfers between devices, transposed_plan(): lax.ppermute(sums, place, [(i, (i + by) % count) for i in range(count)])  2.92 us
    unnamed x20, local copies, waits for them, and re-layouts  2.76 us
    pallas_call x1, Pallas kernels, transposed_plan(): pl.pallas_call(functools.partial(gradient_kernel, (tiles, epochs)), out_s...  1.48 us
  transfers between devices with their start and end apart: 17, of which 7 were waited for; matrix products, arithmetic and copies ran while one was open for 2% of the time, Pallas kernels for 9%

profile of v18, /device:TPU:0, one launch (start us, length us, event | category | flops | bytes accessed | tf_op | source)
XLA Modules:
  0.0 65.8 jit_solution(12045236143648200734)
XLA Ops:
  0.6 1.2 %copy-done = bf16[2,8,64,512]{3,2,1,0:T(8,128)(2,1)S(1)} copy-done((bf16[2,8,64,512]{3,2,1,0:T(8,128)(2,1)S(1)}, bf16[2,8,64,512]{3,2,1,0:T(8,128)(2,1)}, u32[]{:S(2)}) %copy-start) | copy-done | bytes 1048600
  1.9 0.2 shard_map.104
  2.1 0.5 collective-permute-start
  2.6 0.7 %copy-done.7 = s32[8,4]{0,1:T(4,128)S(1)} copy-done((s32[8,4]{0,1:T(4,128)S(1)}, s32[8,4]{0,1:T(4,128)}, u32[]{:S(2)}) %copy-start.7) | copy-done | bytes 152
  3.3 0.1 copy.15
  3.4 0.7 %copy-done.8 = f32[8,4]{0,1:T(4,128)S(1)} copy-done((f32[8,4]{0,1:T(4,128)S(1)}, f32[8,4]{0,1:T(4,128)}, u32[]{:S(2)}) %copy-start.8) | copy-done | bytes 152
  4.1 0.1 copy.16
  4.1 0.1 select_maximum_fusion.params
  4.2 0.1 add_convert_fusion.present
  4.3 0.0 copy-start.3
  4.3 1.3 %shard_map.105 = (bf16[1088,128]{1,0:T(8,128)(2,1)S(1)}, bf16[1088,128]{1,0:T(8,128)(2,1)S(1)}, bf16[1088,128]{1,0:T(8,128)(2,1)S(1)}, bf16[1088,128]{1,0:T(8,128)(2,1)S(1)}) custom-call(s32[1]{0:T(128)} %bitcast.me, f32[2]{0:T(128)S(1)} %add_convert_fusion.present, bf16[2,8,64,512]{3,2,1,0:T(8,128)(2,1)S(1)} %copy-done.1, ...), custom_call_target="tpu_custom_call" | custom-call | flops 3000000 | bytes 4000000 | tf_op jit(solution)/shard_map/pallas_call | solution.py:613
  5.6 2.7 %collective-permute-start.3 = (bf16[1088,128]{1,0:T(8,128)(2,1)S(1)}, bf16[1088,128]{1,0:T(8,128)(2,1)S(1)}, u32[]{:S(2)}, u32[]{:S(2)}) collective-permute-start(bf16[1088,128]{1,0:T(8,128)(2,1)S(1)} %get-tuple-element.24), channel_id=1, source_target_pairs={{0,4},{4,8},{8,12},{12,0},{1,5},{5,9},{9,13},{13,1},{2,6},{6,10},{... | collective-permute-start | bytes 835592 | tf_op jit(solution)/shard_map/ppermute | solution.py:577
  8.3 2.6 %collective-permute-start.2 = (bf16[1088,128]{1,0:T(8,128)(2,1)S(1)}, bf16[1088,128]{1,0:T(8,128)(2,1)S(1)}, u32[]{:S(2)}, u32[]{:S(2)}) collective-permute-start(bf16[1088,128]{1,0:T(8,128)(2,1)S(1)} %get-tuple-element.25), channel_id=1, source_target_pairs={{0,8},{4,12},{8,0},{12,4},{1,9},{5,13},{9,1},{13,5},{2,10},{6,14},... | collective-permute-start | bytes 835592 | tf_op jit(solution)/shard_map/ppermute | solution.py:577
  10.8 0.1 add_convert_fusion.1.present
  10.9 1.3 %collective-permute-start.1 = (bf16[1088,128]{1,0:T(8,128)(2,1)S(1)}, bf16[1088,128]{1,0:T(8,128)(2,1)S(1)}, u32[]{:S(2)}, u32[]{:S(2)}) collective-permute-start(bf16[1088,128]{1,0:T(8,128)(2,1)S(1)} %get-tuple-element.26), channel_id=1, source_target_pairs={{0,12},{4,0},{8,4},{12,8},{1,13},{5,1},{9,5},{13,9},{2,14},{6,2},{... | collective-permute-start | bytes 835592 | tf_op jit(solution)/shard_map/ppermute | solution.py:577
  12.3 0.1 slice.24
  12.4 1.5 %collective-permute-start.7 = (bf16[272,128]{1,0:T(8,128)(2,1)S(1)}, bf16[272,128]{1,0:T(8,128)(2,1)S(1)}, u32[]{:S(2)}, u32[]{:S(2)}) collective-permute-start(bf16[272,128]{1,0:T(8,128)(2,1)S(1)} %bitcast.17), channel_id=1, source_target_pairs={{0,2},{2,0},{1,3},{3,1},{4,6},{6,4},{5,7},{7,5},{8,10},{10,8},{9,1... | collective-permute-start | bytes 208904 | tf_op jit(solution)/shard_map/ppermute | solution.py:632
  13.9 0.1 shard_map.106
  14.0 4.0 %collective-permute-done.3.refs_3_ = bf16[1088,128]{1,0:T(8,128)(2,1)S(1)} collective-permute-done((bf16[1088,128]{1,0:T(8,128)(2,1)S(1)}, bf16[1088,128]{1,0:T(8,128)(2,1)S(1)}, u32[]{:S(2)}, u32[]{:S(2)}) %collective-permute-start.3) | collective-permute-done | bytes 278560 | tf_op jit(solution)/shard_map/ppermute | solution.py:577
  17.9 1.7 %collective-permute-start.10 = (bf16[272,128]{1,0:T(8,128)(2,1)S(1)}, bf16[272,128]{1,0:T(8,128)(2,1)S(1)}, u32[]{:S(2)}, u32[]{:S(2)}) collective-permute-start(bf16[272,128]{1,0:T(8,128)(2,1)S(1)} %bitcast.19), channel_id=1, source_target_pairs={{0,2},{2,0},{1,3},{3,1},{4,6},{6,4},{5,7},{7,5},{8,10},{10,8},{9,1... | collective-permute-start | bytes 208904 | tf_op jit(solution)/shard_map/ppermute | solution.py:632
  19.6 10.0 %collective-permute-done.2.refs_2_ = bf16[1088,128]{1,0:T(8,128)(2,1)S(1)} collective-permute-done((bf16[1088,128]{1,0:T(8,128)(2,1)S(1)}, bf16[1088,128]{1,0:T(8,128)(2,1)S(1)}, u32[]{:S(2)}, u32[]{:S(2)}) %collective-permute-start.2) | collective-permute-done | bytes 278560 | tf_op jit(solution)/shard_map/ppermute | solution.py:577
  29.6 1.6 %collective-permute-start.9 = (bf16[272,128]{1,0:T(8,128)(2,1)S(1)}, bf16[272,128]{1,0:T(8,128)(2,1)S(1)}, u32[]{:S(2)}, u32[]{:S(2)}) collective-permute-start(bf16[272,128]{1,0:T(8,128)(2,1)S(1)} %bitcast.18), channel_id=1, source_target_pairs={{0,2},{2,0},{1,3},{3,1},{4,6},{6,4},{5,7},{7,5},{8,10},{10,8},{9,1... | collective-permute-start | bytes 208904 | tf_op jit(solution)/shard_map/ppermute | solution.py:632
  31.2 0.0 collective-permute-done.1.refs_1_
  31.2 0.1 slice.34
  31.3 0.1 slice.33
  31.4 0.1 slice.32
  31.4 0.1 slice_add_fusion
  31.5 7.5 %collective-permute-start.4 = (s16[2,128,128]{2,1,0:T(8,128)(2,1)S(1)}, s16[2,128,128]{2,1,0:T(8,128)(2,1)S(1)}, u32[]{:S(2)}, u32[]{:S(2)}) collective-permute-start(s16[2,128,128]{2,1,0:T(8,128)(2,1)S(1)} %get-tuple-element.33), channel_id=1, source_target_pairs={{0,12},{4,0},{8,4},{12,8},{1,13},{5,1},{9,5},{13,9},{2,14},{6,2},{... | collective-permute-start | bytes 196616 | tf_op jit(solution)/shard_map/ppermute | solution.py:577
  39.0 0.0 copy-start.4
  39.1 0.7 %collective-permute-start.6 = (s16[2,128,128]{2,1,0:T(8,128)(2,1)S(1)}, s16[2,128,128]{2,1,0:T(8,128)(2,1)S(1)}, u32[]{:S(2)}, u32[]{:S(2)}) collective-permute-start(s16[2,128,128]{2,1,0:T(8,128)(2,1)S(1)} %get-tuple-element.35), channel_id=1, source_target_pairs={{0,4},{4,8},{8,12},{12,0},{1,5},{5,9},{9,13},{13,1},{2,6},{6,10},{... | collective-permute-start | bytes 196616 | tf_op jit(solution)/shard_map/ppermute | solution.py:577
  39.7 0.0 collective-permute-done.10.refs_7_
  39.7 0.5 collective-permute-start.8
  40.3 0.1 reshape.41.weight
  40.4 0.1 reshape.40.partner
  40.5 3.5 %collective-permute-done.8.refs_5_ = bf16[272,128]{1,0:T(8,128)(2,1)S(1)} collective-permute-done((bf16[272,128]{1,0:T(8,128)(2,1)S(1)}, bf16[272,128]{1,0:T(8,128)(2,1)S(1)}, u32[]{:S(2)}, u32[]{:S(2)}) %collective-permute-start.8) | collective-permute-done | bytes 69664 | tf_op jit(solution)/shard_map/ppermute | solution.py:632
  44.1 6.1 %shard_map.107 = (f32[128,16,128]{2,1,0:T(8,128)S(1)}, f32[128,16,128]{2,1,0:T(8,128)S(1)}) custom-call(s32[128]{0:T(128)S(1)} %reshape.40.partner, f32[128]{0:T(128)S(1)} %reshape.41.weight, f32[2]{0:T(128)S(1)} %add_convert_fusion.1.present, bf16[96,96]{1,0:T(8,128)(2,1)S(1)} %copy-done.6, bf16[256,128]{1,0:T(8,128)(2,1)S(1)} %copy-done.5, ...), custom_call_target="tpu_custom_call" | custom-call | flops 20000000 | bytes 30000000 | tf_op jit(solution)/shard_map/pallas_call | solution.py:679
  50.2 1.5 %shard_map.108 = (f32[32,16,128]{2,1,0:T(8,128)S(1)}, f32[8,128]{1,0:T(8,128)S(1)}) custom-call(s32[128]{0:T(128)S(1)} %reshape.40.partner, s16[2,128,128]{2,1,0:T(8,128)(2,1)S(1)} %get-tuple-element.29.refs_0_, s16[2,128,128]{2,1,0:T(8,128)(2,1)S(1)} %collective-permute-done.4.refs_1_, s16[2,128,128]{2,1,0:T(8,128)(2,1)S(1)} %collective-permute-done.5.refs_2_, ...), custom_call_target="tpu_custom_call" | custom-call | flops 10000000 | bytes 8000000 | tf_op jit(solution)/shard_map/pallas_call | solution.py:695
  51.6 0.1 collective-permute-start.13
  51.7 0.6 collective-permute-start.12
  52.3 0.2 collective-permute-start.11
  52.5 0.6 collective-permute-done.13.refs_3_
  53.0 2.4 %collective-permute-done.12.refs_2_ = f32[8,128]{1,0:T(8,128)S(1)} collective-permute-done((f32[8,128]{1,0:T(8,128)S(1)}, f32[8,128]{1,0:T(8,128)S(1)}, u32[]{:S(2)}, u32[]{:S(2)}) %collective-permute-start.12) | collective-permute-done | bytes 4128 | tf_op jit(solution)/shard_map/ppermute | solution.py:711
  55.4 2.9 %collective-permute-start.14 = (f32[136,128]{1,0:T(8,128)S(1)}, f32[136,128]{1,0:T(8,128)S(1)}, u32[]{:S(2)}, u32[]{:S(2)}) collective-permute-start(f32[136,128]{1,0:T(8,128)S(1)} %get-tuple-element.41), channel_id=1, source_target_pairs={{0,4},{4,8},{8,12},{12,0},{1,5},{5,9},{9,13},{13,1},{2,6},{6,10},{... | collective-permute-start | bytes 208904 | tf_op jit(solution)/shard_map/ppermute | solution.py:577
  58.3 0.9 %collective-permute-start.15 = (f32[136,128]{1,0:T(8,128)S(1)}, f32[136,128]{1,0:T(8,128)S(1)}, u32[]{:S(2)}, u32[]{:S(2)}) collective-permute-start(f32[136,128]{1,0:T(8,128)S(1)} %get-tuple-element.42), channel_id=1, source_target_pairs={{0,8},{4,12},{8,0},{12,4},{1,9},{5,13},{9,1},{13,5},{2,10},{6,14},... | collective-permute-start | bytes 208904 | tf_op jit(solution)/shard_map/ppermute | solution.py:577
  59.2 1.5 %collective-permute-start.16 = (f32[136,128]{1,0:T(8,128)S(1)}, f32[136,128]{1,0:T(8,128)S(1)}, u32[]{:S(2)}, u32[]{:S(2)}) collective-permute-start(f32[136,128]{1,0:T(8,128)S(1)} %get-tuple-element.43), channel_id=1, source_target_pairs={{0,12},{4,0},{8,4},{12,8},{1,13},{5,1},{9,5},{13,9},{2,14},{6,2},{... | collective-permute-start | bytes 208904 | tf_op jit(solution)/shard_map/ppermute | solution.py:577
  61.4 0.8 %collective-permute-done.14.refs_1_ = f32[136,128]{1,0:T(8,128)S(1)} collective-permute-done((f32[136,128]{1,0:T(8,128)S(1)}, f32[136,128]{1,0:T(8,128)S(1)}, u32[]{:S(2)}, u32[]{:S(2)}) %collective-permute-start.14) | collective-permute-done | bytes 69664 | tf_op jit(solution)/shard_map/ppermute | solution.py:577
  62.2 2.6 %collective-permute-done.15.refs_2_ = f32[136,128]{1,0:T(8,128)S(1)} collective-permute-done((f32[136,128]{1,0:T(8,128)S(1)}, f32[136,128]{1,0:T(8,128)S(1)}, u32[]{:S(2)}, u32[]{:S(2)}) %collective-permute-start.15) | collective-permute-done | bytes 69664 | tf_op jit(solution)/shard_map/ppermute | solution.py:577
  64.8 0.9 %shard_map.110 = (f32[8,16,512]{2,1,0:T(8,128)}, f32[8,16,512]{2,1,0:T(8,128)}) custom-call(s32[1]{0:T(128)} %bitcast.me, f32[1]{0:T(128)S(6)} %copy.19.prev_mean, f32[8,16,512]{2,1,0:T(8,128)S(1)} %copy-done.2, f32[8,16,512]{2,1,0:T(8,128)S(1)} %copy-done.3, f32[136,128]{1,0:T(8,128)S(1)} %get-tuple-element.40.refs_0_, ...), custom_call_target="tpu_custom_call" | custom-call | flops 1000000 | bytes 2000000 | tf_op jit(solution)/shard_map/pallas_call | solution.py:722
  (30 shorter events, 0.1 us)
Async XLA Ops:
  0.6 1.2 %copy-start = (bf16[2,8,64,512]{3,2,1,0:T(8,128)(2,1)S(1)}, bf16[2,8,64,512]{3,2,1,0:T(8,128)(2,1)}, u32[]{:S(2)}) copy-start(bf16[2,8,64,512]{3,2,1,0:T(8,128)(2,1)} %slc.1) | copy-start | bytes 3145732
  1.9 2.4 %copy-start.1 = (bf16[2,8,64,512]{3,2,1,0:T(8,128)(2,1)S(1)}, bf16[2,8,64,512]{3,2,1,0:T(8,128)(2,1)}, u32[]{:S(2)}) copy-start(bf16[2,8,64,512]{3,2,1,0:T(8,128)(2,1)} %slc.1) | copy-start | bytes 3145732
  2.1 2.2 %collective-permute-start = (bf16[64,128]{1,0:T(8,128)(2,1)S(1)}, bf16[64,128]{1,0:T(8,128)(2,1)S(1)}, u32[]{:S(2)}, u32[]{:S(2)}) collective-permute-start(bf16[64,128]{1,0:T(8,128)(2,1)S(1)} %shard_map.104), channel_id=1, source_target_pairs={{0,1},{1,0},{2,3},{3,2},{4,5},{5,4},{6,7},{7,6},{8,9},{9,8},{10,11... | collective-permute-start | bytes 49160 | tf_op jit(solution)/shard_map/ppermute | solution.py:568
  2.6 0.7 %copy-start.7 = (s32[8,4]{0,1:T(4,128)S(1)}, s32[8,4]{0,1:T(4,128)}, u32[]{:S(2)}) copy-start(s32[8,4]{0,1:T(4,128)} %param.10) | copy-start | bytes 388
  3.4 0.7 %copy-start.8 = (f32[8,4]{0,1:T(4,128)S(1)}, f32[8,4]{0,1:T(4,128)}, u32[]{:S(2)}) copy-start(f32[8,4]{0,1:T(4,128)} %param.11) | copy-start | bytes 388
  4.3 9.6 %copy-start.2 = (f32[8,16,512]{2,1,0:T(8,128)S(1)}, f32[8,16,512]{2,1,0:T(8,128)}, u32[]{:S(2)}) copy-start(f32[8,16,512]{2,1,0:T(8,128)} %estimate.1) | copy-start | bytes 786436
  4.3 9.5 %copy-start.3 = (f32[8,16,512]{2,1,0:T(8,128)S(1)}, f32[8,16,512]{2,1,0:T(8,128)}, u32[]{:S(2)}) copy-start(f32[8,16,512]{2,1,0:T(8,128)} %direction.1) | copy-start | bytes 786436
  5.6 12.3 %collective-permute-start.3 = (bf16[1088,128]{1,0:T(8,128)(2,1)S(1)}, bf16[1088,128]{1,0:T(8,128)(2,1)S(1)}, u32[]{:S(2)}, u32[]{:S(2)}) collective-permute-start(bf16[1088,128]{1,0:T(8,128)(2,1)S(1)} %get-tuple-element.24), channel_id=1, source_target_pairs={{0,4},{4,8},{8,12},{12,0},{1,5},{5,9},{9,13},{13,1},{2,6},{6,10},{... | collective-permute-start | bytes 835592 | tf_op jit(solution)/shard_map/ppermute | solution.py:577
  8.3 21.4 %collective-permute-start.2 = (bf16[1088,128]{1,0:T(8,128)(2,1)S(1)}, bf16[1088,128]{1,0:T(8,128)(2,1)S(1)}, u32[]{:S(2)}, u32[]{:S(2)}) collective-permute-start(bf16[1088,128]{1,0:T(8,128)(2,1)S(1)} %get-tuple-element.25), channel_id=1, source_target_pairs={{0,8},{4,12},{8,0},{12,4},{1,9},{5,13},{9,1},{13,5},{2,10},{6,14},... | collective-permute-start | bytes 835592 | tf_op jit(solution)/shard_map/ppermute | solution.py:577
  10.9 20.3 %collective-permute-start.1 = (bf16[1088,128]{1,0:T(8,128)(2,1)S(1)}, bf16[1088,128]{1,0:T(8,128)(2,1)S(1)}, u32[]{:S(2)}, u32[]{:S(2)}) collective-permute-start(bf16[1088,128]{1,0:T(8,128)(2,1)S(1)} %get-tuple-element.26), channel_id=1, source_target_pairs={{0,12},{4,0},{8,4},{12,8},{1,13},{5,1},{9,5},{13,9},{2,14},{6,2},{... | collective-permute-start | bytes 835592 | tf_op jit(solution)/shard_map/ppermute | solution.py:577
  12.4 26.7 %collective-permute-start.7 = (bf16[272,128]{1,0:T(8,128)(2,1)S(1)}, bf16[272,128]{1,0:T(8,128)(2,1)S(1)}, u32[]{:S(2)}, u32[]{:S(2)}) collective-permute-start(bf16[272,128]{1,0:T(8,128)(2,1)S(1)} %bitcast.17), channel_id=1, source_target_pairs={{0,2},{2,0},{1,3},{3,1},{4,6},{6,4},{5,7},{7,5},{8,10},{10,8},{9,1... | collective-permute-start | bytes 208904 | tf_op jit(solution)/shard_map/ppermute | solution.py:632
  17.9 21.8 %collective-permute-start.10 = (bf16[272,128]{1,0:T(8,128)(2,1)S(1)}, bf16[272,128]{1,0:T(8,128)(2,1)S(1)}, u32[]{:S(2)}, u32[]{:S(2)}) collective-permute-start(bf16[272,128]{1,0:T(8,128)(2,1)S(1)} %bitcast.19), channel_id=1, source_target_pairs={{0,2},{2,0},{1,3},{3,1},{4,6},{6,4},{5,7},{7,5},{8,10},{10,8},{9,1... | collective-permute-start | bytes 208904 | tf_op jit(solution)/shard_map/ppermute | solution.py:632
  29.6 10.9 %collective-permute-start.9 = (bf16[272,128]{1,0:T(8,128)(2,1)S(1)}, bf16[272,128]{1,0:T(8,128)(2,1)S(1)}, u32[]{:S(2)}, u32[]{:S(2)}) collective-permute-start(bf16[272,128]{1,0:T(8,128)(2,1)S(1)} %bitcast.18), channel_id=1, source_target_pairs={{0,2},{2,0},{1,3},{3,1},{4,6},{6,4},{5,7},{7,5},{8,10},{10,8},{9,1... | collective-permute-start | bytes 208904 | tf_op jit(solution)/shard_map/ppermute | solution.py:632
  31.5 18.6 %collective-permute-start.4 = (s16[2,128,128]{2,1,0:T(8,128)(2,1)S(1)}, s16[2,128,128]{2,1,0:T(8,128)(2,1)S(1)}, u32[]{:S(2)}, u32[]{:S(2)}) collective-permute-start(s16[2,128,128]{2,1,0:T(8,128)(2,1)S(1)} %get-tuple-element.33), channel_id=1, source_target_pairs={{0,12},{4,0},{8,4},{12,8},{1,13},{5,1},{9,5},{13,9},{2,14},{6,2},{... | collective-permute-start | bytes 196616 | tf_op jit(solution)/shard_map/ppermute | solution.py:577
  39.0 11.1 %collective-permute-start.5 = (s16[2,128,128]{2,1,0:T(8,128)(2,1)S(1)}, s16[2,128,128]{2,1,0:T(8,128)(2,1)S(1)}, u32[]{:S(2)}, u32[]{:S(2)}) collective-permute-start(s16[2,128,128]{2,1,0:T(8,128)(2,1)S(1)} %get-tuple-element.34), channel_id=1, source_target_pairs={{0,8},{4,12},{8,0},{12,4},{1,9},{5,13},{9,1},{13,5},{2,10},{6,14},... | collective-permute-start | bytes 196616 | tf_op jit(solution)/shard_map/ppermute | solution.py:577
  39.0 5.0 %copy-start.5 = (bf16[256,128]{1,0:T(8,128)(2,1)S(1)}, bf16[256,128]{1,0:T(8,128)(2,1)}, u32[]{:S(2)}) copy-start(bf16[256,128]{1,0:T(8,128)(2,1)} %constant.33.clone.band) | copy-start | bytes 196612
  39.0 5.0 %copy-start.6 = (bf16[96,96]{1,0:T(8,128)(2,1)S(1)}, bf16[96,96]{1,0:T(8,128)(2,1)}, u32[]{:S(2)}) copy-start(bf16[96,96]{1,0:T(8,128)(2,1)} %constant.32.clone.order) | copy-start | bytes 55300
  39.0 5.0 %copy-start.4 = (bf16[256,128]{1,0:T(8,128)(2,1)S(1)}, bf16[256,128]{1,0:T(8,128)(2,1)}, u32[]{:S(2)}) copy-start(bf16[256,128]{1,0:T(8,128)(2,1)} %constant.34.clone.rim_band) | copy-start | bytes 196612
  39.1 11.1 %collective-permute-start.6 = (s16[2,128,128]{2,1,0:T(8,128)(2,1)S(1)}, s16[2,128,128]{2,1,0:T(8,128)(2,1)S(1)}, u32[]{:S(2)}, u32[]{:S(2)}) collective-permute-start(s16[2,128,128]{2,1,0:T(8,128)(2,1)S(1)} %get-tuple-element.35), channel_id=1, source_target_pairs={{0,4},{4,8},{8,12},{12,0},{1,5},{5,9},{9,13},{13,1},{2,6},{6,10},{... | collective-permute-start | bytes 196616 | tf_op jit(solution)/shard_map/ppermute | solution.py:577
  39.7 4.3 %collective-permute-start.8 = (bf16[272,128]{1,0:T(8,128)(2,1)S(1)}, bf16[272,128]{1,0:T(8,128)(2,1)S(1)}, u32[]{:S(2)}, u32[]{:S(2)}) collective-permute-start(bf16[272,128]{1,0:T(8,128)(2,1)S(1)} %bitcast.20), channel_id=1, source_target_pairs={{0,2},{2,0},{1,3},{3,1},{4,6},{6,4},{5,7},{7,5},{8,10},{10,8},{9,1... | collective-permute-start | bytes 208904 | tf_op jit(solution)/shard_map/ppermute | solution.py:632
  51.6 1.4 %collective-permute-start.13 = (f32[8,128]{1,0:T(8,128)S(1)}, f32[8,128]{1,0:T(8,128)S(1)}, u32[]{:S(2)}, u32[]{:S(2)}) collective-permute-start(f32[8,128]{1,0:T(8,128)S(1)} %get-tuple-element.39.refs_0_), channel_id=1, source_target_pairs={{0,3},{1,0},{2,1},{3,2},{4,7},{5,4},{6,5},{7,6},{8,11},{9,8},{10,9... | collective-permute-start | bytes 12296 | tf_op jit(solution)/shard_map/ppermute | solution.py:711
  51.7 3.7 %collective-permute-start.12 = (f32[8,128]{1,0:T(8,128)S(1)}, f32[8,128]{1,0:T(8,128)S(1)}, u32[]{:S(2)}, u32[]{:S(2)}) collective-permute-start(f32[8,128]{1,0:T(8,128)S(1)} %get-tuple-element.39.refs_0_), channel_id=1, source_target_pairs={{0,2},{1,3},{2,0},{3,1},{4,6},{5,7},{6,4},{7,5},{8,10},{9,11},{10,... | collective-permute-start | bytes 12296 | tf_op jit(solution)/shard_map/ppermute | solution.py:711
  52.3 3.1 %collective-permute-start.11 = (f32[8,128]{1,0:T(8,128)S(1)}, f32[8,128]{1,0:T(8,128)S(1)}, u32[]{:S(2)}, u32[]{:S(2)}) collective-permute-start(f32[8,128]{1,0:T(8,128)S(1)} %get-tuple-element.39.refs_0_), channel_id=1, source_target_pairs={{0,1},{1,2},{2,3},{3,0},{4,5},{5,6},{6,7},{7,4},{8,9},{9,10},{10,1... | collective-permute-start | bytes 12296 | tf_op jit(solution)/shard_map/ppermute | solution.py:711
  55.4 6.8 %collective-permute-start.14 = (f32[136,128]{1,0:T(8,128)S(1)}, f32[136,128]{1,0:T(8,128)S(1)}, u32[]{:S(2)}, u32[]{:S(2)}) collective-permute-start(f32[136,128]{1,0:T(8,128)S(1)} %get-tuple-element.41), channel_id=1, source_target_pairs={{0,4},{4,8},{8,12},{12,0},{1,5},{5,9},{9,13},{13,1},{2,6},{6,10},{... | collective-permute-start | bytes 208904 | tf_op jit(solution)/shard_map/ppermute | solution.py:577
  58.3 6.5 %collective-permute-start.15 = (f32[136,128]{1,0:T(8,128)S(1)}, f32[136,128]{1,0:T(8,128)S(1)}, u32[]{:S(2)}, u32[]{:S(2)}) collective-permute-start(f32[136,128]{1,0:T(8,128)S(1)} %get-tuple-element.42), channel_id=1, source_target_pairs={{0,8},{4,12},{8,0},{12,4},{1,9},{5,13},{9,1},{13,5},{2,10},{6,14},... | collective-permute-start | bytes 208904 | tf_op jit(solution)/shard_map/ppermute | solution.py:577
  59.2 5.6 %collective-permute-start.16 = (f32[136,128]{1,0:T(8,128)S(1)}, f32[136,128]{1,0:T(8,128)S(1)}, u32[]{:S(2)}, u32[]{:S(2)}) collective-permute-start(f32[136,128]{1,0:T(8,128)S(1)} %get-tuple-element.43), channel_id=1, source_target_pairs={{0,12},{4,0},{8,4},{12,8},{1,13},{5,1},{9,5},{13,9},{2,14},{6,2},{... | collective-permute-start | bytes 208904 | tf_op jit(solution)/shard_map/ppermute | solution.py:577

commit v19 on v18

--- a/solution.py
+++ b/solution.py
@@ -1,4 +1,5 @@
 import functools
+import math
 
 import jax
 import jax.numpy as jnp
@@ -136,6 +137,7 @@
 SIDES = 2 * RADIUS
 HALO = 16
 FIELD_STEPS = 16383.0
+GRADIENT_STEPS = 32000.0
 PARAM_LANE = 96
 VMEM = pl.BlockSpec(memory_space=pltpu.VMEM)
 SMEM = pl.BlockSpec(memory_space=pltpu.SMEM)
@@ -519,29 +521,62 @@
         sums[at : at + 1, :] = jnp.sum(value, axis=0, keepdims=True)
 
 
-def return_kernel(tiles, gradient, *refs):
-    pieces = refs[-tiles:]
-    shared = refs[:-tiles]
+def exponent_of(size):
+    power = jnp.ceil(jnp.log(jnp.maximum(size, 1e-30)) * (1.0 / math.log(2.0)))
+    return jnp.clip(power, -110.0, 110.0)
+
+
+def whole(value):
+    return jnp.floor(value + 0.5).astype(jnp.int32).astype(jnp.int16)
+
+
+def number_of(value):
+    return value.astype(jnp.int32).astype(jnp.float32)
+
+
+def code_kernel(gradient, *coded):
+    epochs = gradient.shape[0] // (len(coded) + 1)
+    look_rows = gradient.shape[1]
+    for number, out in enumerate(coded):
+        powers = []
+        for epoch in range(epochs):
+            value = gradient[(number + 1) * epochs + epoch]
+            power = exponent_of(jnp.max(jnp.abs(value), axis=0, keepdims=True))
+            out[epoch * look_rows : (epoch + 1) * look_rows, :] = whole(value * (jnp.exp2(-power) * GRADIENT_STEPS))
+            powers.append(power)
+        powers.append(jnp.zeros((HALO - epochs, LANES), jnp.float32))
+        out[epochs * look_rows :, :] = whole(jnp.concatenate(powers, axis=0))
+
+
+def return_kernel(tiles, *refs):
+    coded, shared = refs[: tiles - 1], refs[tiles - 1 : -tiles]
+    own, pieces = refs[-tiles], refs[1 - tiles :]
     total = shared[0][...]
     for other in shared[1:]:
         total = total + other[...]
-    epochs = gradient.shape[0] // len(pieces)
-    look_rows = gradient.shape[1]
-    for number, piece in enumerate(pieces):
-        for epoch in range(epochs):
-            piece[epoch * look_rows : (epoch + 1) * look_rows, :] = gradient[number * epochs + epoch]
-        piece[epochs * look_rows :, :] = total
-
-
-def update_kernel(cell_count, me, prev_mean, estimate, direction, *refs):
+    own[...] = total
+    power = exponent_of(jnp.abs(total))
+    share = total * jnp.exp2(-power) * float(1 << 14)
+    high = jnp.floor(share + 0.5)
+    low = (share - high) * float(1 << 15)
+    parts = whole(jnp.concatenate([power, high, low, jnp.zeros_like(power)], axis=0))
+    for piece, source in zip(pieces, coded):
+        piece[: source.shape[0], :] = source[...]
+        piece[source.shape[0] :, :] = parts
+
+
+def update_kernel(cell_count, me, prev_mean, estimate, direction, gradient, sums, *refs):
+    pieces = refs[:-2]
     new_estimate, new_direction = refs[-2:]
-    pieces = refs[:-2]
-    tiles = len(pieces)
+    tiles = len(pieces) + 1
     epochs = estimate.shape[0]
     look_rows = estimate.shape[1]
-    total = pieces[0][epochs * look_rows :, :]
-    for piece in pieces[1:]:
-        total = total + piece[epochs * look_rows :, :]
+    coded_rows = epochs * look_rows + HALO
+    total = sums[...]
+    for piece in pieces:
+        parts = number_of(piece[coded_rows:, :])
+        value = (parts[8:16] + parts[16:24] * (1.0 / (1 << 15))) * (1.0 / (1 << 14))
+        total = total + value * jnp.exp2(parts[:8])
     total = jnp.sum(total, axis=1, keepdims=True)
     grad_norm, crossed, grad_term, mixed, old_term = (total[at : at + 1, :] for at in range(5))
     momentum = grad_norm / cell_count / prev_mean[0]
@@ -549,12 +584,18 @@
     step = (grad_norm + momentum * crossed) / curvature
     momentum = jnp.broadcast_to(momentum, (look_rows, LANES))
     step = jnp.broadcast_to(step, (look_rows, LANES))
-    for shift, piece in enumerate(pieces):
+    for shift in range(tiles):
         tile = lax.rem(me[0] - shift + tiles, tiles)
         columns = pl.ds(pl.multiple_of(tile * LANES, LANES), LANES)
+        if shift > 0:
+            piece = pieces[shift - 1]
+            scale = jnp.exp2(number_of(piece[epochs * look_rows : coded_rows, :])) * (1.0 / GRADIENT_STEPS)
         for epoch in range(epochs):
-            gradient = piece[epoch * look_rows : (epoch + 1) * look_rows, :]
-            moved = gradient + momentum * direction[epoch, :, columns]
+            if shift == 0:
+                value = gradient[epoch]
+            else:
+                value = number_of(piece[epoch * look_rows : (epoch + 1) * look_rows, :]) * scale[epoch : epoch + 1, :]
+            moved = value + momentum * direction[epoch, :, columns]
             new_direction[epoch, :, columns] = moved
             new_estimate[epoch, :, columns] = estimate[epoch, :, columns] + step * moved
 
@@ -653,7 +694,7 @@
         return mate.reshape(-1), weight.reshape(-1)
 
     halos = [halo([array.reshape(-1, rows, LANES)]) for array in block]
-    late = lax.optimization_barrier((fields, block))[0]
+    late = lax.optimization_barrier((fields, block, halos[2:]))[0]
     field = [fields[0]] + [fetched(late, shift) for shift in range(1, tiles)]
 
     listed = jnp.concatenate([params_in(shift) for shift in range(tiles)], axis=0)
@@ -709,24 +750,34 @@
     place = ("space", "sub")
     count = spaces * lax.axis_size("sub")
     shared = [sums] + [lax.ppermute(sums, place, [(i, (i + by) % count) for i in range(count)]) for by in range(1, count)]
-    pieces = pl.pallas_call(
+    coded_shape = jax.ShapeDtypeStruct((epochs * look_rows + HALO, LANES), jnp.int16)
+    coded = pl.pallas_call(
+        code_kernel,
+        out_shape=(coded_shape,) * (tiles - 1),
+        in_specs=[VMEM],
+        out_specs=(VMEM,) * (tiles - 1),
+        compiler_params=params_of,
+        cost_estimate=pl.CostEstimate(flops=1_000_000, bytes_accessed=1_000_000, transcendentals=0),
+    )(gradient)
+    piece_shape = jax.ShapeDtypeStruct((epochs * look_rows + HALO + 32, LANES), jnp.int16)
+    own_sums, *pieces = pl.pallas_call(
         functools.partial(return_kernel, tiles),
-        out_shape=(jax.ShapeDtypeStruct((epochs * look_rows + 8, LANES), f32),) * tiles,
-        in_specs=[VMEM] * (1 + count),
+        out_shape=(jax.ShapeDtypeStruct((8, LANES), f32),) + (piece_shape,) * (tiles - 1),
+        in_specs=[VMEM] * (tiles - 1 + count),
         out_specs=(VMEM,) * tiles,
         compiler_params=params_of,
         cost_estimate=pl.CostEstimate(flops=10_000, bytes_accessed=1_000_000, transcendentals=0),
-    )(gradient, *shared)
-    returned = [pieces[0]] + [to_ahead(pieces[by], "epoch", by) for by in range(1, tiles)]
+    )(*coded, *shared)
+    returned = [to_ahead(piece, "epoch", by + 1) for by, piece in enumerate(pieces)]
     cell_count = float(total * look_rows * spaces * columns * lax.axis_size("sub"))
     return pl.pallas_call(
         functools.partial(update_kernel, cell_count),
         out_shape=(jax.ShapeDtypeStruct(estimate.shape, f32),) * 2,
-        in_specs=[SMEM] * 2 + [VMEM] * (2 + tiles),
+        in_specs=[SMEM] * 2 + [VMEM] * (3 + tiles),
         out_specs=(VMEM, VMEM),
         compiler_params=params_of,
         cost_estimate=pl.CostEstimate(flops=1_000_000, bytes_accessed=2_000_000, transcendentals=0),
-    )(me.reshape(1), prev_mean, estimate, direction, *returned)
+    )(me.reshape(1), prev_mean, estimate, direction, gradient[:epochs], own_sums, *returned)
 
 
 def on_device(slc, offsets, weights, estimate, direction, prev_mean):

time: 65.9 us -> 64.4 us (0.977)
  waiting for transfers between devices: 23.9 us -> 21 us
  starting transfers between devices: 26.7 us -> 27.8 us
    ppermute x4, waiting for transfers between devices: 3.55 us -> 2.01 us  [halo(): lax.ppermute(border(jnp.where(space == 0, rows - HALO, 0)), 'space', [(0,...]
    ppermute x9, waiting for transfers between devices: 17.4 us -> 16.3 us  [to_ahead(): return lax.ppermute(x, axis, [(i, (i + by) % size) for i in range(size)])]
    ppermute x3, starting transfers between devices: 0.82 us -> 1.56 us  [transposed_plan(): lax.ppermute(sums, place, [(i, (i + by) % count) for i in range(count)])]
  transfers between devices with their start and end apart: 17 -> 17, of which waited for: 7 -> 7; matrix products, arithmetic and copies ran while one was open for 2% -> 2% of each run, Pallas kernels for 9% -> 10%
where the time goes in v19:
time: 64.4 us; the launch traced here: 64.2 us
  starting transfers between devices  27.8 us (43%)
  waiting for transfers between devices  21 us (33%)
  Pallas kernels  10.2 us (16%)
  local copies, waits for them, and re-layouts  3.32 us (5%)
  between operations  1.49 us (2%)
    ppermute x9, starting transfers between devices, to_ahead(): return lax.ppermute(x, axis, [(i, (i + by) % size) for i in range(size)])  20.3 us
    ppermute x9, waiting for transfers between devices, to_ahead(): return lax.ppermute(x, axis, [(i, (i + by) % size) for i in range(size)])  16.3 us
    pallas_call x1, Pallas kernels, transposed_plan(): pl.pallas_call(functools.partial(pair_kernel, (epochs, rows, len(operands...  6.05 us
    ppermute x4, starting transfers between devices, halo(): lax.ppermute(border(jnp.where(space == 0, rows - HALO, 0)), 'space', [(0,...  5.33 us
    unnamed x20, local copies, waits for them, and re-layouts  2.77 us
    ppermute x3, waiting for transfers between devices, transposed_plan(): lax.ppermute(sums, place, [(i, (i + by) % count) for i in range(count)])  2.74 us
    ppermute x4, waiting for transfers between devices, halo(): lax.ppermute(border(jnp.where(space == 0, rows - HALO, 0)), 'space', [(0,...  2.01 us
    ppermute x3, starting transfers between devices, transposed_plan(): lax.ppermute(sums, place, [(i, (i + by) % count) for i in range(count)])  1.56 us
  transfers between devices with their start and end apart: 17, of which 7 were waited for; matrix products, arithmetic and copies ran while one was open for 2% of the time, Pallas kernels for 10%

profile of v19, /device:TPU:0, one launch (start us, length us, event | category | flops | bytes accessed | tf_op | source)
XLA Modules:
  0.0 64.2 jit_solution(14407290445651515014)
XLA Ops:
  0.6 1.2 %copy-done = bf16[2,8,64,512]{3,2,1,0:T(8,128)(2,1)S(1)} copy-done((bf16[2,8,64,512]{3,2,1,0:T(8,128)(2,1)S(1)}, bf16[2,8,64,512]{3,2,1,0:T(8,128)(2,1)}, u32[]{:S(2)}) %copy-start) | copy-done | bytes 1048600
  1.9 0.2 shard_map.104
  2.1 0.5 collective-permute-start
  2.6 0.7 %copy-done.7 = s32[8,4]{0,1:T(4,128)S(1)} copy-done((s32[8,4]{0,1:T(4,128)S(1)}, s32[8,4]{0,1:T(4,128)}, u32[]{:S(2)}) %copy-start.7) | copy-done | bytes 152
  3.3 0.1 copy.15
  3.4 0.7 %copy-done.8 = f32[8,4]{0,1:T(4,128)S(1)} copy-done((f32[8,4]{0,1:T(4,128)S(1)}, f32[8,4]{0,1:T(4,128)}, u32[]{:S(2)}) %copy-start.8) | copy-done | bytes 152
  4.1 0.1 copy.16
  4.1 0.1 select_maximum_fusion.params
  4.2 0.1 add_convert_fusion.present
  4.3 0.0 copy-start.3
  4.3 1.3 %shard_map.105 = (bf16[1088,128]{1,0:T(8,128)(2,1)S(1)}, bf16[1088,128]{1,0:T(8,128)(2,1)S(1)}, bf16[1088,128]{1,0:T(8,128)(2,1)S(1)}, bf16[1088,128]{1,0:T(8,128)(2,1)S(1)}) custom-call(s32[1]{0:T(128)} %bitcast.me, f32[2]{0:T(128)S(1)} %add_convert_fusion.present, bf16[2,8,64,512]{3,2,1,0:T(8,128)(2,1)S(1)} %copy-done.1, ...), custom_call_target="tpu_custom_call" | custom-call | flops 3000000 | bytes 4000000 | tf_op jit(solution)/shard_map/pallas_call | solution.py:654
  5.6 2.7 %collective-permute-start.3 = (bf16[1088,128]{1,0:T(8,128)(2,1)S(1)}, bf16[1088,128]{1,0:T(8,128)(2,1)S(1)}, u32[]{:S(2)}, u32[]{:S(2)}) collective-permute-start(bf16[1088,128]{1,0:T(8,128)(2,1)S(1)} %get-tuple-element.27), channel_id=1, source_target_pairs={{0,4},{4,8},{8,12},{12,0},{1,5},{5,9},{9,13},{13,1},{2,6},{6,10},{... | collective-permute-start | bytes 835592 | tf_op jit(solution)/shard_map/ppermute | solution.py:618
  8.3 2.6 %collective-permute-start.2 = (bf16[1088,128]{1,0:T(8,128)(2,1)S(1)}, bf16[1088,128]{1,0:T(8,128)(2,1)S(1)}, u32[]{:S(2)}, u32[]{:S(2)}) collective-permute-start(bf16[1088,128]{1,0:T(8,128)(2,1)S(1)} %get-tuple-element.28), channel_id=1, source_target_pairs={{0,8},{4,12},{8,0},{12,4},{1,9},{5,13},{9,1},{13,5},{2,10},{6,14},... | collective-permute-start | bytes 835592 | tf_op jit(solution)/shard_map/ppermute | solution.py:618
  10.8 0.1 add_convert_fusion.1.present
  10.9 1.3 %collective-permute-start.1 = (bf16[1088,128]{1,0:T(8,128)(2,1)S(1)}, bf16[1088,128]{1,0:T(8,128)(2,1)S(1)}, u32[]{:S(2)}, u32[]{:S(2)}) collective-permute-start(bf16[1088,128]{1,0:T(8,128)(2,1)S(1)} %get-tuple-element.29), channel_id=1, source_target_pairs={{0,12},{4,0},{8,4},{12,8},{1,13},{5,1},{9,5},{13,9},{2,14},{6,2},{... | collective-permute-start | bytes 835592 | tf_op jit(solution)/shard_map/ppermute | solution.py:618
  12.3 0.1 slice.27
  12.4 1.5 %collective-permute-start.9 = (bf16[272,128]{1,0:T(8,128)(2,1)S(1)}, bf16[272,128]{1,0:T(8,128)(2,1)S(1)}, u32[]{:S(2)}, u32[]{:S(2)}) collective-permute-start(bf16[272,128]{1,0:T(8,128)(2,1)S(1)} %bitcast.17), channel_id=1, source_target_pairs={{0,2},{2,0},{1,3},{3,1},{4,6},{6,4},{5,7},{7,5},{8,10},{10,8},{9,1... | collective-permute-start | bytes 208904 | tf_op jit(solution)/shard_map/ppermute | solution.py:673
  13.9 0.1 shard_map.106
  14.0 4.0 %collective-permute-done.3.refs_3_ = bf16[1088,128]{1,0:T(8,128)(2,1)S(1)} collective-permute-done((bf16[1088,128]{1,0:T(8,128)(2,1)S(1)}, bf16[1088,128]{1,0:T(8,128)(2,1)S(1)}, u32[]{:S(2)}, u32[]{:S(2)}) %collective-permute-start.3) | collective-permute-done | bytes 278560 | tf_op jit(solution)/shard_map/ppermute | solution.py:618
  17.9 1.7 %collective-permute-start.5 = (bf16[272,128]{1,0:T(8,128)(2,1)S(1)}, bf16[272,128]{1,0:T(8,128)(2,1)S(1)}, u32[]{:S(2)}, u32[]{:S(2)}) collective-permute-start(bf16[272,128]{1,0:T(8,128)(2,1)S(1)} %bitcast.19), channel_id=1, source_target_pairs={{0,2},{2,0},{1,3},{3,1},{4,6},{6,4},{5,7},{7,5},{8,10},{10,8},{9,1... | collective-permute-start | bytes 208904 | tf_op jit(solution)/shard_map/ppermute | solution.py:673
  19.6 10.0 %collective-permute-done.2.refs_2_ = bf16[1088,128]{1,0:T(8,128)(2,1)S(1)} collective-permute-done((bf16[1088,128]{1,0:T(8,128)(2,1)S(1)}, bf16[1088,128]{1,0:T(8,128)(2,1)S(1)}, u32[]{:S(2)}, u32[]{:S(2)}) %collective-permute-start.2) | collective-permute-done | bytes 278560 | tf_op jit(solution)/shard_map/ppermute | solution.py:618
  29.6 1.6 %collective-permute-start.4 = (bf16[272,128]{1,0:T(8,128)(2,1)S(1)}, bf16[272,128]{1,0:T(8,128)(2,1)S(1)}, u32[]{:S(2)}, u32[]{:S(2)}) collective-permute-start(bf16[272,128]{1,0:T(8,128)(2,1)S(1)} %bitcast.20), channel_id=1, source_target_pairs={{0,2},{2,0},{1,3},{3,1},{4,6},{6,4},{5,7},{7,5},{8,10},{10,8},{9,1... | collective-permute-start | bytes 208904 | tf_op jit(solution)/shard_map/ppermute | solution.py:673
  31.2 0.1 slice.38
  31.3 0.1 slice.37
  31.4 0.1 slice.36
  31.4 0.1 slice_add_fusion
  31.5 0.0 copy-start.6
  31.6 0.0 copy-start.4
  31.6 0.6 collective-permute-start.10
  32.2 2.0 %collective-permute-done.4.refs_6_ = bf16[272,128]{1,0:T(8,128)(2,1)S(1)} collective-permute-done((bf16[272,128]{1,0:T(8,128)(2,1)S(1)}, bf16[272,128]{1,0:T(8,128)(2,1)S(1)}, u32[]{:S(2)}, u32[]{:S(2)}) %collective-permute-start.4) | collective-permute-done | bytes 69664 | tf_op jit(solution)/shard_map/ppermute | solution.py:673
  34.2 7.8 %collective-permute-start.6 = (s16[2,128,128]{2,1,0:T(8,128)(2,1)S(1)}, s16[2,128,128]{2,1,0:T(8,128)(2,1)S(1)}, u32[]{:S(2)}, u32[]{:S(2)}) collective-permute-start(s16[2,128,128]{2,1,0:T(8,128)(2,1)S(1)} %get-tuple-element.36), channel_id=1, source_target_pairs={{0,12},{4,0},{8,4},{12,8},{1,13},{5,1},{9,5},{13,9},{2,14},{6,2},{... | collective-permute-start | bytes 196616 | tf_op jit(solution)/shard_map/ppermute | solution.py:618
  42.0 0.6 collective-permute-start.8
  42.5 0.1 reshape.45.weight
  42.6 0.1 reshape.40.partner
  42.8 6.0 %shard_map.107 = (f32[128,16,128]{2,1,0:T(8,128)S(1)}, f32[128,16,128]{2,1,0:T(8,128)S(1)}) custom-call(s32[128]{0:T(128)S(1)} %reshape.40.partner, f32[128]{0:T(128)S(1)} %reshape.45.weight, f32[2]{0:T(128)S(1)} %add_convert_fusion.1.present, bf16[96,96]{1,0:T(8,128)(2,1)S(1)} %copy-done.6, bf16[256,128]{1,0:T(8,128)(2,1)S(1)} %copy-done.5, ...), custom_call_target="tpu_custom_call" | custom-call | flops 20000000 | bytes 30000000 | tf_op jit(solution)/shard_map/pallas_call | solution.py:720
  48.9 1.5 %shard_map.108 = (f32[32,16,128]{2,1,0:T(8,128)S(1)}, f32[8,128]{1,0:T(8,128)S(1)}) custom-call(s32[128]{0:T(128)S(1)} %reshape.40.partner, s16[2,128,128]{2,1,0:T(8,128)(2,1)S(1)} %get-tuple-element.32.refs_0_, s16[2,128,128]{2,1,0:T(8,128)(2,1)S(1)} %collective-permute-done.6.refs_1_, s16[2,128,128]{2,1,0:T(8,128)(2,1)S(1)} %collective-permute-done.7.refs_2_, ...), custom_call_target="tpu_custom_call" | custom-call | flops 10000000 | bytes 8000000 | tf_op jit(solution)/shard_map/pallas_call | solution.py:736
  50.4 0.1 collective-permute-start.13
  50.4 1.3 %collective-permute-start.12 = (f32[8,128]{1,0:T(8,128)S(1)}, f32[8,128]{1,0:T(8,128)S(1)}, u32[]{:S(2)}, u32[]{:S(2)}) collective-permute-start(f32[8,128]{1,0:T(8,128)S(1)} %get-tuple-element.45.refs_3_), channel_id=1, source_target_pairs={{0,2},{1,3},{2,0},{3,1},{4,6},{5,7},{6,4},{7,5},{8,10},{9,11},{10,... | collective-permute-start | bytes 12296 | tf_op jit(solution)/shard_map/ppermute | solution.py:752
  51.8 0.2 collective-permute-start.11
  51.9 0.1 shard_map.109
  52.1 2.0 %collective-permute-done.12.refs_5_ = f32[8,128]{1,0:T(8,128)S(1)} collective-permute-done((f32[8,128]{1,0:T(8,128)S(1)}, f32[8,128]{1,0:T(8,128)S(1)}, u32[]{:S(2)}, u32[]{:S(2)}) %collective-permute-start.12) | collective-permute-done | bytes 4128 | tf_op jit(solution)/shard_map/ppermute | solution.py:752
  54.1 0.7 %collective-permute-done.11.refs_4_ = f32[8,128]{1,0:T(8,128)S(1)} collective-permute-done((f32[8,128]{1,0:T(8,128)S(1)}, f32[8,128]{1,0:T(8,128)S(1)}, u32[]{:S(2)}, u32[]{:S(2)}) %collective-permute-start.11) | collective-permute-done | bytes 4128 | tf_op jit(solution)/shard_map/ppermute | solution.py:752
  54.8 3.0 %collective-permute-start.14 = (s16[176,128]{1,0:T(8,128)(2,1)S(1)}, s16[176,128]{1,0:T(8,128)(2,1)S(1)}, u32[]{:S(2)}, u32[]{:S(2)}) collective-permute-start(s16[176,128]{1,0:T(8,128)(2,1)S(1)} %get-tuple-element.47), channel_id=1, source_target_pairs={{0,4},{4,8},{8,12},{12,0},{1,5},{5,9},{9,13},{13,1},{2,6},{6,10},{... | collective-permute-start | bytes 135176 | tf_op jit(solution)/shard_map/ppermute | solution.py:618
  57.8 0.9 %collective-permute-start.15 = (s16[176,128]{1,0:T(8,128)(2,1)S(1)}, s16[176,128]{1,0:T(8,128)(2,1)S(1)}, u32[]{:S(2)}, u32[]{:S(2)}) collective-permute-start(s16[176,128]{1,0:T(8,128)(2,1)S(1)} %get-tuple-element.48), channel_id=1, source_target_pairs={{0,8},{4,12},{8,0},{12,4},{1,9},{5,13},{9,1},{13,5},{2,10},{6,14},... | collective-permute-start | bytes 135176 | tf_op jit(solution)/shard_map/ppermute | solution.py:618
  58.7 1.5 %collective-permute-start.16 = (s16[176,128]{1,0:T(8,128)(2,1)S(1)}, s16[176,128]{1,0:T(8,128)(2,1)S(1)}, u32[]{:S(2)}, u32[]{:S(2)}) collective-permute-start(s16[176,128]{1,0:T(8,128)(2,1)S(1)} %get-tuple-element.49), channel_id=1, source_target_pairs={{0,12},{4,0},{8,4},{12,8},{1,13},{5,1},{9,5},{13,9},{2,14},{6,2},{... | collective-permute-start | bytes 135176 | tf_op jit(solution)/shard_map/ppermute | solution.py:618
  60.9 1.9 %collective-permute-done.15.refs_1_ = s16[176,128]{1,0:T(8,128)(2,1)S(1)} collective-permute-done((s16[176,128]{1,0:T(8,128)(2,1)S(1)}, s16[176,128]{1,0:T(8,128)(2,1)S(1)}, u32[]{:S(2)}, u32[]{:S(2)}) %collective-permute-start.15) | collective-permute-done | bytes 45088 | tf_op jit(solution)/shard_map/ppermute | solution.py:618
  62.8 0.4 collective-permute-done.16.refs_2_
  63.2 0.9 %shard_map.111 = (f32[8,16,512]{2,1,0:T(8,128)}, f32[8,16,512]{2,1,0:T(8,128)}) custom-call(s32[1]{0:T(128)} %bitcast.me, f32[1]{0:T(128)S(6)} %copy.19.prev_mean, f32[8,16,512]{2,1,0:T(8,128)S(1)} %copy-done.2, f32[8,16,512]{2,1,0:T(8,128)S(1)} %copy-done.3, f32[8,16,128]{2,1,0:T(8,128)S(1)} %slice.35.gradient, f32[8,128]{1,0:T(8,128)S(1)} %get-tuple-element.46.sums, ...), custom_call_target="tpu_custom_call" | custom-call | flops 1000000 | bytes 2000000 | tf_op jit(solution)/shard_map/pallas_call | solution.py:773
  (32 shorter events, 0.2 us)
Async XLA Ops:
  0.6 1.2 %copy-start = (bf16[2,8,64,512]{3,2,1,0:T(8,128)(2,1)S(1)}, bf16[2,8,64,512]{3,2,1,0:T(8,128)(2,1)}, u32[]{:S(2)}) copy-start(bf16[2,8,64,512]{3,2,1,0:T(8,128)(2,1)} %slc.1) | copy-start | bytes 3145732
  1.9 2.4 %copy-start.1 = (bf16[2,8,64,512]{3,2,1,0:T(8,128)(2,1)S(1)}, bf16[2,8,64,512]{3,2,1,0:T(8,128)(2,1)}, u32[]{:S(2)}) copy-start(bf16[2,8,64,512]{3,2,1,0:T(8,128)(2,1)} %slc.1) | copy-start | bytes 3145732
  2.1 2.2 %collective-permute-start = (bf16[64,128]{1,0:T(8,128)(2,1)S(1)}, bf16[64,128]{1,0:T(8,128)(2,1)S(1)}, u32[]{:S(2)}, u32[]{:S(2)}) collective-permute-start(bf16[64,128]{1,0:T(8,128)(2,1)S(1)} %shard_map.104), channel_id=1, source_target_pairs={{0,1},{1,0},{2,3},{3,2},{4,5},{5,4},{6,7},{7,6},{8,9},{9,8},{10,11... | collective-permute-start | bytes 49160 | tf_op jit(solution)/shard_map/ppermute | solution.py:609
  2.6 0.7 %copy-start.7 = (s32[8,4]{0,1:T(4,128)S(1)}, s32[8,4]{0,1:T(4,128)}, u32[]{:S(2)}) copy-start(s32[8,4]{0,1:T(4,128)} %param.10) | copy-start | bytes 388
  3.4 0.7 %copy-start.8 = (f32[8,4]{0,1:T(4,128)S(1)}, f32[8,4]{0,1:T(4,128)}, u32[]{:S(2)}) copy-start(f32[8,4]{0,1:T(4,128)} %param.11) | copy-start | bytes 388
  4.3 9.6 %copy-start.2 = (f32[8,16,512]{2,1,0:T(8,128)S(1)}, f32[8,16,512]{2,1,0:T(8,128)}, u32[]{:S(2)}) copy-start(f32[8,16,512]{2,1,0:T(8,128)} %estimate.1) | copy-start | bytes 786436
  4.3 9.5 %copy-start.3 = (f32[8,16,512]{2,1,0:T(8,128)S(1)}, f32[8,16,512]{2,1,0:T(8,128)}, u32[]{:S(2)}) copy-start(f32[8,16,512]{2,1,0:T(8,128)} %direction.1) | copy-start | bytes 786436
  5.6 12.3 %collective-permute-start.3 = (bf16[1088,128]{1,0:T(8,128)(2,1)S(1)}, bf16[1088,128]{1,0:T(8,128)(2,1)S(1)}, u32[]{:S(2)}, u32[]{:S(2)}) collective-permute-start(bf16[1088,128]{1,0:T(8,128)(2,1)S(1)} %get-tuple-element.27), channel_id=1, source_target_pairs={{0,4},{4,8},{8,12},{12,0},{1,5},{5,9},{9,13},{13,1},{2,6},{6,10},{... | collective-permute-start | bytes 835592 | tf_op jit(solution)/shard_map/ppermute | solution.py:618
  8.3 21.4 %collective-permute-start.2 = (bf16[1088,128]{1,0:T(8,128)(2,1)S(1)}, bf16[1088,128]{1,0:T(8,128)(2,1)S(1)}, u32[]{:S(2)}, u32[]{:S(2)}) collective-permute-start(bf16[1088,128]{1,0:T(8,128)(2,1)S(1)} %get-tuple-element.28), channel_id=1, source_target_pairs={{0,8},{4,12},{8,0},{12,4},{1,9},{5,13},{9,1},{13,5},{2,10},{6,14},... | collective-permute-start | bytes 835592 | tf_op jit(solution)/shard_map/ppermute | solution.py:618
  10.9 20.4 %collective-permute-start.1 = (bf16[1088,128]{1,0:T(8,128)(2,1)S(1)}, bf16[1088,128]{1,0:T(8,128)(2,1)S(1)}, u32[]{:S(2)}, u32[]{:S(2)}) collective-permute-start(bf16[1088,128]{1,0:T(8,128)(2,1)S(1)} %get-tuple-element.29), channel_id=1, source_target_pairs={{0,12},{4,0},{8,4},{12,8},{1,13},{5,1},{9,5},{13,9},{2,14},{6,2},{... | collective-permute-start | bytes 835592 | tf_op jit(solution)/shard_map/ppermute | solution.py:618
  12.4 30.4 %collective-permute-start.9 = (bf16[272,128]{1,0:T(8,128)(2,1)S(1)}, bf16[272,128]{1,0:T(8,128)(2,1)S(1)}, u32[]{:S(2)}, u32[]{:S(2)}) collective-permute-start(bf16[272,128]{1,0:T(8,128)(2,1)S(1)} %bitcast.17), channel_id=1, source_target_pairs={{0,2},{2,0},{1,3},{3,1},{4,6},{6,4},{5,7},{7,5},{8,10},{10,8},{9,1... | collective-permute-start | bytes 208904 | tf_op jit(solution)/shard_map/ppermute | solution.py:673
  17.9 14.2 %collective-permute-start.5 = (bf16[272,128]{1,0:T(8,128)(2,1)S(1)}, bf16[272,128]{1,0:T(8,128)(2,1)S(1)}, u32[]{:S(2)}, u32[]{:S(2)}) collective-permute-start(bf16[272,128]{1,0:T(8,128)(2,1)S(1)} %bitcast.19), channel_id=1, source_target_pairs={{0,2},{2,0},{1,3},{3,1},{4,6},{6,4},{5,7},{7,5},{8,10},{10,8},{9,1... | collective-permute-start | bytes 208904 | tf_op jit(solution)/shard_map/ppermute | solution.py:673
  29.6 4.5 %collective-permute-start.4 = (bf16[272,128]{1,0:T(8,128)(2,1)S(1)}, bf16[272,128]{1,0:T(8,128)(2,1)S(1)}, u32[]{:S(2)}, u32[]{:S(2)}) collective-permute-start(bf16[272,128]{1,0:T(8,128)(2,1)S(1)} %bitcast.20), channel_id=1, source_target_pairs={{0,2},{2,0},{1,3},{3,1},{4,6},{6,4},{5,7},{7,5},{8,10},{10,8},{9,1... | collective-permute-start | bytes 208904 | tf_op jit(solution)/shard_map/ppermute | solution.py:673
  31.5 11.3 %copy-start.5 = (bf16[256,128]{1,0:T(8,128)(2,1)S(1)}, bf16[256,128]{1,0:T(8,128)(2,1)}, u32[]{:S(2)}) copy-start(bf16[256,128]{1,0:T(8,128)(2,1)} %constant.33.clone.band) | copy-start | bytes 196612
  31.5 11.3 %copy-start.6 = (bf16[96,96]{1,0:T(8,128)(2,1)S(1)}, bf16[96,96]{1,0:T(8,128)(2,1)}, u32[]{:S(2)}) copy-start(bf16[96,96]{1,0:T(8,128)(2,1)} %constant.32.clone.order) | copy-start | bytes 55300
  31.6 11.2 %copy-start.4 = (bf16[256,128]{1,0:T(8,128)(2,1)S(1)}, bf16[256,128]{1,0:T(8,128)(2,1)}, u32[]{:S(2)}) copy-start(bf16[256,128]{1,0:T(8,128)(2,1)} %constant.34.clone.rim_band) | copy-start | bytes 196612
  31.6 11.2 %collective-permute-start.10 = (bf16[272,128]{1,0:T(8,128)(2,1)S(1)}, bf16[272,128]{1,0:T(8,128)(2,1)S(1)}, u32[]{:S(2)}, u32[]{:S(2)}) collective-permute-start(bf16[272,128]{1,0:T(8,128)(2,1)S(1)} %bitcast.18), channel_id=1, source_target_pairs={{0,2},{2,0},{1,3},{3,1},{4,6},{6,4},{5,7},{7,5},{8,10},{10,8},{9,1... | collective-permute-start | bytes 208904 | tf_op jit(solution)/shard_map/ppermute | solution.py:673
  34.2 14.7 %collective-permute-start.6 = (s16[2,128,128]{2,1,0:T(8,128)(2,1)S(1)}, s16[2,128,128]{2,1,0:T(8,128)(2,1)S(1)}, u32[]{:S(2)}, u32[]{:S(2)}) collective-permute-start(s16[2,128,128]{2,1,0:T(8,128)(2,1)S(1)} %get-tuple-element.36), channel_id=1, source_target_pairs={{0,12},{4,0},{8,4},{12,8},{1,13},{5,1},{9,5},{13,9},{2,14},{6,2},{... | collective-permute-start | bytes 196616 | tf_op jit(solution)/shard_map/ppermute | solution.py:618
  42.0 6.9 %collective-permute-start.7 = (s16[2,128,128]{2,1,0:T(8,128)(2,1)S(1)}, s16[2,128,128]{2,1,0:T(8,128)(2,1)S(1)}, u32[]{:S(2)}, u32[]{:S(2)}) collective-permute-start(s16[2,128,128]{2,1,0:T(8,128)(2,1)S(1)} %get-tuple-element.37), channel_id=1, source_target_pairs={{0,8},{4,12},{8,0},{12,4},{1,9},{5,13},{9,1},{13,5},{2,10},{6,14},... | collective-permute-start | bytes 196616 | tf_op jit(solution)/shard_map/ppermute | solution.py:618
  42.0 6.9 %collective-permute-start.8 = (s16[2,128,128]{2,1,0:T(8,128)(2,1)S(1)}, s16[2,128,128]{2,1,0:T(8,128)(2,1)S(1)}, u32[]{:S(2)}, u32[]{:S(2)}) collective-permute-start(s16[2,128,128]{2,1,0:T(8,128)(2,1)S(1)} %get-tuple-element.38), channel_id=1, source_target_pairs={{0,4},{4,8},{8,12},{12,0},{1,5},{5,9},{9,13},{13,1},{2,6},{6,10},{... | collective-permute-start | bytes 196616 | tf_op jit(solution)/shard_map/ppermute | solution.py:618
  50.4 1.7 %collective-permute-start.13 = (f32[8,128]{1,0:T(8,128)S(1)}, f32[8,128]{1,0:T(8,128)S(1)}, u32[]{:S(2)}, u32[]{:S(2)}) collective-permute-start(f32[8,128]{1,0:T(8,128)S(1)} %get-tuple-element.45.refs_3_), channel_id=1, source_target_pairs={{0,3},{1,0},{2,1},{3,2},{4,7},{5,4},{6,5},{7,6},{8,11},{9,8},{10,9... | collective-permute-start | bytes 12296 | tf_op jit(solution)/shard_map/ppermute | solution.py:752
  50.4 3.7 %collective-permute-start.12 = (f32[8,128]{1,0:T(8,128)S(1)}, f32[8,128]{1,0:T(8,128)S(1)}, u32[]{:S(2)}, u32[]{:S(2)}) collective-permute-start(f32[8,128]{1,0:T(8,128)S(1)} %get-tuple-element.45.refs_3_), channel_id=1, source_target_pairs={{0,2},{1,3},{2,0},{3,1},{4,6},{5,7},{6,4},{7,5},{8,10},{9,11},{10,... | collective-permute-start | bytes 12296 | tf_op jit(solution)/shard_map/ppermute | solution.py:752
  51.8 3.0 %collective-permute-start.11 = (f32[8,128]{1,0:T(8,128)S(1)}, f32[8,128]{1,0:T(8,128)S(1)}, u32[]{:S(2)}, u32[]{:S(2)}) collective-permute-start(f32[8,128]{1,0:T(8,128)S(1)} %get-tuple-element.45.refs_3_), channel_id=1, source_target_pairs={{0,1},{1,2},{2,3},{3,0},{4,5},{5,6},{6,7},{7,4},{8,9},{9,10},{10,1... | collective-permute-start | bytes 12296 | tf_op jit(solution)/shard_map/ppermute | solution.py:752
  54.8 6.1 %collective-permute-start.14 = (s16[176,128]{1,0:T(8,128)(2,1)S(1)}, s16[176,128]{1,0:T(8,128)(2,1)S(1)}, u32[]{:S(2)}, u32[]{:S(2)}) collective-permute-start(s16[176,128]{1,0:T(8,128)(2,1)S(1)} %get-tuple-element.47), channel_id=1, source_target_pairs={{0,4},{4,8},{8,12},{12,0},{1,5},{5,9},{9,13},{13,1},{2,6},{6,10},{... | collective-permute-start | bytes 135176 | tf_op jit(solution)/shard_map/ppermute | solution.py:618
  57.8 5.0 %collective-permute-start.15 = (s16[176,128]{1,0:T(8,128)(2,1)S(1)}, s16[176,128]{1,0:T(8,128)(2,1)S(1)}, u32[]{:S(2)}, u32[]{:S(2)}) collective-permute-start(s16[176,128]{1,0:T(8,128)(2,1)S(1)} %get-tuple-element.48), channel_id=1, source_target_pairs={{0,8},{4,12},{8,0},{12,4},{1,9},{5,13},{9,1},{13,5},{2,10},{6,14},... | collective-permute-start | bytes 135176 | tf_op jit(solution)/shard_map/ppermute | solution.py:618
  58.7 4.5 %collective-permute-start.16 = (s16[176,128]{1,0:T(8,128)(2,1)S(1)}, s16[176,128]{1,0:T(8,128)(2,1)S(1)}, u32[]{:S(2)}, u32[]{:S(2)}) collective-permute-start(s16[176,128]{1,0:T(8,128)(2,1)S(1)} %get-tuple-element.49), channel_id=1, source_target_pairs={{0,12},{4,0},{8,4},{12,8},{1,13},{5,1},{9,5},{13,9},{2,14},{6,2},{... | collective-permute-start | bytes 135176 | tf_op jit(solution)/shard_map/ppermute | solution.py:618

commit v20 on v19

--- a/solution.py
+++ b/solution.py
@@ -174,7 +174,7 @@
     look_rows = estimate.shape[1]
     tiles = len(fields)
     for shift, out in enumerate(fields):
-        tile = lax.rem(me[0] + shift, tiles)
+        tile = lax.bitwise_xor(me[0], shift)
         columns = pl.ds(pl.multiple_of(tile * LANES, LANES), LANES)
         for epoch in range(estimate.shape[0]):
             here = slice(epoch * look_rows, (epoch + 1) * look_rows)
@@ -222,7 +222,7 @@
                     total = placed(lane, total, tile_of(slc, part, epoch, tile + 1), 0, at + RADIUS)
         strips[tile] = total.astype(jnp.bfloat16)
     for tile in range(tiles):
-        shift = lax.rem(tile - me[0] + tiles, tiles)
+        shift = lax.bitwise_xor(me[0], tile)
         for number, message in enumerate(messages):
 
             @pl.when(shift == number)
@@ -585,7 +585,7 @@
     momentum = jnp.broadcast_to(momentum, (look_rows, LANES))
     step = jnp.broadcast_to(step, (look_rows, LANES))
     for shift in range(tiles):
-        tile = lax.rem(me[0] - shift + tiles, tiles)
+        tile = lax.bitwise_xor(me[0], shift)
         columns = pl.ds(pl.multiple_of(tile * LANES, LANES), LANES)
         if shift > 0:
             piece = pieces[shift - 1]
@@ -613,9 +613,9 @@
     return lax.ppermute(up, axis, forward), lax.ppermute(down, axis, backward)
 
 
-def to_ahead(x, axis, by):
+def exchanged(x, axis, by):
     size = lax.axis_size(axis)
-    return lax.ppermute(x, axis, [(i, (i + by) % size) for i in range(size)])
+    return lax.ppermute(x, axis, [(i, i ^ by) for i in range(size)])
 
 
 def transposed_plan(slc, offsets, weights, estimate, direction, prev_mean):
@@ -628,9 +628,6 @@
     total = tiles * epochs
     tile_rows = 2 * epochs * rows
     params_of = pltpu.CompilerParams(vmem_limit_bytes=VMEM_BYTES)
-
-    def fetched(messages, shift):
-        return to_ahead(messages[tiles - shift], "epoch", tiles - shift)
 
     sub = lax.axis_index("sub")
     outer_tile = (2, epochs, rows, LANES)
@@ -674,7 +671,7 @@
             return got, got
         return swapped(border(rows - HALO), border(0), "space")
 
-    block = [messages[0]] + [fetched(messages, shift) for shift in range(1, tiles)]
+    block = [messages[0]] + [exchanged(messages[by], "epoch", by) for by in range(1, tiles)]
     estimate, direction, _ = lax.optimization_barrier((estimate, direction, messages))
     fields = pl.pallas_call(
         fields_kernel,
@@ -687,19 +684,15 @@
     def params_in(shift):
         return block[shift][tile_rows : tile_rows + epochs, PARAM_LANE : PARAM_LANE + 4 * SLOTS].astype(f32)
 
-    def pairs_of(blocks, loaded):
-        listed = jnp.concatenate([params_in(block) for block in blocks], axis=0)
-        mate = jnp.arange(len(blocks) * epochs, dtype=jnp.int32)[:, None] + listed[:, :SLOTS].astype(jnp.int32)
-        weight = listed[:, SLOTS : 2 * SLOTS] + listed[:, 2 * SLOTS : 3 * SLOTS] + listed[:, 3 * SLOTS :]
-        return mate.reshape(-1), weight.reshape(-1)
-
     halos = [halo([array.reshape(-1, rows, LANES)]) for array in block]
-    late = lax.optimization_barrier((fields, block, halos[2:]))[0]
-    field = [fields[0]] + [fetched(late, shift) for shift in range(1, tiles)]
+    late = lax.optimization_barrier((fields, block, halos[1:-1]))[0]
+    field = [fields[0]] + [exchanged(late[by], "epoch", by) for by in range(1, tiles)]
 
     listed = jnp.concatenate([params_in(shift) for shift in range(tiles)], axis=0)
-    partner = jnp.arange(total, dtype=jnp.int32)[:, None] + listed[:, :SLOTS].astype(jnp.int32)
-    partner = lax.rem(partner, total).reshape(-1)
+    place = jnp.arange(total, dtype=jnp.int32)[:, None]
+    first = lax.bitwise_xor(place // epochs, me) * epochs + place % epochs
+    mate = lax.rem(first + listed[:, :SLOTS].astype(jnp.int32), total)
+    partner = (lax.bitwise_xor(mate // epochs, me) * epochs + mate % epochs).reshape(-1)
     weight = listed[:, SLOTS : 2 * SLOTS] + listed[:, 2 * SLOTS : 3 * SLOTS] + listed[:, 3 * SLOTS :]
     order = look_order(rows + 2 * HALO, HALO // LOOK - RADIUS)
     bands = column_bands()
@@ -768,7 +761,7 @@
         compiler_params=params_of,
         cost_estimate=pl.CostEstimate(flops=10_000, bytes_accessed=1_000_000, transcendentals=0),
     )(*coded, *shared)
-    returned = [to_ahead(piece, "epoch", by + 1) for by, piece in enumerate(pieces)]
+    returned = [exchanged(piece, "epoch", by + 1) for by, piece in enumerate(pieces)]
     cell_count = float(total * look_rows * spaces * columns * lax.axis_size("sub"))
     return pl.pallas_call(
         functools.partial(update_kernel, cell_count),
@@ -782,8 +775,9 @@
 
 def on_device(slc, offsets, weights, estimate, direction, prev_mean):
     epochs, rows, columns = slc.shape[1:]
-    fits = columns == LANES * lax.axis_size("epoch") and lax.axis_size("epoch") % 2 == 0
-    fits = fits and 2 * epochs * SIDES <= PARAM_LANE and rows % HALO == 0 and epochs == 2 * SLOTS
+    fits = columns == LANES * lax.axis_size("epoch") and lax.axis_size("epoch") > 1
+    size = lax.axis_size("epoch")
+    fits = fits and size & (size - 1) == 0 and 2 * epochs * SIDES <= PARAM_LANE and rows % HALO == 0 and epochs == 2 * SLOTS
     plan = transposed_plan if fits else ring_plan
     return plan(slc, offsets, weights, estimate, direction, prev_mean)
 

time: 64.4 us -> 62.7 us (0.974)
  starting transfers between devices: 27.8 us -> 22.5 us
  waiting for transfers between devices: 21 us -> 24.5 us
    ppermute x9, starting transfers between devices: 20.3 us -> 15.6 us  [exchanged(): return lax.ppermute(x, axis, [(i, i ^ by) for i in range(size)])]
    ppermute x9, waiting for transfers between devices: 16.3 us -> 19.8 us  [exchanged(): return lax.ppermute(x, axis, [(i, i ^ by) for i in range(size)])]
    ppermute x3, starting transfers between devices: 1.56 us -> 0.83 us  [transposed_plan(): lax.ppermute(sums, place, [(i, (i + by) % count) for i in range(count)])]
where the time goes in v20:
time: 62.7 us; the launch traced here: 62.5 us
  waiting for transfers between devices  24.5 us (39%)
  starting transfers between devices  22.5 us (36%)
  Pallas kernels  10.2 us (16%)
  local copies, waits for them, and re-layouts  3.32 us (5%)
  between operations  1.49 us (2%)
    ppermute x9, waiting for transfers between devices, exchanged(): return lax.ppermute(x, axis, [(i, i ^ by) for i in range(size)])  19.8 us
    ppermute x9, starting transfers between devices, exchanged(): return lax.ppermute(x, axis, [(i, i ^ by) for i in range(size)])  15.6 us
    pallas_call x1, Pallas kernels, transposed_plan(): pl.pallas_call(functools.partial(pair_kernel, (epochs, rows, len(operands...  6.05 us
    ppermute x4, starting transfers between devices, halo(): lax.ppermute(border(jnp.where(space == 0, rows - HALO, 0)), 'space', [(0,...  5.55 us
    ppermute x3, waiting for transfers between devices, transposed_plan(): lax.ppermute(sums, place, [(i, (i + by) % count) for i in range(count)])  2.8 us
    unnamed x20, local copies, waits for them, and re-layouts  2.76 us
    ppermute x4, waiting for transfers between devices, halo(): lax.ppermute(border(jnp.where(space == 0, rows - HALO, 0)), 'space', [(0,...  1.85 us
    pallas_call x1, Pallas kernels, transposed_plan(): pl.pallas_call(functools.partial(gradient_kernel, (tiles, epochs)), out_s...  1.47 us
  transfers between devices with their start and end apart: 17, of which 7 were waited for; matrix products, arithmetic and copies ran while one was open for 2% of the time, Pallas kernels for 10%

profile of v20, /device:TPU:0, one launch (start us, length us, event | category | flops | bytes accessed | tf_op | source)
XLA Modules:
  0.0 62.5 jit_solution(4117511448051997209)
XLA Ops:
  0.6 1.2 %copy-done = bf16[2,8,64,512]{3,2,1,0:T(8,128)(2,1)S(1)} copy-done((bf16[2,8,64,512]{3,2,1,0:T(8,128)(2,1)S(1)}, bf16[2,8,64,512]{3,2,1,0:T(8,128)(2,1)}, u32[]{:S(2)}) %copy-start) | copy-done | bytes 1048600
  1.9 0.2 shard_map.104
  2.1 0.5 collective-permute-start
  2.6 0.7 %copy-done.7 = s32[8,4]{0,1:T(4,128)S(1)} copy-done((s32[8,4]{0,1:T(4,128)S(1)}, s32[8,4]{0,1:T(4,128)}, u32[]{:S(2)}) %copy-start.7) | copy-done | bytes 152
  3.3 0.1 copy.15
  3.4 0.7 %copy-done.8 = f32[8,4]{0,1:T(4,128)S(1)} copy-done((f32[8,4]{0,1:T(4,128)S(1)}, f32[8,4]{0,1:T(4,128)}, u32[]{:S(2)}) %copy-start.8) | copy-done | bytes 152
  4.1 0.1 copy.16
  4.1 0.1 select_maximum_fusion.params
  4.2 0.1 add_convert_fusion.present
  4.3 1.3 %shard_map.105 = (bf16[1088,128]{1,0:T(8,128)(2,1)S(1)}, bf16[1088,128]{1,0:T(8,128)(2,1)S(1)}, bf16[1088,128]{1,0:T(8,128)(2,1)S(1)}, bf16[1088,128]{1,0:T(8,128)(2,1)S(1)}) custom-call(s32[1]{0:T(128)} %bitcast.me, f32[2]{0:T(128)S(1)} %add_convert_fusion.present, bf16[2,8,64,512]{3,2,1,0:T(8,128)(2,1)S(1)} %copy-done.1, ...), custom_call_target="tpu_custom_call" | custom-call | flops 3000000 | bytes 4000000 | tf_op jit(solution)/shard_map/pallas_call | solution.py:651
  5.6 2.7 %collective-permute-start.1 = (bf16[1088,128]{1,0:T(8,128)(2,1)S(1)}, bf16[1088,128]{1,0:T(8,128)(2,1)S(1)}, u32[]{:S(2)}, u32[]{:S(2)}) collective-permute-start(bf16[1088,128]{1,0:T(8,128)(2,1)S(1)} %get-tuple-element.27), channel_id=1, source_target_pairs={{0,4},{4,0},{8,12},{12,8},{1,5},{5,1},{9,13},{13,9},{2,6},{6,2},{1... | collective-permute-start | bytes 835592 | tf_op jit(solution)/shard_map/ppermute | solution.py:618
  8.3 2.6 %collective-permute-start.2 = (bf16[1088,128]{1,0:T(8,128)(2,1)S(1)}, bf16[1088,128]{1,0:T(8,128)(2,1)S(1)}, u32[]{:S(2)}, u32[]{:S(2)}) collective-permute-start(bf16[1088,128]{1,0:T(8,128)(2,1)S(1)} %get-tuple-element.28), channel_id=1, source_target_pairs={{0,8},{4,12},{8,0},{12,4},{1,9},{5,13},{9,1},{13,5},{2,10},{6,14},... | collective-permute-start | bytes 835592 | tf_op jit(solution)/shard_map/ppermute | solution.py:618
  10.9 0.1 add_convert_fusion.1.present
  10.9 0.0 collective-permute-start.3
  11.0 0.1 slice.27
  11.0 1.7 %collective-permute-start.9 = (bf16[272,128]{1,0:T(8,128)(2,1)S(1)}, bf16[272,128]{1,0:T(8,128)(2,1)S(1)}, u32[]{:S(2)}, u32[]{:S(2)}) collective-permute-start(bf16[272,128]{1,0:T(8,128)(2,1)S(1)} %bitcast.17), channel_id=1, source_target_pairs={{0,2},{2,0},{1,3},{3,1},{4,6},{6,4},{5,7},{7,5},{8,10},{10,8},{9,1... | collective-permute-start | bytes 208904 | tf_op jit(solution)/shard_map/ppermute | solution.py:670
  12.7 0.1 shard_map.106
  12.9 8.3 %collective-permute-done.1.refs_1_ = bf16[1088,128]{1,0:T(8,128)(2,1)S(1)} collective-permute-done((bf16[1088,128]{1,0:T(8,128)(2,1)S(1)}, bf16[1088,128]{1,0:T(8,128)(2,1)S(1)}, u32[]{:S(2)}, u32[]{:S(2)}) %collective-permute-start.1) | collective-permute-done | bytes 278560 | tf_op jit(solution)/shard_map/ppermute | solution.py:618
  21.1 1.7 %collective-permute-start.4 = (bf16[272,128]{1,0:T(8,128)(2,1)S(1)}, bf16[272,128]{1,0:T(8,128)(2,1)S(1)}, u32[]{:S(2)}, u32[]{:S(2)}) collective-permute-start(bf16[272,128]{1,0:T(8,128)(2,1)S(1)} %bitcast.19), channel_id=1, source_target_pairs={{0,2},{2,0},{1,3},{3,1},{4,6},{6,4},{5,7},{7,5},{8,10},{10,8},{9,1... | collective-permute-start | bytes 208904 | tf_op jit(solution)/shard_map/ppermute | solution.py:670
  22.8 7.8 %collective-permute-done.2.refs_2_ = bf16[1088,128]{1,0:T(8,128)(2,1)S(1)} collective-permute-done((bf16[1088,128]{1,0:T(8,128)(2,1)S(1)}, bf16[1088,128]{1,0:T(8,128)(2,1)S(1)}, u32[]{:S(2)}, u32[]{:S(2)}) %collective-permute-start.2) | collective-permute-done | bytes 278560 | tf_op jit(solution)/shard_map/ppermute | solution.py:618
  30.6 1.6 %collective-permute-start.5 = (bf16[272,128]{1,0:T(8,128)(2,1)S(1)}, bf16[272,128]{1,0:T(8,128)(2,1)S(1)}, u32[]{:S(2)}, u32[]{:S(2)}) collective-permute-start(bf16[272,128]{1,0:T(8,128)(2,1)S(1)} %bitcast.20), channel_id=1, source_target_pairs={{0,2},{2,0},{1,3},{3,1},{4,6},{6,4},{5,7},{7,5},{8,10},{10,8},{9,1... | collective-permute-start | bytes 208904 | tf_op jit(solution)/shard_map/ppermute | solution.py:670
  32.2 0.6 collective-permute-start.10
  32.8 0.1 slice.36
  32.9 0.1 slice.37
  33.0 0.1 slice.38
  33.1 0.0 copy-start.5
  33.1 0.1 fusion.5
  33.2 1.8 %collective-permute-done.5.refs_6_ = bf16[272,128]{1,0:T(8,128)(2,1)S(1)} collective-permute-done((bf16[272,128]{1,0:T(8,128)(2,1)S(1)}, bf16[272,128]{1,0:T(8,128)(2,1)S(1)}, u32[]{:S(2)}, u32[]{:S(2)}) %collective-permute-start.5) | collective-permute-done | bytes 69664 | tf_op jit(solution)/shard_map/ppermute | solution.py:670
  35.0 3.4 %collective-permute-start.6 = (s16[2,128,128]{2,1,0:T(8,128)(2,1)S(1)}, s16[2,128,128]{2,1,0:T(8,128)(2,1)S(1)}, u32[]{:S(2)}, u32[]{:S(2)}) collective-permute-start(s16[2,128,128]{2,1,0:T(8,128)(2,1)S(1)} %get-tuple-element.36), channel_id=1, source_target_pairs={{0,4},{4,0},{8,12},{12,8},{1,5},{5,1},{9,13},{13,9},{2,6},{6,2},{1... | collective-permute-start | bytes 196616 | tf_op jit(solution)/shard_map/ppermute | solution.py:618
  38.5 1.1 %collective-permute-start.7 = (s16[2,128,128]{2,1,0:T(8,128)(2,1)S(1)}, s16[2,128,128]{2,1,0:T(8,128)(2,1)S(1)}, u32[]{:S(2)}, u32[]{:S(2)}) collective-permute-start(s16[2,128,128]{2,1,0:T(8,128)(2,1)S(1)} %get-tuple-element.37), channel_id=1, source_target_pairs={{0,8},{4,12},{8,0},{12,4},{1,9},{5,13},{9,1},{13,5},{2,10},{6,14},... | collective-permute-start | bytes 196616 | tf_op jit(solution)/shard_map/ppermute | solution.py:618
  39.5 1.4 %collective-permute-start.8 = (s16[2,128,128]{2,1,0:T(8,128)(2,1)S(1)}, s16[2,128,128]{2,1,0:T(8,128)(2,1)S(1)}, u32[]{:S(2)}, u32[]{:S(2)}) collective-permute-start(s16[2,128,128]{2,1,0:T(8,128)(2,1)S(1)} %get-tuple-element.38), channel_id=1, source_target_pairs={{0,12},{4,8},{8,4},{12,0},{1,13},{5,9},{9,5},{13,1},{2,14},{6,10},... | collective-permute-start | bytes 196616 | tf_op jit(solution)/shard_map/ppermute | solution.py:618
  40.9 0.1 slice_add_fusion
  41.0 0.1 reshape.97.partner
  41.1 0.1 reshape.102.weight
  41.3 6.1 %shard_map.107 = (f32[128,16,128]{2,1,0:T(8,128)S(1)}, f32[128,16,128]{2,1,0:T(8,128)S(1)}) custom-call(s32[128]{0:T(128)S(1)} %reshape.97.partner, f32[128]{0:T(128)S(1)} %reshape.102.weight, f32[2]{0:T(128)S(1)} %add_convert_fusion.1.present, bf16[96,96]{1,0:T(8,128)(2,1)S(1)} %copy-done.6, bf16[256,128]{1,0:T(8,128)(2,1)S(1)} %copy-done.5, ...), custom_call_target="tpu_custom_call" | custom-call | flops 20000000 | bytes 30000000 | tf_op jit(solution)/shard_map/pallas_call | solution.py:713
  47.4 1.5 %shard_map.108 = (f32[32,16,128]{2,1,0:T(8,128)S(1)}, f32[8,128]{1,0:T(8,128)S(1)}) custom-call(s32[128]{0:T(128)S(1)} %reshape.97.partner, s16[2,128,128]{2,1,0:T(8,128)(2,1)S(1)} %get-tuple-element.32.refs_0_, s16[2,128,128]{2,1,0:T(8,128)(2,1)S(1)} %collective-permute-done.6.refs_1_, s16[2,128,128]{2,1,0:T(8,128)(2,1)S(1)} %collective-permute-done.7.refs_2_, ...), custom_call_target="tpu_custom_call" | custom-call | flops 10000000 | bytes 8000000 | tf_op jit(solution)/shard_map/pallas_call | solution.py:729
  48.8 0.1 collective-permute-start.13
  48.9 0.6 collective-permute-start.12
  49.5 0.2 collective-permute-start.11
  49.7 0.1 shard_map.109
  49.8 0.4 collective-permute-done.13.refs_6_
  50.2 2.4 %collective-permute-done.12.refs_5_ = f32[8,128]{1,0:T(8,128)S(1)} collective-permute-done((f32[8,128]{1,0:T(8,128)S(1)}, f32[8,128]{1,0:T(8,128)S(1)}, u32[]{:S(2)}, u32[]{:S(2)}) %collective-permute-start.12) | collective-permute-done | bytes 4128 | tf_op jit(solution)/shard_map/ppermute | solution.py:745
  52.6 1.1 %collective-permute-start.14 = (s16[176,128]{1,0:T(8,128)(2,1)S(1)}, s16[176,128]{1,0:T(8,128)(2,1)S(1)}, u32[]{:S(2)}, u32[]{:S(2)}) collective-permute-start(s16[176,128]{1,0:T(8,128)(2,1)S(1)} %get-tuple-element.47), channel_id=1, source_target_pairs={{0,4},{4,0},{8,12},{12,8},{1,5},{5,1},{9,13},{13,9},{2,6},{6,2},{1... | collective-permute-start | bytes 135176 | tf_op jit(solution)/shard_map/ppermute | solution.py:618
  53.7 2.0 %collective-permute-start.15 = (s16[176,128]{1,0:T(8,128)(2,1)S(1)}, s16[176,128]{1,0:T(8,128)(2,1)S(1)}, u32[]{:S(2)}, u32[]{:S(2)}) collective-permute-start(s16[176,128]{1,0:T(8,128)(2,1)S(1)} %get-tuple-element.48), channel_id=1, source_target_pairs={{0,8},{4,12},{8,0},{12,4},{1,9},{5,13},{9,1},{13,5},{2,10},{6,14},... | collective-permute-start | bytes 135176 | tf_op jit(solution)/shard_map/ppermute | solution.py:618
  55.7 1.4 %collective-permute-start.16 = (s16[176,128]{1,0:T(8,128)(2,1)S(1)}, s16[176,128]{1,0:T(8,128)(2,1)S(1)}, u32[]{:S(2)}, u32[]{:S(2)}) collective-permute-start(s16[176,128]{1,0:T(8,128)(2,1)S(1)} %get-tuple-element.49), channel_id=1, source_target_pairs={{0,12},{4,8},{8,4},{12,0},{1,13},{5,9},{9,5},{13,1},{2,14},{6,10},... | collective-permute-start | bytes 135176 | tf_op jit(solution)/shard_map/ppermute | solution.py:618
  57.8 0.9 %collective-permute-done.15.refs_1_ = s16[176,128]{1,0:T(8,128)(2,1)S(1)} collective-permute-done((s16[176,128]{1,0:T(8,128)(2,1)S(1)}, s16[176,128]{1,0:T(8,128)(2,1)S(1)}, u32[]{:S(2)}, u32[]{:S(2)}) %collective-permute-start.15) | collective-permute-done | bytes 45088 | tf_op jit(solution)/shard_map/ppermute | solution.py:618
  58.7 2.9 %collective-permute-done.16.refs_2_ = s16[176,128]{1,0:T(8,128)(2,1)S(1)} collective-permute-done((s16[176,128]{1,0:T(8,128)(2,1)S(1)}, s16[176,128]{1,0:T(8,128)(2,1)S(1)}, u32[]{:S(2)}, u32[]{:S(2)}) %collective-permute-start.16) | collective-permute-done | bytes 45088 | tf_op jit(solution)/shard_map/ppermute | solution.py:618
  61.5 0.9 %shard_map.111 = (f32[8,16,512]{2,1,0:T(8,128)}, f32[8,16,512]{2,1,0:T(8,128)}) custom-call(s32[1]{0:T(128)} %bitcast.me, f32[1]{0:T(128)S(6)} %copy.19.prev_mean, f32[8,16,512]{2,1,0:T(8,128)S(1)} %copy-done.2, f32[8,16,512]{2,1,0:T(8,128)S(1)} %copy-done.3, f32[8,16,128]{2,1,0:T(8,128)S(1)} %slice.35.gradient, f32[8,128]{1,0:T(8,128)S(1)} %get-tuple-element.46.sums, ...), custom_call_target="tpu_custom_call" | custom-call | flops 1000000 | bytes 2000000 | tf_op jit(solution)/shard_map/pallas_call | solution.py:766
  (33 shorter events, 0.2 us)
Async XLA Ops:
  0.6 1.2 %copy-start = (bf16[2,8,64,512]{3,2,1,0:T(8,128)(2,1)S(1)}, bf16[2,8,64,512]{3,2,1,0:T(8,128)(2,1)}, u32[]{:S(2)}) copy-start(bf16[2,8,64,512]{3,2,1,0:T(8,128)(2,1)} %slc.1) | copy-start | bytes 3145732
  1.9 2.4 %copy-start.1 = (bf16[2,8,64,512]{3,2,1,0:T(8,128)(2,1)S(1)}, bf16[2,8,64,512]{3,2,1,0:T(8,128)(2,1)}, u32[]{:S(2)}) copy-start(bf16[2,8,64,512]{3,2,1,0:T(8,128)(2,1)} %slc.1) | copy-start | bytes 3145732
  2.1 2.2 %collective-permute-start = (bf16[64,128]{1,0:T(8,128)(2,1)S(1)}, bf16[64,128]{1,0:T(8,128)(2,1)S(1)}, u32[]{:S(2)}, u32[]{:S(2)}) collective-permute-start(bf16[64,128]{1,0:T(8,128)(2,1)S(1)} %shard_map.104), channel_id=1, source_target_pairs={{0,1},{1,0},{2,3},{3,2},{4,5},{5,4},{6,7},{7,6},{8,9},{9,8},{10,11... | collective-permute-start | bytes 49160 | tf_op jit(solution)/shard_map/ppermute | solution.py:609
  2.6 0.7 %copy-start.7 = (s32[8,4]{0,1:T(4,128)S(1)}, s32[8,4]{0,1:T(4,128)}, u32[]{:S(2)}) copy-start(s32[8,4]{0,1:T(4,128)} %param.10) | copy-start | bytes 388
  3.4 0.7 %copy-start.8 = (f32[8,4]{0,1:T(4,128)S(1)}, f32[8,4]{0,1:T(4,128)}, u32[]{:S(2)}) copy-start(f32[8,4]{0,1:T(4,128)} %param.11) | copy-start | bytes 388
  4.3 8.4 %copy-start.2 = (f32[8,16,512]{2,1,0:T(8,128)S(1)}, f32[8,16,512]{2,1,0:T(8,128)}, u32[]{:S(2)}) copy-start(f32[8,16,512]{2,1,0:T(8,128)} %estimate.1) | copy-start | bytes 786436
  4.3 8.4 %copy-start.3 = (f32[8,16,512]{2,1,0:T(8,128)S(1)}, f32[8,16,512]{2,1,0:T(8,128)}, u32[]{:S(2)}) copy-start(f32[8,16,512]{2,1,0:T(8,128)} %direction.1) | copy-start | bytes 786436
  5.6 15.5 %collective-permute-start.1 = (bf16[1088,128]{1,0:T(8,128)(2,1)S(1)}, bf16[1088,128]{1,0:T(8,128)(2,1)S(1)}, u32[]{:S(2)}, u32[]{:S(2)}) collective-permute-start(bf16[1088,128]{1,0:T(8,128)(2,1)S(1)} %get-tuple-element.27), channel_id=1, source_target_pairs={{0,4},{4,0},{8,12},{12,8},{1,5},{5,1},{9,13},{13,9},{2,6},{6,2},{1... | collective-permute-start | bytes 835592 | tf_op jit(solution)/shard_map/ppermute | solution.py:618
  8.3 22.4 %collective-permute-start.2 = (bf16[1088,128]{1,0:T(8,128)(2,1)S(1)}, bf16[1088,128]{1,0:T(8,128)(2,1)S(1)}, u32[]{:S(2)}, u32[]{:S(2)}) collective-permute-start(bf16[1088,128]{1,0:T(8,128)(2,1)S(1)} %get-tuple-element.28), channel_id=1, source_target_pairs={{0,8},{4,12},{8,0},{12,4},{1,9},{5,13},{9,1},{13,5},{2,10},{6,14},... | collective-permute-start | bytes 835592 | tf_op jit(solution)/shard_map/ppermute | solution.py:618
  10.9 21.3 %collective-permute-start.3 = (bf16[1088,128]{1,0:T(8,128)(2,1)S(1)}, bf16[1088,128]{1,0:T(8,128)(2,1)S(1)}, u32[]{:S(2)}, u32[]{:S(2)}) collective-permute-start(bf16[1088,128]{1,0:T(8,128)(2,1)S(1)} %get-tuple-element.29), channel_id=1, source_target_pairs={{0,12},{4,8},{8,4},{12,0},{1,13},{5,9},{9,5},{13,1},{2,14},{6,10},... | collective-permute-start | bytes 835592 | tf_op jit(solution)/shard_map/ppermute | solution.py:618
  11.0 30.2 %collective-permute-start.9 = (bf16[272,128]{1,0:T(8,128)(2,1)S(1)}, bf16[272,128]{1,0:T(8,128)(2,1)S(1)}, u32[]{:S(2)}, u32[]{:S(2)}) collective-permute-start(bf16[272,128]{1,0:T(8,128)(2,1)S(1)} %bitcast.17), channel_id=1, source_target_pairs={{0,2},{2,0},{1,3},{3,1},{4,6},{6,4},{5,7},{7,5},{8,10},{10,8},{9,1... | collective-permute-start | bytes 208904 | tf_op jit(solution)/shard_map/ppermute | solution.py:670
  21.1 12.0 %collective-permute-start.4 = (bf16[272,128]{1,0:T(8,128)(2,1)S(1)}, bf16[272,128]{1,0:T(8,128)(2,1)S(1)}, u32[]{:S(2)}, u32[]{:S(2)}) collective-permute-start(bf16[272,128]{1,0:T(8,128)(2,1)S(1)} %bitcast.19), channel_id=1, source_target_pairs={{0,2},{2,0},{1,3},{3,1},{4,6},{6,4},{5,7},{7,5},{8,10},{10,8},{9,1... | collective-permute-start | bytes 208904 | tf_op jit(solution)/shard_map/ppermute | solution.py:670
  30.6 4.4 %collective-permute-start.5 = (bf16[272,128]{1,0:T(8,128)(2,1)S(1)}, bf16[272,128]{1,0:T(8,128)(2,1)S(1)}, u32[]{:S(2)}, u32[]{:S(2)}) collective-permute-start(bf16[272,128]{1,0:T(8,128)(2,1)S(1)} %bitcast.20), channel_id=1, source_target_pairs={{0,2},{2,0},{1,3},{3,1},{4,6},{6,4},{5,7},{7,5},{8,10},{10,8},{9,1... | collective-permute-start | bytes 208904 | tf_op jit(solution)/shard_map/ppermute | solution.py:670
  32.2 9.0 %collective-permute-start.10 = (bf16[272,128]{1,0:T(8,128)(2,1)S(1)}, bf16[272,128]{1,0:T(8,128)(2,1)S(1)}, u32[]{:S(2)}, u32[]{:S(2)}) collective-permute-start(bf16[272,128]{1,0:T(8,128)(2,1)S(1)} %bitcast.18), channel_id=1, source_target_pairs={{0,2},{2,0},{1,3},{3,1},{4,6},{6,4},{5,7},{7,5},{8,10},{10,8},{9,1... | collective-permute-start | bytes 208904 | tf_op jit(solution)/shard_map/ppermute | solution.py:670
  33.0 8.2 %copy-start.6 = (bf16[96,96]{1,0:T(8,128)(2,1)S(1)}, bf16[96,96]{1,0:T(8,128)(2,1)}, u32[]{:S(2)}) copy-start(bf16[96,96]{1,0:T(8,128)(2,1)} %constant.80.clone.order) | copy-start | bytes 55300
  33.1 8.2 %copy-start.4 = (bf16[256,128]{1,0:T(8,128)(2,1)S(1)}, bf16[256,128]{1,0:T(8,128)(2,1)}, u32[]{:S(2)}) copy-start(bf16[256,128]{1,0:T(8,128)(2,1)} %constant.82.clone.rim_band) | copy-start | bytes 196612
  33.1 8.2 %copy-start.5 = (bf16[256,128]{1,0:T(8,128)(2,1)S(1)}, bf16[256,128]{1,0:T(8,128)(2,1)}, u32[]{:S(2)}) copy-start(bf16[256,128]{1,0:T(8,128)(2,1)} %constant.81.clone.band) | copy-start | bytes 196612
  35.0 12.3 %collective-permute-start.6 = (s16[2,128,128]{2,1,0:T(8,128)(2,1)S(1)}, s16[2,128,128]{2,1,0:T(8,128)(2,1)S(1)}, u32[]{:S(2)}, u32[]{:S(2)}) collective-permute-start(s16[2,128,128]{2,1,0:T(8,128)(2,1)S(1)} %get-tuple-element.36), channel_id=1, source_target_pairs={{0,4},{4,0},{8,12},{12,8},{1,5},{5,1},{9,13},{13,9},{2,6},{6,2},{1... | collective-permute-start | bytes 196616 | tf_op jit(solution)/shard_map/ppermute | solution.py:618
  38.5 8.9 %collective-permute-start.7 = (s16[2,128,128]{2,1,0:T(8,128)(2,1)S(1)}, s16[2,128,128]{2,1,0:T(8,128)(2,1)S(1)}, u32[]{:S(2)}, u32[]{:S(2)}) collective-permute-start(s16[2,128,128]{2,1,0:T(8,128)(2,1)S(1)} %get-tuple-element.37), channel_id=1, source_target_pairs={{0,8},{4,12},{8,0},{12,4},{1,9},{5,13},{9,1},{13,5},{2,10},{6,14},... | collective-permute-start | bytes 196616 | tf_op jit(solution)/shard_map/ppermute | solution.py:618
  39.5 7.8 %collective-permute-start.8 = (s16[2,128,128]{2,1,0:T(8,128)(2,1)S(1)}, s16[2,128,128]{2,1,0:T(8,128)(2,1)S(1)}, u32[]{:S(2)}, u32[]{:S(2)}) collective-permute-start(s16[2,128,128]{2,1,0:T(8,128)(2,1)S(1)} %get-tuple-element.38), channel_id=1, source_target_pairs={{0,12},{4,8},{8,4},{12,0},{1,13},{5,9},{9,5},{13,1},{2,14},{6,10},... | collective-permute-start | bytes 196616 | tf_op jit(solution)/shard_map/ppermute | solution.py:618
  48.8 1.4 %collective-permute-start.13 = (f32[8,128]{1,0:T(8,128)S(1)}, f32[8,128]{1,0:T(8,128)S(1)}, u32[]{:S(2)}, u32[]{:S(2)}) collective-permute-start(f32[8,128]{1,0:T(8,128)S(1)} %get-tuple-element.45.refs_3_), channel_id=1, source_target_pairs={{0,3},{1,0},{2,1},{3,2},{4,7},{5,4},{6,5},{7,6},{8,11},{9,8},{10,9... | collective-permute-start | bytes 12296 | tf_op jit(solution)/shard_map/ppermute | solution.py:745
  48.9 3.7 %collective-permute-start.12 = (f32[8,128]{1,0:T(8,128)S(1)}, f32[8,128]{1,0:T(8,128)S(1)}, u32[]{:S(2)}, u32[]{:S(2)}) collective-permute-start(f32[8,128]{1,0:T(8,128)S(1)} %get-tuple-element.45.refs_3_), channel_id=1, source_target_pairs={{0,2},{1,3},{2,0},{3,1},{4,6},{5,7},{6,4},{7,5},{8,10},{9,11},{10,... | collective-permute-start | bytes 12296 | tf_op jit(solution)/shard_map/ppermute | solution.py:745
  49.5 3.1 %collective-permute-start.11 = (f32[8,128]{1,0:T(8,128)S(1)}, f32[8,128]{1,0:T(8,128)S(1)}, u32[]{:S(2)}, u32[]{:S(2)}) collective-permute-start(f32[8,128]{1,0:T(8,128)S(1)} %get-tuple-element.45.refs_3_), channel_id=1, source_target_pairs={{0,1},{1,2},{2,3},{3,0},{4,5},{5,6},{6,7},{7,4},{8,9},{9,10},{10,1... | collective-permute-start | bytes 12296 | tf_op jit(solution)/shard_map/ppermute | solution.py:745
  52.6 5.1 %collective-permute-start.14 = (s16[176,128]{1,0:T(8,128)(2,1)S(1)}, s16[176,128]{1,0:T(8,128)(2,1)S(1)}, u32[]{:S(2)}, u32[]{:S(2)}) collective-permute-start(s16[176,128]{1,0:T(8,128)(2,1)S(1)} %get-tuple-element.47), channel_id=1, source_target_pairs={{0,4},{4,0},{8,12},{12,8},{1,5},{5,1},{9,13},{13,9},{2,6},{6,2},{1... | collective-permute-start | bytes 135176 | tf_op jit(solution)/shard_map/ppermute | solution.py:618
  53.7 5.0 %collective-permute-start.15 = (s16[176,128]{1,0:T(8,128)(2,1)S(1)}, s16[176,128]{1,0:T(8,128)(2,1)S(1)}, u32[]{:S(2)}, u32[]{:S(2)}) collective-permute-start(s16[176,128]{1,0:T(8,128)(2,1)S(1)} %get-tuple-element.48), channel_id=1, source_target_pairs={{0,8},{4,12},{8,0},{12,4},{1,9},{5,13},{9,1},{13,5},{2,10},{6,14},... | collective-permute-start | bytes 135176 | tf_op jit(solution)/shard_map/ppermute | solution.py:618
  55.7 5.8 %collective-permute-start.16 = (s16[176,128]{1,0:T(8,128)(2,1)S(1)}, s16[176,128]{1,0:T(8,128)(2,1)S(1)}, u32[]{:S(2)}, u32[]{:S(2)}) collective-permute-start(s16[176,128]{1,0:T(8,128)(2,1)S(1)} %get-tuple-element.49), channel_id=1, source_target_pairs={{0,12},{4,8},{8,4},{12,0},{1,13},{5,9},{9,5},{13,1},{2,14},{6,10},... | collective-permute-start | bytes 135176 | tf_op jit(solution)/shard_map/ppermute | solution.py:618

commit v21 on v20

--- a/solution.py
+++ b/solution.py
@@ -671,7 +671,9 @@
             return got, got
         return swapped(border(rows - HALO), border(0), "space")
 
-    block = [messages[0]] + [exchanged(messages[by], "epoch", by) for by in range(1, tiles)]
+    turns = sorted(range(1, tiles), key=lambda by: (by == tiles - 1, by == 1))
+    block = {by: exchanged(messages[by], "epoch", by) for by in turns}
+    block[0] = messages[0]
     estimate, direction, _ = lax.optimization_barrier((estimate, direction, messages))
     fields = pl.pallas_call(
         fields_kernel,
@@ -684,9 +686,14 @@
     def params_in(shift):
         return block[shift][tile_rows : tile_rows + epochs, PARAM_LANE : PARAM_LANE + 4 * SLOTS].astype(f32)
 
-    halos = [halo([array.reshape(-1, rows, LANES)]) for array in block]
-    late = lax.optimization_barrier((fields, block, halos[1:-1]))[0]
-    field = [fields[0]] + [exchanged(late[by], "epoch", by) for by in range(1, tiles)]
+    halos = {by: halo([block[by].reshape(-1, rows, LANES)]) for by in [0] + turns}
+    field = {0: fields[0]}
+    for at, by in enumerate(turns):
+        awaited = [halos[0]] + [block[other] for other in turns[: at + 1]]
+        if by == turns[-1]:
+            awaited += [halos[other] for other in turns[:-1]]
+        field[by] = exchanged(lax.optimization_barrier((fields[by], awaited))[0], "epoch", by)
+    block, field = ([array[by] for by in range(tiles)] for array in (block, field))
 
     listed = jnp.concatenate([params_in(shift) for shift in range(tiles)], axis=0)
     place = jnp.arange(total, dtype=jnp.int32)[:, None]

time: 62.7 us -> 64.1 us (1.022)
  starting transfers between devices: 22.5 us -> 23.9 us
    ppermute x3, starting transfers between devices: 0.83 us -> 1.78 us  [transposed_plan(): lax.ppermute(sums, place, [(i, (i + by) % count) for i in range(count)])]
where the time goes in v21:
time: 64.1 us; the launch traced here: 63.9 us
  waiting for transfers between devices  24.5 us (38%)
  starting transfers between devices  23.9 us (37%)
  Pallas kernels  10.2 us (16%)
  local copies, waits for them, and re-layouts  3.32 us (5%)
  between operations  1.49 us (2%)
    ppermute x9, waiting for transfers between devices, exchanged(): return lax.ppermute(x, axis, [(i, i ^ by) for i in range(size)])  19.9 us
    ppermute x9, starting transfers between devices, exchanged(): return lax.ppermute(x, axis, [(i, i ^ by) for i in range(size)])  16.1 us
    pallas_call x1, Pallas kernels, transposed_plan(): pl.pallas_call(functools.partial(pair_kernel, (epochs, rows, len(operands...  6.05 us
    ppermute x4, starting transfers between devices, halo(): lax.ppermute(border(jnp.where(space == 0, rows - HALO, 0)), 'space', [(0,...  5.55 us
    unnamed x20, local copies, waits for them, and re-layouts  2.76 us
    ppermute x3, waiting for transfers between devices, transposed_plan(): lax.ppermute(sums, place, [(i, (i + by) % count) for i in range(count)])  2.74 us
    ppermute x4, waiting for transfers between devices, halo(): lax.ppermute(border(jnp.where(space == 0, rows - HALO, 0)), 'space', [(0,...  1.85 us
    ppermute x3, starting transfers between devices, transposed_plan(): lax.ppermute(sums, place, [(i, (i + by) % count) for i in range(count)])  1.78 us
  transfers between devices with their start and end apart: 17, of which 7 were waited for; matrix products, arithmetic and copies ran while one was open for 2% of the time, Pallas kernels for 10%

profile of v21, /device:TPU:0, one launch (start us, length us, event | category | flops | bytes accessed | tf_op | source)
XLA Modules:
  0.0 63.9 jit_solution(12915829407849290959)
XLA Ops:
  0.6 1.2 %copy-done = bf16[2,8,64,512]{3,2,1,0:T(8,128)(2,1)S(1)} copy-done((bf16[2,8,64,512]{3,2,1,0:T(8,128)(2,1)S(1)}, bf16[2,8,64,512]{3,2,1,0:T(8,128)(2,1)}, u32[]{:S(2)}) %copy-start) | copy-done | bytes 1048600
  1.9 0.2 shard_map.104
  2.1 0.5 collective-permute-start
  2.6 0.7 %copy-done.7 = s32[8,4]{0,1:T(4,128)S(1)} copy-done((s32[8,4]{0,1:T(4,128)S(1)}, s32[8,4]{0,1:T(4,128)}, u32[]{:S(2)}) %copy-start.7) | copy-done | bytes 152
  3.3 0.1 copy.15
  3.4 0.7 %copy-done.8 = f32[8,4]{0,1:T(4,128)S(1)} copy-done((f32[8,4]{0,1:T(4,128)S(1)}, f32[8,4]{0,1:T(4,128)}, u32[]{:S(2)}) %copy-start.8) | copy-done | bytes 152
  4.1 0.1 copy.16
  4.1 0.1 select_maximum_fusion.params
  4.2 0.1 add_convert_fusion.present
  4.3 0.0 copy-start.3
  4.3 1.3 %shard_map.105 = (bf16[1088,128]{1,0:T(8,128)(2,1)S(1)}, bf16[1088,128]{1,0:T(8,128)(2,1)S(1)}, bf16[1088,128]{1,0:T(8,128)(2,1)S(1)}, bf16[1088,128]{1,0:T(8,128)(2,1)S(1)}) custom-call(s32[1]{0:T(128)} %bitcast.me, f32[2]{0:T(128)S(1)} %add_convert_fusion.present, bf16[2,8,64,512]{3,2,1,0:T(8,128)(2,1)S(1)} %copy-done.1, ...), custom_call_target="tpu_custom_call" | custom-call | flops 3000000 | bytes 4000000 | tf_op jit(solution)/shard_map/pallas_call | solution.py:651
  5.6 2.7 %collective-permute-start.1 = (bf16[1088,128]{1,0:T(8,128)(2,1)S(1)}, bf16[1088,128]{1,0:T(8,128)(2,1)S(1)}, u32[]{:S(2)}, u32[]{:S(2)}) collective-permute-start(bf16[1088,128]{1,0:T(8,128)(2,1)S(1)} %get-tuple-element.27), channel_id=1, source_target_pairs={{0,4},{4,0},{8,12},{12,8},{1,5},{5,1},{9,13},{13,9},{2,6},{6,2},{1... | collective-permute-start | bytes 835592 | tf_op jit(solution)/shard_map/ppermute | solution.py:618
  8.3 2.6 %collective-permute-start.2 = (bf16[1088,128]{1,0:T(8,128)(2,1)S(1)}, bf16[1088,128]{1,0:T(8,128)(2,1)S(1)}, u32[]{:S(2)}, u32[]{:S(2)}) collective-permute-start(bf16[1088,128]{1,0:T(8,128)(2,1)S(1)} %get-tuple-element.28), channel_id=1, source_target_pairs={{0,8},{4,12},{8,0},{12,4},{1,9},{5,13},{9,1},{13,5},{2,10},{6,14},... | collective-permute-start | bytes 835592 | tf_op jit(solution)/shard_map/ppermute | solution.py:618
  10.9 0.1 add_convert_fusion.1.present
  10.9 0.0 collective-permute-start.3
  11.0 0.1 slice.27
  11.0 1.7 %collective-permute-start.4 = (bf16[272,128]{1,0:T(8,128)(2,1)S(1)}, bf16[272,128]{1,0:T(8,128)(2,1)S(1)}, u32[]{:S(2)}, u32[]{:S(2)}) collective-permute-start(bf16[272,128]{1,0:T(8,128)(2,1)S(1)} %bitcast.20), channel_id=1, source_target_pairs={{0,2},{2,0},{1,3},{3,1},{4,6},{6,4},{5,7},{7,5},{8,10},{10,8},{9,1... | collective-permute-start | bytes 208904 | tf_op jit(solution)/shard_map/ppermute | solution.py:670
  12.7 0.1 shard_map.106
  12.9 8.3 %collective-permute-done.1.refs_1_ = bf16[1088,128]{1,0:T(8,128)(2,1)S(1)} collective-permute-done((bf16[1088,128]{1,0:T(8,128)(2,1)S(1)}, bf16[1088,128]{1,0:T(8,128)(2,1)S(1)}, u32[]{:S(2)}, u32[]{:S(2)}) %collective-permute-start.1) | collective-permute-done | bytes 278560 | tf_op jit(solution)/shard_map/ppermute | solution.py:618
  21.1 1.7 %collective-permute-start.8 = (bf16[272,128]{1,0:T(8,128)(2,1)S(1)}, bf16[272,128]{1,0:T(8,128)(2,1)S(1)}, u32[]{:S(2)}, u32[]{:S(2)}) collective-permute-start(bf16[272,128]{1,0:T(8,128)(2,1)S(1)} %bitcast.17), channel_id=1, source_target_pairs={{0,2},{2,0},{1,3},{3,1},{4,6},{6,4},{5,7},{7,5},{8,10},{10,8},{9,1... | collective-permute-start | bytes 208904 | tf_op jit(solution)/shard_map/ppermute | solution.py:670
  22.8 7.8 %collective-permute-done.2.refs_2_ = bf16[1088,128]{1,0:T(8,128)(2,1)S(1)} collective-permute-done((bf16[1088,128]{1,0:T(8,128)(2,1)S(1)}, bf16[1088,128]{1,0:T(8,128)(2,1)S(1)}, u32[]{:S(2)}, u32[]{:S(2)}) %collective-permute-start.2) | collective-permute-done | bytes 278560 | tf_op jit(solution)/shard_map/ppermute | solution.py:618
  30.6 3.0 %collective-permute-start.6 = (s16[2,128,128]{2,1,0:T(8,128)(2,1)S(1)}, s16[2,128,128]{2,1,0:T(8,128)(2,1)S(1)}, u32[]{:S(2)}, u32[]{:S(2)}) collective-permute-start(s16[2,128,128]{2,1,0:T(8,128)(2,1)S(1)} %get-tuple-element.36), channel_id=1, source_target_pairs={{0,8},{4,12},{8,0},{12,4},{1,9},{5,13},{9,1},{13,5},{2,10},{6,14},... | collective-permute-start | bytes 196616 | tf_op jit(solution)/shard_map/ppermute | solution.py:618
  33.7 1.6 %collective-permute-start.7 = (bf16[272,128]{1,0:T(8,128)(2,1)S(1)}, bf16[272,128]{1,0:T(8,128)(2,1)S(1)}, u32[]{:S(2)}, u32[]{:S(2)}) collective-permute-start(bf16[272,128]{1,0:T(8,128)(2,1)S(1)} %bitcast.19), channel_id=1, source_target_pairs={{0,2},{2,0},{1,3},{3,1},{4,6},{6,4},{5,7},{7,5},{8,10},{10,8},{9,1... | collective-permute-start | bytes 208904 | tf_op jit(solution)/shard_map/ppermute | solution.py:670
  35.3 0.6 collective-permute-start.10
  35.9 0.1 slice.36
  35.9 0.1 slice.37
  36.0 0.1 slice.38
  36.1 0.0 copy-start.5
  36.1 0.1 fusion.5
  36.2 1.8 %collective-permute-done.7.refs_6_ = bf16[272,128]{1,0:T(8,128)(2,1)S(1)} collective-permute-done((bf16[272,128]{1,0:T(8,128)(2,1)S(1)}, bf16[272,128]{1,0:T(8,128)(2,1)S(1)}, u32[]{:S(2)}, u32[]{:S(2)}) %collective-permute-start.7) | collective-permute-done | bytes 69664 | tf_op jit(solution)/shard_map/ppermute | solution.py:670
  38.1 1.3 %collective-permute-start.9 = (s16[2,128,128]{2,1,0:T(8,128)(2,1)S(1)}, s16[2,128,128]{2,1,0:T(8,128)(2,1)S(1)}, u32[]{:S(2)}, u32[]{:S(2)}) collective-permute-start(s16[2,128,128]{2,1,0:T(8,128)(2,1)S(1)} %get-tuple-element.38), channel_id=1, source_target_pairs={{0,12},{4,8},{8,4},{12,0},{1,13},{5,9},{9,5},{13,1},{2,14},{6,10},... | collective-permute-start | bytes 196616 | tf_op jit(solution)/shard_map/ppermute | solution.py:618
  39.4 0.1 slice_add_fusion
  39.5 0.1 reshape.97.partner
  39.6 0.1 reshape.104.weight
  39.7 6.1 %shard_map.107 = (f32[128,16,128]{2,1,0:T(8,128)S(1)}, f32[128,16,128]{2,1,0:T(8,128)S(1)}) custom-call(s32[128]{0:T(128)S(1)} %reshape.97.partner, f32[128]{0:T(128)S(1)} %reshape.104.weight, f32[2]{0:T(128)S(1)} %add_convert_fusion.1.present, bf16[96,96]{1,0:T(8,128)(2,1)S(1)} %copy-done.6, bf16[256,128]{1,0:T(8,128)(2,1)S(1)} %copy-done.5, ...), custom_call_target="tpu_custom_call" | custom-call | flops 20000000 | bytes 30000000 | tf_op jit(solution)/shard_map/pallas_call | solution.py:720
  45.8 1.5 %shard_map.108 = (f32[32,16,128]{2,1,0:T(8,128)S(1)}, f32[8,128]{1,0:T(8,128)S(1)}) custom-call(s32[128]{0:T(128)S(1)} %reshape.97.partner, s16[2,128,128]{2,1,0:T(8,128)(2,1)S(1)} %get-tuple-element.32.refs_0_, s16[2,128,128]{2,1,0:T(8,128)(2,1)S(1)} %collective-permute-done.5.refs_1_, s16[2,128,128]{2,1,0:T(8,128)(2,1)S(1)} %collective-permute-done.6.refs_2_, ...), custom_call_target="tpu_custom_call" | custom-call | flops 10000000 | bytes 8000000 | tf_op jit(solution)/shard_map/pallas_call | solution.py:736
  47.3 0.1 collective-permute-start.13
  47.4 1.6 %collective-permute-start.12 = (f32[8,128]{1,0:T(8,128)S(1)}, f32[8,128]{1,0:T(8,128)S(1)}, u32[]{:S(2)}, u32[]{:S(2)}) collective-permute-start(f32[8,128]{1,0:T(8,128)S(1)} %get-tuple-element.45.refs_3_), channel_id=1, source_target_pairs={{0,2},{1,3},{2,0},{3,1},{4,6},{5,7},{6,4},{7,5},{8,10},{9,11},{10,... | collective-permute-start | bytes 12296 | tf_op jit(solution)/shard_map/ppermute | solution.py:752
  48.9 0.2 collective-permute-start.11
  49.1 0.1 shard_map.109
  49.2 1.8 %collective-permute-done.12.refs_5_ = f32[8,128]{1,0:T(8,128)S(1)} collective-permute-done((f32[8,128]{1,0:T(8,128)S(1)}, f32[8,128]{1,0:T(8,128)S(1)}, u32[]{:S(2)}, u32[]{:S(2)}) %collective-permute-start.12) | collective-permute-done | bytes 4128 | tf_op jit(solution)/shard_map/ppermute | solution.py:752
  51.1 0.9 %collective-permute-done.11.refs_4_ = f32[8,128]{1,0:T(8,128)S(1)} collective-permute-done((f32[8,128]{1,0:T(8,128)S(1)}, f32[8,128]{1,0:T(8,128)S(1)}, u32[]{:S(2)}, u32[]{:S(2)}) %collective-permute-start.11) | collective-permute-done | bytes 4128 | tf_op jit(solution)/shard_map/ppermute | solution.py:752
  52.0 3.2 %collective-permute-start.14 = (s16[176,128]{1,0:T(8,128)(2,1)S(1)}, s16[176,128]{1,0:T(8,128)(2,1)S(1)}, u32[]{:S(2)}, u32[]{:S(2)}) collective-permute-start(s16[176,128]{1,0:T(8,128)(2,1)S(1)} %get-tuple-element.47), channel_id=1, source_target_pairs={{0,4},{4,0},{8,12},{12,8},{1,5},{5,1},{9,13},{13,9},{2,6},{6,2},{1... | collective-permute-start | bytes 135176 | tf_op jit(solution)/shard_map/ppermute | solution.py:618
  55.3 1.8 %collective-permute-start.15 = (s16[176,128]{1,0:T(8,128)(2,1)S(1)}, s16[176,128]{1,0:T(8,128)(2,1)S(1)}, u32[]{:S(2)}, u32[]{:S(2)}) collective-permute-start(s16[176,128]{1,0:T(8,128)(2,1)S(1)} %get-tuple-element.48), channel_id=1, source_target_pairs={{0,8},{4,12},{8,0},{12,4},{1,9},{5,13},{9,1},{13,5},{2,10},{6,14},... | collective-permute-start | bytes 135176 | tf_op jit(solution)/shard_map/ppermute | solution.py:618
  57.1 1.4 %collective-permute-start.16 = (s16[176,128]{1,0:T(8,128)(2,1)S(1)}, s16[176,128]{1,0:T(8,128)(2,1)S(1)}, u32[]{:S(2)}, u32[]{:S(2)}) collective-permute-start(s16[176,128]{1,0:T(8,128)(2,1)S(1)} %get-tuple-element.49), channel_id=1, source_target_pairs={{0,12},{4,8},{8,4},{12,0},{1,13},{5,9},{9,5},{13,1},{2,14},{6,10},... | collective-permute-start | bytes 135176 | tf_op jit(solution)/shard_map/ppermute | solution.py:618
  59.1 1.4 %collective-permute-done.15.refs_1_ = s16[176,128]{1,0:T(8,128)(2,1)S(1)} collective-permute-done((s16[176,128]{1,0:T(8,128)(2,1)S(1)}, s16[176,128]{1,0:T(8,128)(2,1)S(1)}, u32[]{:S(2)}, u32[]{:S(2)}) %collective-permute-start.15) | collective-permute-done | bytes 45088 | tf_op jit(solution)/shard_map/ppermute | solution.py:618
  60.5 2.5 %collective-permute-done.16.refs_2_ = s16[176,128]{1,0:T(8,128)(2,1)S(1)} collective-permute-done((s16[176,128]{1,0:T(8,128)(2,1)S(1)}, s16[176,128]{1,0:T(8,128)(2,1)S(1)}, u32[]{:S(2)}, u32[]{:S(2)}) %collective-permute-start.16) | collective-permute-done | bytes 45088 | tf_op jit(solution)/shard_map/ppermute | solution.py:618
  63.0 0.9 %shard_map.111 = (f32[8,16,512]{2,1,0:T(8,128)}, f32[8,16,512]{2,1,0:T(8,128)}) custom-call(s32[1]{0:T(128)} %bitcast.me, f32[1]{0:T(128)S(6)} %copy.19.prev_mean, f32[8,16,512]{2,1,0:T(8,128)S(1)} %copy-done.2, f32[8,16,512]{2,1,0:T(8,128)S(1)} %copy-done.3, f32[8,16,128]{2,1,0:T(8,128)S(1)} %slice.35.gradient, f32[8,128]{1,0:T(8,128)S(1)} %get-tuple-element.46.sums, ...), custom_call_target="tpu_custom_call" | custom-call | flops 1000000 | bytes 2000000 | tf_op jit(solution)/shard_map/pallas_call | solution.py:773
  (33 shorter events, 0.2 us)
Async XLA Ops:
  0.6 1.2 %copy-start = (bf16[2,8,64,512]{3,2,1,0:T(8,128)(2,1)S(1)}, bf16[2,8,64,512]{3,2,1,0:T(8,128)(2,1)}, u32[]{:S(2)}) copy-start(bf16[2,8,64,512]{3,2,1,0:T(8,128)(2,1)} %slc.1) | copy-start | bytes 3145732
  1.9 2.4 %copy-start.1 = (bf16[2,8,64,512]{3,2,1,0:T(8,128)(2,1)S(1)}, bf16[2,8,64,512]{3,2,1,0:T(8,128)(2,1)}, u32[]{:S(2)}) copy-start(bf16[2,8,64,512]{3,2,1,0:T(8,128)(2,1)} %slc.1) | copy-start | bytes 3145732
  2.1 2.2 %collective-permute-start = (bf16[64,128]{1,0:T(8,128)(2,1)S(1)}, bf16[64,128]{1,0:T(8,128)(2,1)S(1)}, u32[]{:S(2)}, u32[]{:S(2)}) collective-permute-start(bf16[64,128]{1,0:T(8,128)(2,1)S(1)} %shard_map.104), channel_id=1, source_target_pairs={{0,1},{1,0},{2,3},{3,2},{4,5},{5,4},{6,7},{7,6},{8,9},{9,8},{10,11... | collective-permute-start | bytes 49160 | tf_op jit(solution)/shard_map/ppermute | solution.py:609
  2.6 0.7 %copy-start.7 = (s32[8,4]{0,1:T(4,128)S(1)}, s32[8,4]{0,1:T(4,128)}, u32[]{:S(2)}) copy-start(s32[8,4]{0,1:T(4,128)} %param.10) | copy-start | bytes 388
  3.4 0.7 %copy-start.8 = (f32[8,4]{0,1:T(4,128)S(1)}, f32[8,4]{0,1:T(4,128)}, u32[]{:S(2)}) copy-start(f32[8,4]{0,1:T(4,128)} %param.11) | copy-start | bytes 388
  4.3 8.4 %copy-start.2 = (f32[8,16,512]{2,1,0:T(8,128)S(1)}, f32[8,16,512]{2,1,0:T(8,128)}, u32[]{:S(2)}) copy-start(f32[8,16,512]{2,1,0:T(8,128)} %estimate.1) | copy-start | bytes 786436
  4.3 8.4 %copy-start.3 = (f32[8,16,512]{2,1,0:T(8,128)S(1)}, f32[8,16,512]{2,1,0:T(8,128)}, u32[]{:S(2)}) copy-start(f32[8,16,512]{2,1,0:T(8,128)} %direction.1) | copy-start | bytes 786436
  5.6 15.5 %collective-permute-start.1 = (bf16[1088,128]{1,0:T(8,128)(2,1)S(1)}, bf16[1088,128]{1,0:T(8,128)(2,1)S(1)}, u32[]{:S(2)}, u32[]{:S(2)}) collective-permute-start(bf16[1088,128]{1,0:T(8,128)(2,1)S(1)} %get-tuple-element.27), channel_id=1, source_target_pairs={{0,4},{4,0},{8,12},{12,8},{1,5},{5,1},{9,13},{13,9},{2,6},{6,2},{1... | collective-permute-start | bytes 835592 | tf_op jit(solution)/shard_map/ppermute | solution.py:618
  8.3 22.4 %collective-permute-start.2 = (bf16[1088,128]{1,0:T(8,128)(2,1)S(1)}, bf16[1088,128]{1,0:T(8,128)(2,1)S(1)}, u32[]{:S(2)}, u32[]{:S(2)}) collective-permute-start(bf16[1088,128]{1,0:T(8,128)(2,1)S(1)} %get-tuple-element.28), channel_id=1, source_target_pairs={{0,8},{4,12},{8,0},{12,4},{1,9},{5,13},{9,1},{13,5},{2,10},{6,14},... | collective-permute-start | bytes 835592 | tf_op jit(solution)/shard_map/ppermute | solution.py:618
  10.9 24.3 %collective-permute-start.3 = (bf16[1088,128]{1,0:T(8,128)(2,1)S(1)}, bf16[1088,128]{1,0:T(8,128)(2,1)S(1)}, u32[]{:S(2)}, u32[]{:S(2)}) collective-permute-start(bf16[1088,128]{1,0:T(8,128)(2,1)S(1)} %get-tuple-element.29), channel_id=1, source_target_pairs={{0,12},{4,8},{8,4},{12,0},{1,13},{5,9},{9,5},{13,1},{2,14},{6,10},... | collective-permute-start | bytes 835592 | tf_op jit(solution)/shard_map/ppermute | solution.py:618
  11.0 11.8 %collective-permute-start.4 = (bf16[272,128]{1,0:T(8,128)(2,1)S(1)}, bf16[272,128]{1,0:T(8,128)(2,1)S(1)}, u32[]{:S(2)}, u32[]{:S(2)}) collective-permute-start(bf16[272,128]{1,0:T(8,128)(2,1)S(1)} %bitcast.20), channel_id=1, source_target_pairs={{0,2},{2,0},{1,3},{3,1},{4,6},{6,4},{5,7},{7,5},{8,10},{10,8},{9,1... | collective-permute-start | bytes 208904 | tf_op jit(solution)/shard_map/ppermute | solution.py:670
  21.1 15.1 %collective-permute-start.8 = (bf16[272,128]{1,0:T(8,128)(2,1)S(1)}, bf16[272,128]{1,0:T(8,128)(2,1)S(1)}, u32[]{:S(2)}, u32[]{:S(2)}) collective-permute-start(bf16[272,128]{1,0:T(8,128)(2,1)S(1)} %bitcast.17), channel_id=1, source_target_pairs={{0,2},{2,0},{1,3},{3,1},{4,6},{6,4},{5,7},{7,5},{8,10},{10,8},{9,1... | collective-permute-start | bytes 208904 | tf_op jit(solution)/shard_map/ppermute | solution.py:670
  30.6 15.2 %collective-permute-start.5 = (s16[2,128,128]{2,1,0:T(8,128)(2,1)S(1)}, s16[2,128,128]{2,1,0:T(8,128)(2,1)S(1)}, u32[]{:S(2)}, u32[]{:S(2)}) collective-permute-start(s16[2,128,128]{2,1,0:T(8,128)(2,1)S(1)} %get-tuple-element.34), channel_id=1, source_target_pairs={{0,4},{4,0},{8,12},{12,8},{1,5},{5,1},{9,13},{13,9},{2,6},{6,2},{1... | collective-permute-start | bytes 196616 | tf_op jit(solution)/shard_map/ppermute | solution.py:618
  30.6 15.2 %collective-permute-start.6 = (s16[2,128,128]{2,1,0:T(8,128)(2,1)S(1)}, s16[2,128,128]{2,1,0:T(8,128)(2,1)S(1)}, u32[]{:S(2)}, u32[]{:S(2)}) collective-permute-start(s16[2,128,128]{2,1,0:T(8,128)(2,1)S(1)} %get-tuple-element.36), channel_id=1, source_target_pairs={{0,8},{4,12},{8,0},{12,4},{1,9},{5,13},{9,1},{13,5},{2,10},{6,14},... | collective-permute-start | bytes 196616 | tf_op jit(solution)/shard_map/ppermute | solution.py:618
  33.7 4.4 %collective-permute-start.7 = (bf16[272,128]{1,0:T(8,128)(2,1)S(1)}, bf16[272,128]{1,0:T(8,128)(2,1)S(1)}, u32[]{:S(2)}, u32[]{:S(2)}) collective-permute-start(bf16[272,128]{1,0:T(8,128)(2,1)S(1)} %bitcast.19), channel_id=1, source_target_pairs={{0,2},{2,0},{1,3},{3,1},{4,6},{6,4},{5,7},{7,5},{8,10},{10,8},{9,1... | collective-permute-start | bytes 208904 | tf_op jit(solution)/shard_map/ppermute | solution.py:670
  35.3 4.4 %collective-permute-start.10 = (bf16[272,128]{1,0:T(8,128)(2,1)S(1)}, bf16[272,128]{1,0:T(8,128)(2,1)S(1)}, u32[]{:S(2)}, u32[]{:S(2)}) collective-permute-start(bf16[272,128]{1,0:T(8,128)(2,1)S(1)} %bitcast.18), channel_id=1, source_target_pairs={{0,2},{2,0},{1,3},{3,1},{4,6},{6,4},{5,7},{7,5},{8,10},{10,8},{9,1... | collective-permute-start | bytes 208904 | tf_op jit(solution)/shard_map/ppermute | solution.py:670
  36.1 3.6 %copy-start.6 = (bf16[96,96]{1,0:T(8,128)(2,1)S(1)}, bf16[96,96]{1,0:T(8,128)(2,1)}, u32[]{:S(2)}) copy-start(bf16[96,96]{1,0:T(8,128)(2,1)} %constant.80.clone.order) | copy-start | bytes 55300
  36.1 3.6 %copy-start.4 = (bf16[256,128]{1,0:T(8,128)(2,1)S(1)}, bf16[256,128]{1,0:T(8,128)(2,1)}, u32[]{:S(2)}) copy-start(bf16[256,128]{1,0:T(8,128)(2,1)} %constant.82.clone.rim_band) | copy-start | bytes 196612
  36.1 3.6 %copy-start.5 = (bf16[256,128]{1,0:T(8,128)(2,1)S(1)}, bf16[256,128]{1,0:T(8,128)(2,1)}, u32[]{:S(2)}) copy-start(bf16[256,128]{1,0:T(8,128)(2,1)} %constant.81.clone.band) | copy-start | bytes 196612
  38.1 7.8 %collective-permute-start.9 = (s16[2,128,128]{2,1,0:T(8,128)(2,1)S(1)}, s16[2,128,128]{2,1,0:T(8,128)(2,1)S(1)}, u32[]{:S(2)}, u32[]{:S(2)}) collective-permute-start(s16[2,128,128]{2,1,0:T(8,128)(2,1)S(1)} %get-tuple-element.38), channel_id=1, source_target_pairs={{0,12},{4,8},{8,4},{12,0},{1,13},{5,9},{9,5},{13,1},{2,14},{6,10},... | collective-permute-start | bytes 196616 | tf_op jit(solution)/shard_map/ppermute | solution.py:618
  47.3 1.9 %collective-permute-start.13 = (f32[8,128]{1,0:T(8,128)S(1)}, f32[8,128]{1,0:T(8,128)S(1)}, u32[]{:S(2)}, u32[]{:S(2)}) collective-permute-start(f32[8,128]{1,0:T(8,128)S(1)} %get-tuple-element.45.refs_3_), channel_id=1, source_target_pairs={{0,3},{1,0},{2,1},{3,2},{4,7},{5,4},{6,5},{7,6},{8,11},{9,8},{10,9... | collective-permute-start | bytes 12296 | tf_op jit(solution)/shard_map/ppermute | solution.py:752
  47.4 3.7 %collective-permute-start.12 = (f32[8,128]{1,0:T(8,128)S(1)}, f32[8,128]{1,0:T(8,128)S(1)}, u32[]{:S(2)}, u32[]{:S(2)}) collective-permute-start(f32[8,128]{1,0:T(8,128)S(1)} %get-tuple-element.45.refs_3_), channel_id=1, source_target_pairs={{0,2},{1,3},{2,0},{3,1},{4,6},{5,7},{6,4},{7,5},{8,10},{9,11},{10,... | collective-permute-start | bytes 12296 | tf_op jit(solution)/shard_map/ppermute | solution.py:752
  48.9 3.0 %collective-permute-start.11 = (f32[8,128]{1,0:T(8,128)S(1)}, f32[8,128]{1,0:T(8,128)S(1)}, u32[]{:S(2)}, u32[]{:S(2)}) collective-permute-start(f32[8,128]{1,0:T(8,128)S(1)} %get-tuple-element.45.refs_3_), channel_id=1, source_target_pairs={{0,1},{1,2},{2,3},{3,0},{4,5},{5,6},{6,7},{7,4},{8,9},{9,10},{10,1... | collective-permute-start | bytes 12296 | tf_op jit(solution)/shard_map/ppermute | solution.py:752
  52.0 7.1 %collective-permute-start.14 = (s16[176,128]{1,0:T(8,128)(2,1)S(1)}, s16[176,128]{1,0:T(8,128)(2,1)S(1)}, u32[]{:S(2)}, u32[]{:S(2)}) collective-permute-start(s16[176,128]{1,0:T(8,128)(2,1)S(1)} %get-tuple-element.47), channel_id=1, source_target_pairs={{0,4},{4,0},{8,12},{12,8},{1,5},{5,1},{9,13},{13,9},{2,6},{6,2},{1... | collective-permute-start | bytes 135176 | tf_op jit(solution)/shard_map/ppermute | solution.py:618
  55.3 5.3 %collective-permute-start.15 = (s16[176,128]{1,0:T(8,128)(2,1)S(1)}, s16[176,128]{1,0:T(8,128)(2,1)S(1)}, u32[]{:S(2)}, u32[]{:S(2)}) collective-permute-start(s16[176,128]{1,0:T(8,128)(2,1)S(1)} %get-tuple-element.48), channel_id=1, source_target_pairs={{0,8},{4,12},{8,0},{12,4},{1,9},{5,13},{9,1},{13,5},{2,10},{6,14},... | collective-permute-start | bytes 135176 | tf_op jit(solution)/shard_map/ppermute | solution.py:618
  57.1 5.9 %collective-permute-start.16 = (s16[176,128]{1,0:T(8,128)(2,1)S(1)}, s16[176,128]{1,0:T(8,128)(2,1)S(1)}, u32[]{:S(2)}, u32[]{:S(2)}) collective-permute-start(s16[176,128]{1,0:T(8,128)(2,1)S(1)} %get-tuple-element.49), channel_id=1, source_target_pairs={{0,12},{4,8},{8,4},{12,0},{1,13},{5,9},{9,5},{13,1},{2,14},{6,10},... | collective-permute-start | bytes 135176 | tf_op jit(solution)/shard_map/ppermute | solution.py:618

commit v22 on v20

--- a/solution.py
+++ b/solution.py
@@ -671,7 +671,11 @@
             return got, got
         return swapped(border(rows - HALO), border(0), "space")
 
-    block = [messages[0]] + [exchanged(messages[by], "epoch", by) for by in range(1, tiles)]
+    turns = list(range(2, tiles)) + [1]
+    halos = {0: halo([messages[0].reshape(-1, rows, LANES)])}
+    near = lax.optimization_barrier((messages[1], halos[0]))[0]
+    block = {by: exchanged(near if by == 1 else messages[by], "epoch", by) for by in turns}
+    block[0] = messages[0]
     estimate, direction, _ = lax.optimization_barrier((estimate, direction, messages))
     fields = pl.pallas_call(
         fields_kernel,
@@ -684,9 +688,11 @@
     def params_in(shift):
         return block[shift][tile_rows : tile_rows + epochs, PARAM_LANE : PARAM_LANE + 4 * SLOTS].astype(f32)
 
-    halos = [halo([array.reshape(-1, rows, LANES)]) for array in block]
-    late = lax.optimization_barrier((fields, block, halos[1:-1]))[0]
-    field = [fields[0]] + [exchanged(late[by], "epoch", by) for by in range(1, tiles)]
+    halos.update({by: halo([block[by].reshape(-1, rows, LANES)]) for by in turns})
+    late = lax.optimization_barrier((fields, block, [halos[by] for by in turns[:-2]]))[0]
+    field = {by: exchanged(late[by], "epoch", by) for by in range(1, tiles)}
+    field[0] = fields[0]
+    block, field = ([array[by] for by in range(tiles)] for array in (block, field))
 
     listed = jnp.concatenate([params_in(shift) for shift in range(tiles)], axis=0)
     place = jnp.arange(total, dtype=jnp.int32)[:, None]

time: 62.7 us -> 64.2 us (1.024)
  starting transfers between devices: 22.5 us -> 25.7 us
  waiting for transfers between devices: 24.5 us -> 22.4 us
    ppermute x9, starting transfers between devices: 15.6 us -> 18.1 us  [exchanged(): return lax.ppermute(x, axis, [(i, i ^ by) for i in range(size)])]
    ppermute x9, waiting for transfers between devices: 19.8 us -> 18.2 us  [exchanged(): return lax.ppermute(x, axis, [(i, i ^ by) for i in range(size)])]
    ppermute x3, starting transfers between devices: 0.83 us -> 1.78 us  [transposed_plan(): lax.ppermute(sums, place, [(i, (i + by) % count) for i in range(count)])]
where the time goes in v22:
time: 64.2 us; the launch traced here: 63.9 us
  starting transfers between devices  25.7 us (40%)
  waiting for transfers between devices  22.4 us (35%)
  Pallas kernels  10.2 us (16%)
  local copies, waits for them, and re-layouts  3.76 us (6%)
  between operations  1.45 us (2%)
    ppermute x9, waiting for transfers between devices, exchanged(): return lax.ppermute(x, axis, [(i, i ^ by) for i in range(size)])  18.2 us
    ppermute x9, starting transfers between devices, exchanged(): return lax.ppermute(x, axis, [(i, i ^ by) for i in range(size)])  18.1 us
    pallas_call x1, Pallas kernels, transposed_plan(): pl.pallas_call(functools.partial(pair_kernel, (epochs, rows, len(operands...  6.05 us
    ppermute x4, starting transfers between devices, halo(): lax.ppermute(border(jnp.where(space == 0, rows - HALO, 0)), 'space', [(0,...  5.31 us
    unnamed x20, local copies, waits for them, and re-layouts  3.2 us
    ppermute x3, waiting for transfers between devices, transposed_plan(): lax.ppermute(sums, place, [(i, (i + by) % count) for i in range(count)])  2.74 us
    ppermute x3, starting transfers between devices, transposed_plan(): lax.ppermute(sums, place, [(i, (i + by) % count) for i in range(count)])  1.78 us
    pallas_call x1, Pallas kernels, transposed_plan(): pl.pallas_call(functools.partial(gradient_kernel, (tiles, epochs)), out_s...  1.47 us
  transfers between devices with their start and end apart: 17, of which 7 were waited for; matrix products, arithmetic and copies ran while one was open for 2% of the time, Pallas kernels for 10%

profile of v22, /device:TPU:0, one launch (start us, length us, event | category | flops | bytes accessed | tf_op | source)
XLA Modules:
  0.0 63.9 jit_solution(4386395355781627415)
XLA Ops:
  0.6 1.2 %copy-done = bf16[2,8,64,512]{3,2,1,0:T(8,128)(2,1)S(1)} copy-done((bf16[2,8,64,512]{3,2,1,0:T(8,128)(2,1)S(1)}, bf16[2,8,64,512]{3,2,1,0:T(8,128)(2,1)}, u32[]{:S(2)}) %copy-start) | copy-done | bytes 1048600
  1.9 0.2 shard_map.104
  2.1 0.5 collective-permute-start
  2.6 0.7 %copy-done.7 = s32[8,4]{0,1:T(4,128)S(1)} copy-done((s32[8,4]{0,1:T(4,128)S(1)}, s32[8,4]{0,1:T(4,128)}, u32[]{:S(2)}) %copy-start.7) | copy-done | bytes 152
  3.3 0.1 copy.15
  3.4 0.7 %copy-done.8 = f32[8,4]{0,1:T(4,128)S(1)} copy-done((f32[8,4]{0,1:T(4,128)S(1)}, f32[8,4]{0,1:T(4,128)}, u32[]{:S(2)}) %copy-start.8) | copy-done | bytes 152
  4.1 0.1 copy.16
  4.1 0.1 select_maximum_fusion.params
  4.2 0.1 add_convert_fusion.present
  4.3 1.3 %shard_map.105 = (bf16[1088,128]{1,0:T(8,128)(2,1)S(1)}, bf16[1088,128]{1,0:T(8,128)(2,1)S(1)}, bf16[1088,128]{1,0:T(8,128)(2,1)S(1)}, bf16[1088,128]{1,0:T(8,128)(2,1)S(1)}) custom-call(s32[1]{0:T(128)} %bitcast.me, f32[2]{0:T(128)S(1)} %add_convert_fusion.present, bf16[2,8,64,512]{3,2,1,0:T(8,128)(2,1)S(1)} %copy-done.1, ...), custom_call_target="tpu_custom_call" | custom-call | flops 3000000 | bytes 4000000 | tf_op jit(solution)/shard_map/pallas_call | solution.py:651
  5.6 3.7 %collective-permute-start.3 = (bf16[1088,128]{1,0:T(8,128)(2,1)S(1)}, bf16[1088,128]{1,0:T(8,128)(2,1)S(1)}, u32[]{:S(2)}, u32[]{:S(2)}) collective-permute-start(bf16[1088,128]{1,0:T(8,128)(2,1)S(1)} %get-tuple-element.29), channel_id=1, source_target_pairs={{0,8},{4,12},{8,0},{12,4},{1,9},{5,13},{9,1},{13,5},{2,10},{6,14},... | collective-permute-start | bytes 835592 | tf_op jit(solution)/shard_map/ppermute | solution.py:618
  9.3 1.6 %collective-permute-start.1 = (bf16[272,128]{1,0:T(8,128)(2,1)S(1)}, bf16[272,128]{1,0:T(8,128)(2,1)S(1)}, u32[]{:S(2)}, u32[]{:S(2)}) collective-permute-start(bf16[272,128]{1,0:T(8,128)(2,1)S(1)} %bitcast.20), channel_id=1, source_target_pairs={{0,2},{2,0},{1,3},{3,1},{4,6},{6,4},{5,7},{7,5},{8,10},{10,8},{9,1... | collective-permute-start | bytes 208904 | tf_op jit(solution)/shard_map/ppermute | solution.py:670
  10.8 1.3 %collective-permute-start.4 = (bf16[1088,128]{1,0:T(8,128)(2,1)S(1)}, bf16[1088,128]{1,0:T(8,128)(2,1)S(1)}, u32[]{:S(2)}, u32[]{:S(2)}) collective-permute-start(bf16[1088,128]{1,0:T(8,128)(2,1)S(1)} %get-tuple-element.30), channel_id=1, source_target_pairs={{0,12},{4,8},{8,4},{12,0},{1,13},{5,9},{9,5},{13,1},{2,14},{6,10},... | collective-permute-start | bytes 835592 | tf_op jit(solution)/shard_map/ppermute | solution.py:618
  12.2 1.5 %collective-permute-done.1.refs_4_ = bf16[272,128]{1,0:T(8,128)(2,1)S(1)} collective-permute-done((bf16[272,128]{1,0:T(8,128)(2,1)S(1)}, bf16[272,128]{1,0:T(8,128)(2,1)S(1)}, u32[]{:S(2)}, u32[]{:S(2)}) %collective-permute-start.1) | collective-permute-done | bytes 69664 | tf_op jit(solution)/shard_map/ppermute | solution.py:670
  13.7 1.6 %collective-permute-start.2 = (bf16[1088,128]{1,0:T(8,128)(2,1)S(1)}, bf16[1088,128]{1,0:T(8,128)(2,1)S(1)}, u32[]{:S(2)}, u32[]{:S(2)}) collective-permute-start(bf16[1088,128]{1,0:T(8,128)(2,1)S(1)} %get-tuple-element.33), channel_id=1, source_target_pairs={{0,4},{4,0},{8,12},{12,8},{1,5},{5,1},{9,13},{13,9},{2,6},{6,2},{1... | collective-permute-start | bytes 835592 | tf_op jit(solution)/shard_map/ppermute | solution.py:618
  15.2 0.1 add_convert_fusion.1.present
  15.3 0.1 slice.27
  15.4 0.1 shard_map.106
  15.5 13.3 %collective-permute-done.3.refs_2_ = bf16[1088,128]{1,0:T(8,128)(2,1)S(1)} collective-permute-done((bf16[1088,128]{1,0:T(8,128)(2,1)S(1)}, bf16[1088,128]{1,0:T(8,128)(2,1)S(1)}, u32[]{:S(2)}, u32[]{:S(2)}) %collective-permute-start.3) | collective-permute-done | bytes 278560 | tf_op jit(solution)/shard_map/ppermute | solution.py:618
  28.8 1.8 %collective-permute-start.5 = (bf16[272,128]{1,0:T(8,128)(2,1)S(1)}, bf16[272,128]{1,0:T(8,128)(2,1)S(1)}, u32[]{:S(2)}, u32[]{:S(2)}) collective-permute-start(bf16[272,128]{1,0:T(8,128)(2,1)S(1)} %bitcast.19), channel_id=1, source_target_pairs={{0,2},{2,0},{1,3},{3,1},{4,6},{6,4},{5,7},{7,5},{8,10},{10,8},{9,1... | collective-permute-start | bytes 208904 | tf_op jit(solution)/shard_map/ppermute | solution.py:670
  30.6 0.4 collective-permute-start.10
  31.0 0.1 slice.37
  31.1 1.3 %collective-permute-done.2.refs_1_ = bf16[1088,128]{1,0:T(8,128)(2,1)S(1)} collective-permute-done((bf16[1088,128]{1,0:T(8,128)(2,1)S(1)}, bf16[1088,128]{1,0:T(8,128)(2,1)S(1)}, u32[]{:S(2)}, u32[]{:S(2)}) %collective-permute-start.2) | collective-permute-done | bytes 278560 | tf_op jit(solution)/shard_map/ppermute | solution.py:618
  32.4 1.6 %collective-permute-start.9 = (bf16[272,128]{1,0:T(8,128)(2,1)S(1)}, bf16[272,128]{1,0:T(8,128)(2,1)S(1)}, u32[]{:S(2)}, u32[]{:S(2)}) collective-permute-start(bf16[272,128]{1,0:T(8,128)(2,1)S(1)} %bitcast.18), channel_id=1, source_target_pairs={{0,2},{2,0},{1,3},{3,1},{4,6},{6,4},{5,7},{7,5},{8,10},{10,8},{9,1... | collective-permute-start | bytes 208904 | tf_op jit(solution)/shard_map/ppermute | solution.py:670
  34.0 3.7 %collective-permute-start.6 = (s16[2,128,128]{2,1,0:T(8,128)(2,1)S(1)}, s16[2,128,128]{2,1,0:T(8,128)(2,1)S(1)}, u32[]{:S(2)}, u32[]{:S(2)}) collective-permute-start(s16[2,128,128]{2,1,0:T(8,128)(2,1)S(1)} %get-tuple-element.38), channel_id=1, source_target_pairs={{0,4},{4,0},{8,12},{12,8},{1,5},{5,1},{9,13},{13,9},{2,6},{6,2},{1... | collective-permute-start | bytes 196616 | tf_op jit(solution)/shard_map/ppermute | solution.py:618
  37.6 1.9 %collective-permute-start.7 = (s16[2,128,128]{2,1,0:T(8,128)(2,1)S(1)}, s16[2,128,128]{2,1,0:T(8,128)(2,1)S(1)}, u32[]{:S(2)}, u32[]{:S(2)}) collective-permute-start(s16[2,128,128]{2,1,0:T(8,128)(2,1)S(1)} %get-tuple-element.39), channel_id=1, source_target_pairs={{0,8},{4,12},{8,0},{12,4},{1,9},{5,13},{9,1},{13,5},{2,10},{6,14},... | collective-permute-start | bytes 196616 | tf_op jit(solution)/shard_map/ppermute | solution.py:618
  39.5 1.5 %collective-permute-start.8 = (s16[2,128,128]{2,1,0:T(8,128)(2,1)S(1)}, s16[2,128,128]{2,1,0:T(8,128)(2,1)S(1)}, u32[]{:S(2)}, u32[]{:S(2)}) collective-permute-start(s16[2,128,128]{2,1,0:T(8,128)(2,1)S(1)} %get-tuple-element.40), channel_id=1, source_target_pairs={{0,12},{4,8},{8,4},{12,0},{1,13},{5,9},{9,5},{13,1},{2,14},{6,10},... | collective-permute-start | bytes 196616 | tf_op jit(solution)/shard_map/ppermute | solution.py:618
  41.0 0.1 slice.36
  41.1 0.1 fusion.5
  41.2 0.1 slice_add_fusion
  41.3 0.1 reshape.99.partner
  41.4 0.1 reshape.102.weight
  41.5 0.3 copy-done.6
  41.8 0.1 copy-done.4
  41.9 6.0 %shard_map.107 = (f32[128,16,128]{2,1,0:T(8,128)S(1)}, f32[128,16,128]{2,1,0:T(8,128)S(1)}) custom-call(s32[128]{0:T(128)S(1)} %reshape.99.partner, f32[128]{0:T(128)S(1)} %reshape.102.weight, f32[2]{0:T(128)S(1)} %add_convert_fusion.1.present, bf16[96,96]{1,0:T(8,128)(2,1)S(1)} %copy-done.6, bf16[256,128]{1,0:T(8,128)(2,1)S(1)} %copy-done.5, ...), custom_call_target="tpu_custom_call" | custom-call | flops 20000000 | bytes 30000000 | tf_op jit(solution)/shard_map/pallas_call | solution.py:719
  48.0 1.5 %shard_map.108 = (f32[32,16,128]{2,1,0:T(8,128)S(1)}, f32[8,128]{1,0:T(8,128)S(1)}) custom-call(s32[128]{0:T(128)S(1)} %reshape.99.partner, s16[2,128,128]{2,1,0:T(8,128)(2,1)S(1)} %get-tuple-element.34.refs_0_, s16[2,128,128]{2,1,0:T(8,128)(2,1)S(1)} %collective-permute-done.6.refs_1_, s16[2,128,128]{2,1,0:T(8,128)(2,1)S(1)} %collective-permute-done.7.refs_2_, ...), custom_call_target="tpu_custom_call" | custom-call | flops 10000000 | bytes 8000000 | tf_op jit(solution)/shard_map/pallas_call | solution.py:735
  49.5 0.1 collective-permute-start.13
  49.6 1.5 %collective-permute-start.12 = (f32[8,128]{1,0:T(8,128)S(1)}, f32[8,128]{1,0:T(8,128)S(1)}, u32[]{:S(2)}, u32[]{:S(2)}) collective-permute-start(f32[8,128]{1,0:T(8,128)S(1)} %get-tuple-element.47.refs_3_), channel_id=1, source_target_pairs={{0,2},{1,3},{2,0},{3,1},{4,6},{5,7},{6,4},{7,5},{8,10},{9,11},{10,... | collective-permute-start | bytes 12296 | tf_op jit(solution)/shard_map/ppermute | solution.py:751
  51.1 0.2 collective-permute-start.11
  51.3 0.1 shard_map.109
  51.4 1.8 %collective-permute-done.12.refs_5_ = f32[8,128]{1,0:T(8,128)S(1)} collective-permute-done((f32[8,128]{1,0:T(8,128)S(1)}, f32[8,128]{1,0:T(8,128)S(1)}, u32[]{:S(2)}, u32[]{:S(2)}) %collective-permute-start.12) | collective-permute-done | bytes 4128 | tf_op jit(solution)/shard_map/ppermute | solution.py:751
  53.2 0.9 %collective-permute-done.11.refs_4_ = f32[8,128]{1,0:T(8,128)S(1)} collective-permute-done((f32[8,128]{1,0:T(8,128)S(1)}, f32[8,128]{1,0:T(8,128)S(1)}, u32[]{:S(2)}, u32[]{:S(2)}) %collective-permute-start.11) | collective-permute-done | bytes 4128 | tf_op jit(solution)/shard_map/ppermute | solution.py:751
  54.2 0.6 collective-permute-start.14
  54.8 2.4 %collective-permute-start.15 = (s16[176,128]{1,0:T(8,128)(2,1)S(1)}, s16[176,128]{1,0:T(8,128)(2,1)S(1)}, u32[]{:S(2)}, u32[]{:S(2)}) collective-permute-start(s16[176,128]{1,0:T(8,128)(2,1)S(1)} %get-tuple-element.50), channel_id=1, source_target_pairs={{0,8},{4,12},{8,0},{12,4},{1,9},{5,13},{9,1},{13,5},{2,10},{6,14},... | collective-permute-start | bytes 135176 | tf_op jit(solution)/shard_map/ppermute | solution.py:618
  57.2 1.5 %collective-permute-start.16 = (s16[176,128]{1,0:T(8,128)(2,1)S(1)}, s16[176,128]{1,0:T(8,128)(2,1)S(1)}, u32[]{:S(2)}, u32[]{:S(2)}) collective-permute-start(s16[176,128]{1,0:T(8,128)(2,1)S(1)} %get-tuple-element.51), channel_id=1, source_target_pairs={{0,12},{4,8},{8,4},{12,0},{1,13},{5,9},{9,5},{13,1},{2,14},{6,10},... | collective-permute-start | bytes 135176 | tf_op jit(solution)/shard_map/ppermute | solution.py:618
  59.3 0.8 %collective-permute-done.15.refs_1_ = s16[176,128]{1,0:T(8,128)(2,1)S(1)} collective-permute-done((s16[176,128]{1,0:T(8,128)(2,1)S(1)}, s16[176,128]{1,0:T(8,128)(2,1)S(1)}, u32[]{:S(2)}, u32[]{:S(2)}) %collective-permute-start.15) | collective-permute-done | bytes 45088 | tf_op jit(solution)/shard_map/ppermute | solution.py:618
  60.1 2.9 %collective-permute-done.16.refs_2_ = s16[176,128]{1,0:T(8,128)(2,1)S(1)} collective-permute-done((s16[176,128]{1,0:T(8,128)(2,1)S(1)}, s16[176,128]{1,0:T(8,128)(2,1)S(1)}, u32[]{:S(2)}, u32[]{:S(2)}) %collective-permute-start.16) | collective-permute-done | bytes 45088 | tf_op jit(solution)/shard_map/ppermute | solution.py:618
  63.0 0.9 %shard_map.111 = (f32[8,16,512]{2,1,0:T(8,128)}, f32[8,16,512]{2,1,0:T(8,128)}) custom-call(s32[1]{0:T(128)} %bitcast.me, f32[1]{0:T(128)S(6)} %copy.19.prev_mean, f32[8,16,512]{2,1,0:T(8,128)S(1)} %copy-done.2, f32[8,16,512]{2,1,0:T(8,128)S(1)} %copy-done.3, f32[8,16,128]{2,1,0:T(8,128)S(1)} %slice.35.gradient, f32[8,128]{1,0:T(8,128)S(1)} %get-tuple-element.48.sums, ...), custom_call_target="tpu_custom_call" | custom-call | flops 1000000 | bytes 2000000 | tf_op jit(solution)/shard_map/pallas_call | solution.py:772
  (33 shorter events, 0.3 us)
Async XLA Ops:
  0.6 1.2 %copy-start = (bf16[2,8,64,512]{3,2,1,0:T(8,128)(2,1)S(1)}, bf16[2,8,64,512]{3,2,1,0:T(8,128)(2,1)}, u32[]{:S(2)}) copy-start(bf16[2,8,64,512]{3,2,1,0:T(8,128)(2,1)} %slc.1) | copy-start | bytes 3145732
  1.9 2.4 %copy-start.1 = (bf16[2,8,64,512]{3,2,1,0:T(8,128)(2,1)S(1)}, bf16[2,8,64,512]{3,2,1,0:T(8,128)(2,1)}, u32[]{:S(2)}) copy-start(bf16[2,8,64,512]{3,2,1,0:T(8,128)(2,1)} %slc.1) | copy-start | bytes 3145732
  2.1 2.2 %collective-permute-start = (bf16[64,128]{1,0:T(8,128)(2,1)S(1)}, bf16[64,128]{1,0:T(8,128)(2,1)S(1)}, u32[]{:S(2)}, u32[]{:S(2)}) collective-permute-start(bf16[64,128]{1,0:T(8,128)(2,1)S(1)} %shard_map.104), channel_id=1, source_target_pairs={{0,1},{1,0},{2,3},{3,2},{4,5},{5,4},{6,7},{7,6},{8,9},{9,8},{10,11... | collective-permute-start | bytes 49160 | tf_op jit(solution)/shard_map/ppermute | solution.py:609
  2.6 0.7 %copy-start.7 = (s32[8,4]{0,1:T(4,128)S(1)}, s32[8,4]{0,1:T(4,128)}, u32[]{:S(2)}) copy-start(s32[8,4]{0,1:T(4,128)} %param.10) | copy-start | bytes 388
  3.4 0.7 %copy-start.8 = (f32[8,4]{0,1:T(4,128)S(1)}, f32[8,4]{0,1:T(4,128)}, u32[]{:S(2)}) copy-start(f32[8,4]{0,1:T(4,128)} %param.11) | copy-start | bytes 388
  4.3 11.1 %copy-start.2 = (f32[8,16,512]{2,1,0:T(8,128)S(1)}, f32[8,16,512]{2,1,0:T(8,128)}, u32[]{:S(2)}) copy-start(f32[8,16,512]{2,1,0:T(8,128)} %estimate.1) | copy-start | bytes 786436
  4.3 11.1 %copy-start.3 = (f32[8,16,512]{2,1,0:T(8,128)S(1)}, f32[8,16,512]{2,1,0:T(8,128)}, u32[]{:S(2)}) copy-start(f32[8,16,512]{2,1,0:T(8,128)} %direction.1) | copy-start | bytes 786436
  5.6 23.2 %collective-permute-start.3 = (bf16[1088,128]{1,0:T(8,128)(2,1)S(1)}, bf16[1088,128]{1,0:T(8,128)(2,1)S(1)}, u32[]{:S(2)}, u32[]{:S(2)}) collective-permute-start(bf16[1088,128]{1,0:T(8,128)(2,1)S(1)} %get-tuple-element.29), channel_id=1, source_target_pairs={{0,8},{4,12},{8,0},{12,4},{1,9},{5,13},{9,1},{13,5},{2,10},{6,14},... | collective-permute-start | bytes 835592 | tf_op jit(solution)/shard_map/ppermute | solution.py:618
  9.3 4.4 %collective-permute-start.1 = (bf16[272,128]{1,0:T(8,128)(2,1)S(1)}, bf16[272,128]{1,0:T(8,128)(2,1)S(1)}, u32[]{:S(2)}, u32[]{:S(2)}) collective-permute-start(bf16[272,128]{1,0:T(8,128)(2,1)S(1)} %bitcast.20), channel_id=1, source_target_pairs={{0,2},{2,0},{1,3},{3,1},{4,6},{6,4},{5,7},{7,5},{8,10},{10,8},{9,1... | collective-permute-start | bytes 208904 | tf_op jit(solution)/shard_map/ppermute | solution.py:670
  10.8 19.7 %collective-permute-start.4 = (bf16[1088,128]{1,0:T(8,128)(2,1)S(1)}, bf16[1088,128]{1,0:T(8,128)(2,1)S(1)}, u32[]{:S(2)}, u32[]{:S(2)}) collective-permute-start(bf16[1088,128]{1,0:T(8,128)(2,1)S(1)} %get-tuple-element.30), channel_id=1, source_target_pairs={{0,12},{4,8},{8,4},{12,0},{1,13},{5,9},{9,5},{13,1},{2,14},{6,10},... | collective-permute-start | bytes 835592 | tf_op jit(solution)/shard_map/ppermute | solution.py:618
  13.7 18.7 %collective-permute-start.2 = (bf16[1088,128]{1,0:T(8,128)(2,1)S(1)}, bf16[1088,128]{1,0:T(8,128)(2,1)S(1)}, u32[]{:S(2)}, u32[]{:S(2)}) collective-permute-start(bf16[1088,128]{1,0:T(8,128)(2,1)S(1)} %get-tuple-element.33), channel_id=1, source_target_pairs={{0,4},{4,0},{8,12},{12,8},{1,5},{5,1},{9,13},{13,9},{2,6},{6,2},{1... | collective-permute-start | bytes 835592 | tf_op jit(solution)/shard_map/ppermute | solution.py:618
  28.8 5.2 %collective-permute-start.5 = (bf16[272,128]{1,0:T(8,128)(2,1)S(1)}, bf16[272,128]{1,0:T(8,128)(2,1)S(1)}, u32[]{:S(2)}, u32[]{:S(2)}) collective-permute-start(bf16[272,128]{1,0:T(8,128)(2,1)S(1)} %bitcast.19), channel_id=1, source_target_pairs={{0,2},{2,0},{1,3},{3,1},{4,6},{6,4},{5,7},{7,5},{8,10},{10,8},{9,1... | collective-permute-start | bytes 208904 | tf_op jit(solution)/shard_map/ppermute | solution.py:670
  30.6 10.9 %collective-permute-start.10 = (bf16[272,128]{1,0:T(8,128)(2,1)S(1)}, bf16[272,128]{1,0:T(8,128)(2,1)S(1)}, u32[]{:S(2)}, u32[]{:S(2)}) collective-permute-start(bf16[272,128]{1,0:T(8,128)(2,1)S(1)} %bitcast.17), channel_id=1, source_target_pairs={{0,2},{2,0},{1,3},{3,1},{4,6},{6,4},{5,7},{7,5},{8,10},{10,8},{9,1... | collective-permute-start | bytes 208904 | tf_op jit(solution)/shard_map/ppermute | solution.py:670
  32.4 9.1 %collective-permute-start.9 = (bf16[272,128]{1,0:T(8,128)(2,1)S(1)}, bf16[272,128]{1,0:T(8,128)(2,1)S(1)}, u32[]{:S(2)}, u32[]{:S(2)}) collective-permute-start(bf16[272,128]{1,0:T(8,128)(2,1)S(1)} %bitcast.18), channel_id=1, source_target_pairs={{0,2},{2,0},{1,3},{3,1},{4,6},{6,4},{5,7},{7,5},{8,10},{10,8},{9,1... | collective-permute-start | bytes 208904 | tf_op jit(solution)/shard_map/ppermute | solution.py:670
  34.0 14.0 %collective-permute-start.6 = (s16[2,128,128]{2,1,0:T(8,128)(2,1)S(1)}, s16[2,128,128]{2,1,0:T(8,128)(2,1)S(1)}, u32[]{:S(2)}, u32[]{:S(2)}) collective-permute-start(s16[2,128,128]{2,1,0:T(8,128)(2,1)S(1)} %get-tuple-element.38), channel_id=1, source_target_pairs={{0,4},{4,0},{8,12},{12,8},{1,5},{5,1},{9,13},{13,9},{2,6},{6,2},{1... | collective-permute-start | bytes 196616 | tf_op jit(solution)/shard_map/ppermute | solution.py:618
  37.6 10.4 %collective-permute-start.7 = (s16[2,128,128]{2,1,0:T(8,128)(2,1)S(1)}, s16[2,128,128]{2,1,0:T(8,128)(2,1)S(1)}, u32[]{:S(2)}, u32[]{:S(2)}) collective-permute-start(s16[2,128,128]{2,1,0:T(8,128)(2,1)S(1)} %get-tuple-element.39), channel_id=1, source_target_pairs={{0,8},{4,12},{8,0},{12,4},{1,9},{5,13},{9,1},{13,5},{2,10},{6,14},... | collective-permute-start | bytes 196616 | tf_op jit(solution)/shard_map/ppermute | solution.py:618
  39.5 8.5 %collective-permute-start.8 = (s16[2,128,128]{2,1,0:T(8,128)(2,1)S(1)}, s16[2,128,128]{2,1,0:T(8,128)(2,1)S(1)}, u32[]{:S(2)}, u32[]{:S(2)}) collective-permute-start(s16[2,128,128]{2,1,0:T(8,128)(2,1)S(1)} %get-tuple-element.40), channel_id=1, source_target_pairs={{0,12},{4,8},{8,4},{12,0},{1,13},{5,9},{9,5},{13,1},{2,14},{6,10},... | collective-permute-start | bytes 196616 | tf_op jit(solution)/shard_map/ppermute | solution.py:618
  41.1 0.7 %copy-start.6 = (bf16[96,96]{1,0:T(8,128)(2,1)S(1)}, bf16[96,96]{1,0:T(8,128)(2,1)}, u32[]{:S(2)}) copy-start(bf16[96,96]{1,0:T(8,128)(2,1)} %constant.80.clone.order) | copy-start | bytes 55300
  41.1 0.8 %copy-start.4 = (bf16[256,128]{1,0:T(8,128)(2,1)S(1)}, bf16[256,128]{1,0:T(8,128)(2,1)}, u32[]{:S(2)}) copy-start(bf16[256,128]{1,0:T(8,128)(2,1)} %constant.82.clone.rim_band) | copy-start | bytes 196612
  41.1 0.9 %copy-start.5 = (bf16[256,128]{1,0:T(8,128)(2,1)S(1)}, bf16[256,128]{1,0:T(8,128)(2,1)}, u32[]{:S(2)}) copy-start(bf16[256,128]{1,0:T(8,128)(2,1)} %constant.81.clone.band) | copy-start | bytes 196612
  49.5 1.9 %collective-permute-start.13 = (f32[8,128]{1,0:T(8,128)S(1)}, f32[8,128]{1,0:T(8,128)S(1)}, u32[]{:S(2)}, u32[]{:S(2)}) collective-permute-start(f32[8,128]{1,0:T(8,128)S(1)} %get-tuple-element.47.refs_3_), channel_id=1, source_target_pairs={{0,3},{1,0},{2,1},{3,2},{4,7},{5,4},{6,5},{7,6},{8,11},{9,8},{10,9... | collective-permute-start | bytes 12296 | tf_op jit(solution)/shard_map/ppermute | solution.py:751
  49.6 3.6 %collective-permute-start.12 = (f32[8,128]{1,0:T(8,128)S(1)}, f32[8,128]{1,0:T(8,128)S(1)}, u32[]{:S(2)}, u32[]{:S(2)}) collective-permute-start(f32[8,128]{1,0:T(8,128)S(1)} %get-tuple-element.47.refs_3_), channel_id=1, source_target_pairs={{0,2},{1,3},{2,0},{3,1},{4,6},{5,7},{6,4},{7,5},{8,10},{9,11},{10,... | collective-permute-start | bytes 12296 | tf_op jit(solution)/shard_map/ppermute | solution.py:751
  51.1 3.0 %collective-permute-start.11 = (f32[8,128]{1,0:T(8,128)S(1)}, f32[8,128]{1,0:T(8,128)S(1)}, u32[]{:S(2)}, u32[]{:S(2)}) collective-permute-start(f32[8,128]{1,0:T(8,128)S(1)} %get-tuple-element.47.refs_3_), channel_id=1, source_target_pairs={{0,1},{1,2},{2,3},{3,0},{4,5},{5,6},{6,7},{7,4},{8,9},{9,10},{10,1... | collective-permute-start | bytes 12296 | tf_op jit(solution)/shard_map/ppermute | solution.py:751
  54.2 5.1 %collective-permute-start.14 = (s16[176,128]{1,0:T(8,128)(2,1)S(1)}, s16[176,128]{1,0:T(8,128)(2,1)S(1)}, u32[]{:S(2)}, u32[]{:S(2)}) collective-permute-start(s16[176,128]{1,0:T(8,128)(2,1)S(1)} %get-tuple-element.49), channel_id=1, source_target_pairs={{0,4},{4,0},{8,12},{12,8},{1,5},{5,1},{9,13},{13,9},{2,6},{6,2},{1... | collective-permute-start | bytes 135176 | tf_op jit(solution)/shard_map/ppermute | solution.py:618
  54.8 5.3 %collective-permute-start.15 = (s16[176,128]{1,0:T(8,128)(2,1)S(1)}, s16[176,128]{1,0:T(8,128)(2,1)S(1)}, u32[]{:S(2)}, u32[]{:S(2)}) collective-permute-start(s16[176,128]{1,0:T(8,128)(2,1)S(1)} %get-tuple-element.50), channel_id=1, source_target_pairs={{0,8},{4,12},{8,0},{12,4},{1,9},{5,13},{9,1},{13,5},{2,10},{6,14},... | collective-permute-start | bytes 135176 | tf_op jit(solution)/shard_map/ppermute | solution.py:618
  57.2 5.8 %collective-permute-start.16 = (s16[176,128]{1,0:T(8,128)(2,1)S(1)}, s16[176,128]{1,0:T(8,128)(2,1)S(1)}, u32[]{:S(2)}, u32[]{:S(2)}) collective-permute-start(s16[176,128]{1,0:T(8,128)(2,1)S(1)} %get-tuple-element.51), channel_id=1, source_target_pairs={{0,12},{4,8},{8,4},{12,0},{1,13},{5,9},{9,5},{13,1},{2,14},{6,10},... | collective-permute-start | bytes 135176 | tf_op jit(solution)/shard_map/ppermute | solution.py:618

commit v23 on v20

--- a/solution.py
+++ b/solution.py
@@ -548,35 +548,16 @@
         out[epochs * look_rows :, :] = whole(jnp.concatenate(powers, axis=0))
 
 
-def return_kernel(tiles, *refs):
-    coded, shared = refs[: tiles - 1], refs[tiles - 1 : -tiles]
-    own, pieces = refs[-tiles], refs[1 - tiles :]
-    total = shared[0][...]
-    for other in shared[1:]:
-        total = total + other[...]
-    own[...] = total
-    power = exponent_of(jnp.abs(total))
-    share = total * jnp.exp2(-power) * float(1 << 14)
-    high = jnp.floor(share + 0.5)
-    low = (share - high) * float(1 << 15)
-    parts = whole(jnp.concatenate([power, high, low, jnp.zeros_like(power)], axis=0))
-    for piece, source in zip(pieces, coded):
-        piece[: source.shape[0], :] = source[...]
-        piece[source.shape[0] :, :] = parts
-
-
-def update_kernel(cell_count, me, prev_mean, estimate, direction, gradient, sums, *refs):
-    pieces = refs[:-2]
+def update_kernel(cell_count, me, prev_mean, estimate, direction, gradient, *refs):
     new_estimate, new_direction = refs[-2:]
-    tiles = len(pieces) + 1
+    tiles = estimate.shape[2] // LANES
+    pieces, scalars = refs[: tiles - 1], refs[tiles - 1 : -2]
     epochs = estimate.shape[0]
     look_rows = estimate.shape[1]
     coded_rows = epochs * look_rows + HALO
-    total = sums[...]
-    for piece in pieces:
-        parts = number_of(piece[coded_rows:, :])
-        value = (parts[8:16] + parts[16:24] * (1.0 / (1 << 15))) * (1.0 / (1 << 14))
-        total = total + value * jnp.exp2(parts[:8])
+    total = scalars[0][...]
+    for other in scalars[1:]:
+        total = total + other[...]
     total = jnp.sum(total, axis=1, keepdims=True)
     grad_norm, crossed, grad_term, mixed, old_term = (total[at : at + 1, :] for at in range(5))
     momentum = grad_norm / cell_count / prev_mean[0]
@@ -752,25 +733,18 @@
         compiler_params=params_of,
         cost_estimate=pl.CostEstimate(flops=1_000_000, bytes_accessed=1_000_000, transcendentals=0),
     )(gradient)
-    piece_shape = jax.ShapeDtypeStruct((epochs * look_rows + HALO + 32, LANES), jnp.int16)
-    own_sums, *pieces = pl.pallas_call(
-        functools.partial(return_kernel, tiles),
-        out_shape=(jax.ShapeDtypeStruct((8, LANES), f32),) + (piece_shape,) * (tiles - 1),
-        in_specs=[VMEM] * (tiles - 1 + count),
-        out_specs=(VMEM,) * tiles,
-        compiler_params=params_of,
-        cost_estimate=pl.CostEstimate(flops=10_000, bytes_accessed=1_000_000, transcendentals=0),
-    )(*coded, *shared)
-    returned = [exchanged(piece, "epoch", by + 1) for by, piece in enumerate(pieces)]
+    returned = [exchanged(piece, "epoch", by + 1) for by, piece in enumerate(coded)]
+    here = lax.optimization_barrier((sum(shared[1:], shared[0]), returned[0]))[0]
+    scalars = [here] + [exchanged(here, "epoch", by) for by in range(1, tiles)]
     cell_count = float(total * look_rows * spaces * columns * lax.axis_size("sub"))
     return pl.pallas_call(
         functools.partial(update_kernel, cell_count),
         out_shape=(jax.ShapeDtypeStruct(estimate.shape, f32),) * 2,
-        in_specs=[SMEM] * 2 + [VMEM] * (3 + tiles),
+        in_specs=[SMEM] * 2 + [VMEM] * (2 + 2 * tiles),
         out_specs=(VMEM, VMEM),
         compiler_params=params_of,
         cost_estimate=pl.CostEstimate(flops=1_000_000, bytes_accessed=2_000_000, transcendentals=0),
-    )(me.reshape(1), prev_mean, estimate, direction, gradient[:epochs], own_sums, *returned)
+    )(me.reshape(1), prev_mean, estimate, direction, gradient[:epochs], *returned, *scalars)
 
 
 def on_device(slc, offsets, weights, estimate, direction, prev_mean):

time: 62.7 us -> 62.4 us (level)
  waiting for transfers between devices: 24.5 us -> 19.8 us
  starting transfers between devices: 22.5 us -> 27 us
    ppermute x9 -> x12, starting transfers between devices: 15.6 us -> 20.1 us  [exchanged(): return lax.ppermute(x, axis, [(i, i ^ by) for i in range(size)])]
    ppermute x3, waiting for transfers between devices: 2.8 us -> 0.01 us  [transposed_plan(): lax.ppermute(sums, place, [(i, (i + by) % count) for i in range(count)])]
    ppermute x9 -> x12, waiting for transfers between devices: 19.8 us -> 17.9 us  [exchanged(): return lax.ppermute(x, axis, [(i, i ^ by) for i in range(size)])]
  transfers between devices with their start and end apart: 17 -> 20, of which waited for: 7 -> 5; matrix products, arithmetic and copies ran while one was open for 2% -> 2% of each run, Pallas kernels for 10% -> 10%
where the time goes in v23:
time: 62.4 us; the launch traced here: 62.2 us
  starting transfers between devices  27 us (43%)
  waiting for transfers between devices  19.8 us (32%)
  Pallas kernels  10.2 us (16%)
  local copies, waits for them, and re-layouts  3.32 us (5%)
  between operations  1.51 us (2%)
    ppermute x12, starting transfers between devices, exchanged(): return lax.ppermute(x, axis, [(i, i ^ by) for i in range(size)])  20.1 us
    ppermute x12, waiting for transfers between devices, exchanged(): return lax.ppermute(x, axis, [(i, i ^ by) for i in range(size)])  17.9 us
    pallas_call x1, Pallas kernels, transposed_plan(): pl.pallas_call(functools.partial(pair_kernel, (epochs, rows, len(operands...  6.05 us
    ppermute x4, starting transfers between devices, halo(): lax.ppermute(border(jnp.where(space == 0, rows - HALO, 0)), 'space', [(0,...  5.55 us
    unnamed x20, local copies, waits for them, and re-layouts  2.76 us
    ppermute x4, waiting for transfers between devices, halo(): lax.ppermute(border(jnp.where(space == 0, rows - HALO, 0)), 'space', [(0,...  1.85 us
    pallas_call x1, Pallas kernels, transposed_plan(): pl.pallas_call(functools.partial(gradient_kernel, (tiles, epochs)), out_s...  1.46 us
    pallas_call x1, Pallas kernels, transposed_plan(): pl.pallas_call(pack_kernel, out_shape=(jax.ShapeDtypeStruct((tile_rows +...  1.26 us
  transfers between devices with their start and end apart: 20, of which 5 were waited for; matrix products, arithmetic and copies ran while one was open for 2% of the time, Pallas kernels for 10%

profile of v23, /device:TPU:0, one launch (start us, length us, event | category | flops | bytes accessed | tf_op | source)
XLA Modules:
  0.0 62.2 jit_solution(12748001113009529045)
XLA Ops:
  0.6 1.2 %copy-done = bf16[2,8,64,512]{3,2,1,0:T(8,128)(2,1)S(1)} copy-done((bf16[2,8,64,512]{3,2,1,0:T(8,128)(2,1)S(1)}, bf16[2,8,64,512]{3,2,1,0:T(8,128)(2,1)}, u32[]{:S(2)}) %copy-start) | copy-done | bytes 1048600
  1.9 0.2 shard_map.104
  2.1 0.5 collective-permute-start
  2.6 0.7 %copy-done.7 = s32[8,4]{0,1:T(4,128)S(1)} copy-done((s32[8,4]{0,1:T(4,128)S(1)}, s32[8,4]{0,1:T(4,128)}, u32[]{:S(2)}) %copy-start.7) | copy-done | bytes 152
  3.3 0.1 copy.15
  3.4 0.7 %copy-done.8 = f32[8,4]{0,1:T(4,128)S(1)} copy-done((f32[8,4]{0,1:T(4,128)S(1)}, f32[8,4]{0,1:T(4,128)}, u32[]{:S(2)}) %copy-start.8) | copy-done | bytes 152
  4.1 0.1 copy.16
  4.1 0.1 select_maximum_fusion.params
  4.2 0.1 add_convert_fusion.present
  4.3 1.3 %shard_map.105 = (bf16[1088,128]{1,0:T(8,128)(2,1)S(1)}, bf16[1088,128]{1,0:T(8,128)(2,1)S(1)}, bf16[1088,128]{1,0:T(8,128)(2,1)S(1)}, bf16[1088,128]{1,0:T(8,128)(2,1)S(1)}) custom-call(s32[1]{0:T(128)} %bitcast.me, f32[2]{0:T(128)S(1)} %add_convert_fusion.present, bf16[2,8,64,512]{3,2,1,0:T(8,128)(2,1)S(1)} %copy-done.1, ...), custom_call_target="tpu_custom_call" | custom-call | flops 3000000 | bytes 4000000 | tf_op jit(solution)/shard_map/pallas_call | solution.py:632
  5.6 2.7 %collective-permute-start.1 = (bf16[1088,128]{1,0:T(8,128)(2,1)S(1)}, bf16[1088,128]{1,0:T(8,128)(2,1)S(1)}, u32[]{:S(2)}, u32[]{:S(2)}) collective-permute-start(bf16[1088,128]{1,0:T(8,128)(2,1)S(1)} %get-tuple-element.24), channel_id=1, source_target_pairs={{0,4},{4,0},{8,12},{12,8},{1,5},{5,1},{9,13},{13,9},{2,6},{6,2},{1... | collective-permute-start | bytes 835592 | tf_op jit(solution)/shard_map/ppermute | solution.py:599
  8.3 2.6 %collective-permute-start.2 = (bf16[1088,128]{1,0:T(8,128)(2,1)S(1)}, bf16[1088,128]{1,0:T(8,128)(2,1)S(1)}, u32[]{:S(2)}, u32[]{:S(2)}) collective-permute-start(bf16[1088,128]{1,0:T(8,128)(2,1)S(1)} %get-tuple-element.25), channel_id=1, source_target_pairs={{0,8},{4,12},{8,0},{12,4},{1,9},{5,13},{9,1},{13,5},{2,10},{6,14},... | collective-permute-start | bytes 835592 | tf_op jit(solution)/shard_map/ppermute | solution.py:599
  10.9 0.1 add_convert_fusion.1.present
  10.9 0.0 collective-permute-start.3
  11.0 0.1 slice.27
  11.0 1.7 %collective-permute-start.9 = (bf16[272,128]{1,0:T(8,128)(2,1)S(1)}, bf16[272,128]{1,0:T(8,128)(2,1)S(1)}, u32[]{:S(2)}, u32[]{:S(2)}) collective-permute-start(bf16[272,128]{1,0:T(8,128)(2,1)S(1)} %bitcast.17), channel_id=1, source_target_pairs={{0,2},{2,0},{1,3},{3,1},{4,6},{6,4},{5,7},{7,5},{8,10},{10,8},{9,1... | collective-permute-start | bytes 208904 | tf_op jit(solution)/shard_map/ppermute | solution.py:651
  12.7 0.1 shard_map.106
  12.9 8.3 %collective-permute-done.1.refs_1_ = bf16[1088,128]{1,0:T(8,128)(2,1)S(1)} collective-permute-done((bf16[1088,128]{1,0:T(8,128)(2,1)S(1)}, bf16[1088,128]{1,0:T(8,128)(2,1)S(1)}, u32[]{:S(2)}, u32[]{:S(2)}) %collective-permute-start.1) | collective-permute-done | bytes 278560 | tf_op jit(solution)/shard_map/ppermute | solution.py:599
  21.1 1.7 %collective-permute-start.4 = (bf16[272,128]{1,0:T(8,128)(2,1)S(1)}, bf16[272,128]{1,0:T(8,128)(2,1)S(1)}, u32[]{:S(2)}, u32[]{:S(2)}) collective-permute-start(bf16[272,128]{1,0:T(8,128)(2,1)S(1)} %bitcast.19), channel_id=1, source_target_pairs={{0,2},{2,0},{1,3},{3,1},{4,6},{6,4},{5,7},{7,5},{8,10},{10,8},{9,1... | collective-permute-start | bytes 208904 | tf_op jit(solution)/shard_map/ppermute | solution.py:651
  22.8 7.8 %collective-permute-done.2.refs_2_ = bf16[1088,128]{1,0:T(8,128)(2,1)S(1)} collective-permute-done((bf16[1088,128]{1,0:T(8,128)(2,1)S(1)}, bf16[1088,128]{1,0:T(8,128)(2,1)S(1)}, u32[]{:S(2)}, u32[]{:S(2)}) %collective-permute-start.2) | collective-permute-done | bytes 278560 | tf_op jit(solution)/shard_map/ppermute | solution.py:599
  30.6 1.6 %collective-permute-start.5 = (bf16[272,128]{1,0:T(8,128)(2,1)S(1)}, bf16[272,128]{1,0:T(8,128)(2,1)S(1)}, u32[]{:S(2)}, u32[]{:S(2)}) collective-permute-start(bf16[272,128]{1,0:T(8,128)(2,1)S(1)} %bitcast.20), channel_id=1, source_target_pairs={{0,2},{2,0},{1,3},{3,1},{4,6},{6,4},{5,7},{7,5},{8,10},{10,8},{9,1... | collective-permute-start | bytes 208904 | tf_op jit(solution)/shard_map/ppermute | solution.py:651
  32.2 0.6 collective-permute-start.10
  32.8 0.1 slice.36
  32.9 0.1 slice.37
  33.0 0.1 slice.38
  33.1 0.0 copy-start.5
  33.1 0.1 fusion.5
  33.2 1.8 %collective-permute-done.5.refs_6_ = bf16[272,128]{1,0:T(8,128)(2,1)S(1)} collective-permute-done((bf16[272,128]{1,0:T(8,128)(2,1)S(1)}, bf16[272,128]{1,0:T(8,128)(2,1)S(1)}, u32[]{:S(2)}, u32[]{:S(2)}) %collective-permute-start.5) | collective-permute-done | bytes 69664 | tf_op jit(solution)/shard_map/ppermute | solution.py:651
  35.0 3.4 %collective-permute-start.6 = (s16[2,128,128]{2,1,0:T(8,128)(2,1)S(1)}, s16[2,128,128]{2,1,0:T(8,128)(2,1)S(1)}, u32[]{:S(2)}, u32[]{:S(2)}) collective-permute-start(s16[2,128,128]{2,1,0:T(8,128)(2,1)S(1)} %get-tuple-element.33), channel_id=1, source_target_pairs={{0,4},{4,0},{8,12},{12,8},{1,5},{5,1},{9,13},{13,9},{2,6},{6,2},{1... | collective-permute-start | bytes 196616 | tf_op jit(solution)/shard_map/ppermute | solution.py:599
  38.5 1.1 %collective-permute-start.7 = (s16[2,128,128]{2,1,0:T(8,128)(2,1)S(1)}, s16[2,128,128]{2,1,0:T(8,128)(2,1)S(1)}, u32[]{:S(2)}, u32[]{:S(2)}) collective-permute-start(s16[2,128,128]{2,1,0:T(8,128)(2,1)S(1)} %get-tuple-element.34), channel_id=1, source_target_pairs={{0,8},{4,12},{8,0},{12,4},{1,9},{5,13},{9,1},{13,5},{2,10},{6,14},... | collective-permute-start | bytes 196616 | tf_op jit(solution)/shard_map/ppermute | solution.py:599
  39.5 1.4 %collective-permute-start.8 = (s16[2,128,128]{2,1,0:T(8,128)(2,1)S(1)}, s16[2,128,128]{2,1,0:T(8,128)(2,1)S(1)}, u32[]{:S(2)}, u32[]{:S(2)}) collective-permute-start(s16[2,128,128]{2,1,0:T(8,128)(2,1)S(1)} %get-tuple-element.35), channel_id=1, source_target_pairs={{0,12},{4,8},{8,4},{12,0},{1,13},{5,9},{9,5},{13,1},{2,14},{6,10},... | collective-permute-start | bytes 196616 | tf_op jit(solution)/shard_map/ppermute | solution.py:599
  40.9 0.1 slice_add_fusion
  41.0 0.1 reshape.97.partner
  41.1 0.1 reshape.102.weight
  41.3 6.1 %shard_map.107 = (f32[128,16,128]{2,1,0:T(8,128)S(1)}, f32[128,16,128]{2,1,0:T(8,128)S(1)}) custom-call(s32[128]{0:T(128)S(1)} %reshape.97.partner, f32[128]{0:T(128)S(1)} %reshape.102.weight, f32[2]{0:T(128)S(1)} %add_convert_fusion.1.present, bf16[96,96]{1,0:T(8,128)(2,1)S(1)} %copy-done.6, bf16[256,128]{1,0:T(8,128)(2,1)S(1)} %copy-done.5, ...), custom_call_target="tpu_custom_call" | custom-call | flops 20000000 | bytes 30000000 | tf_op jit(solution)/shard_map/pallas_call | solution.py:694
  47.4 1.5 %shard_map.108 = (f32[32,16,128]{2,1,0:T(8,128)S(1)}, f32[8,128]{1,0:T(8,128)S(1)}) custom-call(s32[128]{0:T(128)S(1)} %reshape.97.partner, s16[2,128,128]{2,1,0:T(8,128)(2,1)S(1)} %get-tuple-element.29.refs_0_, s16[2,128,128]{2,1,0:T(8,128)(2,1)S(1)} %collective-permute-done.6.refs_1_, s16[2,128,128]{2,1,0:T(8,128)(2,1)S(1)} %collective-permute-done.7.refs_2_, ...), custom_call_target="tpu_custom_call" | custom-call | flops 10000000 | bytes 8000000 | tf_op jit(solution)/shard_map/pallas_call | solution.py:710
  48.8 0.1 collective-permute-start.16
  48.9 0.6 collective-permute-start.15
  49.5 0.2 collective-permute-start.14
  49.7 0.1 shard_map.109
  49.8 1.1 %collective-permute-start.11 = (s16[144,128]{1,0:T(8,128)(2,1)S(1)}, s16[144,128]{1,0:T(8,128)(2,1)S(1)}, u32[]{:S(2)}, u32[]{:S(2)}) collective-permute-start(s16[144,128]{1,0:T(8,128)(2,1)S(1)} %get-tuple-element.39), channel_id=1, source_target_pairs={{0,4},{4,0},{8,12},{12,8},{1,5},{5,1},{9,13},{13,9},{2,6},{6,2},{1... | collective-permute-start | bytes 110600 | tf_op jit(solution)/shard_map/ppermute | solution.py:599
  50.9 2.0 %collective-permute-start.12 = (s16[144,128]{1,0:T(8,128)(2,1)S(1)}, s16[144,128]{1,0:T(8,128)(2,1)S(1)}, u32[]{:S(2)}, u32[]{:S(2)}) collective-permute-start(s16[144,128]{1,0:T(8,128)(2,1)S(1)} %get-tuple-element.40), channel_id=1, source_target_pairs={{0,8},{4,12},{8,0},{12,4},{1,9},{5,13},{9,1},{13,5},{2,10},{6,14},... | collective-permute-start | bytes 110600 | tf_op jit(solution)/shard_map/ppermute | solution.py:599
  52.8 1.4 %collective-permute-start.13 = (s16[144,128]{1,0:T(8,128)(2,1)S(1)}, s16[144,128]{1,0:T(8,128)(2,1)S(1)}, u32[]{:S(2)}, u32[]{:S(2)}) collective-permute-start(s16[144,128]{1,0:T(8,128)(2,1)S(1)} %get-tuple-element.41), channel_id=1, source_target_pairs={{0,12},{4,8},{8,4},{12,0},{1,13},{5,9},{9,5},{13,1},{2,14},{6,10},... | collective-permute-start | bytes 110600 | tf_op jit(solution)/shard_map/ppermute | solution.py:599
  54.3 2.5 %collective-permute-start.19 = (f32[8,128]{1,0:T(8,128)S(1)}, f32[8,128]{1,0:T(8,128)S(1)}, u32[]{:S(2)}, u32[]{:S(2)}) collective-permute-start(f32[8,128]{1,0:T(8,128)S(1)} %add_add_fusion.refs_3_), channel_id=1, source_target_pairs={{0,12},{4,8},{8,4},{12,0},{1,13},{5,9},{9,5},{13,1},{2,14},{6,10},... | collective-permute-start | bytes 12296 | tf_op jit(solution)/shard_map/ppermute | solution.py:599
  56.8 2.0 %collective-permute-start.17 = (f32[8,128]{1,0:T(8,128)S(1)}, f32[8,128]{1,0:T(8,128)S(1)}, u32[]{:S(2)}, u32[]{:S(2)}) collective-permute-start(f32[8,128]{1,0:T(8,128)S(1)} %add_add_fusion.refs_3_), channel_id=1, source_target_pairs={{0,4},{4,0},{8,12},{12,8},{1,5},{5,1},{9,13},{13,9},{2,6},{6,2},{1... | collective-permute-start | bytes 12296 | tf_op jit(solution)/shard_map/ppermute | solution.py:599
  59.4 0.4 collective-permute-done.19.refs_6_
  59.8 1.5 %collective-permute-done.18.refs_5_ = f32[8,128]{1,0:T(8,128)S(1)} collective-permute-done((f32[8,128]{1,0:T(8,128)S(1)}, f32[8,128]{1,0:T(8,128)S(1)}, u32[]{:S(2)}, u32[]{:S(2)}) %collective-permute-start.18) | collective-permute-done | bytes 4128 | tf_op jit(solution)/shard_map/ppermute | solution.py:599
  61.3 0.9 %shard_map.110 = (f32[8,16,512]{2,1,0:T(8,128)}, f32[8,16,512]{2,1,0:T(8,128)}) custom-call(s32[1]{0:T(128)} %bitcast.me, f32[1]{0:T(128)S(6)} %copy.19.prev_mean, f32[8,16,512]{2,1,0:T(8,128)S(1)} %copy-done.2, f32[8,16,512]{2,1,0:T(8,128)S(1)} %copy-done.3, f32[8,16,128]{2,1,0:T(8,128)S(1)} %slice.35.gradient, ...), custom_call_target="tpu_custom_call" | custom-call | flops 1000000 | bytes 2000000 | tf_op jit(solution)/shard_map/pallas_call | solution.py:740
  (39 shorter events, 0.1 us)
Async XLA Ops:
  0.6 1.2 %copy-start = (bf16[2,8,64,512]{3,2,1,0:T(8,128)(2,1)S(1)}, bf16[2,8,64,512]{3,2,1,0:T(8,128)(2,1)}, u32[]{:S(2)}) copy-start(bf16[2,8,64,512]{3,2,1,0:T(8,128)(2,1)} %slc.1) | copy-start | bytes 3145732
  1.9 2.4 %copy-start.1 = (bf16[2,8,64,512]{3,2,1,0:T(8,128)(2,1)S(1)}, bf16[2,8,64,512]{3,2,1,0:T(8,128)(2,1)}, u32[]{:S(2)}) copy-start(bf16[2,8,64,512]{3,2,1,0:T(8,128)(2,1)} %slc.1) | copy-start | bytes 3145732
  2.1 2.2 %collective-permute-start = (bf16[64,128]{1,0:T(8,128)(2,1)S(1)}, bf16[64,128]{1,0:T(8,128)(2,1)S(1)}, u32[]{:S(2)}, u32[]{:S(2)}) collective-permute-start(bf16[64,128]{1,0:T(8,128)(2,1)S(1)} %shard_map.104), channel_id=1, source_target_pairs={{0,1},{1,0},{2,3},{3,2},{4,5},{5,4},{6,7},{7,6},{8,9},{9,8},{10,11... | collective-permute-start | bytes 49160 | tf_op jit(solution)/shard_map/ppermute | solution.py:590
  2.6 0.7 %copy-start.7 = (s32[8,4]{0,1:T(4,128)S(1)}, s32[8,4]{0,1:T(4,128)}, u32[]{:S(2)}) copy-start(s32[8,4]{0,1:T(4,128)} %param.10) | copy-start | bytes 388
  3.4 0.7 %copy-start.8 = (f32[8,4]{0,1:T(4,128)S(1)}, f32[8,4]{0,1:T(4,128)}, u32[]{:S(2)}) copy-start(f32[8,4]{0,1:T(4,128)} %param.11) | copy-start | bytes 388
  4.3 8.4 %copy-start.2 = (f32[8,16,512]{2,1,0:T(8,128)S(1)}, f32[8,16,512]{2,1,0:T(8,128)}, u32[]{:S(2)}) copy-start(f32[8,16,512]{2,1,0:T(8,128)} %estimate.1) | copy-start | bytes 786436
  4.3 8.4 %copy-start.3 = (f32[8,16,512]{2,1,0:T(8,128)S(1)}, f32[8,16,512]{2,1,0:T(8,128)}, u32[]{:S(2)}) copy-start(f32[8,16,512]{2,1,0:T(8,128)} %direction.1) | copy-start | bytes 786436
  5.6 15.5 %collective-permute-start.1 = (bf16[1088,128]{1,0:T(8,128)(2,1)S(1)}, bf16[1088,128]{1,0:T(8,128)(2,1)S(1)}, u32[]{:S(2)}, u32[]{:S(2)}) collective-permute-start(bf16[1088,128]{1,0:T(8,128)(2,1)S(1)} %get-tuple-element.24), channel_id=1, source_target_pairs={{0,4},{4,0},{8,12},{12,8},{1,5},{5,1},{9,13},{13,9},{2,6},{6,2},{1... | collective-permute-start | bytes 835592 | tf_op jit(solution)/shard_map/ppermute | solution.py:599
  8.3 22.4 %collective-permute-start.2 = (bf16[1088,128]{1,0:T(8,128)(2,1)S(1)}, bf16[1088,128]{1,0:T(8,128)(2,1)S(1)}, u32[]{:S(2)}, u32[]{:S(2)}) collective-permute-start(bf16[1088,128]{1,0:T(8,128)(2,1)S(1)} %get-tuple-element.25), channel_id=1, source_target_pairs={{0,8},{4,12},{8,0},{12,4},{1,9},{5,13},{9,1},{13,5},{2,10},{6,14},... | collective-permute-start | bytes 835592 | tf_op jit(solution)/shard_map/ppermute | solution.py:599
  10.9 21.3 %collective-permute-start.3 = (bf16[1088,128]{1,0:T(8,128)(2,1)S(1)}, bf16[1088,128]{1,0:T(8,128)(2,1)S(1)}, u32[]{:S(2)}, u32[]{:S(2)}) collective-permute-start(bf16[1088,128]{1,0:T(8,128)(2,1)S(1)} %get-tuple-element.26), channel_id=1, source_target_pairs={{0,12},{4,8},{8,4},{12,0},{1,13},{5,9},{9,5},{13,1},{2,14},{6,10},... | collective-permute-start | bytes 835592 | tf_op jit(solution)/shard_map/ppermute | solution.py:599
  11.0 30.2 %collective-permute-start.9 = (bf16[272,128]{1,0:T(8,128)(2,1)S(1)}, bf16[272,128]{1,0:T(8,128)(2,1)S(1)}, u32[]{:S(2)}, u32[]{:S(2)}) collective-permute-start(bf16[272,128]{1,0:T(8,128)(2,1)S(1)} %bitcast.17), channel_id=1, source_target_pairs={{0,2},{2,0},{1,3},{3,1},{4,6},{6,4},{5,7},{7,5},{8,10},{10,8},{9,1... | collective-permute-start | bytes 208904 | tf_op jit(solution)/shard_map/ppermute | solution.py:651
  21.1 12.0 %collective-permute-start.4 = (bf16[272,128]{1,0:T(8,128)(2,1)S(1)}, bf16[272,128]{1,0:T(8,128)(2,1)S(1)}, u32[]{:S(2)}, u32[]{:S(2)}) collective-permute-start(bf16[272,128]{1,0:T(8,128)(2,1)S(1)} %bitcast.19), channel_id=1, source_target_pairs={{0,2},{2,0},{1,3},{3,1},{4,6},{6,4},{5,7},{7,5},{8,10},{10,8},{9,1... | collective-permute-start | bytes 208904 | tf_op jit(solution)/shard_map/ppermute | solution.py:651
  30.6 4.4 %collective-permute-start.5 = (bf16[272,128]{1,0:T(8,128)(2,1)S(1)}, bf16[272,128]{1,0:T(8,128)(2,1)S(1)}, u32[]{:S(2)}, u32[]{:S(2)}) collective-permute-start(bf16[272,128]{1,0:T(8,128)(2,1)S(1)} %bitcast.20), channel_id=1, source_target_pairs={{0,2},{2,0},{1,3},{3,1},{4,6},{6,4},{5,7},{7,5},{8,10},{10,8},{9,1... | collective-permute-start | bytes 208904 | tf_op jit(solution)/shard_map/ppermute | solution.py:651
  32.2 9.0 %collective-permute-start.10 = (bf16[272,128]{1,0:T(8,128)(2,1)S(1)}, bf16[272,128]{1,0:T(8,128)(2,1)S(1)}, u32[]{:S(2)}, u32[]{:S(2)}) collective-permute-start(bf16[272,128]{1,0:T(8,128)(2,1)S(1)} %bitcast.18), channel_id=1, source_target_pairs={{0,2},{2,0},{1,3},{3,1},{4,6},{6,4},{5,7},{7,5},{8,10},{10,8},{9,1... | collective-permute-start | bytes 208904 | tf_op jit(solution)/shard_map/ppermute | solution.py:651
  33.0 8.2 %copy-start.6 = (bf16[96,96]{1,0:T(8,128)(2,1)S(1)}, bf16[96,96]{1,0:T(8,128)(2,1)}, u32[]{:S(2)}) copy-start(bf16[96,96]{1,0:T(8,128)(2,1)} %constant.80.clone.order) | copy-start | bytes 55300
  33.1 8.2 %copy-start.4 = (bf16[256,128]{1,0:T(8,128)(2,1)S(1)}, bf16[256,128]{1,0:T(8,128)(2,1)}, u32[]{:S(2)}) copy-start(bf16[256,128]{1,0:T(8,128)(2,1)} %constant.82.clone.rim_band) | copy-start | bytes 196612
  33.1 8.2 %copy-start.5 = (bf16[256,128]{1,0:T(8,128)(2,1)S(1)}, bf16[256,128]{1,0:T(8,128)(2,1)}, u32[]{:S(2)}) copy-start(bf16[256,128]{1,0:T(8,128)(2,1)} %constant.81.clone.band) | copy-start | bytes 196612
  35.0 12.3 %collective-permute-start.6 = (s16[2,128,128]{2,1,0:T(8,128)(2,1)S(1)}, s16[2,128,128]{2,1,0:T(8,128)(2,1)S(1)}, u32[]{:S(2)}, u32[]{:S(2)}) collective-permute-start(s16[2,128,128]{2,1,0:T(8,128)(2,1)S(1)} %get-tuple-element.33), channel_id=1, source_target_pairs={{0,4},{4,0},{8,12},{12,8},{1,5},{5,1},{9,13},{13,9},{2,6},{6,2},{1... | collective-permute-start | bytes 196616 | tf_op jit(solution)/shard_map/ppermute | solution.py:599
  38.5 8.9 %collective-permute-start.7 = (s16[2,128,128]{2,1,0:T(8,128)(2,1)S(1)}, s16[2,128,128]{2,1,0:T(8,128)(2,1)S(1)}, u32[]{:S(2)}, u32[]{:S(2)}) collective-permute-start(s16[2,128,128]{2,1,0:T(8,128)(2,1)S(1)} %get-tuple-element.34), channel_id=1, source_target_pairs={{0,8},{4,12},{8,0},{12,4},{1,9},{5,13},{9,1},{13,5},{2,10},{6,14},... | collective-permute-start | bytes 196616 | tf_op jit(solution)/shard_map/ppermute | solution.py:599
  39.5 7.8 %collective-permute-start.8 = (s16[2,128,128]{2,1,0:T(8,128)(2,1)S(1)}, s16[2,128,128]{2,1,0:T(8,128)(2,1)S(1)}, u32[]{:S(2)}, u32[]{:S(2)}) collective-permute-start(s16[2,128,128]{2,1,0:T(8,128)(2,1)S(1)} %get-tuple-element.35), channel_id=1, source_target_pairs={{0,12},{4,8},{8,4},{12,0},{1,13},{5,9},{9,5},{13,1},{2,14},{6,10},... | collective-permute-start | bytes 196616 | tf_op jit(solution)/shard_map/ppermute | solution.py:599
  48.8 4.0 %collective-permute-start.16 = (f32[8,128]{1,0:T(8,128)S(1)}, f32[8,128]{1,0:T(8,128)S(1)}, u32[]{:S(2)}, u32[]{:S(2)}) collective-permute-start(f32[8,128]{1,0:T(8,128)S(1)} %get-tuple-element.42), channel_id=1, source_target_pairs={{0,3},{1,0},{2,1},{3,2},{4,7},{5,4},{6,5},{7,6},{8,11},{9,8},{10,9... | collective-permute-start | bytes 12296 | tf_op jit(solution)/shard_map/ppermute | solution.py:726
  48.9 5.3 %collective-permute-start.15 = (f32[8,128]{1,0:T(8,128)S(1)}, f32[8,128]{1,0:T(8,128)S(1)}, u32[]{:S(2)}, u32[]{:S(2)}) collective-permute-start(f32[8,128]{1,0:T(8,128)S(1)} %get-tuple-element.42), channel_id=1, source_target_pairs={{0,2},{1,3},{2,0},{3,1},{4,6},{5,7},{6,4},{7,5},{8,10},{9,11},{10,... | collective-permute-start | bytes 12296 | tf_op jit(solution)/shard_map/ppermute | solution.py:726
  49.5 4.7 %collective-permute-start.14 = (f32[8,128]{1,0:T(8,128)S(1)}, f32[8,128]{1,0:T(8,128)S(1)}, u32[]{:S(2)}, u32[]{:S(2)}) collective-permute-start(f32[8,128]{1,0:T(8,128)S(1)} %get-tuple-element.42), channel_id=1, source_target_pairs={{0,1},{1,2},{2,3},{3,0},{4,5},{5,6},{6,7},{7,4},{8,9},{9,10},{10,1... | collective-permute-start | bytes 12296 | tf_op jit(solution)/shard_map/ppermute | solution.py:726
  49.8 4.5 %collective-permute-start.11 = (s16[144,128]{1,0:T(8,128)(2,1)S(1)}, s16[144,128]{1,0:T(8,128)(2,1)S(1)}, u32[]{:S(2)}, u32[]{:S(2)}) collective-permute-start(s16[144,128]{1,0:T(8,128)(2,1)S(1)} %get-tuple-element.39), channel_id=1, source_target_pairs={{0,4},{4,0},{8,12},{12,8},{1,5},{5,1},{9,13},{13,9},{2,6},{6,2},{1... | collective-permute-start | bytes 110600 | tf_op jit(solution)/shard_map/ppermute | solution.py:599
  50.9 8.5 %collective-permute-start.12 = (s16[144,128]{1,0:T(8,128)(2,1)S(1)}, s16[144,128]{1,0:T(8,128)(2,1)S(1)}, u32[]{:S(2)}, u32[]{:S(2)}) collective-permute-start(s16[144,128]{1,0:T(8,128)(2,1)S(1)} %get-tuple-element.40), channel_id=1, source_target_pairs={{0,8},{4,12},{8,0},{12,4},{1,9},{5,13},{9,1},{13,5},{2,10},{6,14},... | collective-permute-start | bytes 110600 | tf_op jit(solution)/shard_map/ppermute | solution.py:599
  52.8 6.6 %collective-permute-start.13 = (s16[144,128]{1,0:T(8,128)(2,1)S(1)}, s16[144,128]{1,0:T(8,128)(2,1)S(1)}, u32[]{:S(2)}, u32[]{:S(2)}) collective-permute-start(s16[144,128]{1,0:T(8,128)(2,1)S(1)} %get-tuple-element.41), channel_id=1, source_target_pairs={{0,12},{4,8},{8,4},{12,0},{1,13},{5,9},{9,5},{13,1},{2,14},{6,10},... | collective-permute-start | bytes 110600 | tf_op jit(solution)/shard_map/ppermute | solution.py:599
  54.3 5.5 %collective-permute-start.19 = (f32[8,128]{1,0:T(8,128)S(1)}, f32[8,128]{1,0:T(8,128)S(1)}, u32[]{:S(2)}, u32[]{:S(2)}) collective-permute-start(f32[8,128]{1,0:T(8,128)S(1)} %add_add_fusion.refs_3_), channel_id=1, source_target_pairs={{0,12},{4,8},{8,4},{12,0},{1,13},{5,9},{9,5},{13,1},{2,14},{6,10},... | collective-permute-start | bytes 12296 | tf_op jit(solution)/shard_map/ppermute | solution.py:599
  56.8 4.5 %collective-permute-start.18 = (f32[8,128]{1,0:T(8,128)S(1)}, f32[8,128]{1,0:T(8,128)S(1)}, u32[]{:S(2)}, u32[]{:S(2)}) collective-permute-start(f32[8,128]{1,0:T(8,128)S(1)} %add_add_fusion.refs_3_), channel_id=1, source_target_pairs={{0,8},{4,12},{8,0},{12,4},{1,9},{5,13},{9,1},{13,5},{2,10},{6,14},... | collective-permute-start | bytes 12296 | tf_op jit(solution)/shard_map/ppermute | solution.py:599
  56.8 4.5 %collective-permute-start.17 = (f32[8,128]{1,0:T(8,128)S(1)}, f32[8,128]{1,0:T(8,128)S(1)}, u32[]{:S(2)}, u32[]{:S(2)}) collective-permute-start(f32[8,128]{1,0:T(8,128)S(1)} %add_add_fusion.refs_3_), channel_id=1, source_target_pairs={{0,4},{4,0},{8,12},{12,8},{1,5},{5,1},{9,13},{13,9},{2,6},{6,2},{1... | collective-permute-start | bytes 12296 | tf_op jit(solution)/shard_map/ppermute | solution.py:599

commit v24 on v23

--- a/solution.py
+++ b/solution.py
@@ -667,7 +667,8 @@
 
     halos = [halo([array.reshape(-1, rows, LANES)]) for array in block]
     late = lax.optimization_barrier((fields, block, halos[1:-1]))[0]
-    field = [fields[0]] + [exchanged(late[by], "epoch", by) for by in range(1, tiles)]
+    near = lax.optimization_barrier((fields[1], block[1], halos[0]))[0]
+    field = [fields[0], exchanged(near, "epoch", 1)] + [exchanged(late[by], "epoch", by) for by in range(2, tiles)]
 
     listed = jnp.concatenate([params_in(shift) for shift in range(tiles)], axis=0)
     place = jnp.arange(total, dtype=jnp.int32)[:, None]

time: 62.4 us -> 62.4 us (level)
    ppermute x4, waiting for transfers between devices: 1.85 us -> 4.18 us  [halo(): lax.ppermute(border(jnp.where(space == 0, rows - HALO, 0)), 'space', [(0,...]
    ppermute x12, waiting for transfers between devices: 17.9 us -> 15.6 us  [exchanged(): return lax.ppermute(x, axis, [(i, i ^ by) for i in range(size)])]
  transfers between devices with their start and end apart: 20 -> 20, of which waited for: 5 -> 6; matrix products, arithmetic and copies ran while one was open for 2% -> 2% of each run, Pallas kernels for 10% -> 10%
where the time goes in v24:
time: 62.4 us; the launch traced here: 62.2 us
  starting transfers between devices  26.9 us (43%)
  waiting for transfers between devices  19.8 us (32%)
  Pallas kernels  10.2 us (16%)
  local copies, waits for them, and re-layouts  3.32 us (5%)
  between operations  1.49 us (2%)
    ppermute x12, starting transfers between devices, exchanged(): return lax.ppermute(x, axis, [(i, i ^ by) for i in range(size)])  20.2 us
    ppermute x12, waiting for transfers between devices, exchanged(): return lax.ppermute(x, axis, [(i, i ^ by) for i in range(size)])  15.6 us
    pallas_call x1, Pallas kernels, transposed_plan(): pl.pallas_call(functools.partial(pair_kernel, (epochs, rows, len(operands...  6.04 us
    ppermute x4, starting transfers between devices, halo(): lax.ppermute(border(jnp.where(space == 0, rows - HALO, 0)), 'space', [(0,...  5.42 us
    ppermute x4, waiting for transfers between devices, halo(): lax.ppermute(border(jnp.where(space == 0, rows - HALO, 0)), 'space', [(0,...  4.18 us
    unnamed x20, local copies, waits for them, and re-layouts  2.76 us
    pallas_call x1, Pallas kernels, transposed_plan(): pl.pallas_call(functools.partial(gradient_kernel, (tiles, epochs)), out_s...  1.48 us
    pallas_call x1, Pallas kernels, transposed_plan(): pl.pallas_call(pack_kernel, out_shape=(jax.ShapeDtypeStruct((tile_rows +...  1.26 us
  transfers between devices with their start and end apart: 20, of which 6 were waited for; matrix products, arithmetic and copies ran while one was open for 2% of the time, Pallas kernels for 10%

profile of v24, /device:TPU:0, one launch (start us, length us, event | category | flops | bytes accessed | tf_op | source)
XLA Modules:
  0.0 62.2 jit_solution(5016661642097256085)
XLA Ops:
  0.6 1.2 %copy-done = bf16[2,8,64,512]{3,2,1,0:T(8,128)(2,1)S(1)} copy-done((bf16[2,8,64,512]{3,2,1,0:T(8,128)(2,1)S(1)}, bf16[2,8,64,512]{3,2,1,0:T(8,128)(2,1)}, u32[]{:S(2)}) %copy-start) | copy-done | bytes 1048600
  1.9 0.2 shard_map.104
  2.1 0.5 collective-permute-start
  2.6 0.7 %copy-done.7 = s32[8,4]{0,1:T(4,128)S(1)} copy-done((s32[8,4]{0,1:T(4,128)S(1)}, s32[8,4]{0,1:T(4,128)}, u32[]{:S(2)}) %copy-start.7) | copy-done | bytes 152
  3.3 0.1 copy.15
  3.4 0.7 %copy-done.8 = f32[8,4]{0,1:T(4,128)S(1)} copy-done((f32[8,4]{0,1:T(4,128)S(1)}, f32[8,4]{0,1:T(4,128)}, u32[]{:S(2)}) %copy-start.8) | copy-done | bytes 152
  4.1 0.1 copy.16
  4.1 0.1 select_maximum_fusion.params
  4.2 0.1 add_convert_fusion.present
  4.3 1.3 %shard_map.105 = (bf16[1088,128]{1,0:T(8,128)(2,1)S(1)}, bf16[1088,128]{1,0:T(8,128)(2,1)S(1)}, bf16[1088,128]{1,0:T(8,128)(2,1)S(1)}, bf16[1088,128]{1,0:T(8,128)(2,1)S(1)}) custom-call(s32[1]{0:T(128)} %bitcast.me, f32[2]{0:T(128)S(1)} %add_convert_fusion.present, bf16[2,8,64,512]{3,2,1,0:T(8,128)(2,1)S(1)} %copy-done.1, ...), custom_call_target="tpu_custom_call" | custom-call | flops 3000000 | bytes 4000000 | tf_op jit(solution)/shard_map/pallas_call | solution.py:632
  5.6 2.7 %collective-permute-start.1 = (bf16[1088,128]{1,0:T(8,128)(2,1)S(1)}, bf16[1088,128]{1,0:T(8,128)(2,1)S(1)}, u32[]{:S(2)}, u32[]{:S(2)}) collective-permute-start(bf16[1088,128]{1,0:T(8,128)(2,1)S(1)} %get-tuple-element.24), channel_id=1, source_target_pairs={{0,4},{4,0},{8,12},{12,8},{1,5},{5,1},{9,13},{13,9},{2,6},{6,2},{1... | collective-permute-start | bytes 835592 | tf_op jit(solution)/shard_map/ppermute | solution.py:599
  8.3 2.6 %collective-permute-start.2 = (bf16[1088,128]{1,0:T(8,128)(2,1)S(1)}, bf16[1088,128]{1,0:T(8,128)(2,1)S(1)}, u32[]{:S(2)}, u32[]{:S(2)}) collective-permute-start(bf16[1088,128]{1,0:T(8,128)(2,1)S(1)} %get-tuple-element.25), channel_id=1, source_target_pairs={{0,8},{4,12},{8,0},{12,4},{1,9},{5,13},{9,1},{13,5},{2,10},{6,14},... | collective-permute-start | bytes 835592 | tf_op jit(solution)/shard_map/ppermute | solution.py:599
  10.9 1.6 %collective-permute-start.4 = (bf16[272,128]{1,0:T(8,128)(2,1)S(1)}, bf16[272,128]{1,0:T(8,128)(2,1)S(1)}, u32[]{:S(2)}, u32[]{:S(2)}) collective-permute-start(bf16[272,128]{1,0:T(8,128)(2,1)S(1)} %bitcast.20), channel_id=1, source_target_pairs={{0,2},{2,0},{1,3},{3,1},{4,6},{6,4},{5,7},{7,5},{8,10},{10,8},{9,1... | collective-permute-start | bytes 208904 | tf_op jit(solution)/shard_map/ppermute | solution.py:651
  12.4 0.2 collective-permute-start.3
  12.6 0.1 add_convert_fusion.1.present
  12.7 0.1 slice.27
  12.8 0.1 shard_map.106
  12.9 2.3 %collective-permute-done.4.refs_4_ = bf16[272,128]{1,0:T(8,128)(2,1)S(1)} collective-permute-done((bf16[272,128]{1,0:T(8,128)(2,1)S(1)}, bf16[272,128]{1,0:T(8,128)(2,1)S(1)}, u32[]{:S(2)}, u32[]{:S(2)}) %collective-permute-start.4) | collective-permute-done | bytes 69664 | tf_op jit(solution)/shard_map/ppermute | solution.py:651
  15.2 5.9 %collective-permute-done.1.refs_1_ = bf16[1088,128]{1,0:T(8,128)(2,1)S(1)} collective-permute-done((bf16[1088,128]{1,0:T(8,128)(2,1)S(1)}, bf16[1088,128]{1,0:T(8,128)(2,1)S(1)}, u32[]{:S(2)}, u32[]{:S(2)}) %collective-permute-start.1) | collective-permute-done | bytes 278560 | tf_op jit(solution)/shard_map/ppermute | solution.py:599
  21.1 1.7 %collective-permute-start.6 = (bf16[272,128]{1,0:T(8,128)(2,1)S(1)}, bf16[272,128]{1,0:T(8,128)(2,1)S(1)}, u32[]{:S(2)}, u32[]{:S(2)}) collective-permute-start(bf16[272,128]{1,0:T(8,128)(2,1)S(1)} %bitcast.18), channel_id=1, source_target_pairs={{0,2},{2,0},{1,3},{3,1},{4,6},{6,4},{5,7},{7,5},{8,10},{10,8},{9,1... | collective-permute-start | bytes 208904 | tf_op jit(solution)/shard_map/ppermute | solution.py:651
  22.8 7.8 %collective-permute-done.2.refs_2_ = bf16[1088,128]{1,0:T(8,128)(2,1)S(1)} collective-permute-done((bf16[1088,128]{1,0:T(8,128)(2,1)S(1)}, bf16[1088,128]{1,0:T(8,128)(2,1)S(1)}, u32[]{:S(2)}, u32[]{:S(2)}) %collective-permute-start.2) | collective-permute-done | bytes 278560 | tf_op jit(solution)/shard_map/ppermute | solution.py:599
  30.7 1.6 %collective-permute-start.7 = (bf16[272,128]{1,0:T(8,128)(2,1)S(1)}, bf16[272,128]{1,0:T(8,128)(2,1)S(1)}, u32[]{:S(2)}, u32[]{:S(2)}) collective-permute-start(bf16[272,128]{1,0:T(8,128)(2,1)S(1)} %bitcast.19), channel_id=1, source_target_pairs={{0,2},{2,0},{1,3},{3,1},{4,6},{6,4},{5,7},{7,5},{8,10},{10,8},{9,1... | collective-permute-start | bytes 208904 | tf_op jit(solution)/shard_map/ppermute | solution.py:651
  32.3 0.6 collective-permute-start.10
  32.9 0.1 slice.36
  32.9 0.1 slice.37
  33.0 0.1 slice.38
  33.1 0.0 copy-start.5
  33.1 0.1 fusion.5
  33.2 1.8 %collective-permute-done.7.refs_6_ = bf16[272,128]{1,0:T(8,128)(2,1)S(1)} collective-permute-done((bf16[272,128]{1,0:T(8,128)(2,1)S(1)}, bf16[272,128]{1,0:T(8,128)(2,1)S(1)}, u32[]{:S(2)}, u32[]{:S(2)}) %collective-permute-start.7) | collective-permute-done | bytes 69664 | tf_op jit(solution)/shard_map/ppermute | solution.py:651
  35.1 4.4 %collective-permute-start.8 = (s16[2,128,128]{2,1,0:T(8,128)(2,1)S(1)}, s16[2,128,128]{2,1,0:T(8,128)(2,1)S(1)}, u32[]{:S(2)}, u32[]{:S(2)}) collective-permute-start(s16[2,128,128]{2,1,0:T(8,128)(2,1)S(1)} %get-tuple-element.34), channel_id=1, source_target_pairs={{0,8},{4,12},{8,0},{12,4},{1,9},{5,13},{9,1},{13,5},{2,10},{6,14},... | collective-permute-start | bytes 196616 | tf_op jit(solution)/shard_map/ppermute | solution.py:599
  39.5 1.3 %collective-permute-start.9 = (s16[2,128,128]{2,1,0:T(8,128)(2,1)S(1)}, s16[2,128,128]{2,1,0:T(8,128)(2,1)S(1)}, u32[]{:S(2)}, u32[]{:S(2)}) collective-permute-start(s16[2,128,128]{2,1,0:T(8,128)(2,1)S(1)} %get-tuple-element.35), channel_id=1, source_target_pairs={{0,12},{4,8},{8,4},{12,0},{1,13},{5,9},{9,5},{13,1},{2,14},{6,10},... | collective-permute-start | bytes 196616 | tf_op jit(solution)/shard_map/ppermute | solution.py:599
  40.9 0.1 slice_add_fusion
  40.9 0.1 reshape.97.partner
  41.0 0.1 reshape.104.weight
  41.2 6.0 %shard_map.107 = (f32[128,16,128]{2,1,0:T(8,128)S(1)}, f32[128,16,128]{2,1,0:T(8,128)S(1)}) custom-call(s32[128]{0:T(128)S(1)} %reshape.97.partner, f32[128]{0:T(128)S(1)} %reshape.104.weight, f32[2]{0:T(128)S(1)} %add_convert_fusion.1.present, bf16[96,96]{1,0:T(8,128)(2,1)S(1)} %copy-done.6, bf16[256,128]{1,0:T(8,128)(2,1)S(1)} %copy-done.5, ...), custom_call_target="tpu_custom_call" | custom-call | flops 20000000 | bytes 30000000 | tf_op jit(solution)/shard_map/pallas_call | solution.py:695
  47.3 1.5 %shard_map.108 = (f32[32,16,128]{2,1,0:T(8,128)S(1)}, f32[8,128]{1,0:T(8,128)S(1)}) custom-call(s32[128]{0:T(128)S(1)} %reshape.97.partner, s16[2,128,128]{2,1,0:T(8,128)(2,1)S(1)} %get-tuple-element.29.refs_0_, s16[2,128,128]{2,1,0:T(8,128)(2,1)S(1)} %collective-permute-done.5.refs_1_, s16[2,128,128]{2,1,0:T(8,128)(2,1)S(1)} %collective-permute-done.8.refs_2_, ...), custom_call_target="tpu_custom_call" | custom-call | flops 10000000 | bytes 8000000 | tf_op jit(solution)/shard_map/pallas_call | solution.py:711
  48.8 0.1 collective-permute-start.16
  48.8 0.6 collective-permute-start.15
  49.4 0.2 collective-permute-start.14
  49.6 0.1 shard_map.109
  49.7 0.7 %collective-permute-start.11 = (s16[144,128]{1,0:T(8,128)(2,1)S(1)}, s16[144,128]{1,0:T(8,128)(2,1)S(1)}, u32[]{:S(2)}, u32[]{:S(2)}) collective-permute-start(s16[144,128]{1,0:T(8,128)(2,1)S(1)} %get-tuple-element.39), channel_id=1, source_target_pairs={{0,4},{4,0},{8,12},{12,8},{1,5},{5,1},{9,13},{13,9},{2,6},{6,2},{1... | collective-permute-start | bytes 110600 | tf_op jit(solution)/shard_map/ppermute | solution.py:599
  50.4 2.4 %collective-permute-start.12 = (s16[144,128]{1,0:T(8,128)(2,1)S(1)}, s16[144,128]{1,0:T(8,128)(2,1)S(1)}, u32[]{:S(2)}, u32[]{:S(2)}) collective-permute-start(s16[144,128]{1,0:T(8,128)(2,1)S(1)} %get-tuple-element.40), channel_id=1, source_target_pairs={{0,8},{4,12},{8,0},{12,4},{1,9},{5,13},{9,1},{13,5},{2,10},{6,14},... | collective-permute-start | bytes 110600 | tf_op jit(solution)/shard_map/ppermute | solution.py:599
  52.8 1.3 %collective-permute-start.13 = (s16[144,128]{1,0:T(8,128)(2,1)S(1)}, s16[144,128]{1,0:T(8,128)(2,1)S(1)}, u32[]{:S(2)}, u32[]{:S(2)}) collective-permute-start(s16[144,128]{1,0:T(8,128)(2,1)S(1)} %get-tuple-element.41), channel_id=1, source_target_pairs={{0,12},{4,8},{8,4},{12,0},{1,13},{5,9},{9,5},{13,1},{2,14},{6,10},... | collective-permute-start | bytes 110600 | tf_op jit(solution)/shard_map/ppermute | solution.py:599
  54.2 2.5 %collective-permute-start.19 = (f32[8,128]{1,0:T(8,128)S(1)}, f32[8,128]{1,0:T(8,128)S(1)}, u32[]{:S(2)}, u32[]{:S(2)}) collective-permute-start(f32[8,128]{1,0:T(8,128)S(1)} %add_add_fusion.refs_3_), channel_id=1, source_target_pairs={{0,12},{4,8},{8,4},{12,0},{1,13},{5,9},{9,5},{13,1},{2,14},{6,10},... | collective-permute-start | bytes 12296 | tf_op jit(solution)/shard_map/ppermute | solution.py:599
  56.7 1.9 %collective-permute-start.17 = (f32[8,128]{1,0:T(8,128)S(1)}, f32[8,128]{1,0:T(8,128)S(1)}, u32[]{:S(2)}, u32[]{:S(2)}) collective-permute-start(f32[8,128]{1,0:T(8,128)S(1)} %add_add_fusion.refs_3_), channel_id=1, source_target_pairs={{0,4},{4,0},{8,12},{12,8},{1,5},{5,1},{9,13},{13,9},{2,6},{6,2},{1... | collective-permute-start | bytes 12296 | tf_op jit(solution)/shard_map/ppermute | solution.py:599
  59.3 0.3 collective-permute-done.19.refs_6_
  59.7 1.6 %collective-permute-done.18.refs_5_ = f32[8,128]{1,0:T(8,128)S(1)} collective-permute-done((f32[8,128]{1,0:T(8,128)S(1)}, f32[8,128]{1,0:T(8,128)S(1)}, u32[]{:S(2)}, u32[]{:S(2)}) %collective-permute-start.18) | collective-permute-done | bytes 4128 | tf_op jit(solution)/shard_map/ppermute | solution.py:599
  61.2 0.9 %shard_map.110 = (f32[8,16,512]{2,1,0:T(8,128)}, f32[8,16,512]{2,1,0:T(8,128)}) custom-call(s32[1]{0:T(128)} %bitcast.me, f32[1]{0:T(128)S(6)} %copy.19.prev_mean, f32[8,16,512]{2,1,0:T(8,128)S(1)} %copy-done.2, f32[8,16,512]{2,1,0:T(8,128)S(1)} %copy-done.3, f32[8,16,128]{2,1,0:T(8,128)S(1)} %slice.35.gradient, ...), custom_call_target="tpu_custom_call" | custom-call | flops 1000000 | bytes 2000000 | tf_op jit(solution)/shard_map/pallas_call | solution.py:741
  (39 shorter events, 0.1 us)
Async XLA Ops:
  0.6 1.2 %copy-start = (bf16[2,8,64,512]{3,2,1,0:T(8,128)(2,1)S(1)}, bf16[2,8,64,512]{3,2,1,0:T(8,128)(2,1)}, u32[]{:S(2)}) copy-start(bf16[2,8,64,512]{3,2,1,0:T(8,128)(2,1)} %slc.1) | copy-start | bytes 3145732
  1.9 2.4 %copy-start.1 = (bf16[2,8,64,512]{3,2,1,0:T(8,128)(2,1)S(1)}, bf16[2,8,64,512]{3,2,1,0:T(8,128)(2,1)}, u32[]{:S(2)}) copy-start(bf16[2,8,64,512]{3,2,1,0:T(8,128)(2,1)} %slc.1) | copy-start | bytes 3145732
  2.1 2.2 %collective-permute-start = (bf16[64,128]{1,0:T(8,128)(2,1)S(1)}, bf16[64,128]{1,0:T(8,128)(2,1)S(1)}, u32[]{:S(2)}, u32[]{:S(2)}) collective-permute-start(bf16[64,128]{1,0:T(8,128)(2,1)S(1)} %shard_map.104), channel_id=1, source_target_pairs={{0,1},{1,0},{2,3},{3,2},{4,5},{5,4},{6,7},{7,6},{8,9},{9,8},{10,11... | collective-permute-start | bytes 49160 | tf_op jit(solution)/shard_map/ppermute | solution.py:590
  2.6 0.7 %copy-start.7 = (s32[8,4]{0,1:T(4,128)S(1)}, s32[8,4]{0,1:T(4,128)}, u32[]{:S(2)}) copy-start(s32[8,4]{0,1:T(4,128)} %param.10) | copy-start | bytes 388
  3.4 0.7 %copy-start.8 = (f32[8,4]{0,1:T(4,128)S(1)}, f32[8,4]{0,1:T(4,128)}, u32[]{:S(2)}) copy-start(f32[8,4]{0,1:T(4,128)} %param.11) | copy-start | bytes 388
  4.3 8.5 %copy-start.2 = (f32[8,16,512]{2,1,0:T(8,128)S(1)}, f32[8,16,512]{2,1,0:T(8,128)}, u32[]{:S(2)}) copy-start(f32[8,16,512]{2,1,0:T(8,128)} %estimate.1) | copy-start | bytes 786436
  4.3 8.5 %copy-start.3 = (f32[8,16,512]{2,1,0:T(8,128)S(1)}, f32[8,16,512]{2,1,0:T(8,128)}, u32[]{:S(2)}) copy-start(f32[8,16,512]{2,1,0:T(8,128)} %direction.1) | copy-start | bytes 786436
  5.6 15.5 %collective-permute-start.1 = (bf16[1088,128]{1,0:T(8,128)(2,1)S(1)}, bf16[1088,128]{1,0:T(8,128)(2,1)S(1)}, u32[]{:S(2)}, u32[]{:S(2)}) collective-permute-start(bf16[1088,128]{1,0:T(8,128)(2,1)S(1)} %get-tuple-element.24), channel_id=1, source_target_pairs={{0,4},{4,0},{8,12},{12,8},{1,5},{5,1},{9,13},{13,9},{2,6},{6,2},{1... | collective-permute-start | bytes 835592 | tf_op jit(solution)/shard_map/ppermute | solution.py:599
  8.3 22.4 %collective-permute-start.2 = (bf16[1088,128]{1,0:T(8,128)(2,1)S(1)}, bf16[1088,128]{1,0:T(8,128)(2,1)S(1)}, u32[]{:S(2)}, u32[]{:S(2)}) collective-permute-start(bf16[1088,128]{1,0:T(8,128)(2,1)S(1)} %get-tuple-element.25), channel_id=1, source_target_pairs={{0,8},{4,12},{8,0},{12,4},{1,9},{5,13},{9,1},{13,5},{2,10},{6,14},... | collective-permute-start | bytes 835592 | tf_op jit(solution)/shard_map/ppermute | solution.py:599
  10.9 4.4 %collective-permute-start.4 = (bf16[272,128]{1,0:T(8,128)(2,1)S(1)}, bf16[272,128]{1,0:T(8,128)(2,1)S(1)}, u32[]{:S(2)}, u32[]{:S(2)}) collective-permute-start(bf16[272,128]{1,0:T(8,128)(2,1)S(1)} %bitcast.20), channel_id=1, source_target_pairs={{0,2},{2,0},{1,3},{3,1},{4,6},{6,4},{5,7},{7,5},{8,10},{10,8},{9,1... | collective-permute-start | bytes 208904 | tf_op jit(solution)/shard_map/ppermute | solution.py:651
  12.4 19.8 %collective-permute-start.3 = (bf16[1088,128]{1,0:T(8,128)(2,1)S(1)}, bf16[1088,128]{1,0:T(8,128)(2,1)S(1)}, u32[]{:S(2)}, u32[]{:S(2)}) collective-permute-start(bf16[1088,128]{1,0:T(8,128)(2,1)S(1)} %get-tuple-element.26), channel_id=1, source_target_pairs={{0,12},{4,8},{8,4},{12,0},{1,13},{5,9},{9,5},{13,1},{2,14},{6,10},... | collective-permute-start | bytes 835592 | tf_op jit(solution)/shard_map/ppermute | solution.py:599
  21.1 26.1 %collective-permute-start.5 = (s16[2,128,128]{2,1,0:T(8,128)(2,1)S(1)}, s16[2,128,128]{2,1,0:T(8,128)(2,1)S(1)}, u32[]{:S(2)}, u32[]{:S(2)}) collective-permute-start(s16[2,128,128]{2,1,0:T(8,128)(2,1)S(1)} %get-tuple-element.31), channel_id=1, source_target_pairs={{0,4},{4,0},{8,12},{12,8},{1,5},{5,1},{9,13},{13,9},{2,6},{6,2},{1... | collective-permute-start | bytes 196616 | tf_op jit(solution)/shard_map/ppermute | solution.py:599
  21.1 12.1 %collective-permute-start.6 = (bf16[272,128]{1,0:T(8,128)(2,1)S(1)}, bf16[272,128]{1,0:T(8,128)(2,1)S(1)}, u32[]{:S(2)}, u32[]{:S(2)}) collective-permute-start(bf16[272,128]{1,0:T(8,128)(2,1)S(1)} %bitcast.18), channel_id=1, source_target_pairs={{0,2},{2,0},{1,3},{3,1},{4,6},{6,4},{5,7},{7,5},{8,10},{10,8},{9,1... | collective-permute-start | bytes 208904 | tf_op jit(solution)/shard_map/ppermute | solution.py:651
  30.7 4.4 %collective-permute-start.7 = (bf16[272,128]{1,0:T(8,128)(2,1)S(1)}, bf16[272,128]{1,0:T(8,128)(2,1)S(1)}, u32[]{:S(2)}, u32[]{:S(2)}) collective-permute-start(bf16[272,128]{1,0:T(8,128)(2,1)S(1)} %bitcast.19), channel_id=1, source_target_pairs={{0,2},{2,0},{1,3},{3,1},{4,6},{6,4},{5,7},{7,5},{8,10},{10,8},{9,1... | collective-permute-start | bytes 208904 | tf_op jit(solution)/shard_map/ppermute | solution.py:651
  32.3 8.9 %collective-permute-start.10 = (bf16[272,128]{1,0:T(8,128)(2,1)S(1)}, bf16[272,128]{1,0:T(8,128)(2,1)S(1)}, u32[]{:S(2)}, u32[]{:S(2)}) collective-permute-start(bf16[272,128]{1,0:T(8,128)(2,1)S(1)} %bitcast.17), channel_id=1, source_target_pairs={{0,2},{2,0},{1,3},{3,1},{4,6},{6,4},{5,7},{7,5},{8,10},{10,8},{9,1... | collective-permute-start | bytes 208904 | tf_op jit(solution)/shard_map/ppermute | solution.py:651
  33.1 8.1 %copy-start.6 = (bf16[96,96]{1,0:T(8,128)(2,1)S(1)}, bf16[96,96]{1,0:T(8,128)(2,1)}, u32[]{:S(2)}) copy-start(bf16[96,96]{1,0:T(8,128)(2,1)} %constant.80.clone.order) | copy-start | bytes 55300
  33.1 8.1 %copy-start.4 = (bf16[256,128]{1,0:T(8,128)(2,1)S(1)}, bf16[256,128]{1,0:T(8,128)(2,1)}, u32[]{:S(2)}) copy-start(bf16[256,128]{1,0:T(8,128)(2,1)} %constant.82.clone.rim_band) | copy-start | bytes 196612
  33.1 8.1 %copy-start.5 = (bf16[256,128]{1,0:T(8,128)(2,1)S(1)}, bf16[256,128]{1,0:T(8,128)(2,1)}, u32[]{:S(2)}) copy-start(bf16[256,128]{1,0:T(8,128)(2,1)} %constant.81.clone.band) | copy-start | bytes 196612
  35.1 12.2 %collective-permute-start.8 = (s16[2,128,128]{2,1,0:T(8,128)(2,1)S(1)}, s16[2,128,128]{2,1,0:T(8,128)(2,1)S(1)}, u32[]{:S(2)}, u32[]{:S(2)}) collective-permute-start(s16[2,128,128]{2,1,0:T(8,128)(2,1)S(1)} %get-tuple-element.34), channel_id=1, source_target_pairs={{0,8},{4,12},{8,0},{12,4},{1,9},{5,13},{9,1},{13,5},{2,10},{6,14},... | collective-permute-start | bytes 196616 | tf_op jit(solution)/shard_map/ppermute | solution.py:599
  39.5 7.8 %collective-permute-start.9 = (s16[2,128,128]{2,1,0:T(8,128)(2,1)S(1)}, s16[2,128,128]{2,1,0:T(8,128)(2,1)S(1)}, u32[]{:S(2)}, u32[]{:S(2)}) collective-permute-start(s16[2,128,128]{2,1,0:T(8,128)(2,1)S(1)} %get-tuple-element.35), channel_id=1, source_target_pairs={{0,12},{4,8},{8,4},{12,0},{1,13},{5,9},{9,5},{13,1},{2,14},{6,10},... | collective-permute-start | bytes 196616 | tf_op jit(solution)/shard_map/ppermute | solution.py:599
  48.8 4.1 %collective-permute-start.16 = (f32[8,128]{1,0:T(8,128)S(1)}, f32[8,128]{1,0:T(8,128)S(1)}, u32[]{:S(2)}, u32[]{:S(2)}) collective-permute-start(f32[8,128]{1,0:T(8,128)S(1)} %get-tuple-element.42), channel_id=1, source_target_pairs={{0,3},{1,0},{2,1},{3,2},{4,7},{5,4},{6,5},{7,6},{8,11},{9,8},{10,9... | collective-permute-start | bytes 12296 | tf_op jit(solution)/shard_map/ppermute | solution.py:727
  48.8 5.3 %collective-permute-start.15 = (f32[8,128]{1,0:T(8,128)S(1)}, f32[8,128]{1,0:T(8,128)S(1)}, u32[]{:S(2)}, u32[]{:S(2)}) collective-permute-start(f32[8,128]{1,0:T(8,128)S(1)} %get-tuple-element.42), channel_id=1, source_target_pairs={{0,2},{1,3},{2,0},{3,1},{4,6},{5,7},{6,4},{7,5},{8,10},{9,11},{10,... | collective-permute-start | bytes 12296 | tf_op jit(solution)/shard_map/ppermute | solution.py:727
  49.4 4.7 %collective-permute-start.14 = (f32[8,128]{1,0:T(8,128)S(1)}, f32[8,128]{1,0:T(8,128)S(1)}, u32[]{:S(2)}, u32[]{:S(2)}) collective-permute-start(f32[8,128]{1,0:T(8,128)S(1)} %get-tuple-element.42), channel_id=1, source_target_pairs={{0,1},{1,2},{2,3},{3,0},{4,5},{5,6},{6,7},{7,4},{8,9},{9,10},{10,1... | collective-permute-start | bytes 12296 | tf_op jit(solution)/shard_map/ppermute | solution.py:727
  49.7 4.5 %collective-permute-start.11 = (s16[144,128]{1,0:T(8,128)(2,1)S(1)}, s16[144,128]{1,0:T(8,128)(2,1)S(1)}, u32[]{:S(2)}, u32[]{:S(2)}) collective-permute-start(s16[144,128]{1,0:T(8,128)(2,1)S(1)} %get-tuple-element.39), channel_id=1, source_target_pairs={{0,4},{4,0},{8,12},{12,8},{1,5},{5,1},{9,13},{13,9},{2,6},{6,2},{1... | collective-permute-start | bytes 110600 | tf_op jit(solution)/shard_map/ppermute | solution.py:599
  50.4 8.9 %collective-permute-start.12 = (s16[144,128]{1,0:T(8,128)(2,1)S(1)}, s16[144,128]{1,0:T(8,128)(2,1)S(1)}, u32[]{:S(2)}, u32[]{:S(2)}) collective-permute-start(s16[144,128]{1,0:T(8,128)(2,1)S(1)} %get-tuple-element.40), channel_id=1, source_target_pairs={{0,8},{4,12},{8,0},{12,4},{1,9},{5,13},{9,1},{13,5},{2,10},{6,14},... | collective-permute-start | bytes 110600 | tf_op jit(solution)/shard_map/ppermute | solution.py:599
  52.8 6.5 %collective-permute-start.13 = (s16[144,128]{1,0:T(8,128)(2,1)S(1)}, s16[144,128]{1,0:T(8,128)(2,1)S(1)}, u32[]{:S(2)}, u32[]{:S(2)}) collective-permute-start(s16[144,128]{1,0:T(8,128)(2,1)S(1)} %get-tuple-element.41), channel_id=1, source_target_pairs={{0,12},{4,8},{8,4},{12,0},{1,13},{5,9},{9,5},{13,1},{2,14},{6,10},... | collective-permute-start | bytes 110600 | tf_op jit(solution)/shard_map/ppermute | solution.py:599
  54.2 5.5 %collective-permute-start.19 = (f32[8,128]{1,0:T(8,128)S(1)}, f32[8,128]{1,0:T(8,128)S(1)}, u32[]{:S(2)}, u32[]{:S(2)}) collective-permute-start(f32[8,128]{1,0:T(8,128)S(1)} %add_add_fusion.refs_3_), channel_id=1, source_target_pairs={{0,12},{4,8},{8,4},{12,0},{1,13},{5,9},{9,5},{13,1},{2,14},{6,10},... | collective-permute-start | bytes 12296 | tf_op jit(solution)/shard_map/ppermute | solution.py:599
  56.7 4.5 %collective-permute-start.18 = (f32[8,128]{1,0:T(8,128)S(1)}, f32[8,128]{1,0:T(8,128)S(1)}, u32[]{:S(2)}, u32[]{:S(2)}) collective-permute-start(f32[8,128]{1,0:T(8,128)S(1)} %add_add_fusion.refs_3_), channel_id=1, source_target_pairs={{0,8},{4,12},{8,0},{12,4},{1,9},{5,13},{9,1},{13,5},{2,10},{6,14},... | collective-permute-start | bytes 12296 | tf_op jit(solution)/shard_map/ppermute | solution.py:599
  56.7 4.5 %collective-permute-start.17 = (f32[8,128]{1,0:T(8,128)S(1)}, f32[8,128]{1,0:T(8,128)S(1)}, u32[]{:S(2)}, u32[]{:S(2)}) collective-permute-start(f32[8,128]{1,0:T(8,128)S(1)} %add_add_fusion.refs_3_), channel_id=1, source_target_pairs={{0,4},{4,0},{8,12},{12,8},{1,5},{5,1},{9,13},{13,9},{2,6},{6,2},{1... | collective-permute-start | bytes 12296 | tf_op jit(solution)/shard_map/ppermute | solution.py:599
